TPU v7x, 32 devices: a whole 2x2x4 slice. The times are simulated.
32 devices in a mesh: img: 4 (over y, core), seq: 8 (over z, x).
Axes of the slice: x: 2, y: 2, z: 4, core: 2. Of those that a mesh axis runs over, the one named last changes fastest.
Arguments:
- llm_grads: bfloat16 [4, 256, 8192], P('img', 'seq'), may hold values from -6 to 6
- token_target: int32 [4, 256], P('img', 'seq'), may hold values from 0 to 255, as said below
- patches: bfloat16 [4, 1024, 1280], P('img', 'seq'), may hold values from -150 to 150
- gain: float32 [1280], replicated, may hold values from 0.5 to 1.5
- w_down: bfloat16 [5120, 8192], P(None, 'img'), may hold values from -0.078125 to 0.078125
- queries: bfloat16 [4, 1024, 1280], P('img', 'seq'), may hold values from -40 to 40
- keys: bfloat16 [4, 1024, 1280], P('img', 'seq'), may hold values from -5 to 5
- values: bfloat16 [4, 1024, 1280], P('img', 'seq'), may hold values from -5 to 5
- window_ids: int32 [4, 8, 32], P('img', 'seq'), may hold values from 0 to 3, never falling along the last dimension, each value on 1 to 16 neighbouring positions
Outputs:
- grad_q: bfloat16 [4, 1024, 1280], P('img', 'seq')
- grad_k: bfloat16 [4, 1024, 1280], P('img', 'seq')
- grad_v: bfloat16 [4, 1024, 1280], P('img', 'seq')
- gain_grad: float32 [1280], replicated
- bias_grad: float32 [8192], replicated
Inputs may be any that keep to these rules, and one draw needn't show every extreme that they name: In each group i, token_target[i] is a permutation: position s * 32 + j (held by index s of seq) holds merged token d * 32 + m (held by index d of seq). At most 8 position of one seq index holds a merged token of any one seq index, and in every group some pair of seq indices has exactly 8.
All inputs are finite; a program needn't handle non-finite values.
Results may differ from a plain program's by a relative error of at most 0.024.
Values may be sent and summed in bfloat16 or wider, within the bound.
No kernel may reach another device: no remote copies, remote signals or barrier semaphores. Data moves between devices by JAX's collectives and lax.ppermute only.
A program may use at most 64 MiB of HBM per device.

v0:
```python
import math

import jax
import jax.numpy as jnp
from jax import lax
from jax.sharding import PartitionSpec as P

HEADS = 16
HEAD_DIM = 80


def earlier_equal(labels, order_key):
    same_label = labels[:, None] == labels[None, :]
    earlier = order_key[None, :] < order_key[:, None]
    return jnp.sum(jnp.logical_and(same_label, earlier), axis=1)


def pack_rows(row_values, targets, peer_count, capacity):
    row_count = row_values.shape[0]
    destination = targets // row_count
    local_row = targets % row_count
    slot_index = destination * capacity + earlier_equal(
        destination, jnp.arange(row_count, dtype=jnp.int32)
    )
    matches = slot_index[None, :] == jnp.arange(peer_count * capacity, dtype=jnp.int32)[:, None]
    selector = matches.astype(row_values.dtype)
    packed = jnp.dot(selector, row_values, preferred_element_type=jnp.float32).astype(
        row_values.dtype
    )
    slot_rows = jnp.sum(jnp.where(matches, local_row[None, :] + 1, 0), axis=1) - 1
    slot_labels = slot_rows.astype(jnp.float32).astype(jnp.bfloat16).reshape(peer_count, capacity)
    return (packed.reshape(peer_count, capacity, row_values.shape[1]), slot_labels)


def unpack_rows(received, slot_labels, row_count):
    flat_rows = received.reshape(-1, received.shape[2])
    flat_labels = slot_labels.reshape(-1).astype(jnp.float32).astype(jnp.int32)
    selector = (flat_labels[None, :] == jnp.arange(row_count, dtype=jnp.int32)[:, None]).astype(
        flat_rows.dtype
    )
    return jnp.dot(selector, flat_rows, preferred_element_type=jnp.float32).astype(flat_rows.dtype)


def project_rows(row_values, w_down):
    columns = lax.all_to_all(row_values, "img", split_axis=1, concat_axis=0, tiled=True)
    return lax.psum_scatter(
        lax.dot_general(
            columns, w_down, (((1,), (1,)), ((), ())), preferred_element_type=jnp.float32
        ).astype(jnp.bfloat16),
        "img",
        scatter_dimension=0,
        tiled=True,
    ).astype(jnp.float32)


def window_backward(query_rows, key_rows, value_rows, grad_rows, window_labels):
    patch_count = query_rows.shape[0]
    patch_width = query_rows.shape[1]
    score_scale = 1.0 / math.sqrt(HEAD_DIM)
    labels = jnp.repeat(window_labels, 4)
    allowed = labels[:, None] == labels[None, :]
    query_heads = query_rows.reshape(patch_count, HEADS, HEAD_DIM)
    key_heads = key_rows.reshape(patch_count, HEADS, HEAD_DIM)
    value_heads = value_rows.reshape(patch_count, HEADS, HEAD_DIM)
    grad_heads = grad_rows.reshape(patch_count, HEADS, HEAD_DIM)
    scores = (
        jnp.einsum("phd,qhd->hpq", query_heads, key_heads, preferred_element_type=jnp.float32)
        * score_scale
    )
    scores = jnp.where(allowed[None, :, :], scores, -jnp.inf)
    peak = jnp.max(scores, axis=2, keepdims=True)
    raw_weights = jnp.exp(scores - peak)
    probs = raw_weights / jnp.sum(raw_weights, axis=2, keepdims=True)
    probs_bf = probs.astype(jnp.bfloat16)
    attended = jnp.einsum("hpq,qhd->phd", probs_bf, value_heads, preferred_element_type=jnp.float32)
    row_delta = jnp.sum(grad_heads.astype(jnp.float32) * attended, axis=2)
    prob_grads = jnp.einsum(
        "phd,qhd->hpq", grad_heads, value_heads, preferred_element_type=jnp.float32
    )
    score_bf = (probs * (prob_grads - jnp.transpose(row_delta)[:, :, None])).astype(jnp.bfloat16)
    grad_query = (
        jnp.einsum("hpq,qhd->phd", score_bf, key_heads, preferred_element_type=jnp.float32)
        * score_scale
    )
    grad_key = (
        jnp.einsum("hpq,phd->qhd", score_bf, query_heads, preferred_element_type=jnp.float32)
        * score_scale
    )
    grad_value = jnp.einsum(
        "hpq,phd->qhd", probs_bf, grad_heads, preferred_element_type=jnp.float32
    )
    return (
        grad_query.reshape(patch_count, patch_width).astype(jnp.bfloat16),
        grad_key.reshape(patch_count, patch_width).astype(jnp.bfloat16),
        grad_value.reshape(patch_count, patch_width).astype(jnp.bfloat16),
    )


def body(llm_grads, token_target, patches, gain, w_down, queries, keys, values, window_ids):
    grad_rows = llm_grads[0]
    targets = token_target[0]
    row_count = grad_rows.shape[0]
    peer_count = lax.axis_size("seq")
    capacity = max(1, 2 * row_count // peer_count)
    packed, slot_labels = pack_rows(grad_rows, targets, peer_count, capacity)
    arrived, arrived_labels = (
        lax.all_to_all(packed, "seq", split_axis=0, concat_axis=0, tiled=True),
        lax.all_to_all(slot_labels, "seq", split_axis=0, concat_axis=0, tiled=True),
    )
    merged = project_rows(unpack_rows(arrived, arrived_labels, row_count), w_down).astype(
        jnp.bfloat16
    )
    patch_width = patches.shape[2]
    patch_grads = merged.reshape(-1, patch_width).astype(jnp.float32)
    inputs = patches[0].astype(jnp.float32)
    inverse_rms = lax.rsqrt(jnp.mean(inputs * inputs, axis=1, keepdims=True) + 1e-06)
    normed = inputs * inverse_rms
    gain_part = jnp.sum(patch_grads * normed, axis=0)
    bias_part = jnp.sum(grad_rows.astype(jnp.float32), axis=0)
    gain_total, bias_total = lax.psum((gain_part, bias_part), ("img", "seq"))
    device_count = lax.axis_size("img") * lax.axis_size("seq")
    gain_grad = gain_total / math.sqrt(device_count * inputs.shape[0])
    bias_grad = bias_total / math.sqrt(device_count * row_count)
    scaled = gain[None, :] * patch_grads
    out_grads = (
        inverse_rms * (scaled - normed * jnp.mean(scaled * normed, axis=1, keepdims=True))
    ).astype(jnp.bfloat16)
    grad_query, grad_key, grad_value = window_backward(
        queries[0], keys[0], values[0], out_grads, window_ids[0, 0]
    )
    return (grad_query[None], grad_key[None], grad_value[None], gain_grad, bias_grad)


def solution(mesh):
    return jax.shard_map(
        body,
        mesh=mesh,
        in_specs=(
            P("img", "seq", None),
            P("img", "seq"),
            P("img", "seq", None),
            P(),
            P(None, "img"),
            P("img", "seq", None),
            P("img", "seq", None),
            P("img", "seq", None),
            P("img", "seq", None),
        ),
        out_specs=(P("img", "seq", None), P("img", "seq", None), P("img", "seq", None), P(), P()),
        check_vma=False,
    )
```

profile of v0, /device:TPU:0, one launch (start us, length us, event | category | flops | bytes accessed | tf_op | source)
XLA Modules:
  0.0 160.4 jit_solution(11609788322834745050)
XLA Ops:
  7.2 0.0 copy-start
  7.2 0.0 copy-start.5
  7.2 0.0 copy-start.2
  7.2 0.0 copy-start.6
  7.2 0.7 fusion.19
  7.9 0.7 and_select_fusion.1
  8.6 0.2 convert_reduce_fusion.1
  8.8 0.1 select_reduce_fusion
  8.9 0.7 convert_element_type.184
  9.6 7.3 %all-to-all-start = ((bf16[8,1,8]{2,1,0:T(2,128)(2,1)}), bf16[8,1,8]{2,1,0:T(2,128)(2,1)S(1)}, u32[]{:S(2)}, u32[]{:S(2)}) async-start(bf16[8,1,8]{2,1,0:T(2,128)(2,1)} %convert_element_type.184), calls=%async_computation | async-start | bytes 8192 | tf_op jit(solution)/shard_map/all_to_all | solution.py:108
  16.8 2.6 %fusion.1 = bf16[8,8,8192]{2,1,0:T(8,128)(2,1)} fusion(bf16[1,32,8192]{2,1,0:T(8,128)(2,1)} %param.9, s32[32]{0:T(128)S(1)} %fusion.20), kind=kOutput, calls=%fused_computation.2 | convolution fusion | flops 34080768 | bytes 1572992 | tf_op jit(solution)/shard_map/dot_general | solution.py:27
  19.4 0.0 copy-start.1
  19.4 3.8 %all-to-all-done = bf16[8,1,8]{2,1,0:T(2,128)(2,1)S(1)} async-done(((bf16[8,1,8]{2,1,0:T(2,128)(2,1)}), bf16[8,1,8]{2,1,0:T(2,128)(2,1)S(1)}, u32[]{:S(2)}, u32[]{:S(2)}) %all-to-all-start) | async-done | bytes 160 | tf_op jit(solution)/shard_map/all_to_all | solution.py:108
  23.2 3.6 %all-to-all-start.1 = ((bf16[8,8,8192]{2,1,0:T(8,128)(2,1)}), bf16[8,8,8192]{2,1,0:T(8,128)(2,1)S(1)}, u32[]{:S(2)}, u32[]{:S(2)}) async-start(bf16[8,8,8192]{2,1,0:T(8,128)(2,1)} %fusion.1), calls=%async_computation.1 | async-start | bytes 2097152 | tf_op jit(solution)/shard_map/all_to_all | solution.py:107
  26.8 0.0 reduce-scatter.2.cloned.1.call-start
  26.9 0.1 convert_element_type.156
  26.9 24.6 %all-to-all-done.1 = bf16[8,8,8192]{2,1,0:T(8,128)(2,1)S(1)} async-done(((bf16[8,8,8192]{2,1,0:T(8,128)(2,1)}), bf16[8,8,8192]{2,1,0:T(8,128)(2,1)S(1)}, u32[]{:S(2)}, u32[]{:S(2)}) %all-to-all-start.1) | async-done | bytes 1048608 | tf_op jit(solution)/shard_map/all_to_all | solution.py:107
  51.5 0.3 convolution_convert_fusion.1
  51.8 0.0 copy-start.3
  51.8 0.0 copy-start.4
  51.9 11.6 %all_to_all.30 = bf16[32,4,2048]{2,0,1:T(8,128)(2,1)S(1)} all-to-all(bf16[32,4,2048]{2,0,1:T(8,128)(2,1)S(1)} %bitcast.78), channel_id=1, replica_groups=mesh['img'=4,'seq'=8] {'img'}, dimensions={1} | all-to-all | bytes 1048576 | tf_op jit(solution)/shard_map/all_to_all | solution.py:45
  63.4 12.3 %convolution_convert_fusion.2 = bf16[128,5120]{1,0:T(8,128)(2,1)} fusion(bf16[128,2048]{1,0:T(8,128)(2,1)S(1)} %bitcast.75, bf16[5120,2048]{1,0:T(8,128)(2,1)} %param.13), kind=kOutput, calls=%fused_computation.4 | convolution fusion | flops 2685009920 | bytes 22806528 | tf_op jit(solution)/shard_map/dot_general | solution.py:47
  75.8 0.0 reduce-scatter.2.cloned.1.call-update
  75.8 0.0 copy-done
  75.8 0.2 copy.64
  76.0 0.0 copy-done.5
  76.0 0.1 mul.84
  76.1 0.0 copy-done.2
  76.1 0.2 copy.59
  76.3 0.0 copy-done.3
  76.3 0.2 copy.60
  76.5 0.0 copy-done.6
  76.5 0.1 broadcast_in_dim.24
  76.6 0.1 eq.64
  76.7 0.0 copy-done.4
  76.7 0.9 copy.65
  77.6 0.1 fusion.12
  77.7 0.0 copy-done.1
  77.7 0.1 convert_reduce_fusion
  77.9 0.1 broadcast_compare_fusion
  78.0 1.5 fusion.26
  79.5 20.9 %reduce-scatter.2.cloned.1.call-done = bf16[32,5120]{1,0:T(8,128)(2,1)} async-done(((bf16[128,5120]{1,0:T(8,128)(2,1)}), bf16[32,5120]{1,0:T(8,128)(2,1)}) %reduce-scatter.2.cloned.1.call-update) | async-done | bytes 327696 | tf_op jit(solution)/shard_map/reduce_scatter | solution.py:46
  100.4 1.2 reshape.205
  101.5 0.3 multiply_reduce_fusion
  101.8 1.5 reshape.203
  103.4 0.4 copy.63
  103.8 0.2 multiply_convert_fusion
  104.0 1.7 %fusion.10 = f32[128,16]{0,1:T(8,128)S(1)} fusion(bf16[128,16,80]{0,2,1:T(8,128)(2,1)} %bitcast.85, bf16[128,16,80]{0,2,1:T(8,128)(2,1)S(1)} %multiply_convert_fusion, f32[16,128,128]{1,2,0:T(8,128)} %get-tuple-element.32, f32[16,128]{1,0:T(8,128)S(1)} %get-tuple-element.31), kind=kOutput, calls=%fused_computation.19 | convolution fusion | flops 42956800 | bytes 1720320 | tf_op jit(solution)/shard_map/hpq,qhd->phd/dot_general | solution.py:75
  105.7 1.7 %fusion.6 = bf16[16,128,128]{1,2,0:T(8,128)(2,1)S(1)} fusion(bf16[128,16,80]{0,2,1:T(8,128)(2,1)S(1)} %multiply_convert_fusion, bf16[128,16,80]{0,2,1:T(8,128)(2,1)} %bitcast.86, f32[16,128]{1,0:T(8,128)S(1)} %bitcast.90, f32[16,128,128]{1,2,0:T(8,128)} %get-tuple-element.32, f32[16,128]{1,0:T(8,128)S(1)} %get-tuple-element.31), kind=kOutput, calls=%fused_computation.11 | convolution fusion | flops 42991616 | bytes 2244608 | tf_op jit(solution)/shard_map/phd,qhd->hpq/dot_general | solution.py:77
  107.4 0.5 fusion.8
  107.9 0.3 fusion.9
  108.3 1.7 %convolution_convert_fusion.3 = bf16[16,80,128]{2,1,0:T(8,128)(2,1)S(1)} fusion(bf16[128,16,80]{0,2,1:T(8,128)(2,1)S(1)} %multiply_convert_fusion, f32[16,128,128]{1,2,0:T(8,128)} %get-tuple-element.32, f32[16,128]{1,0:T(8,128)S(1)} %get-tuple-element.31), kind=kOutput, calls=%fused_computation.18 | convolution fusion | flops 42631168 | bytes 1712128 | tf_op jit(solution)/shard_map/hpq,phd->qhd/dot_general | solution.py:89
  110.0 0.9 copy.72
  110.9 0.9 copy.71
  111.8 0.9 copy.73
  112.7 39.7 %all-reduce = (f32[1280]{0:T(1024)S(1)}, f32[8192]{0:T(1024)S(1)}) all-reduce(f32[1280]{0:T(1024)S(1)} %get-tuple-element.25, f32[8192]{0:T(1024)S(1)} %convert_reduce_fusion), channel_id=1, replica_groups=mesh['img'=4,'seq'=8] {'img','seq'}, use_global_device_ids=true, to_apply=%region_9.10 | all-reduce | flops 9472 | bytes 75776 | tf_op jit(solution)/shard_map/psum | solution.py:120
  152.4 0.6 broadcast_multiply_fusion
  153.0 0.6 broadcast_multiply_fusion.1
  (6 shorter events, 0.1 us)
Async XLA Ops:
  7.2 68.6 %copy-start = (bf16[1,128,1280]{2,1,0:T(8,128)(2,1)S(1)}, bf16[1,128,1280]{2,1,0:T(8,128)(2,1)}, u32[]{:S(2)}) copy-start(bf16[1,128,1280]{2,1,0:T(8,128)(2,1)} %param.11) | copy-start | bytes 983044
  7.2 68.8 %copy-start.5 = (f32[1280]{0:T(1024)S(1)}, f32[1280]{0:T(1024)}, u32[]{:S(2)}) copy-start(f32[1280]{0:T(1024)} %param.12) | copy-start | bytes 15364
  7.2 68.9 %copy-start.2 = (bf16[1,128,1280]{2,1,0:T(8,128)(2,1)S(1)}, bf16[1,128,1280]{2,1,0:T(8,128)(2,1)}, u32[]{:S(2)}) copy-start(bf16[1,128,1280]{2,1,0:T(8,128)(2,1)} %param.14) | copy-start | bytes 983044
  7.2 69.3 %copy-start.6 = (s32[1,1,32]{2,1,0:T(1,128)S(1)}, s32[1,1,32]{2,1,0:T(1,128)}, u32[]{:S(2)}) copy-start(s32[1,1,32]{2,1,0:T(1,128)} %param.17) | copy-start | bytes 388
  9.6 13.6 %all-to-all-start = ((bf16[8,1,8]{2,1,0:T(2,128)(2,1)}), bf16[8,1,8]{2,1,0:T(2,128)(2,1)S(1)}, u32[]{:S(2)}, u32[]{:S(2)}) async-start(bf16[8,1,8]{2,1,0:T(2,128)(2,1)} %convert_element_type.184), calls=%async_computation | async-start | bytes 8192 | tf_op jit(solution)/shard_map/all_to_all | solution.py:108
  19.4 58.3 %copy-start.1 = (bf16[1,32,8192]{2,1,0:T(8,128)(2,1)S(1)}, bf16[1,32,8192]{2,1,0:T(8,128)(2,1)}, u32[]{:S(2)}) copy-start(bf16[1,32,8192]{2,1,0:T(8,128)(2,1)} %param.9) | copy-start | bytes 1572868
  23.2 28.3 %all-to-all-start.1 = ((bf16[8,8,8192]{2,1,0:T(8,128)(2,1)}), bf16[8,8,8192]{2,1,0:T(8,128)(2,1)S(1)}, u32[]{:S(2)}, u32[]{:S(2)}) async-start(bf16[8,8,8192]{2,1,0:T(8,128)(2,1)} %fusion.1), calls=%async_computation.1 | async-start | bytes 2097152 | tf_op jit(solution)/shard_map/all_to_all | solution.py:107
  26.8 73.6 %reduce-scatter.2.cloned.1.call-start = ((), (), s32[]{:S(2)}) async-start(), calls=%async_computation.4 | async-start | bytes 1638400 | tf_op jit(solution)/shard_map/reduce_scatter | solution.py:46
  51.8 24.5 %copy-start.3 = (bf16[1,128,1280]{2,1,0:T(8,128)(2,1)S(1)}, bf16[1,128,1280]{2,1,0:T(8,128)(2,1)}, u32[]{:S(2)}) copy-start(bf16[1,128,1280]{2,1,0:T(8,128)(2,1)} %param.15) | copy-start | bytes 983044
  51.8 24.9 %copy-start.4 = (bf16[1,128,1280]{2,1,0:T(8,128)(2,1)S(1)}, bf16[1,128,1280]{2,1,0:T(8,128)(2,1)}, u32[]{:S(2)}) copy-start(bf16[1,128,1280]{2,1,0:T(8,128)(2,1)} %param.16) | copy-start | bytes 983044
Sparse Core Ops, SparseCore 0:
  75.9 24.4 reduce-scatter.1
where the time goes:
time: 161 us; the launch traced here: 160 us
  blocking collectives  51.2 us (32%)
  waiting for transfers between devices  49.3 us (31%)
  matrix products  22.6 us (14%)
  between operations  14.3 us (9%)
  starting transfers between devices  10.9 us (7%)
  local copies, waits for them, and re-layouts  8.4 us (5%)
  other arithmetic  3.81 us (2%)
    psum x1, blocking collectives, body(): gain_total, bias_total = lax.psum((gain_part, bias_part), ('img', 'seq'))  39.7 us
    all_to_all x1, waiting for transfers between devices, body(): lax.all_to_all(packed, 'seq', split_axis=0, concat_axis=0, tiled=True)  24.6 us
    reduce_scatter x1, waiting for transfers between devices, project_rows(): lax.psum_scatter(lax.dot_general(columns, w_down, (((1,), (1,)), ((), ())...  20.9 us
    dot_general x1, matrix products, project_rows(): lax.dot_general(columns, w_down, (((1,), (1,)), ((), ())), preferred_elem...  12.3 us
    all_to_all x1, blocking collectives, project_rows(): lax.all_to_all(row_values, 'img', split_axis=1, concat_axis=0, tiled=True)  11.6 us
    all_to_all x1, starting transfers between devices, body(): lax.all_to_all(slot_labels, 'seq', split_axis=0, concat_axis=0, tiled=True)  7.25 us
    unnamed x20, local copies, waits for them, and re-layouts  4.07 us
    all_to_all x1, waiting for transfers between devices, body(): lax.all_to_all(slot_labels, 'seq', split_axis=0, concat_axis=0, tiled=True)  3.81 us
  transfers between devices with their start and end apart: 3, of which 3 were waited for; matrix products, arithmetic and copies ran while one was open for 4% of the time, Pallas kernels for 0%

commit v1 on v0

v1 whole, which is shorter than its diff:
```python
import functools
import math

import jax
import jax.numpy as jnp
from jax import lax
from jax.experimental import pallas as pl
from jax.experimental.pallas import tpu as pltpu
from jax.sharding import PartitionSpec as P

HEADS = 16
HEAD_DIM = 80
LANES = 128
CHUNKS = (2, 2)
DIRECT = 8
VMEM_BYTES = 40 * 1024 * 1024

F32 = jnp.float32
BF16 = jnp.bfloat16


def iota(shape, axis):
    return lax.broadcasted_iota(jnp.int32, shape, axis)


def dot(a, b, over):
    return lax.dot_general(a, b, ((over[:1], over[1:]), ((), ())), preferred_element_type=F32)


def vmem(count):
    return [pl.BlockSpec(memory_space=pltpu.VMEM)] * count


def swap(x, axis, mask):
    n = lax.axis_size(axis)
    return lax.ppermute(x, axis, [(i, i ^ mask) for i in range(n)])


def tree_sum(terms):
    while len(terms) > 1:
        terms = [terms[i] + terms[i + 1] for i in range(0, len(terms), 2)]
    return terms[0]


def sum_over(x, axis):
    n = lax.axis_size(axis)
    if n > DIRECT:
        return lax.psum(x, axis)
    return tree_sum([x] + [swap(x, axis, mask) for mask in range(1, n)])


def head_windows():
    windows = []
    for head in range(HEADS):
        low, high = head * HEAD_DIM, (head + 1) * HEAD_DIM
        start = low // LANES * LANES
        windows.append((low, high, start, -(-high // LANES) * LANES))
    return windows


def lane_mask(low, high, start, stop):
    at = iota((1, stop - start), 1) + start
    return jnp.logical_and(at >= low, at < high)


def masked(x, low, high, start, stop):
    return jnp.where(lane_mask(low, high, start, stop), x, jnp.zeros_like(x))


def project_kernel(blocks, first, tile, tiles, with_sum, *refs):
    x_refs, w_ref = refs[:blocks], refs[blocks]
    outs = refs[blocks + 1 : 2 * blocks + 1]
    w_tiles, sems = refs[-2:]
    copies = [
        pltpu.make_async_copy(w_ref.at[pl.ds(first + t * tile, tile)], w_tiles.at[t], sems.at[t])
        for t in range(tiles)
    ]
    for copy in copies:
        copy.start()
    x = jnp.concatenate([ref[...] for ref in x_refs], axis=0)
    rows = x_refs[0].shape[0]
    if with_sum:
        ones = jnp.ones((16, x.shape[0]), BF16)
        refs[2 * blocks + 1][...] = dot(ones, x, (1, 0))[:1]
    for t in range(tiles):
        copies[t].wait()
        product = dot(x, w_tiles[t], (1, 1)).astype(BF16)
        for j in range(blocks):
            outs[j][:, t * tile : (t + 1) * tile] = product[j * rows : (j + 1) * rows]


def project(x_blocks, w_down, first, width, with_sum):
    blocks, (rows, depth) = len(x_blocks), x_blocks[0].shape
    tile = 256
    tiles = width // tile
    out_shape = [jax.ShapeDtypeStruct((rows, width), BF16)] * blocks
    if with_sum:
        out_shape = out_shape + [jax.ShapeDtypeStruct((1, depth), F32)]
    out = pl.pallas_call(
        functools.partial(project_kernel, blocks, first, tile, tiles, with_sum),
        out_shape=out_shape,
        in_specs=vmem(blocks) + [pl.BlockSpec(memory_space=pl.ANY)],
        out_specs=vmem(len(out_shape)),
        scratch_shapes=[
            pltpu.VMEM((tiles, tile, depth), BF16),
            pltpu.SemaphoreType.DMA((tiles,)),
        ],
        compiler_params=pltpu.CompilerParams(vmem_limit_bytes=VMEM_BYTES),
        cost_estimate=pl.CostEstimate(
            flops=2 * blocks * rows * depth * width,
            bytes_accessed=2 * width * depth,
            transcendentals=0,
        ),
        name="project",
    )(*x_blocks, w_down)
    return out[:blocks], (out[blocks] if with_sum else None)


def pack_kernel(peers, capacity, direct, labelled, blocks, me_ref, targets_ref, *refs):
    terms, outs = refs[:blocks], refs[blocks:]
    targets = targets_ref[...]
    rows = targets.shape[1]
    dest = targets // rows
    local = targets - dest * rows
    dest_column = jnp.sum(
        jnp.where(iota((rows, rows), 0) == iota((rows, rows), 1), dest, 0), axis=1, keepdims=True
    )
    same_before = jnp.logical_and(dest_column == dest, iota((rows, rows), 0) < iota((rows, rows), 1))
    rank = jnp.sum(same_before.astype(jnp.int32), axis=0, keepdims=True)
    slots = peers * capacity
    slot = iota((slots, rows), 0)
    holder = slot // capacity
    if direct:
        holder = holder ^ me_ref[0]
    chosen = jnp.logical_and(dest == holder, rank == slot % capacity)
    total = terms[0][...].astype(F32)
    for term in terms[1:]:
        total = total + term[...].astype(F32)
    width = total.shape[1]
    packed = dot(chosen.astype(F32).astype(BF16), total.astype(BF16), (1, 0))
    if labelled:
        label = jnp.sum(jnp.where(chosen, local + 1, 0), axis=1, keepdims=True) - 1
        packed = jnp.concatenate(
            [packed, jnp.broadcast_to(label.astype(F32), (slots, LANES))], axis=1
        )
    if not direct:
        outs[0][...] = packed.astype(BF16)
        return
    for m in range(peers):
        outs[m][...] = packed[m * capacity : (m + 1) * capacity].astype(BF16)


def pack(terms, targets, me, peers, capacity, direct, labelled):
    rows, width = terms[0].shape
    width = width + (LANES if labelled else 0)
    if direct:
        out_shape = [jax.ShapeDtypeStruct((capacity, width), BF16)] * peers
    else:
        out_shape = [jax.ShapeDtypeStruct((peers * capacity, width), BF16)]
    return pl.pallas_call(
        functools.partial(pack_kernel, peers, capacity, direct, labelled, len(terms)),
        out_shape=out_shape,
        in_specs=[pl.BlockSpec(memory_space=pltpu.SMEM)] + vmem(1 + len(terms)),
        out_specs=vmem(len(out_shape)),
        compiler_params=pltpu.CompilerParams(vmem_limit_bytes=VMEM_BYTES),
        cost_estimate=pl.CostEstimate(
            flops=2 * rows * peers * capacity * width,
            bytes_accessed=2 * (len(terms) * rows + peers * capacity) * width,
            transcendentals=0,
        ),
        name="pack",
    )(me, targets, *terms)


def route(packed, peers, capacity, direct):
    if direct:
        return [packed[0]] + [swap(packed[m], "seq", m) for m in range(1, peers)]
    width = packed[0].shape[1]
    sent = packed[0].reshape(peers, capacity, width)
    got = lax.all_to_all(sent, "seq", split_axis=0, concat_axis=0, tiled=True)
    return [got.reshape(peers * capacity, width)]


def probs_kernel(q_ref, k_ref, ids_ref, probs_ref, probs_t_ref):
    patches = q_ref.shape[0]
    ids = ids_ref[...]
    per_token = patches // ids.shape[1]
    token = iota((patches, ids.shape[1]), 0) // per_token
    column = jnp.sum(
        jnp.where(token == iota((patches, ids.shape[1]), 1), ids, 0), axis=1, keepdims=True
    )
    square = (patches, patches)
    row = jnp.sum(
        jnp.where(iota(square, 0) == iota(square, 1), column, 0), axis=0, keepdims=True
    )
    allowed = column == row
    scale = 1.0 / math.sqrt(HEAD_DIM)
    for head, (low, high, start, stop) in enumerate(head_windows()):
        q = masked(q_ref[:, start:stop], low, high, start, stop)
        k = k_ref[:, start:stop]
        for out, scores, axis in (
            (probs_ref, dot(q, k, (1, 1)), 1),
            (probs_t_ref, dot(k, q, (1, 1)), 0),
        ):
            scores = jnp.where(allowed, scores * scale, -jnp.inf)
            weights = jnp.exp(scores - jnp.max(scores, axis=axis, keepdims=True))
            out[head] = weights / jnp.sum(weights, axis=axis, keepdims=True)


def window_probs(queries, keys, ids):
    patches = queries.shape[0]
    shape = jax.ShapeDtypeStruct((HEADS, patches, patches), F32)
    return pl.pallas_call(
        probs_kernel,
        out_shape=[shape, shape],
        in_specs=vmem(3),
        out_specs=vmem(2),
        compiler_params=pltpu.CompilerParams(vmem_limit_bytes=VMEM_BYTES),
        cost_estimate=pl.CostEstimate(
            flops=8 * HEADS * patches * patches * LANES,
            bytes_accessed=8 * HEADS * patches * patches,
            transcendentals=2 * HEADS * patches * patches,
        ),
        name="probs",
    )(queries, keys, ids)


def norm_kernel(counts, parts, slots, patches_ref, gain_ref, *refs):
    chunks, at = [], 0
    for count in counts:
        chunks.append([ref[...].astype(F32) for ref in refs[at : at + count]])
        at += count
    out_ref, gain_grad_ref = refs[at:]
    patches, width = patches_ref.shape
    chunks = [jnp.concatenate(chunk, axis=0) for chunk in chunks]
    labels = chunks[0][:, parts[0] * width :][:, :1]
    columns = []
    for chunk, count in zip(chunks, parts):
        columns += [chunk[:, c * width : (c + 1) * width] for c in range(count)]
    held = jnp.concatenate(columns, axis=0).astype(BF16)
    lanes = len(columns) * slots
    lane = iota((slots, lanes), 1)
    row_of_lane = jnp.sum(
        jnp.where(lane % slots == iota((slots, lanes), 0), labels, 0.0), axis=0, keepdims=True
    ).astype(jnp.int32)
    patch_of_lane = row_of_lane * len(columns) + iota((1, lanes), 1) // slots
    patch_of_lane = jnp.where(row_of_lane < 0, -1, patch_of_lane)
    chosen = patch_of_lane == iota((patches, lanes), 0)
    patch_grads = dot(chosen.astype(F32).astype(BF16), held, (1, 0))
    inputs = patches_ref[...].astype(F32)
    inverse_rms = lax.rsqrt(jnp.mean(inputs * inputs, axis=1, keepdims=True) + 1e-06)
    normed = inputs * inverse_rms
    gain_grad_ref[...] = jnp.sum(patch_grads * normed, axis=0, keepdims=True)
    scaled = gain_ref[...] * patch_grads
    out_ref[...] = (
        inverse_rms * (scaled - normed * jnp.mean(scaled * normed, axis=1, keepdims=True))
    ).astype(BF16)


def norm_backward(received, parts, slots, patches, gain):
    counts = [len(chunk) for chunk in received]
    flat = [x for chunk in received for x in chunk]
    count, width = patches.shape
    return pl.pallas_call(
        functools.partial(norm_kernel, counts, parts, slots),
        out_shape=[
            jax.ShapeDtypeStruct((count, width), BF16),
            jax.ShapeDtypeStruct((1, width), F32),
        ],
        in_specs=vmem(2 + len(flat)),
        out_specs=vmem(2),
        compiler_params=pltpu.CompilerParams(vmem_limit_bytes=VMEM_BYTES),
        cost_estimate=pl.CostEstimate(
            flops=2 * count * width * slots * sum(parts),
            bytes_accessed=2 * width * (2 * count + slots * sum(parts)),
            transcendentals=0,
        ),
        name="norm",
    )(patches, gain, *flat)


def window_kernel(g_ref, q_ref, k_ref, v_ref, probs_ref, probs_t_ref, dq_ref, dk_ref, dv_ref):
    width = g_ref.shape[1]
    windows = head_windows()
    scores, scores_t, probs_t = [], [], []
    for head, (low, high, start, stop) in enumerate(windows):
        g = masked(g_ref[:, start:stop], low, high, start, stop)
        v = v_ref[:, start:stop]
        found = []
        for ref, grads, axis in (
            (probs_ref, dot(g, v, (1, 1)), 1),
            (probs_t_ref, dot(v, g, (1, 1)), 0),
        ):
            probs = ref[head]
            rounded = probs.astype(BF16)
            delta = jnp.sum(rounded.astype(F32) * grads, axis=axis, keepdims=True)
            found.append(((probs * (grads - delta)).astype(BF16), rounded))
        scores.append(found[0][0])
        scores_t.append(found[1][0])
        probs_t.append(found[1][1])
    scale = 1.0 / math.sqrt(HEAD_DIM)
    for start in range(0, width, LANES):
        stop = start + LANES
        heads = [h for h, (low, high, _, _) in enumerate(windows) if low < stop and high > start]
        for out, left, right_ref, factor in (
            (dq_ref, scores, k_ref, scale),
            (dk_ref, scores_t, q_ref, scale),
            (dv_ref, probs_t, g_ref, 1.0),
        ):
            right = right_ref[:, start:stop]
            rows = [masked(right, windows[h][0], windows[h][1], start, stop) for h in heads]
            product = dot(
                jnp.concatenate([left[h] for h in heads], axis=1),
                jnp.concatenate(rows, axis=0),
                (1, 0),
            )
            out[:, start:stop] = (product * factor).astype(BF16)


def window_backward(out_grads, queries, keys, values, probs, probs_t):
    patches, width = queries.shape
    shape = jax.ShapeDtypeStruct((patches, width), BF16)
    return pl.pallas_call(
        window_kernel,
        out_shape=[shape] * 3,
        in_specs=vmem(6),
        out_specs=vmem(3),
        compiler_params=pltpu.CompilerParams(vmem_limit_bytes=VMEM_BYTES),
        cost_estimate=pl.CostEstimate(
            flops=10 * HEADS * patches * patches * LANES,
            bytes_accessed=8 * HEADS * patches * patches + 14 * patches * width,
            transcendentals=0,
        ),
        name="window",
    )(out_grads, queries, keys, values, probs, probs_t)


def body(llm_grads, token_target, patches, gain, w_down, queries, keys, values, window_ids):
    grad_rows = llm_grads[0]
    rows = grad_rows.shape[0]
    images, peers = lax.axis_size("img"), lax.axis_size("seq")
    image, me = lax.axis_index("img"), lax.axis_index("seq")
    capacity = max(1, 2 * rows // peers)
    slots = peers * capacity
    direct = peers <= DIRECT
    block = w_down.shape[1]
    width = patches.shape[2]

    def column_block(index):
        return lax.dynamic_slice(grad_rows, (0, index * block), (rows, block))

    x_blocks = [column_block(image)]
    x_blocks += [swap(column_block(image ^ j), "img", j) for j in range(1, images)]
    probs, probs_t = window_probs(queries[0], keys[0], window_ids[0])

    received, first = [], 0
    for index, count in enumerate(CHUNKS):
        terms, sums = project(x_blocks, w_down, first, count * width, index == 0)
        first += count * width
        if index == 0:
            bias_part = sums
        terms = [terms[0]] + [swap(terms[j], "img", j) for j in range(1, images)]
        packed = pack(terms, token_target, me.reshape(1), peers, capacity, direct, index == 0)
        received.append(route(packed, peers, capacity, direct))

    bias_block = sum_over(bias_part, "seq")
    bias_blocks = [bias_block] + [swap(bias_block, "img", j) for j in range(1, images)]
    bias_total = jnp.zeros((images, 1, block), F32)
    for j in range(images):
        bias_total = lax.dynamic_update_slice(bias_total, bias_blocks[j][None], (image ^ j, 0, 0))
    bias_total = bias_total.reshape(-1)

    out_grads, gain_part = norm_backward(received, CHUNKS, slots, patches[0], gain[None])
    gain_total = sum_over(sum_over(gain_part, "seq"), "img")[0]
    grads = window_backward(out_grads, queries[0], keys[0], values[0], probs, probs_t)
    devices = images * peers
    gain_grad = gain_total / math.sqrt(devices * patches.shape[1])
    bias_grad = bias_total / math.sqrt(devices * rows)
    return (grads[0][None], grads[1][None], grads[2][None], gain_grad, bias_grad)


def solution(mesh):
    return jax.shard_map(
        body,
        mesh=mesh,
        in_specs=(
            P("img", "seq", None),
            P("img", "seq"),
            P("img", "seq", None),
            P(),
            P(None, "img"),
            P("img", "seq", None),
            P("img", "seq", None),
            P("img", "seq", None),
            P("img", "seq", None),
        ),
        out_specs=(P("img", "seq", None), P("img", "seq", None), P("img", "seq", None), P(), P()),
        check_vma=False,
    )
```

time: 161 us -> 120 us (0.75)
  blocking collectives: 51.2 us -> 0 us
  starting transfers between devices: 10.9 us -> 55.5 us
  waiting for transfers between devices: 49.3 us -> 24.8 us
  Pallas kernels: 0 us -> 23 us
  matrix products: 22.6 us -> 0 us
  between operations: 14.3 us -> 0.87 us
  local copies, waits for them, and re-layouts: 8.4 us -> 13.2 us
  other arithmetic: 3.81 us -> 2.09 us
    ppermute x0 -> x43, starting transfers between devices: none -> 55.5 us  [swap(): return lax.ppermute(x, axis, [(i, i ^ mask) for i in range(n)])]
    psum x1 -> x0, blocking collectives: 39.7 us -> none  [body(): gain_total, bias_total = lax.psum((gain_part, bias_part), ('img', 'seq'))]
    all_to_all x2 -> x0, waiting for transfers between devices: 28.4 us -> none  [the longest x1 24.6 us: body(): lax.all_to_all(packed, 'seq', split_axis=0, concat_axis=0, tiled=True)]
    ppermute x0 -> x43, waiting for transfers between devices: none -> 24.8 us  [swap(): return lax.ppermute(x, axis, [(i, i ^ mask) for i in range(n)])]
    pallas_call x0 -> x7, Pallas kernels: none -> 23 us  [the longest x2 16.9 us: project(): pl.pallas_call(functools.partial(project_kernel, blocks, first, tile, til...]
    dot_general x8 -> x0, matrix products: 21.1 us -> none  [the longest x1 12.3 us: project_rows(): lax.dot_general(columns, w_down, (((1,), (1,)), ((), ())), preferred_elem...]
    reduce_scatter x1 -> x0, waiting for transfers between devices: 20.9 us -> none  [project_rows(): lax.psum_scatter(lax.dot_general(columns, w_down, (((1,), (1,)), ((), ())...]
    all_to_all x1 -> x0, blocking collectives: 11.6 us -> none  [project_rows(): lax.all_to_all(row_values, 'img', split_axis=1, concat_axis=0, tiled=True)]
  transfers between devices with their start and end apart: 3 -> 43, of which waited for: 3 -> 10; matrix products, arithmetic and copies ran while one was open for 4% -> 4% of each run, Pallas kernels for 0% -> 12%
where the time goes in v1:
time: 120 us
  starting transfers between devices  55.5 us (46%)
  waiting for transfers between devices  24.8 us (21%)
  Pallas kernels  23 us (19%)
  local copies, waits for them, and re-layouts  13.2 us (11%)
  other arithmetic  2.09 us (2%)
    ppermute x43, starting transfers between devices, swap(): return lax.ppermute(x, axis, [(i, i ^ mask) for i in range(n)])  55.5 us
    ppermute x43, waiting for transfers between devices, swap(): return lax.ppermute(x, axis, [(i, i ^ mask) for i in range(n)])  24.8 us
    pallas_call x2, Pallas kernels, project(): pl.pallas_call(functools.partial(project_kernel, blocks, first, tile, til...  16.9 us
    unnamed x38, local copies, waits for them, and re-layouts  8.18 us
    dynamic_update_slice x3, local copies, waits for them, and re-layouts, body(): lax.dynamic_update_slice(bias_total, bias_blocks[j][None], (image ^ j, 0,...  3.19 us
    pallas_call x1, Pallas kernels, window_backward(): pl.pallas_call(window_kernel, out_shape=[shape] * 3, in_specs=vmem(6), ou...  2.41 us
  transfers between devices with their start and end apart: 43, of which 10 were waited for; matrix products, arithmetic and copies ran while one was open for 4% of the time, Pallas kernels for 12%

profile of v1, /device:TPU:0, one launch (start us, length us, event | category | flops | bytes accessed | tf_op | source)
XLA Modules:
  0.0 119.6 jit_solution(16117867181957364412)
XLA Ops:
  0.7 1.1 dynamic-slice_bitcast_fusion
  2.3 2.6 %collective-permute-start.1 = (bf16[32,2048]{1,0:T(8,128)(2,1)S(1)}, bf16[32,2048]{1,0:T(8,128)(2,1)S(1)}, u32[]{:S(2)}, u32[]{:S(2)}) collective-permute-start(bf16[32,2048]{1,0:T(8,128)(2,1)S(1)} %get-tuple-element.74), channel_id=1, source_target_pairs={{0,16},{8,24},{16,0},{24,8},{1,17},{9,25},{17,1},{25,9},{2,18},{10... | collective-permute-start | bytes 393224 | tf_op jit(solution)/shard_map/ppermute | solution.py:36
  5.0 4.3 %collective-permute-done.1.refs_2_ = bf16[32,2048]{1,0:T(8,128)(2,1)S(1)} collective-permute-done((bf16[32,2048]{1,0:T(8,128)(2,1)S(1)}, bf16[32,2048]{1,0:T(8,128)(2,1)S(1)}, u32[]{:S(2)}, u32[]{:S(2)}) %collective-permute-start.1) | collective-permute-done | bytes 131104 | tf_op jit(solution)/shard_map/ppermute | solution.py:36
  9.3 2.3 %collective-permute-done.2.refs_3_ = bf16[32,2048]{1,0:T(8,128)(2,1)S(1)} collective-permute-done((bf16[32,2048]{1,0:T(8,128)(2,1)S(1)}, bf16[32,2048]{1,0:T(8,128)(2,1)S(1)}, u32[]{:S(2)}, u32[]{:S(2)}) %collective-permute-start.2) | collective-permute-done | bytes 131104 | tf_op jit(solution)/shard_map/ppermute | solution.py:36
  11.6 8.5 %project.3 = (bf16[32,2560]{1,0:T(8,128)(2,1)S(1)}, bf16[32,2560]{1,0:T(8,128)(2,1)S(1)}, bf16[32,2560]{1,0:T(8,128)(2,1)S(1)}, bf16[32,2560]{1,0:T(8,128)(2,1)S(1)}) custom-call(bf16[32,2048]{1,0:T(8,128)(2,1)S(1)} %get-tuple-element.73.refs_0_, bf16[32,2048]{1,0:T(8,128)(2,1)S(1)} %collective-permute-done.refs_1_, ...), custom_call_target="tpu_custom_call" | custom-call | flops 1342177280 | bytes 10485760 | tf_op jit(solution)/shard_map/project/pallas_call | solution.py:99
  20.3 8.5 %project.2 = (bf16[32,2560]{1,0:T(8,128)(2,1)S(1)}, bf16[32,2560]{1,0:T(8,128)(2,1)S(1)}, bf16[32,2560]{1,0:T(8,128)(2,1)S(1)}, bf16[32,2560]{1,0:T(8,128)(2,1)S(1)}, f32[1,2048]{1,0:T(1,128)S(1)}) custom-call(bf16[32,2048]{1,0:T(8,128)(2,1)S(1)} %get-tuple-element.73.refs_0_, bf16[32,2048]{1,0:T(8,128)(2,1)S(1)} %collective-permute-done.refs_1_, ...), custom_call_target="tpu_custom_call" | custom-call | flops 1342177280 | bytes 10485760 | tf_op jit(solution)/shard_map/project/pallas_call | solution.py:99
  28.8 0.7 copy-done.4
  29.4 3.8 %collective-permute-start.38 = (f32[1,2048]{1,0:T(1,128)S(1)}, f32[1,2048]{1,0:T(1,128)S(1)}, u32[]{:S(2)}, u32[]{:S(2)}) collective-permute-start(f32[1,2048]{1,0:T(1,128)S(1)} %get-tuple-element.68), channel_id=1, source_target_pairs={{0,6},{1,7},{2,4},{3,5},{4,2},{5,3},{6,0},{7,1},{8,14},{9,15},{10,... | collective-permute-start | bytes 24584 | tf_op jit(solution)/shard_map/ppermute | solution.py:36
  33.2 1.2 collective-permute-start.39
  34.4 0.8 collective-permute-start.36
  35.2 1.9 %collective-permute-start.37 = (f32[1,2048]{1,0:T(1,128)S(1)}, f32[1,2048]{1,0:T(1,128)S(1)}, u32[]{:S(2)}, u32[]{:S(2)}) collective-permute-start(f32[1,2048]{1,0:T(1,128)S(1)} %get-tuple-element.68), channel_id=1, source_target_pairs={{0,5},{1,4},{2,7},{3,6},{4,1},{5,0},{6,3},{7,2},{8,13},{9,12},{10,... | collective-permute-start | bytes 24584 | tf_op jit(solution)/shard_map/ppermute | solution.py:36
  37.1 1.4 %collective-permute-start.34 = (f32[1,2048]{1,0:T(1,128)S(1)}, f32[1,2048]{1,0:T(1,128)S(1)}, u32[]{:S(2)}, u32[]{:S(2)}) collective-permute-start(f32[1,2048]{1,0:T(1,128)S(1)} %get-tuple-element.68), channel_id=1, source_target_pairs={{0,2},{1,3},{2,0},{3,1},{4,6},{5,7},{6,4},{7,5},{8,10},{9,11},{10,... | collective-permute-start | bytes 24584 | tf_op jit(solution)/shard_map/ppermute | solution.py:36
  38.5 1.0 collective-permute-done.39
  39.6 0.7 collective-permute-start.35
  40.2 0.8 collective-permute-start.33
  41.1 1.6 %collective-permute-start.4 = (bf16[32,2560]{1,0:T(8,128)(2,1)S(1)}, bf16[32,2560]{1,0:T(8,128)(2,1)S(1)}, u32[]{:S(2)}, u32[]{:S(2)}) collective-permute-start(bf16[32,2560]{1,0:T(8,128)(2,1)S(1)} %get-tuple-element.39), channel_id=1, source_target_pairs={{0,16},{8,24},{16,0},{24,8},{1,17},{9,25},{17,1},{25,9},{2,18},{10... | collective-permute-start | bytes 491528 | tf_op jit(solution)/shard_map/ppermute | solution.py:36
  42.7 1.5 %collective-permute-done.35 = f32[1,2048]{1,0:T(1,128)S(1)} collective-permute-done((f32[1,2048]{1,0:T(1,128)S(1)}, f32[1,2048]{1,0:T(1,128)S(1)}, u32[]{:S(2)}, u32[]{:S(2)}) %collective-permute-start.35) | collective-permute-done | bytes 8224 | tf_op jit(solution)/shard_map/ppermute | solution.py:36
  44.1 1.5 %collective-permute-start.14 = (bf16[32,2560]{1,0:T(8,128)(2,1)S(1)}, bf16[32,2560]{1,0:T(8,128)(2,1)S(1)}, u32[]{:S(2)}, u32[]{:S(2)}) collective-permute-start(bf16[32,2560]{1,0:T(8,128)(2,1)S(1)} %get-tuple-element.51), channel_id=1, source_target_pairs={{0,16},{8,24},{16,0},{24,8},{1,17},{9,25},{17,1},{25,9},{2,18},{10... | collective-permute-start | bytes 491528 | tf_op jit(solution)/shard_map/ppermute | solution.py:36
  45.7 1.4 %collective-permute-start.15 = (bf16[32,2560]{1,0:T(8,128)(2,1)S(1)}, bf16[32,2560]{1,0:T(8,128)(2,1)S(1)}, u32[]{:S(2)}, u32[]{:S(2)}) collective-permute-start(bf16[32,2560]{1,0:T(8,128)(2,1)S(1)} %get-tuple-element.52), channel_id=1, source_target_pairs={{0,24},{8,16},{16,8},{24,0},{1,25},{9,17},{17,9},{25,1},{2,26},{10... | collective-permute-start | bytes 491528 | tf_op jit(solution)/shard_map/ppermute | solution.py:36
  47.2 8.0 %collective-permute-done.14.refs_2_ = bf16[32,2560]{1,0:T(8,128)(2,1)S(1)} collective-permute-done((bf16[32,2560]{1,0:T(8,128)(2,1)S(1)}, bf16[32,2560]{1,0:T(8,128)(2,1)S(1)}, u32[]{:S(2)}, u32[]{:S(2)}) %collective-permute-start.14) | collective-permute-done | bytes 163872 | tf_op jit(solution)/shard_map/ppermute | solution.py:36
  55.2 2.6 %collective-permute-done.15.refs_3_ = bf16[32,2560]{1,0:T(8,128)(2,1)S(1)} collective-permute-done((bf16[32,2560]{1,0:T(8,128)(2,1)S(1)}, bf16[32,2560]{1,0:T(8,128)(2,1)S(1)}, u32[]{:S(2)}, u32[]{:S(2)}) %collective-permute-start.15) | collective-permute-done | bytes 163872 | tf_op jit(solution)/shard_map/ppermute | solution.py:36
  57.8 1.0 pack.3
  58.7 0.6 copy-done.13
  59.3 0.6 copy-done.14
  60.0 0.6 copy-done.15
  60.6 1.4 %collective-permute-start.16 = (bf16[8,2560]{1,0:T(8,128)(2,1)}, bf16[8,2560]{1,0:T(8,128)(2,1)S(1)}, u32[]{:S(2)}, u32[]{:S(2)}) collective-permute-start(bf16[8,2560]{1,0:T(8,128)(2,1)} %get-tuple-element.54), channel_id=1, source_target_pairs={{0,1},{1,0},{2,3},{3,2},{4,5},{5,4},{6,7},{7,6},{8,9},{9,8},{10,11... | collective-permute-start | bytes 122888 | tf_op jit(solution)/shard_map/ppermute | solution.py:36
  62.0 2.0 %collective-permute-start.17 = (bf16[8,2560]{1,0:T(8,128)(2,1)}, bf16[8,2560]{1,0:T(8,128)(2,1)S(1)}, u32[]{:S(2)}, u32[]{:S(2)}) collective-permute-start(bf16[8,2560]{1,0:T(8,128)(2,1)} %get-tuple-element.55), channel_id=1, source_target_pairs={{0,2},{1,3},{2,0},{3,1},{4,6},{5,7},{6,4},{7,5},{8,10},{9,11},{10,... | collective-permute-start | bytes 122888 | tf_op jit(solution)/shard_map/ppermute | solution.py:36
  64.1 0.7 copy-done.6
  64.7 1.0 collective-permute-start.18
  65.7 0.7 copy-done.8
  66.4 0.9 collective-permute-start.19
  67.3 0.7 copy-done.10
  67.9 1.5 %collective-permute-start.41 = (f32[1,2048]{1,0:T(1,128)S(1)}, f32[1,2048]{1,0:T(1,128)}, u32[]{:S(2)}, u32[]{:S(2)}) collective-permute-start(f32[1,2048]{1,0:T(1,128)S(1)} %get-tuple-element.70), channel_id=1, source_target_pairs={{0,16},{8,24},{16,0},{24,8},{1,17},{9,25},{17,1},{25,9},{2,18},{10... | collective-permute-start | bytes 24584 | tf_op jit(solution)/shard_map/ppermute | solution.py:36
  69.5 1.1 probs.1
  70.5 0.7 broadcast_in_dim.27.gain_ref
  71.3 0.9 copy-done.5
  72.2 0.9 copy-done.7
  73.1 0.9 copy-done.9
  74.0 0.9 copy-done.11
  75.3 1.5 %collective-permute-start.6 = (bf16[8,2688]{1,0:T(8,128)(2,1)S(1)}, bf16[8,2688]{1,0:T(8,128)(2,1)S(1)}, u32[]{:S(2)}, u32[]{:S(2)}) collective-permute-start(bf16[8,2688]{1,0:T(8,128)(2,1)S(1)} %get-tuple-element.42), channel_id=1, source_target_pairs={{0,1},{1,0},{2,3},{3,2},{4,5},{5,4},{6,7},{7,6},{8,9},{9,8},{10,11... | collective-permute-start | bytes 129032 | tf_op jit(solution)/shard_map/ppermute | solution.py:36
  76.8 2.0 %collective-permute-start.7 = (bf16[8,2688]{1,0:T(8,128)(2,1)S(1)}, bf16[8,2688]{1,0:T(8,128)(2,1)S(1)}, u32[]{:S(2)}, u32[]{:S(2)}) collective-permute-start(bf16[8,2688]{1,0:T(8,128)(2,1)S(1)} %get-tuple-element.43), channel_id=1, source_target_pairs={{0,2},{1,3},{2,0},{3,1},{4,6},{5,7},{6,4},{7,5},{8,10},{9,11},{10,... | collective-permute-start | bytes 129032 | tf_op jit(solution)/shard_map/ppermute | solution.py:36
  78.7 2.1 %collective-permute-start.20 = (bf16[8,2560]{1,0:T(8,128)(2,1)}, bf16[8,2560]{1,0:T(8,128)(2,1)S(1)}, u32[]{:S(2)}, u32[]{:S(2)}) collective-permute-start(bf16[8,2560]{1,0:T(8,128)(2,1)} %copy-done.15), channel_id=1, source_target_pairs={{0,5},{1,4},{2,7},{3,6},{4,1},{5,0},{6,3},{7,2},{8,13},{9,12},{10,... | collective-permute-start | bytes 122888 | tf_op jit(solution)/shard_map/ppermute | solution.py:36
  81.2 3.4 %collective-permute-start.22 = (bf16[8,2560]{1,0:T(8,128)(2,1)}, bf16[8,2560]{1,0:T(8,128)(2,1)S(1)}, u32[]{:S(2)}, u32[]{:S(2)}) collective-permute-start(bf16[8,2560]{1,0:T(8,128)(2,1)} %copy-done.13), channel_id=1, source_target_pairs={{0,7},{1,6},{2,5},{3,4},{4,3},{5,2},{6,1},{7,0},{8,15},{9,14},{10,... | collective-permute-start | bytes 122888 | tf_op jit(solution)/shard_map/ppermute | solution.py:36
  84.6 1.3 %bitcast_dynamic-update-slice_fusion.2 = f32[4,1,2048]{2,1,0:T(1,128)} fusion(f32[4,1,2048]{2,1,0:T(1,128)} %copy-done.17, s32[]{:T(128)S(6)} %select_n.29, f32[1,2048]{1,0:T(1,128)} %copy-done.18), kind=kLoop, calls=%fused_computation.7 | loop fusion | bytes 16388 | tf_op jit(solution)/shard_map/dynamic_update_slice | solution.py:370
  85.9 1.2 %collective-permute-done.21.refs_14_ = bf16[8,2560]{1,0:T(8,128)(2,1)S(1)} collective-permute-done((bf16[8,2560]{1,0:T(8,128)(2,1)}, bf16[8,2560]{1,0:T(8,128)(2,1)S(1)}, u32[]{:S(2)}, u32[]{:S(2)}) %collective-permute-start.21) | collective-permute-done | bytes 40992 | tf_op jit(solution)/shard_map/ppermute | solution.py:36
  87.1 0.7 collective-permute-start.9
  88.1 2.0 %collective-permute-start.10 = (bf16[8,2688]{1,0:T(8,128)(2,1)S(1)}, bf16[8,2688]{1,0:T(8,128)(2,1)S(1)}, u32[]{:S(2)}, u32[]{:S(2)}) collective-permute-start(bf16[8,2688]{1,0:T(8,128)(2,1)S(1)} %get-tuple-element.46), channel_id=1, source_target_pairs={{0,5},{1,4},{2,7},{3,6},{4,1},{5,0},{6,3},{7,2},{8,13},{9,12},{10,... | collective-permute-start | bytes 129032 | tf_op jit(solution)/shard_map/ppermute | solution.py:36
  90.1 1.5 %collective-permute-start.11 = (bf16[8,2688]{1,0:T(8,128)(2,1)S(1)}, bf16[8,2688]{1,0:T(8,128)(2,1)S(1)}, u32[]{:S(2)}, u32[]{:S(2)}) collective-permute-start(bf16[8,2688]{1,0:T(8,128)(2,1)S(1)} %get-tuple-element.47), channel_id=1, source_target_pairs={{0,6},{1,7},{2,4},{3,5},{4,2},{5,3},{6,0},{7,1},{8,14},{9,15},{10,... | collective-permute-start | bytes 129032 | tf_op jit(solution)/shard_map/ppermute | solution.py:36
  91.6 3.2 %collective-permute-start.12 = (bf16[8,2688]{1,0:T(8,128)(2,1)S(1)}, bf16[8,2688]{1,0:T(8,128)(2,1)S(1)}, u32[]{:S(2)}, u32[]{:S(2)}) collective-permute-start(bf16[8,2688]{1,0:T(8,128)(2,1)S(1)} %get-tuple-element.48), channel_id=1, source_target_pairs={{0,7},{1,6},{2,5},{3,4},{4,3},{5,2},{6,1},{7,0},{8,15},{9,14},{10,... | collective-permute-start | bytes 129032 | tf_op jit(solution)/shard_map/ppermute | solution.py:36
  94.8 1.3 %bitcast_dynamic-update-slice_fusion.1 = f32[4,1,2048]{2,1,0:T(1,128)} fusion(f32[4,1,2048]{2,1,0:T(1,128)} %bitcast_dynamic-update-slice_fusion.2, s32[]{:T(128)S(6)} %select_n.30, f32[1,2048]{1,0:T(1,128)} %collective-permute-done.41), kind=kLoop, calls=%fused_computation.6 | loop fusion | bytes 16388 | tf_op jit(solution)/shard_map/dynamic_update_slice | solution.py:370
  96.1 2.2 %collective-permute-done.12.refs_7_ = bf16[8,2688]{1,0:T(8,128)(2,1)S(1)} collective-permute-done((bf16[8,2688]{1,0:T(8,128)(2,1)S(1)}, bf16[8,2688]{1,0:T(8,128)(2,1)S(1)}, u32[]{:S(2)}, u32[]{:S(2)}) %collective-permute-start.12) | collective-permute-done | bytes 43040 | tf_op jit(solution)/shard_map/ppermute | solution.py:36
  98.3 1.3 %norm.1 = (bf16[128,1280]{1,0:T(8,128)(2,1)S(1)}, f32[1,1280]{1,0:T(1,128)S(1)}) custom-call(bf16[128,1280]{1,0:T(8,128)(2,1)S(1)} %bitcast.26, f32[1,1280]{1,0:T(1,128)S(1)} %broadcast_in_dim.27.gain_ref, bf16[8,2688]{1,0:T(8,128)(2,1)S(1)} %get-tuple-element.41.refs_0_, bf16[8,2688]{1,0:T(8,128)(2,1)S(1)} %collective-permute-done.6.refs_1_, ...), custom_call_target="tpu_custom_call" | custom-call | flops 83886080 | bytes 1310720 | tf_op jit(solution)/shard_map/norm/pallas_call | solution.py:264
  99.7 2.4 %collective-permute-start.28 = (f32[1,1280]{1,0:T(1,128)S(1)}, f32[1,1280]{1,0:T(1,128)S(1)}, u32[]{:S(2)}, u32[]{:S(2)}) collective-permute-start(f32[1,1280]{1,0:T(1,128)S(1)} %get-tuple-element.67), channel_id=1, source_target_pairs={{0,6},{1,7},{2,4},{3,5},{4,2},{5,3},{6,0},{7,1},{8,14},{9,15},{10,... | collective-permute-start | bytes 15368 | tf_op jit(solution)/shard_map/ppermute | solution.py:36
  102.1 2.1 %collective-permute-start.29 = (f32[1,1280]{1,0:T(1,128)S(1)}, f32[1,1280]{1,0:T(1,128)S(1)}, u32[]{:S(2)}, u32[]{:S(2)}) collective-permute-start(f32[1,1280]{1,0:T(1,128)S(1)} %get-tuple-element.67), channel_id=1, source_target_pairs={{0,7},{1,6},{2,5},{3,4},{4,3},{5,2},{6,1},{7,0},{8,15},{9,14},{10,... | collective-permute-start | bytes 15368 | tf_op jit(solution)/shard_map/ppermute | solution.py:36
  104.2 0.6 bitcast_dynamic-update-slice_fusion
  104.8 3.2 %collective-permute-start.27 = (f32[1,1280]{1,0:T(1,128)S(1)}, f32[1,1280]{1,0:T(1,128)S(1)}, u32[]{:S(2)}, u32[]{:S(2)}) collective-permute-start(f32[1,1280]{1,0:T(1,128)S(1)} %get-tuple-element.67), channel_id=1, source_target_pairs={{0,5},{1,4},{2,7},{3,6},{4,1},{5,0},{6,3},{7,2},{8,13},{9,12},{10,... | collective-permute-start | bytes 15368 | tf_op jit(solution)/shard_map/ppermute | solution.py:36
  108.0 2.7 %collective-permute-start.25 = (f32[1,1280]{1,0:T(1,128)S(1)}, f32[1,1280]{1,0:T(1,128)S(1)}, u32[]{:S(2)}, u32[]{:S(2)}) collective-permute-start(f32[1,1280]{1,0:T(1,128)S(1)} %get-tuple-element.67), channel_id=1, source_target_pairs={{0,3},{1,2},{2,1},{3,0},{4,7},{5,6},{6,5},{7,4},{8,11},{9,10},{10,... | collective-permute-start | bytes 15368 | tf_op jit(solution)/shard_map/ppermute | solution.py:36
  110.7 0.8 collective-permute-start.23
  111.5 1.4 %broadcast_multiply_fusion = f32[4,1,2048]{2,1,0:T(1,128)} fusion(f32[4,1,2048]{2,1,0:T(1,128)} %bitcast_dynamic-update-slice_fusion), kind=kLoop, calls=%fused_computation.4 | loop fusion | flops 8192 | bytes 65536 | tf_op jit(solution)/shard_map/div | solution.py:378
  112.9 1.4 %collective-permute-done.23 = f32[1,1280]{1,0:T(1,128)S(1)} collective-permute-done((f32[1,1280]{1,0:T(1,128)S(1)}, f32[1,1280]{1,0:T(1,128)S(1)}, u32[]{:S(2)}, u32[]{:S(2)}) %collective-permute-start.23) | collective-permute-done | bytes 5152 | tf_op jit(solution)/shard_map/ppermute | solution.py:36
  114.3 0.6 collective-permute-start.31
  114.9 1.6 %collective-permute-start.30 = (f32[1,1280]{1,0:T(1,128)S(1)}, f32[1,1280]{1,0:T(1,128)S(1)}, u32[]{:S(2)}, u32[]{:S(2)}) collective-permute-start(f32[1,1280]{1,0:T(1,128)S(1)} %add_add_fusion.1), channel_id=1, source_target_pairs={{0,8},{8,0},{16,24},{24,16},{1,9},{9,1},{17,25},{25,17},{2,10},{10... | collective-permute-start | bytes 15368 | tf_op jit(solution)/shard_map/ppermute | solution.py:36
  116.5 2.4 %window.1 = (bf16[128,1280]{1,0:T(8,128)(2,1)}, bf16[128,1280]{1,0:T(8,128)(2,1)}, bf16[128,1280]{1,0:T(8,128)(2,1)}) custom-call(bf16[128,1280]{1,0:T(8,128)(2,1)S(1)} %get-tuple-element.61.g_ref, bf16[128,1280]{1,0:T(8,128)(2,1)S(1)} %bitcast.28, bf16[128,1280]{1,0:T(8,128)(2,1)S(1)} %bitcast.30, bf16[128,1280]{1,0:T(8,128)(2,1)S(1)} %bitcast.31, ...), custom_call_target="tpu_custom_call" | custom-call | flops 335544320 | bytes 4390912 | tf_op jit(solution)/shard_map/window/pallas_call | solution.py:323
  118.9 0.6 multiply_reduce_fusion
  (77 shorter events, 2.0 us)
Async XLA Ops:
  1.8 3.2 %collective-permute-start = (bf16[32,2048]{1,0:T(8,128)(2,1)S(1)}, bf16[32,2048]{1,0:T(8,128)(2,1)S(1)}, u32[]{:S(2)}, u32[]{:S(2)}) collective-permute-start(bf16[32,2048]{1,0:T(8,128)(2,1)S(1)} %get-tuple-element.72), channel_id=1, source_target_pairs={{0,8},{8,0},{16,24},{24,16},{1,9},{9,1},{17,25},{25,17},{2,10},{10... | collective-permute-start | bytes 393224 | tf_op jit(solution)/shard_map/ppermute | solution.py:36
  2.3 6.9 %collective-permute-start.1 = (bf16[32,2048]{1,0:T(8,128)(2,1)S(1)}, bf16[32,2048]{1,0:T(8,128)(2,1)S(1)}, u32[]{:S(2)}, u32[]{:S(2)}) collective-permute-start(bf16[32,2048]{1,0:T(8,128)(2,1)S(1)} %get-tuple-element.74), channel_id=1, source_target_pairs={{0,16},{8,24},{16,0},{24,8},{1,17},{9,25},{17,1},{25,9},{2,18},{10... | collective-permute-start | bytes 393224 | tf_op jit(solution)/shard_map/ppermute | solution.py:36
  4.9 6.6 %collective-permute-start.2 = (bf16[32,2048]{1,0:T(8,128)(2,1)S(1)}, bf16[32,2048]{1,0:T(8,128)(2,1)S(1)}, u32[]{:S(2)}, u32[]{:S(2)}) collective-permute-start(bf16[32,2048]{1,0:T(8,128)(2,1)S(1)} %get-tuple-element.71), channel_id=1, source_target_pairs={{0,24},{8,16},{16,8},{24,0},{1,25},{9,17},{17,9},{25,1},{2,26},{10... | collective-permute-start | bytes 393224 | tf_op jit(solution)/shard_map/ppermute | solution.py:36
  11.6 46.2 %copy-start.12 = (s32[1,32]{1,0:T(1,128)S(1)}, s32[1,32]{1,0:T(1,128)}, u32[]{:S(2)}) copy-start(s32[1,32]{1,0:T(1,128)} %targets_ref.3) | copy-start | bytes 388
  11.6 57.9 %copy-start.1 = (bf16[1,128,1280]{2,1,0:T(8,128)(2,1)S(1)}, bf16[1,128,1280]{2,1,0:T(8,128)(2,1)}, u32[]{:S(2)}) copy-start(bf16[1,128,1280]{2,1,0:T(8,128)(2,1)} %param.14) | copy-start | bytes 983044
  11.6 57.9 %copy-start.2 = (bf16[1,128,1280]{2,1,0:T(8,128)(2,1)S(1)}, bf16[1,128,1280]{2,1,0:T(8,128)(2,1)}, u32[]{:S(2)}) copy-start(bf16[1,128,1280]{2,1,0:T(8,128)(2,1)} %param.15) | copy-start | bytes 983044
  11.6 57.9 %copy-start.16 = (s32[1,1,32]{2,1,0:T(1,128)S(1)}, s32[1,1,32]{2,1,0:T(1,128)}, u32[]{:S(2)}) copy-start(s32[1,1,32]{2,1,0:T(1,128)} %param.17) | copy-start | bytes 388
  11.6 86.8 %copy-start = (bf16[1,128,1280]{2,1,0:T(8,128)(2,1)S(1)}, bf16[1,128,1280]{2,1,0:T(8,128)(2,1)}, u32[]{:S(2)}) copy-start(bf16[1,128,1280]{2,1,0:T(8,128)(2,1)} %param.11) | copy-start | bytes 983044
  11.6 104.9 %copy-start.3 = (bf16[1,128,1280]{2,1,0:T(8,128)(2,1)S(1)}, bf16[1,128,1280]{2,1,0:T(8,128)(2,1)}, u32[]{:S(2)}) copy-start(bf16[1,128,1280]{2,1,0:T(8,128)(2,1)} %param.16) | copy-start | bytes 983044
  20.1 25.6 %collective-permute-start.13 = (bf16[32,2560]{1,0:T(8,128)(2,1)S(1)}, bf16[32,2560]{1,0:T(8,128)(2,1)S(1)}, u32[]{:S(2)}, u32[]{:S(2)}) collective-permute-start(bf16[32,2560]{1,0:T(8,128)(2,1)S(1)} %get-tuple-element.50), channel_id=1, source_target_pairs={{0,8},{8,0},{16,24},{24,16},{1,9},{9,1},{17,25},{25,17},{2,10},{10... | collective-permute-start | bytes 491528 | tf_op jit(solution)/shard_map/ppermute | solution.py:36
  28.7 0.7 copy-start.4
  29.4 7.7 %collective-permute-start.38 = (f32[1,2048]{1,0:T(1,128)S(1)}, f32[1,2048]{1,0:T(1,128)S(1)}, u32[]{:S(2)}, u32[]{:S(2)}) collective-permute-start(f32[1,2048]{1,0:T(1,128)S(1)} %get-tuple-element.68), channel_id=1, source_target_pairs={{0,6},{1,7},{2,4},{3,5},{4,2},{5,3},{6,0},{7,1},{8,14},{9,15},{10,... | collective-permute-start | bytes 24584 | tf_op jit(solution)/shard_map/ppermute | solution.py:36
  33.2 6.3 %collective-permute-start.39 = (f32[1,2048]{1,0:T(1,128)S(1)}, f32[1,2048]{1,0:T(1,128)S(1)}, u32[]{:S(2)}, u32[]{:S(2)}) collective-permute-start(f32[1,2048]{1,0:T(1,128)S(1)} %get-tuple-element.68), channel_id=1, source_target_pairs={{0,7},{1,6},{2,5},{3,4},{4,3},{5,2},{6,1},{7,0},{8,15},{9,14},{10,... | collective-permute-start | bytes 24584 | tf_op jit(solution)/shard_map/ppermute | solution.py:36
  34.4 5.9 %collective-permute-start.36 = (f32[1,2048]{1,0:T(1,128)S(1)}, f32[1,2048]{1,0:T(1,128)S(1)}, u32[]{:S(2)}, u32[]{:S(2)}) collective-permute-start(f32[1,2048]{1,0:T(1,128)S(1)} %get-tuple-element.68), channel_id=1, source_target_pairs={{0,4},{1,5},{2,6},{3,7},{4,0},{5,1},{6,2},{7,3},{8,12},{9,13},{10,... | collective-permute-start | bytes 24584 | tf_op jit(solution)/shard_map/ppermute | solution.py:36
  35.2 5.9 %collective-permute-start.37 = (f32[1,2048]{1,0:T(1,128)S(1)}, f32[1,2048]{1,0:T(1,128)S(1)}, u32[]{:S(2)}, u32[]{:S(2)}) collective-permute-start(f32[1,2048]{1,0:T(1,128)S(1)} %get-tuple-element.68), channel_id=1, source_target_pairs={{0,5},{1,4},{2,7},{3,6},{4,1},{5,0},{6,3},{7,2},{8,13},{9,12},{10,... | collective-permute-start | bytes 24584 | tf_op jit(solution)/shard_map/ppermute | solution.py:36
  37.1 4.0 %collective-permute-start.34 = (f32[1,2048]{1,0:T(1,128)S(1)}, f32[1,2048]{1,0:T(1,128)S(1)}, u32[]{:S(2)}, u32[]{:S(2)}) collective-permute-start(f32[1,2048]{1,0:T(1,128)S(1)} %get-tuple-element.68), channel_id=1, source_target_pairs={{0,2},{1,3},{2,0},{3,1},{4,6},{5,7},{6,4},{7,5},{8,10},{9,11},{10,... | collective-permute-start | bytes 24584 | tf_op jit(solution)/shard_map/ppermute | solution.py:36
  39.6 4.5 %collective-permute-start.35 = (f32[1,2048]{1,0:T(1,128)S(1)}, f32[1,2048]{1,0:T(1,128)S(1)}, u32[]{:S(2)}, u32[]{:S(2)}) collective-permute-start(f32[1,2048]{1,0:T(1,128)S(1)} %get-tuple-element.68), channel_id=1, source_target_pairs={{0,3},{1,2},{2,1},{3,0},{4,7},{5,6},{6,5},{7,4},{8,11},{9,10},{10,... | collective-permute-start | bytes 24584 | tf_op jit(solution)/shard_map/ppermute | solution.py:36
  40.2 3.9 %collective-permute-start.33 = (f32[1,2048]{1,0:T(1,128)S(1)}, f32[1,2048]{1,0:T(1,128)S(1)}, u32[]{:S(2)}, u32[]{:S(2)}) collective-permute-start(f32[1,2048]{1,0:T(1,128)S(1)} %get-tuple-element.68), channel_id=1, source_target_pairs={{0,1},{1,0},{2,3},{3,2},{4,5},{5,4},{6,7},{7,6},{8,9},{9,8},{10,11... | collective-permute-start | bytes 24584 | tf_op jit(solution)/shard_map/ppermute | solution.py:36
  41.1 23.0 %collective-permute-start.3 = (bf16[32,2560]{1,0:T(8,128)(2,1)S(1)}, bf16[32,2560]{1,0:T(8,128)(2,1)S(1)}, u32[]{:S(2)}, u32[]{:S(2)}) collective-permute-start(bf16[32,2560]{1,0:T(8,128)(2,1)S(1)} %get-tuple-element.38), channel_id=1, source_target_pairs={{0,8},{8,0},{16,24},{24,16},{1,9},{9,1},{17,25},{25,17},{2,10},{10... | collective-permute-start | bytes 491528 | tf_op jit(solution)/shard_map/ppermute | solution.py:36
  41.1 24.6 %collective-permute-start.4 = (bf16[32,2560]{1,0:T(8,128)(2,1)S(1)}, bf16[32,2560]{1,0:T(8,128)(2,1)S(1)}, u32[]{:S(2)}, u32[]{:S(2)}) collective-permute-start(bf16[32,2560]{1,0:T(8,128)(2,1)S(1)} %get-tuple-element.39), channel_id=1, source_target_pairs={{0,16},{8,24},{16,0},{24,8},{1,17},{9,25},{17,1},{25,9},{2,18},{10... | collective-permute-start | bytes 491528 | tf_op jit(solution)/shard_map/ppermute | solution.py:36
  44.1 23.2 %collective-permute-start.5 = (bf16[32,2560]{1,0:T(8,128)(2,1)S(1)}, bf16[32,2560]{1,0:T(8,128)(2,1)S(1)}, u32[]{:S(2)}, u32[]{:S(2)}) collective-permute-start(bf16[32,2560]{1,0:T(8,128)(2,1)S(1)} %get-tuple-element.40), channel_id=1, source_target_pairs={{0,24},{8,16},{16,8},{24,0},{1,25},{9,17},{17,9},{25,1},{2,26},{10... | collective-permute-start | bytes 491528 | tf_op jit(solution)/shard_map/ppermute | solution.py:36
  44.1 11.0 %collective-permute-start.14 = (bf16[32,2560]{1,0:T(8,128)(2,1)S(1)}, bf16[32,2560]{1,0:T(8,128)(2,1)S(1)}, u32[]{:S(2)}, u32[]{:S(2)}) collective-permute-start(bf16[32,2560]{1,0:T(8,128)(2,1)S(1)} %get-tuple-element.51), channel_id=1, source_target_pairs={{0,16},{8,24},{16,0},{24,8},{1,17},{9,25},{17,1},{25,9},{2,18},{10... | collective-permute-start | bytes 491528 | tf_op jit(solution)/shard_map/ppermute | solution.py:36
  45.7 12.1 %collective-permute-start.15 = (bf16[32,2560]{1,0:T(8,128)(2,1)S(1)}, bf16[32,2560]{1,0:T(8,128)(2,1)S(1)}, u32[]{:S(2)}, u32[]{:S(2)}) collective-permute-start(bf16[32,2560]{1,0:T(8,128)(2,1)S(1)} %get-tuple-element.52), channel_id=1, source_target_pairs={{0,24},{8,16},{16,8},{24,0},{1,25},{9,17},{17,9},{25,1},{2,26},{10... | collective-permute-start | bytes 491528 | tf_op jit(solution)/shard_map/ppermute | solution.py:36
  47.2 10.6 %copy-start.17 = (f32[4,1,2048]{2,1,0:T(1,128)}, f32[4,1,2048]{2,1,0:T(1,128)S(1)}, u32[]{:S(2)}) copy-start(f32[4,1,2048]{2,1,0:T(1,128)S(1)} %get-tuple-element.69) | copy-start | bytes 98308
  55.2 6.8 %collective-permute-start.40 = (f32[1,2048]{1,0:T(1,128)S(1)}, f32[1,2048]{1,0:T(1,128)S(1)}, u32[]{:S(2)}, u32[]{:S(2)}) collective-permute-start(f32[1,2048]{1,0:T(1,128)S(1)} %get-tuple-element.70), channel_id=1, source_target_pairs={{0,8},{8,0},{16,24},{24,16},{1,9},{9,1},{17,25},{25,17},{2,10},{10... | collective-permute-start | bytes 24584 | tf_op jit(solution)/shard_map/ppermute | solution.py:36
  58.7 0.6 copy-start.13
  59.3 0.6 copy-start.14
  60.0 0.6 copy-start.15
  60.6 16.2 %collective-permute-start.16 = (bf16[8,2560]{1,0:T(8,128)(2,1)}, bf16[8,2560]{1,0:T(8,128)(2,1)S(1)}, u32[]{:S(2)}, u32[]{:S(2)}) collective-permute-start(bf16[8,2560]{1,0:T(8,128)(2,1)} %get-tuple-element.54), channel_id=1, source_target_pairs={{0,1},{1,0},{2,3},{3,2},{4,5},{5,4},{6,7},{7,6},{8,9},{9,8},{10,11... | collective-permute-start | bytes 122888 | tf_op jit(solution)/shard_map/ppermute | solution.py:36
  62.0 7.4 %copy-start.18 = (f32[1,2048]{1,0:T(1,128)}, f32[1,2048]{1,0:T(1,128)S(1)}, u32[]{:S(2)}) copy-start(f32[1,2048]{1,0:T(1,128)S(1)} %collective-permute-done.40) | copy-start | bytes 24580
  62.0 16.7 %collective-permute-start.17 = (bf16[8,2560]{1,0:T(8,128)(2,1)}, bf16[8,2560]{1,0:T(8,128)(2,1)S(1)}, u32[]{:S(2)}, u32[]{:S(2)}) collective-permute-start(bf16[8,2560]{1,0:T(8,128)(2,1)} %get-tuple-element.55), channel_id=1, source_target_pairs={{0,2},{1,3},{2,0},{3,1},{4,6},{5,7},{6,4},{7,5},{8,10},{9,11},{10,... | collective-permute-start | bytes 122888 | tf_op jit(solution)/shard_map/ppermute | solution.py:36
  64.1 0.7 copy-start.6
  64.7 16.1 %collective-permute-start.18 = (bf16[8,2560]{1,0:T(8,128)(2,1)}, bf16[8,2560]{1,0:T(8,128)(2,1)}, u32[]{:S(2)}, u32[]{:S(2)}) collective-permute-start(bf16[8,2560]{1,0:T(8,128)(2,1)} %get-tuple-element.56), channel_id=1, source_target_pairs={{0,3},{1,2},{2,1},{3,0},{4,7},{5,6},{6,5},{7,4},{8,11},{9,10},{10,... | collective-permute-start | bytes 122888 | tf_op jit(solution)/shard_map/ppermute | solution.py:36
  65.7 0.7 copy-start.8
  66.4 14.8 %collective-permute-start.19 = (bf16[8,2560]{1,0:T(8,128)(2,1)}, bf16[8,2560]{1,0:T(8,128)(2,1)}, u32[]{:S(2)}, u32[]{:S(2)}) collective-permute-start(bf16[8,2560]{1,0:T(8,128)(2,1)} %get-tuple-element.57), channel_id=1, source_target_pairs={{0,4},{1,5},{2,6},{3,7},{4,0},{5,1},{6,2},{7,3},{8,12},{9,13},{10,... | collective-permute-start | bytes 122888 | tf_op jit(solution)/shard_map/ppermute | solution.py:36
  67.3 0.7 copy-start.10
  67.9 7.3 %collective-permute-start.41 = (f32[1,2048]{1,0:T(1,128)S(1)}, f32[1,2048]{1,0:T(1,128)}, u32[]{:S(2)}, u32[]{:S(2)}) collective-permute-start(f32[1,2048]{1,0:T(1,128)S(1)} %get-tuple-element.70), channel_id=1, source_target_pairs={{0,16},{8,24},{16,0},{24,8},{1,17},{9,25},{17,1},{25,9},{2,18},{10... | collective-permute-start | bytes 24584 | tf_op jit(solution)/shard_map/ppermute | solution.py:36
  71.3 0.9 copy-start.5
  72.2 0.9 copy-start.7
  73.1 0.9 copy-start.9
  74.0 0.9 copy-start.11
  75.3 14.9 %collective-permute-start.6 = (bf16[8,2688]{1,0:T(8,128)(2,1)S(1)}, bf16[8,2688]{1,0:T(8,128)(2,1)S(1)}, u32[]{:S(2)}, u32[]{:S(2)}) collective-permute-start(bf16[8,2688]{1,0:T(8,128)(2,1)S(1)} %get-tuple-element.42), channel_id=1, source_target_pairs={{0,1},{1,0},{2,3},{3,2},{4,5},{5,4},{6,7},{7,6},{8,9},{9,8},{10,11... | collective-permute-start | bytes 129032 | tf_op jit(solution)/shard_map/ppermute | solution.py:36
  76.8 14.8 %collective-permute-start.7 = (bf16[8,2688]{1,0:T(8,128)(2,1)S(1)}, bf16[8,2688]{1,0:T(8,128)(2,1)S(1)}, u32[]{:S(2)}, u32[]{:S(2)}) collective-permute-start(bf16[8,2688]{1,0:T(8,128)(2,1)S(1)} %get-tuple-element.43), channel_id=1, source_target_pairs={{0,2},{1,3},{2,0},{3,1},{4,6},{5,7},{6,4},{7,5},{8,10},{9,11},{10,... | collective-permute-start | bytes 129032 | tf_op jit(solution)/shard_map/ppermute | solution.py:36
  78.7 7.2 %collective-permute-start.20 = (bf16[8,2560]{1,0:T(8,128)(2,1)}, bf16[8,2560]{1,0:T(8,128)(2,1)S(1)}, u32[]{:S(2)}, u32[]{:S(2)}) collective-permute-start(bf16[8,2560]{1,0:T(8,128)(2,1)} %copy-done.15), channel_id=1, source_target_pairs={{0,5},{1,4},{2,7},{3,6},{4,1},{5,0},{6,3},{7,2},{8,13},{9,12},{10,... | collective-permute-start | bytes 122888 | tf_op jit(solution)/shard_map/ppermute | solution.py:36
  80.8 6.3 %collective-permute-start.21 = (bf16[8,2560]{1,0:T(8,128)(2,1)}, bf16[8,2560]{1,0:T(8,128)(2,1)S(1)}, u32[]{:S(2)}, u32[]{:S(2)}) collective-permute-start(bf16[8,2560]{1,0:T(8,128)(2,1)} %copy-done.14), channel_id=1, source_target_pairs={{0,6},{1,7},{2,4},{3,5},{4,2},{5,3},{6,0},{7,1},{8,14},{9,15},{10,... | collective-permute-start | bytes 122888 | tf_op jit(solution)/shard_map/ppermute | solution.py:36
  81.2 6.9 %collective-permute-start.22 = (bf16[8,2560]{1,0:T(8,128)(2,1)}, bf16[8,2560]{1,0:T(8,128)(2,1)S(1)}, u32[]{:S(2)}, u32[]{:S(2)}) collective-permute-start(bf16[8,2560]{1,0:T(8,128)(2,1)} %copy-done.13), channel_id=1, source_target_pairs={{0,7},{1,6},{2,5},{3,4},{4,3},{5,2},{6,1},{7,0},{8,15},{9,14},{10,... | collective-permute-start | bytes 122888 | tf_op jit(solution)/shard_map/ppermute | solution.py:36
  85.9 10.2 %collective-permute-start.8 = (bf16[8,2688]{1,0:T(8,128)(2,1)S(1)}, bf16[8,2688]{1,0:T(8,128)(2,1)S(1)}, u32[]{:S(2)}, u32[]{:S(2)}) collective-permute-start(bf16[8,2688]{1,0:T(8,128)(2,1)S(1)} %get-tuple-element.44), channel_id=1, source_target_pairs={{0,3},{1,2},{2,1},{3,0},{4,7},{5,6},{6,5},{7,4},{8,11},{9,10},{10,... | collective-permute-start | bytes 129032 | tf_op jit(solution)/shard_map/ppermute | solution.py:36
  87.1 9.0 %collective-permute-start.9 = (bf16[8,2688]{1,0:T(8,128)(2,1)S(1)}, bf16[8,2688]{1,0:T(8,128)(2,1)S(1)}, u32[]{:S(2)}, u32[]{:S(2)}) collective-permute-start(bf16[8,2688]{1,0:T(8,128)(2,1)S(1)} %get-tuple-element.45), channel_id=1, source_target_pairs={{0,4},{1,5},{2,6},{3,7},{4,0},{5,1},{6,2},{7,3},{8,12},{9,13},{10,... | collective-permute-start | bytes 129032 | tf_op jit(solution)/shard_map/ppermute | solution.py:36
  88.1 8.0 %collective-permute-start.10 = (bf16[8,2688]{1,0:T(8,128)(2,1)S(1)}, bf16[8,2688]{1,0:T(8,128)(2,1)S(1)}, u32[]{:S(2)}, u32[]{:S(2)}) collective-permute-start(bf16[8,2688]{1,0:T(8,128)(2,1)S(1)} %get-tuple-element.46), channel_id=1, source_target_pairs={{0,5},{1,4},{2,7},{3,6},{4,1},{5,0},{6,3},{7,2},{8,13},{9,12},{10,... | collective-permute-start | bytes 129032 | tf_op jit(solution)/shard_map/ppermute | solution.py:36
  90.1 6.0 %collective-permute-start.11 = (bf16[8,2688]{1,0:T(8,128)(2,1)S(1)}, bf16[8,2688]{1,0:T(8,128)(2,1)S(1)}, u32[]{:S(2)}, u32[]{:S(2)}) collective-permute-start(bf16[8,2688]{1,0:T(8,128)(2,1)S(1)} %get-tuple-element.47), channel_id=1, source_target_pairs={{0,6},{1,7},{2,4},{3,5},{4,2},{5,3},{6,0},{7,1},{8,14},{9,15},{10,... | collective-permute-start | bytes 129032 | tf_op jit(solution)/shard_map/ppermute | solution.py:36
  91.6 6.7 %collective-permute-start.12 = (bf16[8,2688]{1,0:T(8,128)(2,1)S(1)}, bf16[8,2688]{1,0:T(8,128)(2,1)S(1)}, u32[]{:S(2)}, u32[]{:S(2)}) collective-permute-start(bf16[8,2688]{1,0:T(8,128)(2,1)S(1)} %get-tuple-element.48), channel_id=1, source_target_pairs={{0,7},{1,6},{2,5},{3,4},{4,3},{5,2},{6,1},{7,0},{8,15},{9,14},{10,... | collective-permute-start | bytes 129032 | tf_op jit(solution)/shard_map/ppermute | solution.py:36
  96.1 8.1 %collective-permute-start.42 = (f32[1,2048]{1,0:T(1,128)S(1)}, f32[1,2048]{1,0:T(1,128)S(1)}, u32[]{:S(2)}, u32[]{:S(2)}) collective-permute-start(f32[1,2048]{1,0:T(1,128)S(1)} %get-tuple-element.70), channel_id=1, source_target_pairs={{0,24},{8,16},{16,8},{24,0},{1,25},{9,17},{17,9},{25,1},{2,26},{10... | collective-permute-start | bytes 24584 | tf_op jit(solution)/shard_map/ppermute | solution.py:36
  99.7 8.3 %collective-permute-start.28 = (f32[1,1280]{1,0:T(1,128)S(1)}, f32[1,1280]{1,0:T(1,128)S(1)}, u32[]{:S(2)}, u32[]{:S(2)}) collective-permute-start(f32[1,1280]{1,0:T(1,128)S(1)} %get-tuple-element.67), channel_id=1, source_target_pairs={{0,6},{1,7},{2,4},{3,5},{4,2},{5,3},{6,0},{7,1},{8,14},{9,15},{10,... | collective-permute-start | bytes 15368 | tf_op jit(solution)/shard_map/ppermute | solution.py:36
  102.1 8.6 %collective-permute-start.29 = (f32[1,1280]{1,0:T(1,128)S(1)}, f32[1,1280]{1,0:T(1,128)S(1)}, u32[]{:S(2)}, u32[]{:S(2)}) collective-permute-start(f32[1,1280]{1,0:T(1,128)S(1)} %get-tuple-element.67), channel_id=1, source_target_pairs={{0,7},{1,6},{2,5},{3,4},{4,3},{5,2},{6,1},{7,0},{8,15},{9,14},{10,... | collective-permute-start | bytes 15368 | tf_op jit(solution)/shard_map/ppermute | solution.py:36
  104.8 8.1 %collective-permute-start.26 = (f32[1,1280]{1,0:T(1,128)S(1)}, f32[1,1280]{1,0:T(1,128)S(1)}, u32[]{:S(2)}, u32[]{:S(2)}) collective-permute-start(f32[1,1280]{1,0:T(1,128)S(1)} %get-tuple-element.67), channel_id=1, source_target_pairs={{0,4},{1,5},{2,6},{3,7},{4,0},{5,1},{6,2},{7,3},{8,12},{9,13},{10,... | collective-permute-start | bytes 15368 | tf_op jit(solution)/shard_map/ppermute | solution.py:36
  104.8 8.1 %collective-permute-start.27 = (f32[1,1280]{1,0:T(1,128)S(1)}, f32[1,1280]{1,0:T(1,128)S(1)}, u32[]{:S(2)}, u32[]{:S(2)}) collective-permute-start(f32[1,1280]{1,0:T(1,128)S(1)} %get-tuple-element.67), channel_id=1, source_target_pairs={{0,5},{1,4},{2,7},{3,6},{4,1},{5,0},{6,3},{7,2},{8,13},{9,12},{10,... | collective-permute-start | bytes 15368 | tf_op jit(solution)/shard_map/ppermute | solution.py:36
  108.0 4.9 %collective-permute-start.24 = (f32[1,1280]{1,0:T(1,128)S(1)}, f32[1,1280]{1,0:T(1,128)S(1)}, u32[]{:S(2)}, u32[]{:S(2)}) collective-permute-start(f32[1,1280]{1,0:T(1,128)S(1)} %get-tuple-element.67), channel_id=1, source_target_pairs={{0,2},{1,3},{2,0},{3,1},{4,6},{5,7},{6,4},{7,5},{8,10},{9,11},{10,... | collective-permute-start | bytes 15368 | tf_op jit(solution)/shard_map/ppermute | solution.py:36
  108.0 4.9 %collective-permute-start.25 = (f32[1,1280]{1,0:T(1,128)S(1)}, f32[1,1280]{1,0:T(1,128)S(1)}, u32[]{:S(2)}, u32[]{:S(2)}) collective-permute-start(f32[1,1280]{1,0:T(1,128)S(1)} %get-tuple-element.67), channel_id=1, source_target_pairs={{0,3},{1,2},{2,1},{3,0},{4,7},{5,6},{6,5},{7,4},{8,11},{9,10},{10,... | collective-permute-start | bytes 15368 | tf_op jit(solution)/shard_map/ppermute | solution.py:36
  110.7 3.6 %collective-permute-start.23 = (f32[1,1280]{1,0:T(1,128)S(1)}, f32[1,1280]{1,0:T(1,128)S(1)}, u32[]{:S(2)}, u32[]{:S(2)}) collective-permute-start(f32[1,1280]{1,0:T(1,128)S(1)} %get-tuple-element.67), channel_id=1, source_target_pairs={{0,1},{1,0},{2,3},{3,2},{4,5},{5,4},{6,7},{7,6},{8,9},{9,8},{10,11... | collective-permute-start | bytes 15368 | tf_op jit(solution)/shard_map/ppermute | solution.py:36
  114.3 4.6 %collective-permute-start.31 = (f32[1,1280]{1,0:T(1,128)S(1)}, f32[1,1280]{1,0:T(1,128)S(1)}, u32[]{:S(2)}, u32[]{:S(2)}) collective-permute-start(f32[1,1280]{1,0:T(1,128)S(1)} %add_add_fusion.1), channel_id=1, source_target_pairs={{0,16},{8,24},{16,0},{24,8},{1,17},{9,25},{17,1},{25,9},{2,18},{10... | collective-permute-start | bytes 15368 | tf_op jit(solution)/shard_map/ppermute | solution.py:36
  114.9 4.1 %collective-permute-start.32 = (f32[1,1280]{1,0:T(1,128)S(1)}, f32[1,1280]{1,0:T(1,128)S(1)}, u32[]{:S(2)}, u32[]{:S(2)}) collective-permute-start(f32[1,1280]{1,0:T(1,128)S(1)} %add_add_fusion.1), channel_id=1, source_target_pairs={{0,24},{8,16},{16,8},{24,0},{1,25},{9,17},{17,9},{25,1},{2,26},{10... | collective-permute-start | bytes 15368 | tf_op jit(solution)/shard_map/ppermute | solution.py:36
  114.9 4.1 %collective-permute-start.30 = (f32[1,1280]{1,0:T(1,128)S(1)}, f32[1,1280]{1,0:T(1,128)S(1)}, u32[]{:S(2)}, u32[]{:S(2)}) collective-permute-start(f32[1,1280]{1,0:T(1,128)S(1)} %add_add_fusion.1), channel_id=1, source_target_pairs={{0,8},{8,0},{16,24},{24,16},{1,9},{9,1},{17,25},{25,17},{2,10},{10... | collective-permute-start | bytes 15368 | tf_op jit(solution)/shard_map/ppermute | solution.py:36

commit v2 on v1

--- a/solution.py
+++ b/solution.py
@@ -12,7 +12,6 @@
 HEAD_DIM = 80
 LANES = 128
 CHUNKS = (2, 2)
-DIRECT = 8
 VMEM_BYTES = 40 * 1024 * 1024
 
 F32 = jnp.float32
@@ -29,24 +28,6 @@
 
 def vmem(count):
     return [pl.BlockSpec(memory_space=pltpu.VMEM)] * count
-
-
-def swap(x, axis, mask):
-    n = lax.axis_size(axis)
-    return lax.ppermute(x, axis, [(i, i ^ mask) for i in range(n)])
-
-
-def tree_sum(terms):
-    while len(terms) > 1:
-        terms = [terms[i] + terms[i + 1] for i in range(0, len(terms), 2)]
-    return terms[0]
-
-
-def sum_over(x, axis):
-    n = lax.axis_size(axis)
-    if n > DIRECT:
-        return lax.psum(x, axis)
-    return tree_sum([x] + [swap(x, axis, mask) for mask in range(1, n)])
 
 
 def head_windows():
@@ -67,39 +48,37 @@
     return jnp.where(lane_mask(low, high, start, stop), x, jnp.zeros_like(x))
 
 
-def project_kernel(blocks, first, tile, tiles, with_sum, *refs):
-    x_refs, w_ref = refs[:blocks], refs[blocks]
-    outs = refs[blocks + 1 : 2 * blocks + 1]
-    w_tiles, sems = refs[-2:]
+def project_kernel(first, tile, tiles, with_sum, x_ref, w_ref, *refs):
+    out_ref, (w_tiles, sems) = refs[0], refs[-2:]
     copies = [
         pltpu.make_async_copy(w_ref.at[pl.ds(first + t * tile, tile)], w_tiles.at[t], sems.at[t])
         for t in range(tiles)
     ]
     for copy in copies:
         copy.start()
-    x = jnp.concatenate([ref[...] for ref in x_refs], axis=0)
-    rows = x_refs[0].shape[0]
+    x = x_ref[...]
     if with_sum:
-        ones = jnp.ones((16, x.shape[0]), BF16)
-        refs[2 * blocks + 1][...] = dot(ones, x, (1, 0))[:1]
+        refs[1][...] = dot(jnp.ones((16, x.shape[0]), BF16), x, (1, 0))[:1]
+    x = x.T
     for t in range(tiles):
         copies[t].wait()
-        product = dot(x, w_tiles[t], (1, 1)).astype(BF16)
-        for j in range(blocks):
-            outs[j][:, t * tile : (t + 1) * tile] = product[j * rows : (j + 1) * rows]
-
-
-def project(x_blocks, w_down, first, width, with_sum):
-    blocks, (rows, depth) = len(x_blocks), x_blocks[0].shape
-    tile = 256
+        product = dot(w_tiles[t], x, (1, 0))
+        out_ref[:, t * tile : (t + 1) * tile] = product.T.astype(BF16)
+
+
+def project(x, w_down, first, width, with_sum):
+    rows, depth = x.shape
+    tile = 512
+    while width % tile:
+        tile //= 2
     tiles = width // tile
-    out_shape = [jax.ShapeDtypeStruct((rows, width), BF16)] * blocks
+    out_shape = [jax.ShapeDtypeStruct((rows, width), BF16)]
     if with_sum:
         out_shape = out_shape + [jax.ShapeDtypeStruct((1, depth), F32)]
-    out = pl.pallas_call(
-        functools.partial(project_kernel, blocks, first, tile, tiles, with_sum),
+    return pl.pallas_call(
+        functools.partial(project_kernel, first, tile, tiles, with_sum),
         out_shape=out_shape,
-        in_specs=vmem(blocks) + [pl.BlockSpec(memory_space=pl.ANY)],
+        in_specs=vmem(1) + [pl.BlockSpec(memory_space=pl.ANY)],
         out_specs=vmem(len(out_shape)),
         scratch_shapes=[
             pltpu.VMEM((tiles, tile, depth), BF16),
@@ -107,17 +86,16 @@
         ],
         compiler_params=pltpu.CompilerParams(vmem_limit_bytes=VMEM_BYTES),
         cost_estimate=pl.CostEstimate(
-            flops=2 * blocks * rows * depth * width,
+            flops=2 * rows * depth * width,
             bytes_accessed=2 * width * depth,
             transcendentals=0,
         ),
         name="project",
-    )(*x_blocks, w_down)
-    return out[:blocks], (out[blocks] if with_sum else None)
-
-
-def pack_kernel(peers, capacity, direct, labelled, blocks, me_ref, targets_ref, *refs):
-    terms, outs = refs[:blocks], refs[blocks:]
+    )(x, w_down)
+
+
+def pack_kernel(peers, capacity, first, carries, targets_ref, terms_ref, *refs):
+    out_ref = refs[-1]
     targets = targets_ref[...]
     rows = targets.shape[1]
     dest = targets // rows
@@ -129,56 +107,57 @@
     rank = jnp.sum(same_before.astype(jnp.int32), axis=0, keepdims=True)
     slots = peers * capacity
     slot = iota((slots, rows), 0)
-    holder = slot // capacity
-    if direct:
-        holder = holder ^ me_ref[0]
-    chosen = jnp.logical_and(dest == holder, rank == slot % capacity)
-    total = terms[0][...].astype(F32)
-    for term in terms[1:]:
-        total = total + term[...].astype(F32)
-    width = total.shape[1]
+    chosen = jnp.logical_and(dest == slot // capacity, rank == slot % capacity)
+    total = terms_ref[0].astype(F32)
+    for term in range(1, terms_ref.shape[0]):
+        total = total + terms_ref[term].astype(F32)
     packed = dot(chosen.astype(F32).astype(BF16), total.astype(BF16), (1, 0))
-    if labelled:
+    if first:
         label = jnp.sum(jnp.where(chosen, local + 1, 0), axis=1, keepdims=True) - 1
         packed = jnp.concatenate(
             [packed, jnp.broadcast_to(label.astype(F32), (slots, LANES))], axis=1
         )
-    if not direct:
-        outs[0][...] = packed.astype(BF16)
-        return
-    for m in range(peers):
-        outs[m][...] = packed[m * capacity : (m + 1) * capacity].astype(BF16)
-
-
-def pack(terms, targets, me, peers, capacity, direct, labelled):
-    rows, width = terms[0].shape
-    width = width + (LANES if labelled else 0)
-    if direct:
-        out_shape = [jax.ShapeDtypeStruct((capacity, width), BF16)] * peers
-    else:
-        out_shape = [jax.ShapeDtypeStruct((peers * capacity, width), BF16)]
-    return pl.pallas_call(
-        functools.partial(pack_kernel, peers, capacity, direct, labelled, len(terms)),
-        out_shape=out_shape,
-        in_specs=[pl.BlockSpec(memory_space=pltpu.SMEM)] + vmem(1 + len(terms)),
-        out_specs=vmem(len(out_shape)),
+    if carries:
+        sums = refs[0][...]
+        high = sums.astype(BF16).astype(F32)
+        middle = (sums - high).astype(BF16).astype(F32)
+        low = (sums - high - middle).astype(BF16).astype(F32)
+        extra = jnp.zeros((slots, LANES), F32)
+        row = iota((slots, LANES), 0)
+        pieces = sums.shape[1] // peers // LANES
+        for peer in range(peers):
+            for level, values in enumerate((high, middle, low)):
+                for piece in range(pieces):
+                    at = (peer * pieces + piece) * LANES
+                    line = jnp.broadcast_to(values[:, at : at + LANES], (slots, LANES))
+                    extra = jnp.where(row == peer * capacity + level * pieces + piece, line, extra)
+        packed = jnp.concatenate([packed, extra], axis=1)
+    out_ref[...] = packed.astype(BF16)
+
+
+def pack(terms, targets, sums, peers, capacity, first, carries):
+    _, rows, width = terms.shape
+    width = width + (LANES if first else 0) + (LANES if carries else 0)
+    return pl.pallas_call(
+        functools.partial(pack_kernel, peers, capacity, first, carries),
+        out_shape=jax.ShapeDtypeStruct((peers * capacity, width), BF16),
+        in_specs=vmem(3 if carries else 2),
+        out_specs=pl.BlockSpec(memory_space=pltpu.VMEM),
         compiler_params=pltpu.CompilerParams(vmem_limit_bytes=VMEM_BYTES),
         cost_estimate=pl.CostEstimate(
             flops=2 * rows * peers * capacity * width,
-            bytes_accessed=2 * (len(terms) * rows + peers * capacity) * width,
+            bytes_accessed=2 * (terms.shape[0] * rows + peers * capacity) * width,
             transcendentals=0,
         ),
         name="pack",
-    )(me, targets, *terms)
-
-
-def route(packed, peers, capacity, direct):
-    if direct:
-        return [packed[0]] + [swap(packed[m], "seq", m) for m in range(1, peers)]
-    width = packed[0].shape[1]
-    sent = packed[0].reshape(peers, capacity, width)
-    got = lax.all_to_all(sent, "seq", split_axis=0, concat_axis=0, tiled=True)
-    return [got.reshape(peers * capacity, width)]
+    )(*((targets, terms, sums) if carries else (targets, terms)))
+
+
+def exchange(x, axis, pieces):
+    shape = x.shape
+    if x.ndim == 2:
+        x = x.reshape(pieces, -1, shape[1])
+    return lax.all_to_all(x, axis, split_axis=0, concat_axis=0, tiled=True).reshape(shape)
 
 
 def probs_kernel(q_ref, k_ref, ids_ref, probs_ref, probs_t_ref):
@@ -225,18 +204,15 @@
     )(queries, keys, ids)
 
 
-def norm_kernel(counts, parts, slots, patches_ref, gain_ref, *refs):
-    chunks, at = [], 0
-    for count in counts:
-        chunks.append([ref[...].astype(F32) for ref in refs[at : at + count]])
-        at += count
-    out_ref, gain_grad_ref = refs[at:]
+def norm_kernel(parts, peers, copies, patches_ref, gain_ref, *refs):
+    chunk_refs, (out_ref, share_ref) = refs[:-2], refs[-2:]
     patches, width = patches_ref.shape
-    chunks = [jnp.concatenate(chunk, axis=0) for chunk in chunks]
-    labels = chunks[0][:, parts[0] * width :][:, :1]
+    slots = chunk_refs[0].shape[0]
+    first, count = chunk_refs[0], parts[0]
+    labels = first[:, count * width : count * width + LANES].astype(F32)[:, :1]
     columns = []
-    for chunk, count in zip(chunks, parts):
-        columns += [chunk[:, c * width : (c + 1) * width] for c in range(count)]
+    for ref, count in zip(chunk_refs, parts):
+        columns += [ref[:, c * width : (c + 1) * width].astype(F32) for c in range(count)]
     held = jnp.concatenate(columns, axis=0).astype(BF16)
     lanes = len(columns) * slots
     lane = iota((slots, lanes), 1)
@@ -250,24 +226,33 @@
     inputs = patches_ref[...].astype(F32)
     inverse_rms = lax.rsqrt(jnp.mean(inputs * inputs, axis=1, keepdims=True) + 1e-06)
     normed = inputs * inverse_rms
-    gain_grad_ref[...] = jnp.sum(patch_grads * normed, axis=0, keepdims=True)
+    gain_part = jnp.sum(patch_grads * normed, axis=0, keepdims=True)
+    if copies:
+        rows = [gain_part[:, at : at + LANES] for at in range(0, width, LANES)]
+        carried = first[:, parts[0] * width + LANES :].astype(F32)
+        capacity = slots // peers
+        pieces = share_ref.shape[1] - len(rows)
+        for piece in range(pieces):
+            kept = iota((slots, LANES), 0) % capacity % pieces == piece
+            kept = jnp.logical_and(kept, iota((slots, LANES), 0) % capacity < 3 * pieces)
+            rows.append(jnp.sum(jnp.where(kept, carried, 0.0), axis=0, keepdims=True))
+        for at, row in enumerate(rows):
+            share_ref[:, at : at + 1, :] = jnp.broadcast_to(row[None], (copies, 1, LANES))
+    else:
+        share_ref[...] = gain_part
     scaled = gain_ref[...] * patch_grads
     out_ref[...] = (
         inverse_rms * (scaled - normed * jnp.mean(scaled * normed, axis=1, keepdims=True))
     ).astype(BF16)
 
 
-def norm_backward(received, parts, slots, patches, gain):
-    counts = [len(chunk) for chunk in received]
-    flat = [x for chunk in received for x in chunk]
+def norm_backward(received, parts, peers, patches, gain, share):
     count, width = patches.shape
-    return pl.pallas_call(
-        functools.partial(norm_kernel, counts, parts, slots),
-        out_shape=[
-            jax.ShapeDtypeStruct((count, width), BF16),
-            jax.ShapeDtypeStruct((1, width), F32),
-        ],
-        in_specs=vmem(2 + len(flat)),
+    slots = received[0].shape[0]
+    return pl.pallas_call(
+        functools.partial(norm_kernel, parts, peers, share[0] if len(share) == 3 else 0),
+        out_shape=[jax.ShapeDtypeStruct((count, width), BF16), jax.ShapeDtypeStruct(share, F32)],
+        in_specs=vmem(2 + len(received)),
         out_specs=vmem(2),
         compiler_params=pltpu.CompilerParams(vmem_limit_bytes=VMEM_BYTES),
         cost_estimate=pl.CostEstimate(
@@ -276,7 +261,7 @@
             transcendentals=0,
         ),
         name="norm",
-    )(patches, gain, *flat)
+    )(patches, gain, *received)
 
 
 def window_kernel(g_ref, q_ref, k_ref, v_ref, probs_ref, probs_t_ref, dq_ref, dk_ref, dv_ref):
@@ -339,41 +324,41 @@
     grad_rows = llm_grads[0]
     rows = grad_rows.shape[0]
     images, peers = lax.axis_size("img"), lax.axis_size("seq")
-    image, me = lax.axis_index("img"), lax.axis_index("seq")
+    devices = images * peers
     capacity = max(1, 2 * rows // peers)
-    slots = peers * capacity
-    direct = peers <= DIRECT
     block = w_down.shape[1]
     width = patches.shape[2]
-
-    def column_block(index):
-        return lax.dynamic_slice(grad_rows, (0, index * block), (rows, block))
-
-    x_blocks = [column_block(image)]
-    x_blocks += [swap(column_block(image ^ j), "img", j) for j in range(1, images)]
+    pieces = block // peers // LANES
+    carries = pieces > 0 and 3 * pieces <= capacity
+
+    columns = grad_rows.reshape(rows, images, block).transpose(1, 0, 2)
+    x = exchange(columns, "img", images).reshape(images * rows, block)
     probs, probs_t = window_probs(queries[0], keys[0], window_ids[0])
 
     received, first = [], 0
     for index, count in enumerate(CHUNKS):
-        terms, sums = project(x_blocks, w_down, first, count * width, index == 0)
+        partial = project(x, w_down, first, count * width, index == 0)
         first += count * width
         if index == 0:
-            bias_part = sums
-        terms = [terms[0]] + [swap(terms[j], "img", j) for j in range(1, images)]
-        packed = pack(terms, token_target, me.reshape(1), peers, capacity, direct, index == 0)
-        received.append(route(packed, peers, capacity, direct))
-
-    bias_block = sum_over(bias_part, "seq")
-    bias_blocks = [bias_block] + [swap(bias_block, "img", j) for j in range(1, images)]
-    bias_total = jnp.zeros((images, 1, block), F32)
-    for j in range(images):
-        bias_total = lax.dynamic_update_slice(bias_total, bias_blocks[j][None], (image ^ j, 0, 0))
-    bias_total = bias_total.reshape(-1)
-
-    out_grads, gain_part = norm_backward(received, CHUNKS, slots, patches[0], gain[None])
-    gain_total = sum_over(sum_over(gain_part, "seq"), "img")[0]
+            bias_part = partial[1]
+        terms = exchange(partial[0].reshape(images, rows, -1), "img", images)
+        begins = index == 0
+        packed = pack(
+            terms, token_target, bias_part, peers, capacity, begins, begins and carries
+        )
+        received.append(exchange(packed, "seq", peers))
+
+    gain_rows = width // LANES
+    share = (devices, gain_rows + pieces, LANES) if carries else (1, width)
+    out_grads, shared = norm_backward(received, CHUNKS, peers, patches[0], gain[None], share)
+    if carries:
+        shared = exchange(shared, ("img", "seq"), devices)
+        gain_total = jnp.sum(shared[:, :gain_rows], axis=0).reshape(-1)
+        bias_total = shared[:, gain_rows:].reshape(-1)
+    else:
+        gain_total = lax.psum(shared[0], ("img", "seq"))
+        bias_total = lax.all_gather(lax.psum(bias_part[0], "seq"), "img", tiled=True)
     grads = window_backward(out_grads, queries[0], keys[0], values[0], probs, probs_t)
-    devices = images * peers
     gain_grad = gain_total / math.sqrt(devices * patches.shape[1])
     bias_grad = bias_total / math.sqrt(devices * rows)
     return (grads[0][None], grads[1][None], grads[2][None], gain_grad, bias_grad)

time: 120 us -> 97.8 us (0.81)
  starting transfers between devices: 55.5 us -> 19.1 us
  blocking collectives: 0 us -> 12.9 us
  waiting for transfers between devices: 24.8 us -> 37.6 us
  local copies, waits for them, and re-layouts: 13.2 us -> 1.76 us
    ppermute x43 -> x0, starting transfers between devices: 55.5 us -> none  [swap(): return lax.ppermute(x, axis, [(i, i ^ mask) for i in range(n)])]
    all_to_all x0 -> x5, waiting for transfers between devices: none -> 37.6 us  [exchange(): lax.all_to_all(x, axis, split_axis=0, concat_axis=0, tiled=True)]
    ppermute x43 -> x0, waiting for transfers between devices: 24.8 us -> none  [swap(): return lax.ppermute(x, axis, [(i, i ^ mask) for i in range(n)])]
    all_to_all x0 -> x5, starting transfers between devices: none -> 19.1 us  [exchange(): lax.all_to_all(x, axis, split_axis=0, concat_axis=0, tiled=True)]
    all_to_all x0 -> x1, blocking collectives: none -> 12.9 us  [exchange(): lax.all_to_all(x, axis, split_axis=0, concat_axis=0, tiled=True)]
    unnamed x38 -> x14, local copies, waits for them, and re-layouts: 8.18 us -> 0.03 us
    dynamic_update_slice x3 -> x0, local copies, waits for them, and re-layouts: 3.19 us -> none  [body(): lax.dynamic_update_slice(bias_total, bias_blocks[j][None], (image ^ j, 0,...]
    another operation x0 -> x2, local copies, waits for them, and re-layouts: none -> 1.73 us  [body(): columns = grad_rows.reshape(rows, images, block).transpose(1, 0, 2)]
  transfers between devices with their start and end apart: 43 -> 5, of which waited for: 10 -> 5; matrix products, arithmetic and copies ran while one was open for 4% -> 0% of each run, Pallas kernels for 12% -> 14%
where the time goes in v2:
time: 97.8 us; the launch traced here: 97.2 us
  waiting for transfers between devices  37.6 us (38%)
  Pallas kernels  23.8 us (24%)
  starting transfers between devices  19.1 us (20%)
  blocking collectives  12.9 us (13%)
  local copies, waits for them, and re-layouts  1.76 us (2%)
  other arithmetic  1.27 us (1%)
    all_to_all x5, waiting for transfers between devices, exchange(): lax.all_to_all(x, axis, split_axis=0, concat_axis=0, tiled=True)  37.6 us
    all_to_all x5, starting transfers between devices, exchange(): lax.all_to_all(x, axis, split_axis=0, concat_axis=0, tiled=True)  19.1 us
    pallas_call x2, Pallas kernels, project(): pl.pallas_call(functools.partial(project_kernel, first, tile, tiles, with...  17.1 us
    all_to_all x1, blocking collectives, exchange(): lax.all_to_all(x, axis, split_axis=0, concat_axis=0, tiled=True)  12.9 us
    pallas_call x1, Pallas kernels, window_backward(): pl.pallas_call(window_kernel, out_shape=[shape] * 3, in_specs=vmem(6), ou...  2.38 us
    pallas_call x2, Pallas kernels, pack(): pl.pallas_call(functools.partial(pack_kernel, peers, capacity, first, car...  2.13 us
  transfers between devices with their start and end apart: 5, of which 5 were waited for; matrix products, arithmetic and copies ran while one was open for 0% of the time, Pallas kernels for 14%

profile of v2, /device:TPU:0, one launch (start us, length us, event | category | flops | bytes accessed | tf_op | source)
XLA Modules:
  0.0 97.2 jit_solution(2775861551508891720)
XLA Ops:
  0.6 1.4 %reshape_squeeze.3 = bf16[32,4,2048]{2,1,0:T(4,128)(2,1)S(1)} reshape(bf16[1,32,8192]{2,1,0:T(8,128)(2,1)} %param.9) | data formatting | bytes 1048576 | tf_op jit(solution)/shard_map/reshape;squeeze | solution.py:334
  2.1 0.3 copy.16
  2.4 12.9 %all_to_all.30 = bf16[4,32,2048]{2,1,0:T(8,128)(2,1)S(1)} all-to-all(bf16[4,32,2048]{2,1,0:T(8,128)(2,1)S(1)} %bitcast.32), channel_id=1, replica_groups=mesh['img'=4,'seq'=8] {'img'}, dimensions={0} | all-to-all | bytes 1048576 | tf_op jit(solution)/shard_map/all_to_all | solution.py:160
  15.2 0.0 copy-start.4
  15.2 0.0 copy-start.6
  15.3 0.0 copy-start
  15.3 0.0 copy-start.1
  15.3 0.0 copy-start.2
  15.3 0.0 copy-start.5
  15.3 0.0 copy-start.3
  15.3 8.6 %project.3 = bf16[128,2560]{1,0:T(8,128)(2,1)} custom-call(bf16[128,2048]{1,0:T(8,128)(2,1)S(1)} %bitcast.21, bf16[5120,2048]{1,0:T(8,128)(2,1)} %w_ref.3), custom_call_target="tpu_custom_call" | custom-call | flops 1342177280 | bytes 10485760 | tf_op jit(solution)/shard_map/project/pallas_call | solution.py:78
  23.9 3.5 %all-to-all-start.3 = ((bf16[4,32,2560]{2,1,0:T(8,128)(2,1)}), bf16[4,32,2560]{2,1,0:T(8,128)(2,1)S(1)}, u32[]{:S(2)}, u32[]{:S(2)}) async-start(bf16[4,32,2560]{2,1,0:T(8,128)(2,1)} %bitcast.6), calls=%async_computation.3 | async-start | bytes 1310720 | tf_op jit(solution)/shard_map/all_to_all | solution.py:160
  27.4 8.5 %project.2 = (bf16[128,2560]{1,0:T(8,128)(2,1)}, f32[1,2048]{1,0:T(1,128)S(1)}) custom-call(bf16[128,2048]{1,0:T(8,128)(2,1)S(1)} %bitcast.22, bf16[5120,2048]{1,0:T(8,128)(2,1)} %w_ref.3), custom_call_target="tpu_custom_call" | custom-call | flops 1342177280 | bytes 10485760 | tf_op jit(solution)/shard_map/project/pallas_call | solution.py:78
  35.9 1.7 %all-to-all-done.3.terms_ref = bf16[4,32,2560]{2,1,0:T(8,128)(2,1)S(1)} async-done(((bf16[4,32,2560]{2,1,0:T(8,128)(2,1)}), bf16[4,32,2560]{2,1,0:T(8,128)(2,1)S(1)}, u32[]{:S(2)}, u32[]{:S(2)}) %all-to-all-start.3) | async-done | bytes 655392 | tf_op jit(solution)/shard_map/all_to_all | solution.py:160
  37.6 3.5 %all-to-all-start.1 = ((bf16[4,32,2560]{2,1,0:T(8,128)(2,1)}), bf16[4,32,2560]{2,1,0:T(8,128)(2,1)S(1)}, u32[]{:S(2)}, u32[]{:S(2)}) async-start(bf16[4,32,2560]{2,1,0:T(8,128)(2,1)} %bitcast.3), calls=%async_computation.1 | async-start | bytes 1310720 | tf_op jit(solution)/shard_map/all_to_all | solution.py:160
  41.1 0.0 copy-done.4
  41.1 1.1 %pack.3 = bf16[64,2560]{1,0:T(8,128)(2,1)} custom-call(s32[1,32]{1,0:T(1,128)S(1)} %copy-done.4, bf16[4,32,2560]{2,1,0:T(8,128)(2,1)S(1)} %all-to-all-done.3.terms_ref), custom_call_target="tpu_custom_call" | custom-call | flops 10485760 | bytes 983040 | tf_op jit(solution)/shard_map/pack/pallas_call | solution.py:141
  42.1 9.2 %all-to-all-done.1.terms_ref = bf16[4,32,2560]{2,1,0:T(8,128)(2,1)S(1)} async-done(((bf16[4,32,2560]{2,1,0:T(8,128)(2,1)}), bf16[4,32,2560]{2,1,0:T(8,128)(2,1)S(1)}, u32[]{:S(2)}, u32[]{:S(2)}) %all-to-all-start.1) | async-done | bytes 655392 | tf_op jit(solution)/shard_map/all_to_all | solution.py:160
  51.3 5.8 %all-to-all-start.4 = ((bf16[8,8,2560]{2,1,0:T(8,128)(2,1)}), bf16[8,8,2560]{2,1,0:T(8,128)(2,1)S(1)}, u32[]{:S(2)}, u32[]{:S(2)}) async-start(bf16[8,8,2560]{2,1,0:T(8,128)(2,1)} %bitcast.7), calls=%async_computation.4 | async-start | bytes 655360 | tf_op jit(solution)/shard_map/all_to_all | solution.py:160
  57.1 1.1 %pack.2 = bf16[64,2816]{1,0:T(8,128)(2,1)} custom-call(s32[1,32]{1,0:T(1,128)S(1)} %copy-done.4, bf16[4,32,2560]{2,1,0:T(8,128)(2,1)S(1)} %all-to-all-done.1.terms_ref, f32[1,2048]{1,0:T(1,128)S(1)} %get-tuple-element.15.refs_0_), custom_call_target="tpu_custom_call" | custom-call | flops 11534336 | bytes 1081344 | tf_op jit(solution)/shard_map/pack/pallas_call | solution.py:141
  58.2 9.0 %all-to-all-done.4 = bf16[8,8,2560]{2,1,0:T(8,128)(2,1)S(1)} async-done(((bf16[8,8,2560]{2,1,0:T(8,128)(2,1)}), bf16[8,8,2560]{2,1,0:T(8,128)(2,1)S(1)}, u32[]{:S(2)}, u32[]{:S(2)}) %all-to-all-start.4) | async-done | bytes 327712 | tf_op jit(solution)/shard_map/all_to_all | solution.py:160
  67.2 3.6 %all-to-all-start.2 = ((bf16[8,8,2816]{2,1,0:T(8,128)(2,1)}), bf16[8,8,2816]{2,1,0:T(8,128)(2,1)S(1)}, u32[]{:S(2)}, u32[]{:S(2)}) async-start(bf16[8,8,2816]{2,1,0:T(8,128)(2,1)} %bitcast.4), calls=%async_computation.2 | async-start | bytes 720896 | tf_op jit(solution)/shard_map/all_to_all | solution.py:160
  70.8 0.0 copy-done.6
  70.8 10.6 %all-to-all-done.2 = bf16[8,8,2816]{2,1,0:T(8,128)(2,1)S(1)} async-done(((bf16[8,8,2816]{2,1,0:T(8,128)(2,1)}), bf16[8,8,2816]{2,1,0:T(8,128)(2,1)S(1)}, u32[]{:S(2)}, u32[]{:S(2)}) %all-to-all-start.2) | async-done | bytes 360480 | tf_op jit(solution)/shard_map/all_to_all | solution.py:160
  81.4 0.0 copy-done
  81.4 1.2 %norm.1 = (bf16[128,1280]{1,0:T(8,128)(2,1)S(1)}, f32[32,12,128]{2,1,0:T(8,128)}) custom-call(bf16[128,1280]{1,0:T(8,128)(2,1)S(1)} %bitcast.25, f32[1,1280]{1,0:T(1,128)S(1)} %broadcast_in_dim.12.gain_ref, bf16[64,2816]{1,0:T(8,128)(2,1)S(1)} %bitcast.23, bf16[64,2560]{1,0:T(8,128)(2,1)S(1)} %bitcast.24), custom_call_target="tpu_custom_call" | custom-call | flops 83886080 | bytes 1310720 | tf_op jit(solution)/shard_map/norm/pallas_call | solution.py:252
  82.6 2.7 %all-to-all-start.5 = ((f32[32,12,128]{2,1,0:T(8,128)}), f32[32,12,128]{2,1,0:T(8,128)S(1)}, u32[]{:S(2)}, u32[]{:S(2)}) async-start(f32[32,12,128]{2,1,0:T(8,128)} %get-tuple-element.22), calls=%async_computation.5 | async-start | bytes 524288 | tf_op jit(solution)/shard_map/all_to_all | solution.py:160
  85.3 0.0 copy-done.1
  85.3 0.0 copy-done.2
  85.3 0.0 copy-done.5
  85.3 1.1 %probs.1 = (f32[16,128,128]{2,1,0:T(8,128)S(1)}, f32[16,128,128]{2,1,0:T(8,128)S(1)}) custom-call(bf16[128,1280]{1,0:T(8,128)(2,1)S(1)} %bitcast.26, bf16[128,1280]{1,0:T(8,128)(2,1)S(1)} %bitcast.28, s32[1,32]{1,0:T(1,128)S(1)} %bitcast.31), custom_call_target="tpu_custom_call" | custom-call | flops 268435456 | bytes 2097152 | tf_op jit(solution)/shard_map/probs/pallas_call | solution.py:192
  86.4 0.0 copy-done.3
  86.4 2.4 %window.1 = (bf16[128,1280]{1,0:T(8,128)(2,1)}, bf16[128,1280]{1,0:T(8,128)(2,1)}, bf16[128,1280]{1,0:T(8,128)(2,1)}) custom-call(bf16[128,1280]{1,0:T(8,128)(2,1)S(1)} %get-tuple-element.16.g_ref, bf16[128,1280]{1,0:T(8,128)(2,1)S(1)} %bitcast.27, bf16[128,1280]{1,0:T(8,128)(2,1)S(1)} %bitcast.29, bf16[128,1280]{1,0:T(8,128)(2,1)S(1)} %bitcast.30, ...), custom_call_target="tpu_custom_call" | custom-call | flops 335544320 | bytes 4390912 | tf_op jit(solution)/shard_map/window/pallas_call | solution.py:308
  88.8 7.2 %all-to-all-done.5 = f32[32,12,128]{2,1,0:T(8,128)S(1)} async-done(((f32[32,12,128]{2,1,0:T(8,128)}), f32[32,12,128]{2,1,0:T(8,128)S(1)}, u32[]{:S(2)}, u32[]{:S(2)}) %all-to-all-start.5) | async-done | bytes 196640 | tf_op jit(solution)/shard_map/all_to_all | solution.py:160
  96.0 0.6 multiply_bitcast_fusion
  96.6 0.6 slice_multiply_fusion
  (2 shorter events, 0.0 us)
Async XLA Ops:
  15.2 25.8 %copy-start.4 = (s32[1,32]{1,0:T(1,128)S(1)}, s32[1,32]{1,0:T(1,128)}, u32[]{:S(2)}) copy-start(s32[1,32]{1,0:T(1,128)} %targets_ref.3) | copy-start | bytes 388
  15.2 55.6 %copy-start.6 = (f32[1280]{0:T(1024)S(1)}, f32[1280]{0:T(1024)}, u32[]{:S(2)}) copy-start(f32[1280]{0:T(1024)} %param.12) | copy-start | bytes 15364
  15.3 66.1 %copy-start = (bf16[1,128,1280]{2,1,0:T(8,128)(2,1)S(1)}, bf16[1,128,1280]{2,1,0:T(8,128)(2,1)}, u32[]{:S(2)}) copy-start(bf16[1,128,1280]{2,1,0:T(8,128)(2,1)} %param.11) | copy-start | bytes 983044
  15.3 70.1 %copy-start.1 = (bf16[1,128,1280]{2,1,0:T(8,128)(2,1)S(1)}, bf16[1,128,1280]{2,1,0:T(8,128)(2,1)}, u32[]{:S(2)}) copy-start(bf16[1,128,1280]{2,1,0:T(8,128)(2,1)} %param.14) | copy-start | bytes 983044
  15.3 70.1 %copy-start.2 = (bf16[1,128,1280]{2,1,0:T(8,128)(2,1)S(1)}, bf16[1,128,1280]{2,1,0:T(8,128)(2,1)}, u32[]{:S(2)}) copy-start(bf16[1,128,1280]{2,1,0:T(8,128)(2,1)} %param.15) | copy-start | bytes 983044
  15.3 70.1 %copy-start.5 = (s32[1,1,32]{2,1,0:T(1,128)S(1)}, s32[1,1,32]{2,1,0:T(1,128)}, u32[]{:S(2)}) copy-start(s32[1,1,32]{2,1,0:T(1,128)} %param.17) | copy-start | bytes 388
  15.3 71.1 %copy-start.3 = (bf16[1,128,1280]{2,1,0:T(8,128)(2,1)S(1)}, bf16[1,128,1280]{2,1,0:T(8,128)(2,1)}, u32[]{:S(2)}) copy-start(bf16[1,128,1280]{2,1,0:T(8,128)(2,1)} %param.16) | copy-start | bytes 983044
  23.9 13.7 %all-to-all-start.3 = ((bf16[4,32,2560]{2,1,0:T(8,128)(2,1)}), bf16[4,32,2560]{2,1,0:T(8,128)(2,1)S(1)}, u32[]{:S(2)}, u32[]{:S(2)}) async-start(bf16[4,32,2560]{2,1,0:T(8,128)(2,1)} %bitcast.6), calls=%async_computation.3 | async-start | bytes 1310720 | tf_op jit(solution)/shard_map/all_to_all | solution.py:160
  37.6 13.7 %all-to-all-start.1 = ((bf16[4,32,2560]{2,1,0:T(8,128)(2,1)}), bf16[4,32,2560]{2,1,0:T(8,128)(2,1)S(1)}, u32[]{:S(2)}, u32[]{:S(2)}) async-start(bf16[4,32,2560]{2,1,0:T(8,128)(2,1)} %bitcast.3), calls=%async_computation.1 | async-start | bytes 1310720 | tf_op jit(solution)/shard_map/all_to_all | solution.py:160
  51.3 15.9 %all-to-all-start.4 = ((bf16[8,8,2560]{2,1,0:T(8,128)(2,1)}), bf16[8,8,2560]{2,1,0:T(8,128)(2,1)S(1)}, u32[]{:S(2)}, u32[]{:S(2)}) async-start(bf16[8,8,2560]{2,1,0:T(8,128)(2,1)} %bitcast.7), calls=%async_computation.4 | async-start | bytes 655360 | tf_op jit(solution)/shard_map/all_to_all | solution.py:160
  67.2 14.2 %all-to-all-start.2 = ((bf16[8,8,2816]{2,1,0:T(8,128)(2,1)}), bf16[8,8,2816]{2,1,0:T(8,128)(2,1)S(1)}, u32[]{:S(2)}, u32[]{:S(2)}) async-start(bf16[8,8,2816]{2,1,0:T(8,128)(2,1)} %bitcast.4), calls=%async_computation.2 | async-start | bytes 720896 | tf_op jit(solution)/shard_map/all_to_all | solution.py:160
  82.6 13.4 %all-to-all-start.5 = ((f32[32,12,128]{2,1,0:T(8,128)}), f32[32,12,128]{2,1,0:T(8,128)S(1)}, u32[]{:S(2)}, u32[]{:S(2)}) async-start(f32[32,12,128]{2,1,0:T(8,128)} %get-tuple-element.22), calls=%async_computation.5 | async-start | bytes 524288 | tf_op jit(solution)/shard_map/all_to_all | solution.py:160

commit v3 on v2

--- a/solution.py
+++ b/solution.py
@@ -12,7 +12,7 @@
 HEAD_DIM = 80
 LANES = 128
 CHUNKS = (2, 2)
-VMEM_BYTES = 40 * 1024 * 1024
+VMEM_BYTES = 24 * 1024 * 1024
 
 F32 = jnp.float32
 BF16 = jnp.bfloat16
@@ -48,54 +48,70 @@
     return jnp.where(lane_mask(low, high, start, stop), x, jnp.zeros_like(x))
 
 
-def project_kernel(first, tile, tiles, with_sum, x_ref, w_ref, *refs):
-    out_ref, (w_tiles, sems) = refs[0], refs[-2:]
-    copies = [
-        pltpu.make_async_copy(w_ref.at[pl.ds(first + t * tile, tile)], w_tiles.at[t], sems.at[t])
-        for t in range(tiles)
-    ]
-    for copy in copies:
-        copy.start()
-    x = x_ref[...]
+def project_kernel(blocks, tile, with_sum, *refs):
+    x_refs, w_ref = refs[:blocks], refs[blocks]
+    keep_ref, send_ref = refs[blocks + 1 : blocks + 3]
+    x = jnp.concatenate([ref[...] for ref in x_refs], axis=0)
     if with_sum:
-        refs[1][...] = dot(jnp.ones((16, x.shape[0]), BF16), x, (1, 0))[:1]
+        refs[blocks + 3][...] = dot(jnp.ones((16, x.shape[0]), BF16), x, (1, 0))[:1]
     x = x.T
-    for t in range(tiles):
-        copies[t].wait()
-        product = dot(w_tiles[t], x, (1, 0))
-        out_ref[:, t * tile : (t + 1) * tile] = product.T.astype(BF16)
-
-
-def project(x, w_down, first, width, with_sum):
-    rows, depth = x.shape
+    half = keep_ref.shape[0]
+    for t in range(0, w_ref.shape[0], tile):
+        product = dot(w_ref[t : t + tile], x, (1, 0)).T.astype(BF16)
+        keep_ref[:, t : t + tile] = product[:half]
+        send_ref[:, t : t + tile] = product[half:]
+
+
+def project(x_blocks, w_rows, with_sum):
+    blocks, (rows, depth) = len(x_blocks), x_blocks[0].shape
+    width = w_rows.shape[0]
     tile = 512
     while width % tile:
         tile //= 2
-    tiles = width // tile
-    out_shape = [jax.ShapeDtypeStruct((rows, width), BF16)]
+    out_shape = [jax.ShapeDtypeStruct((blocks * rows // 2, width), BF16)] * 2
     if with_sum:
         out_shape = out_shape + [jax.ShapeDtypeStruct((1, depth), F32)]
     return pl.pallas_call(
-        functools.partial(project_kernel, first, tile, tiles, with_sum),
+        functools.partial(project_kernel, blocks, tile, with_sum),
         out_shape=out_shape,
-        in_specs=vmem(1) + [pl.BlockSpec(memory_space=pl.ANY)],
+        in_specs=vmem(blocks + 1),
         out_specs=vmem(len(out_shape)),
-        scratch_shapes=[
-            pltpu.VMEM((tiles, tile, depth), BF16),
-            pltpu.SemaphoreType.DMA((tiles,)),
-        ],
-        compiler_params=pltpu.CompilerParams(vmem_limit_bytes=VMEM_BYTES),
-        cost_estimate=pl.CostEstimate(
-            flops=2 * rows * depth * width,
+        compiler_params=pltpu.CompilerParams(vmem_limit_bytes=VMEM_BYTES),
+        cost_estimate=pl.CostEstimate(
+            flops=2 * blocks * rows * depth * width,
             bytes_accessed=2 * width * depth,
             transcendentals=0,
         ),
         name="project",
-    )(x, w_down)
-
-
-def pack_kernel(peers, capacity, first, carries, targets_ref, terms_ref, *refs):
-    out_ref = refs[-1]
+    )(*x_blocks, w_rows)
+
+
+def halve_kernel(kept_ref, got_ref, keep_ref, send_ref):
+    half = keep_ref.shape[0]
+    keep_ref[...] = kept_ref[:half].astype(F32) + got_ref[:half].astype(F32)
+    send_ref[...] = (kept_ref[half:].astype(F32) + got_ref[half:].astype(F32)).astype(BF16)
+
+
+def halve(kept, got):
+    rows, width = kept.shape
+    return pl.pallas_call(
+        halve_kernel,
+        out_shape=[
+            jax.ShapeDtypeStruct((rows // 2, width), F32),
+            jax.ShapeDtypeStruct((rows // 2, width), BF16),
+        ],
+        in_specs=vmem(2),
+        out_specs=vmem(2),
+        compiler_params=pltpu.CompilerParams(vmem_limit_bytes=VMEM_BYTES),
+        cost_estimate=pl.CostEstimate(
+            flops=rows * width, bytes_accessed=7 * rows * width, transcendentals=0
+        ),
+        name="halve",
+    )(kept, got)
+
+
+def pack_kernel(peers, capacity, chunks, carries, targets_ref, *refs):
+    terms, out_ref = refs[: 2 * chunks], refs[-1]
     targets = targets_ref[...]
     rows = targets.shape[1]
     dest = targets // rows
@@ -108,17 +124,18 @@
     slots = peers * capacity
     slot = iota((slots, rows), 0)
     chosen = jnp.logical_and(dest == slot // capacity, rank == slot % capacity)
-    total = terms_ref[0].astype(F32)
-    for term in range(1, terms_ref.shape[0]):
-        total = total + terms_ref[term].astype(F32)
-    packed = dot(chosen.astype(F32).astype(BF16), total.astype(BF16), (1, 0))
-    if first:
-        label = jnp.sum(jnp.where(chosen, local + 1, 0), axis=1, keepdims=True) - 1
-        packed = jnp.concatenate(
-            [packed, jnp.broadcast_to(label.astype(F32), (slots, LANES))], axis=1
-        )
+    selector = chosen.astype(F32).astype(BF16)
+    at = 0
+    for chunk in range(chunks):
+        kept, got = terms[2 * chunk], terms[2 * chunk + 1]
+        total = (kept[...].astype(F32) + got[...].astype(F32)).astype(BF16)
+        width = total.shape[1]
+        out_ref[:, at : at + width] = dot(selector, total, (1, 0)).astype(BF16)
+        at += width
+    label = jnp.sum(jnp.where(chosen, local + 1, 0), axis=1, keepdims=True) - 1
+    out_ref[:, at : at + LANES] = jnp.broadcast_to(label.astype(F32), (slots, LANES)).astype(BF16)
     if carries:
-        sums = refs[0][...]
+        sums = refs[2 * chunks][...]
         high = sums.astype(BF16).astype(F32)
         middle = (sums - high).astype(BF16).astype(F32)
         low = (sums - high - middle).astype(BF16).astype(F32)
@@ -128,29 +145,34 @@
         for peer in range(peers):
             for level, values in enumerate((high, middle, low)):
                 for piece in range(pieces):
-                    at = (peer * pieces + piece) * LANES
-                    line = jnp.broadcast_to(values[:, at : at + LANES], (slots, LANES))
+                    start = (peer * pieces + piece) * LANES
+                    line = jnp.broadcast_to(values[:, start : start + LANES], (slots, LANES))
                     extra = jnp.where(row == peer * capacity + level * pieces + piece, line, extra)
-        packed = jnp.concatenate([packed, extra], axis=1)
-    out_ref[...] = packed.astype(BF16)
-
-
-def pack(terms, targets, sums, peers, capacity, first, carries):
-    _, rows, width = terms.shape
-    width = width + (LANES if first else 0) + (LANES if carries else 0)
-    return pl.pallas_call(
-        functools.partial(pack_kernel, peers, capacity, first, carries),
+        out_ref[:, at + LANES : at + 2 * LANES] = extra.astype(BF16)
+
+
+def pack(terms, targets, sums, peers, capacity, carries):
+    rows = targets.shape[1]
+    width = sum(kept.shape[1] for kept, _ in terms) + (2 * LANES if carries else LANES)
+    operands = [targets] + [x for pair in terms for x in pair] + ([sums] if carries else [])
+    return pl.pallas_call(
+        functools.partial(pack_kernel, peers, capacity, len(terms), carries),
         out_shape=jax.ShapeDtypeStruct((peers * capacity, width), BF16),
-        in_specs=vmem(3 if carries else 2),
+        in_specs=vmem(len(operands)),
         out_specs=pl.BlockSpec(memory_space=pltpu.VMEM),
         compiler_params=pltpu.CompilerParams(vmem_limit_bytes=VMEM_BYTES),
         cost_estimate=pl.CostEstimate(
             flops=2 * rows * peers * capacity * width,
-            bytes_accessed=2 * (terms.shape[0] * rows + peers * capacity) * width,
+            bytes_accessed=(6 * rows + 2 * peers * capacity) * width,
             transcendentals=0,
         ),
         name="pack",
-    )(*((targets, terms, sums) if carries else (targets, terms)))
+    )(*operands)
+
+
+def swap(x, axis, mask):
+    n = lax.axis_size(axis)
+    return lax.ppermute(x, axis, [(i, i ^ mask) for i in range(n)])
 
 
 def exchange(x, axis, pieces):
@@ -204,15 +226,12 @@
     )(queries, keys, ids)
 
 
-def norm_kernel(parts, peers, copies, patches_ref, gain_ref, *refs):
-    chunk_refs, (out_ref, share_ref) = refs[:-2], refs[-2:]
+def norm_kernel(peers, copies, patches_ref, gain_ref, routed_ref, out_ref, share_ref):
     patches, width = patches_ref.shape
-    slots = chunk_refs[0].shape[0]
-    first, count = chunk_refs[0], parts[0]
-    labels = first[:, count * width : count * width + LANES].astype(F32)[:, :1]
-    columns = []
-    for ref, count in zip(chunk_refs, parts):
-        columns += [ref[:, c * width : (c + 1) * width].astype(F32) for c in range(count)]
+    slots = routed_ref.shape[0]
+    per_token = routed_ref.shape[1] // width
+    labels = routed_ref[:, per_token * width : per_token * width + LANES].astype(F32)[:, :1]
+    columns = [routed_ref[:, c * width : (c + 1) * width].astype(F32) for c in range(per_token)]
     held = jnp.concatenate(columns, axis=0).astype(BF16)
     lanes = len(columns) * slots
     lane = iota((slots, lanes), 1)
@@ -229,7 +248,7 @@
     gain_part = jnp.sum(patch_grads * normed, axis=0, keepdims=True)
     if copies:
         rows = [gain_part[:, at : at + LANES] for at in range(0, width, LANES)]
-        carried = first[:, parts[0] * width + LANES :].astype(F32)
+        carried = routed_ref[:, per_token * width + LANES :].astype(F32)
         capacity = slots // peers
         pieces = share_ref.shape[1] - len(rows)
         for piece in range(pieces):
@@ -246,22 +265,21 @@
     ).astype(BF16)
 
 
-def norm_backward(received, parts, peers, patches, gain, share):
+def norm_backward(routed, peers, patches, gain, share):
     count, width = patches.shape
-    slots = received[0].shape[0]
-    return pl.pallas_call(
-        functools.partial(norm_kernel, parts, peers, share[0] if len(share) == 3 else 0),
+    return pl.pallas_call(
+        functools.partial(norm_kernel, peers, share[0] if len(share) == 3 else 0),
         out_shape=[jax.ShapeDtypeStruct((count, width), BF16), jax.ShapeDtypeStruct(share, F32)],
-        in_specs=vmem(2 + len(received)),
+        in_specs=vmem(3),
         out_specs=vmem(2),
         compiler_params=pltpu.CompilerParams(vmem_limit_bytes=VMEM_BYTES),
         cost_estimate=pl.CostEstimate(
-            flops=2 * count * width * slots * sum(parts),
-            bytes_accessed=2 * width * (2 * count + slots * sum(parts)),
+            flops=2 * count * routed.size,
+            bytes_accessed=4 * count * width + 2 * routed.size,
             transcendentals=0,
         ),
         name="norm",
-    )(patches, gain, *received)
+    )(patches, gain, routed)
 
 
 def window_kernel(g_ref, q_ref, k_ref, v_ref, probs_ref, probs_t_ref, dq_ref, dk_ref, dv_ref):
@@ -331,26 +349,37 @@
     pieces = block // peers // LANES
     carries = pieces > 0 and 3 * pieces <= capacity
 
-    columns = grad_rows.reshape(rows, images, block).transpose(1, 0, 2)
-    x = exchange(columns, "img", images).reshape(images * rows, block)
+    order = [0]
+    while len(order) < images:
+        order = [2 * j for j in order] + [2 * j + 1 for j in order]
+    image = lax.axis_index("img")
+
+    def columns(j):
+        return lax.dynamic_slice(grad_rows, (0, (image ^ j) * block), (rows, block))
+
+    x_blocks = [columns(0)] + [swap(columns(j), "img", j) for j in range(1, images)]
+    x_blocks = [x_blocks[j] for j in order]
     probs, probs_t = window_probs(queries[0], keys[0], window_ids[0])
 
-    received, first = [], 0
+    terms, first = [], 0
     for index, count in enumerate(CHUNKS):
-        partial = project(x, w_down, first, count * width, index == 0)
+        w_rows = lax.slice_in_dim(w_down, first, first + count * width)
+        w_rows = pltpu.with_memory_space_constraint(w_rows, pltpu.VMEM)
         first += count * width
+        kept, sent, *sums = project(x_blocks, w_rows, index == 0)
         if index == 0:
-            bias_part = partial[1]
-        terms = exchange(partial[0].reshape(images, rows, -1), "img", images)
-        begins = index == 0
-        packed = pack(
-            terms, token_target, bias_part, peers, capacity, begins, begins and carries
-        )
-        received.append(exchange(packed, "seq", peers))
+            bias_part = sums[0]
+        mask = 1
+        while 2 * mask < images:
+            kept, sent = halve(kept, swap(sent, "img", mask))
+            mask *= 2
+        terms.append((kept, swap(sent, "img", mask)))
+    packed = pack(terms, token_target, bias_part, peers, capacity, carries)
+    routed = exchange(packed, "seq", peers)
 
     gain_rows = width // LANES
     share = (devices, gain_rows + pieces, LANES) if carries else (1, width)
-    out_grads, shared = norm_backward(received, CHUNKS, peers, patches[0], gain[None], share)
+    out_grads, shared = norm_backward(routed, peers, patches[0], gain[None], share)
     if carries:
         shared = exchange(shared, ("img", "seq"), devices)
         gain_total = jnp.sum(shared[:, :gain_rows], axis=0).reshape(-1)

time: 97.8 us -> 72.1 us (0.74)
  blocking collectives: 12.9 us -> 0 us
  Pallas kernels: 23.8 us -> 12.1 us
  local copies, waits for them, and re-layouts: 1.76 us -> 9.73 us
  waiting for transfers between devices: 37.6 us -> 31.2 us
  starting transfers between devices: 19.1 us -> 16.7 us
    all_to_all x5 -> x2, waiting for transfers between devices: 37.6 us -> 24.5 us  [exchange(): lax.all_to_all(x, axis, split_axis=0, concat_axis=0, tiled=True)]
    all_to_all x1 -> x0, blocking collectives: 12.9 us -> none  [exchange(): lax.all_to_all(x, axis, split_axis=0, concat_axis=0, tiled=True)]
    pallas_call x5 -> x6, Pallas kernels: 20.4 us -> 8.63 us  [the longest x2 6.02 us: project(): pl.pallas_call(functools.partial(project_kernel, blocks, tile, with_sum),...]
    all_to_all x5 -> x2, starting transfers between devices: 19.1 us -> 9.64 us  [exchange(): lax.all_to_all(x, axis, split_axis=0, concat_axis=0, tiled=True)]
    slice x0 -> x1, local copies, waits for them, and re-layouts: none -> 8.54 us  [body(): w_rows = lax.slice_in_dim(w_down, first, first + count * width)]
    ppermute x0 -> x7, starting transfers between devices: none -> 7.06 us  [swap(): return lax.ppermute(x, axis, [(i, i ^ mask) for i in range(n)])]
    ppermute x0 -> x7, waiting for transfers between devices: none -> 6.74 us  [swap(): return lax.ppermute(x, axis, [(i, i ^ mask) for i in range(n)])]
    another operation x2 -> x0, local copies, waits for them, and re-layouts: 1.73 us -> none  [body(): columns = grad_rows.reshape(rows, images, block).transpose(1, 0, 2)]
  transfers between devices with their start and end apart: 5 -> 9, of which waited for: 5 -> 4; matrix products, arithmetic and copies ran while one was open for 0% -> 12% of each run, Pallas kernels for 14% -> 9%
where the time goes in v3:
time: 72.1 us; the launch traced here: 71.8 us
  waiting for transfers between devices  31.2 us (43%)
  starting transfers between devices  16.7 us (23%)
  Pallas kernels  12.1 us (17%)
  local copies, waits for them, and re-layouts  9.73 us (13%)
  other arithmetic  1.27 us (2%)
  between operations  0.83 us (1%)
    all_to_all x2, waiting for transfers between devices, exchange(): lax.all_to_all(x, axis, split_axis=0, concat_axis=0, tiled=True)  24.5 us
    all_to_all x2, starting transfers between devices, exchange(): lax.all_to_all(x, axis, split_axis=0, concat_axis=0, tiled=True)  9.64 us
    slice x1, local copies, waits for them, and re-layouts, body(): w_rows = lax.slice_in_dim(w_down, first, first + count * width)  8.54 us
    ppermute x7, starting transfers between devices, swap(): return lax.ppermute(x, axis, [(i, i ^ mask) for i in range(n)])  7.06 us
    ppermute x7, waiting for transfers between devices, swap(): return lax.ppermute(x, axis, [(i, i ^ mask) for i in range(n)])  6.74 us
    pallas_call x2, Pallas kernels, project(): pl.pallas_call(functools.partial(project_kernel, blocks, tile, with_sum),...  6.02 us
    pallas_call x1, Pallas kernels, window_backward(): pl.pallas_call(window_kernel, out_shape=[shape] * 3, in_specs=vmem(6), ou...  2.42 us
  transfers between devices with their start and end apart: 9, of which 4 were waited for; matrix products, arithmetic and copies ran while one was open for 12% of the time, Pallas kernels for 9%

profile of v3, /device:TPU:0, one launch (start us, length us, event | category | flops | bytes accessed | tf_op | source)
XLA Modules:
  0.0 71.8 jit_solution(10919284831912072198)
XLA Ops:
  0.7 1.1 %dynamic-slice_bitcast_fusion = (bf16[32,2048]{1,0:T(8,128)(2,1)S(1)}, bf16[32,2048]{1,0:T(8,128)(2,1)S(1)}, bf16[32,2048]{1,0:T(8,128)(2,1)S(1)}, bf16[32,2048]{1,0:T(8,128)(2,1)S(1)}) fusion(bf16[1,32,8192]{2,1,0:T(8,128)(2,1)} %param.9, s32[]{:T(128)S(6)} %select_n.15, s32[]{:T(128)S(6)} %select_n.13, s32[]{:T(128)S(6)} %select_n.12, s32[]{:T(128)S(6)} %select_n.14), kind=kLoop, calls=%fused_computation.1 | loop fusion | bytes 1048592 | tf_op jit(solution)/shard_map/dynamic_slice | solution.py:358
  1.8 3.0 %collective-permute-start = (bf16[32,2048]{1,0:T(8,128)(2,1)S(1)}, bf16[32,2048]{1,0:T(8,128)(2,1)S(1)}, u32[]{:S(2)}, u32[]{:S(2)}) collective-permute-start(bf16[32,2048]{1,0:T(8,128)(2,1)S(1)} %get-tuple-element.40), channel_id=1, source_target_pairs={{0,16},{8,24},{16,0},{24,8},{1,17},{9,25},{17,1},{25,9},{2,18},{10... | collective-permute-start | bytes 393224 | tf_op jit(solution)/shard_map/ppermute | solution.py:175
  4.8 0.0 collective-permute-start.1
  4.8 0.2 collective-permute-start.2
  5.0 8.5 %fusion = (bf16[2560,2048]{1,0:T(8,128)(2,1)S(1)}, bf16[2560,2048]{1,0:T(8,128)(2,1)S(1)}) fusion(bf16[5120,2048]{1,0:T(8,128)(2,1)} %param.13), kind=kLoop, calls=%fused_computation.7 | loop fusion | bytes 41943040 | tf_op jit(solution)/shard_map/slice | solution.py:366
  13.6 0.0 collective-permute-done.refs_1_
  13.6 0.0 collective-permute-done.1.refs_2_
  13.6 0.0 collective-permute-done.2.refs_3_
  13.6 0.0 copy-start.4
  13.6 0.0 copy-start.6
  13.6 0.0 copy-start
  13.7 3.0 %project.3 = (bf16[64,2560]{1,0:T(8,128)(2,1)S(1)}, bf16[64,2560]{1,0:T(8,128)(2,1)S(1)}) custom-call(bf16[32,2048]{1,0:T(8,128)(2,1)S(1)} %get-tuple-element.41.refs_0_, bf16[32,2048]{1,0:T(8,128)(2,1)S(1)} %collective-permute-done.refs_1_, bf16[32,2048]{1,0:T(8,128)(2,1)S(1)} %collective-permute-done.1.refs_2_, ...), custom_call_target="tpu_custom_call" | custom-call | flops 1342177280 | bytes 10485760 | tf_op jit(solution)/shard_map/project/pallas_call | solution.py:74
  16.6 0.0 copy-start.1
  16.7 0.0 copy-start.2
  16.7 0.0 copy-start.5
  16.7 0.0 copy-start.3
  16.7 0.4 collective-permute-start.5
  17.1 3.0 %project.2 = (bf16[64,2560]{1,0:T(8,128)(2,1)S(1)}, bf16[64,2560]{1,0:T(8,128)(2,1)S(1)}, f32[1,2048]{1,0:T(1,128)S(1)}) custom-call(bf16[32,2048]{1,0:T(8,128)(2,1)S(1)} %get-tuple-element.41.refs_0_, bf16[32,2048]{1,0:T(8,128)(2,1)S(1)} %collective-permute-done.refs_1_, bf16[32,2048]{1,0:T(8,128)(2,1)S(1)} %collective-permute-done.1.refs_2_, ...), custom_call_target="tpu_custom_call" | custom-call | flops 1342177280 | bytes 10485760 | tf_op jit(solution)/shard_map/project/pallas_call | solution.py:74
  20.1 0.3 collective-permute-start.3
  20.4 0.0 collective-permute-done.5.got_ref
  20.4 0.1 halve.3
  20.5 2.0 %collective-permute-start.6 = (bf16[32,2560]{1,0:T(8,128)(2,1)S(1)}, bf16[32,2560]{1,0:T(8,128)(2,1)S(1)}, u32[]{:S(2)}, u32[]{:S(2)}) collective-permute-start(bf16[32,2560]{1,0:T(8,128)(2,1)S(1)} %get-tuple-element.28), channel_id=1, source_target_pairs={{0,16},{8,24},{16,0},{24,8},{1,17},{9,25},{17,1},{25,9},{2,18},{10... | collective-permute-start | bytes 491528 | tf_op jit(solution)/shard_map/ppermute | solution.py:175
  22.5 0.0 collective-permute-done.3.got_ref
  22.5 0.1 halve.2
  22.5 1.2 %collective-permute-start.4 = (bf16[32,2560]{1,0:T(8,128)(2,1)S(1)}, bf16[32,2560]{1,0:T(8,128)(2,1)S(1)}, u32[]{:S(2)}, u32[]{:S(2)}) collective-permute-start(bf16[32,2560]{1,0:T(8,128)(2,1)S(1)} %get-tuple-element.24), channel_id=1, source_target_pairs={{0,16},{8,24},{16,0},{24,8},{1,17},{9,25},{17,1},{25,9},{2,18},{10... | collective-permute-start | bytes 491528 | tf_op jit(solution)/shard_map/ppermute | solution.py:175
  23.7 3.8 %collective-permute-done.6.refs_3_ = bf16[32,2560]{1,0:T(8,128)(2,1)S(1)} collective-permute-done((bf16[32,2560]{1,0:T(8,128)(2,1)S(1)}, bf16[32,2560]{1,0:T(8,128)(2,1)S(1)}, u32[]{:S(2)}, u32[]{:S(2)}) %collective-permute-start.6) | collective-permute-done | bytes 163872 | tf_op jit(solution)/shard_map/ppermute | solution.py:175
  27.6 2.9 %collective-permute-done.4.refs_1_ = bf16[32,2560]{1,0:T(8,128)(2,1)S(1)} collective-permute-done((bf16[32,2560]{1,0:T(8,128)(2,1)S(1)}, bf16[32,2560]{1,0:T(8,128)(2,1)S(1)}, u32[]{:S(2)}, u32[]{:S(2)}) %collective-permute-start.4) | collective-permute-done | bytes 163872 | tf_op jit(solution)/shard_map/ppermute | solution.py:175
  30.4 0.0 copy-done.4
  30.4 1.3 %pack.1 = bf16[64,5376]{1,0:T(8,128)(2,1)} custom-call(s32[1,32]{1,0:T(1,128)S(1)} %copy-done.4, f32[32,2560]{1,0:T(8,128)S(1)} %get-tuple-element.23.refs_0_, bf16[32,2560]{1,0:T(8,128)(2,1)S(1)} %collective-permute-done.4.refs_1_, f32[32,2560]{1,0:T(8,128)S(1)} %get-tuple-element.27.refs_2_, bf16[32,2560]{1,0:T(8,128)(2,1)S(1)} %collective-permute-done.6.refs_3_, ...), custom_call_target="tpu_custom_call" | custom-call | flops 22020096 | bytes 1720320 | tf_op jit(solution)/shard_map/pack/pallas_call | solution.py:158
  31.7 5.9 %all-to-all-start = ((bf16[8,8,5376]{2,1,0:T(8,128)(2,1)}), bf16[8,8,5376]{2,1,0:T(8,128)(2,1)S(1)}, u32[]{:S(2)}, u32[]{:S(2)}) async-start(bf16[8,8,5376]{2,1,0:T(8,128)(2,1)} %bitcast.5), calls=%async_computation | async-start | bytes 1376256 | tf_op jit(solution)/shard_map/all_to_all | solution.py:182
  37.7 0.0 copy-done.6
  37.7 17.3 %all-to-all-done = bf16[8,8,5376]{2,1,0:T(8,128)(2,1)S(1)} async-done(((bf16[8,8,5376]{2,1,0:T(8,128)(2,1)}), bf16[8,8,5376]{2,1,0:T(8,128)(2,1)S(1)}, u32[]{:S(2)}, u32[]{:S(2)}) %all-to-all-start) | async-done | bytes 688160 | tf_op jit(solution)/shard_map/all_to_all | solution.py:182
  55.0 0.0 copy-done
  55.0 1.2 %norm.1 = (bf16[128,1280]{1,0:T(8,128)(2,1)S(1)}, f32[32,12,128]{2,1,0:T(8,128)}) custom-call(bf16[128,1280]{1,0:T(8,128)(2,1)S(1)} %bitcast.22, f32[1,1280]{1,0:T(1,128)S(1)} %broadcast_in_dim.12.gain_ref, bf16[64,5376]{1,0:T(8,128)(2,1)S(1)} %bitcast.21), custom_call_target="tpu_custom_call" | custom-call | flops 88080384 | bytes 1343488 | tf_op jit(solution)/shard_map/norm/pallas_call | solution.py:270
  56.2 3.7 %all-to-all-start.1 = ((f32[32,12,128]{2,1,0:T(8,128)}), f32[32,12,128]{2,1,0:T(8,128)S(1)}, u32[]{:S(2)}, u32[]{:S(2)}) async-start(f32[32,12,128]{2,1,0:T(8,128)} %get-tuple-element.36), calls=%async_computation.1 | async-start | bytes 524288 | tf_op jit(solution)/shard_map/all_to_all | solution.py:182
  59.9 0.0 copy-done.1
  59.9 0.0 copy-done.2
  59.9 0.0 copy-done.5
  60.0 1.1 %probs.1 = (f32[16,128,128]{2,1,0:T(8,128)S(1)}, f32[16,128,128]{2,1,0:T(8,128)S(1)}) custom-call(bf16[128,1280]{1,0:T(8,128)(2,1)S(1)} %bitcast.23, bf16[128,1280]{1,0:T(8,128)(2,1)S(1)} %bitcast.25, s32[1,32]{1,0:T(1,128)S(1)} %bitcast.28), custom_call_target="tpu_custom_call" | custom-call | flops 268435456 | bytes 2097152 | tf_op jit(solution)/shard_map/probs/pallas_call | solution.py:214
  61.0 0.0 copy-done.3
  61.0 2.4 %window.1 = (bf16[128,1280]{1,0:T(8,128)(2,1)}, bf16[128,1280]{1,0:T(8,128)(2,1)}, bf16[128,1280]{1,0:T(8,128)(2,1)}) custom-call(bf16[128,1280]{1,0:T(8,128)(2,1)S(1)} %get-tuple-element.30.g_ref, bf16[128,1280]{1,0:T(8,128)(2,1)S(1)} %bitcast.24, bf16[128,1280]{1,0:T(8,128)(2,1)S(1)} %bitcast.26, bf16[128,1280]{1,0:T(8,128)(2,1)S(1)} %bitcast.27, ...), custom_call_target="tpu_custom_call" | custom-call | flops 335544320 | bytes 4390912 | tf_op jit(solution)/shard_map/window/pallas_call | solution.py:326
  63.5 7.1 %all-to-all-done.1 = f32[32,12,128]{2,1,0:T(8,128)S(1)} async-done(((f32[32,12,128]{2,1,0:T(8,128)}), f32[32,12,128]{2,1,0:T(8,128)S(1)}, u32[]{:S(2)}, u32[]{:S(2)}) %all-to-all-start.1) | async-done | bytes 196640 | tf_op jit(solution)/shard_map/all_to_all | solution.py:182
  70.6 0.6 multiply_bitcast_fusion
  71.2 0.6 slice_multiply_fusion
  (2 shorter events, 0.0 us)
Async XLA Ops:
  1.8 11.8 %collective-permute-start = (bf16[32,2048]{1,0:T(8,128)(2,1)S(1)}, bf16[32,2048]{1,0:T(8,128)(2,1)S(1)}, u32[]{:S(2)}, u32[]{:S(2)}) collective-permute-start(bf16[32,2048]{1,0:T(8,128)(2,1)S(1)} %get-tuple-element.40), channel_id=1, source_target_pairs={{0,16},{8,24},{16,0},{24,8},{1,17},{9,25},{17,1},{25,9},{2,18},{10... | collective-permute-start | bytes 393224 | tf_op jit(solution)/shard_map/ppermute | solution.py:175
  4.8 8.8 %collective-permute-start.1 = (bf16[32,2048]{1,0:T(8,128)(2,1)S(1)}, bf16[32,2048]{1,0:T(8,128)(2,1)S(1)}, u32[]{:S(2)}, u32[]{:S(2)}) collective-permute-start(bf16[32,2048]{1,0:T(8,128)(2,1)S(1)} %get-tuple-element.42), channel_id=1, source_target_pairs={{0,8},{8,0},{16,24},{24,16},{1,9},{9,1},{17,25},{25,17},{2,10},{10... | collective-permute-start | bytes 393224 | tf_op jit(solution)/shard_map/ppermute | solution.py:175
  4.8 8.8 %collective-permute-start.2 = (bf16[32,2048]{1,0:T(8,128)(2,1)S(1)}, bf16[32,2048]{1,0:T(8,128)(2,1)S(1)}, u32[]{:S(2)}, u32[]{:S(2)}) collective-permute-start(bf16[32,2048]{1,0:T(8,128)(2,1)S(1)} %get-tuple-element.39), channel_id=1, source_target_pairs={{0,24},{8,16},{16,8},{24,0},{1,25},{9,17},{17,9},{25,1},{2,26},{10... | collective-permute-start | bytes 393224 | tf_op jit(solution)/shard_map/ppermute | solution.py:175
  13.6 16.8 %copy-start.4 = (s32[1,32]{1,0:T(1,128)S(1)}, s32[1,32]{1,0:T(1,128)}, u32[]{:S(2)}) copy-start(s32[1,32]{1,0:T(1,128)} %targets_ref.1) | copy-start | bytes 388
  13.6 24.0 %copy-start.6 = (f32[1280]{0:T(1024)S(1)}, f32[1280]{0:T(1024)}, u32[]{:S(2)}) copy-start(f32[1280]{0:T(1024)} %param.12) | copy-start | bytes 15364
  13.6 41.4 %copy-start = (bf16[1,128,1280]{2,1,0:T(8,128)(2,1)S(1)}, bf16[1,128,1280]{2,1,0:T(8,128)(2,1)}, u32[]{:S(2)}) copy-start(bf16[1,128,1280]{2,1,0:T(8,128)(2,1)} %param.11) | copy-start | bytes 983044
  16.6 43.3 %copy-start.1 = (bf16[1,128,1280]{2,1,0:T(8,128)(2,1)S(1)}, bf16[1,128,1280]{2,1,0:T(8,128)(2,1)}, u32[]{:S(2)}) copy-start(bf16[1,128,1280]{2,1,0:T(8,128)(2,1)} %param.14) | copy-start | bytes 983044
  16.7 43.3 %copy-start.2 = (bf16[1,128,1280]{2,1,0:T(8,128)(2,1)S(1)}, bf16[1,128,1280]{2,1,0:T(8,128)(2,1)}, u32[]{:S(2)}) copy-start(bf16[1,128,1280]{2,1,0:T(8,128)(2,1)} %param.15) | copy-start | bytes 983044
  16.7 43.3 %copy-start.5 = (s32[1,1,32]{2,1,0:T(1,128)S(1)}, s32[1,1,32]{2,1,0:T(1,128)}, u32[]{:S(2)}) copy-start(s32[1,1,32]{2,1,0:T(1,128)} %param.17) | copy-start | bytes 388
  16.7 44.4 %copy-start.3 = (bf16[1,128,1280]{2,1,0:T(8,128)(2,1)S(1)}, bf16[1,128,1280]{2,1,0:T(8,128)(2,1)}, u32[]{:S(2)}) copy-start(bf16[1,128,1280]{2,1,0:T(8,128)(2,1)} %param.16) | copy-start | bytes 983044
  16.7 3.7 %collective-permute-start.5 = (bf16[64,2560]{1,0:T(8,128)(2,1)S(1)}, bf16[64,2560]{1,0:T(8,128)(2,1)S(1)}, u32[]{:S(2)}, u32[]{:S(2)}) collective-permute-start(bf16[64,2560]{1,0:T(8,128)(2,1)S(1)} %get-tuple-element.26), channel_id=1, source_target_pairs={{0,8},{8,0},{16,24},{24,16},{1,9},{9,1},{17,25},{25,17},{2,10},{10... | collective-permute-start | bytes 983048 | tf_op jit(solution)/shard_map/ppermute | solution.py:175
  20.1 2.3 %collective-permute-start.3 = (bf16[64,2560]{1,0:T(8,128)(2,1)S(1)}, bf16[64,2560]{1,0:T(8,128)(2,1)S(1)}, u32[]{:S(2)}, u32[]{:S(2)}) collective-permute-start(bf16[64,2560]{1,0:T(8,128)(2,1)S(1)} %get-tuple-element.22), channel_id=1, source_target_pairs={{0,8},{8,0},{16,24},{24,16},{1,9},{9,1},{17,25},{25,17},{2,10},{10... | collective-permute-start | bytes 983048 | tf_op jit(solution)/shard_map/ppermute | solution.py:175
  20.5 7.1 %collective-permute-start.6 = (bf16[32,2560]{1,0:T(8,128)(2,1)S(1)}, bf16[32,2560]{1,0:T(8,128)(2,1)S(1)}, u32[]{:S(2)}, u32[]{:S(2)}) collective-permute-start(bf16[32,2560]{1,0:T(8,128)(2,1)S(1)} %get-tuple-element.28), channel_id=1, source_target_pairs={{0,16},{8,24},{16,0},{24,8},{1,17},{9,25},{17,1},{25,9},{2,18},{10... | collective-permute-start | bytes 491528 | tf_op jit(solution)/shard_map/ppermute | solution.py:175
  22.5 7.9 %collective-permute-start.4 = (bf16[32,2560]{1,0:T(8,128)(2,1)S(1)}, bf16[32,2560]{1,0:T(8,128)(2,1)S(1)}, u32[]{:S(2)}, u32[]{:S(2)}) collective-permute-start(bf16[32,2560]{1,0:T(8,128)(2,1)S(1)} %get-tuple-element.24), channel_id=1, source_target_pairs={{0,16},{8,24},{16,0},{24,8},{1,17},{9,25},{17,1},{25,9},{2,18},{10... | collective-permute-start | bytes 491528 | tf_op jit(solution)/shard_map/ppermute | solution.py:175
  31.7 23.3 %all-to-all-start = ((bf16[8,8,5376]{2,1,0:T(8,128)(2,1)}), bf16[8,8,5376]{2,1,0:T(8,128)(2,1)S(1)}, u32[]{:S(2)}, u32[]{:S(2)}) async-start(bf16[8,8,5376]{2,1,0:T(8,128)(2,1)} %bitcast.5), calls=%async_computation | async-start | bytes 1376256 | tf_op jit(solution)/shard_map/all_to_all | solution.py:182
  56.2 14.3 %all-to-all-start.1 = ((f32[32,12,128]{2,1,0:T(8,128)}), f32[32,12,128]{2,1,0:T(8,128)S(1)}, u32[]{:S(2)}, u32[]{:S(2)}) async-start(f32[32,12,128]{2,1,0:T(8,128)} %get-tuple-element.36), calls=%async_computation.1 | async-start | bytes 524288 | tf_op jit(solution)/shard_map/all_to_all | solution.py:182

commit v4 on v3

--- a/solution.py
+++ b/solution.py
@@ -12,7 +12,8 @@
 HEAD_DIM = 80
 LANES = 128
 CHUNKS = (2, 2)
-VMEM_BYTES = 24 * 1024 * 1024
+DIRECT = 8
+VMEM_BYTES = 32 * 1024 * 1024
 
 F32 = jnp.float32
 BF16 = jnp.bfloat16
@@ -48,34 +49,44 @@
     return jnp.where(lane_mask(low, high, start, stop), x, jnp.zeros_like(x))
 
 
-def project_kernel(blocks, tile, with_sum, *refs):
+def project_kernel(blocks, first, tile, tiles, with_sum, *refs):
     x_refs, w_ref = refs[:blocks], refs[blocks]
     keep_ref, send_ref = refs[blocks + 1 : blocks + 3]
+    w_tiles, sems = refs[-2:]
+    copies = [
+        pltpu.make_async_copy(w_ref.at[pl.ds(first + t * tile, tile)], w_tiles.at[t], sems.at[t])
+        for t in range(tiles)
+    ]
+    for t, copy in enumerate(copies):
+        copy.start(priority=t % 2)
     x = jnp.concatenate([ref[...] for ref in x_refs], axis=0)
     if with_sum:
         refs[blocks + 3][...] = dot(jnp.ones((16, x.shape[0]), BF16), x, (1, 0))[:1]
     x = x.T
     half = keep_ref.shape[0]
-    for t in range(0, w_ref.shape[0], tile):
-        product = dot(w_ref[t : t + tile], x, (1, 0)).T.astype(BF16)
-        keep_ref[:, t : t + tile] = product[:half]
-        send_ref[:, t : t + tile] = product[half:]
-
-
-def project(x_blocks, w_rows, with_sum):
+    for t in range(tiles):
+        copies[t].wait()
+        product = dot(w_tiles[t], x, (1, 0)).T.astype(BF16)
+        keep_ref[:, t * tile : (t + 1) * tile] = product[:half]
+        send_ref[:, t * tile : (t + 1) * tile] = product[half:]
+
+
+def project(x_blocks, w_down, first, width, with_sum):
     blocks, (rows, depth) = len(x_blocks), x_blocks[0].shape
-    width = w_rows.shape[0]
-    tile = 512
-    while width % tile:
-        tile //= 2
+    tile = 256
+    tiles = width // tile
     out_shape = [jax.ShapeDtypeStruct((blocks * rows // 2, width), BF16)] * 2
     if with_sum:
         out_shape = out_shape + [jax.ShapeDtypeStruct((1, depth), F32)]
     return pl.pallas_call(
-        functools.partial(project_kernel, blocks, tile, with_sum),
+        functools.partial(project_kernel, blocks, first, tile, tiles, with_sum),
         out_shape=out_shape,
-        in_specs=vmem(blocks + 1),
+        in_specs=vmem(blocks) + [pl.BlockSpec(memory_space=pl.ANY)],
         out_specs=vmem(len(out_shape)),
+        scratch_shapes=[
+            pltpu.VMEM((tiles, tile, depth), BF16),
+            pltpu.SemaphoreType.DMA((tiles,)),
+        ],
         compiler_params=pltpu.CompilerParams(vmem_limit_bytes=VMEM_BYTES),
         cost_estimate=pl.CostEstimate(
             flops=2 * blocks * rows * depth * width,
@@ -83,7 +94,7 @@
             transcendentals=0,
         ),
         name="project",
-    )(*x_blocks, w_rows)
+    )(*x_blocks, w_down)
 
 
 def halve_kernel(kept_ref, got_ref, keep_ref, send_ref):
@@ -110,12 +121,11 @@
     )(kept, got)
 
 
-def pack_kernel(peers, capacity, chunks, carries, targets_ref, *refs):
+def pack_kernel(peers, capacity, chunks, targets_ref, *refs):
     terms, out_ref = refs[: 2 * chunks], refs[-1]
     targets = targets_ref[...]
     rows = targets.shape[1]
     dest = targets // rows
-    local = targets - dest * rows
     dest_column = jnp.sum(
         jnp.where(iota((rows, rows), 0) == iota((rows, rows), 1), dest, 0), axis=1, keepdims=True
     )
@@ -132,31 +142,14 @@
         width = total.shape[1]
         out_ref[:, at : at + width] = dot(selector, total, (1, 0)).astype(BF16)
         at += width
-    label = jnp.sum(jnp.where(chosen, local + 1, 0), axis=1, keepdims=True) - 1
-    out_ref[:, at : at + LANES] = jnp.broadcast_to(label.astype(F32), (slots, LANES)).astype(BF16)
-    if carries:
-        sums = refs[2 * chunks][...]
-        high = sums.astype(BF16).astype(F32)
-        middle = (sums - high).astype(BF16).astype(F32)
-        low = (sums - high - middle).astype(BF16).astype(F32)
-        extra = jnp.zeros((slots, LANES), F32)
-        row = iota((slots, LANES), 0)
-        pieces = sums.shape[1] // peers // LANES
-        for peer in range(peers):
-            for level, values in enumerate((high, middle, low)):
-                for piece in range(pieces):
-                    start = (peer * pieces + piece) * LANES
-                    line = jnp.broadcast_to(values[:, start : start + LANES], (slots, LANES))
-                    extra = jnp.where(row == peer * capacity + level * pieces + piece, line, extra)
-        out_ref[:, at + LANES : at + 2 * LANES] = extra.astype(BF16)
-
-
-def pack(terms, targets, sums, peers, capacity, carries):
+
+
+def pack(terms, targets, peers, capacity):
     rows = targets.shape[1]
-    width = sum(kept.shape[1] for kept, _ in terms) + (2 * LANES if carries else LANES)
-    operands = [targets] + [x for pair in terms for x in pair] + ([sums] if carries else [])
-    return pl.pallas_call(
-        functools.partial(pack_kernel, peers, capacity, len(terms), carries),
+    width = sum(kept.shape[1] for kept, _ in terms)
+    operands = [targets] + [x for pair in terms for x in pair]
+    return pl.pallas_call(
+        functools.partial(pack_kernel, peers, capacity, len(terms)),
         out_shape=jax.ShapeDtypeStruct((peers * capacity, width), BF16),
         in_specs=vmem(len(operands)),
         out_specs=pl.BlockSpec(memory_space=pltpu.VMEM),
@@ -168,6 +161,78 @@
         ),
         name="pack",
     )(*operands)
+
+
+def spread_kernel(capacity, me_ref, targets_ref, patches_ref, out_ref, labels_ref):
+    targets = targets_ref[:, 0, :]
+    peers, rows = targets.shape
+    dest = targets // rows
+    local = (targets - dest * rows).astype(F32).astype(BF16)
+    mine = (dest == me_ref[0]).astype(F32).astype(BF16)
+    earlier = (iota((rows, rows), 0) < iota((rows, rows), 1)).astype(F32).astype(BF16)
+    rank = dot(mine, earlier, (1, 0)).astype(BF16)
+    slots = peers * capacity
+    holder = (iota((slots, peers), 0) // capacity == iota((slots, peers), 1)).astype(F32).astype(BF16)
+    mine, rank, local = (dot(holder, x, (1, 0)) for x in (mine, rank, local))
+    place = (iota((slots, rows), 0) % capacity).astype(F32)
+    chosen = jnp.logical_and(mine == 1.0, rank == place)
+    label = jnp.sum(jnp.where(chosen, local + 1.0, 0.0), axis=1, keepdims=True) - 1.0
+    labels_ref[...] = jnp.broadcast_to(label, (slots, LANES))
+    patches, width = patches_ref.shape
+    per_token = patches // rows
+    label = label.astype(jnp.int32)
+    held = patches_ref[...]
+    for c in range(per_token):
+        wanted = jnp.where(label < 0, -1, label * per_token + c)
+        selector = (wanted == iota((slots, patches), 1)).astype(F32).astype(BF16)
+        out_ref[:, c * width : (c + 1) * width] = dot(selector, held, (1, 0)).astype(BF16)
+
+
+def spread(me, targets, patches, capacity):
+    peers, _, rows = targets.shape
+    count, width = patches.shape
+    slots, wide = peers * capacity, count // rows * width
+    return pl.pallas_call(
+        functools.partial(spread_kernel, capacity),
+        out_shape=[
+            jax.ShapeDtypeStruct((slots, wide), BF16),
+            jax.ShapeDtypeStruct((slots, LANES), F32),
+        ],
+        in_specs=[pl.BlockSpec(memory_space=pltpu.SMEM)] + vmem(2),
+        out_specs=vmem(2),
+        compiler_params=pltpu.CompilerParams(vmem_limit_bytes=VMEM_BYTES),
+        cost_estimate=pl.CostEstimate(
+            flops=2 * count * slots * wide,
+            bytes_accessed=2 * (count * width + slots * wide),
+            transcendentals=0,
+        ),
+        name="spread",
+    )(me, targets, patches)
+
+
+def share_kernel(width, packed_ref, patches_ref, sums_ref, out_ref):
+    total = jnp.zeros((1, width), F32)
+    for at in range(0, packed_ref.shape[1], width):
+        inputs = patches_ref[:, at : at + width].astype(F32)
+        inverse_rms = lax.rsqrt(jnp.mean(inputs * inputs, axis=1, keepdims=True) + 1e-06)
+        terms = packed_ref[:, at : at + width].astype(F32) * (inputs * inverse_rms)
+        total = total + jnp.sum(terms, axis=0, keepdims=True)
+    out_ref[:, :width] = total
+    out_ref[:, width:] = sums_ref[...]
+
+
+def gain_and_bias_share(packed, patches, sums, width):
+    return pl.pallas_call(
+        functools.partial(share_kernel, width),
+        out_shape=jax.ShapeDtypeStruct((1, width + sums.shape[1]), F32),
+        in_specs=vmem(3),
+        out_specs=pl.BlockSpec(memory_space=pltpu.VMEM),
+        compiler_params=pltpu.CompilerParams(vmem_limit_bytes=VMEM_BYTES),
+        cost_estimate=pl.CostEstimate(
+            flops=6 * packed.size, bytes_accessed=4 * packed.size, transcendentals=0
+        ),
+        name="share",
+    )(packed, patches, sums)
 
 
 def swap(x, axis, mask):
@@ -226,52 +291,39 @@
     )(queries, keys, ids)
 
 
-def norm_kernel(peers, copies, patches_ref, gain_ref, routed_ref, out_ref, share_ref):
+def norm_kernel(patches_ref, gain_ref, labels_ref, routed_ref, out_ref):
     patches, width = patches_ref.shape
     slots = routed_ref.shape[0]
     per_token = routed_ref.shape[1] // width
-    labels = routed_ref[:, per_token * width : per_token * width + LANES].astype(F32)[:, :1]
     columns = [routed_ref[:, c * width : (c + 1) * width].astype(F32) for c in range(per_token)]
     held = jnp.concatenate(columns, axis=0).astype(BF16)
-    lanes = len(columns) * slots
+    lanes = per_token * slots
     lane = iota((slots, lanes), 1)
     row_of_lane = jnp.sum(
-        jnp.where(lane % slots == iota((slots, lanes), 0), labels, 0.0), axis=0, keepdims=True
+        jnp.where(lane % slots == iota((slots, lanes), 0), labels_ref[:, :1], 0.0),
+        axis=0,
+        keepdims=True,
     ).astype(jnp.int32)
-    patch_of_lane = row_of_lane * len(columns) + iota((1, lanes), 1) // slots
+    patch_of_lane = row_of_lane * per_token + iota((1, lanes), 1) // slots
     patch_of_lane = jnp.where(row_of_lane < 0, -1, patch_of_lane)
     chosen = patch_of_lane == iota((patches, lanes), 0)
     patch_grads = dot(chosen.astype(F32).astype(BF16), held, (1, 0))
     inputs = patches_ref[...].astype(F32)
     inverse_rms = lax.rsqrt(jnp.mean(inputs * inputs, axis=1, keepdims=True) + 1e-06)
     normed = inputs * inverse_rms
-    gain_part = jnp.sum(patch_grads * normed, axis=0, keepdims=True)
-    if copies:
-        rows = [gain_part[:, at : at + LANES] for at in range(0, width, LANES)]
-        carried = routed_ref[:, per_token * width + LANES :].astype(F32)
-        capacity = slots // peers
-        pieces = share_ref.shape[1] - len(rows)
-        for piece in range(pieces):
-            kept = iota((slots, LANES), 0) % capacity % pieces == piece
-            kept = jnp.logical_and(kept, iota((slots, LANES), 0) % capacity < 3 * pieces)
-            rows.append(jnp.sum(jnp.where(kept, carried, 0.0), axis=0, keepdims=True))
-        for at, row in enumerate(rows):
-            share_ref[:, at : at + 1, :] = jnp.broadcast_to(row[None], (copies, 1, LANES))
-    else:
-        share_ref[...] = gain_part
     scaled = gain_ref[...] * patch_grads
     out_ref[...] = (
         inverse_rms * (scaled - normed * jnp.mean(scaled * normed, axis=1, keepdims=True))
     ).astype(BF16)
 
 
-def norm_backward(routed, peers, patches, gain, share):
+def norm_backward(routed, labels, patches, gain):
     count, width = patches.shape
     return pl.pallas_call(
-        functools.partial(norm_kernel, peers, share[0] if len(share) == 3 else 0),
-        out_shape=[jax.ShapeDtypeStruct((count, width), BF16), jax.ShapeDtypeStruct(share, F32)],
-        in_specs=vmem(3),
-        out_specs=vmem(2),
+        norm_kernel,
+        out_shape=jax.ShapeDtypeStruct((count, width), BF16),
+        in_specs=vmem(4),
+        out_specs=pl.BlockSpec(memory_space=pltpu.VMEM),
         compiler_params=pltpu.CompilerParams(vmem_limit_bytes=VMEM_BYTES),
         cost_estimate=pl.CostEstimate(
             flops=2 * count * routed.size,
@@ -279,7 +331,7 @@
             transcendentals=0,
         ),
         name="norm",
-    )(patches, gain, routed)
+    )(patches, gain, labels, routed)
 
 
 def window_kernel(g_ref, q_ref, k_ref, v_ref, probs_ref, probs_t_ref, dq_ref, dk_ref, dv_ref):
@@ -338,35 +390,71 @@
     )(out_grads, queries, keys, values, probs, probs_t)
 
 
+def finish_kernel(blocks, width, image_ref, *refs):
+    shares, (gain_ref, bias_ref) = refs[:blocks], refs[blocks:]
+    gains = [ref[:, :width] for ref in shares]
+    while len(gains) > 1:
+        gains = [gains[i] + gains[i + 1] for i in range(0, len(gains), 2)]
+    gain_ref[...] = gains[0]
+    for j in range(blocks):
+        bias_ref[pl.ds(image_ref[0] ^ j, 1), :] = shares[j][:, width:]
+
+
+def sum_shares(share, width):
+    images, peers = lax.axis_size("img"), lax.axis_size("seq")
+    block = share.shape[1] - width
+    if max(images, peers) > DIRECT:
+        gain = lax.psum(share[0, :width], ("img", "seq"))
+        bias = lax.all_gather(lax.psum(share[0, width:], "seq"), "img", tiled=True)
+        return gain, bias
+    mask = 1
+    while mask < peers:
+        share = share + swap(share, "seq", mask)
+        mask *= 2
+    shares = [share] + [swap(share, "img", j) for j in range(1, images)]
+    gain, bias = pl.pallas_call(
+        functools.partial(finish_kernel, images, width),
+        out_shape=[
+            jax.ShapeDtypeStruct((1, width), F32),
+            jax.ShapeDtypeStruct((images, block), F32),
+        ],
+        in_specs=[pl.BlockSpec(memory_space=pltpu.SMEM)] + vmem(images),
+        out_specs=vmem(2),
+        name="finish",
+    )(lax.axis_index("img").reshape(1), *shares)
+    return gain[0], bias.reshape(-1)
+
+
 def body(llm_grads, token_target, patches, gain, w_down, queries, keys, values, window_ids):
     grad_rows = llm_grads[0]
     rows = grad_rows.shape[0]
     images, peers = lax.axis_size("img"), lax.axis_size("seq")
-    devices = images * peers
+    image, me = lax.axis_index("img"), lax.axis_index("seq")
     capacity = max(1, 2 * rows // peers)
     block = w_down.shape[1]
     width = patches.shape[2]
-    pieces = block // peers // LANES
-    carries = pieces > 0 and 3 * pieces <= capacity
 
     order = [0]
     while len(order) < images:
         order = [2 * j for j in order] + [2 * j + 1 for j in order]
-    image = lax.axis_index("img")
 
     def columns(j):
         return lax.dynamic_slice(grad_rows, (0, (image ^ j) * block), (rows, block))
 
     x_blocks = [columns(0)] + [swap(columns(j), "img", j) for j in range(1, images)]
-    x_blocks = [x_blocks[j] for j in order]
+
+    targets = exchange(jnp.broadcast_to(token_target[None], (peers, 1, rows)), "seq", peers)
+    spread_patches, labels = spread(me.reshape(1), targets, patches[0], capacity)
+    slot_patches = exchange(spread_patches, "seq", peers)
     probs, probs_t = window_probs(queries[0], keys[0], window_ids[0])
+    x_blocks, spread_patches = lax.optimization_barrier((x_blocks, spread_patches))
 
     terms, first = [], 0
     for index, count in enumerate(CHUNKS):
-        w_rows = lax.slice_in_dim(w_down, first, first + count * width)
-        w_rows = pltpu.with_memory_space_constraint(w_rows, pltpu.VMEM)
+        kept, sent, *sums = project(
+            [x_blocks[j] for j in order], w_down, first, count * width, index == 0
+        )
         first += count * width
-        kept, sent, *sums = project(x_blocks, w_rows, index == 0)
         if index == 0:
             bias_part = sums[0]
         mask = 1
@@ -374,22 +462,15 @@
             kept, sent = halve(kept, swap(sent, "img", mask))
             mask *= 2
         terms.append((kept, swap(sent, "img", mask)))
-    packed = pack(terms, token_target, bias_part, peers, capacity, carries)
+    packed = pack(terms, token_target, peers, capacity)
     routed = exchange(packed, "seq", peers)
 
-    gain_rows = width // LANES
-    share = (devices, gain_rows + pieces, LANES) if carries else (1, width)
-    out_grads, shared = norm_backward(routed, peers, patches[0], gain[None], share)
-    if carries:
-        shared = exchange(shared, ("img", "seq"), devices)
-        gain_total = jnp.sum(shared[:, :gain_rows], axis=0).reshape(-1)
-        bias_total = shared[:, gain_rows:].reshape(-1)
-    else:
-        gain_total = lax.psum(shared[0], ("img", "seq"))
-        bias_total = lax.all_gather(lax.psum(bias_part[0], "seq"), "img", tiled=True)
+    share = gain_and_bias_share(packed, slot_patches, bias_part, width)
+    gain_total, bias_total = sum_shares(share, width)
+    out_grads = norm_backward(routed, labels, patches[0], gain[None])
     grads = window_backward(out_grads, queries[0], keys[0], values[0], probs, probs_t)
-    gain_grad = gain_total / math.sqrt(devices * patches.shape[1])
-    bias_grad = bias_total / math.sqrt(devices * rows)
+    gain_grad = gain_total / math.sqrt(images * peers * patches.shape[1])
+    bias_grad = bias_total / math.sqrt(images * peers * rows)
     return (grads[0][None], grads[1][None], grads[2][None], gain_grad, bias_grad)
 
 

time: 72.1 us -> 105 us (1.46)
  Pallas kernels: 12.1 us -> 26.7 us
  starting transfers between devices: 16.7 us -> 30.3 us
  local copies, waits for them, and re-layouts: 9.73 us -> 14.7 us
  waiting for transfers between devices: 31.2 us -> 29.4 us
    all_to_all x2 -> x3, waiting for transfers between devices: 24.5 us -> 6.39 us  [exchange(): lax.all_to_all(x, axis, split_axis=0, concat_axis=0, tiled=True)]
    ppermute x7 -> x13, waiting for transfers between devices: 6.74 us -> 23 us  [swap(): return lax.ppermute(x, axis, [(i, i ^ mask) for i in range(n)])]
    pallas_call x3 -> x6, Pallas kernels: 7.2 us -> 21.8 us  [the longest x2 17 us: project(): pl.pallas_call(functools.partial(project_kernel, blocks, first, tile, til...]
    unnamed x14 -> x31, local copies, waits for them, and re-layouts: 0.04 us -> 12.3 us
    slice x1 -> x0, local copies, waits for them, and re-layouts: 8.54 us -> none  [body(): w_rows = lax.slice_in_dim(w_down, first, first + count * width)]
    all_to_all x2 -> x3, starting transfers between devices: 9.64 us -> 16.7 us  [exchange(): lax.all_to_all(x, axis, split_axis=0, concat_axis=0, tiled=True)]
    ppermute x7 -> x13, starting transfers between devices: 7.06 us -> 13.6 us  [swap(): return lax.ppermute(x, axis, [(i, i ^ mask) for i in range(n)])]
    broadcast_in_dim x1 -> x2, local copies, waits for them, and re-layouts: 0.01 us -> 1.26 us  [the longest x1 1.25 us: body(): jnp.broadcast_to(token_target[None], (peers, 1, rows))]
  transfers between devices with their start and end apart: 9 -> 16, of which waited for: 4 -> 9; matrix products, arithmetic and copies ran while one was open for 12% -> 4% of each run, Pallas kernels for 9% -> 21%
where the time goes in v4:
time: 105 us; the launch traced here: 104 us
  starting transfers between devices  30.3 us (29%)
  waiting for transfers between devices  29.4 us (28%)
  Pallas kernels  26.7 us (25%)
  local copies, waits for them, and re-layouts  14.7 us (14%)
  other arithmetic  2.12 us (2%)
    ppermute x13, waiting for transfers between devices, swap(): return lax.ppermute(x, axis, [(i, i ^ mask) for i in range(n)])  23 us
    pallas_call x2, Pallas kernels, project(): pl.pallas_call(functools.partial(project_kernel, blocks, first, tile, til...  17 us
    all_to_all x3, starting transfers between devices, exchange(): lax.all_to_all(x, axis, split_axis=0, concat_axis=0, tiled=True)  16.7 us
    ppermute x13, starting transfers between devices, swap(): return lax.ppermute(x, axis, [(i, i ^ mask) for i in range(n)])  13.6 us
    unnamed x31, local copies, waits for them, and re-layouts  12.3 us
    all_to_all x3, waiting for transfers between devices, exchange(): lax.all_to_all(x, axis, split_axis=0, concat_axis=0, tiled=True)  6.39 us
    pallas_call x1, Pallas kernels, window_backward(): pl.pallas_call(window_kernel, out_shape=[shape] * 3, in_specs=vmem(6), ou...  2.37 us
  transfers between devices with their start and end apart: 16, of which 9 were waited for; matrix products, arithmetic and copies ran while one was open for 4% of the time, Pallas kernels for 21%

profile of v4, /device:TPU:0, one launch (start us, length us, event | category | flops | bytes accessed | tf_op | source)
XLA Modules:
  0.0 104.1 jit_solution(15958772859568749687)
XLA Ops:
  0.6 1.3 %broadcast_in_dim.22 = s32[8,1,32]{2,1,0:T(1,128)} broadcast(s32[32]{0:T(128)} %bitcast.35), dimensions={2} | broadcast | bytes 1152 | tf_op jit(solution)/shard_map/broadcast_in_dim | solution.py:446
  1.9 7.3 %all-to-all-start = ((s32[8,1,32]{2,1,0:T(1,128)}), s32[8,1,32]{2,1,0:T(1,128)S(1)}, u32[]{:S(2)}, u32[]{:S(2)}) async-start(s32[8,1,32]{2,1,0:T(1,128)} %broadcast_in_dim.22), calls=%async_computation | async-start | bytes 8192 | tf_op jit(solution)/shard_map/all_to_all | solution.py:247
  9.1 6.4 %all-to-all-done.targets_ref = s32[8,1,32]{2,1,0:T(1,128)S(1)} async-done(((s32[8,1,32]{2,1,0:T(1,128)}), s32[8,1,32]{2,1,0:T(1,128)S(1)}, u32[]{:S(2)}, u32[]{:S(2)}) %all-to-all-start) | async-done | bytes 1056 | tf_op jit(solution)/shard_map/all_to_all | solution.py:247
  15.5 1.0 copy-done.1
  16.5 1.5 %spread.1 = (bf16[64,5120]{1,0:T(8,128)(2,1)}, f32[64,128]{1,0:T(8,128)S(1)}) custom-call(s32[1]{0:T(128)} %bitcast.1.me_ref, s32[8,1,32]{2,1,0:T(1,128)S(1)} %all-to-all-done.targets_ref, bf16[128,1280]{1,0:T(8,128)(2,1)S(1)} %bitcast.28), custom_call_target="tpu_custom_call" | custom-call | flops 83886080 | bytes 983040 | tf_op jit(solution)/shard_map/spread/pallas_call | solution.py:195
  18.0 3.5 %all-to-all-start.2 = ((bf16[8,8,5120]{2,1,0:T(8,128)(2,1)}), bf16[8,8,5120]{2,1,0:T(8,128)(2,1)S(1)}, u32[]{:S(2)}, u32[]{:S(2)}) async-start(bf16[8,8,5120]{2,1,0:T(8,128)(2,1)} %bitcast.17), calls=%async_computation.2 | async-start | bytes 1310720 | tf_op jit(solution)/shard_map/all_to_all | solution.py:247
  21.6 1.1 %dynamic-slice_bitcast_fusion = (bf16[32,2048]{1,0:T(8,128)(2,1)S(1)}, bf16[32,2048]{1,0:T(8,128)(2,1)S(1)}, bf16[32,2048]{1,0:T(8,128)(2,1)S(1)}, bf16[32,2048]{1,0:T(8,128)(2,1)S(1)}) fusion(bf16[1,32,8192]{2,1,0:T(8,128)(2,1)} %param.9, s32[]{:T(128)S(6)} %select_n.15, s32[]{:T(128)S(6)} %select_n.13, s32[]{:T(128)S(6)} %select_n.12, s32[]{:T(128)S(6)} %select_n.14), kind=kLoop, calls=%fused_computation | loop fusion | bytes 1048592 | tf_op jit(solution)/shard_map/dynamic_slice | solution.py:442
  22.7 0.1 collective-permute-start.2
  22.8 1.6 %collective-permute-start = (bf16[32,2048]{1,0:T(8,128)(2,1)S(1)}, bf16[32,2048]{1,0:T(8,128)(2,1)S(1)}, u32[]{:S(2)}, u32[]{:S(2)}) collective-permute-start(bf16[32,2048]{1,0:T(8,128)(2,1)S(1)} %get-tuple-element.50), channel_id=1, source_target_pairs={{0,8},{8,0},{16,24},{24,16},{1,9},{9,1},{17,25},{25,17},{2,10},{10... | collective-permute-start | bytes 393224 | tf_op jit(solution)/shard_map/ppermute | solution.py:240
  24.4 0.5 collective-permute-start.1
  24.9 3.6 %collective-permute-done.2.refs_3_ = bf16[32,2048]{1,0:T(8,128)(2,1)S(1)} collective-permute-done((bf16[32,2048]{1,0:T(8,128)(2,1)S(1)}, bf16[32,2048]{1,0:T(8,128)(2,1)S(1)}, u32[]{:S(2)}, u32[]{:S(2)}) %collective-permute-start.2) | collective-permute-done | bytes 131104 | tf_op jit(solution)/shard_map/ppermute | solution.py:240
  28.5 0.0 collective-permute-done.refs_2_
  28.5 2.9 %collective-permute-done.1.refs_1_ = bf16[32,2048]{1,0:T(8,128)(2,1)S(1)} collective-permute-done((bf16[32,2048]{1,0:T(8,128)(2,1)S(1)}, bf16[32,2048]{1,0:T(8,128)(2,1)S(1)}, u32[]{:S(2)}, u32[]{:S(2)}) %collective-permute-start.1) | collective-permute-done | bytes 131104 | tf_op jit(solution)/shard_map/ppermute | solution.py:240
  31.4 7.0 %copy-done = bf16[5120,2048]{1,0:T(8,128)(2,1)S(1)} copy-done((bf16[5120,2048]{1,0:T(8,128)(2,1)S(1)}, bf16[5120,2048]{1,0:T(8,128)(2,1)}, u32[]{:S(2)}) %copy-start) | copy-done | bytes 20971544
  38.4 0.0 copy-start.9
  38.4 0.0 copy-start.2
  38.4 8.6 %project.2 = (bf16[64,2560]{1,0:T(8,128)(2,1)S(1)}, bf16[64,2560]{1,0:T(8,128)(2,1)S(1)}, f32[1,2048]{1,0:T(1,128)S(1)}) custom-call(bf16[32,2048]{1,0:T(8,128)(2,1)S(1)} %get-tuple-element.29.refs_0_, bf16[32,2048]{1,0:T(8,128)(2,1)S(1)} %collective-permute-done.1.refs_1_, bf16[32,2048]{1,0:T(8,128)(2,1)S(1)} %collective-permute-done.refs_2_, ...), custom_call_target="tpu_custom_call" | custom-call | flops 1342177280 | bytes 10485760 | tf_op jit(solution)/shard_map/project/pallas_call | solution.py:81
  47.0 0.1 collective-permute-start.3
  47.1 8.4 %project.3 = (bf16[64,2560]{1,0:T(8,128)(2,1)S(1)}, bf16[64,2560]{1,0:T(8,128)(2,1)S(1)}) custom-call(bf16[32,2048]{1,0:T(8,128)(2,1)S(1)} %get-tuple-element.29.refs_0_, bf16[32,2048]{1,0:T(8,128)(2,1)S(1)} %collective-permute-done.1.refs_1_, bf16[32,2048]{1,0:T(8,128)(2,1)S(1)} %collective-permute-done.refs_2_, ...), custom_call_target="tpu_custom_call" | custom-call | flops 1342177280 | bytes 10485760 | tf_op jit(solution)/shard_map/project/pallas_call | solution.py:81
  55.5 0.5 collective-permute-start.5
  56.0 0.0 collective-permute-done.3.got_ref
  56.0 0.1 halve.2
  56.1 0.3 collective-permute-start.4
  56.4 0.9 collective-permute-done.5.got_ref
  57.3 0.1 halve.3
  57.4 1.0 collective-permute-start.6
  58.3 4.9 %collective-permute-done.4.refs_1_ = bf16[32,2560]{1,0:T(8,128)(2,1)S(1)} collective-permute-done((bf16[32,2560]{1,0:T(8,128)(2,1)S(1)}, bf16[32,2560]{1,0:T(8,128)(2,1)S(1)}, u32[]{:S(2)}, u32[]{:S(2)}) %collective-permute-start.4) | collective-permute-done | bytes 163872 | tf_op jit(solution)/shard_map/ppermute | solution.py:240
  63.2 2.6 %collective-permute-done.6.refs_3_ = bf16[32,2560]{1,0:T(8,128)(2,1)S(1)} collective-permute-done((bf16[32,2560]{1,0:T(8,128)(2,1)S(1)}, bf16[32,2560]{1,0:T(8,128)(2,1)S(1)}, u32[]{:S(2)}, u32[]{:S(2)}) %collective-permute-start.6) | collective-permute-done | bytes 163872 | tf_op jit(solution)/shard_map/ppermute | solution.py:240
  65.8 0.0 copy-done.8
  65.8 1.3 %pack.1.packed_ref = bf16[64,5120]{1,0:T(8,128)(2,1)} custom-call(s32[1,32]{1,0:T(1,128)S(1)} %copy-done.8, f32[32,2560]{1,0:T(8,128)S(1)} %get-tuple-element.35.refs_0_, bf16[32,2560]{1,0:T(8,128)(2,1)S(1)} %collective-permute-done.4.refs_1_, f32[32,2560]{1,0:T(8,128)S(1)} %get-tuple-element.39.refs_2_, bf16[32,2560]{1,0:T(8,128)(2,1)S(1)} %collective-permute-done.6.refs_3_), custom_call_target="tpu_custom_call" | custom-call | flops 20971520 | bytes 1638400 | tf_op jit(solution)/shard_map/pack/pallas_call | solution.py:151
  67.1 0.0 all-to-all-done.2
  67.1 5.9 %all-to-all-start.1 = ((bf16[8,8,5120]{2,1,0:T(8,128)(2,1)}), bf16[8,8,5120]{2,1,0:T(8,128)(2,1)S(1)}, u32[]{:S(2)}, u32[]{:S(2)}) async-start(bf16[8,8,5120]{2,1,0:T(8,128)(2,1)} %bitcast.7), calls=%async_computation.1 | async-start | bytes 1310720 | tf_op jit(solution)/shard_map/all_to_all | solution.py:247
  73.0 1.5 %share.1 = f32[1,3328]{1,0:T(1,128)S(1)} custom-call(bf16[64,5120]{1,0:T(8,128)(2,1)} %pack.1.packed_ref, bf16[64,5120]{1,0:T(8,128)(2,1)S(1)} %bitcast.26, f32[1,2048]{1,0:T(1,128)S(1)} %get-tuple-element.46.sums_ref), custom_call_target="tpu_custom_call" | custom-call | flops 1966080 | bytes 1310720 | tf_op jit(solution)/shard_map/share/pallas_call | solution.py:225
  74.5 2.1 %collective-permute-start.7 = (f32[1,3328]{1,0:T(1,128)S(1)}, f32[1,3328]{1,0:T(1,128)S(1)}, u32[]{:S(2)}, u32[]{:S(2)}) collective-permute-start(f32[1,3328]{1,0:T(1,128)S(1)} %share.1), channel_id=1, source_target_pairs={{0,1},{1,0},{2,3},{3,2},{4,5},{5,4},{6,7},{7,6},{8,9},{9,8},{10,11... | collective-permute-start | bytes 39944 | tf_op jit(solution)/shard_map/ppermute | solution.py:240
  76.6 3.0 %collective-permute-done.7 = f32[1,3328]{1,0:T(1,128)S(1)} collective-permute-done((f32[1,3328]{1,0:T(1,128)S(1)}, f32[1,3328]{1,0:T(1,128)S(1)}, u32[]{:S(2)}, u32[]{:S(2)}) %collective-permute-start.7) | collective-permute-done | bytes 13344 | tf_op jit(solution)/shard_map/ppermute | solution.py:240
  79.6 0.8 collective-permute-start.8
  80.4 3.0 %collective-permute-done.8 = f32[1,3328]{1,0:T(1,128)S(1)} collective-permute-done((f32[1,3328]{1,0:T(1,128)S(1)}, f32[1,3328]{1,0:T(1,128)S(1)}, u32[]{:S(2)}, u32[]{:S(2)}) %collective-permute-start.8) | collective-permute-done | bytes 13344 | tf_op jit(solution)/shard_map/ppermute | solution.py:240
  83.4 4.7 %collective-permute-start.9 = (f32[1,3328]{1,0:T(1,128)S(1)}, f32[1,3328]{1,0:T(1,128)S(1)}, u32[]{:S(2)}, u32[]{:S(2)}) collective-permute-start(f32[1,3328]{1,0:T(1,128)S(1)} %add.26), channel_id=1, source_target_pairs={{0,4},{1,5},{2,6},{3,7},{4,0},{5,1},{6,2},{7,3},{8,12},{9,13},{10,... | collective-permute-start | bytes 39944 | tf_op jit(solution)/shard_map/ppermute | solution.py:240
  88.1 0.0 copy-done.14
  88.1 2.1 %collective-permute-done.9 = f32[1,3328]{1,0:T(1,128)S(1)} collective-permute-done((f32[1,3328]{1,0:T(1,128)S(1)}, f32[1,3328]{1,0:T(1,128)S(1)}, u32[]{:S(2)}, u32[]{:S(2)}) %collective-permute-start.9) | collective-permute-done | bytes 13344 | tf_op jit(solution)/shard_map/ppermute | solution.py:240
  90.3 0.0 copy-start.10
  90.3 0.1 collective-permute-start.12
  90.4 0.8 collective-permute-start.11
  91.2 1.1 %collective-permute-start.10 = (f32[1,3328]{1,0:T(1,128)S(1)}, f32[1,3328]{1,0:T(1,128)S(1)}, u32[]{:S(2)}, u32[]{:S(2)}) collective-permute-start(f32[1,3328]{1,0:T(1,128)S(1)} %add.27.refs_0_), channel_id=1, source_target_pairs={{0,8},{8,0},{16,24},{24,16},{1,9},{9,1},{17,25},{25,17},{2,10},{10... | collective-permute-start | bytes 39944 | tf_op jit(solution)/shard_map/ppermute | solution.py:240
  92.2 0.0 copy-done.9
  92.2 1.1 %probs.1 = (f32[16,128,128]{2,1,0:T(8,128)S(1)}, f32[16,128,128]{2,1,0:T(8,128)S(1)}) custom-call(bf16[128,1280]{1,0:T(8,128)(2,1)S(1)} %bitcast.30, bf16[128,1280]{1,0:T(8,128)(2,1)S(1)} %bitcast.32, s32[1,32]{1,0:T(1,128)S(1)} %bitcast.36), custom_call_target="tpu_custom_call" | custom-call | flops 268435456 | bytes 2097152 | tf_op jit(solution)/shard_map/probs/pallas_call | solution.py:279
  93.3 1.0 copy-done.3
  94.3 0.0 collective-permute-done.12.refs_3_
  94.3 0.0 collective-permute-done.11.refs_2_
  94.3 0.0 copy-start.12
  94.3 0.0 collective-permute-done.10.refs_1_
  94.3 0.0 copy-start.13
  94.3 0.5 copy-done.11
  94.9 0.0 copy-done.12
  94.9 0.0 copy-done.13
  94.9 1.4 %finish.1 = (f32[1,1280]{1,0:T(1,128)}, f32[4,2048]{1,0:T(4,128)}) custom-call(s32[1]{0:T(128)} %bitcast.16.image_ref, f32[1,3328]{1,0:T(1,128)} %copy-done.10, f32[1,3328]{1,0:T(1,128)} %copy-done.13, f32[1,3328]{1,0:T(1,128)} %copy-done.12, f32[1,3328]{1,0:T(1,128)} %copy-done.11), custom_call_target="tpu_custom_call" | custom-call | tf_op jit(solution)/shard_map/finish/pallas_call | solution.py:415
  96.3 0.8 multiply_bitcast_fusion
  97.1 0.6 copy.14
  97.7 1.3 %multiply_reduce_fusion = f32[1280]{0:T(1024)} fusion(f32[1,1280]{1,0:T(1,128)} %get-tuple-element.47), kind=kLoop, calls=%fused_computation.5 | loop fusion | flops 1280 | bytes 10240 | tf_op jit(solution)/shard_map/div | solution.py:472
  99.0 0.0 all-to-all-done.1
  99.0 0.5 norm.1.g_ref
  99.5 1.2 %copy-done.4 = f32[16,128,128]{2,1,0:T(8,128)S(1)} copy-done((f32[16,128,128]{2,1,0:T(8,128)S(1)}, f32[16,128,128]{2,1,0:T(8,128)}, u32[]{:S(2)}) %copy-start.4) | copy-done | bytes 1048600
  100.7 1.0 copy-done.7
  101.7 2.4 %window.1 = (bf16[128,1280]{1,0:T(8,128)(2,1)}, bf16[128,1280]{1,0:T(8,128)(2,1)}, bf16[128,1280]{1,0:T(8,128)(2,1)}) custom-call(bf16[128,1280]{1,0:T(8,128)(2,1)S(1)} %norm.1.g_ref, bf16[128,1280]{1,0:T(8,128)(2,1)S(1)} %bitcast.31, bf16[128,1280]{1,0:T(8,128)(2,1)S(1)} %bitcast.33, bf16[128,1280]{1,0:T(8,128)(2,1)S(1)} %bitcast.34, ...), custom_call_target="tpu_custom_call" | custom-call | flops 335544320 | bytes 4390912 | tf_op jit(solution)/shard_map/window/pallas_call | solution.py:378
  (18 shorter events, 0.1 us)
Async XLA Ops:
  1.9 13.6 %all-to-all-start = ((s32[8,1,32]{2,1,0:T(1,128)}), s32[8,1,32]{2,1,0:T(1,128)S(1)}, u32[]{:S(2)}, u32[]{:S(2)}) async-start(s32[8,1,32]{2,1,0:T(1,128)} %broadcast_in_dim.22), calls=%async_computation | async-start | bytes 8192 | tf_op jit(solution)/shard_map/all_to_all | solution.py:247
  15.5 1.0 copy-start.1
  18.0 49.1 %all-to-all-start.2 = ((bf16[8,8,5120]{2,1,0:T(8,128)(2,1)}), bf16[8,8,5120]{2,1,0:T(8,128)(2,1)S(1)}, u32[]{:S(2)}, u32[]{:S(2)}) async-start(bf16[8,8,5120]{2,1,0:T(8,128)(2,1)} %bitcast.17), calls=%async_computation.2 | async-start | bytes 1310720 | tf_op jit(solution)/shard_map/all_to_all | solution.py:247
  22.7 5.8 %collective-permute-start.2 = (bf16[32,2048]{1,0:T(8,128)(2,1)S(1)}, bf16[32,2048]{1,0:T(8,128)(2,1)S(1)}, u32[]{:S(2)}, u32[]{:S(2)}) collective-permute-start(bf16[32,2048]{1,0:T(8,128)(2,1)S(1)} %get-tuple-element.49), channel_id=1, source_target_pairs={{0,24},{8,16},{16,8},{24,0},{1,25},{9,17},{17,9},{25,1},{2,26},{10... | collective-permute-start | bytes 393224 | tf_op jit(solution)/shard_map/ppermute | solution.py:240
  22.8 5.7 %collective-permute-start = (bf16[32,2048]{1,0:T(8,128)(2,1)S(1)}, bf16[32,2048]{1,0:T(8,128)(2,1)S(1)}, u32[]{:S(2)}, u32[]{:S(2)}) collective-permute-start(bf16[32,2048]{1,0:T(8,128)(2,1)S(1)} %get-tuple-element.50), channel_id=1, source_target_pairs={{0,8},{8,0},{16,24},{24,16},{1,9},{9,1},{17,25},{25,17},{2,10},{10... | collective-permute-start | bytes 393224 | tf_op jit(solution)/shard_map/ppermute | solution.py:240
  24.4 7.0 %collective-permute-start.1 = (bf16[32,2048]{1,0:T(8,128)(2,1)S(1)}, bf16[32,2048]{1,0:T(8,128)(2,1)S(1)}, u32[]{:S(2)}, u32[]{:S(2)}) collective-permute-start(bf16[32,2048]{1,0:T(8,128)(2,1)S(1)} %get-tuple-element.52), channel_id=1, source_target_pairs={{0,16},{8,24},{16,0},{24,8},{1,17},{9,25},{17,1},{25,9},{2,18},{10... | collective-permute-start | bytes 393224 | tf_op jit(solution)/shard_map/ppermute | solution.py:240
  31.4 7.0 %copy-start = (bf16[5120,2048]{1,0:T(8,128)(2,1)S(1)}, bf16[5120,2048]{1,0:T(8,128)(2,1)}, u32[]{:S(2)}) copy-start(bf16[5120,2048]{1,0:T(8,128)(2,1)} %refs_4_.3) | copy-start | bytes 62914564
  38.4 27.5 %copy-start.8 = (s32[1,32]{1,0:T(1,128)S(1)}, s32[1,32]{1,0:T(1,128)}, u32[]{:S(2)}) copy-start(s32[1,32]{1,0:T(1,128)} %targets_ref.1) | copy-start | bytes 388
  38.4 49.8 %copy-start.14 = (f32[1280]{0:T(1024)S(1)}, f32[1280]{0:T(1024)}, u32[]{:S(2)}) copy-start(f32[1280]{0:T(1024)} %param.12) | copy-start | bytes 15364
  38.4 53.9 %copy-start.5 = (bf16[1,128,1280]{2,1,0:T(8,128)(2,1)S(1)}, bf16[1,128,1280]{2,1,0:T(8,128)(2,1)}, u32[]{:S(2)}) copy-start(bf16[1,128,1280]{2,1,0:T(8,128)(2,1)} %param.14) | copy-start | bytes 983044
  38.4 53.9 %copy-start.6 = (bf16[1,128,1280]{2,1,0:T(8,128)(2,1)S(1)}, bf16[1,128,1280]{2,1,0:T(8,128)(2,1)}, u32[]{:S(2)}) copy-start(bf16[1,128,1280]{2,1,0:T(8,128)(2,1)} %param.15) | copy-start | bytes 983044
  38.4 53.9 %copy-start.9 = (s32[1,1,32]{2,1,0:T(1,128)S(1)}, s32[1,1,32]{2,1,0:T(1,128)}, u32[]{:S(2)}) copy-start(s32[1,1,32]{2,1,0:T(1,128)} %param.17) | copy-start | bytes 388
  38.4 60.6 %copy-start.2 = (bf16[1,128,1280]{2,1,0:T(8,128)(2,1)S(1)}, bf16[1,128,1280]{2,1,0:T(8,128)(2,1)}, u32[]{:S(2)}) copy-start(bf16[1,128,1280]{2,1,0:T(8,128)(2,1)} %param.11) | copy-start | bytes 983044
  47.0 9.1 %collective-permute-start.3 = (bf16[64,2560]{1,0:T(8,128)(2,1)S(1)}, bf16[64,2560]{1,0:T(8,128)(2,1)S(1)}, u32[]{:S(2)}, u32[]{:S(2)}) collective-permute-start(bf16[64,2560]{1,0:T(8,128)(2,1)S(1)} %get-tuple-element.34), channel_id=1, source_target_pairs={{0,8},{8,0},{16,24},{24,16},{1,9},{9,1},{17,25},{25,17},{2,10},{10... | collective-permute-start | bytes 983048 | tf_op jit(solution)/shard_map/ppermute | solution.py:240
  55.5 1.8 %collective-permute-start.5 = (bf16[64,2560]{1,0:T(8,128)(2,1)S(1)}, bf16[64,2560]{1,0:T(8,128)(2,1)S(1)}, u32[]{:S(2)}, u32[]{:S(2)}) collective-permute-start(bf16[64,2560]{1,0:T(8,128)(2,1)S(1)} %get-tuple-element.38), channel_id=1, source_target_pairs={{0,8},{8,0},{16,24},{24,16},{1,9},{9,1},{17,25},{25,17},{2,10},{10... | collective-permute-start | bytes 983048 | tf_op jit(solution)/shard_map/ppermute | solution.py:240
  56.1 7.1 %collective-permute-start.4 = (bf16[32,2560]{1,0:T(8,128)(2,1)S(1)}, bf16[32,2560]{1,0:T(8,128)(2,1)S(1)}, u32[]{:S(2)}, u32[]{:S(2)}) collective-permute-start(bf16[32,2560]{1,0:T(8,128)(2,1)S(1)} %get-tuple-element.36), channel_id=1, source_target_pairs={{0,16},{8,24},{16,0},{24,8},{1,17},{9,25},{17,1},{25,9},{2,18},{10... | collective-permute-start | bytes 491528 | tf_op jit(solution)/shard_map/ppermute | solution.py:240
  57.4 8.5 %collective-permute-start.6 = (bf16[32,2560]{1,0:T(8,128)(2,1)S(1)}, bf16[32,2560]{1,0:T(8,128)(2,1)S(1)}, u32[]{:S(2)}, u32[]{:S(2)}) collective-permute-start(bf16[32,2560]{1,0:T(8,128)(2,1)S(1)} %get-tuple-element.40), channel_id=1, source_target_pairs={{0,16},{8,24},{16,0},{24,8},{1,17},{9,25},{17,1},{25,9},{2,18},{10... | collective-permute-start | bytes 491528 | tf_op jit(solution)/shard_map/ppermute | solution.py:240
  67.1 31.9 %all-to-all-start.1 = ((bf16[8,8,5120]{2,1,0:T(8,128)(2,1)}), bf16[8,8,5120]{2,1,0:T(8,128)(2,1)S(1)}, u32[]{:S(2)}, u32[]{:S(2)}) async-start(bf16[8,8,5120]{2,1,0:T(8,128)(2,1)} %bitcast.7), calls=%async_computation.1 | async-start | bytes 1310720 | tf_op jit(solution)/shard_map/all_to_all | solution.py:247
  74.5 5.1 %collective-permute-start.7 = (f32[1,3328]{1,0:T(1,128)S(1)}, f32[1,3328]{1,0:T(1,128)S(1)}, u32[]{:S(2)}, u32[]{:S(2)}) collective-permute-start(f32[1,3328]{1,0:T(1,128)S(1)} %share.1), channel_id=1, source_target_pairs={{0,1},{1,0},{2,3},{3,2},{4,5},{5,4},{6,7},{7,6},{8,9},{9,8},{10,11... | collective-permute-start | bytes 39944 | tf_op jit(solution)/shard_map/ppermute | solution.py:240
  79.6 3.8 %collective-permute-start.8 = (f32[1,3328]{1,0:T(1,128)S(1)}, f32[1,3328]{1,0:T(1,128)S(1)}, u32[]{:S(2)}, u32[]{:S(2)}) collective-permute-start(f32[1,3328]{1,0:T(1,128)S(1)} %add.25), channel_id=1, source_target_pairs={{0,2},{1,3},{2,0},{3,1},{4,6},{5,7},{6,4},{7,5},{8,10},{9,11},{10,... | collective-permute-start | bytes 39944 | tf_op jit(solution)/shard_map/ppermute | solution.py:240
  83.4 6.8 %collective-permute-start.9 = (f32[1,3328]{1,0:T(1,128)S(1)}, f32[1,3328]{1,0:T(1,128)S(1)}, u32[]{:S(2)}, u32[]{:S(2)}) collective-permute-start(f32[1,3328]{1,0:T(1,128)S(1)} %add.26), channel_id=1, source_target_pairs={{0,4},{1,5},{2,6},{3,7},{4,0},{5,1},{6,2},{7,3},{8,12},{9,13},{10,... | collective-permute-start | bytes 39944 | tf_op jit(solution)/shard_map/ppermute | solution.py:240
  90.3 4.0 %copy-start.10 = (f32[1,3328]{1,0:T(1,128)}, f32[1,3328]{1,0:T(1,128)S(1)}, u32[]{:S(2)}) copy-start(f32[1,3328]{1,0:T(1,128)S(1)} %add.27.refs_0_) | copy-start | bytes 39940
  90.3 4.0 %collective-permute-start.12 = (f32[1,3328]{1,0:T(1,128)S(1)}, f32[1,3328]{1,0:T(1,128)S(1)}, u32[]{:S(2)}, u32[]{:S(2)}) collective-permute-start(f32[1,3328]{1,0:T(1,128)S(1)} %add.27.refs_0_), channel_id=1, source_target_pairs={{0,24},{8,16},{16,8},{24,0},{1,25},{9,17},{17,9},{25,1},{2,26},{10... | collective-permute-start | bytes 39944 | tf_op jit(solution)/shard_map/ppermute | solution.py:240
  90.4 3.9 %collective-permute-start.11 = (f32[1,3328]{1,0:T(1,128)S(1)}, f32[1,3328]{1,0:T(1,128)S(1)}, u32[]{:S(2)}, u32[]{:S(2)}) collective-permute-start(f32[1,3328]{1,0:T(1,128)S(1)} %add.27.refs_0_), channel_id=1, source_target_pairs={{0,16},{8,24},{16,0},{24,8},{1,17},{9,25},{17,1},{25,9},{2,18},{10... | collective-permute-start | bytes 39944 | tf_op jit(solution)/shard_map/ppermute | solution.py:240
  91.2 3.1 %collective-permute-start.10 = (f32[1,3328]{1,0:T(1,128)S(1)}, f32[1,3328]{1,0:T(1,128)S(1)}, u32[]{:S(2)}, u32[]{:S(2)}) collective-permute-start(f32[1,3328]{1,0:T(1,128)S(1)} %add.27.refs_0_), channel_id=1, source_target_pairs={{0,8},{8,0},{16,24},{24,16},{1,9},{9,1},{17,25},{25,17},{2,10},{10... | collective-permute-start | bytes 39944 | tf_op jit(solution)/shard_map/ppermute | solution.py:240
  93.3 1.0 copy-start.3
  94.3 0.6 copy-start.11
  94.3 0.6 copy-start.12
  94.3 0.6 copy-start.13
  99.5 1.2 %copy-start.4 = (f32[16,128,128]{2,1,0:T(8,128)S(1)}, f32[16,128,128]{2,1,0:T(8,128)}, u32[]{:S(2)}) copy-start(f32[16,128,128]{2,1,0:T(8,128)} %copy-done.3) | copy-start | bytes 3145732
  100.7 1.0 copy-start.7

commit v5 on v3

--- a/solution.py
+++ b/solution.py
@@ -12,6 +12,7 @@
 HEAD_DIM = 80
 LANES = 128
 CHUNKS = (2, 2)
+DIRECT = 8
 VMEM_BYTES = 24 * 1024 * 1024
 
 F32 = jnp.float32
@@ -110,8 +111,8 @@
     )(kept, got)
 
 
-def pack_kernel(peers, capacity, chunks, carries, targets_ref, *refs):
-    terms, out_ref = refs[: 2 * chunks], refs[-1]
+def pack_kernel(peers, capacity, direct, labelled, carries, me_ref, targets_ref, kept_ref, got_ref, *refs):
+    outs = refs[1:] if carries else refs
     targets = targets_ref[...]
     rows = targets.shape[1]
     dest = targets // rows
@@ -123,43 +124,55 @@
     rank = jnp.sum(same_before.astype(jnp.int32), axis=0, keepdims=True)
     slots = peers * capacity
     slot = iota((slots, rows), 0)
-    chosen = jnp.logical_and(dest == slot // capacity, rank == slot % capacity)
-    selector = chosen.astype(F32).astype(BF16)
-    at = 0
-    for chunk in range(chunks):
-        kept, got = terms[2 * chunk], terms[2 * chunk + 1]
-        total = (kept[...].astype(F32) + got[...].astype(F32)).astype(BF16)
-        width = total.shape[1]
-        out_ref[:, at : at + width] = dot(selector, total, (1, 0)).astype(BF16)
-        at += width
-    label = jnp.sum(jnp.where(chosen, local + 1, 0), axis=1, keepdims=True) - 1
-    out_ref[:, at : at + LANES] = jnp.broadcast_to(label.astype(F32), (slots, LANES)).astype(BF16)
+    holder = slot // capacity
+    if direct:
+        holder = holder ^ me_ref[0]
+    chosen = jnp.logical_and(dest == holder, rank == slot % capacity)
+    total = (kept_ref[...].astype(F32) + got_ref[...].astype(F32)).astype(BF16)
+    parts = [dot(chosen.astype(F32).astype(BF16), total, (1, 0))]
+    if labelled:
+        label = jnp.sum(jnp.where(chosen, local + 1, 0), axis=1, keepdims=True) - 1
+        parts.append(jnp.broadcast_to(label.astype(F32), (slots, LANES)))
     if carries:
-        sums = refs[2 * chunks][...]
+        sums = refs[0][...]
         high = sums.astype(BF16).astype(F32)
         middle = (sums - high).astype(BF16).astype(F32)
         low = (sums - high - middle).astype(BF16).astype(F32)
         extra = jnp.zeros((slots, LANES), F32)
-        row = iota((slots, LANES), 0)
+        row = iota((slots, LANES), 0) % capacity
+        peer = iota((slots, LANES), 0) // capacity
+        if direct:
+            peer = peer ^ me_ref[0]
         pieces = sums.shape[1] // peers // LANES
-        for peer in range(peers):
+        for p in range(peers):
             for level, values in enumerate((high, middle, low)):
                 for piece in range(pieces):
-                    start = (peer * pieces + piece) * LANES
+                    start = (p * pieces + piece) * LANES
                     line = jnp.broadcast_to(values[:, start : start + LANES], (slots, LANES))
-                    extra = jnp.where(row == peer * capacity + level * pieces + piece, line, extra)
-        out_ref[:, at + LANES : at + 2 * LANES] = extra.astype(BF16)
-
-
-def pack(terms, targets, sums, peers, capacity, carries):
-    rows = targets.shape[1]
-    width = sum(kept.shape[1] for kept, _ in terms) + (2 * LANES if carries else LANES)
-    operands = [targets] + [x for pair in terms for x in pair] + ([sums] if carries else [])
-    return pl.pallas_call(
-        functools.partial(pack_kernel, peers, capacity, len(terms), carries),
-        out_shape=jax.ShapeDtypeStruct((peers * capacity, width), BF16),
-        in_specs=vmem(len(operands)),
-        out_specs=pl.BlockSpec(memory_space=pltpu.VMEM),
+                    here = jnp.logical_and(peer == p, row == level * pieces + piece)
+                    extra = jnp.where(here, line, extra)
+        parts.append(extra)
+    packed = jnp.concatenate(parts, axis=1) if len(parts) > 1 else parts[0]
+    if not direct:
+        outs[0][...] = packed.astype(BF16)
+        return
+    for m in range(peers):
+        outs[m][...] = packed[m * capacity : (m + 1) * capacity].astype(BF16)
+
+
+def pack(kept, got, targets, me, sums, peers, capacity, direct, labelled):
+    rows, width = kept.shape
+    width = width + (LANES if labelled else 0) + (0 if sums is None else LANES)
+    operands = [me, targets, kept, got] + ([] if sums is None else [sums])
+    if direct:
+        out_shape = [jax.ShapeDtypeStruct((capacity, width), BF16)] * peers
+    else:
+        out_shape = [jax.ShapeDtypeStruct((peers * capacity, width), BF16)]
+    return pl.pallas_call(
+        functools.partial(pack_kernel, peers, capacity, direct, labelled, sums is not None),
+        out_shape=out_shape,
+        in_specs=[pl.BlockSpec(memory_space=pltpu.SMEM)] + vmem(len(operands) - 1),
+        out_specs=vmem(len(out_shape)),
         compiler_params=pltpu.CompilerParams(vmem_limit_bytes=VMEM_BYTES),
         cost_estimate=pl.CostEstimate(
             flops=2 * rows * peers * capacity * width,
@@ -168,6 +181,18 @@
         ),
         name="pack",
     )(*operands)
+
+
+def route(packed, peers, direct):
+    if not direct:
+        return [exchange(packed[0], "seq", peers)]
+    routed = {0: packed[0]}
+    half = peers // 2
+    for near in range(half):
+        for m in (half + near, near):
+            if m:
+                routed[m] = swap(packed[m], "seq", m)
+    return [routed[m] for m in range(peers)]
 
 
 def swap(x, axis, mask):
@@ -226,19 +251,27 @@
     )(queries, keys, ids)
 
 
-def norm_kernel(peers, copies, patches_ref, gain_ref, routed_ref, out_ref, share_ref):
+def norm_kernel(counts, parts, capacity, share, patches_ref, gain_ref, *refs):
+    chunks, at = [], 0
+    for count in counts:
+        pieces = [ref[...].astype(F32) for ref in refs[at : at + count]]
+        chunks.append(jnp.concatenate(pieces, axis=0) if count > 1 else pieces[0])
+        at += count
+    out_ref, share_ref = refs[at:]
     patches, width = patches_ref.shape
-    slots = routed_ref.shape[0]
-    per_token = routed_ref.shape[1] // width
-    labels = routed_ref[:, per_token * width : per_token * width + LANES].astype(F32)[:, :1]
-    columns = [routed_ref[:, c * width : (c + 1) * width].astype(F32) for c in range(per_token)]
+    slots = chunks[0].shape[0]
+    columns = []
+    for chunk, count in zip(chunks, parts):
+        columns += [chunk[:, c * width : (c + 1) * width] for c in range(count)]
+    per_token = len(columns)
     held = jnp.concatenate(columns, axis=0).astype(BF16)
-    lanes = len(columns) * slots
+    labels = chunks[0][:, parts[0] * width : parts[0] * width + 1]
+    lanes = per_token * slots
     lane = iota((slots, lanes), 1)
     row_of_lane = jnp.sum(
         jnp.where(lane % slots == iota((slots, lanes), 0), labels, 0.0), axis=0, keepdims=True
     ).astype(jnp.int32)
-    patch_of_lane = row_of_lane * len(columns) + iota((1, lanes), 1) // slots
+    patch_of_lane = row_of_lane * per_token + iota((1, lanes), 1) // slots
     patch_of_lane = jnp.where(row_of_lane < 0, -1, patch_of_lane)
     chosen = patch_of_lane == iota((patches, lanes), 0)
     patch_grads = dot(chosen.astype(F32).astype(BF16), held, (1, 0))
@@ -246,40 +279,91 @@
     inverse_rms = lax.rsqrt(jnp.mean(inputs * inputs, axis=1, keepdims=True) + 1e-06)
     normed = inputs * inverse_rms
     gain_part = jnp.sum(patch_grads * normed, axis=0, keepdims=True)
-    if copies:
-        rows = [gain_part[:, at : at + LANES] for at in range(0, width, LANES)]
-        carried = routed_ref[:, per_token * width + LANES :].astype(F32)
-        capacity = slots // peers
-        pieces = share_ref.shape[1] - len(rows)
-        for piece in range(pieces):
-            kept = iota((slots, LANES), 0) % capacity % pieces == piece
-            kept = jnp.logical_and(kept, iota((slots, LANES), 0) % capacity < 3 * pieces)
-            rows.append(jnp.sum(jnp.where(kept, carried, 0.0), axis=0, keepdims=True))
-        for at, row in enumerate(rows):
-            share_ref[:, at : at + 1, :] = jnp.broadcast_to(row[None], (copies, 1, LANES))
-    else:
-        share_ref[...] = gain_part
+    copies = share_ref.shape[0]
+    share_ref[:, :, :width] = jnp.broadcast_to(gain_part[None], (copies, 1, width))
+    if share:
+        carried = chunks[0][:, parts[0] * width + LANES :]
+        row = iota((slots, LANES), 0) % capacity
+        for piece in range(share):
+            kept = jnp.logical_and(row % share == piece, row < 3 * share)
+            line = jnp.sum(jnp.where(kept, carried, 0.0), axis=0, keepdims=True)
+            share_ref[:, :, width + piece * LANES : width + (piece + 1) * LANES] = jnp.broadcast_to(
+                line[None], (copies, 1, LANES)
+            )
     scaled = gain_ref[...] * patch_grads
     out_ref[...] = (
         inverse_rms * (scaled - normed * jnp.mean(scaled * normed, axis=1, keepdims=True))
     ).astype(BF16)
 
 
-def norm_backward(routed, peers, patches, gain, share):
+def norm_backward(received, parts, capacity, patches, gain, copies, share):
+    counts = [len(chunk) for chunk in received]
+    flat = [x for chunk in received for x in chunk]
     count, width = patches.shape
-    return pl.pallas_call(
-        functools.partial(norm_kernel, peers, share[0] if len(share) == 3 else 0),
-        out_shape=[jax.ShapeDtypeStruct((count, width), BF16), jax.ShapeDtypeStruct(share, F32)],
-        in_specs=vmem(3),
+    routed = sum(x.size for x in flat)
+    return pl.pallas_call(
+        functools.partial(norm_kernel, counts, parts, capacity, share),
+        out_shape=[
+            jax.ShapeDtypeStruct((count, width), BF16),
+            jax.ShapeDtypeStruct((copies, 1, width + share * LANES), F32),
+        ],
+        in_specs=vmem(2 + len(flat)),
         out_specs=vmem(2),
         compiler_params=pltpu.CompilerParams(vmem_limit_bytes=VMEM_BYTES),
         cost_estimate=pl.CostEstimate(
-            flops=2 * count * routed.size,
-            bytes_accessed=4 * count * width + 2 * routed.size,
+            flops=2 * count * routed,
+            bytes_accessed=4 * count * width + 2 * routed,
             transcendentals=0,
         ),
         name="norm",
-    )(patches, gain, routed)
+    )(patches, gain, *flat)
+
+
+def gather_kernel(width, shared_ref, out_ref):
+    copies, _, wide = shared_ref.shape
+    total = shared_ref[0, :, :width]
+    for copy in range(1, copies):
+        total = total + shared_ref[copy, :, :width]
+    out_ref[:, :width] = total
+    piece = wide - width
+    for copy in range(copies):
+        at = width + copy * piece
+        out_ref[:, at : at + piece] = shared_ref[copy, :, width:]
+
+
+def finish_kernel(blocks, width, gain_scale, bias_scale, image_ref, *refs):
+    shares, (gain_ref, bias_ref) = refs[:blocks], refs[blocks:]
+    gains = [ref[:, :width] for ref in shares]
+    while len(gains) > 1:
+        gains = [gains[i] + gains[i + 1] for i in range(0, len(gains), 2)]
+    gain_ref[...] = gains[0] * gain_scale
+    for j in range(blocks):
+        bias_ref[pl.ds(image_ref[0] ^ j, 1), :] = shares[j][:, width:] * bias_scale
+
+
+def sum_shares(shared, width, gain_scale, bias_scale):
+    images, peers = lax.axis_size("img"), lax.axis_size("seq")
+    shared = exchange(shared, "seq", peers)
+    piece = shared.shape[2] - width
+    share = pl.pallas_call(
+        functools.partial(gather_kernel, width),
+        out_shape=jax.ShapeDtypeStruct((1, width + peers * piece), F32),
+        in_specs=vmem(1),
+        out_specs=pl.BlockSpec(memory_space=pltpu.VMEM),
+        name="gather",
+    )(shared)
+    shares = [share] + [swap(share, "img", j) for j in range(1, images)]
+    gain, bias = pl.pallas_call(
+        functools.partial(finish_kernel, images, width, gain_scale, bias_scale),
+        out_shape=[
+            jax.ShapeDtypeStruct((1, width), F32),
+            jax.ShapeDtypeStruct((images, peers * piece), F32),
+        ],
+        in_specs=[pl.BlockSpec(memory_space=pltpu.SMEM)] + vmem(images),
+        out_specs=vmem(2),
+        name="finish",
+    )(lax.axis_index("img").reshape(1), *shares)
+    return gain[0], bias.reshape(-1)
 
 
 def window_kernel(g_ref, q_ref, k_ref, v_ref, probs_ref, probs_t_ref, dq_ref, dk_ref, dv_ref):
@@ -342,17 +426,16 @@
     grad_rows = llm_grads[0]
     rows = grad_rows.shape[0]
     images, peers = lax.axis_size("img"), lax.axis_size("seq")
-    devices = images * peers
     capacity = max(1, 2 * rows // peers)
     block = w_down.shape[1]
     width = patches.shape[2]
     pieces = block // peers // LANES
-    carries = pieces > 0 and 3 * pieces <= capacity
+    direct = max(images, peers) <= DIRECT and pieces > 0 and 3 * pieces <= capacity
 
     order = [0]
     while len(order) < images:
         order = [2 * j for j in order] + [2 * j + 1 for j in order]
-    image = lax.axis_index("img")
+    image, me = lax.axis_index("img"), lax.axis_index("seq")
 
     def columns(j):
         return lax.dynamic_slice(grad_rows, (0, (image ^ j) * block), (rows, block))
@@ -360,8 +443,9 @@
     x_blocks = [columns(0)] + [swap(columns(j), "img", j) for j in range(1, images)]
     x_blocks = [x_blocks[j] for j in order]
     probs, probs_t = window_probs(queries[0], keys[0], window_ids[0])
-
-    terms, first = [], 0
+    token_target, probs, probs_t = lax.optimization_barrier((token_target, probs, probs_t))
+
+    received, first = [], 0
     for index, count in enumerate(CHUNKS):
         w_rows = lax.slice_in_dim(w_down, first, first + count * width)
         w_rows = pltpu.with_memory_space_constraint(w_rows, pltpu.VMEM)
@@ -373,23 +457,25 @@
         while 2 * mask < images:
             kept, sent = halve(kept, swap(sent, "img", mask))
             mask *= 2
-        terms.append((kept, swap(sent, "img", mask)))
-    packed = pack(terms, token_target, bias_part, peers, capacity, carries)
-    routed = exchange(packed, "seq", peers)
-
-    gain_rows = width // LANES
-    share = (devices, gain_rows + pieces, LANES) if carries else (1, width)
-    out_grads, shared = norm_backward(routed, peers, patches[0], gain[None], share)
-    if carries:
-        shared = exchange(shared, ("img", "seq"), devices)
-        gain_total = jnp.sum(shared[:, :gain_rows], axis=0).reshape(-1)
-        bias_total = shared[:, gain_rows:].reshape(-1)
+        got = swap(sent, "img", mask)
+        carried = bias_part if index == 0 and direct else None
+        packed = pack(
+            kept, got, token_target, me.reshape(1), carried, peers, capacity, direct, index == 0
+        )
+        received.append(route(packed, peers, direct))
+
+    gain_scale = 1.0 / math.sqrt(images * peers * patches.shape[1])
+    bias_scale = 1.0 / math.sqrt(images * peers * rows)
+    share, copies = (pieces, peers) if direct else (0, 1)
+    out_grads, shared = norm_backward(
+        received, CHUNKS, capacity, patches[0], gain[None], copies, share
+    )
+    if direct:
+        gain_grad, bias_grad = sum_shares(shared, width, gain_scale, bias_scale)
     else:
-        gain_total = lax.psum(shared[0], ("img", "seq"))
-        bias_total = lax.all_gather(lax.psum(bias_part[0], "seq"), "img", tiled=True)
+        gain_grad = lax.psum(shared[0, 0], ("img", "seq")) * gain_scale
+        bias_grad = lax.all_gather(lax.psum(bias_part[0], "seq"), "img", tiled=True) * bias_scale
     grads = window_backward(out_grads, queries[0], keys[0], values[0], probs, probs_t)
-    gain_grad = gain_total / math.sqrt(devices * patches.shape[1])
-    bias_grad = bias_total / math.sqrt(devices * rows)
     return (grads[0][None], grads[1][None], grads[2][None], gain_grad, bias_grad)
 
 

time: 72.1 us -> 83.7 us (1.16)
  waiting for transfers between devices: 31.2 us -> 12.6 us
  starting transfers between devices: 16.7 us -> 27.7 us
  blocking collectives: 0 us -> 10.4 us
  Pallas kernels: 12.1 us -> 16.7 us
  local copies, waits for them, and re-layouts: 9.73 us -> 13.6 us
    all_to_all x2 -> x0, waiting for transfers between devices: 24.5 us -> none  [exchange(): lax.all_to_all(x, axis, split_axis=0, concat_axis=0, tiled=True)]
    ppermute x7 -> x24, starting transfers between devices: 7.06 us -> 27.7 us  [swap(): return lax.ppermute(x, axis, [(i, i ^ mask) for i in range(n)])]
    all_to_all x0 -> x1, blocking collectives: none -> 10.4 us  [exchange(): lax.all_to_all(x, axis, split_axis=0, concat_axis=0, tiled=True)]
    all_to_all x2 -> x0, starting transfers between devices: 9.64 us -> none  [exchange(): lax.all_to_all(x, axis, split_axis=0, concat_axis=0, tiled=True)]
    ppermute x7 -> x24, waiting for transfers between devices: 6.74 us -> 12.6 us  [swap(): return lax.ppermute(x, axis, [(i, i ^ mask) for i in range(n)])]
    unnamed x14 -> x23, local copies, waits for them, and re-layouts: 0.04 us -> 3.95 us
    pallas_call x2 -> x5, Pallas kernels: 2.46 us -> 5.83 us  [the longest x2 2.51 us: pack(): pl.pallas_call(functools.partial(pack_kernel, peers, capacity, direct, la...]
    pallas_call x0 -> x1, other arithmetic: none -> 1.31 us  [sum_shares(): pl.pallas_call(functools.partial(finish_kernel, images, width, gain_scale...]
  transfers between devices with their start and end apart: 9 -> 24, of which waited for: 4 -> 6; matrix products, arithmetic and copies ran while one was open for 12% -> 10% of each run, Pallas kernels for 9% -> 13%
where the time goes in v5:
time: 83.7 us; the launch traced here: 83.2 us
  starting transfers between devices  27.7 us (33%)
  Pallas kernels  16.7 us (20%)
  local copies, waits for them, and re-layouts  13.6 us (16%)
  waiting for transfers between devices  12.6 us (15%)
  blocking collectives  10.4 us (12%)
  other arithmetic  1.31 us (2%)
  between operations  0.85 us (1%)
    ppermute x24, starting transfers between devices, swap(): return lax.ppermute(x, axis, [(i, i ^ mask) for i in range(n)])  27.7 us
    ppermute x24, waiting for transfers between devices, swap(): return lax.ppermute(x, axis, [(i, i ^ mask) for i in range(n)])  12.6 us
    all_to_all x1, blocking collectives, exchange(): lax.all_to_all(x, axis, split_axis=0, concat_axis=0, tiled=True)  10.4 us
    slice x1, local copies, waits for them, and re-layouts, body(): w_rows = lax.slice_in_dim(w_down, first, first + count * width)  8.54 us
    pallas_call x2, Pallas kernels, project(): pl.pallas_call(functools.partial(project_kernel, blocks, tile, with_sum),...  6.03 us
    unnamed x23, local copies, waits for them, and re-layouts  3.95 us
    pallas_call x2, Pallas kernels, pack(): pl.pallas_call(functools.partial(pack_kernel, peers, capacity, direct, la...  2.51 us
    pallas_call x1, Pallas kernels, window_backward(): pl.pallas_call(window_kernel, out_shape=[shape] * 3, in_specs=vmem(6), ou...  2.38 us
  transfers between devices with their start and end apart: 24, of which 6 were waited for; matrix products, arithmetic and copies ran while one was open for 10% of the time, Pallas kernels for 13%

profile of v5, /device:TPU:0, one launch (start us, length us, event | category | flops | bytes accessed | tf_op | source)
XLA Modules:
  0.0 83.2 jit_solution(3765602289435315140)
XLA Ops:
  0.7 1.1 %dynamic-slice_bitcast_fusion = (bf16[32,2048]{1,0:T(8,128)(2,1)S(1)}, bf16[32,2048]{1,0:T(8,128)(2,1)S(1)}, bf16[32,2048]{1,0:T(8,128)(2,1)S(1)}, bf16[32,2048]{1,0:T(8,128)(2,1)S(1)}) fusion(bf16[1,32,8192]{2,1,0:T(8,128)(2,1)} %param.9, s32[]{:T(128)S(6)} %select_n.15, s32[]{:T(128)S(6)} %select_n.13, s32[]{:T(128)S(6)} %select_n.12, s32[]{:T(128)S(6)} %select_n.14), kind=kLoop, calls=%fused_computation | loop fusion | bytes 1048592 | tf_op jit(solution)/shard_map/dynamic_slice | solution.py:441
  1.8 3.0 %collective-permute-start = (bf16[32,2048]{1,0:T(8,128)(2,1)S(1)}, bf16[32,2048]{1,0:T(8,128)(2,1)S(1)}, u32[]{:S(2)}, u32[]{:S(2)}) collective-permute-start(bf16[32,2048]{1,0:T(8,128)(2,1)S(1)} %get-tuple-element.82), channel_id=1, source_target_pairs={{0,16},{8,24},{16,0},{24,8},{1,17},{9,25},{17,1},{25,9},{2,18},{10... | collective-permute-start | bytes 393224 | tf_op jit(solution)/shard_map/ppermute | solution.py:200
  4.8 0.0 collective-permute-start.1
  4.8 0.2 collective-permute-start.2
  5.0 8.5 %fusion = (bf16[2560,2048]{1,0:T(8,128)(2,1)S(1)}, bf16[2560,2048]{1,0:T(8,128)(2,1)S(1)}) fusion(bf16[5120,2048]{1,0:T(8,128)(2,1)} %param.13), kind=kLoop, calls=%fused_computation.4 | loop fusion | bytes 41943040 | tf_op jit(solution)/shard_map/slice | solution.py:450
  13.6 0.0 collective-permute-done.refs_1_
  13.6 0.0 collective-permute-done.1.refs_2_
  13.6 0.0 copy-start.1
  13.6 0.0 copy-start.2
  13.6 0.0 copy-start.6
  13.7 0.0 copy-start.5
  13.7 0.0 copy-start.10
  13.7 0.0 copy-start
  13.7 3.0 %project.3 = (bf16[64,2560]{1,0:T(8,128)(2,1)S(1)}, bf16[64,2560]{1,0:T(8,128)(2,1)S(1)}) custom-call(bf16[32,2048]{1,0:T(8,128)(2,1)S(1)} %get-tuple-element.83.refs_0_, bf16[32,2048]{1,0:T(8,128)(2,1)S(1)} %collective-permute-done.refs_1_, bf16[32,2048]{1,0:T(8,128)(2,1)S(1)} %collective-permute-done.1.refs_2_, ...), custom_call_target="tpu_custom_call" | custom-call | flops 1342177280 | bytes 10485760 | tf_op jit(solution)/shard_map/project/pallas_call | solution.py:75
  16.7 0.4 collective-permute-start.12
  17.1 3.0 %project.2 = (bf16[64,2560]{1,0:T(8,128)(2,1)S(1)}, bf16[64,2560]{1,0:T(8,128)(2,1)S(1)}, f32[1,2048]{1,0:T(1,128)S(1)}) custom-call(bf16[32,2048]{1,0:T(8,128)(2,1)S(1)} %get-tuple-element.83.refs_0_, bf16[32,2048]{1,0:T(8,128)(2,1)S(1)} %collective-permute-done.refs_1_, bf16[32,2048]{1,0:T(8,128)(2,1)S(1)} %collective-permute-done.1.refs_2_, ...), custom_call_target="tpu_custom_call" | custom-call | flops 1342177280 | bytes 10485760 | tf_op jit(solution)/shard_map/project/pallas_call | solution.py:75
  20.1 0.3 collective-permute-start.3
  20.4 0.7 halve.3
  21.1 1.9 %collective-permute-start.13 = (bf16[32,2560]{1,0:T(8,128)(2,1)}, bf16[32,2560]{1,0:T(8,128)(2,1)}, u32[]{:S(2)}, u32[]{:S(2)}) collective-permute-start(bf16[32,2560]{1,0:T(8,128)(2,1)} %get-tuple-element.61), channel_id=1, source_target_pairs={{0,16},{8,24},{16,0},{24,8},{1,17},{9,25},{17,1},{25,9},{2,18},{10... | collective-permute-start | bytes 491528 | tf_op jit(solution)/shard_map/ppermute | solution.py:200
  23.0 0.7 halve.2
  23.7 0.5 collective-permute-start.4
  24.3 1.1 %probs.1 = (f32[16,128,128]{2,1,0:T(8,128)S(1)}, f32[16,128,128]{2,1,0:T(8,128)S(1)}) custom-call(bf16[128,1280]{1,0:T(8,128)(2,1)S(1)} %bitcast.21, bf16[128,1280]{1,0:T(8,128)(2,1)S(1)} %bitcast.23, s32[1,32]{1,0:T(1,128)S(1)} %bitcast.26), custom_call_target="tpu_custom_call" | custom-call | flops 268435456 | bytes 2097152 | tf_op jit(solution)/shard_map/probs/pallas_call | solution.py:239
  25.4 3.1 %collective-permute-done.13.got_ref = bf16[32,2560]{1,0:T(8,128)(2,1)} collective-permute-done((bf16[32,2560]{1,0:T(8,128)(2,1)}, bf16[32,2560]{1,0:T(8,128)(2,1)}, u32[]{:S(2)}, u32[]{:S(2)}) %collective-permute-start.13) | collective-permute-done | bytes 163872 | tf_op jit(solution)/shard_map/ppermute | solution.py:200
  28.4 1.2 %pack.3 = (bf16[8,2560]{1,0:T(8,128)(2,1)S(1)}, bf16[8,2560]{1,0:T(8,128)(2,1)S(1)}, bf16[8,2560]{1,0:T(8,128)(2,1)S(1)}, bf16[8,2560]{1,0:T(8,128)(2,1)S(1)}, b...) custom-call(s32[1]{0:T(128)} %bitcast.1.me_ref, ...), custom_call_target="tpu_custom_call" | custom-call | flops 10485760 | bytes 819200 | tf_op jit(solution)/shard_map/pack/pallas_call | solution.py:171
  29.7 2.0 %collective-permute-start.14 = (bf16[8,2560]{1,0:T(8,128)(2,1)S(1)}, bf16[8,2560]{1,0:T(8,128)(2,1)S(1)}, u32[]{:S(2)}, u32[]{:S(2)}) collective-permute-start(bf16[8,2560]{1,0:T(8,128)(2,1)S(1)} %get-tuple-element.63), channel_id=1, source_target_pairs={{0,1},{1,0},{2,3},{3,2},{4,5},{5,4},{6,7},{7,6},{8,9},{9,8},{10,11... | collective-permute-start | bytes 122888 | tf_op jit(solution)/shard_map/ppermute | solution.py:200
  31.7 1.6 %collective-permute-start.15 = (bf16[8,2560]{1,0:T(8,128)(2,1)S(1)}, bf16[8,2560]{1,0:T(8,128)(2,1)S(1)}, u32[]{:S(2)}, u32[]{:S(2)}) collective-permute-start(bf16[8,2560]{1,0:T(8,128)(2,1)S(1)} %get-tuple-element.64), channel_id=1, source_target_pairs={{0,2},{1,3},{2,0},{3,1},{4,6},{5,7},{6,4},{7,5},{8,10},{9,11},{10,... | collective-permute-start | bytes 122888 | tf_op jit(solution)/shard_map/ppermute | solution.py:200
  33.3 3.0 %collective-permute-start.17 = (bf16[8,2560]{1,0:T(8,128)(2,1)S(1)}, bf16[8,2560]{1,0:T(8,128)(2,1)S(1)}, u32[]{:S(2)}, u32[]{:S(2)}) collective-permute-start(bf16[8,2560]{1,0:T(8,128)(2,1)S(1)} %get-tuple-element.66), channel_id=1, source_target_pairs={{0,4},{1,5},{2,6},{3,7},{4,0},{5,1},{6,2},{7,3},{8,12},{9,13},{10,... | collective-permute-start | bytes 122888 | tf_op jit(solution)/shard_map/ppermute | solution.py:200
  36.3 0.0 collective-permute-done.4.got_ref
  36.3 1.3 %pack.2 = (bf16[8,2816]{1,0:T(8,128)(2,1)S(1)}, bf16[8,2816]{1,0:T(8,128)(2,1)S(1)}, bf16[8,2816]{1,0:T(8,128)(2,1)S(1)}, bf16[8,2816]{1,0:T(8,128)(2,1)S(1)}, b...) custom-call(s32[1]{0:T(128)} %bitcast.1.me_ref, ...), custom_call_target="tpu_custom_call" | custom-call | flops 11534336 | bytes 901120 | tf_op jit(solution)/shard_map/pack/pallas_call | solution.py:171
  37.6 1.4 %collective-permute-start.10 = (bf16[8,2816]{1,0:T(8,128)(2,1)S(1)}, bf16[8,2816]{1,0:T(8,128)(2,1)S(1)}, u32[]{:S(2)}, u32[]{:S(2)}) collective-permute-start(bf16[8,2816]{1,0:T(8,128)(2,1)S(1)} %get-tuple-element.56), channel_id=1, source_target_pairs={{0,6},{1,7},{2,4},{3,5},{4,2},{5,3},{6,0},{7,1},{8,14},{9,15},{10,... | collective-permute-start | bytes 135176 | tf_op jit(solution)/shard_map/ppermute | solution.py:200
  39.0 3.4 %collective-permute-start.11 = (bf16[8,2816]{1,0:T(8,128)(2,1)S(1)}, bf16[8,2816]{1,0:T(8,128)(2,1)S(1)}, u32[]{:S(2)}, u32[]{:S(2)}) collective-permute-start(bf16[8,2816]{1,0:T(8,128)(2,1)S(1)} %get-tuple-element.57), channel_id=1, source_target_pairs={{0,7},{1,6},{2,5},{3,4},{4,3},{5,2},{6,1},{7,0},{8,15},{9,14},{10,... | collective-permute-start | bytes 135176 | tf_op jit(solution)/shard_map/ppermute | solution.py:200
  42.4 0.0 collective-permute-done.15.refs_10_
  42.4 0.0 collective-permute-start.18
  42.4 0.0 collective-permute-done.16.refs_11_
  42.4 2.1 %collective-permute-start.19 = (bf16[8,2560]{1,0:T(8,128)(2,1)S(1)}, bf16[8,2560]{1,0:T(8,128)(2,1)S(1)}, u32[]{:S(2)}, u32[]{:S(2)}) collective-permute-start(bf16[8,2560]{1,0:T(8,128)(2,1)S(1)} %get-tuple-element.68), channel_id=1, source_target_pairs={{0,6},{1,7},{2,4},{3,5},{4,2},{5,3},{6,0},{7,1},{8,14},{9,15},{10,... | collective-permute-start | bytes 122888 | tf_op jit(solution)/shard_map/ppermute | solution.py:200
  44.5 0.0 collective-permute-done.17.refs_12_
  44.5 1.9 %collective-permute-start.20 = (bf16[8,2560]{1,0:T(8,128)(2,1)S(1)}, bf16[8,2560]{1,0:T(8,128)(2,1)S(1)}, u32[]{:S(2)}, u32[]{:S(2)}) collective-permute-start(bf16[8,2560]{1,0:T(8,128)(2,1)S(1)} %get-tuple-element.69), channel_id=1, source_target_pairs={{0,7},{1,6},{2,5},{3,4},{4,3},{5,2},{6,1},{7,0},{8,15},{9,14},{10,... | collective-permute-start | bytes 122888 | tf_op jit(solution)/shard_map/ppermute | solution.py:200
  46.4 2.2 %collective-permute-done.18.refs_13_ = bf16[8,2560]{1,0:T(8,128)(2,1)S(1)} collective-permute-done((bf16[8,2560]{1,0:T(8,128)(2,1)S(1)}, bf16[8,2560]{1,0:T(8,128)(2,1)S(1)}, u32[]{:S(2)}, u32[]{:S(2)}) %collective-permute-start.18) | collective-permute-done | bytes 40992 | tf_op jit(solution)/shard_map/ppermute | solution.py:200
  48.6 0.2 collective-permute-start.5
  48.8 0.0 collective-permute-done.19.refs_14_
  48.8 2.4 %collective-permute-done.20.refs_15_ = bf16[8,2560]{1,0:T(8,128)(2,1)S(1)} collective-permute-done((bf16[8,2560]{1,0:T(8,128)(2,1)S(1)}, bf16[8,2560]{1,0:T(8,128)(2,1)S(1)}, u32[]{:S(2)}, u32[]{:S(2)}) %collective-permute-start.20) | collective-permute-done | bytes 40992 | tf_op jit(solution)/shard_map/ppermute | solution.py:200
  51.2 0.9 %collective-permute-start.7 = (bf16[8,2816]{1,0:T(8,128)(2,1)S(1)}, bf16[8,2816]{1,0:T(8,128)(2,1)S(1)}, u32[]{:S(2)}, u32[]{:S(2)}) collective-permute-start(bf16[8,2816]{1,0:T(8,128)(2,1)S(1)} %get-tuple-element.53), channel_id=1, source_target_pairs={{0,3},{1,2},{2,1},{3,0},{4,7},{5,6},{6,5},{7,4},{8,11},{9,10},{10,... | collective-permute-start | bytes 135176 | tf_op jit(solution)/shard_map/ppermute | solution.py:200
  52.1 0.0 collective-permute-done.10.refs_6_
  52.1 1.6 %collective-permute-start.8 = (bf16[8,2816]{1,0:T(8,128)(2,1)S(1)}, bf16[8,2816]{1,0:T(8,128)(2,1)S(1)}, u32[]{:S(2)}, u32[]{:S(2)}) collective-permute-start(bf16[8,2816]{1,0:T(8,128)(2,1)S(1)} %get-tuple-element.54), channel_id=1, source_target_pairs={{0,4},{1,5},{2,6},{3,7},{4,0},{5,1},{6,2},{7,3},{8,12},{9,13},{10,... | collective-permute-start | bytes 135176 | tf_op jit(solution)/shard_map/ppermute | solution.py:200
  53.7 0.0 collective-permute-done.11.refs_7_
  53.7 1.4 %collective-permute-start.9 = (bf16[8,2816]{1,0:T(8,128)(2,1)S(1)}, bf16[8,2816]{1,0:T(8,128)(2,1)S(1)}, u32[]{:S(2)}, u32[]{:S(2)}) collective-permute-start(bf16[8,2816]{1,0:T(8,128)(2,1)S(1)} %get-tuple-element.55), channel_id=1, source_target_pairs={{0,5},{1,4},{2,7},{3,6},{4,1},{5,0},{6,3},{7,2},{8,13},{9,12},{10,... | collective-permute-start | bytes 135176 | tf_op jit(solution)/shard_map/ppermute | solution.py:200
  55.1 0.0 collective-permute-done.6.refs_2_
  55.1 1.0 %collective-permute-done.7.refs_3_ = bf16[8,2816]{1,0:T(8,128)(2,1)S(1)} collective-permute-done((bf16[8,2816]{1,0:T(8,128)(2,1)S(1)}, bf16[8,2816]{1,0:T(8,128)(2,1)S(1)}, u32[]{:S(2)}, u32[]{:S(2)}) %collective-permute-start.7) | collective-permute-done | bytes 45088 | tf_op jit(solution)/shard_map/ppermute | solution.py:200
  56.1 0.9 %collective-permute-done.8.refs_4_ = bf16[8,2816]{1,0:T(8,128)(2,1)S(1)} collective-permute-done((bf16[8,2816]{1,0:T(8,128)(2,1)S(1)}, bf16[8,2816]{1,0:T(8,128)(2,1)S(1)}, u32[]{:S(2)}, u32[]{:S(2)}) %collective-permute-start.8) | collective-permute-done | bytes 45088 | tf_op jit(solution)/shard_map/ppermute | solution.py:200
  57.1 2.9 %collective-permute-done.9.refs_5_ = bf16[8,2816]{1,0:T(8,128)(2,1)S(1)} collective-permute-done((bf16[8,2816]{1,0:T(8,128)(2,1)S(1)}, bf16[8,2816]{1,0:T(8,128)(2,1)S(1)}, u32[]{:S(2)}, u32[]{:S(2)}) %collective-permute-start.9) | collective-permute-done | bytes 45088 | tf_op jit(solution)/shard_map/ppermute | solution.py:200
  60.0 0.5 norm.1
  60.5 10.4 %all_to_all.5.shared_ref = f32[8,1,1536]{2,1,0:T(1,128)} all-to-all(f32[8,1,1536]{2,1,0:T(1,128)S(1)} %get-tuple-element.76), channel_id=1, replica_groups=mesh['img'=4,'seq'=8] {'seq'}, dimensions={0} | all-to-all | bytes 98304 | tf_op jit(solution)/shard_map/all_to_all | solution.py:207
  70.9 1.4 %gather.1.refs_0_ = f32[1,3328]{1,0:T(1,128)} custom-call(f32[8,1,1536]{2,1,0:T(1,128)} %all_to_all.5.shared_ref), custom_call_target="tpu_custom_call" | custom-call | tf_op jit(solution)/shard_map/gather/pallas_call | solution.py:348
  72.3 1.5 %collective-permute-start.22 = (f32[1,3328]{1,0:T(1,128)}, f32[1,3328]{1,0:T(1,128)S(1)}, u32[]{:S(2)}, u32[]{:S(2)}) collective-permute-start(f32[1,3328]{1,0:T(1,128)} %gather.1.refs_0_), channel_id=1, source_target_pairs={{0,16},{8,24},{16,0},{24,8},{1,17},{9,25},{17,1},{25,9},{2,18},{10... | collective-permute-start | bytes 39944 | tf_op jit(solution)/shard_map/ppermute | solution.py:200
  73.8 0.3 collective-permute-start.23
  74.2 1.0 %copy-done.3 = bf16[1,128,1280]{2,1,0:T(8,128)(2,1)S(1)} copy-done((bf16[1,128,1280]{2,1,0:T(8,128)(2,1)S(1)}, bf16[1,128,1280]{2,1,0:T(8,128)(2,1)}, u32[]{:S(2)}) %copy-start.3) | copy-done | bytes 327704
  75.1 1.0 %copy-done.4 = bf16[1,128,1280]{2,1,0:T(8,128)(2,1)S(1)} copy-done((bf16[1,128,1280]{2,1,0:T(8,128)(2,1)S(1)}, bf16[1,128,1280]{2,1,0:T(8,128)(2,1)}, u32[]{:S(2)}) %copy-start.4) | copy-done | bytes 327704
  76.1 2.4 %window.1 = (bf16[128,1280]{1,0:T(8,128)(2,1)}, bf16[128,1280]{1,0:T(8,128)(2,1)}, bf16[128,1280]{1,0:T(8,128)(2,1)}) custom-call(bf16[128,1280]{1,0:T(8,128)(2,1)S(1)} %get-tuple-element.70.g_ref, bf16[128,1280]{1,0:T(8,128)(2,1)S(1)} %bitcast.22, bf16[128,1280]{1,0:T(8,128)(2,1)S(1)} %bitcast.24, bf16[128,1280]{1,0:T(8,128)(2,1)S(1)} %bitcast.25, ...), custom_call_target="tpu_custom_call" | custom-call | flops 335544320 | bytes 4390912 | tf_op jit(solution)/shard_map/window/pallas_call | solution.py:410
  78.5 0.6 copy-done.7
  79.1 0.0 copy-done.8
  79.1 0.0 copy-done.9
  79.1 1.4 %finish.1 = (f32[1,1280]{1,0:T(1,128)}, f32[4,2048]{1,0:T(4,128)}) custom-call(s32[1]{0:T(128)} %bitcast.13.image_ref, f32[1,3328]{1,0:T(1,128)} %gather.1.refs_0_, f32[1,3328]{1,0:T(1,128)} %copy-done.7, f32[1,3328]{1,0:T(1,128)} %copy-done.8, f32[1,3328]{1,0:T(1,128)} %copy-done.9), custom_call_target="tpu_custom_call" | custom-call | tf_op jit(solution)/shard_map/finish/pallas_call | solution.py:356
  80.5 1.4 %copy.14 = f32[1,16,4,128]{3,1,2,0:T(8,128)} copy(f32[1,16,4,128]{3,2,1,0:T(4,128)} %bitcast.28) | data formatting | bytes 65536
  81.9 1.3 %reduce = f32[1280]{0:T(1024)} reduce(f32[1,1280]{1,0:T(1,128)} %get-tuple-element.77, f32[]{:T(128)} %constant.31), dimensions={0}, to_apply=%get-tuple-element.77.reduce_sub_computation | reduce | bytes 10244 | tf_op jit(solution)/shard_map/finish/pallas_call | solution.py:356
  (23 shorter events, 0.1 us)
Async XLA Ops:
  1.8 11.8 %collective-permute-start = (bf16[32,2048]{1,0:T(8,128)(2,1)S(1)}, bf16[32,2048]{1,0:T(8,128)(2,1)S(1)}, u32[]{:S(2)}, u32[]{:S(2)}) collective-permute-start(bf16[32,2048]{1,0:T(8,128)(2,1)S(1)} %get-tuple-element.82), channel_id=1, source_target_pairs={{0,16},{8,24},{16,0},{24,8},{1,17},{9,25},{17,1},{25,9},{2,18},{10... | collective-permute-start | bytes 393224 | tf_op jit(solution)/shard_map/ppermute | solution.py:200
  4.8 8.8 %collective-permute-start.1 = (bf16[32,2048]{1,0:T(8,128)(2,1)S(1)}, bf16[32,2048]{1,0:T(8,128)(2,1)S(1)}, u32[]{:S(2)}, u32[]{:S(2)}) collective-permute-start(bf16[32,2048]{1,0:T(8,128)(2,1)S(1)} %get-tuple-element.84), channel_id=1, source_target_pairs={{0,8},{8,0},{16,24},{24,16},{1,9},{9,1},{17,25},{25,17},{2,10},{10... | collective-permute-start | bytes 393224 | tf_op jit(solution)/shard_map/ppermute | solution.py:200
  4.8 8.8 %collective-permute-start.2 = (bf16[32,2048]{1,0:T(8,128)(2,1)S(1)}, bf16[32,2048]{1,0:T(8,128)(2,1)S(1)}, u32[]{:S(2)}, u32[]{:S(2)}) collective-permute-start(bf16[32,2048]{1,0:T(8,128)(2,1)S(1)} %get-tuple-element.81), channel_id=1, source_target_pairs={{0,24},{8,16},{16,8},{24,0},{1,25},{9,17},{17,9},{25,1},{2,26},{10... | collective-permute-start | bytes 393224 | tf_op jit(solution)/shard_map/ppermute | solution.py:200
  13.6 10.7 %copy-start.1 = (bf16[1,128,1280]{2,1,0:T(8,128)(2,1)S(1)}, bf16[1,128,1280]{2,1,0:T(8,128)(2,1)}, u32[]{:S(2)}) copy-start(bf16[1,128,1280]{2,1,0:T(8,128)(2,1)} %param.14) | copy-start | bytes 983044
  13.6 10.7 %copy-start.2 = (bf16[1,128,1280]{2,1,0:T(8,128)(2,1)S(1)}, bf16[1,128,1280]{2,1,0:T(8,128)(2,1)}, u32[]{:S(2)}) copy-start(bf16[1,128,1280]{2,1,0:T(8,128)(2,1)} %param.15) | copy-start | bytes 983044
  13.6 10.6 %copy-start.6 = (s32[1,1,32]{2,1,0:T(1,128)S(1)}, s32[1,1,32]{2,1,0:T(1,128)}, u32[]{:S(2)}) copy-start(s32[1,1,32]{2,1,0:T(1,128)} %param.17) | copy-start | bytes 388
  13.7 14.8 %copy-start.5 = (s32[1,32]{1,0:T(1,128)S(1)}, s32[1,32]{1,0:T(1,128)}, u32[]{:S(2)}) copy-start(s32[1,32]{1,0:T(1,128)} %targets_ref.1) | copy-start | bytes 388
  13.7 41.4 %copy-start.10 = (f32[1280]{0:T(1024)S(1)}, f32[1280]{0:T(1024)}, u32[]{:S(2)}) copy-start(f32[1280]{0:T(1024)} %param.12) | copy-start | bytes 15364
  13.7 46.3 %copy-start = (bf16[1,128,1280]{2,1,0:T(8,128)(2,1)S(1)}, bf16[1,128,1280]{2,1,0:T(8,128)(2,1)}, u32[]{:S(2)}) copy-start(bf16[1,128,1280]{2,1,0:T(8,128)(2,1)} %param.11) | copy-start | bytes 983044
  16.7 3.7 %collective-permute-start.12 = (bf16[64,2560]{1,0:T(8,128)(2,1)S(1)}, bf16[64,2560]{1,0:T(8,128)(2,1)S(1)}, u32[]{:S(2)}, u32[]{:S(2)}) collective-permute-start(bf16[64,2560]{1,0:T(8,128)(2,1)S(1)} %get-tuple-element.59), channel_id=1, source_target_pairs={{0,8},{8,0},{16,24},{24,16},{1,9},{9,1},{17,25},{25,17},{2,10},{10... | collective-permute-start | bytes 983048 | tf_op jit(solution)/shard_map/ppermute | solution.py:200
  20.1 2.9 %collective-permute-start.3 = (bf16[64,2560]{1,0:T(8,128)(2,1)S(1)}, bf16[64,2560]{1,0:T(8,128)(2,1)S(1)}, u32[]{:S(2)}, u32[]{:S(2)}) collective-permute-start(bf16[64,2560]{1,0:T(8,128)(2,1)S(1)} %get-tuple-element.46), channel_id=1, source_target_pairs={{0,8},{8,0},{16,24},{24,16},{1,9},{9,1},{17,25},{25,17},{2,10},{10... | collective-permute-start | bytes 983048 | tf_op jit(solution)/shard_map/ppermute | solution.py:200
  21.1 7.3 %collective-permute-start.13 = (bf16[32,2560]{1,0:T(8,128)(2,1)}, bf16[32,2560]{1,0:T(8,128)(2,1)}, u32[]{:S(2)}, u32[]{:S(2)}) collective-permute-start(bf16[32,2560]{1,0:T(8,128)(2,1)} %get-tuple-element.61), channel_id=1, source_target_pairs={{0,16},{8,24},{16,0},{24,8},{1,17},{9,25},{17,1},{25,9},{2,18},{10... | collective-permute-start | bytes 491528 | tf_op jit(solution)/shard_map/ppermute | solution.py:200
  23.7 12.5 %collective-permute-start.4 = (bf16[32,2560]{1,0:T(8,128)(2,1)}, bf16[32,2560]{1,0:T(8,128)(2,1)}, u32[]{:S(2)}, u32[]{:S(2)}) collective-permute-start(bf16[32,2560]{1,0:T(8,128)(2,1)} %get-tuple-element.48), channel_id=1, source_target_pairs={{0,16},{8,24},{16,0},{24,8},{1,17},{9,25},{17,1},{25,9},{2,18},{10... | collective-permute-start | bytes 491528 | tf_op jit(solution)/shard_map/ppermute | solution.py:200
  29.7 9.3 %collective-permute-start.14 = (bf16[8,2560]{1,0:T(8,128)(2,1)S(1)}, bf16[8,2560]{1,0:T(8,128)(2,1)S(1)}, u32[]{:S(2)}, u32[]{:S(2)}) collective-permute-start(bf16[8,2560]{1,0:T(8,128)(2,1)S(1)} %get-tuple-element.63), channel_id=1, source_target_pairs={{0,1},{1,0},{2,3},{3,2},{4,5},{5,4},{6,7},{7,6},{8,9},{9,8},{10,11... | collective-permute-start | bytes 122888 | tf_op jit(solution)/shard_map/ppermute | solution.py:200
  31.7 10.7 %collective-permute-start.15 = (bf16[8,2560]{1,0:T(8,128)(2,1)S(1)}, bf16[8,2560]{1,0:T(8,128)(2,1)S(1)}, u32[]{:S(2)}, u32[]{:S(2)}) collective-permute-start(bf16[8,2560]{1,0:T(8,128)(2,1)S(1)} %get-tuple-element.64), channel_id=1, source_target_pairs={{0,2},{1,3},{2,0},{3,1},{4,6},{5,7},{6,4},{7,5},{8,10},{9,11},{10,... | collective-permute-start | bytes 122888 | tf_op jit(solution)/shard_map/ppermute | solution.py:200
  33.3 9.1 %collective-permute-start.16 = (bf16[8,2560]{1,0:T(8,128)(2,1)S(1)}, bf16[8,2560]{1,0:T(8,128)(2,1)S(1)}, u32[]{:S(2)}, u32[]{:S(2)}) collective-permute-start(bf16[8,2560]{1,0:T(8,128)(2,1)S(1)} %get-tuple-element.65), channel_id=1, source_target_pairs={{0,3},{1,2},{2,1},{3,0},{4,7},{5,6},{6,5},{7,4},{8,11},{9,10},{10,... | collective-permute-start | bytes 122888 | tf_op jit(solution)/shard_map/ppermute | solution.py:200
  33.3 11.2 %collective-permute-start.17 = (bf16[8,2560]{1,0:T(8,128)(2,1)S(1)}, bf16[8,2560]{1,0:T(8,128)(2,1)S(1)}, u32[]{:S(2)}, u32[]{:S(2)}) collective-permute-start(bf16[8,2560]{1,0:T(8,128)(2,1)S(1)} %get-tuple-element.66), channel_id=1, source_target_pairs={{0,4},{1,5},{2,6},{3,7},{4,0},{5,1},{6,2},{7,3},{8,12},{9,13},{10,... | collective-permute-start | bytes 122888 | tf_op jit(solution)/shard_map/ppermute | solution.py:200
  37.6 14.6 %collective-permute-start.10 = (bf16[8,2816]{1,0:T(8,128)(2,1)S(1)}, bf16[8,2816]{1,0:T(8,128)(2,1)S(1)}, u32[]{:S(2)}, u32[]{:S(2)}) collective-permute-start(bf16[8,2816]{1,0:T(8,128)(2,1)S(1)} %get-tuple-element.56), channel_id=1, source_target_pairs={{0,6},{1,7},{2,4},{3,5},{4,2},{5,3},{6,0},{7,1},{8,14},{9,15},{10,... | collective-permute-start | bytes 135176 | tf_op jit(solution)/shard_map/ppermute | solution.py:200
  39.0 14.7 %collective-permute-start.11 = (bf16[8,2816]{1,0:T(8,128)(2,1)S(1)}, bf16[8,2816]{1,0:T(8,128)(2,1)S(1)}, u32[]{:S(2)}, u32[]{:S(2)}) collective-permute-start(bf16[8,2816]{1,0:T(8,128)(2,1)S(1)} %get-tuple-element.57), channel_id=1, source_target_pairs={{0,7},{1,6},{2,5},{3,4},{4,3},{5,2},{6,1},{7,0},{8,15},{9,14},{10,... | collective-permute-start | bytes 135176 | tf_op jit(solution)/shard_map/ppermute | solution.py:200
  42.4 6.2 %collective-permute-start.18 = (bf16[8,2560]{1,0:T(8,128)(2,1)S(1)}, bf16[8,2560]{1,0:T(8,128)(2,1)S(1)}, u32[]{:S(2)}, u32[]{:S(2)}) collective-permute-start(bf16[8,2560]{1,0:T(8,128)(2,1)S(1)} %get-tuple-element.67), channel_id=1, source_target_pairs={{0,5},{1,4},{2,7},{3,6},{4,1},{5,0},{6,3},{7,2},{8,13},{9,12},{10,... | collective-permute-start | bytes 122888 | tf_op jit(solution)/shard_map/ppermute | solution.py:200
  42.4 6.5 %collective-permute-start.19 = (bf16[8,2560]{1,0:T(8,128)(2,1)S(1)}, bf16[8,2560]{1,0:T(8,128)(2,1)S(1)}, u32[]{:S(2)}, u32[]{:S(2)}) collective-permute-start(bf16[8,2560]{1,0:T(8,128)(2,1)S(1)} %get-tuple-element.68), channel_id=1, source_target_pairs={{0,6},{1,7},{2,4},{3,5},{4,2},{5,3},{6,0},{7,1},{8,14},{9,15},{10,... | collective-permute-start | bytes 122888 | tf_op jit(solution)/shard_map/ppermute | solution.py:200
  44.5 6.7 %collective-permute-start.20 = (bf16[8,2560]{1,0:T(8,128)(2,1)S(1)}, bf16[8,2560]{1,0:T(8,128)(2,1)S(1)}, u32[]{:S(2)}, u32[]{:S(2)}) collective-permute-start(bf16[8,2560]{1,0:T(8,128)(2,1)S(1)} %get-tuple-element.69), channel_id=1, source_target_pairs={{0,7},{1,6},{2,5},{3,4},{4,3},{5,2},{6,1},{7,0},{8,15},{9,14},{10,... | collective-permute-start | bytes 122888 | tf_op jit(solution)/shard_map/ppermute | solution.py:200
  48.6 6.5 %collective-permute-start.5 = (bf16[8,2816]{1,0:T(8,128)(2,1)S(1)}, bf16[8,2816]{1,0:T(8,128)(2,1)S(1)}, u32[]{:S(2)}, u32[]{:S(2)}) collective-permute-start(bf16[8,2816]{1,0:T(8,128)(2,1)S(1)} %get-tuple-element.51), channel_id=1, source_target_pairs={{0,1},{1,0},{2,3},{3,2},{4,5},{5,4},{6,7},{7,6},{8,9},{9,8},{10,11... | collective-permute-start | bytes 135176 | tf_op jit(solution)/shard_map/ppermute | solution.py:200
  48.8 6.3 %collective-permute-start.6 = (bf16[8,2816]{1,0:T(8,128)(2,1)S(1)}, bf16[8,2816]{1,0:T(8,128)(2,1)S(1)}, u32[]{:S(2)}, u32[]{:S(2)}) collective-permute-start(bf16[8,2816]{1,0:T(8,128)(2,1)S(1)} %get-tuple-element.52), channel_id=1, source_target_pairs={{0,2},{1,3},{2,0},{3,1},{4,6},{5,7},{6,4},{7,5},{8,10},{9,11},{10,... | collective-permute-start | bytes 135176 | tf_op jit(solution)/shard_map/ppermute | solution.py:200
  51.2 4.9 %collective-permute-start.7 = (bf16[8,2816]{1,0:T(8,128)(2,1)S(1)}, bf16[8,2816]{1,0:T(8,128)(2,1)S(1)}, u32[]{:S(2)}, u32[]{:S(2)}) collective-permute-start(bf16[8,2816]{1,0:T(8,128)(2,1)S(1)} %get-tuple-element.53), channel_id=1, source_target_pairs={{0,3},{1,2},{2,1},{3,0},{4,7},{5,6},{6,5},{7,4},{8,11},{9,10},{10,... | collective-permute-start | bytes 135176 | tf_op jit(solution)/shard_map/ppermute | solution.py:200
  52.1 4.9 %collective-permute-start.8 = (bf16[8,2816]{1,0:T(8,128)(2,1)S(1)}, bf16[8,2816]{1,0:T(8,128)(2,1)S(1)}, u32[]{:S(2)}, u32[]{:S(2)}) collective-permute-start(bf16[8,2816]{1,0:T(8,128)(2,1)S(1)} %get-tuple-element.54), channel_id=1, source_target_pairs={{0,4},{1,5},{2,6},{3,7},{4,0},{5,1},{6,2},{7,3},{8,12},{9,13},{10,... | collective-permute-start | bytes 135176 | tf_op jit(solution)/shard_map/ppermute | solution.py:200
  53.7 6.3 %collective-permute-start.9 = (bf16[8,2816]{1,0:T(8,128)(2,1)S(1)}, bf16[8,2816]{1,0:T(8,128)(2,1)S(1)}, u32[]{:S(2)}, u32[]{:S(2)}) collective-permute-start(bf16[8,2816]{1,0:T(8,128)(2,1)S(1)} %get-tuple-element.55), channel_id=1, source_target_pairs={{0,5},{1,4},{2,7},{3,6},{4,1},{5,0},{6,3},{7,2},{8,13},{9,12},{10,... | collective-permute-start | bytes 135176 | tf_op jit(solution)/shard_map/ppermute | solution.py:200
  72.3 6.2 %collective-permute-start.21 = (f32[1,3328]{1,0:T(1,128)}, f32[1,3328]{1,0:T(1,128)S(1)}, u32[]{:S(2)}, u32[]{:S(2)}) collective-permute-start(f32[1,3328]{1,0:T(1,128)} %gather.1.refs_0_), channel_id=1, source_target_pairs={{0,8},{8,0},{16,24},{24,16},{1,9},{9,1},{17,25},{25,17},{2,10},{10... | collective-permute-start | bytes 39944 | tf_op jit(solution)/shard_map/ppermute | solution.py:200
  72.3 6.2 %collective-permute-start.22 = (f32[1,3328]{1,0:T(1,128)}, f32[1,3328]{1,0:T(1,128)S(1)}, u32[]{:S(2)}, u32[]{:S(2)}) collective-permute-start(f32[1,3328]{1,0:T(1,128)} %gather.1.refs_0_), channel_id=1, source_target_pairs={{0,16},{8,24},{16,0},{24,8},{1,17},{9,25},{17,1},{25,9},{2,18},{10... | collective-permute-start | bytes 39944 | tf_op jit(solution)/shard_map/ppermute | solution.py:200
  73.8 4.7 %collective-permute-start.23 = (f32[1,3328]{1,0:T(1,128)}, f32[1,3328]{1,0:T(1,128)S(1)}, u32[]{:S(2)}, u32[]{:S(2)}) collective-permute-start(f32[1,3328]{1,0:T(1,128)} %gather.1.refs_0_), channel_id=1, source_target_pairs={{0,24},{8,16},{16,8},{24,0},{1,25},{9,17},{17,9},{25,1},{2,26},{10... | collective-permute-start | bytes 39944 | tf_op jit(solution)/shard_map/ppermute | solution.py:200
  74.2 1.0 %copy-start.3 = (bf16[1,128,1280]{2,1,0:T(8,128)(2,1)S(1)}, bf16[1,128,1280]{2,1,0:T(8,128)(2,1)}, u32[]{:S(2)}) copy-start(bf16[1,128,1280]{2,1,0:T(8,128)(2,1)} %param.15) | copy-start | bytes 983044
  75.1 1.0 %copy-start.4 = (bf16[1,128,1280]{2,1,0:T(8,128)(2,1)S(1)}, bf16[1,128,1280]{2,1,0:T(8,128)(2,1)}, u32[]{:S(2)}) copy-start(bf16[1,128,1280]{2,1,0:T(8,128)(2,1)} %param.16) | copy-start | bytes 983044
  78.5 0.6 copy-start.7
  78.5 0.6 copy-start.8
  78.5 0.6 copy-start.9

commit v6 on v3

--- a/solution.py
+++ b/solution.py
@@ -12,6 +12,7 @@
 HEAD_DIM = 80
 LANES = 128
 CHUNKS = (2, 2)
+DIRECT = 8
 VMEM_BYTES = 24 * 1024 * 1024
 
 F32 = jnp.float32
@@ -110,8 +111,8 @@
     )(kept, got)
 
 
-def pack_kernel(peers, capacity, chunks, carries, targets_ref, *refs):
-    terms, out_ref = refs[: 2 * chunks], refs[-1]
+def pack_kernel(peers, capacity, direct, chunks, me_ref, targets_ref, *refs):
+    terms, outs = refs[: 2 * chunks], refs[2 * chunks :]
     targets = targets_ref[...]
     rows = targets.shape[1]
     dest = targets // rows
@@ -123,43 +124,41 @@
     rank = jnp.sum(same_before.astype(jnp.int32), axis=0, keepdims=True)
     slots = peers * capacity
     slot = iota((slots, rows), 0)
-    chosen = jnp.logical_and(dest == slot // capacity, rank == slot % capacity)
+    holder = slot // capacity
+    if direct:
+        holder = holder ^ me_ref[0]
+    chosen = jnp.logical_and(dest == holder, rank == slot % capacity)
     selector = chosen.astype(F32).astype(BF16)
+    label = jnp.sum(jnp.where(chosen, local + 1, 0), axis=1, keepdims=True) - 1
+    parts = []
+    for chunk in range(chunks):
+        total = (terms[2 * chunk][...].astype(F32) + terms[2 * chunk + 1][...].astype(F32)).astype(BF16)
+        parts.append(dot(selector, total, (1, 0)))
+    parts.append(jnp.broadcast_to(label.astype(F32), (slots, LANES)))
     at = 0
-    for chunk in range(chunks):
-        kept, got = terms[2 * chunk], terms[2 * chunk + 1]
-        total = (kept[...].astype(F32) + got[...].astype(F32)).astype(BF16)
-        width = total.shape[1]
-        out_ref[:, at : at + width] = dot(selector, total, (1, 0)).astype(BF16)
+    for part in parts:
+        width = part.shape[1]
+        if direct:
+            for m in range(peers):
+                outs[m][:, at : at + width] = part[m * capacity : (m + 1) * capacity].astype(BF16)
+        else:
+            outs[0][:, at : at + width] = part.astype(BF16)
         at += width
-    label = jnp.sum(jnp.where(chosen, local + 1, 0), axis=1, keepdims=True) - 1
-    out_ref[:, at : at + LANES] = jnp.broadcast_to(label.astype(F32), (slots, LANES)).astype(BF16)
-    if carries:
-        sums = refs[2 * chunks][...]
-        high = sums.astype(BF16).astype(F32)
-        middle = (sums - high).astype(BF16).astype(F32)
-        low = (sums - high - middle).astype(BF16).astype(F32)
-        extra = jnp.zeros((slots, LANES), F32)
-        row = iota((slots, LANES), 0)
-        pieces = sums.shape[1] // peers // LANES
-        for peer in range(peers):
-            for level, values in enumerate((high, middle, low)):
-                for piece in range(pieces):
-                    start = (peer * pieces + piece) * LANES
-                    line = jnp.broadcast_to(values[:, start : start + LANES], (slots, LANES))
-                    extra = jnp.where(row == peer * capacity + level * pieces + piece, line, extra)
-        out_ref[:, at + LANES : at + 2 * LANES] = extra.astype(BF16)
-
-
-def pack(terms, targets, sums, peers, capacity, carries):
+
+
+def pack(terms, targets, me, peers, capacity, direct):
     rows = targets.shape[1]
-    width = sum(kept.shape[1] for kept, _ in terms) + (2 * LANES if carries else LANES)
-    operands = [targets] + [x for pair in terms for x in pair] + ([sums] if carries else [])
-    return pl.pallas_call(
-        functools.partial(pack_kernel, peers, capacity, len(terms), carries),
-        out_shape=jax.ShapeDtypeStruct((peers * capacity, width), BF16),
-        in_specs=vmem(len(operands)),
-        out_specs=pl.BlockSpec(memory_space=pltpu.VMEM),
+    width = sum(kept.shape[1] for kept, _ in terms) + LANES
+    operands = [me, targets] + [x for pair in terms for x in pair]
+    if direct:
+        out_shape = [jax.ShapeDtypeStruct((capacity, width), BF16)] * peers
+    else:
+        out_shape = [jax.ShapeDtypeStruct((peers * capacity, width), BF16)]
+    return pl.pallas_call(
+        functools.partial(pack_kernel, peers, capacity, direct, len(terms)),
+        out_shape=out_shape,
+        in_specs=[pl.BlockSpec(memory_space=pltpu.SMEM)] + vmem(len(operands) - 1),
+        out_specs=vmem(len(out_shape)),
         compiler_params=pltpu.CompilerParams(vmem_limit_bytes=VMEM_BYTES),
         cost_estimate=pl.CostEstimate(
             flops=2 * rows * peers * capacity * width,
@@ -168,6 +167,18 @@
         ),
         name="pack",
     )(*operands)
+
+
+def route(packed, peers, direct):
+    if not direct:
+        return [exchange(packed[0], "seq", peers)]
+    routed = {0: packed[0]}
+    half = peers // 2
+    for near in range(half):
+        for m in (half + near, near):
+            if m:
+                routed[m] = swap(packed[m], "seq", m)
+    return [routed[m] for m in range(peers)]
 
 
 def swap(x, axis, mask):
@@ -226,60 +237,79 @@
     )(queries, keys, ids)
 
 
-def norm_kernel(peers, copies, patches_ref, gain_ref, routed_ref, out_ref, share_ref):
+def norm_kernel(patches_ref, gain_ref, *refs):
+    pieces, (out_ref, gain_grad_ref) = refs[:-2], refs[-2:]
     patches, width = patches_ref.shape
-    slots = routed_ref.shape[0]
-    per_token = routed_ref.shape[1] // width
-    labels = routed_ref[:, per_token * width : per_token * width + LANES].astype(F32)[:, :1]
-    columns = [routed_ref[:, c * width : (c + 1) * width].astype(F32) for c in range(per_token)]
+    pieces = [ref[...].astype(F32) for ref in pieces]
+    routed = jnp.concatenate(pieces, axis=0) if len(pieces) > 1 else pieces[0]
+    slots, wide = routed.shape
+    per_token = wide // width
+    columns = [routed[:, c * width : (c + 1) * width] for c in range(per_token)]
     held = jnp.concatenate(columns, axis=0).astype(BF16)
-    lanes = len(columns) * slots
+    labels = routed[:, per_token * width : per_token * width + 1]
+    lanes = per_token * slots
     lane = iota((slots, lanes), 1)
     row_of_lane = jnp.sum(
         jnp.where(lane % slots == iota((slots, lanes), 0), labels, 0.0), axis=0, keepdims=True
     ).astype(jnp.int32)
-    patch_of_lane = row_of_lane * len(columns) + iota((1, lanes), 1) // slots
+    patch_of_lane = row_of_lane * per_token + iota((1, lanes), 1) // slots
     patch_of_lane = jnp.where(row_of_lane < 0, -1, patch_of_lane)
     chosen = patch_of_lane == iota((patches, lanes), 0)
     patch_grads = dot(chosen.astype(F32).astype(BF16), held, (1, 0))
     inputs = patches_ref[...].astype(F32)
     inverse_rms = lax.rsqrt(jnp.mean(inputs * inputs, axis=1, keepdims=True) + 1e-06)
     normed = inputs * inverse_rms
-    gain_part = jnp.sum(patch_grads * normed, axis=0, keepdims=True)
-    if copies:
-        rows = [gain_part[:, at : at + LANES] for at in range(0, width, LANES)]
-        carried = routed_ref[:, per_token * width + LANES :].astype(F32)
-        capacity = slots // peers
-        pieces = share_ref.shape[1] - len(rows)
-        for piece in range(pieces):
-            kept = iota((slots, LANES), 0) % capacity % pieces == piece
-            kept = jnp.logical_and(kept, iota((slots, LANES), 0) % capacity < 3 * pieces)
-            rows.append(jnp.sum(jnp.where(kept, carried, 0.0), axis=0, keepdims=True))
-        for at, row in enumerate(rows):
-            share_ref[:, at : at + 1, :] = jnp.broadcast_to(row[None], (copies, 1, LANES))
-    else:
-        share_ref[...] = gain_part
+    gain_grad_ref[...] = jnp.sum(patch_grads * normed, axis=0, keepdims=True)
     scaled = gain_ref[...] * patch_grads
     out_ref[...] = (
         inverse_rms * (scaled - normed * jnp.mean(scaled * normed, axis=1, keepdims=True))
     ).astype(BF16)
 
 
-def norm_backward(routed, peers, patches, gain, share):
+def norm_backward(received, patches, gain):
     count, width = patches.shape
-    return pl.pallas_call(
-        functools.partial(norm_kernel, peers, share[0] if len(share) == 3 else 0),
-        out_shape=[jax.ShapeDtypeStruct((count, width), BF16), jax.ShapeDtypeStruct(share, F32)],
-        in_specs=vmem(3),
+    routed = sum(x.size for x in received)
+    return pl.pallas_call(
+        norm_kernel,
+        out_shape=[
+            jax.ShapeDtypeStruct((count, width), BF16),
+            jax.ShapeDtypeStruct((1, width), F32),
+        ],
+        in_specs=vmem(2 + len(received)),
         out_specs=vmem(2),
         compiler_params=pltpu.CompilerParams(vmem_limit_bytes=VMEM_BYTES),
         cost_estimate=pl.CostEstimate(
-            flops=2 * count * routed.size,
-            bytes_accessed=4 * count * width + 2 * routed.size,
+            flops=2 * count * routed,
+            bytes_accessed=4 * count * width + 2 * routed,
             transcendentals=0,
         ),
         name="norm",
-    )(patches, gain, routed)
+    )(patches, gain, *received)
+
+
+def sum_over(x, axis):
+    n = lax.axis_size(axis)
+    if n > DIRECT:
+        return lax.psum(x, axis)
+    mask = 1
+    while mask < n:
+        x = x + swap(x, axis, mask)
+        mask *= 2
+    return x
+
+
+def side_by_side(x, axis):
+    n = lax.axis_size(axis)
+    if n > DIRECT:
+        return lax.all_gather(x[0], axis, tiled=True)[None]
+    place = lax.axis_index(axis)
+    mask = 1
+    while mask < n:
+        other = swap(x, axis, mask)
+        first = place & mask == 0
+        x = jnp.concatenate([jnp.where(first, x, other), jnp.where(first, other, x)], axis=1)
+        mask *= 2
+    return x
 
 
 def window_kernel(g_ref, q_ref, k_ref, v_ref, probs_ref, probs_t_ref, dq_ref, dk_ref, dv_ref):
@@ -342,17 +372,15 @@
     grad_rows = llm_grads[0]
     rows = grad_rows.shape[0]
     images, peers = lax.axis_size("img"), lax.axis_size("seq")
-    devices = images * peers
     capacity = max(1, 2 * rows // peers)
     block = w_down.shape[1]
     width = patches.shape[2]
-    pieces = block // peers // LANES
-    carries = pieces > 0 and 3 * pieces <= capacity
+    direct = peers <= DIRECT
 
     order = [0]
     while len(order) < images:
         order = [2 * j for j in order] + [2 * j + 1 for j in order]
-    image = lax.axis_index("img")
+    image, me = lax.axis_index("img"), lax.axis_index("seq")
 
     def columns(j):
         return lax.dynamic_slice(grad_rows, (0, (image ^ j) * block), (rows, block))
@@ -360,6 +388,7 @@
     x_blocks = [columns(0)] + [swap(columns(j), "img", j) for j in range(1, images)]
     x_blocks = [x_blocks[j] for j in order]
     probs, probs_t = window_probs(queries[0], keys[0], window_ids[0])
+    token_target, probs, probs_t = lax.optimization_barrier((token_target, probs, probs_t))
 
     terms, first = [], 0
     for index, count in enumerate(CHUNKS):
@@ -374,22 +403,15 @@
             kept, sent = halve(kept, swap(sent, "img", mask))
             mask *= 2
         terms.append((kept, swap(sent, "img", mask)))
-    packed = pack(terms, token_target, bias_part, peers, capacity, carries)
-    routed = exchange(packed, "seq", peers)
-
-    gain_rows = width // LANES
-    share = (devices, gain_rows + pieces, LANES) if carries else (1, width)
-    out_grads, shared = norm_backward(routed, peers, patches[0], gain[None], share)
-    if carries:
-        shared = exchange(shared, ("img", "seq"), devices)
-        gain_total = jnp.sum(shared[:, :gain_rows], axis=0).reshape(-1)
-        bias_total = shared[:, gain_rows:].reshape(-1)
-    else:
-        gain_total = lax.psum(shared[0], ("img", "seq"))
-        bias_total = lax.all_gather(lax.psum(bias_part[0], "seq"), "img", tiled=True)
+    packed = pack(terms, token_target, me.reshape(1), peers, capacity, direct)
+    received = route(packed, peers, direct)
+
+    bias_total = side_by_side(sum_over(bias_part, "seq"), "img")[0]
+    out_grads, gain_part = norm_backward(received, patches[0], gain[None])
+    gain_total = sum_over(sum_over(gain_part, "img"), "seq")[0]
+    gain_grad = gain_total / math.sqrt(images * peers * patches.shape[1])
+    bias_grad = bias_total / math.sqrt(images * peers * rows)
     grads = window_backward(out_grads, queries[0], keys[0], values[0], probs, probs_t)
-    gain_grad = gain_total / math.sqrt(devices * patches.shape[1])
-    bias_grad = bias_total / math.sqrt(devices * rows)
     return (grads[0][None], grads[1][None], grads[2][None], gain_grad, bias_grad)
 
 

time: 72.1 us -> 80.8 us (1.12)
  starting transfers between devices: 16.7 us -> 32.4 us
  waiting for transfers between devices: 31.2 us -> 21.3 us
  local copies, waits for them, and re-layouts: 9.73 us -> 11.7 us
    ppermute x7 -> x24, starting transfers between devices: 7.06 us -> 32.4 us  [swap(): return lax.ppermute(x, axis, [(i, i ^ mask) for i in range(n)])]
    all_to_all x2 -> x0, waiting for transfers between devices: 24.5 us -> none  [exchange(): lax.all_to_all(x, axis, split_axis=0, concat_axis=0, tiled=True)]
    ppermute x7 -> x24, waiting for transfers between devices: 6.74 us -> 21.3 us  [swap(): return lax.ppermute(x, axis, [(i, i ^ mask) for i in range(n)])]
    all_to_all x2 -> x0, starting transfers between devices: 9.64 us -> none  [exchange(): lax.all_to_all(x, axis, split_axis=0, concat_axis=0, tiled=True)]
    unnamed x14 -> x16, local copies, waits for them, and re-layouts: 0.04 us -> 1.98 us
    pallas_call x2, Pallas kernels: 0.14 us -> 1.41 us  [halve(): pl.pallas_call(halve_kernel, out_shape=[jax.ShapeDtypeStruct((rows // 2,...]
  transfers between devices with their start and end apart: 9 -> 24, of which waited for: 4 -> 9; matrix products, arithmetic and copies ran while one was open for 12% -> 12% of each run, Pallas kernels for 9% -> 12%
where the time goes in v6:
time: 80.8 us; the launch traced here: 80.6 us
  starting transfers between devices  32.4 us (40%)
  waiting for transfers between devices  21.3 us (26%)
  Pallas kernels  12.8 us (16%)
  local copies, waits for them, and re-layouts  11.7 us (14%)
  other arithmetic  1.39 us (2%)
  between operations  0.91 us (1%)
    ppermute x24, starting transfers between devices, swap(): return lax.ppermute(x, axis, [(i, i ^ mask) for i in range(n)])  32.4 us
    ppermute x24, waiting for transfers between devices, swap(): return lax.ppermute(x, axis, [(i, i ^ mask) for i in range(n)])  21.3 us
    slice x1, local copies, waits for them, and re-layouts, body(): w_rows = lax.slice_in_dim(w_down, first, first + count * width)  8.54 us
    pallas_call x2, Pallas kernels, project(): pl.pallas_call(functools.partial(project_kernel, blocks, tile, with_sum),...  6.04 us
    pallas_call x1, Pallas kernels, window_backward(): pl.pallas_call(window_kernel, out_shape=[shape] * 3, in_specs=vmem(6), ou...  2.37 us
    unnamed x16, local copies, waits for them, and re-layouts  1.98 us
  transfers between devices with their start and end apart: 24, of which 9 were waited for; matrix products, arithmetic and copies ran while one was open for 12% of the time, Pallas kernels for 12%

profile of v6, /device:TPU:0, one launch (start us, length us, event | category | flops | bytes accessed | tf_op | source)
XLA Modules:
  0.0 80.6 jit_solution(8946939031423951047)
XLA Ops:
  0.7 1.1 %dynamic-slice_bitcast_fusion = (bf16[32,2048]{1,0:T(8,128)(2,1)S(1)}, bf16[32,2048]{1,0:T(8,128)(2,1)S(1)}, bf16[32,2048]{1,0:T(8,128)(2,1)S(1)}, bf16[32,2048]{1,0:T(8,128)(2,1)S(1)}) fusion(bf16[1,32,8192]{2,1,0:T(8,128)(2,1)} %param.9, s32[]{:T(128)S(6)} %select_n.39, s32[]{:T(128)S(6)} %select_n.37, s32[]{:T(128)S(6)} %select_n.36, s32[]{:T(128)S(6)} %select_n.38), kind=kLoop, calls=%fused_computation | loop fusion | bytes 1048592 | tf_op jit(solution)/shard_map/dynamic_slice | solution.py:386
  1.8 3.0 %collective-permute-start = (bf16[32,2048]{1,0:T(8,128)(2,1)S(1)}, bf16[32,2048]{1,0:T(8,128)(2,1)S(1)}, u32[]{:S(2)}, u32[]{:S(2)}) collective-permute-start(bf16[32,2048]{1,0:T(8,128)(2,1)S(1)} %get-tuple-element.62), channel_id=1, source_target_pairs={{0,16},{8,24},{16,0},{24,8},{1,17},{9,25},{17,1},{25,9},{2,18},{10... | collective-permute-start | bytes 393224 | tf_op jit(solution)/shard_map/ppermute | solution.py:186
  4.8 0.0 collective-permute-start.1
  4.8 0.2 collective-permute-start.2
  5.0 8.5 %fusion = (bf16[2560,2048]{1,0:T(8,128)(2,1)S(1)}, bf16[2560,2048]{1,0:T(8,128)(2,1)S(1)}) fusion(bf16[5120,2048]{1,0:T(8,128)(2,1)} %param.13), kind=kLoop, calls=%fused_computation.11 | loop fusion | bytes 41943040 | tf_op jit(solution)/shard_map/slice | solution.py:395
  13.6 0.0 collective-permute-done.refs_1_
  13.6 0.0 collective-permute-done.1.refs_2_
  13.6 0.0 collective-permute-done.2.refs_3_
  13.6 0.0 copy-start.1
  13.6 0.0 copy-start.2
  13.6 0.0 copy-start.6
  13.7 0.0 copy-start.7
  13.7 0.0 copy-start.5
  13.7 0.0 copy-start
  13.7 3.0 %project.3 = (bf16[64,2560]{1,0:T(8,128)(2,1)S(1)}, bf16[64,2560]{1,0:T(8,128)(2,1)S(1)}) custom-call(bf16[32,2048]{1,0:T(8,128)(2,1)S(1)} %get-tuple-element.63.refs_0_, bf16[32,2048]{1,0:T(8,128)(2,1)S(1)} %collective-permute-done.refs_1_, bf16[32,2048]{1,0:T(8,128)(2,1)S(1)} %collective-permute-done.1.refs_2_, ...), custom_call_target="tpu_custom_call" | custom-call | flops 1342177280 | bytes 10485760 | tf_op jit(solution)/shard_map/project/pallas_call | solution.py:75
  16.7 0.4 collective-permute-start.5
  17.1 3.1 %project.2 = (bf16[64,2560]{1,0:T(8,128)(2,1)S(1)}, bf16[64,2560]{1,0:T(8,128)(2,1)S(1)}, f32[1,2048]{1,0:T(1,128)S(1)}) custom-call(bf16[32,2048]{1,0:T(8,128)(2,1)S(1)} %get-tuple-element.63.refs_0_, bf16[32,2048]{1,0:T(8,128)(2,1)S(1)} %collective-permute-done.refs_1_, bf16[32,2048]{1,0:T(8,128)(2,1)S(1)} %collective-permute-done.1.refs_2_, ...), custom_call_target="tpu_custom_call" | custom-call | flops 1342177280 | bytes 10485760 | tf_op jit(solution)/shard_map/project/pallas_call | solution.py:75
  20.1 0.3 collective-permute-start.3
  20.4 0.0 collective-permute-done.5.got_ref
  20.4 0.7 halve.3
  21.1 1.9 %collective-permute-start.6 = (bf16[32,2560]{1,0:T(8,128)(2,1)}, bf16[32,2560]{1,0:T(8,128)(2,1)}, u32[]{:S(2)}, u32[]{:S(2)}) collective-permute-start(bf16[32,2560]{1,0:T(8,128)(2,1)} %get-tuple-element.42), channel_id=1, source_target_pairs={{0,16},{8,24},{16,0},{24,8},{1,17},{9,25},{17,1},{25,9},{2,18},{10... | collective-permute-start | bytes 491528 | tf_op jit(solution)/shard_map/ppermute | solution.py:186
  23.0 0.7 halve.2
  23.7 0.6 collective-permute-start.4
  24.3 1.5 %collective-permute-start.19 = (f32[1,2048]{1,0:T(1,128)S(1)}, f32[1,2048]{1,0:T(1,128)S(1)}, u32[]{:S(2)}, u32[]{:S(2)}) collective-permute-start(f32[1,2048]{1,0:T(1,128)S(1)} %get-tuple-element.58), channel_id=1, source_target_pairs={{0,1},{1,0},{2,3},{3,2},{4,5},{5,4},{6,7},{7,6},{8,9},{9,8},{10,11... | collective-permute-start | bytes 24584 | tf_op jit(solution)/shard_map/ppermute | solution.py:186
  25.8 2.2 %collective-permute-done.19 = f32[1,2048]{1,0:T(1,128)S(1)} collective-permute-done((f32[1,2048]{1,0:T(1,128)S(1)}, f32[1,2048]{1,0:T(1,128)S(1)}, u32[]{:S(2)}, u32[]{:S(2)}) %collective-permute-start.19) | collective-permute-done | bytes 8224 | tf_op jit(solution)/shard_map/ppermute | solution.py:186
  27.9 1.7 %collective-permute-start.20 = (f32[1,2048]{1,0:T(1,128)S(1)}, f32[1,2048]{1,0:T(1,128)S(1)}, u32[]{:S(2)}, u32[]{:S(2)}) collective-permute-start(f32[1,2048]{1,0:T(1,128)S(1)} %add.45), channel_id=1, source_target_pairs={{0,2},{1,3},{2,0},{3,1},{4,6},{5,7},{6,4},{7,5},{8,10},{9,11},{10,... | collective-permute-start | bytes 24584 | tf_op jit(solution)/shard_map/ppermute | solution.py:186
  29.6 2.1 %collective-permute-done.20 = f32[1,2048]{1,0:T(1,128)S(1)} collective-permute-done((f32[1,2048]{1,0:T(1,128)S(1)}, f32[1,2048]{1,0:T(1,128)S(1)}, u32[]{:S(2)}, u32[]{:S(2)}) %collective-permute-start.20) | collective-permute-done | bytes 8224 | tf_op jit(solution)/shard_map/ppermute | solution.py:186
  31.7 2.7 %collective-permute-start.21 = (f32[1,2048]{1,0:T(1,128)S(1)}, f32[1,2048]{1,0:T(1,128)S(1)}, u32[]{:S(2)}, u32[]{:S(2)}) collective-permute-start(f32[1,2048]{1,0:T(1,128)S(1)} %add.46), channel_id=1, source_target_pairs={{0,4},{1,5},{2,6},{3,7},{4,0},{5,1},{6,2},{7,3},{8,12},{9,13},{10,... | collective-permute-start | bytes 24584 | tf_op jit(solution)/shard_map/ppermute | solution.py:186
  34.3 2.0 %collective-permute-done.21 = f32[1,2048]{1,0:T(1,128)S(1)} collective-permute-done((f32[1,2048]{1,0:T(1,128)S(1)}, f32[1,2048]{1,0:T(1,128)S(1)}, u32[]{:S(2)}, u32[]{:S(2)}) %collective-permute-start.21) | collective-permute-done | bytes 8224 | tf_op jit(solution)/shard_map/ppermute | solution.py:186
  36.3 0.1 collective-permute-start.22
  36.4 1.1 %probs.1 = (f32[16,128,128]{2,1,0:T(8,128)S(1)}, f32[16,128,128]{2,1,0:T(8,128)S(1)}) custom-call(bf16[128,1280]{1,0:T(8,128)(2,1)S(1)} %bitcast.19, bf16[128,1280]{1,0:T(8,128)(2,1)S(1)} %bitcast.21, s32[1,32]{1,0:T(1,128)S(1)} %bitcast.24), custom_call_target="tpu_custom_call" | custom-call | flops 268435456 | bytes 2097152 | tf_op jit(solution)/shard_map/probs/pallas_call | solution.py:225
  37.5 0.0 collective-permute-done.6.refs_3_
  37.5 0.0 collective-permute-done.4.refs_1_
  37.5 1.4 %pack.1 = (bf16[8,5248]{1,0:T(8,128)(2,1)S(1)}, bf16[8,5248]{1,0:T(8,128)(2,1)S(1)}, bf16[8,5248]{1,0:T(8,128)(2,1)S(1)}, bf16[8,5248]{1,0:T(8,128)(2,1)S(1)}, b...) custom-call(s32[1]{0:T(128)} %bitcast.1.me_ref, ...), custom_call_target="tpu_custom_call" | custom-call | flops 21495808 | bytes 1679360 | tf_op jit(solution)/shard_map/pack/pallas_call | solution.py:157
  39.0 2.7 %collective-permute-start.10 = (bf16[8,5248]{1,0:T(8,128)(2,1)S(1)}, bf16[8,5248]{1,0:T(8,128)(2,1)S(1)}, u32[]{:S(2)}, u32[]{:S(2)}) collective-permute-start(bf16[8,5248]{1,0:T(8,128)(2,1)S(1)} %get-tuple-element.47), channel_id=1, source_target_pairs={{0,4},{1,5},{2,6},{3,7},{4,0},{5,1},{6,2},{7,3},{8,12},{9,13},{10,... | collective-permute-start | bytes 251912 | tf_op jit(solution)/shard_map/ppermute | solution.py:186
  41.6 1.3 %collective-permute-start.11 = (bf16[8,5248]{1,0:T(8,128)(2,1)S(1)}, bf16[8,5248]{1,0:T(8,128)(2,1)S(1)}, u32[]{:S(2)}, u32[]{:S(2)}) collective-permute-start(bf16[8,5248]{1,0:T(8,128)(2,1)S(1)} %get-tuple-element.48), channel_id=1, source_target_pairs={{0,5},{1,4},{2,7},{3,6},{4,1},{5,0},{6,3},{7,2},{8,13},{9,12},{10,... | collective-permute-start | bytes 251912 | tf_op jit(solution)/shard_map/ppermute | solution.py:186
  42.9 3.7 %collective-permute-start.12 = (bf16[8,5248]{1,0:T(8,128)(2,1)S(1)}, bf16[8,5248]{1,0:T(8,128)(2,1)S(1)}, u32[]{:S(2)}, u32[]{:S(2)}) collective-permute-start(bf16[8,5248]{1,0:T(8,128)(2,1)S(1)} %get-tuple-element.49), channel_id=1, source_target_pairs={{0,6},{1,7},{2,4},{3,5},{4,2},{5,3},{6,0},{7,1},{8,14},{9,15},{10,... | collective-permute-start | bytes 251912 | tf_op jit(solution)/shard_map/ppermute | solution.py:186
  46.6 0.2 collective-permute-start.13
  46.8 1.5 %collective-permute-start.7 = (bf16[8,5248]{1,0:T(8,128)(2,1)S(1)}, bf16[8,5248]{1,0:T(8,128)(2,1)S(1)}, u32[]{:S(2)}, u32[]{:S(2)}) collective-permute-start(bf16[8,5248]{1,0:T(8,128)(2,1)S(1)} %get-tuple-element.44), channel_id=1, source_target_pairs={{0,1},{1,0},{2,3},{3,2},{4,5},{5,4},{6,7},{7,6},{8,9},{9,8},{10,11... | collective-permute-start | bytes 251912 | tf_op jit(solution)/shard_map/ppermute | solution.py:186
  48.3 4.5 %collective-permute-start.8 = (bf16[8,5248]{1,0:T(8,128)(2,1)S(1)}, bf16[8,5248]{1,0:T(8,128)(2,1)S(1)}, u32[]{:S(2)}, u32[]{:S(2)}) collective-permute-start(bf16[8,5248]{1,0:T(8,128)(2,1)S(1)} %get-tuple-element.45), channel_id=1, source_target_pairs={{0,2},{1,3},{2,0},{3,1},{4,6},{5,7},{6,4},{7,5},{8,10},{9,11},{10,... | collective-permute-start | bytes 251912 | tf_op jit(solution)/shard_map/ppermute | solution.py:186
  52.7 2.4 %collective-permute-done.11.refs_5_ = bf16[8,5248]{1,0:T(8,128)(2,1)S(1)} collective-permute-done((bf16[8,5248]{1,0:T(8,128)(2,1)S(1)}, bf16[8,5248]{1,0:T(8,128)(2,1)S(1)}, u32[]{:S(2)}, u32[]{:S(2)}) %collective-permute-start.11) | collective-permute-done | bytes 84000 | tf_op jit(solution)/shard_map/ppermute | solution.py:186
  55.2 0.3 collective-permute-start.9
  55.5 0.0 collective-permute-done.12.refs_6_
  55.5 1.5 %collective-permute-start.23 = (f32[1,4096]{1,0:T(1,128)S(1)}, f32[1,4096]{1,0:T(1,128)S(1)}, u32[]{:S(2)}, u32[]{:S(2)}) collective-permute-start(f32[1,4096]{1,0:T(1,128)S(1)} %pad_maximum_fusion), channel_id=1, source_target_pairs={{0,16},{8,24},{16,0},{24,8},{1,17},{9,25},{17,1},{25,9},{2,18},{10... | collective-permute-start | bytes 49160 | tf_op jit(solution)/shard_map/ppermute | solution.py:186
  57.0 0.0 collective-permute-done.7.refs_1_
  57.0 0.0 collective-permute-done.8.refs_2_
  57.0 3.5 %collective-permute-done.9.refs_3_ = bf16[8,5248]{1,0:T(8,128)(2,1)S(1)} collective-permute-done((bf16[8,5248]{1,0:T(8,128)(2,1)S(1)}, bf16[8,5248]{1,0:T(8,128)(2,1)S(1)}, u32[]{:S(2)}, u32[]{:S(2)}) %collective-permute-start.9) | collective-permute-done | bytes 84000 | tf_op jit(solution)/shard_map/ppermute | solution.py:186
  60.5 0.5 norm.1
  61.1 0.1 collective-permute-start.14
  61.1 1.2 %collective-permute-done.14 = f32[1,1280]{1,0:T(1,128)S(1)} collective-permute-done((f32[1,1280]{1,0:T(1,128)S(1)}, f32[1,1280]{1,0:T(1,128)S(1)}, u32[]{:S(2)}, u32[]{:S(2)}) %collective-permute-start.14) | collective-permute-done | bytes 5152 | tf_op jit(solution)/shard_map/ppermute | solution.py:186
  62.3 1.5 %collective-permute-start.15 = (f32[1,1280]{1,0:T(1,128)S(1)}, f32[1,1280]{1,0:T(1,128)S(1)}, u32[]{:S(2)}, u32[]{:S(2)}) collective-permute-start(f32[1,1280]{1,0:T(1,128)S(1)} %add.40), channel_id=1, source_target_pairs={{0,16},{8,24},{16,0},{24,8},{1,17},{9,25},{17,1},{25,9},{2,18},{10... | collective-permute-start | bytes 15368 | tf_op jit(solution)/shard_map/ppermute | solution.py:186
  63.8 2.1 %collective-permute-done.15 = f32[1,1280]{1,0:T(1,128)S(1)} collective-permute-done((f32[1,1280]{1,0:T(1,128)S(1)}, f32[1,1280]{1,0:T(1,128)S(1)}, u32[]{:S(2)}, u32[]{:S(2)}) %collective-permute-start.15) | collective-permute-done | bytes 5152 | tf_op jit(solution)/shard_map/ppermute | solution.py:186
  66.0 0.5 collective-permute-start.16
  66.5 0.0 collective-permute-done.23
  66.6 3.1 %collective-permute-done.16 = f32[1,1280]{1,0:T(1,128)S(1)} collective-permute-done((f32[1,1280]{1,0:T(1,128)S(1)}, f32[1,1280]{1,0:T(1,128)S(1)}, u32[]{:S(2)}, u32[]{:S(2)}) %collective-permute-start.16) | collective-permute-done | bytes 5152 | tf_op jit(solution)/shard_map/ppermute | solution.py:186
  69.7 0.2 collective-permute-start.17
  69.9 0.6 maximum_multiply_fusion
  70.6 2.8 %collective-permute-done.17 = f32[1,1280]{1,0:T(1,128)S(1)} collective-permute-done((f32[1,1280]{1,0:T(1,128)S(1)}, f32[1,1280]{1,0:T(1,128)S(1)}, u32[]{:S(2)}, u32[]{:S(2)}) %collective-permute-start.17) | collective-permute-done | bytes 5152 | tf_op jit(solution)/shard_map/ppermute | solution.py:186
  73.4 2.3 %collective-permute-start.18 = (f32[1,1280]{1,0:T(1,128)S(1)}, f32[1,1280]{1,0:T(1,128)S(1)}, u32[]{:S(2)}, u32[]{:S(2)}) collective-permute-start(f32[1,1280]{1,0:T(1,128)S(1)} %add.43), channel_id=1, source_target_pairs={{0,4},{1,5},{2,6},{3,7},{4,0},{5,1},{6,2},{7,3},{8,12},{9,13},{10,... | collective-permute-start | bytes 15368 | tf_op jit(solution)/shard_map/ppermute | solution.py:186
  75.6 1.0 %copy-done.3 = bf16[1,128,1280]{2,1,0:T(8,128)(2,1)S(1)} copy-done((bf16[1,128,1280]{2,1,0:T(8,128)(2,1)S(1)}, bf16[1,128,1280]{2,1,0:T(8,128)(2,1)}, u32[]{:S(2)}) %copy-start.3) | copy-done | bytes 327704
  76.6 1.0 %copy-done.4 = bf16[1,128,1280]{2,1,0:T(8,128)(2,1)S(1)} copy-done((bf16[1,128,1280]{2,1,0:T(8,128)(2,1)S(1)}, bf16[1,128,1280]{2,1,0:T(8,128)(2,1)}, u32[]{:S(2)}) %copy-start.4) | copy-done | bytes 327704
  77.6 2.4 %window.1 = (bf16[128,1280]{1,0:T(8,128)(2,1)}, bf16[128,1280]{1,0:T(8,128)(2,1)}, bf16[128,1280]{1,0:T(8,128)(2,1)}) custom-call(bf16[128,1280]{1,0:T(8,128)(2,1)S(1)} %get-tuple-element.51.g_ref, bf16[128,1280]{1,0:T(8,128)(2,1)S(1)} %bitcast.20, bf16[128,1280]{1,0:T(8,128)(2,1)S(1)} %bitcast.22, bf16[128,1280]{1,0:T(8,128)(2,1)S(1)} %bitcast.23, ...), custom_call_target="tpu_custom_call" | custom-call | flops 335544320 | bytes 4390912 | tf_op jit(solution)/shard_map/window/pallas_call | solution.py:356
  79.9 0.0 collective-permute-done.18
  79.9 0.6 multiply_reduce_fusion
  (23 shorter events, 0.2 us)
Async XLA Ops:
  1.8 11.8 %collective-permute-start = (bf16[32,2048]{1,0:T(8,128)(2,1)S(1)}, bf16[32,2048]{1,0:T(8,128)(2,1)S(1)}, u32[]{:S(2)}, u32[]{:S(2)}) collective-permute-start(bf16[32,2048]{1,0:T(8,128)(2,1)S(1)} %get-tuple-element.62), channel_id=1, source_target_pairs={{0,16},{8,24},{16,0},{24,8},{1,17},{9,25},{17,1},{25,9},{2,18},{10... | collective-permute-start | bytes 393224 | tf_op jit(solution)/shard_map/ppermute | solution.py:186
  4.8 8.8 %collective-permute-start.1 = (bf16[32,2048]{1,0:T(8,128)(2,1)S(1)}, bf16[32,2048]{1,0:T(8,128)(2,1)S(1)}, u32[]{:S(2)}, u32[]{:S(2)}) collective-permute-start(bf16[32,2048]{1,0:T(8,128)(2,1)S(1)} %get-tuple-element.64), channel_id=1, source_target_pairs={{0,8},{8,0},{16,24},{24,16},{1,9},{9,1},{17,25},{25,17},{2,10},{10... | collective-permute-start | bytes 393224 | tf_op jit(solution)/shard_map/ppermute | solution.py:186
  4.8 8.8 %collective-permute-start.2 = (bf16[32,2048]{1,0:T(8,128)(2,1)S(1)}, bf16[32,2048]{1,0:T(8,128)(2,1)S(1)}, u32[]{:S(2)}, u32[]{:S(2)}) collective-permute-start(bf16[32,2048]{1,0:T(8,128)(2,1)S(1)} %get-tuple-element.61), channel_id=1, source_target_pairs={{0,24},{8,16},{16,8},{24,0},{1,25},{9,17},{17,9},{25,1},{2,26},{10... | collective-permute-start | bytes 393224 | tf_op jit(solution)/shard_map/ppermute | solution.py:186
  13.6 22.8 %copy-start.1 = (bf16[1,128,1280]{2,1,0:T(8,128)(2,1)S(1)}, bf16[1,128,1280]{2,1,0:T(8,128)(2,1)}, u32[]{:S(2)}) copy-start(bf16[1,128,1280]{2,1,0:T(8,128)(2,1)} %param.14) | copy-start | bytes 983044
  13.6 22.8 %copy-start.2 = (bf16[1,128,1280]{2,1,0:T(8,128)(2,1)S(1)}, bf16[1,128,1280]{2,1,0:T(8,128)(2,1)}, u32[]{:S(2)}) copy-start(bf16[1,128,1280]{2,1,0:T(8,128)(2,1)} %param.15) | copy-start | bytes 983044
  13.6 22.8 %copy-start.6 = (s32[1,1,32]{2,1,0:T(1,128)S(1)}, s32[1,1,32]{2,1,0:T(1,128)}, u32[]{:S(2)}) copy-start(s32[1,1,32]{2,1,0:T(1,128)} %param.17) | copy-start | bytes 388
  13.7 23.8 %copy-start.7 = (f32[1280]{0:T(1024)S(1)}, f32[1280]{0:T(1024)}, u32[]{:S(2)}) copy-start(f32[1280]{0:T(1024)} %param.12) | copy-start | bytes 15364
  13.7 23.9 %copy-start.5 = (s32[1,32]{1,0:T(1,128)S(1)}, s32[1,32]{1,0:T(1,128)}, u32[]{:S(2)}) copy-start(s32[1,32]{1,0:T(1,128)} %targets_ref) | copy-start | bytes 388
  13.7 46.8 %copy-start = (bf16[1,128,1280]{2,1,0:T(8,128)(2,1)S(1)}, bf16[1,128,1280]{2,1,0:T(8,128)(2,1)}, u32[]{:S(2)}) copy-start(bf16[1,128,1280]{2,1,0:T(8,128)(2,1)} %param.11) | copy-start | bytes 983044
  16.7 3.7 %collective-permute-start.5 = (bf16[64,2560]{1,0:T(8,128)(2,1)S(1)}, bf16[64,2560]{1,0:T(8,128)(2,1)S(1)}, u32[]{:S(2)}, u32[]{:S(2)}) collective-permute-start(bf16[64,2560]{1,0:T(8,128)(2,1)S(1)} %get-tuple-element.40), channel_id=1, source_target_pairs={{0,8},{8,0},{16,24},{24,16},{1,9},{9,1},{17,25},{25,17},{2,10},{10... | collective-permute-start | bytes 983048 | tf_op jit(solution)/shard_map/ppermute | solution.py:186
  20.1 2.9 %collective-permute-start.3 = (bf16[64,2560]{1,0:T(8,128)(2,1)S(1)}, bf16[64,2560]{1,0:T(8,128)(2,1)S(1)}, u32[]{:S(2)}, u32[]{:S(2)}) collective-permute-start(bf16[64,2560]{1,0:T(8,128)(2,1)S(1)} %get-tuple-element.36), channel_id=1, source_target_pairs={{0,8},{8,0},{16,24},{24,16},{1,9},{9,1},{17,25},{25,17},{2,10},{10... | collective-permute-start | bytes 983048 | tf_op jit(solution)/shard_map/ppermute | solution.py:186
  21.1 16.4 %collective-permute-start.6 = (bf16[32,2560]{1,0:T(8,128)(2,1)}, bf16[32,2560]{1,0:T(8,128)(2,1)}, u32[]{:S(2)}, u32[]{:S(2)}) collective-permute-start(bf16[32,2560]{1,0:T(8,128)(2,1)} %get-tuple-element.42), channel_id=1, source_target_pairs={{0,16},{8,24},{16,0},{24,8},{1,17},{9,25},{17,1},{25,9},{2,18},{10... | collective-permute-start | bytes 491528 | tf_op jit(solution)/shard_map/ppermute | solution.py:186
  23.7 13.8 %collective-permute-start.4 = (bf16[32,2560]{1,0:T(8,128)(2,1)}, bf16[32,2560]{1,0:T(8,128)(2,1)}, u32[]{:S(2)}, u32[]{:S(2)}) collective-permute-start(bf16[32,2560]{1,0:T(8,128)(2,1)} %get-tuple-element.38), channel_id=1, source_target_pairs={{0,16},{8,24},{16,0},{24,8},{1,17},{9,25},{17,1},{25,9},{2,18},{10... | collective-permute-start | bytes 491528 | tf_op jit(solution)/shard_map/ppermute | solution.py:186
  24.3 3.7 %collective-permute-start.19 = (f32[1,2048]{1,0:T(1,128)S(1)}, f32[1,2048]{1,0:T(1,128)S(1)}, u32[]{:S(2)}, u32[]{:S(2)}) collective-permute-start(f32[1,2048]{1,0:T(1,128)S(1)} %get-tuple-element.58), channel_id=1, source_target_pairs={{0,1},{1,0},{2,3},{3,2},{4,5},{5,4},{6,7},{7,6},{8,9},{9,8},{10,11... | collective-permute-start | bytes 24584 | tf_op jit(solution)/shard_map/ppermute | solution.py:186
  27.9 3.7 %collective-permute-start.20 = (f32[1,2048]{1,0:T(1,128)S(1)}, f32[1,2048]{1,0:T(1,128)S(1)}, u32[]{:S(2)}, u32[]{:S(2)}) collective-permute-start(f32[1,2048]{1,0:T(1,128)S(1)} %add.45), channel_id=1, source_target_pairs={{0,2},{1,3},{2,0},{3,1},{4,6},{5,7},{6,4},{7,5},{8,10},{9,11},{10,... | collective-permute-start | bytes 24584 | tf_op jit(solution)/shard_map/ppermute | solution.py:186
  31.7 4.6 %collective-permute-start.21 = (f32[1,2048]{1,0:T(1,128)S(1)}, f32[1,2048]{1,0:T(1,128)S(1)}, u32[]{:S(2)}, u32[]{:S(2)}) collective-permute-start(f32[1,2048]{1,0:T(1,128)S(1)} %add.46), channel_id=1, source_target_pairs={{0,4},{1,5},{2,6},{3,7},{4,0},{5,1},{6,2},{7,3},{8,12},{9,13},{10,... | collective-permute-start | bytes 24584 | tf_op jit(solution)/shard_map/ppermute | solution.py:186
  36.3 6.6 %collective-permute-start.22 = (f32[1,2048]{1,0:T(1,128)S(1)}, f32[1,2048]{1,0:T(1,128)S(1)}, u32[]{:S(2)}, u32[]{:S(2)}) collective-permute-start(f32[1,2048]{1,0:T(1,128)S(1)} %add.47), channel_id=1, source_target_pairs={{0,8},{8,0},{16,24},{24,16},{1,9},{9,1},{17,25},{25,17},{2,10},{10... | collective-permute-start | bytes 24584 | tf_op jit(solution)/shard_map/ppermute | solution.py:186
  39.0 9.3 %collective-permute-start.10 = (bf16[8,5248]{1,0:T(8,128)(2,1)S(1)}, bf16[8,5248]{1,0:T(8,128)(2,1)S(1)}, u32[]{:S(2)}, u32[]{:S(2)}) collective-permute-start(bf16[8,5248]{1,0:T(8,128)(2,1)S(1)} %get-tuple-element.47), channel_id=1, source_target_pairs={{0,4},{1,5},{2,6},{3,7},{4,0},{5,1},{6,2},{7,3},{8,12},{9,13},{10,... | collective-permute-start | bytes 251912 | tf_op jit(solution)/shard_map/ppermute | solution.py:186
  41.6 13.5 %collective-permute-start.11 = (bf16[8,5248]{1,0:T(8,128)(2,1)S(1)}, bf16[8,5248]{1,0:T(8,128)(2,1)S(1)}, u32[]{:S(2)}, u32[]{:S(2)}) collective-permute-start(bf16[8,5248]{1,0:T(8,128)(2,1)S(1)} %get-tuple-element.48), channel_id=1, source_target_pairs={{0,5},{1,4},{2,7},{3,6},{4,1},{5,0},{6,3},{7,2},{8,13},{9,12},{10,... | collective-permute-start | bytes 251912 | tf_op jit(solution)/shard_map/ppermute | solution.py:186
  42.9 12.5 %collective-permute-start.12 = (bf16[8,5248]{1,0:T(8,128)(2,1)S(1)}, bf16[8,5248]{1,0:T(8,128)(2,1)S(1)}, u32[]{:S(2)}, u32[]{:S(2)}) collective-permute-start(bf16[8,5248]{1,0:T(8,128)(2,1)S(1)} %get-tuple-element.49), channel_id=1, source_target_pairs={{0,6},{1,7},{2,4},{3,5},{4,2},{5,3},{6,0},{7,1},{8,14},{9,15},{10,... | collective-permute-start | bytes 251912 | tf_op jit(solution)/shard_map/ppermute | solution.py:186
  46.6 10.4 %collective-permute-start.13 = (bf16[8,5248]{1,0:T(8,128)(2,1)S(1)}, bf16[8,5248]{1,0:T(8,128)(2,1)S(1)}, u32[]{:S(2)}, u32[]{:S(2)}) collective-permute-start(bf16[8,5248]{1,0:T(8,128)(2,1)S(1)} %get-tuple-element.50), channel_id=1, source_target_pairs={{0,7},{1,6},{2,5},{3,4},{4,3},{5,2},{6,1},{7,0},{8,15},{9,14},{10,... | collective-permute-start | bytes 251912 | tf_op jit(solution)/shard_map/ppermute | solution.py:186
  46.8 10.2 %collective-permute-start.7 = (bf16[8,5248]{1,0:T(8,128)(2,1)S(1)}, bf16[8,5248]{1,0:T(8,128)(2,1)S(1)}, u32[]{:S(2)}, u32[]{:S(2)}) collective-permute-start(bf16[8,5248]{1,0:T(8,128)(2,1)S(1)} %get-tuple-element.44), channel_id=1, source_target_pairs={{0,1},{1,0},{2,3},{3,2},{4,5},{5,4},{6,7},{7,6},{8,9},{9,8},{10,11... | collective-permute-start | bytes 251912 | tf_op jit(solution)/shard_map/ppermute | solution.py:186
  48.3 8.7 %collective-permute-start.8 = (bf16[8,5248]{1,0:T(8,128)(2,1)S(1)}, bf16[8,5248]{1,0:T(8,128)(2,1)S(1)}, u32[]{:S(2)}, u32[]{:S(2)}) collective-permute-start(bf16[8,5248]{1,0:T(8,128)(2,1)S(1)} %get-tuple-element.45), channel_id=1, source_target_pairs={{0,2},{1,3},{2,0},{3,1},{4,6},{5,7},{6,4},{7,5},{8,10},{9,11},{10,... | collective-permute-start | bytes 251912 | tf_op jit(solution)/shard_map/ppermute | solution.py:186
  55.2 5.4 %collective-permute-start.9 = (bf16[8,5248]{1,0:T(8,128)(2,1)S(1)}, bf16[8,5248]{1,0:T(8,128)(2,1)S(1)}, u32[]{:S(2)}, u32[]{:S(2)}) collective-permute-start(bf16[8,5248]{1,0:T(8,128)(2,1)S(1)} %get-tuple-element.46), channel_id=1, source_target_pairs={{0,3},{1,2},{2,1},{3,0},{4,7},{5,6},{6,5},{7,4},{8,11},{9,10},{10,... | collective-permute-start | bytes 251912 | tf_op jit(solution)/shard_map/ppermute | solution.py:186
  55.5 11.1 %collective-permute-start.23 = (f32[1,4096]{1,0:T(1,128)S(1)}, f32[1,4096]{1,0:T(1,128)S(1)}, u32[]{:S(2)}, u32[]{:S(2)}) collective-permute-start(f32[1,4096]{1,0:T(1,128)S(1)} %pad_maximum_fusion), channel_id=1, source_target_pairs={{0,16},{8,24},{16,0},{24,8},{1,17},{9,25},{17,1},{25,9},{2,18},{10... | collective-permute-start | bytes 49160 | tf_op jit(solution)/shard_map/ppermute | solution.py:186
  61.1 1.2 %collective-permute-start.14 = (f32[1,1280]{1,0:T(1,128)S(1)}, f32[1,1280]{1,0:T(1,128)S(1)}, u32[]{:S(2)}, u32[]{:S(2)}) collective-permute-start(f32[1,1280]{1,0:T(1,128)S(1)} %get-tuple-element.57), channel_id=1, source_target_pairs={{0,8},{8,0},{16,24},{24,16},{1,9},{9,1},{17,25},{25,17},{2,10},{10... | collective-permute-start | bytes 15368 | tf_op jit(solution)/shard_map/ppermute | solution.py:186
  62.3 3.7 %collective-permute-start.15 = (f32[1,1280]{1,0:T(1,128)S(1)}, f32[1,1280]{1,0:T(1,128)S(1)}, u32[]{:S(2)}, u32[]{:S(2)}) collective-permute-start(f32[1,1280]{1,0:T(1,128)S(1)} %add.40), channel_id=1, source_target_pairs={{0,16},{8,24},{16,0},{24,8},{1,17},{9,25},{17,1},{25,9},{2,18},{10... | collective-permute-start | bytes 15368 | tf_op jit(solution)/shard_map/ppermute | solution.py:186
  66.0 3.7 %collective-permute-start.16 = (f32[1,1280]{1,0:T(1,128)S(1)}, f32[1,1280]{1,0:T(1,128)S(1)}, u32[]{:S(2)}, u32[]{:S(2)}) collective-permute-start(f32[1,1280]{1,0:T(1,128)S(1)} %add.41), channel_id=1, source_target_pairs={{0,1},{1,0},{2,3},{3,2},{4,5},{5,4},{6,7},{7,6},{8,9},{9,8},{10,11... | collective-permute-start | bytes 15368 | tf_op jit(solution)/shard_map/ppermute | solution.py:186
  69.7 3.7 %collective-permute-start.17 = (f32[1,1280]{1,0:T(1,128)S(1)}, f32[1,1280]{1,0:T(1,128)S(1)}, u32[]{:S(2)}, u32[]{:S(2)}) collective-permute-start(f32[1,1280]{1,0:T(1,128)S(1)} %add.42), channel_id=1, source_target_pairs={{0,2},{1,3},{2,0},{3,1},{4,6},{5,7},{6,4},{7,5},{8,10},{9,11},{10,... | collective-permute-start | bytes 15368 | tf_op jit(solution)/shard_map/ppermute | solution.py:186
  73.4 6.6 %collective-permute-start.18 = (f32[1,1280]{1,0:T(1,128)S(1)}, f32[1,1280]{1,0:T(1,128)S(1)}, u32[]{:S(2)}, u32[]{:S(2)}) collective-permute-start(f32[1,1280]{1,0:T(1,128)S(1)} %add.43), channel_id=1, source_target_pairs={{0,4},{1,5},{2,6},{3,7},{4,0},{5,1},{6,2},{7,3},{8,12},{9,13},{10,... | collective-permute-start | bytes 15368 | tf_op jit(solution)/shard_map/ppermute | solution.py:186
  75.6 1.0 %copy-start.3 = (bf16[1,128,1280]{2,1,0:T(8,128)(2,1)S(1)}, bf16[1,128,1280]{2,1,0:T(8,128)(2,1)}, u32[]{:S(2)}) copy-start(bf16[1,128,1280]{2,1,0:T(8,128)(2,1)} %param.15) | copy-start | bytes 983044
  76.6 1.0 %copy-start.4 = (bf16[1,128,1280]{2,1,0:T(8,128)(2,1)S(1)}, bf16[1,128,1280]{2,1,0:T(8,128)(2,1)}, u32[]{:S(2)}) copy-start(bf16[1,128,1280]{2,1,0:T(8,128)(2,1)} %param.16) | copy-start | bytes 983044

commit v7 on v3

--- a/solution.py
+++ b/solution.py
@@ -12,7 +12,7 @@
 HEAD_DIM = 80
 LANES = 128
 CHUNKS = (2, 2)
-VMEM_BYTES = 24 * 1024 * 1024
+VMEM_BYTES = 16 * 1024 * 1024
 
 F32 = jnp.float32
 BF16 = jnp.bfloat16
@@ -48,7 +48,7 @@
     return jnp.where(lane_mask(low, high, start, stop), x, jnp.zeros_like(x))
 
 
-def project_kernel(blocks, tile, with_sum, *refs):
+def project_kernel(blocks, first, tile, with_sum, *refs):
     x_refs, w_ref = refs[:blocks], refs[blocks]
     keep_ref, send_ref = refs[blocks + 1 : blocks + 3]
     x = jnp.concatenate([ref[...] for ref in x_refs], axis=0)
@@ -56,15 +56,14 @@
         refs[blocks + 3][...] = dot(jnp.ones((16, x.shape[0]), BF16), x, (1, 0))[:1]
     x = x.T
     half = keep_ref.shape[0]
-    for t in range(0, w_ref.shape[0], tile):
-        product = dot(w_ref[t : t + tile], x, (1, 0)).T.astype(BF16)
+    for t in range(0, keep_ref.shape[1], tile):
+        product = dot(w_ref[first + t : first + t + tile], x, (1, 0)).T.astype(BF16)
         keep_ref[:, t : t + tile] = product[:half]
         send_ref[:, t : t + tile] = product[half:]
 
 
-def project(x_blocks, w_rows, with_sum):
+def project(x_blocks, w_down, first, width, with_sum):
     blocks, (rows, depth) = len(x_blocks), x_blocks[0].shape
-    width = w_rows.shape[0]
     tile = 512
     while width % tile:
         tile //= 2
@@ -72,7 +71,7 @@
     if with_sum:
         out_shape = out_shape + [jax.ShapeDtypeStruct((1, depth), F32)]
     return pl.pallas_call(
-        functools.partial(project_kernel, blocks, tile, with_sum),
+        functools.partial(project_kernel, blocks, first, tile, with_sum),
         out_shape=out_shape,
         in_specs=vmem(blocks + 1),
         out_specs=vmem(len(out_shape)),
@@ -83,7 +82,22 @@
             transcendentals=0,
         ),
         name="project",
-    )(*x_blocks, w_rows)
+    )(*x_blocks, pltpu.with_memory_space_constraint(w_down, pltpu.VMEM))
+
+
+def hold_kernel(w_ref, out_ref):
+    del w_ref, out_ref
+
+
+def hold(w_down):
+    return pl.pallas_call(
+        hold_kernel,
+        out_shape=jax.ShapeDtypeStruct(w_down.shape, w_down.dtype),
+        in_specs=[pl.BlockSpec(memory_space=pl.ANY)],
+        out_specs=pl.BlockSpec(memory_space=pl.ANY),
+        input_output_aliases={0: 0},
+        name="hold",
+    )(w_down)
 
 
 def halve_kernel(kept_ref, got_ref, keep_ref, send_ref):
@@ -226,7 +240,7 @@
     )(queries, keys, ids)
 
 
-def norm_kernel(peers, copies, patches_ref, gain_ref, routed_ref, out_ref, share_ref):
+def norm_kernel(peers, carries, patches_ref, gain_ref, routed_ref, out_ref, share_ref):
     patches, width = patches_ref.shape
     slots = routed_ref.shape[0]
     per_token = routed_ref.shape[1] // width
@@ -246,19 +260,19 @@
     inverse_rms = lax.rsqrt(jnp.mean(inputs * inputs, axis=1, keepdims=True) + 1e-06)
     normed = inputs * inverse_rms
     gain_part = jnp.sum(patch_grads * normed, axis=0, keepdims=True)
-    if copies:
-        rows = [gain_part[:, at : at + LANES] for at in range(0, width, LANES)]
+    share_ref[:, :, :width] = jnp.broadcast_to(gain_part[None], (share_ref.shape[0], 1, width))
+    if carries:
         carried = routed_ref[:, per_token * width + LANES :].astype(F32)
         capacity = slots // peers
-        pieces = share_ref.shape[1] - len(rows)
+        pieces = (share_ref.shape[2] - width) // LANES
+        row = iota((slots, LANES), 0) % capacity
         for piece in range(pieces):
-            kept = iota((slots, LANES), 0) % capacity % pieces == piece
-            kept = jnp.logical_and(kept, iota((slots, LANES), 0) % capacity < 3 * pieces)
-            rows.append(jnp.sum(jnp.where(kept, carried, 0.0), axis=0, keepdims=True))
-        for at, row in enumerate(rows):
-            share_ref[:, at : at + 1, :] = jnp.broadcast_to(row[None], (copies, 1, LANES))
-    else:
-        share_ref[...] = gain_part
+            kept = jnp.logical_and(row % pieces == piece, row < 3 * pieces)
+            line = jnp.sum(jnp.where(kept, carried, 0.0), axis=0, keepdims=True)
+            at = width + piece * LANES
+            share_ref[:, :, at : at + LANES] = jnp.broadcast_to(
+                line[None], (share_ref.shape[0], 1, LANES)
+            )
     scaled = gain_ref[...] * patch_grads
     out_ref[...] = (
         inverse_rms * (scaled - normed * jnp.mean(scaled * normed, axis=1, keepdims=True))
@@ -268,7 +282,7 @@
 def norm_backward(routed, peers, patches, gain, share):
     count, width = patches.shape
     return pl.pallas_call(
-        functools.partial(norm_kernel, peers, share[0] if len(share) == 3 else 0),
+        functools.partial(norm_kernel, peers, share[2] > width),
         out_shape=[jax.ShapeDtypeStruct((count, width), BF16), jax.ShapeDtypeStruct(share, F32)],
         in_specs=vmem(3),
         out_specs=vmem(2),
@@ -361,12 +375,11 @@
     x_blocks = [x_blocks[j] for j in order]
     probs, probs_t = window_probs(queries[0], keys[0], window_ids[0])
 
+    w_down = hold(w_down)
     terms, first = [], 0
     for index, count in enumerate(CHUNKS):
-        w_rows = lax.slice_in_dim(w_down, first, first + count * width)
-        w_rows = pltpu.with_memory_space_constraint(w_rows, pltpu.VMEM)
+        kept, sent, *sums = project(x_blocks, w_down, first, count * width, index == 0)
         first += count * width
-        kept, sent, *sums = project(x_blocks, w_rows, index == 0)
         if index == 0:
             bias_part = sums[0]
         mask = 1
@@ -377,15 +390,14 @@
     packed = pack(terms, token_target, bias_part, peers, capacity, carries)
     routed = exchange(packed, "seq", peers)
 
-    gain_rows = width // LANES
-    share = (devices, gain_rows + pieces, LANES) if carries else (1, width)
+    share = (devices, 1, width + pieces * LANES) if carries else (1, 1, width)
     out_grads, shared = norm_backward(routed, peers, patches[0], gain[None], share)
     if carries:
         shared = exchange(shared, ("img", "seq"), devices)
-        gain_total = jnp.sum(shared[:, :gain_rows], axis=0).reshape(-1)
-        bias_total = shared[:, gain_rows:].reshape(-1)
+        gain_total = jnp.sum(shared[:, 0, :width], axis=0)
+        bias_total = shared[:, 0, width:].reshape(-1)
     else:
-        gain_total = lax.psum(shared[0], ("img", "seq"))
+        gain_total = lax.psum(shared[0, 0], ("img", "seq"))
         bias_total = lax.all_gather(lax.psum(bias_part[0], "seq"), "img", tiled=True)
     grads = window_backward(out_grads, queries[0], keys[0], values[0], probs, probs_t)
     gain_grad = gain_total / math.sqrt(devices * patches.shape[1])

time: 72.1 us -> 91.1 us (1.26)
  local copies, waits for them, and re-layouts: 9.73 us -> 24.6 us
  waiting for transfers between devices: 31.2 us -> 35.3 us
    unnamed x14 -> x19, local copies, waits for them, and re-layouts: 0.04 us -> 24.6 us
    slice x1 -> x0, local copies, waits for them, and re-layouts: 8.54 us -> none  [body(): w_rows = lax.slice_in_dim(w_down, first, first + count * width)]
    ppermute x7, waiting for transfers between devices: 6.74 us -> 12.4 us  [swap(): return lax.ppermute(x, axis, [(i, i ^ mask) for i in range(n)])]
    all_to_all x2, waiting for transfers between devices: 24.5 us -> 22.9 us  [exchange(): lax.all_to_all(x, axis, split_axis=0, concat_axis=0, tiled=True)]
    dynamic_slice x1, local copies, waits for them, and re-layouts: 1.15 us -> 0.04 us  [columns(): return lax.dynamic_slice(grad_rows, (0, (image ^ j) * block), (rows, block))]
    pallas_call x3 -> x4, Pallas kernels: 7.2 us -> 7.1 us  [the longest x2 6.02 us: project(): pl.pallas_call(functools.partial(project_kernel, blocks, first, tile, wit...]
  transfers between devices with their start and end apart: 9 -> 9, of which waited for: 4 -> 6; matrix products, arithmetic and copies ran while one was open for 12% -> 0% of each run, Pallas kernels for 9% -> 7%
where the time goes in v7:
time: 91.1 us; the launch traced here: 90.7 us
  waiting for transfers between devices  35.3 us (39%)
  local copies, waits for them, and re-layouts  24.6 us (27%)
  starting transfers between devices  16.7 us (18%)
  Pallas kernels  12 us (13%)
  other arithmetic  1.33 us (1%)
    unnamed x19, local copies, waits for them, and re-layouts  24.6 us
    all_to_all x2, waiting for transfers between devices, exchange(): lax.all_to_all(x, axis, split_axis=0, concat_axis=0, tiled=True)  22.9 us
    ppermute x7, waiting for transfers between devices, swap(): return lax.ppermute(x, axis, [(i, i ^ mask) for i in range(n)])  12.4 us
    all_to_all x2, starting transfers between devices, exchange(): lax.all_to_all(x, axis, split_axis=0, concat_axis=0, tiled=True)  9.7 us
    ppermute x7, starting transfers between devices, swap(): return lax.ppermute(x, axis, [(i, i ^ mask) for i in range(n)])  6.98 us
    pallas_call x2, Pallas kernels, project(): pl.pallas_call(functools.partial(project_kernel, blocks, first, tile, wit...  6.02 us
    pallas_call x1, Pallas kernels, window_backward(): pl.pallas_call(window_kernel, out_shape=[shape] * 3, in_specs=vmem(6), ou...  2.38 us
  transfers between devices with their start and end apart: 9, of which 6 were waited for; matrix products, arithmetic and copies ran while one was open for 0% of the time, Pallas kernels for 7%

profile of v7, /device:TPU:0, one launch (start us, length us, event | category | flops | bytes accessed | tf_op | source)
XLA Modules:
  0.0 90.7 jit_solution(16008930131607735173)
XLA Ops:
  0.6 0.0 copy-start.7
  0.6 17.6 %copy.17.w_ref = bf16[5120,2048]{1,0:T(8,128)(2,1)} copy(bf16[5120,2048]{1,0:T(8,128)(2,1)} %param.13) | data formatting | bytes 41943040
  18.2 0.0 copy-done.7
  18.3 3.0 %collective-permute-start = (bf16[32,2048]{1,0:T(8,128)(2,1)S(1)}, bf16[32,2048]{1,0:T(8,128)(2,1)S(1)}, u32[]{:S(2)}, u32[]{:S(2)}) collective-permute-start(bf16[32,2048]{1,0:T(8,128)(2,1)S(1)} %get-tuple-element.38), channel_id=1, source_target_pairs={{0,16},{8,24},{16,0},{24,8},{1,17},{9,25},{17,1},{25,9},{2,18},{10... | collective-permute-start | bytes 393224 | tf_op jit(solution)/shard_map/ppermute | solution.py:189
  21.3 0.0 collective-permute-start.1
  21.3 0.2 collective-permute-start.2
  21.5 3.7 %collective-permute-done.refs_1_ = bf16[32,2048]{1,0:T(8,128)(2,1)S(1)} collective-permute-done((bf16[32,2048]{1,0:T(8,128)(2,1)S(1)}, bf16[32,2048]{1,0:T(8,128)(2,1)S(1)}, u32[]{:S(2)}, u32[]{:S(2)}) %collective-permute-start) | collective-permute-done | bytes 131104 | tf_op jit(solution)/shard_map/ppermute | solution.py:189
  25.2 0.0 collective-permute-done.1.refs_2_
  25.2 1.9 %collective-permute-done.2.refs_3_ = bf16[32,2048]{1,0:T(8,128)(2,1)S(1)} collective-permute-done((bf16[32,2048]{1,0:T(8,128)(2,1)S(1)}, bf16[32,2048]{1,0:T(8,128)(2,1)S(1)}, u32[]{:S(2)}, u32[]{:S(2)}) %collective-permute-start.2) | collective-permute-done | bytes 131104 | tf_op jit(solution)/shard_map/ppermute | solution.py:189
  27.2 0.0 copy-start
  27.2 7.0 %copy-done = bf16[5120,2048]{1,0:T(8,128)(2,1)S(1)} copy-done((bf16[5120,2048]{1,0:T(8,128)(2,1)S(1)}, bf16[5120,2048]{1,0:T(8,128)(2,1)}, u32[]{:S(2)}) %copy-start) | copy-done | bytes 20971544
  34.1 0.0 copy-start.5
  34.1 0.0 copy-start.8
  34.1 0.0 copy-start.1
  34.1 0.0 copy-start.2
  34.1 0.0 copy-start.3
  34.1 0.0 copy-start.6
  34.2 0.0 copy-start.4
  34.2 3.0 %project.3 = (bf16[64,2560]{1,0:T(8,128)(2,1)S(1)}, bf16[64,2560]{1,0:T(8,128)(2,1)S(1)}) custom-call(bf16[32,2048]{1,0:T(8,128)(2,1)S(1)} %get-tuple-element.39.refs_0_, bf16[32,2048]{1,0:T(8,128)(2,1)S(1)} %collective-permute-done.refs_1_, bf16[32,2048]{1,0:T(8,128)(2,1)S(1)} %collective-permute-done.1.refs_2_, ...), custom_call_target="tpu_custom_call" | custom-call | flops 1342177280 | bytes 10485760 | tf_op jit(solution)/shard_map/project/pallas_call | solution.py:73
  37.2 0.3 collective-permute-start.5
  37.5 3.0 %project.2 = (bf16[64,2560]{1,0:T(8,128)(2,1)S(1)}, bf16[64,2560]{1,0:T(8,128)(2,1)S(1)}, f32[1,2048]{1,0:T(1,128)S(1)}) custom-call(bf16[32,2048]{1,0:T(8,128)(2,1)S(1)} %get-tuple-element.39.refs_0_, bf16[32,2048]{1,0:T(8,128)(2,1)S(1)} %collective-permute-done.refs_1_, bf16[32,2048]{1,0:T(8,128)(2,1)S(1)} %collective-permute-done.1.refs_2_, ...), custom_call_target="tpu_custom_call" | custom-call | flops 1342177280 | bytes 10485760 | tf_op jit(solution)/shard_map/project/pallas_call | solution.py:73
  40.5 0.3 collective-permute-start.3
  40.8 0.0 collective-permute-done.5.got_ref
  40.8 0.1 halve.3
  40.9 1.6 %collective-permute-start.6 = (bf16[32,2560]{1,0:T(8,128)(2,1)S(1)}, bf16[32,2560]{1,0:T(8,128)(2,1)S(1)}, u32[]{:S(2)}, u32[]{:S(2)}) collective-permute-start(bf16[32,2560]{1,0:T(8,128)(2,1)S(1)} %get-tuple-element.28), channel_id=1, source_target_pairs={{0,16},{8,24},{16,0},{24,8},{1,17},{9,25},{17,1},{25,9},{2,18},{10... | collective-permute-start | bytes 491528 | tf_op jit(solution)/shard_map/ppermute | solution.py:189
  42.5 0.0 collective-permute-done.3.got_ref
  42.5 0.1 halve.2
  42.6 1.5 %collective-permute-start.4 = (bf16[32,2560]{1,0:T(8,128)(2,1)S(1)}, bf16[32,2560]{1,0:T(8,128)(2,1)S(1)}, u32[]{:S(2)}, u32[]{:S(2)}) collective-permute-start(bf16[32,2560]{1,0:T(8,128)(2,1)S(1)} %get-tuple-element.24), channel_id=1, source_target_pairs={{0,16},{8,24},{16,0},{24,8},{1,17},{9,25},{17,1},{25,9},{2,18},{10... | collective-permute-start | bytes 491528 | tf_op jit(solution)/shard_map/ppermute | solution.py:189
  44.1 3.9 %collective-permute-done.6.refs_3_ = bf16[32,2560]{1,0:T(8,128)(2,1)S(1)} collective-permute-done((bf16[32,2560]{1,0:T(8,128)(2,1)S(1)}, bf16[32,2560]{1,0:T(8,128)(2,1)S(1)}, u32[]{:S(2)}, u32[]{:S(2)}) %collective-permute-start.6) | collective-permute-done | bytes 163872 | tf_op jit(solution)/shard_map/ppermute | solution.py:189
  48.0 2.9 %collective-permute-done.4.refs_1_ = bf16[32,2560]{1,0:T(8,128)(2,1)S(1)} collective-permute-done((bf16[32,2560]{1,0:T(8,128)(2,1)S(1)}, bf16[32,2560]{1,0:T(8,128)(2,1)S(1)}, u32[]{:S(2)}, u32[]{:S(2)}) %collective-permute-start.4) | collective-permute-done | bytes 163872 | tf_op jit(solution)/shard_map/ppermute | solution.py:189
  50.9 0.0 copy-done.5
  50.9 1.3 %pack.1 = bf16[64,5376]{1,0:T(8,128)(2,1)} custom-call(s32[1,32]{1,0:T(1,128)S(1)} %copy-done.5, f32[32,2560]{1,0:T(8,128)S(1)} %get-tuple-element.23.refs_0_, bf16[32,2560]{1,0:T(8,128)(2,1)S(1)} %collective-permute-done.4.refs_1_, f32[32,2560]{1,0:T(8,128)S(1)} %get-tuple-element.27.refs_2_, bf16[32,2560]{1,0:T(8,128)(2,1)S(1)} %collective-permute-done.6.refs_3_, ...), custom_call_target="tpu_custom_call" | custom-call | flops 22020096 | bytes 1720320 | tf_op jit(solution)/shard_map/pack/pallas_call | solution.py:172
  52.1 6.0 %all-to-all-start = ((bf16[8,8,5376]{2,1,0:T(8,128)(2,1)}), bf16[8,8,5376]{2,1,0:T(8,128)(2,1)S(1)}, u32[]{:S(2)}, u32[]{:S(2)}) async-start(bf16[8,8,5376]{2,1,0:T(8,128)(2,1)} %bitcast.5), calls=%async_computation | async-start | bytes 1376256 | tf_op jit(solution)/shard_map/all_to_all | solution.py:196
  58.2 0.0 copy-done.8
  58.2 17.8 %all-to-all-done = bf16[8,8,5376]{2,1,0:T(8,128)(2,1)S(1)} async-done(((bf16[8,8,5376]{2,1,0:T(8,128)(2,1)}), bf16[8,8,5376]{2,1,0:T(8,128)(2,1)S(1)}, u32[]{:S(2)}, u32[]{:S(2)}) %all-to-all-start) | async-done | bytes 688160 | tf_op jit(solution)/shard_map/all_to_all | solution.py:196
  76.0 0.0 copy-done.1
  76.1 1.1 %norm.1 = (bf16[128,1280]{1,0:T(8,128)(2,1)S(1)}, f32[32,1,1536]{2,1,0:T(1,128)}) custom-call(bf16[128,1280]{1,0:T(8,128)(2,1)S(1)} %bitcast.20, f32[1,1280]{1,0:T(1,128)S(1)} %broadcast_in_dim.12.gain_ref, bf16[64,5376]{1,0:T(8,128)(2,1)S(1)} %bitcast.19), custom_call_target="tpu_custom_call" | custom-call | flops 88080384 | bytes 1343488 | tf_op jit(solution)/shard_map/norm/pallas_call | solution.py:284
  77.1 3.7 %all-to-all-start.1 = ((f32[32,1,1536]{2,1,0:T(1,128)}), f32[32,1,1536]{2,1,0:T(1,128)S(1)}, u32[]{:S(2)}, u32[]{:S(2)}) async-start(f32[32,1,1536]{2,1,0:T(1,128)} %get-tuple-element.36), calls=%async_computation.1 | async-start | bytes 393216 | tf_op jit(solution)/shard_map/all_to_all | solution.py:196
  80.8 0.0 copy-done.2
  80.8 0.0 copy-done.3
  80.8 0.0 copy-done.6
  80.8 1.1 %probs.1 = (f32[16,128,128]{2,1,0:T(8,128)S(1)}, f32[16,128,128]{2,1,0:T(8,128)S(1)}) custom-call(bf16[128,1280]{1,0:T(8,128)(2,1)S(1)} %bitcast.21, bf16[128,1280]{1,0:T(8,128)(2,1)S(1)} %bitcast.23, s32[1,32]{1,0:T(1,128)S(1)} %bitcast.26), custom_call_target="tpu_custom_call" | custom-call | flops 268435456 | bytes 2097152 | tf_op jit(solution)/shard_map/probs/pallas_call | solution.py:228
  81.9 0.0 copy-done.4
  81.9 2.4 %window.1 = (bf16[128,1280]{1,0:T(8,128)(2,1)}, bf16[128,1280]{1,0:T(8,128)(2,1)}, bf16[128,1280]{1,0:T(8,128)(2,1)}) custom-call(bf16[128,1280]{1,0:T(8,128)(2,1)S(1)} %get-tuple-element.30.g_ref, bf16[128,1280]{1,0:T(8,128)(2,1)S(1)} %bitcast.22, bf16[128,1280]{1,0:T(8,128)(2,1)S(1)} %bitcast.24, bf16[128,1280]{1,0:T(8,128)(2,1)S(1)} %bitcast.25, ...), custom_call_target="tpu_custom_call" | custom-call | flops 335544320 | bytes 4390912 | tf_op jit(solution)/shard_map/window/pallas_call | solution.py:340
  84.3 5.1 %all-to-all-done.1 = f32[32,1,1536]{2,1,0:T(1,128)S(1)} async-done(((f32[32,1,1536]{2,1,0:T(1,128)}), f32[32,1,1536]{2,1,0:T(1,128)S(1)}, u32[]{:S(2)}, u32[]{:S(2)}) %all-to-all-start.1) | async-done | bytes 196640 | tf_op jit(solution)/shard_map/all_to_all | solution.py:196
  89.4 0.1 slice_reduce_fusion
  89.4 0.6 broadcast_multiply_fusion
  90.0 0.6 slice_multiply_fusion
  (3 shorter events, 0.0 us)
Async XLA Ops:
  0.6 17.6 %copy-start.7 = (bf16[1,32,8192]{2,1,0:T(8,128)(2,1)S(1)}, bf16[1,32,8192]{2,1,0:T(8,128)(2,1)}, u32[]{:S(2)}) copy-start(bf16[1,32,8192]{2,1,0:T(8,128)(2,1)} %param.9) | copy-start | bytes 1572868
  18.3 7.0 %collective-permute-start = (bf16[32,2048]{1,0:T(8,128)(2,1)S(1)}, bf16[32,2048]{1,0:T(8,128)(2,1)S(1)}, u32[]{:S(2)}, u32[]{:S(2)}) collective-permute-start(bf16[32,2048]{1,0:T(8,128)(2,1)S(1)} %get-tuple-element.38), channel_id=1, source_target_pairs={{0,16},{8,24},{16,0},{24,8},{1,17},{9,25},{17,1},{25,9},{2,18},{10... | collective-permute-start | bytes 393224 | tf_op jit(solution)/shard_map/ppermute | solution.py:189
  21.3 3.9 %collective-permute-start.1 = (bf16[32,2048]{1,0:T(8,128)(2,1)S(1)}, bf16[32,2048]{1,0:T(8,128)(2,1)S(1)}, u32[]{:S(2)}, u32[]{:S(2)}) collective-permute-start(bf16[32,2048]{1,0:T(8,128)(2,1)S(1)} %get-tuple-element.40), channel_id=1, source_target_pairs={{0,8},{8,0},{16,24},{24,16},{1,9},{9,1},{17,25},{25,17},{2,10},{10... | collective-permute-start | bytes 393224 | tf_op jit(solution)/shard_map/ppermute | solution.py:189
  21.3 5.9 %collective-permute-start.2 = (bf16[32,2048]{1,0:T(8,128)(2,1)S(1)}, bf16[32,2048]{1,0:T(8,128)(2,1)S(1)}, u32[]{:S(2)}, u32[]{:S(2)}) collective-permute-start(bf16[32,2048]{1,0:T(8,128)(2,1)S(1)} %get-tuple-element.37), channel_id=1, source_target_pairs={{0,24},{8,16},{16,8},{24,0},{1,25},{9,17},{17,9},{25,1},{2,26},{10... | collective-permute-start | bytes 393224 | tf_op jit(solution)/shard_map/ppermute | solution.py:189
  27.2 7.0 %copy-start = (bf16[5120,2048]{1,0:T(8,128)(2,1)S(1)}, bf16[5120,2048]{1,0:T(8,128)(2,1)}, u32[]{:S(2)}) copy-start(bf16[5120,2048]{1,0:T(8,128)(2,1)} %hold.1.refs_4_) | copy-start | bytes 62914564
  34.1 16.7 %copy-start.5 = (s32[1,32]{1,0:T(1,128)S(1)}, s32[1,32]{1,0:T(1,128)}, u32[]{:S(2)}) copy-start(s32[1,32]{1,0:T(1,128)} %targets_ref.1) | copy-start | bytes 388
  34.1 24.1 %copy-start.8 = (f32[1280]{0:T(1024)S(1)}, f32[1280]{0:T(1024)}, u32[]{:S(2)}) copy-start(f32[1280]{0:T(1024)} %param.12) | copy-start | bytes 15364
  34.1 41.9 %copy-start.1 = (bf16[1,128,1280]{2,1,0:T(8,128)(2,1)S(1)}, bf16[1,128,1280]{2,1,0:T(8,128)(2,1)}, u32[]{:S(2)}) copy-start(bf16[1,128,1280]{2,1,0:T(8,128)(2,1)} %param.11) | copy-start | bytes 983044
  34.1 46.7 %copy-start.2 = (bf16[1,128,1280]{2,1,0:T(8,128)(2,1)S(1)}, bf16[1,128,1280]{2,1,0:T(8,128)(2,1)}, u32[]{:S(2)}) copy-start(bf16[1,128,1280]{2,1,0:T(8,128)(2,1)} %param.14) | copy-start | bytes 983044
  34.1 46.7 %copy-start.3 = (bf16[1,128,1280]{2,1,0:T(8,128)(2,1)S(1)}, bf16[1,128,1280]{2,1,0:T(8,128)(2,1)}, u32[]{:S(2)}) copy-start(bf16[1,128,1280]{2,1,0:T(8,128)(2,1)} %param.15) | copy-start | bytes 983044
  34.1 46.7 %copy-start.6 = (s32[1,1,32]{2,1,0:T(1,128)S(1)}, s32[1,1,32]{2,1,0:T(1,128)}, u32[]{:S(2)}) copy-start(s32[1,1,32]{2,1,0:T(1,128)} %param.17) | copy-start | bytes 388
  34.2 47.8 %copy-start.4 = (bf16[1,128,1280]{2,1,0:T(8,128)(2,1)S(1)}, bf16[1,128,1280]{2,1,0:T(8,128)(2,1)}, u32[]{:S(2)}) copy-start(bf16[1,128,1280]{2,1,0:T(8,128)(2,1)} %param.16) | copy-start | bytes 983044
  37.2 3.7 %collective-permute-start.5 = (bf16[64,2560]{1,0:T(8,128)(2,1)S(1)}, bf16[64,2560]{1,0:T(8,128)(2,1)S(1)}, u32[]{:S(2)}, u32[]{:S(2)}) collective-permute-start(bf16[64,2560]{1,0:T(8,128)(2,1)S(1)} %get-tuple-element.26), channel_id=1, source_target_pairs={{0,8},{8,0},{16,24},{24,16},{1,9},{9,1},{17,25},{25,17},{2,10},{10... | collective-permute-start | bytes 983048 | tf_op jit(solution)/shard_map/ppermute | solution.py:189
  40.5 2.0 %collective-permute-start.3 = (bf16[64,2560]{1,0:T(8,128)(2,1)S(1)}, bf16[64,2560]{1,0:T(8,128)(2,1)S(1)}, u32[]{:S(2)}, u32[]{:S(2)}) collective-permute-start(bf16[64,2560]{1,0:T(8,128)(2,1)S(1)} %get-tuple-element.22), channel_id=1, source_target_pairs={{0,8},{8,0},{16,24},{24,16},{1,9},{9,1},{17,25},{25,17},{2,10},{10... | collective-permute-start | bytes 983048 | tf_op jit(solution)/shard_map/ppermute | solution.py:189
  40.9 7.1 %collective-permute-start.6 = (bf16[32,2560]{1,0:T(8,128)(2,1)S(1)}, bf16[32,2560]{1,0:T(8,128)(2,1)S(1)}, u32[]{:S(2)}, u32[]{:S(2)}) collective-permute-start(bf16[32,2560]{1,0:T(8,128)(2,1)S(1)} %get-tuple-element.28), channel_id=1, source_target_pairs={{0,16},{8,24},{16,0},{24,8},{1,17},{9,25},{17,1},{25,9},{2,18},{10... | collective-permute-start | bytes 491528 | tf_op jit(solution)/shard_map/ppermute | solution.py:189
  42.6 8.3 %collective-permute-start.4 = (bf16[32,2560]{1,0:T(8,128)(2,1)S(1)}, bf16[32,2560]{1,0:T(8,128)(2,1)S(1)}, u32[]{:S(2)}, u32[]{:S(2)}) collective-permute-start(bf16[32,2560]{1,0:T(8,128)(2,1)S(1)} %get-tuple-element.24), channel_id=1, source_target_pairs={{0,16},{8,24},{16,0},{24,8},{1,17},{9,25},{17,1},{25,9},{2,18},{10... | collective-permute-start | bytes 491528 | tf_op jit(solution)/shard_map/ppermute | solution.py:189
  52.1 23.9 %all-to-all-start = ((bf16[8,8,5376]{2,1,0:T(8,128)(2,1)}), bf16[8,8,5376]{2,1,0:T(8,128)(2,1)S(1)}, u32[]{:S(2)}, u32[]{:S(2)}) async-start(bf16[8,8,5376]{2,1,0:T(8,128)(2,1)} %bitcast.5), calls=%async_computation | async-start | bytes 1376256 | tf_op jit(solution)/shard_map/all_to_all | solution.py:196
  77.1 12.2 %all-to-all-start.1 = ((f32[32,1,1536]{2,1,0:T(1,128)}), f32[32,1,1536]{2,1,0:T(1,128)S(1)}, u32[]{:S(2)}, u32[]{:S(2)}) async-start(f32[32,1,1536]{2,1,0:T(1,128)} %get-tuple-element.36), calls=%async_computation.1 | async-start | bytes 393216 | tf_op jit(solution)/shard_map/all_to_all | solution.py:196

commit v8 on v7

--- a/solution.py
+++ b/solution.py
@@ -12,7 +12,8 @@
 HEAD_DIM = 80
 LANES = 128
 CHUNKS = (2, 2)
-VMEM_BYTES = 16 * 1024 * 1024
+VMEM_BYTES = 24 * 1024 * 1024
+PROJECT_VMEM_BYTES = 40 * 1024 * 1024
 
 F32 = jnp.float32
 BF16 = jnp.bfloat16
@@ -48,56 +49,57 @@
     return jnp.where(lane_mask(low, high, start, stop), x, jnp.zeros_like(x))
 
 
-def project_kernel(blocks, first, tile, with_sum, *refs):
-    x_refs, w_ref = refs[:blocks], refs[blocks]
-    keep_ref, send_ref = refs[blocks + 1 : blocks + 3]
+def project_kernel(blocks, tile, last, with_sum, *refs):
+    x_refs, w_ref, w_hbm = refs[:blocks], refs[blocks], refs[blocks + 1]
+    keep_ref, send_ref = refs[blocks + 2 : blocks + 4]
+    w_last, sem = refs[-2:]
+    copy = pltpu.make_async_copy(w_hbm.at[pl.ds(last, w_last.shape[0])], w_last, sem)
+    copy.start()
     x = jnp.concatenate([ref[...] for ref in x_refs], axis=0)
     if with_sum:
-        refs[blocks + 3][...] = dot(jnp.ones((16, x.shape[0]), BF16), x, (1, 0))[:1]
+        refs[blocks + 4][...] = dot(jnp.ones((16, x.shape[0]), BF16), x, (1, 0))[:1]
     x = x.T
     half = keep_ref.shape[0]
-    for t in range(0, keep_ref.shape[1], tile):
-        product = dot(w_ref[first + t : first + t + tile], x, (1, 0)).T.astype(BF16)
-        keep_ref[:, t : t + tile] = product[:half]
-        send_ref[:, t : t + tile] = product[half:]
+
+    def store(w_rows, at):
+        product = dot(w_rows, x, (1, 0)).T.astype(BF16)
+        keep_ref[:, at : at + tile] = product[:half]
+        send_ref[:, at : at + tile] = product[half:]
+
+    for t in range(0, w_ref.shape[0], tile):
+        store(w_ref[t : t + tile], t)
+    copy.wait()
+    for t in range(0, w_last.shape[0], tile):
+        store(w_last[t : t + tile], w_ref.shape[0] + t)
 
 
 def project(x_blocks, w_down, first, width, with_sum):
     blocks, (rows, depth) = len(x_blocks), x_blocks[0].shape
-    tile = 512
-    while width % tile:
+    streamed = width // 4
+    tile = 640
+    while streamed % tile:
         tile //= 2
+    last = first + width - streamed
+    w_rows = pltpu.with_memory_space_constraint(
+        lax.slice_in_dim(w_down, first, last), pltpu.VMEM
+    )
     out_shape = [jax.ShapeDtypeStruct((blocks * rows // 2, width), BF16)] * 2
     if with_sum:
         out_shape = out_shape + [jax.ShapeDtypeStruct((1, depth), F32)]
     return pl.pallas_call(
-        functools.partial(project_kernel, blocks, first, tile, with_sum),
+        functools.partial(project_kernel, blocks, tile, last, with_sum),
         out_shape=out_shape,
-        in_specs=vmem(blocks + 1),
+        in_specs=vmem(blocks + 1) + [pl.BlockSpec(memory_space=pl.ANY)],
         out_specs=vmem(len(out_shape)),
-        compiler_params=pltpu.CompilerParams(vmem_limit_bytes=VMEM_BYTES),
+        scratch_shapes=[pltpu.VMEM((streamed, depth), BF16), pltpu.SemaphoreType.DMA],
+        compiler_params=pltpu.CompilerParams(vmem_limit_bytes=PROJECT_VMEM_BYTES),
         cost_estimate=pl.CostEstimate(
             flops=2 * blocks * rows * depth * width,
             bytes_accessed=2 * width * depth,
             transcendentals=0,
         ),
         name="project",
-    )(*x_blocks, pltpu.with_memory_space_constraint(w_down, pltpu.VMEM))
-
-
-def hold_kernel(w_ref, out_ref):
-    del w_ref, out_ref
-
-
-def hold(w_down):
-    return pl.pallas_call(
-        hold_kernel,
-        out_shape=jax.ShapeDtypeStruct(w_down.shape, w_down.dtype),
-        in_specs=[pl.BlockSpec(memory_space=pl.ANY)],
-        out_specs=pl.BlockSpec(memory_space=pl.ANY),
-        input_output_aliases={0: 0},
-        name="hold",
-    )(w_down)
+    )(*x_blocks, w_rows, w_down)
 
 
 def halve_kernel(kept_ref, got_ref, keep_ref, send_ref):
@@ -375,7 +377,6 @@
     x_blocks = [x_blocks[j] for j in order]
     probs, probs_t = window_probs(queries[0], keys[0], window_ids[0])
 
-    w_down = hold(w_down)
     terms, first = [], 0
     for index, count in enumerate(CHUNKS):
         kept, sent, *sums = project(x_blocks, w_down, first, count * width, index == 0)

time: 91.1 us -> 70.8 us (0.78)
  local copies, waits for them, and re-layouts: 24.6 us -> 7.45 us
  waiting for transfers between devices: 35.3 us -> 29.1 us
  Pallas kernels: 12 us -> 15.1 us
    unnamed x19 -> x14, local copies, waits for them, and re-layouts: 24.6 us -> 0.03 us
    slice x0 -> x1, local copies, waits for them, and re-layouts: none -> 6.27 us  [project(): lax.slice_in_dim(w_down, first, last)]
    ppermute x7, waiting for transfers between devices: 12.4 us -> 6.74 us  [swap(): return lax.ppermute(x, axis, [(i, i ^ mask) for i in range(n)])]
    pallas_call x3 -> x2, Pallas kernels: 6.02 us -> 9.12 us  [project(): pl.pallas_call(functools.partial(project_kernel, blocks, tile, last, with...]
    dynamic_slice x1, local copies, waits for them, and re-layouts: 0.04 us -> 1.14 us  [columns(): return lax.dynamic_slice(grad_rows, (0, (image ^ j) * block), (rows, block))]
  transfers between devices with their start and end apart: 9 -> 9, of which waited for: 6 -> 4; matrix products, arithmetic and copies ran while one was open for 0% -> 9% of each run, Pallas kernels for 7% -> 12%
where the time goes in v8:
time: 70.8 us; the launch traced here: 70.6 us
  waiting for transfers between devices  29.1 us (41%)
  starting transfers between devices  16.7 us (24%)
  Pallas kernels  15.1 us (21%)
  local copies, waits for them, and re-layouts  7.45 us (11%)
  other arithmetic  1.33 us (2%)
  between operations  0.81 us (1%)
    all_to_all x2, waiting for transfers between devices, exchange(): lax.all_to_all(x, axis, split_axis=0, concat_axis=0, tiled=True)  22.4 us
    all_to_all x2, starting transfers between devices, exchange(): lax.all_to_all(x, axis, split_axis=0, concat_axis=0, tiled=True)  9.66 us
    pallas_call x2, Pallas kernels, project(): pl.pallas_call(functools.partial(project_kernel, blocks, tile, last, with...  9.12 us
    ppermute x7, starting transfers between devices, swap(): return lax.ppermute(x, axis, [(i, i ^ mask) for i in range(n)])  7.06 us
    ppermute x7, waiting for transfers between devices, swap(): return lax.ppermute(x, axis, [(i, i ^ mask) for i in range(n)])  6.74 us
    slice x1, local copies, waits for them, and re-layouts, project(): lax.slice_in_dim(w_down, first, last)  6.27 us
    pallas_call x1, Pallas kernels, window_backward(): pl.pallas_call(window_kernel, out_shape=[shape] * 3, in_specs=vmem(6), ou...  2.42 us
  transfers between devices with their start and end apart: 9, of which 4 were waited for; matrix products, arithmetic and copies ran while one was open for 9% of the time, Pallas kernels for 12%

profile of v8, /device:TPU:0, one launch (start us, length us, event | category | flops | bytes accessed | tf_op | source)
XLA Modules:
  0.0 70.6 jit_solution(16412894225618607776)
XLA Ops:
  0.7 1.1 %dynamic-slice_bitcast_fusion = (bf16[32,2048]{1,0:T(8,128)(2,1)S(1)}, bf16[32,2048]{1,0:T(8,128)(2,1)S(1)}, bf16[32,2048]{1,0:T(8,128)(2,1)S(1)}, bf16[32,2048]{1,0:T(8,128)(2,1)S(1)}) fusion(bf16[1,32,8192]{2,1,0:T(8,128)(2,1)} %param.9, s32[]{:T(128)S(6)} %select_n.15, s32[]{:T(128)S(6)} %select_n.13, s32[]{:T(128)S(6)} %select_n.12, s32[]{:T(128)S(6)} %select_n.14), kind=kLoop, calls=%fused_computation.1 | loop fusion | bytes 1048592 | tf_op jit(solution)/shard_map/dynamic_slice | solution.py:374
  1.8 3.0 %collective-permute-start = (bf16[32,2048]{1,0:T(8,128)(2,1)S(1)}, bf16[32,2048]{1,0:T(8,128)(2,1)S(1)}, u32[]{:S(2)}, u32[]{:S(2)}) collective-permute-start(bf16[32,2048]{1,0:T(8,128)(2,1)S(1)} %get-tuple-element.40), channel_id=1, source_target_pairs={{0,16},{8,24},{16,0},{24,8},{1,17},{9,25},{17,1},{25,9},{2,18},{10... | collective-permute-start | bytes 393224 | tf_op jit(solution)/shard_map/ppermute | solution.py:191
  4.8 0.0 collective-permute-start.1
  4.8 0.2 collective-permute-start.2
  5.0 6.3 %fusion = (bf16[1920,2048]{1,0:T(8,128)(2,1)S(1)}, bf16[1920,2048]{1,0:T(8,128)(2,1)S(1)}) fusion(bf16[5120,2048]{1,0:T(8,128)(2,1)} %refs_5_.3), kind=kLoop, calls=%fused_computation.7 | loop fusion | bytes 31457280 | tf_op jit(solution)/shard_map/slice | solution.py:84
  11.3 0.0 collective-permute-done.refs_1_
  11.3 0.0 collective-permute-done.1.refs_2_
  11.3 0.0 collective-permute-done.2.refs_3_
  11.3 4.5 %project.3 = (bf16[64,2560]{1,0:T(8,128)(2,1)S(1)}, bf16[64,2560]{1,0:T(8,128)(2,1)S(1)}) custom-call(bf16[32,2048]{1,0:T(8,128)(2,1)S(1)} %get-tuple-element.41.refs_0_, bf16[32,2048]{1,0:T(8,128)(2,1)S(1)} %collective-permute-done.refs_1_, bf16[32,2048]{1,0:T(8,128)(2,1)S(1)} %collective-permute-done.1.refs_2_, ...), custom_call_target="tpu_custom_call" | custom-call | flops 1342177280 | bytes 10485760 | tf_op jit(solution)/shard_map/project/pallas_call | solution.py:89
  15.9 0.4 collective-permute-start.5
  16.2 0.0 copy-start.4
  16.3 0.0 copy-start.6
  16.3 0.0 copy-start
  16.3 0.0 copy-start.1
  16.3 0.0 copy-start.2
  16.3 0.0 copy-start.5
  16.3 0.0 copy-start.3
  16.3 4.6 %project.2 = (bf16[64,2560]{1,0:T(8,128)(2,1)S(1)}, bf16[64,2560]{1,0:T(8,128)(2,1)S(1)}, f32[1,2048]{1,0:T(1,128)S(1)}) custom-call(bf16[32,2048]{1,0:T(8,128)(2,1)S(1)} %get-tuple-element.41.refs_0_, bf16[32,2048]{1,0:T(8,128)(2,1)S(1)} %collective-permute-done.refs_1_, bf16[32,2048]{1,0:T(8,128)(2,1)S(1)} %collective-permute-done.1.refs_2_, ...), custom_call_target="tpu_custom_call" | custom-call | flops 1342177280 | bytes 10485760 | tf_op jit(solution)/shard_map/project/pallas_call | solution.py:89
  20.9 0.3 collective-permute-start.3
  21.2 0.0 collective-permute-done.5.got_ref
  21.2 0.1 halve.3
  21.2 2.0 %collective-permute-start.6 = (bf16[32,2560]{1,0:T(8,128)(2,1)S(1)}, bf16[32,2560]{1,0:T(8,128)(2,1)S(1)}, u32[]{:S(2)}, u32[]{:S(2)}) collective-permute-start(bf16[32,2560]{1,0:T(8,128)(2,1)S(1)} %get-tuple-element.28), channel_id=1, source_target_pairs={{0,16},{8,24},{16,0},{24,8},{1,17},{9,25},{17,1},{25,9},{2,18},{10... | collective-permute-start | bytes 491528 | tf_op jit(solution)/shard_map/ppermute | solution.py:191
  23.2 0.0 collective-permute-done.3.got_ref
  23.2 0.1 halve.2
  23.3 1.2 %collective-permute-start.4 = (bf16[32,2560]{1,0:T(8,128)(2,1)S(1)}, bf16[32,2560]{1,0:T(8,128)(2,1)S(1)}, u32[]{:S(2)}, u32[]{:S(2)}) collective-permute-start(bf16[32,2560]{1,0:T(8,128)(2,1)S(1)} %get-tuple-element.24), channel_id=1, source_target_pairs={{0,16},{8,24},{16,0},{24,8},{1,17},{9,25},{17,1},{25,9},{2,18},{10... | collective-permute-start | bytes 491528 | tf_op jit(solution)/shard_map/ppermute | solution.py:191
  24.5 3.8 %collective-permute-done.6.refs_3_ = bf16[32,2560]{1,0:T(8,128)(2,1)S(1)} collective-permute-done((bf16[32,2560]{1,0:T(8,128)(2,1)S(1)}, bf16[32,2560]{1,0:T(8,128)(2,1)S(1)}, u32[]{:S(2)}, u32[]{:S(2)}) %collective-permute-start.6) | collective-permute-done | bytes 163872 | tf_op jit(solution)/shard_map/ppermute | solution.py:191
  28.3 2.9 %collective-permute-done.4.refs_1_ = bf16[32,2560]{1,0:T(8,128)(2,1)S(1)} collective-permute-done((bf16[32,2560]{1,0:T(8,128)(2,1)S(1)}, bf16[32,2560]{1,0:T(8,128)(2,1)S(1)}, u32[]{:S(2)}, u32[]{:S(2)}) %collective-permute-start.4) | collective-permute-done | bytes 163872 | tf_op jit(solution)/shard_map/ppermute | solution.py:191
  31.2 0.0 copy-done.4
  31.2 1.3 %pack.1 = bf16[64,5376]{1,0:T(8,128)(2,1)} custom-call(s32[1,32]{1,0:T(1,128)S(1)} %copy-done.4, f32[32,2560]{1,0:T(8,128)S(1)} %get-tuple-element.23.refs_0_, bf16[32,2560]{1,0:T(8,128)(2,1)S(1)} %collective-permute-done.4.refs_1_, f32[32,2560]{1,0:T(8,128)S(1)} %get-tuple-element.27.refs_2_, bf16[32,2560]{1,0:T(8,128)(2,1)S(1)} %collective-permute-done.6.refs_3_, ...), custom_call_target="tpu_custom_call" | custom-call | flops 22020096 | bytes 1720320 | tf_op jit(solution)/shard_map/pack/pallas_call | solution.py:174
  32.5 6.0 %all-to-all-start = ((bf16[8,8,5376]{2,1,0:T(8,128)(2,1)}), bf16[8,8,5376]{2,1,0:T(8,128)(2,1)S(1)}, u32[]{:S(2)}, u32[]{:S(2)}) async-start(bf16[8,8,5376]{2,1,0:T(8,128)(2,1)} %bitcast.5), calls=%async_computation | async-start | bytes 1376256 | tf_op jit(solution)/shard_map/all_to_all | solution.py:198
  38.5 0.0 copy-done.6
  38.5 17.4 %all-to-all-done = bf16[8,8,5376]{2,1,0:T(8,128)(2,1)S(1)} async-done(((bf16[8,8,5376]{2,1,0:T(8,128)(2,1)}), bf16[8,8,5376]{2,1,0:T(8,128)(2,1)S(1)}, u32[]{:S(2)}, u32[]{:S(2)}) %all-to-all-start) | async-done | bytes 688160 | tf_op jit(solution)/shard_map/all_to_all | solution.py:198
  55.9 0.0 copy-done
  55.9 1.1 %norm.1 = (bf16[128,1280]{1,0:T(8,128)(2,1)S(1)}, f32[32,1,1536]{2,1,0:T(1,128)}) custom-call(bf16[128,1280]{1,0:T(8,128)(2,1)S(1)} %bitcast.20, f32[1,1280]{1,0:T(1,128)S(1)} %broadcast_in_dim.12.gain_ref, bf16[64,5376]{1,0:T(8,128)(2,1)S(1)} %bitcast.19), custom_call_target="tpu_custom_call" | custom-call | flops 88080384 | bytes 1343488 | tf_op jit(solution)/shard_map/norm/pallas_call | solution.py:286
  57.0 3.7 %all-to-all-start.1 = ((f32[32,1,1536]{2,1,0:T(1,128)}), f32[32,1,1536]{2,1,0:T(1,128)S(1)}, u32[]{:S(2)}, u32[]{:S(2)}) async-start(f32[32,1,1536]{2,1,0:T(1,128)} %get-tuple-element.36), calls=%async_computation.1 | async-start | bytes 393216 | tf_op jit(solution)/shard_map/all_to_all | solution.py:198
  60.7 0.0 copy-done.1
  60.7 0.0 copy-done.2
  60.7 0.0 copy-done.5
  60.7 1.1 %probs.1 = (f32[16,128,128]{2,1,0:T(8,128)S(1)}, f32[16,128,128]{2,1,0:T(8,128)S(1)}) custom-call(bf16[128,1280]{1,0:T(8,128)(2,1)S(1)} %bitcast.21, bf16[128,1280]{1,0:T(8,128)(2,1)S(1)} %bitcast.23, s32[1,32]{1,0:T(1,128)S(1)} %bitcast.26), custom_call_target="tpu_custom_call" | custom-call | flops 268435456 | bytes 2097152 | tf_op jit(solution)/shard_map/probs/pallas_call | solution.py:230
  61.8 0.0 copy-done.3
  61.8 2.4 %window.1 = (bf16[128,1280]{1,0:T(8,128)(2,1)}, bf16[128,1280]{1,0:T(8,128)(2,1)}, bf16[128,1280]{1,0:T(8,128)(2,1)}) custom-call(bf16[128,1280]{1,0:T(8,128)(2,1)S(1)} %get-tuple-element.30.g_ref, bf16[128,1280]{1,0:T(8,128)(2,1)S(1)} %bitcast.22, bf16[128,1280]{1,0:T(8,128)(2,1)S(1)} %bitcast.24, bf16[128,1280]{1,0:T(8,128)(2,1)S(1)} %bitcast.25, ...), custom_call_target="tpu_custom_call" | custom-call | flops 335544320 | bytes 4390912 | tf_op jit(solution)/shard_map/window/pallas_call | solution.py:342
  64.2 5.0 %all-to-all-done.1 = f32[32,1,1536]{2,1,0:T(1,128)S(1)} async-done(((f32[32,1,1536]{2,1,0:T(1,128)}), f32[32,1,1536]{2,1,0:T(1,128)S(1)}, u32[]{:S(2)}, u32[]{:S(2)}) %all-to-all-start.1) | async-done | bytes 196640 | tf_op jit(solution)/shard_map/all_to_all | solution.py:198
  69.2 0.1 slice_reduce_fusion
  69.3 0.6 broadcast_multiply_fusion
  69.9 0.6 slice_multiply_fusion
  (1 shorter events, 0.0 us)
Async XLA Ops:
  1.8 9.5 %collective-permute-start = (bf16[32,2048]{1,0:T(8,128)(2,1)S(1)}, bf16[32,2048]{1,0:T(8,128)(2,1)S(1)}, u32[]{:S(2)}, u32[]{:S(2)}) collective-permute-start(bf16[32,2048]{1,0:T(8,128)(2,1)S(1)} %get-tuple-element.40), channel_id=1, source_target_pairs={{0,16},{8,24},{16,0},{24,8},{1,17},{9,25},{17,1},{25,9},{2,18},{10... | collective-permute-start | bytes 393224 | tf_op jit(solution)/shard_map/ppermute | solution.py:191
  4.8 6.5 %collective-permute-start.1 = (bf16[32,2048]{1,0:T(8,128)(2,1)S(1)}, bf16[32,2048]{1,0:T(8,128)(2,1)S(1)}, u32[]{:S(2)}, u32[]{:S(2)}) collective-permute-start(bf16[32,2048]{1,0:T(8,128)(2,1)S(1)} %get-tuple-element.42), channel_id=1, source_target_pairs={{0,8},{8,0},{16,24},{24,16},{1,9},{9,1},{17,25},{25,17},{2,10},{10... | collective-permute-start | bytes 393224 | tf_op jit(solution)/shard_map/ppermute | solution.py:191
  4.8 6.5 %collective-permute-start.2 = (bf16[32,2048]{1,0:T(8,128)(2,1)S(1)}, bf16[32,2048]{1,0:T(8,128)(2,1)S(1)}, u32[]{:S(2)}, u32[]{:S(2)}) collective-permute-start(bf16[32,2048]{1,0:T(8,128)(2,1)S(1)} %get-tuple-element.39), channel_id=1, source_target_pairs={{0,24},{8,16},{16,8},{24,0},{1,25},{9,17},{17,9},{25,1},{2,26},{10... | collective-permute-start | bytes 393224 | tf_op jit(solution)/shard_map/ppermute | solution.py:191
  15.9 5.3 %collective-permute-start.5 = (bf16[64,2560]{1,0:T(8,128)(2,1)S(1)}, bf16[64,2560]{1,0:T(8,128)(2,1)S(1)}, u32[]{:S(2)}, u32[]{:S(2)}) collective-permute-start(bf16[64,2560]{1,0:T(8,128)(2,1)S(1)} %get-tuple-element.26), channel_id=1, source_target_pairs={{0,8},{8,0},{16,24},{24,16},{1,9},{9,1},{17,25},{25,17},{2,10},{10... | collective-permute-start | bytes 983048 | tf_op jit(solution)/shard_map/ppermute | solution.py:191
  16.2 15.0 %copy-start.4 = (s32[1,32]{1,0:T(1,128)S(1)}, s32[1,32]{1,0:T(1,128)}, u32[]{:S(2)}) copy-start(s32[1,32]{1,0:T(1,128)} %targets_ref.1) | copy-start | bytes 388
  16.3 22.2 %copy-start.6 = (f32[1280]{0:T(1024)S(1)}, f32[1280]{0:T(1024)}, u32[]{:S(2)}) copy-start(f32[1280]{0:T(1024)} %param.12) | copy-start | bytes 15364
  16.3 39.6 %copy-start = (bf16[1,128,1280]{2,1,0:T(8,128)(2,1)S(1)}, bf16[1,128,1280]{2,1,0:T(8,128)(2,1)}, u32[]{:S(2)}) copy-start(bf16[1,128,1280]{2,1,0:T(8,128)(2,1)} %param.11) | copy-start | bytes 983044
  16.3 44.4 %copy-start.1 = (bf16[1,128,1280]{2,1,0:T(8,128)(2,1)S(1)}, bf16[1,128,1280]{2,1,0:T(8,128)(2,1)}, u32[]{:S(2)}) copy-start(bf16[1,128,1280]{2,1,0:T(8,128)(2,1)} %param.14) | copy-start | bytes 983044
  16.3 44.4 %copy-start.2 = (bf16[1,128,1280]{2,1,0:T(8,128)(2,1)S(1)}, bf16[1,128,1280]{2,1,0:T(8,128)(2,1)}, u32[]{:S(2)}) copy-start(bf16[1,128,1280]{2,1,0:T(8,128)(2,1)} %param.15) | copy-start | bytes 983044
  16.3 44.4 %copy-start.5 = (s32[1,1,32]{2,1,0:T(1,128)S(1)}, s32[1,1,32]{2,1,0:T(1,128)}, u32[]{:S(2)}) copy-start(s32[1,1,32]{2,1,0:T(1,128)} %param.17) | copy-start | bytes 388
  16.3 45.5 %copy-start.3 = (bf16[1,128,1280]{2,1,0:T(8,128)(2,1)S(1)}, bf16[1,128,1280]{2,1,0:T(8,128)(2,1)}, u32[]{:S(2)}) copy-start(bf16[1,128,1280]{2,1,0:T(8,128)(2,1)} %param.16) | copy-start | bytes 983044
  20.9 2.3 %collective-permute-start.3 = (bf16[64,2560]{1,0:T(8,128)(2,1)S(1)}, bf16[64,2560]{1,0:T(8,128)(2,1)S(1)}, u32[]{:S(2)}, u32[]{:S(2)}) collective-permute-start(bf16[64,2560]{1,0:T(8,128)(2,1)S(1)} %get-tuple-element.22), channel_id=1, source_target_pairs={{0,8},{8,0},{16,24},{24,16},{1,9},{9,1},{17,25},{25,17},{2,10},{10... | collective-permute-start | bytes 983048 | tf_op jit(solution)/shard_map/ppermute | solution.py:191
  21.2 7.1 %collective-permute-start.6 = (bf16[32,2560]{1,0:T(8,128)(2,1)S(1)}, bf16[32,2560]{1,0:T(8,128)(2,1)S(1)}, u32[]{:S(2)}, u32[]{:S(2)}) collective-permute-start(bf16[32,2560]{1,0:T(8,128)(2,1)S(1)} %get-tuple-element.28), channel_id=1, source_target_pairs={{0,16},{8,24},{16,0},{24,8},{1,17},{9,25},{17,1},{25,9},{2,18},{10... | collective-permute-start | bytes 491528 | tf_op jit(solution)/shard_map/ppermute | solution.py:191
  23.3 7.9 %collective-permute-start.4 = (bf16[32,2560]{1,0:T(8,128)(2,1)S(1)}, bf16[32,2560]{1,0:T(8,128)(2,1)S(1)}, u32[]{:S(2)}, u32[]{:S(2)}) collective-permute-start(bf16[32,2560]{1,0:T(8,128)(2,1)S(1)} %get-tuple-element.24), channel_id=1, source_target_pairs={{0,16},{8,24},{16,0},{24,8},{1,17},{9,25},{17,1},{25,9},{2,18},{10... | collective-permute-start | bytes 491528 | tf_op jit(solution)/shard_map/ppermute | solution.py:191
  32.5 23.4 %all-to-all-start = ((bf16[8,8,5376]{2,1,0:T(8,128)(2,1)}), bf16[8,8,5376]{2,1,0:T(8,128)(2,1)S(1)}, u32[]{:S(2)}, u32[]{:S(2)}) async-start(bf16[8,8,5376]{2,1,0:T(8,128)(2,1)} %bitcast.5), calls=%async_computation | async-start | bytes 1376256 | tf_op jit(solution)/shard_map/all_to_all | solution.py:198
  57.0 12.3 %all-to-all-start.1 = ((f32[32,1,1536]{2,1,0:T(1,128)}), f32[32,1,1536]{2,1,0:T(1,128)S(1)}, u32[]{:S(2)}, u32[]{:S(2)}) async-start(f32[32,1,1536]{2,1,0:T(1,128)} %get-tuple-element.36), calls=%async_computation.1 | async-start | bytes 393216 | tf_op jit(solution)/shard_map/all_to_all | solution.py:198

commit v9 on v7

--- a/solution.py
+++ b/solution.py
@@ -50,10 +50,10 @@
 
 def project_kernel(blocks, first, tile, with_sum, *refs):
     x_refs, w_ref = refs[:blocks], refs[blocks]
-    keep_ref, send_ref = refs[blocks + 1 : blocks + 3]
+    keep_ref, send_ref = refs[blocks + 2 : blocks + 4]
     x = jnp.concatenate([ref[...] for ref in x_refs], axis=0)
     if with_sum:
-        refs[blocks + 3][...] = dot(jnp.ones((16, x.shape[0]), BF16), x, (1, 0))[:1]
+        refs[blocks + 4][...] = dot(jnp.ones((16, x.shape[0]), BF16), x, (1, 0))[:1]
     x = x.T
     half = keep_ref.shape[0]
     for t in range(0, keep_ref.shape[1], tile):
@@ -62,7 +62,7 @@
         send_ref[:, t : t + tile] = product[half:]
 
 
-def project(x_blocks, w_down, first, width, with_sum):
+def project(x_blocks, w_down, touched, first, width, with_sum):
     blocks, (rows, depth) = len(x_blocks), x_blocks[0].shape
     tile = 512
     while width % tile:
@@ -73,7 +73,7 @@
     return pl.pallas_call(
         functools.partial(project_kernel, blocks, first, tile, with_sum),
         out_shape=out_shape,
-        in_specs=vmem(blocks + 1),
+        in_specs=vmem(blocks + 1) + [pl.BlockSpec(memory_space=pl.ANY)],
         out_specs=vmem(len(out_shape)),
         compiler_params=pltpu.CompilerParams(vmem_limit_bytes=VMEM_BYTES),
         cost_estimate=pl.CostEstimate(
@@ -82,22 +82,25 @@
             transcendentals=0,
         ),
         name="project",
-    )(*x_blocks, pltpu.with_memory_space_constraint(w_down, pltpu.VMEM))
-
-
-def hold_kernel(w_ref, out_ref):
-    del w_ref, out_ref
-
-
-def hold(w_down):
-    return pl.pallas_call(
-        hold_kernel,
-        out_shape=jax.ShapeDtypeStruct(w_down.shape, w_down.dtype),
-        in_specs=[pl.BlockSpec(memory_space=pl.ANY)],
-        out_specs=pl.BlockSpec(memory_space=pl.ANY),
-        input_output_aliases={0: 0},
-        name="hold",
-    )(w_down)
+    )(*x_blocks, pltpu.with_memory_space_constraint(w_down, pltpu.VMEM), touched)
+
+
+def touch_kernel(w_ref, out_ref):
+    out_ref[...] = w_ref[: out_ref.shape[0], : out_ref.shape[1]]
+
+
+def touch(w_down):
+    return pl.pallas_call(
+        touch_kernel,
+        out_shape=jax.ShapeDtypeStruct((16, LANES), w_down.dtype),
+        in_specs=vmem(1),
+        out_specs=pl.BlockSpec(memory_space=pltpu.VMEM),
+        compiler_params=pltpu.CompilerParams(vmem_limit_bytes=VMEM_BYTES),
+        cost_estimate=pl.CostEstimate(
+            flops=0, bytes_accessed=2 * w_down.size, transcendentals=0
+        ),
+        name="touch",
+    )(pltpu.with_memory_space_constraint(w_down, pltpu.VMEM))
 
 
 def halve_kernel(kept_ref, got_ref, keep_ref, send_ref):
@@ -124,8 +127,8 @@
     )(kept, got)
 
 
-def pack_kernel(peers, capacity, chunks, carries, targets_ref, *refs):
-    terms, out_ref = refs[: 2 * chunks], refs[-1]
+def pack_kernel(peers, capacity, at, first, carries, targets_ref, kept_ref, got_ref, *refs):
+    out_ref = refs[-1]
     targets = targets_ref[...]
     rows = targets.shape[1]
     dest = targets // rows
@@ -139,17 +142,18 @@
     slot = iota((slots, rows), 0)
     chosen = jnp.logical_and(dest == slot // capacity, rank == slot % capacity)
     selector = chosen.astype(F32).astype(BF16)
-    at = 0
-    for chunk in range(chunks):
-        kept, got = terms[2 * chunk], terms[2 * chunk + 1]
-        total = (kept[...].astype(F32) + got[...].astype(F32)).astype(BF16)
-        width = total.shape[1]
-        out_ref[:, at : at + width] = dot(selector, total, (1, 0)).astype(BF16)
-        at += width
+    total = (kept_ref[...].astype(F32) + got_ref[...].astype(F32)).astype(BF16)
+    end = at + total.shape[1]
+    out_ref[:, at:end] = dot(selector, total, (1, 0)).astype(BF16)
+    if not first:
+        out_ref[:, :at] = refs[0][:, :at]
+        out_ref[:, end:] = refs[0][:, end:]
+        return
+    wide = out_ref.shape[1] - (2 * LANES if carries else LANES)
     label = jnp.sum(jnp.where(chosen, local + 1, 0), axis=1, keepdims=True) - 1
-    out_ref[:, at : at + LANES] = jnp.broadcast_to(label.astype(F32), (slots, LANES)).astype(BF16)
+    out_ref[:, wide : wide + LANES] = jnp.broadcast_to(label.astype(F32), (slots, LANES)).astype(BF16)
     if carries:
-        sums = refs[2 * chunks][...]
+        sums = refs[0][...]
         high = sums.astype(BF16).astype(F32)
         middle = (sums - high).astype(BF16).astype(F32)
         low = (sums - high - middle).astype(BF16).astype(F32)
@@ -162,16 +166,18 @@
                     start = (peer * pieces + piece) * LANES
                     line = jnp.broadcast_to(values[:, start : start + LANES], (slots, LANES))
                     extra = jnp.where(row == peer * capacity + level * pieces + piece, line, extra)
-        out_ref[:, at + LANES : at + 2 * LANES] = extra.astype(BF16)
-
-
-def pack(terms, targets, sums, peers, capacity, carries):
-    rows = targets.shape[1]
-    width = sum(kept.shape[1] for kept, _ in terms) + (2 * LANES if carries else LANES)
-    operands = [targets] + [x for pair in terms for x in pair] + ([sums] if carries else [])
-    return pl.pallas_call(
-        functools.partial(pack_kernel, peers, capacity, len(terms), carries),
-        out_shape=jax.ShapeDtypeStruct((peers * capacity, width), BF16),
+        out_ref[:, wide + LANES :] = extra.astype(BF16)
+
+
+def pack(packed, kept, got, targets, sums, peers, capacity, at, wide, carries):
+    rows, width = kept.shape
+    first = packed is None
+    operands = [targets, kept, got] + ([sums] if first and carries else [])
+    if not first:
+        operands.append(packed)
+    return pl.pallas_call(
+        functools.partial(pack_kernel, peers, capacity, at, first, carries),
+        out_shape=jax.ShapeDtypeStruct((peers * capacity, wide), BF16),
         in_specs=vmem(len(operands)),
         out_specs=pl.BlockSpec(memory_space=pltpu.VMEM),
         compiler_params=pltpu.CompilerParams(vmem_limit_bytes=VMEM_BYTES),
@@ -375,24 +381,28 @@
     x_blocks = [x_blocks[j] for j in order]
     probs, probs_t = window_probs(queries[0], keys[0], window_ids[0])
 
-    w_down = hold(w_down)
-    terms, first = [], 0
+    touched = touch(w_down)
+    wide = w_down.shape[0] + (2 * LANES if carries else LANES)
+    packed, first = None, 0
     for index, count in enumerate(CHUNKS):
-        kept, sent, *sums = project(x_blocks, w_down, first, count * width, index == 0)
-        first += count * width
+        kept, sent, *sums = project(x_blocks, w_down, touched, first, count * width, index == 0)
+        at, first = first, first + count * width
         if index == 0:
             bias_part = sums[0]
         mask = 1
         while 2 * mask < images:
             kept, sent = halve(kept, swap(sent, "img", mask))
             mask *= 2
-        terms.append((kept, swap(sent, "img", mask)))
-    packed = pack(terms, token_target, bias_part, peers, capacity, carries)
+        got = swap(sent, "img", mask)
+        packed = pack(
+            packed, kept, got, token_target, bias_part, peers, capacity, at, wide, carries
+        )
     routed = exchange(packed, "seq", peers)
 
-    share = (devices, 1, width + pieces * LANES) if carries else (1, 1, width)
+    share = (1, 1, width + pieces * LANES if carries else width)
     out_grads, shared = norm_backward(routed, peers, patches[0], gain[None], share)
     if carries:
+        shared = jnp.broadcast_to(shared, (devices,) + shared.shape[1:])
         shared = exchange(shared, ("img", "seq"), devices)
         gain_total = jnp.sum(shared[:, 0, :width], axis=0)
         bias_total = shared[:, 0, width:].reshape(-1)

time: 91.1 us -> 68.5 us (0.75)
  local copies, waits for them, and re-layouts: 24.6 us -> 8.92 us
  waiting for transfers between devices: 35.3 us -> 28.8 us
    unnamed x19 -> x16, local copies, waits for them, and re-layouts: 24.6 us -> 7.01 us
    ppermute x7, waiting for transfers between devices: 12.4 us -> 6.41 us  [swap(): return lax.ppermute(x, axis, [(i, i ^ mask) for i in range(n)])]
    dynamic_slice x1, local copies, waits for them, and re-layouts: 0.04 us -> 1.14 us  [columns(): return lax.dynamic_slice(grad_rows, (0, (image ^ j) * block), (rows, block))]
  transfers between devices with their start and end apart: 9 -> 9, of which waited for: 6 -> 4; matrix products, arithmetic and copies ran while one was open for 0% -> 0% of each run, Pallas kernels for 7% -> 10%
where the time goes in v9:
time: 68.5 us; the launch traced here: 68.2 us
  waiting for transfers between devices  28.8 us (42%)
  starting transfers between devices  16.7 us (24%)
  Pallas kernels  11.6 us (17%)
  local copies, waits for them, and re-layouts  8.92 us (13%)
  other arithmetic  1.35 us (2%)
  between operations  0.83 us (1%)
    all_to_all x2, waiting for transfers between devices, exchange(): lax.all_to_all(x, axis, split_axis=0, concat_axis=0, tiled=True)  22.4 us
    all_to_all x2, starting transfers between devices, exchange(): lax.all_to_all(x, axis, split_axis=0, concat_axis=0, tiled=True)  9.61 us
    ppermute x7, starting transfers between devices, swap(): return lax.ppermute(x, axis, [(i, i ^ mask) for i in range(n)])  7.07 us
    unnamed x16, local copies, waits for them, and re-layouts  7.01 us
    ppermute x7, waiting for transfers between devices, swap(): return lax.ppermute(x, axis, [(i, i ^ mask) for i in range(n)])  6.41 us
    pallas_call x2, Pallas kernels, project(): pl.pallas_call(functools.partial(project_kernel, blocks, first, tile, wit...  6.01 us
    pallas_call x1, Pallas kernels, window_backward(): pl.pallas_call(window_kernel, out_shape=[shape] * 3, in_specs=vmem(6), ou...  2.38 us
    pallas_call x2, Pallas kernels, pack(): pl.pallas_call(functools.partial(pack_kernel, peers, capacity, at, first,...  1.53 us
  transfers between devices with their start and end apart: 9, of which 4 were waited for; matrix products, arithmetic and copies ran while one was open for 0% of the time, Pallas kernels for 10%

profile of v9, /device:TPU:0, one launch (start us, length us, event | category | flops | bytes accessed | tf_op | source)
XLA Modules:
  0.0 68.2 jit_solution(7743380866265789036)
XLA Ops:
  0.7 1.1 %dynamic-slice_bitcast_fusion = (bf16[32,2048]{1,0:T(8,128)(2,1)S(1)}, bf16[32,2048]{1,0:T(8,128)(2,1)S(1)}, bf16[32,2048]{1,0:T(8,128)(2,1)S(1)}, bf16[32,2048]{1,0:T(8,128)(2,1)S(1)}) fusion(bf16[1,32,8192]{2,1,0:T(8,128)(2,1)} %param.9, s32[]{:T(128)S(6)} %select_n.15, s32[]{:T(128)S(6)} %select_n.13, s32[]{:T(128)S(6)} %select_n.12, s32[]{:T(128)S(6)} %select_n.14), kind=kLoop, calls=%fused_computation.1 | loop fusion | bytes 1048592 | tf_op jit(solution)/shard_map/dynamic_slice | solution.py:378
  1.8 3.0 %collective-permute-start = (bf16[32,2048]{1,0:T(8,128)(2,1)S(1)}, bf16[32,2048]{1,0:T(8,128)(2,1)S(1)}, u32[]{:S(2)}, u32[]{:S(2)}) collective-permute-start(bf16[32,2048]{1,0:T(8,128)(2,1)S(1)} %get-tuple-element.38), channel_id=1, source_target_pairs={{0,16},{8,24},{16,0},{24,8},{1,17},{9,25},{17,1},{25,9},{2,18},{10... | collective-permute-start | bytes 393224 | tf_op jit(solution)/shard_map/ppermute | solution.py:195
  4.8 0.0 collective-permute-start.1
  4.8 0.2 collective-permute-start.2
  5.0 0.0 copy-start
  5.0 7.0 %copy-done = bf16[5120,2048]{1,0:T(8,128)(2,1)S(1)} copy-done((bf16[5120,2048]{1,0:T(8,128)(2,1)S(1)}, bf16[5120,2048]{1,0:T(8,128)(2,1)}, u32[]{:S(2)}) %copy-start) | copy-done | bytes 20971544
  12.0 0.0 collective-permute-done.refs_1_
  12.0 0.0 collective-permute-done.1.refs_2_
  12.0 0.0 collective-permute-done.2.refs_3_
  12.0 0.0 copy-start.5
  12.0 0.0 copy-start.7
  12.0 0.0 copy-start.1
  12.1 0.0 copy-start.2
  12.1 0.0 copy-start.3
  12.1 0.0 copy-start.6
  12.1 0.0 copy-start.4
  12.1 3.0 %project.3 = (bf16[64,2560]{1,0:T(8,128)(2,1)S(1)}, bf16[64,2560]{1,0:T(8,128)(2,1)S(1)}, f32[1,2048]{1,0:T(1,128)S(1)}) custom-call(bf16[32,2048]{1,0:T(8,128)(2,1)S(1)} %get-tuple-element.39.refs_0_, bf16[32,2048]{1,0:T(8,128)(2,1)S(1)} %collective-permute-done.refs_1_, bf16[32,2048]{1,0:T(8,128)(2,1)S(1)} %collective-permute-done.1.refs_2_, ...), custom_call_target="tpu_custom_call" | custom-call | flops 1342177280 | bytes 10485760 | tf_op jit(solution)/shard_map/project/pallas_call | solution.py:73
  15.2 0.4 collective-permute-start.5
  15.5 3.0 %project.2 = (bf16[64,2560]{1,0:T(8,128)(2,1)S(1)}, bf16[64,2560]{1,0:T(8,128)(2,1)S(1)}) custom-call(bf16[32,2048]{1,0:T(8,128)(2,1)S(1)} %get-tuple-element.39.refs_0_, bf16[32,2048]{1,0:T(8,128)(2,1)S(1)} %collective-permute-done.refs_1_, bf16[32,2048]{1,0:T(8,128)(2,1)S(1)} %collective-permute-done.1.refs_2_, ...), custom_call_target="tpu_custom_call" | custom-call | flops 1342177280 | bytes 10485760 | tf_op jit(solution)/shard_map/project/pallas_call | solution.py:73
  18.5 0.2 collective-permute-start.3
  18.8 0.0 collective-permute-done.5.got_ref
  18.8 0.1 halve.3
  18.8 2.0 %collective-permute-start.6 = (bf16[32,2560]{1,0:T(8,128)(2,1)S(1)}, bf16[32,2560]{1,0:T(8,128)(2,1)S(1)}, u32[]{:S(2)}, u32[]{:S(2)}) collective-permute-start(bf16[32,2560]{1,0:T(8,128)(2,1)S(1)} %get-tuple-element.28), channel_id=1, source_target_pairs={{0,16},{8,24},{16,0},{24,8},{1,17},{9,25},{17,1},{25,9},{2,18},{10... | collective-permute-start | bytes 491528 | tf_op jit(solution)/shard_map/ppermute | solution.py:195
  20.9 0.0 collective-permute-done.3.got_ref
  20.9 0.1 halve.2
  20.9 1.2 %collective-permute-start.4 = (bf16[32,2560]{1,0:T(8,128)(2,1)S(1)}, bf16[32,2560]{1,0:T(8,128)(2,1)S(1)}, u32[]{:S(2)}, u32[]{:S(2)}) collective-permute-start(bf16[32,2560]{1,0:T(8,128)(2,1)S(1)} %get-tuple-element.24), channel_id=1, source_target_pairs={{0,16},{8,24},{16,0},{24,8},{1,17},{9,25},{17,1},{25,9},{2,18},{10... | collective-permute-start | bytes 491528 | tf_op jit(solution)/shard_map/ppermute | solution.py:195
  22.1 3.8 %collective-permute-done.6.got_ref = bf16[32,2560]{1,0:T(8,128)(2,1)S(1)} collective-permute-done((bf16[32,2560]{1,0:T(8,128)(2,1)S(1)}, bf16[32,2560]{1,0:T(8,128)(2,1)S(1)}, u32[]{:S(2)}, u32[]{:S(2)}) %collective-permute-start.6) | collective-permute-done | bytes 163872 | tf_op jit(solution)/shard_map/ppermute | solution.py:195
  25.9 0.0 copy-done.5
  25.9 0.3 pack.2.refs_0_
  26.3 2.6 %collective-permute-done.4.got_ref = bf16[32,2560]{1,0:T(8,128)(2,1)S(1)} collective-permute-done((bf16[32,2560]{1,0:T(8,128)(2,1)S(1)}, bf16[32,2560]{1,0:T(8,128)(2,1)S(1)}, u32[]{:S(2)}, u32[]{:S(2)}) %collective-permute-start.4) | collective-permute-done | bytes 163872 | tf_op jit(solution)/shard_map/ppermute | solution.py:195
  28.9 1.2 %pack.3 = bf16[64,5376]{1,0:T(8,128)(2,1)} custom-call(s32[1,32]{1,0:T(1,128)S(1)} %copy-done.5, f32[32,2560]{1,0:T(8,128)S(1)} %get-tuple-element.23.kept_ref, bf16[32,2560]{1,0:T(8,128)(2,1)S(1)} %collective-permute-done.4.got_ref, bf16[64,5376]{1,0:T(8,128)(2,1)S(1)} %pack.2.refs_0_), custom_call_target="tpu_custom_call" | custom-call | flops 10485760 | bytes 819200 | tf_op jit(solution)/shard_map/pack/pallas_call | solution.py:178
  30.1 5.9 %all-to-all-start = ((bf16[8,8,5376]{2,1,0:T(8,128)(2,1)}), bf16[8,8,5376]{2,1,0:T(8,128)(2,1)S(1)}, u32[]{:S(2)}, u32[]{:S(2)}) async-start(bf16[8,8,5376]{2,1,0:T(8,128)(2,1)} %bitcast.5), calls=%async_computation | async-start | bytes 1376256 | tf_op jit(solution)/shard_map/all_to_all | solution.py:202
  36.0 0.0 copy-done.7
  36.0 17.4 %all-to-all-done = bf16[8,8,5376]{2,1,0:T(8,128)(2,1)S(1)} async-done(((bf16[8,8,5376]{2,1,0:T(8,128)(2,1)}), bf16[8,8,5376]{2,1,0:T(8,128)(2,1)S(1)}, u32[]{:S(2)}, u32[]{:S(2)}) %all-to-all-start) | async-done | bytes 688160 | tf_op jit(solution)/shard_map/all_to_all | solution.py:202
  53.4 0.0 copy-done.1
  53.4 0.5 norm.1
  53.9 0.8 %broadcast_in_dim.24 = f32[32,1,1536]{2,1,0:T(1,128)} broadcast(f32[1536]{0:T(1024)S(1)} %reduce.1), dimensions={2} | broadcast | bytes 202752 | tf_op jit(solution)/shard_map/broadcast_in_dim | solution.py:405
  54.7 3.7 %all-to-all-start.1 = ((f32[32,1,1536]{2,1,0:T(1,128)}), f32[32,1,1536]{2,1,0:T(1,128)S(1)}, u32[]{:S(2)}, u32[]{:S(2)}) async-start(f32[32,1,1536]{2,1,0:T(1,128)} %broadcast_in_dim.24), calls=%async_computation.1 | async-start | bytes 393216 | tf_op jit(solution)/shard_map/all_to_all | solution.py:202
  58.4 0.0 copy-done.2
  58.4 0.0 copy-done.3
  58.4 0.0 copy-done.6
  58.4 1.1 %probs.1 = (f32[16,128,128]{2,1,0:T(8,128)S(1)}, f32[16,128,128]{2,1,0:T(8,128)S(1)}) custom-call(bf16[128,1280]{1,0:T(8,128)(2,1)S(1)} %bitcast.21, bf16[128,1280]{1,0:T(8,128)(2,1)S(1)} %bitcast.23, s32[1,32]{1,0:T(1,128)S(1)} %bitcast.26), custom_call_target="tpu_custom_call" | custom-call | flops 268435456 | bytes 2097152 | tf_op jit(solution)/shard_map/probs/pallas_call | solution.py:234
  59.5 0.0 copy-done.4
  59.5 2.4 %window.1 = (bf16[128,1280]{1,0:T(8,128)(2,1)}, bf16[128,1280]{1,0:T(8,128)(2,1)}, bf16[128,1280]{1,0:T(8,128)(2,1)}) custom-call(bf16[128,1280]{1,0:T(8,128)(2,1)S(1)} %get-tuple-element.30.g_ref, bf16[128,1280]{1,0:T(8,128)(2,1)S(1)} %bitcast.22, bf16[128,1280]{1,0:T(8,128)(2,1)S(1)} %bitcast.24, bf16[128,1280]{1,0:T(8,128)(2,1)S(1)} %bitcast.25, ...), custom_call_target="tpu_custom_call" | custom-call | flops 335544320 | bytes 4390912 | tf_op jit(solution)/shard_map/window/pallas_call | solution.py:346
  61.9 5.1 %all-to-all-done.1 = f32[32,1,1536]{2,1,0:T(1,128)S(1)} async-done(((f32[32,1,1536]{2,1,0:T(1,128)}), f32[32,1,1536]{2,1,0:T(1,128)S(1)}, u32[]{:S(2)}, u32[]{:S(2)}) %all-to-all-start.1) | async-done | bytes 196640 | tf_op jit(solution)/shard_map/all_to_all | solution.py:202
  66.9 0.1 slice_reduce_fusion
  67.0 0.6 broadcast_multiply_fusion
  67.6 0.6 slice_multiply_fusion
  (3 shorter events, 0.0 us)
Async XLA Ops:
  1.8 10.2 %collective-permute-start = (bf16[32,2048]{1,0:T(8,128)(2,1)S(1)}, bf16[32,2048]{1,0:T(8,128)(2,1)S(1)}, u32[]{:S(2)}, u32[]{:S(2)}) collective-permute-start(bf16[32,2048]{1,0:T(8,128)(2,1)S(1)} %get-tuple-element.38), channel_id=1, source_target_pairs={{0,16},{8,24},{16,0},{24,8},{1,17},{9,25},{17,1},{25,9},{2,18},{10... | collective-permute-start | bytes 393224 | tf_op jit(solution)/shard_map/ppermute | solution.py:195
  4.8 7.2 %collective-permute-start.1 = (bf16[32,2048]{1,0:T(8,128)(2,1)S(1)}, bf16[32,2048]{1,0:T(8,128)(2,1)S(1)}, u32[]{:S(2)}, u32[]{:S(2)}) collective-permute-start(bf16[32,2048]{1,0:T(8,128)(2,1)S(1)} %get-tuple-element.40), channel_id=1, source_target_pairs={{0,8},{8,0},{16,24},{24,16},{1,9},{9,1},{17,25},{25,17},{2,10},{10... | collective-permute-start | bytes 393224 | tf_op jit(solution)/shard_map/ppermute | solution.py:195
  4.8 7.2 %collective-permute-start.2 = (bf16[32,2048]{1,0:T(8,128)(2,1)S(1)}, bf16[32,2048]{1,0:T(8,128)(2,1)S(1)}, u32[]{:S(2)}, u32[]{:S(2)}) collective-permute-start(bf16[32,2048]{1,0:T(8,128)(2,1)S(1)} %get-tuple-element.37), channel_id=1, source_target_pairs={{0,24},{8,16},{16,8},{24,0},{1,25},{9,17},{17,9},{25,1},{2,26},{10... | collective-permute-start | bytes 393224 | tf_op jit(solution)/shard_map/ppermute | solution.py:195
  5.0 7.0 %copy-start = (bf16[5120,2048]{1,0:T(8,128)(2,1)S(1)}, bf16[5120,2048]{1,0:T(8,128)(2,1)}, u32[]{:S(2)}) copy-start(bf16[5120,2048]{1,0:T(8,128)(2,1)} %refs_4_.3) | copy-start | bytes 62914564
  12.0 13.9 %copy-start.5 = (s32[1,32]{1,0:T(1,128)S(1)}, s32[1,32]{1,0:T(1,128)}, u32[]{:S(2)}) copy-start(s32[1,32]{1,0:T(1,128)} %targets_ref.3) | copy-start | bytes 388
  12.0 23.9 %copy-start.7 = (f32[1280]{0:T(1024)S(1)}, f32[1280]{0:T(1024)}, u32[]{:S(2)}) copy-start(f32[1280]{0:T(1024)} %param.12) | copy-start | bytes 15364
  12.0 41.3 %copy-start.1 = (bf16[1,128,1280]{2,1,0:T(8,128)(2,1)S(1)}, bf16[1,128,1280]{2,1,0:T(8,128)(2,1)}, u32[]{:S(2)}) copy-start(bf16[1,128,1280]{2,1,0:T(8,128)(2,1)} %param.11) | copy-start | bytes 983044
  12.1 46.3 %copy-start.2 = (bf16[1,128,1280]{2,1,0:T(8,128)(2,1)S(1)}, bf16[1,128,1280]{2,1,0:T(8,128)(2,1)}, u32[]{:S(2)}) copy-start(bf16[1,128,1280]{2,1,0:T(8,128)(2,1)} %param.14) | copy-start | bytes 983044
  12.1 46.3 %copy-start.3 = (bf16[1,128,1280]{2,1,0:T(8,128)(2,1)S(1)}, bf16[1,128,1280]{2,1,0:T(8,128)(2,1)}, u32[]{:S(2)}) copy-start(bf16[1,128,1280]{2,1,0:T(8,128)(2,1)} %param.15) | copy-start | bytes 983044
  12.1 46.3 %copy-start.6 = (s32[1,1,32]{2,1,0:T(1,128)S(1)}, s32[1,1,32]{2,1,0:T(1,128)}, u32[]{:S(2)}) copy-start(s32[1,1,32]{2,1,0:T(1,128)} %param.17) | copy-start | bytes 388
  12.1 47.4 %copy-start.4 = (bf16[1,128,1280]{2,1,0:T(8,128)(2,1)S(1)}, bf16[1,128,1280]{2,1,0:T(8,128)(2,1)}, u32[]{:S(2)}) copy-start(bf16[1,128,1280]{2,1,0:T(8,128)(2,1)} %param.16) | copy-start | bytes 983044
  15.2 3.6 %collective-permute-start.5 = (bf16[64,2560]{1,0:T(8,128)(2,1)S(1)}, bf16[64,2560]{1,0:T(8,128)(2,1)S(1)}, u32[]{:S(2)}, u32[]{:S(2)}) collective-permute-start(bf16[64,2560]{1,0:T(8,128)(2,1)S(1)} %get-tuple-element.26), channel_id=1, source_target_pairs={{0,8},{8,0},{16,24},{24,16},{1,9},{9,1},{17,25},{25,17},{2,10},{10... | collective-permute-start | bytes 983048 | tf_op jit(solution)/shard_map/ppermute | solution.py:195
  18.5 2.3 %collective-permute-start.3 = (bf16[64,2560]{1,0:T(8,128)(2,1)S(1)}, bf16[64,2560]{1,0:T(8,128)(2,1)S(1)}, u32[]{:S(2)}, u32[]{:S(2)}) collective-permute-start(bf16[64,2560]{1,0:T(8,128)(2,1)S(1)} %get-tuple-element.22), channel_id=1, source_target_pairs={{0,8},{8,0},{16,24},{24,16},{1,9},{9,1},{17,25},{25,17},{2,10},{10... | collective-permute-start | bytes 983048 | tf_op jit(solution)/shard_map/ppermute | solution.py:195
  18.8 7.1 %collective-permute-start.6 = (bf16[32,2560]{1,0:T(8,128)(2,1)S(1)}, bf16[32,2560]{1,0:T(8,128)(2,1)S(1)}, u32[]{:S(2)}, u32[]{:S(2)}) collective-permute-start(bf16[32,2560]{1,0:T(8,128)(2,1)S(1)} %get-tuple-element.28), channel_id=1, source_target_pairs={{0,16},{8,24},{16,0},{24,8},{1,17},{9,25},{17,1},{25,9},{2,18},{10... | collective-permute-start | bytes 491528 | tf_op jit(solution)/shard_map/ppermute | solution.py:195
  20.9 7.9 %collective-permute-start.4 = (bf16[32,2560]{1,0:T(8,128)(2,1)S(1)}, bf16[32,2560]{1,0:T(8,128)(2,1)S(1)}, u32[]{:S(2)}, u32[]{:S(2)}) collective-permute-start(bf16[32,2560]{1,0:T(8,128)(2,1)S(1)} %get-tuple-element.24), channel_id=1, source_target_pairs={{0,16},{8,24},{16,0},{24,8},{1,17},{9,25},{17,1},{25,9},{2,18},{10... | collective-permute-start | bytes 491528 | tf_op jit(solution)/shard_map/ppermute | solution.py:195
  30.1 23.3 %all-to-all-start = ((bf16[8,8,5376]{2,1,0:T(8,128)(2,1)}), bf16[8,8,5376]{2,1,0:T(8,128)(2,1)S(1)}, u32[]{:S(2)}, u32[]{:S(2)}) async-start(bf16[8,8,5376]{2,1,0:T(8,128)(2,1)} %bitcast.5), calls=%async_computation | async-start | bytes 1376256 | tf_op jit(solution)/shard_map/all_to_all | solution.py:202
  54.7 12.2 %all-to-all-start.1 = ((f32[32,1,1536]{2,1,0:T(1,128)}), f32[32,1,1536]{2,1,0:T(1,128)S(1)}, u32[]{:S(2)}, u32[]{:S(2)}) async-start(f32[32,1,1536]{2,1,0:T(1,128)} %broadcast_in_dim.24), calls=%async_computation.1 | async-start | bytes 393216 | tf_op jit(solution)/shard_map/all_to_all | solution.py:202

commit v10 on v9

--- a/solution.py
+++ b/solution.py
@@ -12,6 +12,7 @@
 HEAD_DIM = 80
 LANES = 128
 CHUNKS = (2, 2)
+DIRECT = 8
 VMEM_BYTES = 16 * 1024 * 1024
 
 F32 = jnp.float32
@@ -127,8 +128,20 @@
     )(kept, got)
 
 
-def pack_kernel(peers, capacity, at, first, carries, targets_ref, kept_ref, got_ref, *refs):
-    out_ref = refs[-1]
+def peer_masks(peers):
+    return (0, 7, 2, 3, 1, 4, 6, 5) if peers == 8 else tuple(range(peers))
+
+
+def block_peer(block, peers, me):
+    peer = jnp.zeros_like(block)
+    for place, mask in enumerate(peer_masks(peers)):
+        peer = jnp.where(block == place, mask ^ me, peer)
+    return peer
+
+
+def pack_kernel(peers, capacity, chunks, direct, carries, me_ref, targets_ref, *refs):
+    terms, refs = refs[: 2 * chunks], refs[2 * chunks :]
+    outs = refs[1:] if carries else refs
     targets = targets_ref[...]
     rows = targets.shape[1]
     dest = targets // rows
@@ -140,46 +153,61 @@
     rank = jnp.sum(same_before.astype(jnp.int32), axis=0, keepdims=True)
     slots = peers * capacity
     slot = iota((slots, rows), 0)
-    chosen = jnp.logical_and(dest == slot // capacity, rank == slot % capacity)
+    holder = slot // capacity
+    if direct:
+        holder = block_peer(holder, peers, me_ref[0])
+    chosen = jnp.logical_and(dest == holder, rank == slot % capacity)
     selector = chosen.astype(F32).astype(BF16)
-    total = (kept_ref[...].astype(F32) + got_ref[...].astype(F32)).astype(BF16)
-    end = at + total.shape[1]
-    out_ref[:, at:end] = dot(selector, total, (1, 0)).astype(BF16)
-    if not first:
-        out_ref[:, :at] = refs[0][:, :at]
-        out_ref[:, end:] = refs[0][:, end:]
-        return
-    wide = out_ref.shape[1] - (2 * LANES if carries else LANES)
+    parts = []
+    for chunk in range(chunks):
+        kept, got = terms[2 * chunk : 2 * chunk + 2]
+        total = (kept[...].astype(F32) + got[...].astype(F32)).astype(BF16)
+        parts.append(dot(selector, total, (1, 0)))
     label = jnp.sum(jnp.where(chosen, local + 1, 0), axis=1, keepdims=True) - 1
-    out_ref[:, wide : wide + LANES] = jnp.broadcast_to(label.astype(F32), (slots, LANES)).astype(BF16)
+    parts.append(jnp.broadcast_to(label.astype(F32), (slots, LANES)))
     if carries:
         sums = refs[0][...]
         high = sums.astype(BF16).astype(F32)
         middle = (sums - high).astype(BF16).astype(F32)
         low = (sums - high - middle).astype(BF16).astype(F32)
         extra = jnp.zeros((slots, LANES), F32)
-        row = iota((slots, LANES), 0)
+        row = iota((slots, LANES), 0) % capacity
+        peer = iota((slots, LANES), 0) // capacity
+        if direct:
+            peer = block_peer(peer, peers, me_ref[0])
         pieces = sums.shape[1] // peers // LANES
-        for peer in range(peers):
+        for p in range(peers):
             for level, values in enumerate((high, middle, low)):
                 for piece in range(pieces):
-                    start = (peer * pieces + piece) * LANES
+                    start = (p * pieces + piece) * LANES
                     line = jnp.broadcast_to(values[:, start : start + LANES], (slots, LANES))
-                    extra = jnp.where(row == peer * capacity + level * pieces + piece, line, extra)
-        out_ref[:, wide + LANES :] = extra.astype(BF16)
-
-
-def pack(packed, kept, got, targets, sums, peers, capacity, at, wide, carries):
-    rows, width = kept.shape
-    first = packed is None
-    operands = [targets, kept, got] + ([sums] if first and carries else [])
-    if not first:
-        operands.append(packed)
-    return pl.pallas_call(
-        functools.partial(pack_kernel, peers, capacity, at, first, carries),
-        out_shape=jax.ShapeDtypeStruct((peers * capacity, wide), BF16),
-        in_specs=vmem(len(operands)),
-        out_specs=pl.BlockSpec(memory_space=pltpu.VMEM),
+                    here = jnp.logical_and(peer == p, row == level * pieces + piece)
+                    extra = jnp.where(here, line, extra)
+        parts.append(extra)
+    at = 0
+    for part in parts:
+        end = at + part.shape[1]
+        if direct:
+            for m in range(peers):
+                outs[m][:, at:end] = part[m * capacity : (m + 1) * capacity].astype(BF16)
+        else:
+            outs[0][:, at:end] = part.astype(BF16)
+        at = end
+
+
+def pack(terms, targets, me, sums, peers, capacity, direct, carries):
+    rows = targets.shape[1]
+    width = sum(kept.shape[1] for kept, _ in terms) + (2 * LANES if carries else LANES)
+    operands = [me, targets] + [x for pair in terms for x in pair] + ([sums] if carries else [])
+    if direct:
+        out_shape = [jax.ShapeDtypeStruct((capacity, width), BF16)] * peers
+    else:
+        out_shape = [jax.ShapeDtypeStruct((peers * capacity, width), BF16)]
+    return pl.pallas_call(
+        functools.partial(pack_kernel, peers, capacity, len(terms), direct, carries),
+        out_shape=out_shape,
+        in_specs=[pl.BlockSpec(memory_space=pltpu.SMEM)] + vmem(len(operands) - 1),
+        out_specs=vmem(len(out_shape)),
         compiler_params=pltpu.CompilerParams(vmem_limit_bytes=VMEM_BYTES),
         cost_estimate=pl.CostEstimate(
             flops=2 * rows * peers * capacity * width,
@@ -188,6 +216,13 @@
         ),
         name="pack",
     )(*operands)
+
+
+def route(packed, peers, direct):
+    if not direct:
+        return [exchange(packed[0], "seq", peers)]
+    masks = peer_masks(peers)
+    return [swap(block, "seq", mask) if mask else block for block, mask in zip(packed, masks)]
 
 
 def swap(x, axis, mask):
@@ -246,12 +281,15 @@
     )(queries, keys, ids)
 
 
-def norm_kernel(peers, carries, patches_ref, gain_ref, routed_ref, out_ref, share_ref):
+def norm_kernel(peers, carries, patches_ref, gain_ref, *refs):
+    pieces, (out_ref, share_ref) = refs[:-2], refs[-2:]
     patches, width = patches_ref.shape
-    slots = routed_ref.shape[0]
-    per_token = routed_ref.shape[1] // width
-    labels = routed_ref[:, per_token * width : per_token * width + LANES].astype(F32)[:, :1]
-    columns = [routed_ref[:, c * width : (c + 1) * width].astype(F32) for c in range(per_token)]
+    pieces = [ref[...].astype(F32) for ref in pieces]
+    routed = jnp.concatenate(pieces, axis=0) if len(pieces) > 1 else pieces[0]
+    slots = routed.shape[0]
+    per_token = routed.shape[1] // width
+    labels = routed[:, per_token * width : per_token * width + 1]
+    columns = [routed[:, c * width : (c + 1) * width] for c in range(per_token)]
     held = jnp.concatenate(columns, axis=0).astype(BF16)
     lanes = len(columns) * slots
     lane = iota((slots, lanes), 1)
@@ -268,7 +306,7 @@
     gain_part = jnp.sum(patch_grads * normed, axis=0, keepdims=True)
     share_ref[:, :, :width] = jnp.broadcast_to(gain_part[None], (share_ref.shape[0], 1, width))
     if carries:
-        carried = routed_ref[:, per_token * width + LANES :].astype(F32)
+        carried = routed[:, per_token * width + LANES :]
         capacity = slots // peers
         pieces = (share_ref.shape[2] - width) // LANES
         row = iota((slots, LANES), 0) % capacity
@@ -285,21 +323,22 @@
     ).astype(BF16)
 
 
-def norm_backward(routed, peers, patches, gain, share):
+def norm_backward(received, peers, patches, gain, share):
     count, width = patches.shape
+    routed = sum(x.size for x in received)
     return pl.pallas_call(
         functools.partial(norm_kernel, peers, share[2] > width),
         out_shape=[jax.ShapeDtypeStruct((count, width), BF16), jax.ShapeDtypeStruct(share, F32)],
-        in_specs=vmem(3),
+        in_specs=vmem(2 + len(received)),
         out_specs=vmem(2),
         compiler_params=pltpu.CompilerParams(vmem_limit_bytes=VMEM_BYTES),
         cost_estimate=pl.CostEstimate(
-            flops=2 * count * routed.size,
-            bytes_accessed=4 * count * width + 2 * routed.size,
+            flops=2 * count * routed,
+            bytes_accessed=4 * count * width + 2 * routed,
             transcendentals=0,
         ),
         name="norm",
-    )(patches, gain, routed)
+    )(patches, gain, *received)
 
 
 def window_kernel(g_ref, q_ref, k_ref, v_ref, probs_ref, probs_t_ref, dq_ref, dk_ref, dv_ref):
@@ -364,6 +403,7 @@
     images, peers = lax.axis_size("img"), lax.axis_size("seq")
     devices = images * peers
     capacity = max(1, 2 * rows // peers)
+    direct = peers <= DIRECT
     block = w_down.shape[1]
     width = patches.shape[2]
     pieces = block // peers // LANES
@@ -372,7 +412,7 @@
     order = [0]
     while len(order) < images:
         order = [2 * j for j in order] + [2 * j + 1 for j in order]
-    image = lax.axis_index("img")
+    image, me = lax.axis_index("img"), lax.axis_index("seq")
 
     def columns(j):
         return lax.dynamic_slice(grad_rows, (0, (image ^ j) * block), (rows, block))
@@ -382,22 +422,19 @@
     probs, probs_t = window_probs(queries[0], keys[0], window_ids[0])
 
     touched = touch(w_down)
-    wide = w_down.shape[0] + (2 * LANES if carries else LANES)
-    packed, first = None, 0
+    terms, first = [], 0
     for index, count in enumerate(CHUNKS):
         kept, sent, *sums = project(x_blocks, w_down, touched, first, count * width, index == 0)
-        at, first = first, first + count * width
+        first += count * width
         if index == 0:
             bias_part = sums[0]
         mask = 1
         while 2 * mask < images:
             kept, sent = halve(kept, swap(sent, "img", mask))
             mask *= 2
-        got = swap(sent, "img", mask)
-        packed = pack(
-            packed, kept, got, token_target, bias_part, peers, capacity, at, wide, carries
-        )
-    routed = exchange(packed, "seq", peers)
+        terms.append((kept, swap(sent, "img", mask)))
+    packed = pack(terms, token_target, me.reshape(1), bias_part, peers, capacity, direct, carries)
+    routed = route(packed, peers, direct)
 
     share = (1, 1, width + pieces * LANES if carries else width)
     out_grads, shared = norm_backward(routed, peers, patches[0], gain[None], share)

time: 68.5 us -> 65.4 us (0.955)
  waiting for transfers between devices: 28.8 us -> 19.5 us
  starting transfers between devices: 16.7 us -> 23.9 us
  Pallas kernels: 11.6 us -> 10.6 us
    all_to_all x2 -> x1, waiting for transfers between devices: 22.4 us -> 5.06 us  [exchange(): lax.all_to_all(x, axis, split_axis=0, concat_axis=0, tiled=True)]
    ppermute x7 -> x14, starting transfers between devices: 7.07 us -> 18 us  [swap(): return lax.ppermute(x, axis, [(i, i ^ mask) for i in range(n)])]
    ppermute x7 -> x14, waiting for transfers between devices: 6.41 us -> 14.4 us  [swap(): return lax.ppermute(x, axis, [(i, i ^ mask) for i in range(n)])]
    all_to_all x2 -> x1, starting transfers between devices: 9.61 us -> 5.94 us  [exchange(): lax.all_to_all(x, axis, split_axis=0, concat_axis=0, tiled=True)]
    pallas_call x2 -> x1, Pallas kernels: 1.53 us -> 0.5 us  [pack(): pl.pallas_call(functools.partial(pack_kernel, peers, capacity, len(terms)...]
  transfers between devices with their start and end apart: 9 -> 15, of which waited for: 4 -> 6; matrix products, arithmetic and copies ran while one was open for 0% -> 0% of each run, Pallas kernels for 10% -> 10%
where the time goes in v10:
time: 65.4 us; the launch traced here: 65.1 us
  starting transfers between devices  23.9 us (37%)
  waiting for transfers between devices  19.5 us (30%)
  Pallas kernels  10.6 us (16%)
  local copies, waits for them, and re-layouts  8.93 us (14%)
  other arithmetic  1.35 us (2%)
  between operations  0.83 us (1%)
    ppermute x14, starting transfers between devices, swap(): return lax.ppermute(x, axis, [(i, i ^ mask) for i in range(n)])  18 us
    ppermute x14, waiting for transfers between devices, swap(): return lax.ppermute(x, axis, [(i, i ^ mask) for i in range(n)])  14.4 us
    unnamed x16, local copies, waits for them, and re-layouts  7.01 us
    pallas_call x2, Pallas kernels, project(): pl.pallas_call(functools.partial(project_kernel, blocks, first, tile, wit...  6.02 us
    all_to_all x1, starting transfers between devices, exchange(): lax.all_to_all(x, axis, split_axis=0, concat_axis=0, tiled=True)  5.94 us
    all_to_all x1, waiting for transfers between devices, exchange(): lax.all_to_all(x, axis, split_axis=0, concat_axis=0, tiled=True)  5.06 us
    pallas_call x1, Pallas kernels, window_backward(): pl.pallas_call(window_kernel, out_shape=[shape] * 3, in_specs=vmem(6), ou...  2.38 us
  transfers between devices with their start and end apart: 15, of which 6 were waited for; matrix products, arithmetic and copies ran while one was open for 0% of the time, Pallas kernels for 10%

profile of v10, /device:TPU:0, one launch (start us, length us, event | category | flops | bytes accessed | tf_op | source)
XLA Modules:
  0.0 65.1 jit_solution(15556987279722344265)
XLA Ops:
  0.7 1.1 %dynamic-slice_bitcast_fusion = (bf16[32,2048]{1,0:T(8,128)(2,1)S(1)}, bf16[32,2048]{1,0:T(8,128)(2,1)S(1)}, bf16[32,2048]{1,0:T(8,128)(2,1)S(1)}, bf16[32,2048]{1,0:T(8,128)(2,1)S(1)}) fusion(bf16[1,32,8192]{2,1,0:T(8,128)(2,1)} %param.9, s32[]{:T(128)S(6)} %select_n.15, s32[]{:T(128)S(6)} %select_n.13, s32[]{:T(128)S(6)} %select_n.12, s32[]{:T(128)S(6)} %select_n.14), kind=kLoop, calls=%fused_computation.1 | loop fusion | bytes 1048592 | tf_op jit(solution)/shard_map/dynamic_slice | solution.py:418
  1.8 3.0 %collective-permute-start = (bf16[32,2048]{1,0:T(8,128)(2,1)S(1)}, bf16[32,2048]{1,0:T(8,128)(2,1)S(1)}, u32[]{:S(2)}, u32[]{:S(2)}) collective-permute-start(bf16[32,2048]{1,0:T(8,128)(2,1)S(1)} %get-tuple-element.54), channel_id=1, source_target_pairs={{0,16},{8,24},{16,0},{24,8},{1,17},{9,25},{17,1},{25,9},{2,18},{10... | collective-permute-start | bytes 393224 | tf_op jit(solution)/shard_map/ppermute | solution.py:230
  4.8 0.0 collective-permute-start.1
  4.8 0.2 collective-permute-start.2
  5.0 0.0 copy-start
  5.0 7.0 %copy-done = bf16[5120,2048]{1,0:T(8,128)(2,1)S(1)} copy-done((bf16[5120,2048]{1,0:T(8,128)(2,1)S(1)}, bf16[5120,2048]{1,0:T(8,128)(2,1)}, u32[]{:S(2)}) %copy-start) | copy-done | bytes 20971544
  12.0 0.0 collective-permute-done.refs_1_
  12.0 0.0 collective-permute-done.1.refs_2_
  12.0 0.0 collective-permute-done.2.refs_3_
  12.0 0.0 copy-start.5
  12.0 0.0 copy-start.7
  12.0 0.0 copy-start.1
  12.1 0.0 copy-start.2
  12.1 0.0 copy-start.3
  12.1 0.0 copy-start.6
  12.1 0.0 copy-start.4
  12.1 3.0 %project.3 = (bf16[64,2560]{1,0:T(8,128)(2,1)S(1)}, bf16[64,2560]{1,0:T(8,128)(2,1)S(1)}) custom-call(bf16[32,2048]{1,0:T(8,128)(2,1)S(1)} %get-tuple-element.55.refs_0_, bf16[32,2048]{1,0:T(8,128)(2,1)S(1)} %collective-permute-done.refs_1_, bf16[32,2048]{1,0:T(8,128)(2,1)S(1)} %collective-permute-done.1.refs_2_, ...), custom_call_target="tpu_custom_call" | custom-call | flops 1342177280 | bytes 10485760 | tf_op jit(solution)/shard_map/project/pallas_call | solution.py:74
  15.1 0.4 collective-permute-start.5
  15.5 3.0 %project.2 = (bf16[64,2560]{1,0:T(8,128)(2,1)S(1)}, bf16[64,2560]{1,0:T(8,128)(2,1)S(1)}, f32[1,2048]{1,0:T(1,128)S(1)}) custom-call(bf16[32,2048]{1,0:T(8,128)(2,1)S(1)} %get-tuple-element.55.refs_0_, bf16[32,2048]{1,0:T(8,128)(2,1)S(1)} %collective-permute-done.refs_1_, bf16[32,2048]{1,0:T(8,128)(2,1)S(1)} %collective-permute-done.1.refs_2_, ...), custom_call_target="tpu_custom_call" | custom-call | flops 1342177280 | bytes 10485760 | tf_op jit(solution)/shard_map/project/pallas_call | solution.py:74
  18.5 0.3 collective-permute-start.3
  18.8 0.0 collective-permute-done.5.got_ref
  18.8 0.1 halve.3
  18.9 2.0 %collective-permute-start.6 = (bf16[32,2560]{1,0:T(8,128)(2,1)S(1)}, bf16[32,2560]{1,0:T(8,128)(2,1)S(1)}, u32[]{:S(2)}, u32[]{:S(2)}) collective-permute-start(bf16[32,2560]{1,0:T(8,128)(2,1)S(1)} %get-tuple-element.36), channel_id=1, source_target_pairs={{0,16},{8,24},{16,0},{24,8},{1,17},{9,25},{17,1},{25,9},{2,18},{10... | collective-permute-start | bytes 491528 | tf_op jit(solution)/shard_map/ppermute | solution.py:230
  20.9 0.0 collective-permute-done.3.got_ref
  20.9 0.1 halve.2
  21.0 1.2 %collective-permute-start.4 = (bf16[32,2560]{1,0:T(8,128)(2,1)S(1)}, bf16[32,2560]{1,0:T(8,128)(2,1)S(1)}, u32[]{:S(2)}, u32[]{:S(2)}) collective-permute-start(bf16[32,2560]{1,0:T(8,128)(2,1)S(1)} %get-tuple-element.32), channel_id=1, source_target_pairs={{0,16},{8,24},{16,0},{24,8},{1,17},{9,25},{17,1},{25,9},{2,18},{10... | collective-permute-start | bytes 491528 | tf_op jit(solution)/shard_map/ppermute | solution.py:230
  22.1 3.8 %collective-permute-done.6.refs_3_ = bf16[32,2560]{1,0:T(8,128)(2,1)S(1)} collective-permute-done((bf16[32,2560]{1,0:T(8,128)(2,1)S(1)}, bf16[32,2560]{1,0:T(8,128)(2,1)S(1)}, u32[]{:S(2)}, u32[]{:S(2)}) %collective-permute-start.6) | collective-permute-done | bytes 163872 | tf_op jit(solution)/shard_map/ppermute | solution.py:230
  25.9 2.9 %collective-permute-done.4.refs_1_ = bf16[32,2560]{1,0:T(8,128)(2,1)S(1)} collective-permute-done((bf16[32,2560]{1,0:T(8,128)(2,1)S(1)}, bf16[32,2560]{1,0:T(8,128)(2,1)S(1)}, u32[]{:S(2)}, u32[]{:S(2)}) %collective-permute-start.4) | collective-permute-done | bytes 163872 | tf_op jit(solution)/shard_map/ppermute | solution.py:230
  28.8 0.0 copy-done.5
  28.8 0.5 pack.1
  29.4 1.7 %collective-permute-start.10 = (bf16[8,5376]{1,0:T(8,128)(2,1)S(1)}, bf16[8,5376]{1,0:T(8,128)(2,1)S(1)}, u32[]{:S(2)}, u32[]{:S(2)}) collective-permute-start(bf16[8,5376]{1,0:T(8,128)(2,1)S(1)} %get-tuple-element.42), channel_id=1, source_target_pairs={{0,1},{1,0},{2,3},{3,2},{4,5},{5,4},{6,7},{7,6},{8,9},{9,8},{10,11... | collective-permute-start | bytes 258056 | tf_op jit(solution)/shard_map/ppermute | solution.py:230
  31.1 2.6 %collective-permute-start.11 = (bf16[8,5376]{1,0:T(8,128)(2,1)S(1)}, bf16[8,5376]{1,0:T(8,128)(2,1)S(1)}, u32[]{:S(2)}, u32[]{:S(2)}) collective-permute-start(bf16[8,5376]{1,0:T(8,128)(2,1)S(1)} %get-tuple-element.43), channel_id=1, source_target_pairs={{0,4},{1,5},{2,6},{3,7},{4,0},{5,1},{6,2},{7,3},{8,12},{9,13},{10,... | collective-permute-start | bytes 258056 | tf_op jit(solution)/shard_map/ppermute | solution.py:230
  33.7 1.3 %collective-permute-start.12 = (bf16[8,5376]{1,0:T(8,128)(2,1)S(1)}, bf16[8,5376]{1,0:T(8,128)(2,1)S(1)}, u32[]{:S(2)}, u32[]{:S(2)}) collective-permute-start(bf16[8,5376]{1,0:T(8,128)(2,1)S(1)} %get-tuple-element.44), channel_id=1, source_target_pairs={{0,6},{1,7},{2,4},{3,5},{4,2},{5,3},{6,0},{7,1},{8,14},{9,15},{10,... | collective-permute-start | bytes 258056 | tf_op jit(solution)/shard_map/ppermute | solution.py:230
  35.0 1.7 %collective-permute-start.13 = (bf16[8,5376]{1,0:T(8,128)(2,1)S(1)}, bf16[8,5376]{1,0:T(8,128)(2,1)S(1)}, u32[]{:S(2)}, u32[]{:S(2)}) collective-permute-start(bf16[8,5376]{1,0:T(8,128)(2,1)S(1)} %get-tuple-element.45), channel_id=1, source_target_pairs={{0,5},{1,4},{2,7},{3,6},{4,1},{5,0},{6,3},{7,2},{8,13},{9,12},{10,... | collective-permute-start | bytes 258056 | tf_op jit(solution)/shard_map/ppermute | solution.py:230
  36.7 1.8 %collective-permute-start.7 = (bf16[8,5376]{1,0:T(8,128)(2,1)S(1)}, bf16[8,5376]{1,0:T(8,128)(2,1)S(1)}, u32[]{:S(2)}, u32[]{:S(2)}) collective-permute-start(bf16[8,5376]{1,0:T(8,128)(2,1)S(1)} %get-tuple-element.39), channel_id=1, source_target_pairs={{0,7},{1,6},{2,5},{3,4},{4,3},{5,2},{6,1},{7,0},{8,15},{9,14},{10,... | collective-permute-start | bytes 258056 | tf_op jit(solution)/shard_map/ppermute | solution.py:230
  38.5 0.0 collective-permute-done.10.refs_4_
  38.5 0.9 %collective-permute-start.8 = (bf16[8,5376]{1,0:T(8,128)(2,1)S(1)}, bf16[8,5376]{1,0:T(8,128)(2,1)S(1)}, u32[]{:S(2)}, u32[]{:S(2)}) collective-permute-start(bf16[8,5376]{1,0:T(8,128)(2,1)S(1)} %get-tuple-element.40), channel_id=1, source_target_pairs={{0,2},{1,3},{2,0},{3,1},{4,6},{5,7},{6,4},{7,5},{8,10},{9,11},{10,... | collective-permute-start | bytes 258056 | tf_op jit(solution)/shard_map/ppermute | solution.py:230
  39.4 3.2 %collective-permute-done.11.refs_5_ = bf16[8,5376]{1,0:T(8,128)(2,1)S(1)} collective-permute-done((bf16[8,5376]{1,0:T(8,128)(2,1)S(1)}, bf16[8,5376]{1,0:T(8,128)(2,1)S(1)}, u32[]{:S(2)}, u32[]{:S(2)}) %collective-permute-start.11) | collective-permute-done | bytes 86048 | tf_op jit(solution)/shard_map/ppermute | solution.py:230
  42.5 0.8 %collective-permute-start.9 = (bf16[8,5376]{1,0:T(8,128)(2,1)S(1)}, bf16[8,5376]{1,0:T(8,128)(2,1)S(1)}, u32[]{:S(2)}, u32[]{:S(2)}) collective-permute-start(bf16[8,5376]{1,0:T(8,128)(2,1)S(1)} %get-tuple-element.41), channel_id=1, source_target_pairs={{0,3},{1,2},{2,1},{3,0},{4,7},{5,6},{6,5},{7,4},{8,11},{9,10},{10,... | collective-permute-start | bytes 258056 | tf_op jit(solution)/shard_map/ppermute | solution.py:230
  43.4 0.0 copy-done.7
  43.4 0.0 collective-permute-done.12.refs_6_
  43.4 3.7 %collective-permute-done.13.refs_7_ = bf16[8,5376]{1,0:T(8,128)(2,1)S(1)} collective-permute-done((bf16[8,5376]{1,0:T(8,128)(2,1)S(1)}, bf16[8,5376]{1,0:T(8,128)(2,1)S(1)}, u32[]{:S(2)}, u32[]{:S(2)}) %collective-permute-start.13) | collective-permute-done | bytes 86048 | tf_op jit(solution)/shard_map/ppermute | solution.py:230
  47.1 0.0 collective-permute-done.7.refs_1_
  47.1 0.0 collective-permute-done.8.refs_2_
  47.1 0.9 %collective-permute-done.9.refs_3_ = bf16[8,5376]{1,0:T(8,128)(2,1)S(1)} collective-permute-done((bf16[8,5376]{1,0:T(8,128)(2,1)S(1)}, bf16[8,5376]{1,0:T(8,128)(2,1)S(1)}, u32[]{:S(2)}, u32[]{:S(2)}) %collective-permute-start.9) | collective-permute-done | bytes 86048 | tf_op jit(solution)/shard_map/ppermute | solution.py:230
  48.0 0.0 copy-done.1
  48.0 0.5 norm.1
  48.5 0.8 %broadcast_in_dim.24 = f32[32,1,1536]{2,1,0:T(1,128)} broadcast(f32[1536]{0:T(1024)S(1)} %reduce.1), dimensions={2} | broadcast | bytes 202752 | tf_op jit(solution)/shard_map/broadcast_in_dim | solution.py:442
  49.3 5.9 %all-to-all-start = ((f32[32,1,1536]{2,1,0:T(1,128)}), f32[32,1,1536]{2,1,0:T(1,128)S(1)}, u32[]{:S(2)}, u32[]{:S(2)}) async-start(f32[32,1,1536]{2,1,0:T(1,128)} %broadcast_in_dim.24), calls=%async_computation | async-start | bytes 393216 | tf_op jit(solution)/shard_map/all_to_all | solution.py:237
  55.3 0.0 copy-done.2
  55.3 0.0 copy-done.3
  55.3 0.0 copy-done.6
  55.3 1.1 %probs.1 = (f32[16,128,128]{2,1,0:T(8,128)S(1)}, f32[16,128,128]{2,1,0:T(8,128)S(1)}) custom-call(bf16[128,1280]{1,0:T(8,128)(2,1)S(1)} %bitcast.19, bf16[128,1280]{1,0:T(8,128)(2,1)S(1)} %bitcast.21, s32[1,32]{1,0:T(1,128)S(1)} %bitcast.24), custom_call_target="tpu_custom_call" | custom-call | flops 268435456 | bytes 2097152 | tf_op jit(solution)/shard_map/probs/pallas_call | solution.py:269
  56.4 0.0 copy-done.4
  56.4 2.4 %window.1 = (bf16[128,1280]{1,0:T(8,128)(2,1)}, bf16[128,1280]{1,0:T(8,128)(2,1)}, bf16[128,1280]{1,0:T(8,128)(2,1)}) custom-call(bf16[128,1280]{1,0:T(8,128)(2,1)S(1)} %get-tuple-element.46.g_ref, bf16[128,1280]{1,0:T(8,128)(2,1)S(1)} %bitcast.20, bf16[128,1280]{1,0:T(8,128)(2,1)S(1)} %bitcast.22, bf16[128,1280]{1,0:T(8,128)(2,1)S(1)} %bitcast.23, ...), custom_call_target="tpu_custom_call" | custom-call | flops 335544320 | bytes 4390912 | tf_op jit(solution)/shard_map/window/pallas_call | solution.py:385
  58.8 5.1 %all-to-all-done = f32[32,1,1536]{2,1,0:T(1,128)S(1)} async-done(((f32[32,1,1536]{2,1,0:T(1,128)}), f32[32,1,1536]{2,1,0:T(1,128)S(1)}, u32[]{:S(2)}, u32[]{:S(2)}) %all-to-all-start) | async-done | bytes 196640 | tf_op jit(solution)/shard_map/all_to_all | solution.py:237
  63.8 0.1 slice_reduce_fusion
  63.9 0.6 broadcast_multiply_fusion
  64.5 0.6 slice_multiply_fusion
  (3 shorter events, 0.0 us)
Async XLA Ops:
  1.8 10.2 %collective-permute-start = (bf16[32,2048]{1,0:T(8,128)(2,1)S(1)}, bf16[32,2048]{1,0:T(8,128)(2,1)S(1)}, u32[]{:S(2)}, u32[]{:S(2)}) collective-permute-start(bf16[32,2048]{1,0:T(8,128)(2,1)S(1)} %get-tuple-element.54), channel_id=1, source_target_pairs={{0,16},{8,24},{16,0},{24,8},{1,17},{9,25},{17,1},{25,9},{2,18},{10... | collective-permute-start | bytes 393224 | tf_op jit(solution)/shard_map/ppermute | solution.py:230
  4.8 7.2 %collective-permute-start.1 = (bf16[32,2048]{1,0:T(8,128)(2,1)S(1)}, bf16[32,2048]{1,0:T(8,128)(2,1)S(1)}, u32[]{:S(2)}, u32[]{:S(2)}) collective-permute-start(bf16[32,2048]{1,0:T(8,128)(2,1)S(1)} %get-tuple-element.56), channel_id=1, source_target_pairs={{0,8},{8,0},{16,24},{24,16},{1,9},{9,1},{17,25},{25,17},{2,10},{10... | collective-permute-start | bytes 393224 | tf_op jit(solution)/shard_map/ppermute | solution.py:230
  4.8 7.2 %collective-permute-start.2 = (bf16[32,2048]{1,0:T(8,128)(2,1)S(1)}, bf16[32,2048]{1,0:T(8,128)(2,1)S(1)}, u32[]{:S(2)}, u32[]{:S(2)}) collective-permute-start(bf16[32,2048]{1,0:T(8,128)(2,1)S(1)} %get-tuple-element.53), channel_id=1, source_target_pairs={{0,24},{8,16},{16,8},{24,0},{1,25},{9,17},{17,9},{25,1},{2,26},{10... | collective-permute-start | bytes 393224 | tf_op jit(solution)/shard_map/ppermute | solution.py:230
  5.0 7.0 %copy-start = (bf16[5120,2048]{1,0:T(8,128)(2,1)S(1)}, bf16[5120,2048]{1,0:T(8,128)(2,1)}, u32[]{:S(2)}) copy-start(bf16[5120,2048]{1,0:T(8,128)(2,1)} %refs_4_.3) | copy-start | bytes 62914564
  12.0 16.8 %copy-start.5 = (s32[1,32]{1,0:T(1,128)S(1)}, s32[1,32]{1,0:T(1,128)}, u32[]{:S(2)}) copy-start(s32[1,32]{1,0:T(1,128)} %targets_ref.1) | copy-start | bytes 388
  12.0 31.4 %copy-start.7 = (f32[1280]{0:T(1024)S(1)}, f32[1280]{0:T(1024)}, u32[]{:S(2)}) copy-start(f32[1280]{0:T(1024)} %param.12) | copy-start | bytes 15364
  12.0 35.9 %copy-start.1 = (bf16[1,128,1280]{2,1,0:T(8,128)(2,1)S(1)}, bf16[1,128,1280]{2,1,0:T(8,128)(2,1)}, u32[]{:S(2)}) copy-start(bf16[1,128,1280]{2,1,0:T(8,128)(2,1)} %param.11) | copy-start | bytes 983044
  12.1 43.2 %copy-start.2 = (bf16[1,128,1280]{2,1,0:T(8,128)(2,1)S(1)}, bf16[1,128,1280]{2,1,0:T(8,128)(2,1)}, u32[]{:S(2)}) copy-start(bf16[1,128,1280]{2,1,0:T(8,128)(2,1)} %param.14) | copy-start | bytes 983044
  12.1 43.2 %copy-start.3 = (bf16[1,128,1280]{2,1,0:T(8,128)(2,1)S(1)}, bf16[1,128,1280]{2,1,0:T(8,128)(2,1)}, u32[]{:S(2)}) copy-start(bf16[1,128,1280]{2,1,0:T(8,128)(2,1)} %param.15) | copy-start | bytes 983044
  12.1 43.2 %copy-start.6 = (s32[1,1,32]{2,1,0:T(1,128)S(1)}, s32[1,1,32]{2,1,0:T(1,128)}, u32[]{:S(2)}) copy-start(s32[1,1,32]{2,1,0:T(1,128)} %param.17) | copy-start | bytes 388
  12.1 44.3 %copy-start.4 = (bf16[1,128,1280]{2,1,0:T(8,128)(2,1)S(1)}, bf16[1,128,1280]{2,1,0:T(8,128)(2,1)}, u32[]{:S(2)}) copy-start(bf16[1,128,1280]{2,1,0:T(8,128)(2,1)} %param.16) | copy-start | bytes 983044
  15.1 3.7 %collective-permute-start.5 = (bf16[64,2560]{1,0:T(8,128)(2,1)S(1)}, bf16[64,2560]{1,0:T(8,128)(2,1)S(1)}, u32[]{:S(2)}, u32[]{:S(2)}) collective-permute-start(bf16[64,2560]{1,0:T(8,128)(2,1)S(1)} %get-tuple-element.34), channel_id=1, source_target_pairs={{0,8},{8,0},{16,24},{24,16},{1,9},{9,1},{17,25},{25,17},{2,10},{10... | collective-permute-start | bytes 983048 | tf_op jit(solution)/shard_map/ppermute | solution.py:230
  18.5 2.4 %collective-permute-start.3 = (bf16[64,2560]{1,0:T(8,128)(2,1)S(1)}, bf16[64,2560]{1,0:T(8,128)(2,1)S(1)}, u32[]{:S(2)}, u32[]{:S(2)}) collective-permute-start(bf16[64,2560]{1,0:T(8,128)(2,1)S(1)} %get-tuple-element.30), channel_id=1, source_target_pairs={{0,8},{8,0},{16,24},{24,16},{1,9},{9,1},{17,25},{25,17},{2,10},{10... | collective-permute-start | bytes 983048 | tf_op jit(solution)/shard_map/ppermute | solution.py:230
  18.9 7.1 %collective-permute-start.6 = (bf16[32,2560]{1,0:T(8,128)(2,1)S(1)}, bf16[32,2560]{1,0:T(8,128)(2,1)S(1)}, u32[]{:S(2)}, u32[]{:S(2)}) collective-permute-start(bf16[32,2560]{1,0:T(8,128)(2,1)S(1)} %get-tuple-element.36), channel_id=1, source_target_pairs={{0,16},{8,24},{16,0},{24,8},{1,17},{9,25},{17,1},{25,9},{2,18},{10... | collective-permute-start | bytes 491528 | tf_op jit(solution)/shard_map/ppermute | solution.py:230
  21.0 7.9 %collective-permute-start.4 = (bf16[32,2560]{1,0:T(8,128)(2,1)S(1)}, bf16[32,2560]{1,0:T(8,128)(2,1)S(1)}, u32[]{:S(2)}, u32[]{:S(2)}) collective-permute-start(bf16[32,2560]{1,0:T(8,128)(2,1)S(1)} %get-tuple-element.32), channel_id=1, source_target_pairs={{0,16},{8,24},{16,0},{24,8},{1,17},{9,25},{17,1},{25,9},{2,18},{10... | collective-permute-start | bytes 491528 | tf_op jit(solution)/shard_map/ppermute | solution.py:230
  29.4 9.1 %collective-permute-start.10 = (bf16[8,5376]{1,0:T(8,128)(2,1)S(1)}, bf16[8,5376]{1,0:T(8,128)(2,1)S(1)}, u32[]{:S(2)}, u32[]{:S(2)}) collective-permute-start(bf16[8,5376]{1,0:T(8,128)(2,1)S(1)} %get-tuple-element.42), channel_id=1, source_target_pairs={{0,1},{1,0},{2,3},{3,2},{4,5},{5,4},{6,7},{7,6},{8,9},{9,8},{10,11... | collective-permute-start | bytes 258056 | tf_op jit(solution)/shard_map/ppermute | solution.py:230
  31.1 11.5 %collective-permute-start.11 = (bf16[8,5376]{1,0:T(8,128)(2,1)S(1)}, bf16[8,5376]{1,0:T(8,128)(2,1)S(1)}, u32[]{:S(2)}, u32[]{:S(2)}) collective-permute-start(bf16[8,5376]{1,0:T(8,128)(2,1)S(1)} %get-tuple-element.43), channel_id=1, source_target_pairs={{0,4},{1,5},{2,6},{3,7},{4,0},{5,1},{6,2},{7,3},{8,12},{9,13},{10,... | collective-permute-start | bytes 258056 | tf_op jit(solution)/shard_map/ppermute | solution.py:230
  33.7 9.7 %collective-permute-start.12 = (bf16[8,5376]{1,0:T(8,128)(2,1)S(1)}, bf16[8,5376]{1,0:T(8,128)(2,1)S(1)}, u32[]{:S(2)}, u32[]{:S(2)}) collective-permute-start(bf16[8,5376]{1,0:T(8,128)(2,1)S(1)} %get-tuple-element.44), channel_id=1, source_target_pairs={{0,6},{1,7},{2,4},{3,5},{4,2},{5,3},{6,0},{7,1},{8,14},{9,15},{10,... | collective-permute-start | bytes 258056 | tf_op jit(solution)/shard_map/ppermute | solution.py:230
  35.0 12.1 %collective-permute-start.13 = (bf16[8,5376]{1,0:T(8,128)(2,1)S(1)}, bf16[8,5376]{1,0:T(8,128)(2,1)S(1)}, u32[]{:S(2)}, u32[]{:S(2)}) collective-permute-start(bf16[8,5376]{1,0:T(8,128)(2,1)S(1)} %get-tuple-element.45), channel_id=1, source_target_pairs={{0,5},{1,4},{2,7},{3,6},{4,1},{5,0},{6,3},{7,2},{8,13},{9,12},{10,... | collective-permute-start | bytes 258056 | tf_op jit(solution)/shard_map/ppermute | solution.py:230
  36.7 10.4 %collective-permute-start.7 = (bf16[8,5376]{1,0:T(8,128)(2,1)S(1)}, bf16[8,5376]{1,0:T(8,128)(2,1)S(1)}, u32[]{:S(2)}, u32[]{:S(2)}) collective-permute-start(bf16[8,5376]{1,0:T(8,128)(2,1)S(1)} %get-tuple-element.39), channel_id=1, source_target_pairs={{0,7},{1,6},{2,5},{3,4},{4,3},{5,2},{6,1},{7,0},{8,15},{9,14},{10,... | collective-permute-start | bytes 258056 | tf_op jit(solution)/shard_map/ppermute | solution.py:230
  38.5 8.6 %collective-permute-start.8 = (bf16[8,5376]{1,0:T(8,128)(2,1)S(1)}, bf16[8,5376]{1,0:T(8,128)(2,1)S(1)}, u32[]{:S(2)}, u32[]{:S(2)}) collective-permute-start(bf16[8,5376]{1,0:T(8,128)(2,1)S(1)} %get-tuple-element.40), channel_id=1, source_target_pairs={{0,2},{1,3},{2,0},{3,1},{4,6},{5,7},{6,4},{7,5},{8,10},{9,11},{10,... | collective-permute-start | bytes 258056 | tf_op jit(solution)/shard_map/ppermute | solution.py:230
  42.5 5.4 %collective-permute-start.9 = (bf16[8,5376]{1,0:T(8,128)(2,1)S(1)}, bf16[8,5376]{1,0:T(8,128)(2,1)S(1)}, u32[]{:S(2)}, u32[]{:S(2)}) collective-permute-start(bf16[8,5376]{1,0:T(8,128)(2,1)S(1)} %get-tuple-element.41), channel_id=1, source_target_pairs={{0,3},{1,2},{2,1},{3,0},{4,7},{5,6},{6,5},{7,4},{8,11},{9,10},{10,... | collective-permute-start | bytes 258056 | tf_op jit(solution)/shard_map/ppermute | solution.py:230
  49.3 14.5 %all-to-all-start = ((f32[32,1,1536]{2,1,0:T(1,128)}), f32[32,1,1536]{2,1,0:T(1,128)S(1)}, u32[]{:S(2)}, u32[]{:S(2)}) async-start(f32[32,1,1536]{2,1,0:T(1,128)} %broadcast_in_dim.24), calls=%async_computation | async-start | bytes 393216 | tf_op jit(solution)/shard_map/all_to_all | solution.py:237

commit v11 on v10

--- a/solution.py
+++ b/solution.py
@@ -65,7 +65,7 @@
 
 def project(x_blocks, w_down, touched, first, width, with_sum):
     blocks, (rows, depth) = len(x_blocks), x_blocks[0].shape
-    tile = 512
+    tile = 1280
     while width % tile:
         tile //= 2
     out_shape = [jax.ShapeDtypeStruct((blocks * rows // 2, width), BF16)] * 2
@@ -129,7 +129,7 @@
 
 
 def peer_masks(peers):
-    return (0, 7, 2, 3, 1, 4, 6, 5) if peers == 8 else tuple(range(peers))
+    return (0, 1, 4, 6, 5, 7, 2, 3) if peers == 8 else tuple(range(peers))
 
 
 def block_peer(block, peers, me):
@@ -303,20 +303,21 @@
     inputs = patches_ref[...].astype(F32)
     inverse_rms = lax.rsqrt(jnp.mean(inputs * inputs, axis=1, keepdims=True) + 1e-06)
     normed = inputs * inverse_rms
-    gain_part = jnp.sum(patch_grads * normed, axis=0, keepdims=True)
-    share_ref[:, :, :width] = jnp.broadcast_to(gain_part[None], (share_ref.shape[0], 1, width))
+    row = jnp.sum(patch_grads * normed, axis=0, keepdims=True)
     if carries:
         carried = routed[:, per_token * width + LANES :]
         capacity = slots // peers
-        pieces = (share_ref.shape[2] - width) // LANES
-        row = iota((slots, LANES), 0) % capacity
+        copies, lines, line_width = share_ref.shape
+        pieces = (lines * line_width - width) // LANES
+        place = iota((slots, LANES), 0) % capacity
+        parts = [row]
         for piece in range(pieces):
-            kept = jnp.logical_and(row % pieces == piece, row < 3 * pieces)
-            line = jnp.sum(jnp.where(kept, carried, 0.0), axis=0, keepdims=True)
-            at = width + piece * LANES
-            share_ref[:, :, at : at + LANES] = jnp.broadcast_to(
-                line[None], (share_ref.shape[0], 1, LANES)
-            )
+            kept = jnp.logical_and(place % pieces == piece, place < 3 * pieces)
+            parts.append(jnp.sum(jnp.where(kept, carried, 0.0), axis=0, keepdims=True))
+        row = jnp.concatenate(parts, axis=1)
+        lines = [row[:, at : at + line_width] for at in range(0, row.shape[1], line_width)]
+        row = jnp.broadcast_to(jnp.concatenate(lines, axis=0)[None], share_ref.shape)
+    share_ref[...] = row.astype(share_ref.dtype)
     scaled = gain_ref[...] * patch_grads
     out_ref[...] = (
         inverse_rms * (scaled - normed * jnp.mean(scaled * normed, axis=1, keepdims=True))
@@ -327,8 +328,8 @@
     count, width = patches.shape
     routed = sum(x.size for x in received)
     return pl.pallas_call(
-        functools.partial(norm_kernel, peers, share[2] > width),
-        out_shape=[jax.ShapeDtypeStruct((count, width), BF16), jax.ShapeDtypeStruct(share, F32)],
+        functools.partial(norm_kernel, peers, len(share.shape) == 3),
+        out_shape=[jax.ShapeDtypeStruct((count, width), BF16), share],
         in_specs=vmem(2 + len(received)),
         out_specs=vmem(2),
         compiler_params=pltpu.CompilerParams(vmem_limit_bytes=VMEM_BYTES),
@@ -407,7 +408,7 @@
     block = w_down.shape[1]
     width = patches.shape[2]
     pieces = block // peers // LANES
-    carries = pieces > 0 and 3 * pieces <= capacity
+    carries = pieces > 0 and 3 * pieces <= capacity and (width // LANES + pieces) % 2 == 0
 
     order = [0]
     while len(order) < images:
@@ -436,16 +437,20 @@
     packed = pack(terms, token_target, me.reshape(1), bias_part, peers, capacity, direct, carries)
     routed = route(packed, peers, direct)
 
-    share = (1, 1, width + pieces * LANES if carries else width)
+    if carries:
+        share = jax.ShapeDtypeStruct((devices, 2, (width + pieces * LANES) // 2), BF16)
+    else:
+        share = jax.ShapeDtypeStruct((1, width), F32)
     out_grads, shared = norm_backward(routed, peers, patches[0], gain[None], share)
     if carries:
-        shared = jnp.broadcast_to(shared, (devices,) + shared.shape[1:])
-        shared = exchange(shared, ("img", "seq"), devices)
-        gain_total = jnp.sum(shared[:, 0, :width], axis=0)
-        bias_total = shared[:, 0, width:].reshape(-1)
+        shared = exchange(shared, ("img", "seq"), devices).astype(F32).reshape(devices, -1)
+        gain_total = jnp.sum(shared[:, :width], axis=0)
+        bias_total = shared[:, width:].reshape(-1)
     else:
-        gain_total = lax.psum(shared[0, 0], ("img", "seq"))
+        gain_total = lax.psum(shared[0], ("img", "seq"))
         bias_total = lax.all_gather(lax.psum(bias_part[0], "seq"), "img", tiled=True)
+    gain_grad = gain_total / math.sqrt(devices * patches.shape[1])
+    bias_grad = bias_total / math.sqrt(devices * rows)
     grads = window_backward(out_grads, queries[0], keys[0], values[0], probs, probs_t)
     gain_grad = gain_total / math.sqrt(devices * patches.shape[1])
     bias_grad = bias_total / math.sqrt(devices * rows)

time: 65.4 us -> 64 us (0.979)
  other arithmetic: 1.35 us -> 0.63 us
    all_to_all x1, waiting for transfers between devices: 5.06 us -> 4.07 us  [exchange(): lax.all_to_all(x, axis, split_axis=0, concat_axis=0, tiled=True)]
    broadcast_in_dim x1 -> x0, local copies, waits for them, and re-layouts: 0.78 us -> none  [body(): shared = jnp.broadcast_to(shared, (devices,) + shared.shape[1:])]
    unnamed x16 -> x18, local copies, waits for them, and re-layouts: 7.01 us -> 7.65 us
where the time goes in v11:
time: 64 us; the launch traced here: 63.8 us
  starting transfers between devices  23.3 us (36%)
  waiting for transfers between devices  19 us (30%)
  Pallas kernels  11.2 us (18%)
  local copies, waits for them, and re-layouts  8.8 us (14%)
  between operations  0.84 us (1%)
    ppermute x14, starting transfers between devices, swap(): return lax.ppermute(x, axis, [(i, i ^ mask) for i in range(n)])  17.7 us
    ppermute x14, waiting for transfers between devices, swap(): return lax.ppermute(x, axis, [(i, i ^ mask) for i in range(n)])  14.9 us
    unnamed x18, local copies, waits for them, and re-layouts  7.65 us
    pallas_call x2, Pallas kernels, project(): pl.pallas_call(functools.partial(project_kernel, blocks, first, tile, wit...  6.05 us
    all_to_all x1, starting transfers between devices, exchange(): lax.all_to_all(x, axis, split_axis=0, concat_axis=0, tiled=True)  5.68 us
    all_to_all x1, waiting for transfers between devices, exchange(): lax.all_to_all(x, axis, split_axis=0, concat_axis=0, tiled=True)  4.07 us
    pallas_call x1, Pallas kernels, window_backward(): pl.pallas_call(window_kernel, out_shape=[shape] * 3, in_specs=vmem(6), ou...  2.38 us
  transfers between devices with their start and end apart: 15, of which 6 were waited for; matrix products, arithmetic and copies ran while one was open for 0% of the time, Pallas kernels for 10%

profile of v11, /device:TPU:0, one launch (start us, length us, event | category | flops | bytes accessed | tf_op | source)
XLA Modules:
  0.0 63.8 jit_solution(7947084814032165717)
XLA Ops:
  0.7 1.1 %dynamic-slice_bitcast_fusion = (bf16[32,2048]{1,0:T(8,128)(2,1)S(1)}, bf16[32,2048]{1,0:T(8,128)(2,1)S(1)}, bf16[32,2048]{1,0:T(8,128)(2,1)S(1)}, bf16[32,2048]{1,0:T(8,128)(2,1)S(1)}) fusion(bf16[1,32,8192]{2,1,0:T(8,128)(2,1)} %param.9, s32[]{:T(128)S(6)} %select_n.15, s32[]{:T(128)S(6)} %select_n.13, s32[]{:T(128)S(6)} %select_n.12, s32[]{:T(128)S(6)} %select_n.14), kind=kLoop, calls=%fused_computation.1 | loop fusion | bytes 1048592 | tf_op jit(solution)/shard_map/dynamic_slice | solution.py:419
  1.8 2.5 %collective-permute-start.2 = (bf16[32,2048]{1,0:T(8,128)(2,1)S(1)}, bf16[32,2048]{1,0:T(8,128)(2,1)S(1)}, u32[]{:S(2)}, u32[]{:S(2)}) collective-permute-start(bf16[32,2048]{1,0:T(8,128)(2,1)S(1)} %get-tuple-element.53), channel_id=1, source_target_pairs={{0,24},{8,16},{16,8},{24,0},{1,25},{9,17},{17,9},{25,1},{2,26},{10... | collective-permute-start | bytes 393224 | tf_op jit(solution)/shard_map/ppermute | solution.py:230
  4.3 0.6 %collective-permute-start = (bf16[32,2048]{1,0:T(8,128)(2,1)S(1)}, bf16[32,2048]{1,0:T(8,128)(2,1)S(1)}, u32[]{:S(2)}, u32[]{:S(2)}) collective-permute-start(bf16[32,2048]{1,0:T(8,128)(2,1)S(1)} %get-tuple-element.54), channel_id=1, source_target_pairs={{0,16},{8,24},{16,0},{24,8},{1,17},{9,25},{17,1},{25,9},{2,18},{10... | collective-permute-start | bytes 393224 | tf_op jit(solution)/shard_map/ppermute | solution.py:230
  4.9 0.0 collective-permute-start.1
  5.0 0.0 copy-start
  5.0 7.0 %copy-done = bf16[5120,2048]{1,0:T(8,128)(2,1)S(1)} copy-done((bf16[5120,2048]{1,0:T(8,128)(2,1)S(1)}, bf16[5120,2048]{1,0:T(8,128)(2,1)}, u32[]{:S(2)}) %copy-start) | copy-done | bytes 20971544
  11.9 0.0 collective-permute-done.2.refs_3_
  11.9 0.0 collective-permute-done.refs_1_
  11.9 0.0 collective-permute-done.1.refs_2_
  11.9 0.0 copy-start.5
  11.9 0.0 copy-start.7
  12.0 0.0 copy-start.1
  12.0 0.0 copy-start.2
  12.0 0.0 copy-start.3
  12.0 0.0 copy-start.6
  12.0 0.0 copy-start.4
  12.0 3.1 %project.2 = (bf16[64,2560]{1,0:T(8,128)(2,1)S(1)}, bf16[64,2560]{1,0:T(8,128)(2,1)S(1)}, f32[1,2048]{1,0:T(1,128)S(1)}) custom-call(bf16[32,2048]{1,0:T(8,128)(2,1)S(1)} %get-tuple-element.55.refs_0_, bf16[32,2048]{1,0:T(8,128)(2,1)S(1)} %collective-permute-done.refs_1_, bf16[32,2048]{1,0:T(8,128)(2,1)S(1)} %collective-permute-done.1.refs_2_, ...), custom_call_target="tpu_custom_call" | custom-call | flops 1342177280 | bytes 10485760 | tf_op jit(solution)/shard_map/project/pallas_call | solution.py:74
  15.1 0.5 collective-permute-start.3
  15.6 3.0 %project.3 = (bf16[64,2560]{1,0:T(8,128)(2,1)S(1)}, bf16[64,2560]{1,0:T(8,128)(2,1)S(1)}) custom-call(bf16[32,2048]{1,0:T(8,128)(2,1)S(1)} %get-tuple-element.55.refs_0_, bf16[32,2048]{1,0:T(8,128)(2,1)S(1)} %collective-permute-done.refs_1_, bf16[32,2048]{1,0:T(8,128)(2,1)S(1)} %collective-permute-done.1.refs_2_, ...), custom_call_target="tpu_custom_call" | custom-call | flops 1342177280 | bytes 10485760 | tf_op jit(solution)/shard_map/project/pallas_call | solution.py:74
  18.6 0.1 collective-permute-start.5
  18.7 0.0 collective-permute-done.3.got_ref
  18.7 0.1 halve.2
  18.8 1.8 %collective-permute-start.4 = (bf16[32,2560]{1,0:T(8,128)(2,1)S(1)}, bf16[32,2560]{1,0:T(8,128)(2,1)S(1)}, u32[]{:S(2)}, u32[]{:S(2)}) collective-permute-start(bf16[32,2560]{1,0:T(8,128)(2,1)S(1)} %get-tuple-element.32), channel_id=1, source_target_pairs={{0,16},{8,24},{16,0},{24,8},{1,17},{9,25},{17,1},{25,9},{2,18},{10... | collective-permute-start | bytes 491528 | tf_op jit(solution)/shard_map/ppermute | solution.py:230
  20.6 0.0 collective-permute-done.5.got_ref
  20.6 0.1 halve.3
  20.7 1.2 %collective-permute-start.6 = (bf16[32,2560]{1,0:T(8,128)(2,1)S(1)}, bf16[32,2560]{1,0:T(8,128)(2,1)S(1)}, u32[]{:S(2)}, u32[]{:S(2)}) collective-permute-start(bf16[32,2560]{1,0:T(8,128)(2,1)S(1)} %get-tuple-element.36), channel_id=1, source_target_pairs={{0,16},{8,24},{16,0},{24,8},{1,17},{9,25},{17,1},{25,9},{2,18},{10... | collective-permute-start | bytes 491528 | tf_op jit(solution)/shard_map/ppermute | solution.py:230
  21.9 4.0 %collective-permute-done.4.refs_1_ = bf16[32,2560]{1,0:T(8,128)(2,1)S(1)} collective-permute-done((bf16[32,2560]{1,0:T(8,128)(2,1)S(1)}, bf16[32,2560]{1,0:T(8,128)(2,1)S(1)}, u32[]{:S(2)}, u32[]{:S(2)}) %collective-permute-start.4) | collective-permute-done | bytes 163872 | tf_op jit(solution)/shard_map/ppermute | solution.py:230
  25.9 3.1 %collective-permute-done.6.refs_3_ = bf16[32,2560]{1,0:T(8,128)(2,1)S(1)} collective-permute-done((bf16[32,2560]{1,0:T(8,128)(2,1)S(1)}, bf16[32,2560]{1,0:T(8,128)(2,1)S(1)}, u32[]{:S(2)}, u32[]{:S(2)}) %collective-permute-start.6) | collective-permute-done | bytes 163872 | tf_op jit(solution)/shard_map/ppermute | solution.py:230
  29.0 0.0 copy-done.5
  29.0 0.5 pack.1
  29.5 1.6 %collective-permute-start.7 = (bf16[8,5376]{1,0:T(8,128)(2,1)S(1)}, bf16[8,5376]{1,0:T(8,128)(2,1)S(1)}, u32[]{:S(2)}, u32[]{:S(2)}) collective-permute-start(bf16[8,5376]{1,0:T(8,128)(2,1)S(1)} %get-tuple-element.39), channel_id=1, source_target_pairs={{0,1},{1,0},{2,3},{3,2},{4,5},{5,4},{6,7},{7,6},{8,9},{9,8},{10,11... | collective-permute-start | bytes 258056 | tf_op jit(solution)/shard_map/ppermute | solution.py:230
  31.0 2.6 %collective-permute-start.8 = (bf16[8,5376]{1,0:T(8,128)(2,1)S(1)}, bf16[8,5376]{1,0:T(8,128)(2,1)S(1)}, u32[]{:S(2)}, u32[]{:S(2)}) collective-permute-start(bf16[8,5376]{1,0:T(8,128)(2,1)S(1)} %get-tuple-element.40), channel_id=1, source_target_pairs={{0,4},{1,5},{2,6},{3,7},{4,0},{5,1},{6,2},{7,3},{8,12},{9,13},{10,... | collective-permute-start | bytes 258056 | tf_op jit(solution)/shard_map/ppermute | solution.py:230
  33.6 1.4 %collective-permute-start.9 = (bf16[8,5376]{1,0:T(8,128)(2,1)S(1)}, bf16[8,5376]{1,0:T(8,128)(2,1)S(1)}, u32[]{:S(2)}, u32[]{:S(2)}) collective-permute-start(bf16[8,5376]{1,0:T(8,128)(2,1)S(1)} %get-tuple-element.41), channel_id=1, source_target_pairs={{0,6},{1,7},{2,4},{3,5},{4,2},{5,3},{6,0},{7,1},{8,14},{9,15},{10,... | collective-permute-start | bytes 258056 | tf_op jit(solution)/shard_map/ppermute | solution.py:230
  35.0 1.6 %collective-permute-start.10 = (bf16[8,5376]{1,0:T(8,128)(2,1)S(1)}, bf16[8,5376]{1,0:T(8,128)(2,1)S(1)}, u32[]{:S(2)}, u32[]{:S(2)}) collective-permute-start(bf16[8,5376]{1,0:T(8,128)(2,1)S(1)} %get-tuple-element.42), channel_id=1, source_target_pairs={{0,5},{1,4},{2,7},{3,6},{4,1},{5,0},{6,3},{7,2},{8,13},{9,12},{10,... | collective-permute-start | bytes 258056 | tf_op jit(solution)/shard_map/ppermute | solution.py:230
  36.6 1.8 %collective-permute-start.11 = (bf16[8,5376]{1,0:T(8,128)(2,1)S(1)}, bf16[8,5376]{1,0:T(8,128)(2,1)S(1)}, u32[]{:S(2)}, u32[]{:S(2)}) collective-permute-start(bf16[8,5376]{1,0:T(8,128)(2,1)S(1)} %get-tuple-element.43), channel_id=1, source_target_pairs={{0,7},{1,6},{2,5},{3,4},{4,3},{5,2},{6,1},{7,0},{8,15},{9,14},{10,... | collective-permute-start | bytes 258056 | tf_op jit(solution)/shard_map/ppermute | solution.py:230
  38.5 0.0 collective-permute-done.7.refs_1_
  38.5 0.9 %collective-permute-start.12 = (bf16[8,5376]{1,0:T(8,128)(2,1)S(1)}, bf16[8,5376]{1,0:T(8,128)(2,1)S(1)}, u32[]{:S(2)}, u32[]{:S(2)}) collective-permute-start(bf16[8,5376]{1,0:T(8,128)(2,1)S(1)} %get-tuple-element.44), channel_id=1, source_target_pairs={{0,2},{1,3},{2,0},{3,1},{4,6},{5,7},{6,4},{7,5},{8,10},{9,11},{10,... | collective-permute-start | bytes 258056 | tf_op jit(solution)/shard_map/ppermute | solution.py:230
  39.4 3.2 %collective-permute-done.8.refs_2_ = bf16[8,5376]{1,0:T(8,128)(2,1)S(1)} collective-permute-done((bf16[8,5376]{1,0:T(8,128)(2,1)S(1)}, bf16[8,5376]{1,0:T(8,128)(2,1)S(1)}, u32[]{:S(2)}, u32[]{:S(2)}) %collective-permute-start.8) | collective-permute-done | bytes 86048 | tf_op jit(solution)/shard_map/ppermute | solution.py:230
  42.6 1.0 %collective-permute-start.13 = (bf16[8,5376]{1,0:T(8,128)(2,1)S(1)}, bf16[8,5376]{1,0:T(8,128)(2,1)S(1)}, u32[]{:S(2)}, u32[]{:S(2)}) collective-permute-start(bf16[8,5376]{1,0:T(8,128)(2,1)S(1)} %get-tuple-element.45), channel_id=1, source_target_pairs={{0,3},{1,2},{2,1},{3,0},{4,7},{5,6},{6,5},{7,4},{8,11},{9,10},{10,... | collective-permute-start | bytes 258056 | tf_op jit(solution)/shard_map/ppermute | solution.py:230
  43.6 0.0 copy-done.7
  43.6 0.0 collective-permute-done.9.refs_3_
  43.6 3.8 %collective-permute-done.10.refs_4_ = bf16[8,5376]{1,0:T(8,128)(2,1)S(1)} collective-permute-done((bf16[8,5376]{1,0:T(8,128)(2,1)S(1)}, bf16[8,5376]{1,0:T(8,128)(2,1)S(1)}, u32[]{:S(2)}, u32[]{:S(2)}) %collective-permute-start.10) | collective-permute-done | bytes 86048 | tf_op jit(solution)/shard_map/ppermute | solution.py:230
  47.4 0.0 collective-permute-done.11.refs_5_
  47.4 0.0 collective-permute-done.12.refs_6_
  47.4 0.7 %collective-permute-done.13.refs_7_ = bf16[8,5376]{1,0:T(8,128)(2,1)S(1)} collective-permute-done((bf16[8,5376]{1,0:T(8,128)(2,1)S(1)}, bf16[8,5376]{1,0:T(8,128)(2,1)S(1)}, u32[]{:S(2)}, u32[]{:S(2)}) %collective-permute-start.13) | collective-permute-done | bytes 86048 | tf_op jit(solution)/shard_map/ppermute | solution.py:230
  48.1 0.0 copy-done.1
  48.1 1.1 %norm.1 = (bf16[128,1280]{1,0:T(8,128)(2,1)S(1)}, bf16[32,2,768]{2,1,0:T(2,128)(2,1)}) custom-call(bf16[128,1280]{1,0:T(8,128)(2,1)S(1)} %bitcast.23, f32[1,1280]{1,0:T(1,128)S(1)} %broadcast_in_dim.12.gain_ref, bf16[8,5376]{1,0:T(8,128)(2,1)S(1)} %get-tuple-element.38.refs_0_, bf16[8,5376]{1,0:T(8,128)(2,1)S(1)} %collective-permute-done.7.refs_1_, ...), custom_call_target="tpu_custom_call" | custom-call | flops 88080384 | bytes 1343488 | tf_op jit(solution)/shard_map/norm/pallas_call | solution.py:330
  49.2 5.7 %all-to-all-start = ((bf16[32,2,768]{2,1,0:T(2,128)(2,1)}), bf16[32,2,768]{2,1,0:T(2,128)(2,1)S(1)}, u32[]{:S(2)}, u32[]{:S(2)}) async-start(bf16[32,2,768]{2,1,0:T(2,128)(2,1)} %get-tuple-element.52), calls=%async_computation | async-start | bytes 196608 | tf_op jit(solution)/shard_map/all_to_all | solution.py:237
  54.9 0.0 copy-done.2
  54.9 0.0 copy-done.3
  54.9 0.0 copy-done.6
  54.9 1.1 %probs.1 = (f32[16,128,128]{2,1,0:T(8,128)S(1)}, f32[16,128,128]{2,1,0:T(8,128)S(1)}) custom-call(bf16[128,1280]{1,0:T(8,128)(2,1)S(1)} %bitcast.24, bf16[128,1280]{1,0:T(8,128)(2,1)S(1)} %bitcast.26, s32[1,32]{1,0:T(1,128)S(1)} %bitcast.29), custom_call_target="tpu_custom_call" | custom-call | flops 268435456 | bytes 2097152 | tf_op jit(solution)/shard_map/probs/pallas_call | solution.py:269
  56.0 0.0 copy-done.4
  56.0 2.4 %window.1 = (bf16[128,1280]{1,0:T(8,128)(2,1)}, bf16[128,1280]{1,0:T(8,128)(2,1)}, bf16[128,1280]{1,0:T(8,128)(2,1)}) custom-call(bf16[128,1280]{1,0:T(8,128)(2,1)S(1)} %get-tuple-element.46.g_ref, bf16[128,1280]{1,0:T(8,128)(2,1)S(1)} %bitcast.25, bf16[128,1280]{1,0:T(8,128)(2,1)S(1)} %bitcast.27, bf16[128,1280]{1,0:T(8,128)(2,1)S(1)} %bitcast.28, ...), custom_call_target="tpu_custom_call" | custom-call | flops 335544320 | bytes 4390912 | tf_op jit(solution)/shard_map/window/pallas_call | solution.py:386
  58.4 4.1 %all-to-all-done = bf16[32,2,768]{2,1,0:T(2,128)(2,1)S(1)} async-done(((bf16[32,2,768]{2,1,0:T(2,128)(2,1)}), bf16[32,2,768]{2,1,0:T(2,128)(2,1)S(1)}, u32[]{:S(2)}, u32[]{:S(2)}) %all-to-all-start) | async-done | bytes 98336 | tf_op jit(solution)/shard_map/all_to_all | solution.py:237
  62.5 0.6 copy.15
  63.2 0.6 broadcast_multiply_fusion
  (5 shorter events, 0.0 us)
Async XLA Ops:
  1.8 10.1 %collective-permute-start.2 = (bf16[32,2048]{1,0:T(8,128)(2,1)S(1)}, bf16[32,2048]{1,0:T(8,128)(2,1)S(1)}, u32[]{:S(2)}, u32[]{:S(2)}) collective-permute-start(bf16[32,2048]{1,0:T(8,128)(2,1)S(1)} %get-tuple-element.53), channel_id=1, source_target_pairs={{0,24},{8,16},{16,8},{24,0},{1,25},{9,17},{17,9},{25,1},{2,26},{10... | collective-permute-start | bytes 393224 | tf_op jit(solution)/shard_map/ppermute | solution.py:230
  4.3 7.7 %collective-permute-start = (bf16[32,2048]{1,0:T(8,128)(2,1)S(1)}, bf16[32,2048]{1,0:T(8,128)(2,1)S(1)}, u32[]{:S(2)}, u32[]{:S(2)}) collective-permute-start(bf16[32,2048]{1,0:T(8,128)(2,1)S(1)} %get-tuple-element.54), channel_id=1, source_target_pairs={{0,16},{8,24},{16,0},{24,8},{1,17},{9,25},{17,1},{25,9},{2,18},{10... | collective-permute-start | bytes 393224 | tf_op jit(solution)/shard_map/ppermute | solution.py:230
  4.9 7.0 %collective-permute-start.1 = (bf16[32,2048]{1,0:T(8,128)(2,1)S(1)}, bf16[32,2048]{1,0:T(8,128)(2,1)S(1)}, u32[]{:S(2)}, u32[]{:S(2)}) collective-permute-start(bf16[32,2048]{1,0:T(8,128)(2,1)S(1)} %get-tuple-element.56), channel_id=1, source_target_pairs={{0,8},{8,0},{16,24},{24,16},{1,9},{9,1},{17,25},{25,17},{2,10},{10... | collective-permute-start | bytes 393224 | tf_op jit(solution)/shard_map/ppermute | solution.py:230
  5.0 7.0 %copy-start = (bf16[5120,2048]{1,0:T(8,128)(2,1)S(1)}, bf16[5120,2048]{1,0:T(8,128)(2,1)}, u32[]{:S(2)}) copy-start(bf16[5120,2048]{1,0:T(8,128)(2,1)} %refs_4_.3) | copy-start | bytes 62914564
  11.9 17.0 %copy-start.5 = (s32[1,32]{1,0:T(1,128)S(1)}, s32[1,32]{1,0:T(1,128)}, u32[]{:S(2)}) copy-start(s32[1,32]{1,0:T(1,128)} %targets_ref.1) | copy-start | bytes 388
  11.9 31.6 %copy-start.7 = (f32[1280]{0:T(1024)S(1)}, f32[1280]{0:T(1024)}, u32[]{:S(2)}) copy-start(f32[1280]{0:T(1024)} %param.12) | copy-start | bytes 15364
  12.0 36.2 %copy-start.1 = (bf16[1,128,1280]{2,1,0:T(8,128)(2,1)S(1)}, bf16[1,128,1280]{2,1,0:T(8,128)(2,1)}, u32[]{:S(2)}) copy-start(bf16[1,128,1280]{2,1,0:T(8,128)(2,1)} %param.11) | copy-start | bytes 983044
  12.0 42.9 %copy-start.2 = (bf16[1,128,1280]{2,1,0:T(8,128)(2,1)S(1)}, bf16[1,128,1280]{2,1,0:T(8,128)(2,1)}, u32[]{:S(2)}) copy-start(bf16[1,128,1280]{2,1,0:T(8,128)(2,1)} %param.14) | copy-start | bytes 983044
  12.0 42.9 %copy-start.3 = (bf16[1,128,1280]{2,1,0:T(8,128)(2,1)S(1)}, bf16[1,128,1280]{2,1,0:T(8,128)(2,1)}, u32[]{:S(2)}) copy-start(bf16[1,128,1280]{2,1,0:T(8,128)(2,1)} %param.15) | copy-start | bytes 983044
  12.0 42.9 %copy-start.6 = (s32[1,1,32]{2,1,0:T(1,128)S(1)}, s32[1,1,32]{2,1,0:T(1,128)}, u32[]{:S(2)}) copy-start(s32[1,1,32]{2,1,0:T(1,128)} %param.17) | copy-start | bytes 388
  12.0 44.0 %copy-start.4 = (bf16[1,128,1280]{2,1,0:T(8,128)(2,1)S(1)}, bf16[1,128,1280]{2,1,0:T(8,128)(2,1)}, u32[]{:S(2)}) copy-start(bf16[1,128,1280]{2,1,0:T(8,128)(2,1)} %param.16) | copy-start | bytes 983044
  15.1 3.6 %collective-permute-start.3 = (bf16[64,2560]{1,0:T(8,128)(2,1)S(1)}, bf16[64,2560]{1,0:T(8,128)(2,1)S(1)}, u32[]{:S(2)}, u32[]{:S(2)}) collective-permute-start(bf16[64,2560]{1,0:T(8,128)(2,1)S(1)} %get-tuple-element.30), channel_id=1, source_target_pairs={{0,8},{8,0},{16,24},{24,16},{1,9},{9,1},{17,25},{25,17},{2,10},{10... | collective-permute-start | bytes 983048 | tf_op jit(solution)/shard_map/ppermute | solution.py:230
  18.6 2.0 %collective-permute-start.5 = (bf16[64,2560]{1,0:T(8,128)(2,1)S(1)}, bf16[64,2560]{1,0:T(8,128)(2,1)S(1)}, u32[]{:S(2)}, u32[]{:S(2)}) collective-permute-start(bf16[64,2560]{1,0:T(8,128)(2,1)S(1)} %get-tuple-element.34), channel_id=1, source_target_pairs={{0,8},{8,0},{16,24},{24,16},{1,9},{9,1},{17,25},{25,17},{2,10},{10... | collective-permute-start | bytes 983048 | tf_op jit(solution)/shard_map/ppermute | solution.py:230
  18.8 7.1 %collective-permute-start.4 = (bf16[32,2560]{1,0:T(8,128)(2,1)S(1)}, bf16[32,2560]{1,0:T(8,128)(2,1)S(1)}, u32[]{:S(2)}, u32[]{:S(2)}) collective-permute-start(bf16[32,2560]{1,0:T(8,128)(2,1)S(1)} %get-tuple-element.32), channel_id=1, source_target_pairs={{0,16},{8,24},{16,0},{24,8},{1,17},{9,25},{17,1},{25,9},{2,18},{10... | collective-permute-start | bytes 491528 | tf_op jit(solution)/shard_map/ppermute | solution.py:230
  20.7 8.3 %collective-permute-start.6 = (bf16[32,2560]{1,0:T(8,128)(2,1)S(1)}, bf16[32,2560]{1,0:T(8,128)(2,1)S(1)}, u32[]{:S(2)}, u32[]{:S(2)}) collective-permute-start(bf16[32,2560]{1,0:T(8,128)(2,1)S(1)} %get-tuple-element.36), channel_id=1, source_target_pairs={{0,16},{8,24},{16,0},{24,8},{1,17},{9,25},{17,1},{25,9},{2,18},{10... | collective-permute-start | bytes 491528 | tf_op jit(solution)/shard_map/ppermute | solution.py:230
  29.5 9.0 %collective-permute-start.7 = (bf16[8,5376]{1,0:T(8,128)(2,1)S(1)}, bf16[8,5376]{1,0:T(8,128)(2,1)S(1)}, u32[]{:S(2)}, u32[]{:S(2)}) collective-permute-start(bf16[8,5376]{1,0:T(8,128)(2,1)S(1)} %get-tuple-element.39), channel_id=1, source_target_pairs={{0,1},{1,0},{2,3},{3,2},{4,5},{5,4},{6,7},{7,6},{8,9},{9,8},{10,11... | collective-permute-start | bytes 258056 | tf_op jit(solution)/shard_map/ppermute | solution.py:230
  31.0 11.5 %collective-permute-start.8 = (bf16[8,5376]{1,0:T(8,128)(2,1)S(1)}, bf16[8,5376]{1,0:T(8,128)(2,1)S(1)}, u32[]{:S(2)}, u32[]{:S(2)}) collective-permute-start(bf16[8,5376]{1,0:T(8,128)(2,1)S(1)} %get-tuple-element.40), channel_id=1, source_target_pairs={{0,4},{1,5},{2,6},{3,7},{4,0},{5,1},{6,2},{7,3},{8,12},{9,13},{10,... | collective-permute-start | bytes 258056 | tf_op jit(solution)/shard_map/ppermute | solution.py:230
  33.6 10.0 %collective-permute-start.9 = (bf16[8,5376]{1,0:T(8,128)(2,1)S(1)}, bf16[8,5376]{1,0:T(8,128)(2,1)S(1)}, u32[]{:S(2)}, u32[]{:S(2)}) collective-permute-start(bf16[8,5376]{1,0:T(8,128)(2,1)S(1)} %get-tuple-element.41), channel_id=1, source_target_pairs={{0,6},{1,7},{2,4},{3,5},{4,2},{5,3},{6,0},{7,1},{8,14},{9,15},{10,... | collective-permute-start | bytes 258056 | tf_op jit(solution)/shard_map/ppermute | solution.py:230
  35.0 12.4 %collective-permute-start.10 = (bf16[8,5376]{1,0:T(8,128)(2,1)S(1)}, bf16[8,5376]{1,0:T(8,128)(2,1)S(1)}, u32[]{:S(2)}, u32[]{:S(2)}) collective-permute-start(bf16[8,5376]{1,0:T(8,128)(2,1)S(1)} %get-tuple-element.42), channel_id=1, source_target_pairs={{0,5},{1,4},{2,7},{3,6},{4,1},{5,0},{6,3},{7,2},{8,13},{9,12},{10,... | collective-permute-start | bytes 258056 | tf_op jit(solution)/shard_map/ppermute | solution.py:230
  36.6 10.8 %collective-permute-start.11 = (bf16[8,5376]{1,0:T(8,128)(2,1)S(1)}, bf16[8,5376]{1,0:T(8,128)(2,1)S(1)}, u32[]{:S(2)}, u32[]{:S(2)}) collective-permute-start(bf16[8,5376]{1,0:T(8,128)(2,1)S(1)} %get-tuple-element.43), channel_id=1, source_target_pairs={{0,7},{1,6},{2,5},{3,4},{4,3},{5,2},{6,1},{7,0},{8,15},{9,14},{10,... | collective-permute-start | bytes 258056 | tf_op jit(solution)/shard_map/ppermute | solution.py:230
  38.5 9.0 %collective-permute-start.12 = (bf16[8,5376]{1,0:T(8,128)(2,1)S(1)}, bf16[8,5376]{1,0:T(8,128)(2,1)S(1)}, u32[]{:S(2)}, u32[]{:S(2)}) collective-permute-start(bf16[8,5376]{1,0:T(8,128)(2,1)S(1)} %get-tuple-element.44), channel_id=1, source_target_pairs={{0,2},{1,3},{2,0},{3,1},{4,6},{5,7},{6,4},{7,5},{8,10},{9,11},{10,... | collective-permute-start | bytes 258056 | tf_op jit(solution)/shard_map/ppermute | solution.py:230
  42.6 5.6 %collective-permute-start.13 = (bf16[8,5376]{1,0:T(8,128)(2,1)S(1)}, bf16[8,5376]{1,0:T(8,128)(2,1)S(1)}, u32[]{:S(2)}, u32[]{:S(2)}) collective-permute-start(bf16[8,5376]{1,0:T(8,128)(2,1)S(1)} %get-tuple-element.45), channel_id=1, source_target_pairs={{0,3},{1,2},{2,1},{3,0},{4,7},{5,6},{6,5},{7,4},{8,11},{9,10},{10,... | collective-permute-start | bytes 258056 | tf_op jit(solution)/shard_map/ppermute | solution.py:230
  49.2 13.2 %all-to-all-start = ((bf16[32,2,768]{2,1,0:T(2,128)(2,1)}), bf16[32,2,768]{2,1,0:T(2,128)(2,1)S(1)}, u32[]{:S(2)}, u32[]{:S(2)}) async-start(bf16[32,2,768]{2,1,0:T(2,128)(2,1)} %get-tuple-element.52), calls=%async_computation | async-start | bytes 196608 | tf_op jit(solution)/shard_map/all_to_all | solution.py:237

commit v12 on v11

--- a/solution.py
+++ b/solution.py
@@ -129,7 +129,7 @@
 
 
 def peer_masks(peers):
-    return (0, 1, 4, 6, 5, 7, 2, 3) if peers == 8 else tuple(range(peers))
+    return (0, 4, 6, 1, 5, 2, 7, 3) if peers == 8 else tuple(range(peers))
 
 
 def block_peer(block, peers, me):
@@ -163,14 +163,18 @@
         kept, got = terms[2 * chunk : 2 * chunk + 2]
         total = (kept[...].astype(F32) + got[...].astype(F32)).astype(BF16)
         parts.append(dot(selector, total, (1, 0)))
-    label = jnp.sum(jnp.where(chosen, local + 1, 0), axis=1, keepdims=True) - 1
-    parts.append(jnp.broadcast_to(label.astype(F32), (slots, LANES)))
     if carries:
+        local = jnp.broadcast_to((local + 1).astype(F32), (16, rows)).astype(BF16)
+        labels = dot(local, selector, (1, 1))[:1] - 1.0
+        square = (slots, slots)
+        own = iota(square, 0) // capacity == iota(square, 1) // capacity
+        own = jnp.logical_and(own, iota(square, 0) % capacity == capacity - 1)
+        turn = (iota((slots, LANES), 0) % capacity == iota((slots, LANES), 1)).astype(F32)
+        extra = dot(jnp.where(own, labels, 0.0).astype(BF16), turn.astype(BF16), (1, 0))
         sums = refs[0][...]
         high = sums.astype(BF16).astype(F32)
         middle = (sums - high).astype(BF16).astype(F32)
         low = (sums - high - middle).astype(BF16).astype(F32)
-        extra = jnp.zeros((slots, LANES), F32)
         row = iota((slots, LANES), 0) % capacity
         peer = iota((slots, LANES), 0) // capacity
         if direct:
@@ -184,6 +188,9 @@
                     here = jnp.logical_and(peer == p, row == level * pieces + piece)
                     extra = jnp.where(here, line, extra)
         parts.append(extra)
+    else:
+        label = jnp.sum(jnp.where(chosen, local + 1, 0), axis=1, keepdims=True) - 1
+        parts.append(jnp.broadcast_to(label.astype(F32), (slots, LANES)))
     at = 0
     for part in parts:
         end = at + part.shape[1]
@@ -197,7 +204,7 @@
 
 def pack(terms, targets, me, sums, peers, capacity, direct, carries):
     rows = targets.shape[1]
-    width = sum(kept.shape[1] for kept, _ in terms) + (2 * LANES if carries else LANES)
+    width = sum(kept.shape[1] for kept, _ in terms) + LANES
     operands = [me, targets] + [x for pair in terms for x in pair] + ([sums] if carries else [])
     if direct:
         out_shape = [jax.ShapeDtypeStruct((capacity, width), BF16)] * peers
@@ -288,14 +295,22 @@
     routed = jnp.concatenate(pieces, axis=0) if len(pieces) > 1 else pieces[0]
     slots = routed.shape[0]
     per_token = routed.shape[1] // width
-    labels = routed[:, per_token * width : per_token * width + 1]
     columns = [routed[:, c * width : (c + 1) * width] for c in range(per_token)]
     held = jnp.concatenate(columns, axis=0).astype(BF16)
-    lanes = len(columns) * slots
-    lane = iota((slots, lanes), 1)
-    row_of_lane = jnp.sum(
-        jnp.where(lane % slots == iota((slots, lanes), 0), labels, 0.0), axis=0, keepdims=True
-    ).astype(jnp.int32)
+    lanes = per_token * slots
+    extra = routed[:, per_token * width :]
+    capacity = slots // peers
+    if carries:
+        place = iota((slots, LANES), 0) % capacity
+        labels = jnp.where(place == capacity - 1, extra, 0.0).astype(BF16)
+        turn = (iota((LANES, lanes), 0) == iota((LANES, lanes), 1) % capacity).astype(F32)
+        spread = dot(labels, turn.astype(BF16), (1, 0))
+        own = iota((slots, lanes), 0) // capacity == iota((slots, lanes), 1) % slots // capacity
+        row_of_lane = jnp.sum(jnp.where(own, spread, 0.0), axis=0, keepdims=True)
+    else:
+        own = iota((slots, lanes), 1) % slots == iota((slots, lanes), 0)
+        row_of_lane = jnp.sum(jnp.where(own, extra[:, :1], 0.0), axis=0, keepdims=True)
+    row_of_lane = row_of_lane.astype(jnp.int32)
     patch_of_lane = row_of_lane * len(columns) + iota((1, lanes), 1) // slots
     patch_of_lane = jnp.where(row_of_lane < 0, -1, patch_of_lane)
     chosen = patch_of_lane == iota((patches, lanes), 0)
@@ -305,15 +320,12 @@
     normed = inputs * inverse_rms
     row = jnp.sum(patch_grads * normed, axis=0, keepdims=True)
     if carries:
-        carried = routed[:, per_token * width + LANES :]
-        capacity = slots // peers
         copies, lines, line_width = share_ref.shape
         pieces = (lines * line_width - width) // LANES
-        place = iota((slots, LANES), 0) % capacity
         parts = [row]
         for piece in range(pieces):
             kept = jnp.logical_and(place % pieces == piece, place < 3 * pieces)
-            parts.append(jnp.sum(jnp.where(kept, carried, 0.0), axis=0, keepdims=True))
+            parts.append(jnp.sum(jnp.where(kept, extra, 0.0), axis=0, keepdims=True))
         row = jnp.concatenate(parts, axis=1)
         lines = [row[:, at : at + line_width] for at in range(0, row.shape[1], line_width)]
         row = jnp.broadcast_to(jnp.concatenate(lines, axis=0)[None], share_ref.shape)
@@ -408,7 +420,7 @@
     block = w_down.shape[1]
     width = patches.shape[2]
     pieces = block // peers // LANES
-    carries = pieces > 0 and 3 * pieces <= capacity and (width // LANES + pieces) % 2 == 0
+    carries = pieces > 0 and 3 * pieces < capacity and (width // LANES + pieces) % 2 == 0
 
     order = [0]
     while len(order) < images:

time: 64 us -> 62.8 us (0.981)
  starting transfers between devices: 23.3 us -> 22.5 us
    all_to_all x1, starting transfers between devices: 5.68 us -> 2.84 us  [exchange(): lax.all_to_all(x, axis, split_axis=0, concat_axis=0, tiled=True)]
    ppermute x14, starting transfers between devices: 17.7 us -> 19.6 us  [swap(): return lax.ppermute(x, axis, [(i, i ^ mask) for i in range(n)])]
  transfers between devices with their start and end apart: 15 -> 15, of which waited for: 6 -> 7; matrix products, arithmetic and copies ran while one was open for 0% -> 0% of each run, Pallas kernels for 10% -> 11%
where the time goes in v12:
time: 62.8 us; the launch traced here: 62.6 us
  starting transfers between devices  22.5 us (36%)
  waiting for transfers between devices  18.5 us (29%)
  Pallas kernels  11.4 us (18%)
  local copies, waits for them, and re-layouts  8.8 us (14%)
  between operations  0.85 us (1%)
  other arithmetic  0.63 us (1%)
    ppermute x14, starting transfers between devices, swap(): return lax.ppermute(x, axis, [(i, i ^ mask) for i in range(n)])  19.6 us
    ppermute x14, waiting for transfers between devices, swap(): return lax.ppermute(x, axis, [(i, i ^ mask) for i in range(n)])  14.4 us
    unnamed x18, local copies, waits for them, and re-layouts  7.65 us
    pallas_call x2, Pallas kernels, project(): pl.pallas_call(functools.partial(project_kernel, blocks, first, tile, wit...  6.05 us
    all_to_all x1, waiting for transfers between devices, exchange(): lax.all_to_all(x, axis, split_axis=0, concat_axis=0, tiled=True)  4.07 us
    all_to_all x1, starting transfers between devices, exchange(): lax.all_to_all(x, axis, split_axis=0, concat_axis=0, tiled=True)  2.84 us
    pallas_call x1, Pallas kernels, window_backward(): pl.pallas_call(window_kernel, out_shape=[shape] * 3, in_specs=vmem(6), ou...  2.38 us
  transfers between devices with their start and end apart: 15, of which 7 were waited for; matrix products, arithmetic and copies ran while one was open for 0% of the time, Pallas kernels for 11%

profile of v12, /device:TPU:0, one launch (start us, length us, event | category | flops | bytes accessed | tf_op | source)
XLA Modules:
  0.0 62.6 jit_solution(2833799588379003204)
XLA Ops:
  0.7 1.1 %dynamic-slice_bitcast_fusion = (bf16[32,2048]{1,0:T(8,128)(2,1)S(1)}, bf16[32,2048]{1,0:T(8,128)(2,1)S(1)}, bf16[32,2048]{1,0:T(8,128)(2,1)S(1)}, bf16[32,2048]{1,0:T(8,128)(2,1)S(1)}) fusion(bf16[1,32,8192]{2,1,0:T(8,128)(2,1)} %param.9, s32[]{:T(128)S(6)} %select_n.15, s32[]{:T(128)S(6)} %select_n.13, s32[]{:T(128)S(6)} %select_n.12, s32[]{:T(128)S(6)} %select_n.14), kind=kLoop, calls=%fused_computation.1 | loop fusion | bytes 1048592 | tf_op jit(solution)/shard_map/dynamic_slice | solution.py:431
  1.8 2.5 %collective-permute-start.2 = (bf16[32,2048]{1,0:T(8,128)(2,1)S(1)}, bf16[32,2048]{1,0:T(8,128)(2,1)S(1)}, u32[]{:S(2)}, u32[]{:S(2)}) collective-permute-start(bf16[32,2048]{1,0:T(8,128)(2,1)S(1)} %get-tuple-element.53), channel_id=1, source_target_pairs={{0,24},{8,16},{16,8},{24,0},{1,25},{9,17},{17,9},{25,1},{2,26},{10... | collective-permute-start | bytes 393224 | tf_op jit(solution)/shard_map/ppermute | solution.py:237
  4.3 0.6 %collective-permute-start = (bf16[32,2048]{1,0:T(8,128)(2,1)S(1)}, bf16[32,2048]{1,0:T(8,128)(2,1)S(1)}, u32[]{:S(2)}, u32[]{:S(2)}) collective-permute-start(bf16[32,2048]{1,0:T(8,128)(2,1)S(1)} %get-tuple-element.54), channel_id=1, source_target_pairs={{0,16},{8,24},{16,0},{24,8},{1,17},{9,25},{17,1},{25,9},{2,18},{10... | collective-permute-start | bytes 393224 | tf_op jit(solution)/shard_map/ppermute | solution.py:237
  4.9 0.0 collective-permute-start.1
  5.0 0.0 copy-start
  5.0 7.0 %copy-done = bf16[5120,2048]{1,0:T(8,128)(2,1)S(1)} copy-done((bf16[5120,2048]{1,0:T(8,128)(2,1)S(1)}, bf16[5120,2048]{1,0:T(8,128)(2,1)}, u32[]{:S(2)}) %copy-start) | copy-done | bytes 20971544
  11.9 0.0 collective-permute-done.2.refs_3_
  11.9 0.0 collective-permute-done.refs_1_
  11.9 0.0 collective-permute-done.1.refs_2_
  11.9 0.0 copy-start.5
  11.9 0.0 copy-start.7
  12.0 0.0 copy-start.1
  12.0 0.0 copy-start.2
  12.0 0.0 copy-start.3
  12.0 0.0 copy-start.6
  12.0 0.0 copy-start.4
  12.0 3.1 %project.2 = (bf16[64,2560]{1,0:T(8,128)(2,1)S(1)}, bf16[64,2560]{1,0:T(8,128)(2,1)S(1)}, f32[1,2048]{1,0:T(1,128)S(1)}) custom-call(bf16[32,2048]{1,0:T(8,128)(2,1)S(1)} %get-tuple-element.55.refs_0_, bf16[32,2048]{1,0:T(8,128)(2,1)S(1)} %collective-permute-done.refs_1_, bf16[32,2048]{1,0:T(8,128)(2,1)S(1)} %collective-permute-done.1.refs_2_, ...), custom_call_target="tpu_custom_call" | custom-call | flops 1342177280 | bytes 10485760 | tf_op jit(solution)/shard_map/project/pallas_call | solution.py:74
  15.1 0.5 collective-permute-start.3
  15.6 3.0 %project.3 = (bf16[64,2560]{1,0:T(8,128)(2,1)S(1)}, bf16[64,2560]{1,0:T(8,128)(2,1)S(1)}) custom-call(bf16[32,2048]{1,0:T(8,128)(2,1)S(1)} %get-tuple-element.55.refs_0_, bf16[32,2048]{1,0:T(8,128)(2,1)S(1)} %collective-permute-done.refs_1_, bf16[32,2048]{1,0:T(8,128)(2,1)S(1)} %collective-permute-done.1.refs_2_, ...), custom_call_target="tpu_custom_call" | custom-call | flops 1342177280 | bytes 10485760 | tf_op jit(solution)/shard_map/project/pallas_call | solution.py:74
  18.6 0.1 collective-permute-start.5
  18.7 0.0 collective-permute-done.3.got_ref
  18.7 0.1 halve.2
  18.8 1.8 %collective-permute-start.4 = (bf16[32,2560]{1,0:T(8,128)(2,1)S(1)}, bf16[32,2560]{1,0:T(8,128)(2,1)S(1)}, u32[]{:S(2)}, u32[]{:S(2)}) collective-permute-start(bf16[32,2560]{1,0:T(8,128)(2,1)S(1)} %get-tuple-element.32), channel_id=1, source_target_pairs={{0,16},{8,24},{16,0},{24,8},{1,17},{9,25},{17,1},{25,9},{2,18},{10... | collective-permute-start | bytes 491528 | tf_op jit(solution)/shard_map/ppermute | solution.py:237
  20.6 0.0 collective-permute-done.5.got_ref
  20.6 0.1 halve.3
  20.7 1.2 %collective-permute-start.6 = (bf16[32,2560]{1,0:T(8,128)(2,1)S(1)}, bf16[32,2560]{1,0:T(8,128)(2,1)S(1)}, u32[]{:S(2)}, u32[]{:S(2)}) collective-permute-start(bf16[32,2560]{1,0:T(8,128)(2,1)S(1)} %get-tuple-element.36), channel_id=1, source_target_pairs={{0,16},{8,24},{16,0},{24,8},{1,17},{9,25},{17,1},{25,9},{2,18},{10... | collective-permute-start | bytes 491528 | tf_op jit(solution)/shard_map/ppermute | solution.py:237
  21.9 4.0 %collective-permute-done.4.refs_1_ = bf16[32,2560]{1,0:T(8,128)(2,1)S(1)} collective-permute-done((bf16[32,2560]{1,0:T(8,128)(2,1)S(1)}, bf16[32,2560]{1,0:T(8,128)(2,1)S(1)}, u32[]{:S(2)}, u32[]{:S(2)}) %collective-permute-start.4) | collective-permute-done | bytes 163872 | tf_op jit(solution)/shard_map/ppermute | solution.py:237
  25.9 3.1 %collective-permute-done.6.refs_3_ = bf16[32,2560]{1,0:T(8,128)(2,1)S(1)} collective-permute-done((bf16[32,2560]{1,0:T(8,128)(2,1)S(1)}, bf16[32,2560]{1,0:T(8,128)(2,1)S(1)}, u32[]{:S(2)}, u32[]{:S(2)}) %collective-permute-start.6) | collective-permute-done | bytes 163872 | tf_op jit(solution)/shard_map/ppermute | solution.py:237
  29.0 0.0 copy-done.5
  29.0 0.7 %pack.1 = (bf16[8,5248]{1,0:T(8,128)(2,1)S(1)}, bf16[8,5248]{1,0:T(8,128)(2,1)S(1)}, bf16[8,5248]{1,0:T(8,128)(2,1)S(1)}, bf16[8,5248]{1,0:T(8,128)(2,1)S(1)}, b...) custom-call(s32[1]{0:T(128)} %bitcast.1.me_ref, ...), custom_call_target="tpu_custom_call" | custom-call | flops 21495808 | bytes 1679360 | tf_op jit(solution)/shard_map/pack/pallas_call | solution.py:213
  29.6 2.7 %collective-permute-start.7 = (bf16[8,5248]{1,0:T(8,128)(2,1)S(1)}, bf16[8,5248]{1,0:T(8,128)(2,1)S(1)}, u32[]{:S(2)}, u32[]{:S(2)}) collective-permute-start(bf16[8,5248]{1,0:T(8,128)(2,1)S(1)} %get-tuple-element.39), channel_id=1, source_target_pairs={{0,4},{1,5},{2,6},{3,7},{4,0},{5,1},{6,2},{7,3},{8,12},{9,13},{10,... | collective-permute-start | bytes 251912 | tf_op jit(solution)/shard_map/ppermute | solution.py:237
  32.3 1.4 %collective-permute-start.8 = (bf16[8,5248]{1,0:T(8,128)(2,1)S(1)}, bf16[8,5248]{1,0:T(8,128)(2,1)S(1)}, u32[]{:S(2)}, u32[]{:S(2)}) collective-permute-start(bf16[8,5248]{1,0:T(8,128)(2,1)S(1)} %get-tuple-element.40), channel_id=1, source_target_pairs={{0,6},{1,7},{2,4},{3,5},{4,2},{5,3},{6,0},{7,1},{8,14},{9,15},{10,... | collective-permute-start | bytes 251912 | tf_op jit(solution)/shard_map/ppermute | solution.py:237
  33.7 1.5 %collective-permute-start.9 = (bf16[8,5248]{1,0:T(8,128)(2,1)S(1)}, bf16[8,5248]{1,0:T(8,128)(2,1)S(1)}, u32[]{:S(2)}, u32[]{:S(2)}) collective-permute-start(bf16[8,5248]{1,0:T(8,128)(2,1)S(1)} %get-tuple-element.41), channel_id=1, source_target_pairs={{0,1},{1,0},{2,3},{3,2},{4,5},{5,4},{6,7},{7,6},{8,9},{9,8},{10,11... | collective-permute-start | bytes 251912 | tf_op jit(solution)/shard_map/ppermute | solution.py:237
  35.1 1.6 %collective-permute-start.10 = (bf16[8,5248]{1,0:T(8,128)(2,1)S(1)}, bf16[8,5248]{1,0:T(8,128)(2,1)S(1)}, u32[]{:S(2)}, u32[]{:S(2)}) collective-permute-start(bf16[8,5248]{1,0:T(8,128)(2,1)S(1)} %get-tuple-element.42), channel_id=1, source_target_pairs={{0,5},{1,4},{2,7},{3,6},{4,1},{5,0},{6,3},{7,2},{8,13},{9,12},{10,... | collective-permute-start | bytes 251912 | tf_op jit(solution)/shard_map/ppermute | solution.py:237
  36.8 1.4 %collective-permute-start.11 = (bf16[8,5248]{1,0:T(8,128)(2,1)S(1)}, bf16[8,5248]{1,0:T(8,128)(2,1)S(1)}, u32[]{:S(2)}, u32[]{:S(2)}) collective-permute-start(bf16[8,5248]{1,0:T(8,128)(2,1)S(1)} %get-tuple-element.43), channel_id=1, source_target_pairs={{0,2},{1,3},{2,0},{3,1},{4,6},{5,7},{6,4},{7,5},{8,10},{9,11},{10,... | collective-permute-start | bytes 251912 | tf_op jit(solution)/shard_map/ppermute | solution.py:237
  38.2 2.0 %collective-permute-done.7.refs_1_ = bf16[8,5248]{1,0:T(8,128)(2,1)S(1)} collective-permute-done((bf16[8,5248]{1,0:T(8,128)(2,1)S(1)}, bf16[8,5248]{1,0:T(8,128)(2,1)S(1)}, u32[]{:S(2)}, u32[]{:S(2)}) %collective-permute-start.7) | collective-permute-done | bytes 84000 | tf_op jit(solution)/shard_map/ppermute | solution.py:237
  40.1 4.3 %collective-permute-start.12 = (bf16[8,5248]{1,0:T(8,128)(2,1)S(1)}, bf16[8,5248]{1,0:T(8,128)(2,1)S(1)}, u32[]{:S(2)}, u32[]{:S(2)}) collective-permute-start(bf16[8,5248]{1,0:T(8,128)(2,1)S(1)} %get-tuple-element.44), channel_id=1, source_target_pairs={{0,7},{1,6},{2,5},{3,4},{4,3},{5,2},{6,1},{7,0},{8,15},{9,14},{10,... | collective-permute-start | bytes 251912 | tf_op jit(solution)/shard_map/ppermute | solution.py:237
  44.4 0.0 collective-permute-done.8.refs_2_
  44.4 0.0 collective-permute-start.13
  44.5 0.0 copy-done.7
  44.5 0.0 collective-permute-done.9.refs_3_
  44.5 1.3 %collective-permute-done.10.refs_4_ = bf16[8,5248]{1,0:T(8,128)(2,1)S(1)} collective-permute-done((bf16[8,5248]{1,0:T(8,128)(2,1)S(1)}, bf16[8,5248]{1,0:T(8,128)(2,1)S(1)}, u32[]{:S(2)}, u32[]{:S(2)}) %collective-permute-start.10) | collective-permute-done | bytes 84000 | tf_op jit(solution)/shard_map/ppermute | solution.py:237
  45.8 0.0 collective-permute-done.11.refs_5_
  45.8 1.7 %collective-permute-done.12.refs_6_ = bf16[8,5248]{1,0:T(8,128)(2,1)S(1)} collective-permute-done((bf16[8,5248]{1,0:T(8,128)(2,1)S(1)}, bf16[8,5248]{1,0:T(8,128)(2,1)S(1)}, u32[]{:S(2)}, u32[]{:S(2)}) %collective-permute-start.12) | collective-permute-done | bytes 84000 | tf_op jit(solution)/shard_map/ppermute | solution.py:237
  47.5 2.3 %collective-permute-done.13.refs_7_ = bf16[8,5248]{1,0:T(8,128)(2,1)S(1)} collective-permute-done((bf16[8,5248]{1,0:T(8,128)(2,1)S(1)}, bf16[8,5248]{1,0:T(8,128)(2,1)S(1)}, u32[]{:S(2)}, u32[]{:S(2)}) %collective-permute-start.13) | collective-permute-done | bytes 84000 | tf_op jit(solution)/shard_map/ppermute | solution.py:237
  49.8 0.0 copy-done.1
  49.8 1.1 %norm.1 = (bf16[128,1280]{1,0:T(8,128)(2,1)S(1)}, bf16[32,2,768]{2,1,0:T(2,128)(2,1)}) custom-call(bf16[128,1280]{1,0:T(8,128)(2,1)S(1)} %bitcast.23, f32[1,1280]{1,0:T(1,128)S(1)} %broadcast_in_dim.12.gain_ref, bf16[8,5248]{1,0:T(8,128)(2,1)S(1)} %get-tuple-element.38.refs_0_, bf16[8,5248]{1,0:T(8,128)(2,1)S(1)} %collective-permute-done.7.refs_1_, ...), custom_call_target="tpu_custom_call" | custom-call | flops 85983232 | bytes 1327104 | tf_op jit(solution)/shard_map/norm/pallas_call | solution.py:342
  50.9 2.8 %all-to-all-start = ((bf16[32,2,768]{2,1,0:T(2,128)(2,1)}), bf16[32,2,768]{2,1,0:T(2,128)(2,1)S(1)}, u32[]{:S(2)}, u32[]{:S(2)}) async-start(bf16[32,2,768]{2,1,0:T(2,128)(2,1)} %get-tuple-element.52), calls=%async_computation | async-start | bytes 196608 | tf_op jit(solution)/shard_map/all_to_all | solution.py:244
  53.8 0.0 copy-done.2
  53.8 0.0 copy-done.3
  53.8 0.0 copy-done.6
  53.8 1.1 %probs.1 = (f32[16,128,128]{2,1,0:T(8,128)S(1)}, f32[16,128,128]{2,1,0:T(8,128)S(1)}) custom-call(bf16[128,1280]{1,0:T(8,128)(2,1)S(1)} %bitcast.24, bf16[128,1280]{1,0:T(8,128)(2,1)S(1)} %bitcast.26, s32[1,32]{1,0:T(1,128)S(1)} %bitcast.29), custom_call_target="tpu_custom_call" | custom-call | flops 268435456 | bytes 2097152 | tf_op jit(solution)/shard_map/probs/pallas_call | solution.py:276
  54.9 0.0 copy-done.4
  54.9 2.4 %window.1 = (bf16[128,1280]{1,0:T(8,128)(2,1)}, bf16[128,1280]{1,0:T(8,128)(2,1)}, bf16[128,1280]{1,0:T(8,128)(2,1)}) custom-call(bf16[128,1280]{1,0:T(8,128)(2,1)S(1)} %get-tuple-element.46.g_ref, bf16[128,1280]{1,0:T(8,128)(2,1)S(1)} %bitcast.25, bf16[128,1280]{1,0:T(8,128)(2,1)S(1)} %bitcast.27, bf16[128,1280]{1,0:T(8,128)(2,1)S(1)} %bitcast.28, ...), custom_call_target="tpu_custom_call" | custom-call | flops 335544320 | bytes 4390912 | tf_op jit(solution)/shard_map/window/pallas_call | solution.py:398
  57.3 4.1 %all-to-all-done = bf16[32,2,768]{2,1,0:T(2,128)(2,1)S(1)} async-done(((bf16[32,2,768]{2,1,0:T(2,128)(2,1)}), bf16[32,2,768]{2,1,0:T(2,128)(2,1)S(1)}, u32[]{:S(2)}, u32[]{:S(2)}) %all-to-all-start) | async-done | bytes 98336 | tf_op jit(solution)/shard_map/all_to_all | solution.py:244
  61.4 0.6 %copy.15 = f32[4,2,8,128]{3,1,2,0:T(2,128)} copy(f32[4,2,8,128]{3,2,1,0:T(8,128)S(1)} %fusion) | data formatting | bytes 65536
  62.0 0.6 broadcast_multiply_fusion
  (5 shorter events, 0.0 us)
Async XLA Ops:
  1.8 10.1 %collective-permute-start.2 = (bf16[32,2048]{1,0:T(8,128)(2,1)S(1)}, bf16[32,2048]{1,0:T(8,128)(2,1)S(1)}, u32[]{:S(2)}, u32[]{:S(2)}) collective-permute-start(bf16[32,2048]{1,0:T(8,128)(2,1)S(1)} %get-tuple-element.53), channel_id=1, source_target_pairs={{0,24},{8,16},{16,8},{24,0},{1,25},{9,17},{17,9},{25,1},{2,26},{10... | collective-permute-start | bytes 393224 | tf_op jit(solution)/shard_map/ppermute | solution.py:237
  4.3 7.7 %collective-permute-start = (bf16[32,2048]{1,0:T(8,128)(2,1)S(1)}, bf16[32,2048]{1,0:T(8,128)(2,1)S(1)}, u32[]{:S(2)}, u32[]{:S(2)}) collective-permute-start(bf16[32,2048]{1,0:T(8,128)(2,1)S(1)} %get-tuple-element.54), channel_id=1, source_target_pairs={{0,16},{8,24},{16,0},{24,8},{1,17},{9,25},{17,1},{25,9},{2,18},{10... | collective-permute-start | bytes 393224 | tf_op jit(solution)/shard_map/ppermute | solution.py:237
  4.9 7.0 %collective-permute-start.1 = (bf16[32,2048]{1,0:T(8,128)(2,1)S(1)}, bf16[32,2048]{1,0:T(8,128)(2,1)S(1)}, u32[]{:S(2)}, u32[]{:S(2)}) collective-permute-start(bf16[32,2048]{1,0:T(8,128)(2,1)S(1)} %get-tuple-element.56), channel_id=1, source_target_pairs={{0,8},{8,0},{16,24},{24,16},{1,9},{9,1},{17,25},{25,17},{2,10},{10... | collective-permute-start | bytes 393224 | tf_op jit(solution)/shard_map/ppermute | solution.py:237
  5.0 7.0 %copy-start = (bf16[5120,2048]{1,0:T(8,128)(2,1)S(1)}, bf16[5120,2048]{1,0:T(8,128)(2,1)}, u32[]{:S(2)}) copy-start(bf16[5120,2048]{1,0:T(8,128)(2,1)} %refs_4_.3) | copy-start | bytes 62914564
  11.9 17.0 %copy-start.5 = (s32[1,32]{1,0:T(1,128)S(1)}, s32[1,32]{1,0:T(1,128)}, u32[]{:S(2)}) copy-start(s32[1,32]{1,0:T(1,128)} %targets_ref.1) | copy-start | bytes 388
  11.9 32.5 %copy-start.7 = (f32[1280]{0:T(1024)S(1)}, f32[1280]{0:T(1024)}, u32[]{:S(2)}) copy-start(f32[1280]{0:T(1024)} %param.12) | copy-start | bytes 15364
  12.0 37.9 %copy-start.1 = (bf16[1,128,1280]{2,1,0:T(8,128)(2,1)S(1)}, bf16[1,128,1280]{2,1,0:T(8,128)(2,1)}, u32[]{:S(2)}) copy-start(bf16[1,128,1280]{2,1,0:T(8,128)(2,1)} %param.11) | copy-start | bytes 983044
  12.0 41.8 %copy-start.2 = (bf16[1,128,1280]{2,1,0:T(8,128)(2,1)S(1)}, bf16[1,128,1280]{2,1,0:T(8,128)(2,1)}, u32[]{:S(2)}) copy-start(bf16[1,128,1280]{2,1,0:T(8,128)(2,1)} %param.14) | copy-start | bytes 983044
  12.0 41.8 %copy-start.3 = (bf16[1,128,1280]{2,1,0:T(8,128)(2,1)S(1)}, bf16[1,128,1280]{2,1,0:T(8,128)(2,1)}, u32[]{:S(2)}) copy-start(bf16[1,128,1280]{2,1,0:T(8,128)(2,1)} %param.15) | copy-start | bytes 983044
  12.0 41.8 %copy-start.6 = (s32[1,1,32]{2,1,0:T(1,128)S(1)}, s32[1,1,32]{2,1,0:T(1,128)}, u32[]{:S(2)}) copy-start(s32[1,1,32]{2,1,0:T(1,128)} %param.17) | copy-start | bytes 388
  12.0 42.9 %copy-start.4 = (bf16[1,128,1280]{2,1,0:T(8,128)(2,1)S(1)}, bf16[1,128,1280]{2,1,0:T(8,128)(2,1)}, u32[]{:S(2)}) copy-start(bf16[1,128,1280]{2,1,0:T(8,128)(2,1)} %param.16) | copy-start | bytes 983044
  15.1 3.6 %collective-permute-start.3 = (bf16[64,2560]{1,0:T(8,128)(2,1)S(1)}, bf16[64,2560]{1,0:T(8,128)(2,1)S(1)}, u32[]{:S(2)}, u32[]{:S(2)}) collective-permute-start(bf16[64,2560]{1,0:T(8,128)(2,1)S(1)} %get-tuple-element.30), channel_id=1, source_target_pairs={{0,8},{8,0},{16,24},{24,16},{1,9},{9,1},{17,25},{25,17},{2,10},{10... | collective-permute-start | bytes 983048 | tf_op jit(solution)/shard_map/ppermute | solution.py:237
  18.6 2.0 %collective-permute-start.5 = (bf16[64,2560]{1,0:T(8,128)(2,1)S(1)}, bf16[64,2560]{1,0:T(8,128)(2,1)S(1)}, u32[]{:S(2)}, u32[]{:S(2)}) collective-permute-start(bf16[64,2560]{1,0:T(8,128)(2,1)S(1)} %get-tuple-element.34), channel_id=1, source_target_pairs={{0,8},{8,0},{16,24},{24,16},{1,9},{9,1},{17,25},{25,17},{2,10},{10... | collective-permute-start | bytes 983048 | tf_op jit(solution)/shard_map/ppermute | solution.py:237
  18.8 7.1 %collective-permute-start.4 = (bf16[32,2560]{1,0:T(8,128)(2,1)S(1)}, bf16[32,2560]{1,0:T(8,128)(2,1)S(1)}, u32[]{:S(2)}, u32[]{:S(2)}) collective-permute-start(bf16[32,2560]{1,0:T(8,128)(2,1)S(1)} %get-tuple-element.32), channel_id=1, source_target_pairs={{0,16},{8,24},{16,0},{24,8},{1,17},{9,25},{17,1},{25,9},{2,18},{10... | collective-permute-start | bytes 491528 | tf_op jit(solution)/shard_map/ppermute | solution.py:237
  20.7 8.3 %collective-permute-start.6 = (bf16[32,2560]{1,0:T(8,128)(2,1)S(1)}, bf16[32,2560]{1,0:T(8,128)(2,1)S(1)}, u32[]{:S(2)}, u32[]{:S(2)}) collective-permute-start(bf16[32,2560]{1,0:T(8,128)(2,1)S(1)} %get-tuple-element.36), channel_id=1, source_target_pairs={{0,16},{8,24},{16,0},{24,8},{1,17},{9,25},{17,1},{25,9},{2,18},{10... | collective-permute-start | bytes 491528 | tf_op jit(solution)/shard_map/ppermute | solution.py:237
  29.6 10.5 %collective-permute-start.7 = (bf16[8,5248]{1,0:T(8,128)(2,1)S(1)}, bf16[8,5248]{1,0:T(8,128)(2,1)S(1)}, u32[]{:S(2)}, u32[]{:S(2)}) collective-permute-start(bf16[8,5248]{1,0:T(8,128)(2,1)S(1)} %get-tuple-element.39), channel_id=1, source_target_pairs={{0,4},{1,5},{2,6},{3,7},{4,0},{5,1},{6,2},{7,3},{8,12},{9,13},{10,... | collective-permute-start | bytes 251912 | tf_op jit(solution)/shard_map/ppermute | solution.py:237
  32.3 12.1 %collective-permute-start.8 = (bf16[8,5248]{1,0:T(8,128)(2,1)S(1)}, bf16[8,5248]{1,0:T(8,128)(2,1)S(1)}, u32[]{:S(2)}, u32[]{:S(2)}) collective-permute-start(bf16[8,5248]{1,0:T(8,128)(2,1)S(1)} %get-tuple-element.40), channel_id=1, source_target_pairs={{0,6},{1,7},{2,4},{3,5},{4,2},{5,3},{6,0},{7,1},{8,14},{9,15},{10,... | collective-permute-start | bytes 251912 | tf_op jit(solution)/shard_map/ppermute | solution.py:237
  33.7 10.8 %collective-permute-start.9 = (bf16[8,5248]{1,0:T(8,128)(2,1)S(1)}, bf16[8,5248]{1,0:T(8,128)(2,1)S(1)}, u32[]{:S(2)}, u32[]{:S(2)}) collective-permute-start(bf16[8,5248]{1,0:T(8,128)(2,1)S(1)} %get-tuple-element.41), channel_id=1, source_target_pairs={{0,1},{1,0},{2,3},{3,2},{4,5},{5,4},{6,7},{7,6},{8,9},{9,8},{10,11... | collective-permute-start | bytes 251912 | tf_op jit(solution)/shard_map/ppermute | solution.py:237
  35.1 10.7 %collective-permute-start.10 = (bf16[8,5248]{1,0:T(8,128)(2,1)S(1)}, bf16[8,5248]{1,0:T(8,128)(2,1)S(1)}, u32[]{:S(2)}, u32[]{:S(2)}) collective-permute-start(bf16[8,5248]{1,0:T(8,128)(2,1)S(1)} %get-tuple-element.42), channel_id=1, source_target_pairs={{0,5},{1,4},{2,7},{3,6},{4,1},{5,0},{6,3},{7,2},{8,13},{9,12},{10,... | collective-permute-start | bytes 251912 | tf_op jit(solution)/shard_map/ppermute | solution.py:237
  36.8 9.0 %collective-permute-start.11 = (bf16[8,5248]{1,0:T(8,128)(2,1)S(1)}, bf16[8,5248]{1,0:T(8,128)(2,1)S(1)}, u32[]{:S(2)}, u32[]{:S(2)}) collective-permute-start(bf16[8,5248]{1,0:T(8,128)(2,1)S(1)} %get-tuple-element.43), channel_id=1, source_target_pairs={{0,2},{1,3},{2,0},{3,1},{4,6},{5,7},{6,4},{7,5},{8,10},{9,11},{10,... | collective-permute-start | bytes 251912 | tf_op jit(solution)/shard_map/ppermute | solution.py:237
  40.1 7.4 %collective-permute-start.12 = (bf16[8,5248]{1,0:T(8,128)(2,1)S(1)}, bf16[8,5248]{1,0:T(8,128)(2,1)S(1)}, u32[]{:S(2)}, u32[]{:S(2)}) collective-permute-start(bf16[8,5248]{1,0:T(8,128)(2,1)S(1)} %get-tuple-element.44), channel_id=1, source_target_pairs={{0,7},{1,6},{2,5},{3,4},{4,3},{5,2},{6,1},{7,0},{8,15},{9,14},{10,... | collective-permute-start | bytes 251912 | tf_op jit(solution)/shard_map/ppermute | solution.py:237
  44.4 5.4 %collective-permute-start.13 = (bf16[8,5248]{1,0:T(8,128)(2,1)S(1)}, bf16[8,5248]{1,0:T(8,128)(2,1)S(1)}, u32[]{:S(2)}, u32[]{:S(2)}) collective-permute-start(bf16[8,5248]{1,0:T(8,128)(2,1)S(1)} %get-tuple-element.45), channel_id=1, source_target_pairs={{0,3},{1,2},{2,1},{3,0},{4,7},{5,6},{6,5},{7,4},{8,11},{9,10},{10,... | collective-permute-start | bytes 251912 | tf_op jit(solution)/shard_map/ppermute | solution.py:237
  50.9 10.4 %all-to-all-start = ((bf16[32,2,768]{2,1,0:T(2,128)(2,1)}), bf16[32,2,768]{2,1,0:T(2,128)(2,1)S(1)}, u32[]{:S(2)}, u32[]{:S(2)}) async-start(bf16[32,2,768]{2,1,0:T(2,128)(2,1)} %get-tuple-element.52), calls=%async_computation | async-start | bytes 196608 | tf_op jit(solution)/shard_map/all_to_all | solution.py:244

commit v13 on v12

--- a/solution.py
+++ b/solution.py
@@ -129,19 +129,25 @@
 
 
 def peer_masks(peers):
-    return (0, 4, 6, 1, 5, 2, 7, 3) if peers == 8 else tuple(range(peers))
-
-
-def block_peer(block, peers, me):
+    return (0, 5, 7, 4, 6, 1, 2, 3) if peers == 8 else tuple(range(peers))
+
+
+def early_masks(peers):
+    return (4, 6) if peers == 8 else ()
+
+
+def block_peer(block, masks, me):
     peer = jnp.zeros_like(block)
-    for place, mask in enumerate(peer_masks(peers)):
+    for place, mask in enumerate(masks):
         peer = jnp.where(block == place, mask ^ me, peer)
     return peer
 
 
-def pack_kernel(peers, capacity, chunks, direct, carries, me_ref, targets_ref, *refs):
-    terms, refs = refs[: 2 * chunks], refs[2 * chunks :]
-    outs = refs[1:] if carries else refs
+def pack_kernel(
+    peers, capacity, chunks, masks, starts, direct, carries, after, me_ref, *refs
+):
+    targets_ref, terms, refs = refs[0], refs[1 : 2 * chunks + 1], refs[2 * chunks + 1 :]
+    outs = refs[after + carries :]
     targets = targets_ref[...]
     rows = targets.shape[1]
     dest = targets // rows
@@ -151,18 +157,14 @@
     )
     same_before = jnp.logical_and(dest_column == dest, iota((rows, rows), 0) < iota((rows, rows), 1))
     rank = jnp.sum(same_before.astype(jnp.int32), axis=0, keepdims=True)
-    slots = peers * capacity
+    slots = len(masks) * capacity
     slot = iota((slots, rows), 0)
     holder = slot // capacity
     if direct:
-        holder = block_peer(holder, peers, me_ref[0])
+        holder = block_peer(holder, masks, me_ref[0])
     chosen = jnp.logical_and(dest == holder, rank == slot % capacity)
     selector = chosen.astype(F32).astype(BF16)
     parts = []
-    for chunk in range(chunks):
-        kept, got = terms[2 * chunk : 2 * chunk + 2]
-        total = (kept[...].astype(F32) + got[...].astype(F32)).astype(BF16)
-        parts.append(dot(selector, total, (1, 0)))
     if carries:
         local = jnp.broadcast_to((local + 1).astype(F32), (16, rows)).astype(BF16)
         labels = dot(local, selector, (1, 1))[:1] - 1.0
@@ -178,7 +180,7 @@
         row = iota((slots, LANES), 0) % capacity
         peer = iota((slots, LANES), 0) // capacity
         if direct:
-            peer = block_peer(peer, peers, me_ref[0])
+            peer = block_peer(peer, masks, me_ref[0])
         pieces = sums.shape[1] // peers // LANES
         for p in range(peers):
             for level, values in enumerate((high, middle, low)):
@@ -191,45 +193,52 @@
     else:
         label = jnp.sum(jnp.where(chosen, local + 1, 0), axis=1, keepdims=True) - 1
         parts.append(jnp.broadcast_to(label.astype(F32), (slots, LANES)))
-    at = 0
-    for part in parts:
-        end = at + part.shape[1]
-        if direct:
-            for m in range(peers):
-                outs[m][:, at:end] = part[m * capacity : (m + 1) * capacity].astype(BF16)
-        else:
-            outs[0][:, at:end] = part.astype(BF16)
-        at = end
-
-
-def pack(terms, targets, me, sums, peers, capacity, direct, carries):
+    for chunk in range(chunks):
+        kept, got = terms[2 * chunk : 2 * chunk + 2]
+        total = (kept[...].astype(F32) + got[...].astype(F32)).astype(BF16)
+        parts.append(dot(selector, total, (1, 0)))
+    if not direct:
+        masks, starts, capacity = masks[:1], starts[:1], slots
+    for block, start in enumerate(starts):
+        at = 0
+        for part in parts[start:]:
+            end = at + part.shape[1]
+            rows_of_block = part[block * capacity : (block + 1) * capacity]
+            outs[block][:, at:end] = rows_of_block.astype(BF16)
+            at = end
+
+
+def pack(terms, targets, me, sums, after, peers, capacity, masks, starts, direct):
     rows = targets.shape[1]
-    width = sum(kept.shape[1] for kept, _ in terms) + LANES
+    carries = sums is not None
+    widths = [LANES] + [kept.shape[1] for kept, _ in terms]
     operands = [me, targets] + [x for pair in terms for x in pair] + ([sums] if carries else [])
+    blocks = len(operands) - 1
+    operands += after
     if direct:
-        out_shape = [jax.ShapeDtypeStruct((capacity, width), BF16)] * peers
+        out_shape = [
+            jax.ShapeDtypeStruct((capacity, sum(widths[start:])), BF16) for start in starts
+        ]
     else:
-        out_shape = [jax.ShapeDtypeStruct((peers * capacity, width), BF16)]
-    return pl.pallas_call(
-        functools.partial(pack_kernel, peers, capacity, len(terms), direct, carries),
+        out_shape = [jax.ShapeDtypeStruct((peers * capacity, sum(widths)), BF16)]
+    return pl.pallas_call(
+        functools.partial(
+            pack_kernel, peers, capacity, len(terms), masks, starts, direct, carries,
+            len(after),
+        ),
         out_shape=out_shape,
-        in_specs=[pl.BlockSpec(memory_space=pltpu.SMEM)] + vmem(len(operands) - 1),
+        in_specs=[pl.BlockSpec(memory_space=pltpu.SMEM)]
+        + vmem(blocks)
+        + [pl.BlockSpec(memory_space=pl.ANY)] * len(after),
         out_specs=vmem(len(out_shape)),
         compiler_params=pltpu.CompilerParams(vmem_limit_bytes=VMEM_BYTES),
         cost_estimate=pl.CostEstimate(
-            flops=2 * rows * peers * capacity * width,
-            bytes_accessed=(6 * rows + 2 * peers * capacity) * width,
+            flops=2 * rows * len(masks) * capacity * sum(widths),
+            bytes_accessed=(6 * rows + 2 * len(masks) * capacity) * sum(widths),
             transcendentals=0,
         ),
         name="pack",
     )(*operands)
-
-
-def route(packed, peers, direct):
-    if not direct:
-        return [exchange(packed[0], "seq", peers)]
-    masks = peer_masks(peers)
-    return [swap(block, "seq", mask) if mask else block for block, mask in zip(packed, masks)]
 
 
 def swap(x, axis, mask):
@@ -288,17 +297,20 @@
     )(queries, keys, ids)
 
 
-def norm_kernel(peers, carries, patches_ref, gain_ref, *refs):
+def norm_kernel(peers, early, carries, patches_ref, gain_ref, *refs):
     pieces, (out_ref, share_ref) = refs[:-2], refs[-2:]
     patches, width = patches_ref.shape
     pieces = [ref[...].astype(F32) for ref in pieces]
+    pieces, begun = pieces[len(early) :], pieces[: len(early)]
+    for place, begin in zip(early, begun):
+        pieces[place] = jnp.concatenate([begin, pieces[place]], axis=1)
     routed = jnp.concatenate(pieces, axis=0) if len(pieces) > 1 else pieces[0]
     slots = routed.shape[0]
     per_token = routed.shape[1] // width
-    columns = [routed[:, c * width : (c + 1) * width] for c in range(per_token)]
+    columns = [routed[:, LANES + c * width : LANES + (c + 1) * width] for c in range(per_token)]
     held = jnp.concatenate(columns, axis=0).astype(BF16)
     lanes = per_token * slots
-    extra = routed[:, per_token * width :]
+    extra = routed[:, :LANES]
     capacity = slots // peers
     if carries:
         place = iota((slots, LANES), 0) % capacity
@@ -336,11 +348,11 @@
     ).astype(BF16)
 
 
-def norm_backward(received, peers, patches, gain, share):
+def norm_backward(received, peers, early, patches, gain, share):
     count, width = patches.shape
     routed = sum(x.size for x in received)
     return pl.pallas_call(
-        functools.partial(norm_kernel, peers, len(share.shape) == 3),
+        functools.partial(norm_kernel, peers, early, len(share.shape) == 3),
         out_shape=[jax.ShapeDtypeStruct((count, width), BF16), share],
         in_specs=vmem(2 + len(received)),
         out_specs=vmem(2),
@@ -446,14 +458,34 @@
             kept, sent = halve(kept, swap(sent, "img", mask))
             mask *= 2
         terms.append((kept, swap(sent, "img", mask)))
-    packed = pack(terms, token_target, me.reshape(1), bias_part, peers, capacity, direct, carries)
-    routed = route(packed, peers, direct)
+    masks = peer_masks(peers)
+    early = early_masks(peers) if direct else ()
+    places = tuple(masks.index(mask) for mask in early)
+    place = me.reshape(1)
+    sums = bias_part if carries else None
+    begun = []
+    if early:
+        begun = list(
+            pack(
+                terms[:1], token_target, place, sums, [], peers, capacity, early,
+                (0,) * len(early), direct,
+            )
+        )
+    starts = tuple(2 if mask in early else 0 for mask in masks)
+    packed = pack(
+        terms, token_target, place, sums, begun, peers, capacity, masks, starts, direct
+    )
+    if direct:
+        routed = [swap(x, "seq", mask) if mask else x for x, mask in zip(packed, masks)]
+    else:
+        routed = [exchange(packed[0], "seq", peers)]
+    routed = [swap(block, "seq", mask) for block, mask in zip(begun, early)] + routed
 
     if carries:
         share = jax.ShapeDtypeStruct((devices, 2, (width + pieces * LANES) // 2), BF16)
     else:
         share = jax.ShapeDtypeStruct((1, width), F32)
-    out_grads, shared = norm_backward(routed, peers, patches[0], gain[None], share)
+    out_grads, shared = norm_backward(routed, peers, places, patches[0], gain[None], share)
     if carries:
         shared = exchange(shared, ("img", "seq"), devices).astype(F32).reshape(devices, -1)
         gain_total = jnp.sum(shared[:, :width], axis=0)

time: 62.8 us -> 62.5 us (level)
  waiting for transfers between devices: 18.5 us -> 11.7 us
  starting transfers between devices: 22.5 us -> 28.6 us
    ppermute x14 -> x16, waiting for transfers between devices: 14.4 us -> 7.6 us  [swap(): return lax.ppermute(x, axis, [(i, i ^ mask) for i in range(n)])]
    ppermute x14 -> x16, starting transfers between devices: 19.6 us -> 24.8 us  [swap(): return lax.ppermute(x, axis, [(i, i ^ mask) for i in range(n)])]
    all_to_all x1, starting transfers between devices: 2.84 us -> 3.77 us  [exchange(): lax.all_to_all(x, axis, split_axis=0, concat_axis=0, tiled=True)]
  transfers between devices with their start and end apart: 15 -> 17, of which waited for: 7 -> 5; matrix products, arithmetic and copies ran while one was open for 0% -> 0% of each run, Pallas kernels for 11% -> 12%
where the time goes in v13:
time: 62.5 us; the launch traced here: 62.3 us
  starting transfers between devices  28.6 us (46%)
  Pallas kernels  11.7 us (19%)
  waiting for transfers between devices  11.7 us (19%)
  local copies, waits for them, and re-layouts  8.8 us (14%)
  between operations  0.85 us (1%)
  other arithmetic  0.63 us (1%)
    ppermute x16, starting transfers between devices, swap(): return lax.ppermute(x, axis, [(i, i ^ mask) for i in range(n)])  24.8 us
    unnamed x18, local copies, waits for them, and re-layouts  7.65 us
    ppermute x16, waiting for transfers between devices, swap(): return lax.ppermute(x, axis, [(i, i ^ mask) for i in range(n)])  7.6 us
    pallas_call x2, Pallas kernels, project(): pl.pallas_call(functools.partial(project_kernel, blocks, first, tile, wit...  6.05 us
    all_to_all x1, waiting for transfers between devices, exchange(): lax.all_to_all(x, axis, split_axis=0, concat_axis=0, tiled=True)  4.07 us
    all_to_all x1, starting transfers between devices, exchange(): lax.all_to_all(x, axis, split_axis=0, concat_axis=0, tiled=True)  3.77 us
    pallas_call x1, Pallas kernels, window_backward(): pl.pallas_call(window_kernel, out_shape=[shape] * 3, in_specs=vmem(6), ou...  2.38 us
  transfers between devices with their start and end apart: 17, of which 5 were waited for; matrix products, arithmetic and copies ran while one was open for 0% of the time, Pallas kernels for 12%

profile of v13, /device:TPU:0, one launch (start us, length us, event | category | flops | bytes accessed | tf_op | source)
XLA Modules:
  0.0 62.3 jit_solution(9046483426225400046)
XLA Ops:
  0.7 1.1 %dynamic-slice_bitcast_fusion = (bf16[32,2048]{1,0:T(8,128)(2,1)S(1)}, bf16[32,2048]{1,0:T(8,128)(2,1)S(1)}, bf16[32,2048]{1,0:T(8,128)(2,1)S(1)}, bf16[32,2048]{1,0:T(8,128)(2,1)S(1)}) fusion(bf16[1,32,8192]{2,1,0:T(8,128)(2,1)} %param.9, s32[]{:T(128)S(6)} %select_n.15, s32[]{:T(128)S(6)} %select_n.13, s32[]{:T(128)S(6)} %select_n.12, s32[]{:T(128)S(6)} %select_n.14), kind=kLoop, calls=%fused_computation.1 | loop fusion | bytes 1048592 | tf_op jit(solution)/shard_map/dynamic_slice | solution.py:443
  1.8 2.5 %collective-permute-start.2 = (bf16[32,2048]{1,0:T(8,128)(2,1)S(1)}, bf16[32,2048]{1,0:T(8,128)(2,1)S(1)}, u32[]{:S(2)}, u32[]{:S(2)}) collective-permute-start(bf16[32,2048]{1,0:T(8,128)(2,1)S(1)} %get-tuple-element.57), channel_id=1, source_target_pairs={{0,24},{8,16},{16,8},{24,0},{1,25},{9,17},{17,9},{25,1},{2,26},{10... | collective-permute-start | bytes 393224 | tf_op jit(solution)/shard_map/ppermute | solution.py:246
  4.3 0.6 %collective-permute-start = (bf16[32,2048]{1,0:T(8,128)(2,1)S(1)}, bf16[32,2048]{1,0:T(8,128)(2,1)S(1)}, u32[]{:S(2)}, u32[]{:S(2)}) collective-permute-start(bf16[32,2048]{1,0:T(8,128)(2,1)S(1)} %get-tuple-element.58), channel_id=1, source_target_pairs={{0,16},{8,24},{16,0},{24,8},{1,17},{9,25},{17,1},{25,9},{2,18},{10... | collective-permute-start | bytes 393224 | tf_op jit(solution)/shard_map/ppermute | solution.py:246
  4.9 0.0 collective-permute-start.1
  5.0 0.0 copy-start
  5.0 7.0 %copy-done = bf16[5120,2048]{1,0:T(8,128)(2,1)S(1)} copy-done((bf16[5120,2048]{1,0:T(8,128)(2,1)S(1)}, bf16[5120,2048]{1,0:T(8,128)(2,1)}, u32[]{:S(2)}) %copy-start) | copy-done | bytes 20971544
  11.9 0.0 collective-permute-done.2.refs_3_
  11.9 0.0 collective-permute-done.refs_1_
  11.9 0.0 collective-permute-done.1.refs_2_
  11.9 0.0 copy-start.5
  11.9 0.0 copy-start.7
  12.0 0.0 copy-start.1
  12.0 0.0 copy-start.2
  12.0 0.0 copy-start.3
  12.0 0.0 copy-start.6
  12.0 0.0 copy-start.4
  12.0 3.1 %project.2 = (bf16[64,2560]{1,0:T(8,128)(2,1)S(1)}, bf16[64,2560]{1,0:T(8,128)(2,1)S(1)}, f32[1,2048]{1,0:T(1,128)S(1)}) custom-call(bf16[32,2048]{1,0:T(8,128)(2,1)S(1)} %get-tuple-element.59.refs_0_, bf16[32,2048]{1,0:T(8,128)(2,1)S(1)} %collective-permute-done.refs_1_, bf16[32,2048]{1,0:T(8,128)(2,1)S(1)} %collective-permute-done.1.refs_2_, ...), custom_call_target="tpu_custom_call" | custom-call | flops 1342177280 | bytes 10485760 | tf_op jit(solution)/shard_map/project/pallas_call | solution.py:74
  15.1 0.5 collective-permute-start.3
  15.6 3.0 %project.3 = (bf16[64,2560]{1,0:T(8,128)(2,1)S(1)}, bf16[64,2560]{1,0:T(8,128)(2,1)S(1)}) custom-call(bf16[32,2048]{1,0:T(8,128)(2,1)S(1)} %get-tuple-element.59.refs_0_, bf16[32,2048]{1,0:T(8,128)(2,1)S(1)} %collective-permute-done.refs_1_, bf16[32,2048]{1,0:T(8,128)(2,1)S(1)} %collective-permute-done.1.refs_2_, ...), custom_call_target="tpu_custom_call" | custom-call | flops 1342177280 | bytes 10485760 | tf_op jit(solution)/shard_map/project/pallas_call | solution.py:74
  18.6 0.1 collective-permute-start.7
  18.7 0.0 collective-permute-done.3.got_ref
  18.7 0.1 halve.2
  18.8 1.8 %collective-permute-start.4 = (bf16[32,2560]{1,0:T(8,128)(2,1)S(1)}, bf16[32,2560]{1,0:T(8,128)(2,1)S(1)}, u32[]{:S(2)}, u32[]{:S(2)}) collective-permute-start(bf16[32,2560]{1,0:T(8,128)(2,1)S(1)} %get-tuple-element.34), channel_id=1, source_target_pairs={{0,16},{8,24},{16,0},{24,8},{1,17},{9,25},{17,1},{25,9},{2,18},{10... | collective-permute-start | bytes 491528 | tf_op jit(solution)/shard_map/ppermute | solution.py:246
  20.6 0.0 collective-permute-done.7.got_ref
  20.6 0.1 halve.3
  20.7 1.2 %collective-permute-start.8 = (bf16[32,2560]{1,0:T(8,128)(2,1)S(1)}, bf16[32,2560]{1,0:T(8,128)(2,1)S(1)}, u32[]{:S(2)}, u32[]{:S(2)}) collective-permute-start(bf16[32,2560]{1,0:T(8,128)(2,1)S(1)} %get-tuple-element.41), channel_id=1, source_target_pairs={{0,16},{8,24},{16,0},{24,8},{1,17},{9,25},{17,1},{25,9},{2,18},{10... | collective-permute-start | bytes 491528 | tf_op jit(solution)/shard_map/ppermute | solution.py:246
  21.9 4.0 %collective-permute-done.4.refs_2_ = bf16[32,2560]{1,0:T(8,128)(2,1)S(1)} collective-permute-done((bf16[32,2560]{1,0:T(8,128)(2,1)S(1)}, bf16[32,2560]{1,0:T(8,128)(2,1)S(1)}, u32[]{:S(2)}, u32[]{:S(2)}) %collective-permute-start.4) | collective-permute-done | bytes 163872 | tf_op jit(solution)/shard_map/ppermute | solution.py:246
  25.9 0.0 copy-done.5
  25.9 0.4 pack.2
  26.3 2.9 %collective-permute-start.5 = (bf16[8,2688]{1,0:T(8,128)(2,1)S(1)}, bf16[8,2688]{1,0:T(8,128)(2,1)S(1)}, u32[]{:S(2)}, u32[]{:S(2)}) collective-permute-start(bf16[8,2688]{1,0:T(8,128)(2,1)S(1)} %get-tuple-element.36.refs_6_), channel_id=1, source_target_pairs={{0,4},{1,5},{2,6},{3,7},{4,0},{5,1},{6,2},{7,3},{8,12},{9,13},{10,... | collective-permute-start | bytes 129032 | tf_op jit(solution)/shard_map/ppermute | solution.py:246
  29.2 1.4 %collective-permute-start.6 = (bf16[8,2688]{1,0:T(8,128)(2,1)S(1)}, bf16[8,2688]{1,0:T(8,128)(2,1)S(1)}, u32[]{:S(2)}, u32[]{:S(2)}) collective-permute-start(bf16[8,2688]{1,0:T(8,128)(2,1)S(1)} %get-tuple-element.37.refs_7_), channel_id=1, source_target_pairs={{0,6},{1,7},{2,4},{3,5},{4,2},{5,3},{6,0},{7,1},{8,14},{9,15},{10,... | collective-permute-start | bytes 129032 | tf_op jit(solution)/shard_map/ppermute | solution.py:246
  30.5 0.0 collective-permute-done.8.refs_4_
  30.5 0.6 pack.3
  31.2 1.8 %collective-permute-start.11 = (bf16[8,2560]{1,0:T(8,128)(2,1)S(1)}, bf16[8,2560]{1,0:T(8,128)(2,1)S(1)}, u32[]{:S(2)}, u32[]{:S(2)}) collective-permute-start(bf16[8,2560]{1,0:T(8,128)(2,1)S(1)} %get-tuple-element.45), channel_id=1, source_target_pairs={{0,4},{1,5},{2,6},{3,7},{4,0},{5,1},{6,2},{7,3},{8,12},{9,13},{10,... | collective-permute-start | bytes 122888 | tf_op jit(solution)/shard_map/ppermute | solution.py:246
  32.9 0.9 %collective-permute-start.12 = (bf16[8,2560]{1,0:T(8,128)(2,1)S(1)}, bf16[8,2560]{1,0:T(8,128)(2,1)S(1)}, u32[]{:S(2)}, u32[]{:S(2)}) collective-permute-start(bf16[8,2560]{1,0:T(8,128)(2,1)S(1)} %get-tuple-element.46), channel_id=1, source_target_pairs={{0,6},{1,7},{2,4},{3,5},{4,2},{5,3},{6,0},{7,1},{8,14},{9,15},{10,... | collective-permute-start | bytes 122888 | tf_op jit(solution)/shard_map/ppermute | solution.py:246
  33.8 2.8 %collective-permute-start.9 = (bf16[8,5248]{1,0:T(8,128)(2,1)S(1)}, bf16[8,5248]{1,0:T(8,128)(2,1)S(1)}, u32[]{:S(2)}, u32[]{:S(2)}) collective-permute-start(bf16[8,5248]{1,0:T(8,128)(2,1)S(1)} %get-tuple-element.43), channel_id=1, source_target_pairs={{0,5},{1,4},{2,7},{3,6},{4,1},{5,0},{6,3},{7,2},{8,13},{9,12},{10,... | collective-permute-start | bytes 251912 | tf_op jit(solution)/shard_map/ppermute | solution.py:246
  36.7 0.1 collective-permute-done.11.refs_5_
  36.8 4.8 %collective-permute-start.10 = (bf16[8,5248]{1,0:T(8,128)(2,1)S(1)}, bf16[8,5248]{1,0:T(8,128)(2,1)S(1)}, u32[]{:S(2)}, u32[]{:S(2)}) collective-permute-start(bf16[8,5248]{1,0:T(8,128)(2,1)S(1)} %get-tuple-element.44), channel_id=1, source_target_pairs={{0,7},{1,6},{2,5},{3,4},{4,3},{5,2},{6,1},{7,0},{8,15},{9,14},{10,... | collective-permute-start | bytes 251912 | tf_op jit(solution)/shard_map/ppermute | solution.py:246
  41.5 0.0 collective-permute-done.12.refs_6_
  41.5 0.0 collective-permute-start.13
  41.6 0.0 collective-permute-done.5.refs_0_
  41.6 1.6 %collective-permute-start.14 = (bf16[8,5248]{1,0:T(8,128)(2,1)S(1)}, bf16[8,5248]{1,0:T(8,128)(2,1)S(1)}, u32[]{:S(2)}, u32[]{:S(2)}) collective-permute-start(bf16[8,5248]{1,0:T(8,128)(2,1)S(1)} %get-tuple-element.48), channel_id=1, source_target_pairs={{0,2},{1,3},{2,0},{3,1},{4,6},{5,7},{6,4},{7,5},{8,10},{9,11},{10,... | collective-permute-start | bytes 251912 | tf_op jit(solution)/shard_map/ppermute | solution.py:246
  43.2 0.0 collective-permute-done.6.refs_1_
  43.2 1.9 %collective-permute-start.15 = (bf16[8,5248]{1,0:T(8,128)(2,1)S(1)}, bf16[8,5248]{1,0:T(8,128)(2,1)S(1)}, u32[]{:S(2)}, u32[]{:S(2)}) collective-permute-start(bf16[8,5248]{1,0:T(8,128)(2,1)S(1)} %get-tuple-element.49), channel_id=1, source_target_pairs={{0,3},{1,2},{2,1},{3,0},{4,7},{5,6},{6,5},{7,4},{8,11},{9,10},{10,... | collective-permute-start | bytes 251912 | tf_op jit(solution)/shard_map/ppermute | solution.py:246
  45.0 0.0 copy-done.7
  45.1 0.0 collective-permute-done.9.refs_3_
  45.1 0.0 collective-permute-done.10.refs_4_
  45.1 1.6 %collective-permute-done.13.refs_7_ = bf16[8,5248]{1,0:T(8,128)(2,1)S(1)} collective-permute-done((bf16[8,5248]{1,0:T(8,128)(2,1)S(1)}, bf16[8,5248]{1,0:T(8,128)(2,1)S(1)}, u32[]{:S(2)}, u32[]{:S(2)}) %collective-permute-start.13) | collective-permute-done | bytes 84000 | tf_op jit(solution)/shard_map/ppermute | solution.py:246
  46.6 0.0 collective-permute-done.14.refs_8_
  46.6 1.9 %collective-permute-done.15.refs_9_ = bf16[8,5248]{1,0:T(8,128)(2,1)S(1)} collective-permute-done((bf16[8,5248]{1,0:T(8,128)(2,1)S(1)}, bf16[8,5248]{1,0:T(8,128)(2,1)S(1)}, u32[]{:S(2)}, u32[]{:S(2)}) %collective-permute-start.15) | collective-permute-done | bytes 84000 | tf_op jit(solution)/shard_map/ppermute | solution.py:246
  48.5 0.0 copy-done.1
  48.5 1.1 %norm.1 = (bf16[128,1280]{1,0:T(8,128)(2,1)S(1)}, bf16[32,2,768]{2,1,0:T(2,128)(2,1)}) custom-call(bf16[128,1280]{1,0:T(8,128)(2,1)S(1)} %bitcast.23, f32[1,1280]{1,0:T(1,128)S(1)} %broadcast_in_dim.12.gain_ref, bf16[8,2688]{1,0:T(8,128)(2,1)S(1)} %collective-permute-done.5.refs_0_, bf16[8,2688]{1,0:T(8,128)(2,1)S(1)} %collective-permute-done.6.refs_1_, ...), custom_call_target="tpu_custom_call" | custom-call | flops 85983232 | bytes 1327104 | tf_op jit(solution)/shard_map/norm/pallas_call | solution.py:354
  49.6 3.8 %all-to-all-start = ((bf16[32,2,768]{2,1,0:T(2,128)(2,1)}), bf16[32,2,768]{2,1,0:T(2,128)(2,1)S(1)}, u32[]{:S(2)}, u32[]{:S(2)}) async-start(bf16[32,2,768]{2,1,0:T(2,128)(2,1)} %get-tuple-element.56), calls=%async_computation | async-start | bytes 196608 | tf_op jit(solution)/shard_map/all_to_all | solution.py:253
  53.4 0.0 copy-done.2
  53.4 0.0 copy-done.3
  53.4 0.0 copy-done.6
  53.4 1.1 %probs.1 = (f32[16,128,128]{2,1,0:T(8,128)S(1)}, f32[16,128,128]{2,1,0:T(8,128)S(1)}) custom-call(bf16[128,1280]{1,0:T(8,128)(2,1)S(1)} %bitcast.24, bf16[128,1280]{1,0:T(8,128)(2,1)S(1)} %bitcast.26, s32[1,32]{1,0:T(1,128)S(1)} %bitcast.29), custom_call_target="tpu_custom_call" | custom-call | flops 268435456 | bytes 2097152 | tf_op jit(solution)/shard_map/probs/pallas_call | solution.py:285
  54.5 0.0 copy-done.4
  54.5 2.4 %window.1 = (bf16[128,1280]{1,0:T(8,128)(2,1)}, bf16[128,1280]{1,0:T(8,128)(2,1)}, bf16[128,1280]{1,0:T(8,128)(2,1)}) custom-call(bf16[128,1280]{1,0:T(8,128)(2,1)S(1)} %get-tuple-element.50.g_ref, bf16[128,1280]{1,0:T(8,128)(2,1)S(1)} %bitcast.25, bf16[128,1280]{1,0:T(8,128)(2,1)S(1)} %bitcast.27, bf16[128,1280]{1,0:T(8,128)(2,1)S(1)} %bitcast.28, ...), custom_call_target="tpu_custom_call" | custom-call | flops 335544320 | bytes 4390912 | tf_op jit(solution)/shard_map/window/pallas_call | solution.py:410
  56.9 4.1 %all-to-all-done = bf16[32,2,768]{2,1,0:T(2,128)(2,1)S(1)} async-done(((bf16[32,2,768]{2,1,0:T(2,128)(2,1)}), bf16[32,2,768]{2,1,0:T(2,128)(2,1)S(1)}, u32[]{:S(2)}, u32[]{:S(2)}) %all-to-all-start) | async-done | bytes 98336 | tf_op jit(solution)/shard_map/all_to_all | solution.py:253
  61.0 0.6 %copy.15 = f32[4,2,8,128]{3,1,2,0:T(2,128)} copy(f32[4,2,8,128]{3,2,1,0:T(8,128)S(1)} %fusion) | data formatting | bytes 65536
  61.7 0.6 broadcast_multiply_fusion
  (5 shorter events, 0.0 us)
Async XLA Ops:
  1.8 10.1 %collective-permute-start.2 = (bf16[32,2048]{1,0:T(8,128)(2,1)S(1)}, bf16[32,2048]{1,0:T(8,128)(2,1)S(1)}, u32[]{:S(2)}, u32[]{:S(2)}) collective-permute-start(bf16[32,2048]{1,0:T(8,128)(2,1)S(1)} %get-tuple-element.57), channel_id=1, source_target_pairs={{0,24},{8,16},{16,8},{24,0},{1,25},{9,17},{17,9},{25,1},{2,26},{10... | collective-permute-start | bytes 393224 | tf_op jit(solution)/shard_map/ppermute | solution.py:246
  4.3 7.7 %collective-permute-start = (bf16[32,2048]{1,0:T(8,128)(2,1)S(1)}, bf16[32,2048]{1,0:T(8,128)(2,1)S(1)}, u32[]{:S(2)}, u32[]{:S(2)}) collective-permute-start(bf16[32,2048]{1,0:T(8,128)(2,1)S(1)} %get-tuple-element.58), channel_id=1, source_target_pairs={{0,16},{8,24},{16,0},{24,8},{1,17},{9,25},{17,1},{25,9},{2,18},{10... | collective-permute-start | bytes 393224 | tf_op jit(solution)/shard_map/ppermute | solution.py:246
  4.9 7.0 %collective-permute-start.1 = (bf16[32,2048]{1,0:T(8,128)(2,1)S(1)}, bf16[32,2048]{1,0:T(8,128)(2,1)S(1)}, u32[]{:S(2)}, u32[]{:S(2)}) collective-permute-start(bf16[32,2048]{1,0:T(8,128)(2,1)S(1)} %get-tuple-element.60), channel_id=1, source_target_pairs={{0,8},{8,0},{16,24},{24,16},{1,9},{9,1},{17,25},{25,17},{2,10},{10... | collective-permute-start | bytes 393224 | tf_op jit(solution)/shard_map/ppermute | solution.py:246
  5.0 7.0 %copy-start = (bf16[5120,2048]{1,0:T(8,128)(2,1)S(1)}, bf16[5120,2048]{1,0:T(8,128)(2,1)}, u32[]{:S(2)}) copy-start(bf16[5120,2048]{1,0:T(8,128)(2,1)} %refs_4_.3) | copy-start | bytes 62914564
  11.9 13.9 %copy-start.5 = (s32[1,32]{1,0:T(1,128)S(1)}, s32[1,32]{1,0:T(1,128)}, u32[]{:S(2)}) copy-start(s32[1,32]{1,0:T(1,128)} %refs_0_.3) | copy-start | bytes 388
  11.9 33.1 %copy-start.7 = (f32[1280]{0:T(1024)S(1)}, f32[1280]{0:T(1024)}, u32[]{:S(2)}) copy-start(f32[1280]{0:T(1024)} %param.12) | copy-start | bytes 15364
  12.0 36.6 %copy-start.1 = (bf16[1,128,1280]{2,1,0:T(8,128)(2,1)S(1)}, bf16[1,128,1280]{2,1,0:T(8,128)(2,1)}, u32[]{:S(2)}) copy-start(bf16[1,128,1280]{2,1,0:T(8,128)(2,1)} %param.11) | copy-start | bytes 983044
  12.0 41.4 %copy-start.2 = (bf16[1,128,1280]{2,1,0:T(8,128)(2,1)S(1)}, bf16[1,128,1280]{2,1,0:T(8,128)(2,1)}, u32[]{:S(2)}) copy-start(bf16[1,128,1280]{2,1,0:T(8,128)(2,1)} %param.14) | copy-start | bytes 983044
  12.0 41.4 %copy-start.3 = (bf16[1,128,1280]{2,1,0:T(8,128)(2,1)S(1)}, bf16[1,128,1280]{2,1,0:T(8,128)(2,1)}, u32[]{:S(2)}) copy-start(bf16[1,128,1280]{2,1,0:T(8,128)(2,1)} %param.15) | copy-start | bytes 983044
  12.0 41.4 %copy-start.6 = (s32[1,1,32]{2,1,0:T(1,128)S(1)}, s32[1,1,32]{2,1,0:T(1,128)}, u32[]{:S(2)}) copy-start(s32[1,1,32]{2,1,0:T(1,128)} %param.17) | copy-start | bytes 388
  12.0 42.5 %copy-start.4 = (bf16[1,128,1280]{2,1,0:T(8,128)(2,1)S(1)}, bf16[1,128,1280]{2,1,0:T(8,128)(2,1)}, u32[]{:S(2)}) copy-start(bf16[1,128,1280]{2,1,0:T(8,128)(2,1)} %param.16) | copy-start | bytes 983044
  15.1 3.6 %collective-permute-start.3 = (bf16[64,2560]{1,0:T(8,128)(2,1)S(1)}, bf16[64,2560]{1,0:T(8,128)(2,1)S(1)}, u32[]{:S(2)}, u32[]{:S(2)}) collective-permute-start(bf16[64,2560]{1,0:T(8,128)(2,1)S(1)} %get-tuple-element.32), channel_id=1, source_target_pairs={{0,8},{8,0},{16,24},{24,16},{1,9},{9,1},{17,25},{25,17},{2,10},{10... | collective-permute-start | bytes 983048 | tf_op jit(solution)/shard_map/ppermute | solution.py:246
  18.6 2.0 %collective-permute-start.7 = (bf16[64,2560]{1,0:T(8,128)(2,1)S(1)}, bf16[64,2560]{1,0:T(8,128)(2,1)S(1)}, u32[]{:S(2)}, u32[]{:S(2)}) collective-permute-start(bf16[64,2560]{1,0:T(8,128)(2,1)S(1)} %get-tuple-element.39), channel_id=1, source_target_pairs={{0,8},{8,0},{16,24},{24,16},{1,9},{9,1},{17,25},{25,17},{2,10},{10... | collective-permute-start | bytes 983048 | tf_op jit(solution)/shard_map/ppermute | solution.py:246
  18.8 7.1 %collective-permute-start.4 = (bf16[32,2560]{1,0:T(8,128)(2,1)S(1)}, bf16[32,2560]{1,0:T(8,128)(2,1)S(1)}, u32[]{:S(2)}, u32[]{:S(2)}) collective-permute-start(bf16[32,2560]{1,0:T(8,128)(2,1)S(1)} %get-tuple-element.34), channel_id=1, source_target_pairs={{0,16},{8,24},{16,0},{24,8},{1,17},{9,25},{17,1},{25,9},{2,18},{10... | collective-permute-start | bytes 491528 | tf_op jit(solution)/shard_map/ppermute | solution.py:246
  20.7 9.9 %collective-permute-start.8 = (bf16[32,2560]{1,0:T(8,128)(2,1)S(1)}, bf16[32,2560]{1,0:T(8,128)(2,1)S(1)}, u32[]{:S(2)}, u32[]{:S(2)}) collective-permute-start(bf16[32,2560]{1,0:T(8,128)(2,1)S(1)} %get-tuple-element.41), channel_id=1, source_target_pairs={{0,16},{8,24},{16,0},{24,8},{1,17},{9,25},{17,1},{25,9},{2,18},{10... | collective-permute-start | bytes 491528 | tf_op jit(solution)/shard_map/ppermute | solution.py:246
  26.3 15.3 %collective-permute-start.5 = (bf16[8,2688]{1,0:T(8,128)(2,1)S(1)}, bf16[8,2688]{1,0:T(8,128)(2,1)S(1)}, u32[]{:S(2)}, u32[]{:S(2)}) collective-permute-start(bf16[8,2688]{1,0:T(8,128)(2,1)S(1)} %get-tuple-element.36.refs_6_), channel_id=1, source_target_pairs={{0,4},{1,5},{2,6},{3,7},{4,0},{5,1},{6,2},{7,3},{8,12},{9,13},{10,... | collective-permute-start | bytes 129032 | tf_op jit(solution)/shard_map/ppermute | solution.py:246
  29.2 14.0 %collective-permute-start.6 = (bf16[8,2688]{1,0:T(8,128)(2,1)S(1)}, bf16[8,2688]{1,0:T(8,128)(2,1)S(1)}, u32[]{:S(2)}, u32[]{:S(2)}) collective-permute-start(bf16[8,2688]{1,0:T(8,128)(2,1)S(1)} %get-tuple-element.37.refs_7_), channel_id=1, source_target_pairs={{0,6},{1,7},{2,4},{3,5},{4,2},{5,3},{6,0},{7,1},{8,14},{9,15},{10,... | collective-permute-start | bytes 129032 | tf_op jit(solution)/shard_map/ppermute | solution.py:246
  31.2 5.6 %collective-permute-start.11 = (bf16[8,2560]{1,0:T(8,128)(2,1)S(1)}, bf16[8,2560]{1,0:T(8,128)(2,1)S(1)}, u32[]{:S(2)}, u32[]{:S(2)}) collective-permute-start(bf16[8,2560]{1,0:T(8,128)(2,1)S(1)} %get-tuple-element.45), channel_id=1, source_target_pairs={{0,4},{1,5},{2,6},{3,7},{4,0},{5,1},{6,2},{7,3},{8,12},{9,13},{10,... | collective-permute-start | bytes 122888 | tf_op jit(solution)/shard_map/ppermute | solution.py:246
  32.9 8.6 %collective-permute-start.12 = (bf16[8,2560]{1,0:T(8,128)(2,1)S(1)}, bf16[8,2560]{1,0:T(8,128)(2,1)S(1)}, u32[]{:S(2)}, u32[]{:S(2)}) collective-permute-start(bf16[8,2560]{1,0:T(8,128)(2,1)S(1)} %get-tuple-element.46), channel_id=1, source_target_pairs={{0,6},{1,7},{2,4},{3,5},{4,2},{5,3},{6,0},{7,1},{8,14},{9,15},{10,... | collective-permute-start | bytes 122888 | tf_op jit(solution)/shard_map/ppermute | solution.py:246
  33.8 11.2 %collective-permute-start.9 = (bf16[8,5248]{1,0:T(8,128)(2,1)S(1)}, bf16[8,5248]{1,0:T(8,128)(2,1)S(1)}, u32[]{:S(2)}, u32[]{:S(2)}) collective-permute-start(bf16[8,5248]{1,0:T(8,128)(2,1)S(1)} %get-tuple-element.43), channel_id=1, source_target_pairs={{0,5},{1,4},{2,7},{3,6},{4,1},{5,0},{6,3},{7,2},{8,13},{9,12},{10,... | collective-permute-start | bytes 251912 | tf_op jit(solution)/shard_map/ppermute | solution.py:246
  36.8 8.3 %collective-permute-start.10 = (bf16[8,5248]{1,0:T(8,128)(2,1)S(1)}, bf16[8,5248]{1,0:T(8,128)(2,1)S(1)}, u32[]{:S(2)}, u32[]{:S(2)}) collective-permute-start(bf16[8,5248]{1,0:T(8,128)(2,1)S(1)} %get-tuple-element.44), channel_id=1, source_target_pairs={{0,7},{1,6},{2,5},{3,4},{4,3},{5,2},{6,1},{7,0},{8,15},{9,14},{10,... | collective-permute-start | bytes 251912 | tf_op jit(solution)/shard_map/ppermute | solution.py:246
  41.5 5.1 %collective-permute-start.13 = (bf16[8,5248]{1,0:T(8,128)(2,1)S(1)}, bf16[8,5248]{1,0:T(8,128)(2,1)S(1)}, u32[]{:S(2)}, u32[]{:S(2)}) collective-permute-start(bf16[8,5248]{1,0:T(8,128)(2,1)S(1)} %get-tuple-element.47), channel_id=1, source_target_pairs={{0,1},{1,0},{2,3},{3,2},{4,5},{5,4},{6,7},{7,6},{8,9},{9,8},{10,11... | collective-permute-start | bytes 251912 | tf_op jit(solution)/shard_map/ppermute | solution.py:246
  41.6 5.1 %collective-permute-start.14 = (bf16[8,5248]{1,0:T(8,128)(2,1)S(1)}, bf16[8,5248]{1,0:T(8,128)(2,1)S(1)}, u32[]{:S(2)}, u32[]{:S(2)}) collective-permute-start(bf16[8,5248]{1,0:T(8,128)(2,1)S(1)} %get-tuple-element.48), channel_id=1, source_target_pairs={{0,2},{1,3},{2,0},{3,1},{4,6},{5,7},{6,4},{7,5},{8,10},{9,11},{10,... | collective-permute-start | bytes 251912 | tf_op jit(solution)/shard_map/ppermute | solution.py:246
  43.2 5.4 %collective-permute-start.15 = (bf16[8,5248]{1,0:T(8,128)(2,1)S(1)}, bf16[8,5248]{1,0:T(8,128)(2,1)S(1)}, u32[]{:S(2)}, u32[]{:S(2)}) collective-permute-start(bf16[8,5248]{1,0:T(8,128)(2,1)S(1)} %get-tuple-element.49), channel_id=1, source_target_pairs={{0,3},{1,2},{2,1},{3,0},{4,7},{5,6},{6,5},{7,4},{8,11},{9,10},{10,... | collective-permute-start | bytes 251912 | tf_op jit(solution)/shard_map/ppermute | solution.py:246
  49.6 11.3 %all-to-all-start = ((bf16[32,2,768]{2,1,0:T(2,128)(2,1)}), bf16[32,2,768]{2,1,0:T(2,128)(2,1)S(1)}, u32[]{:S(2)}, u32[]{:S(2)}) async-start(bf16[32,2,768]{2,1,0:T(2,128)(2,1)} %get-tuple-element.56), calls=%async_computation | async-start | bytes 196608 | tf_op jit(solution)/shard_map/all_to_all | solution.py:253

commit v14 on v13

--- a/solution.py
+++ b/solution.py
@@ -129,7 +129,7 @@
 
 
 def peer_masks(peers):
-    return (0, 5, 7, 4, 6, 1, 2, 3) if peers == 8 else tuple(range(peers))
+    return (0, 5, 1, 7, 2, 3, 4, 6) if peers == 8 else tuple(range(peers))
 
 
 def early_masks(peers):

time: 62.5 us -> 62.3 us (level)
  transfers between devices with their start and end apart: 17 -> 17, of which waited for: 5 -> 6; matrix products, arithmetic and copies ran while one was open for 0% -> 0% of each run, Pallas kernels for 12% -> 12%
where the time goes in v14:
time: 62.3 us; the launch traced here: 62 us
  starting transfers between devices  28.4 us (46%)
  Pallas kernels  11.7 us (19%)
  waiting for transfers between devices  11.6 us (19%)
  local copies, waits for them, and re-layouts  8.8 us (14%)
  between operations  0.85 us (1%)
  other arithmetic  0.63 us (1%)
    ppermute x16, starting transfers between devices, swap(): return lax.ppermute(x, axis, [(i, i ^ mask) for i in range(n)])  24.8 us
    unnamed x18, local copies, waits for them, and re-layouts  7.65 us
    ppermute x16, waiting for transfers between devices, swap(): return lax.ppermute(x, axis, [(i, i ^ mask) for i in range(n)])  7.51 us
    pallas_call x2, Pallas kernels, project(): pl.pallas_call(functools.partial(project_kernel, blocks, first, tile, wit...  6.05 us
    all_to_all x1, waiting for transfers between devices, exchange(): lax.all_to_all(x, axis, split_axis=0, concat_axis=0, tiled=True)  4.07 us
    all_to_all x1, starting transfers between devices, exchange(): lax.all_to_all(x, axis, split_axis=0, concat_axis=0, tiled=True)  3.62 us
    pallas_call x1, Pallas kernels, window_backward(): pl.pallas_call(window_kernel, out_shape=[shape] * 3, in_specs=vmem(6), ou...  2.38 us
  transfers between devices with their start and end apart: 17, of which 6 were waited for; matrix products, arithmetic and copies ran while one was open for 0% of the time, Pallas kernels for 12%

profile of v14, /device:TPU:0, one launch (start us, length us, event | category | flops | bytes accessed | tf_op | source)
XLA Modules:
  0.0 62.0 jit_solution(18425162866936725736)
XLA Ops:
  0.7 1.1 %dynamic-slice_bitcast_fusion = (bf16[32,2048]{1,0:T(8,128)(2,1)S(1)}, bf16[32,2048]{1,0:T(8,128)(2,1)S(1)}, bf16[32,2048]{1,0:T(8,128)(2,1)S(1)}, bf16[32,2048]{1,0:T(8,128)(2,1)S(1)}) fusion(bf16[1,32,8192]{2,1,0:T(8,128)(2,1)} %param.9, s32[]{:T(128)S(6)} %select_n.15, s32[]{:T(128)S(6)} %select_n.13, s32[]{:T(128)S(6)} %select_n.12, s32[]{:T(128)S(6)} %select_n.14), kind=kLoop, calls=%fused_computation.1 | loop fusion | bytes 1048592 | tf_op jit(solution)/shard_map/dynamic_slice | solution.py:443
  1.8 2.5 %collective-permute-start.2 = (bf16[32,2048]{1,0:T(8,128)(2,1)S(1)}, bf16[32,2048]{1,0:T(8,128)(2,1)S(1)}, u32[]{:S(2)}, u32[]{:S(2)}) collective-permute-start(bf16[32,2048]{1,0:T(8,128)(2,1)S(1)} %get-tuple-element.57), channel_id=1, source_target_pairs={{0,24},{8,16},{16,8},{24,0},{1,25},{9,17},{17,9},{25,1},{2,26},{10... | collective-permute-start | bytes 393224 | tf_op jit(solution)/shard_map/ppermute | solution.py:246
  4.3 0.6 %collective-permute-start = (bf16[32,2048]{1,0:T(8,128)(2,1)S(1)}, bf16[32,2048]{1,0:T(8,128)(2,1)S(1)}, u32[]{:S(2)}, u32[]{:S(2)}) collective-permute-start(bf16[32,2048]{1,0:T(8,128)(2,1)S(1)} %get-tuple-element.58), channel_id=1, source_target_pairs={{0,16},{8,24},{16,0},{24,8},{1,17},{9,25},{17,1},{25,9},{2,18},{10... | collective-permute-start | bytes 393224 | tf_op jit(solution)/shard_map/ppermute | solution.py:246
  4.9 0.0 collective-permute-start.1
  5.0 0.0 copy-start
  5.0 7.0 %copy-done = bf16[5120,2048]{1,0:T(8,128)(2,1)S(1)} copy-done((bf16[5120,2048]{1,0:T(8,128)(2,1)S(1)}, bf16[5120,2048]{1,0:T(8,128)(2,1)}, u32[]{:S(2)}) %copy-start) | copy-done | bytes 20971544
  11.9 0.0 collective-permute-done.2.refs_3_
  11.9 0.0 collective-permute-done.refs_1_
  11.9 0.0 collective-permute-done.1.refs_2_
  11.9 0.0 copy-start.5
  11.9 0.0 copy-start.7
  12.0 0.0 copy-start.1
  12.0 0.0 copy-start.2
  12.0 0.0 copy-start.3
  12.0 0.0 copy-start.6
  12.0 0.0 copy-start.4
  12.0 3.1 %project.2 = (bf16[64,2560]{1,0:T(8,128)(2,1)S(1)}, bf16[64,2560]{1,0:T(8,128)(2,1)S(1)}, f32[1,2048]{1,0:T(1,128)S(1)}) custom-call(bf16[32,2048]{1,0:T(8,128)(2,1)S(1)} %get-tuple-element.59.refs_0_, bf16[32,2048]{1,0:T(8,128)(2,1)S(1)} %collective-permute-done.refs_1_, bf16[32,2048]{1,0:T(8,128)(2,1)S(1)} %collective-permute-done.1.refs_2_, ...), custom_call_target="tpu_custom_call" | custom-call | flops 1342177280 | bytes 10485760 | tf_op jit(solution)/shard_map/project/pallas_call | solution.py:74
  15.1 0.5 collective-permute-start.3
  15.6 3.0 %project.3 = (bf16[64,2560]{1,0:T(8,128)(2,1)S(1)}, bf16[64,2560]{1,0:T(8,128)(2,1)S(1)}) custom-call(bf16[32,2048]{1,0:T(8,128)(2,1)S(1)} %get-tuple-element.59.refs_0_, bf16[32,2048]{1,0:T(8,128)(2,1)S(1)} %collective-permute-done.refs_1_, bf16[32,2048]{1,0:T(8,128)(2,1)S(1)} %collective-permute-done.1.refs_2_, ...), custom_call_target="tpu_custom_call" | custom-call | flops 1342177280 | bytes 10485760 | tf_op jit(solution)/shard_map/project/pallas_call | solution.py:74
  18.6 0.1 collective-permute-start.7
  18.7 0.0 collective-permute-done.3.got_ref
  18.7 0.1 halve.2
  18.8 1.8 %collective-permute-start.4 = (bf16[32,2560]{1,0:T(8,128)(2,1)S(1)}, bf16[32,2560]{1,0:T(8,128)(2,1)S(1)}, u32[]{:S(2)}, u32[]{:S(2)}) collective-permute-start(bf16[32,2560]{1,0:T(8,128)(2,1)S(1)} %get-tuple-element.34), channel_id=1, source_target_pairs={{0,16},{8,24},{16,0},{24,8},{1,17},{9,25},{17,1},{25,9},{2,18},{10... | collective-permute-start | bytes 491528 | tf_op jit(solution)/shard_map/ppermute | solution.py:246
  20.6 0.0 collective-permute-done.7.got_ref
  20.6 0.1 halve.3
  20.7 1.2 %collective-permute-start.8 = (bf16[32,2560]{1,0:T(8,128)(2,1)S(1)}, bf16[32,2560]{1,0:T(8,128)(2,1)S(1)}, u32[]{:S(2)}, u32[]{:S(2)}) collective-permute-start(bf16[32,2560]{1,0:T(8,128)(2,1)S(1)} %get-tuple-element.41), channel_id=1, source_target_pairs={{0,16},{8,24},{16,0},{24,8},{1,17},{9,25},{17,1},{25,9},{2,18},{10... | collective-permute-start | bytes 491528 | tf_op jit(solution)/shard_map/ppermute | solution.py:246
  21.9 4.0 %collective-permute-done.4.refs_2_ = bf16[32,2560]{1,0:T(8,128)(2,1)S(1)} collective-permute-done((bf16[32,2560]{1,0:T(8,128)(2,1)S(1)}, bf16[32,2560]{1,0:T(8,128)(2,1)S(1)}, u32[]{:S(2)}, u32[]{:S(2)}) %collective-permute-start.4) | collective-permute-done | bytes 163872 | tf_op jit(solution)/shard_map/ppermute | solution.py:246
  25.9 0.0 copy-done.5
  25.9 0.4 pack.2
  26.3 2.9 %collective-permute-start.5 = (bf16[8,2688]{1,0:T(8,128)(2,1)S(1)}, bf16[8,2688]{1,0:T(8,128)(2,1)S(1)}, u32[]{:S(2)}, u32[]{:S(2)}) collective-permute-start(bf16[8,2688]{1,0:T(8,128)(2,1)S(1)} %get-tuple-element.36.refs_6_), channel_id=1, source_target_pairs={{0,4},{1,5},{2,6},{3,7},{4,0},{5,1},{6,2},{7,3},{8,12},{9,13},{10,... | collective-permute-start | bytes 129032 | tf_op jit(solution)/shard_map/ppermute | solution.py:246
  29.2 1.4 %collective-permute-start.6 = (bf16[8,2688]{1,0:T(8,128)(2,1)S(1)}, bf16[8,2688]{1,0:T(8,128)(2,1)S(1)}, u32[]{:S(2)}, u32[]{:S(2)}) collective-permute-start(bf16[8,2688]{1,0:T(8,128)(2,1)S(1)} %get-tuple-element.37.refs_7_), channel_id=1, source_target_pairs={{0,6},{1,7},{2,4},{3,5},{4,2},{5,3},{6,0},{7,1},{8,14},{9,15},{10,... | collective-permute-start | bytes 129032 | tf_op jit(solution)/shard_map/ppermute | solution.py:246
  30.5 0.0 collective-permute-done.8.refs_4_
  30.5 0.6 pack.3
  31.2 1.8 %collective-permute-start.14 = (bf16[8,2560]{1,0:T(8,128)(2,1)S(1)}, bf16[8,2560]{1,0:T(8,128)(2,1)S(1)}, u32[]{:S(2)}, u32[]{:S(2)}) collective-permute-start(bf16[8,2560]{1,0:T(8,128)(2,1)S(1)} %get-tuple-element.48), channel_id=1, source_target_pairs={{0,4},{1,5},{2,6},{3,7},{4,0},{5,1},{6,2},{7,3},{8,12},{9,13},{10,... | collective-permute-start | bytes 122888 | tf_op jit(solution)/shard_map/ppermute | solution.py:246
  32.9 0.9 %collective-permute-start.15 = (bf16[8,2560]{1,0:T(8,128)(2,1)S(1)}, bf16[8,2560]{1,0:T(8,128)(2,1)S(1)}, u32[]{:S(2)}, u32[]{:S(2)}) collective-permute-start(bf16[8,2560]{1,0:T(8,128)(2,1)S(1)} %get-tuple-element.49), channel_id=1, source_target_pairs={{0,6},{1,7},{2,4},{3,5},{4,2},{5,3},{6,0},{7,1},{8,14},{9,15},{10,... | collective-permute-start | bytes 122888 | tf_op jit(solution)/shard_map/ppermute | solution.py:246
  33.8 2.8 %collective-permute-start.9 = (bf16[8,5248]{1,0:T(8,128)(2,1)S(1)}, bf16[8,5248]{1,0:T(8,128)(2,1)S(1)}, u32[]{:S(2)}, u32[]{:S(2)}) collective-permute-start(bf16[8,5248]{1,0:T(8,128)(2,1)S(1)} %get-tuple-element.43), channel_id=1, source_target_pairs={{0,5},{1,4},{2,7},{3,6},{4,1},{5,0},{6,3},{7,2},{8,13},{9,12},{10,... | collective-permute-start | bytes 251912 | tf_op jit(solution)/shard_map/ppermute | solution.py:246
  36.7 0.1 collective-permute-done.14.refs_8_
  36.8 2.7 %collective-permute-start.10 = (bf16[8,5248]{1,0:T(8,128)(2,1)S(1)}, bf16[8,5248]{1,0:T(8,128)(2,1)S(1)}, u32[]{:S(2)}, u32[]{:S(2)}) collective-permute-start(bf16[8,5248]{1,0:T(8,128)(2,1)S(1)} %get-tuple-element.44), channel_id=1, source_target_pairs={{0,1},{1,0},{2,3},{3,2},{4,5},{5,4},{6,7},{7,6},{8,9},{9,8},{10,11... | collective-permute-start | bytes 251912 | tf_op jit(solution)/shard_map/ppermute | solution.py:246
  39.5 0.0 collective-permute-done.15.refs_9_
  39.5 2.1 %collective-permute-start.11 = (bf16[8,5248]{1,0:T(8,128)(2,1)S(1)}, bf16[8,5248]{1,0:T(8,128)(2,1)S(1)}, u32[]{:S(2)}, u32[]{:S(2)}) collective-permute-start(bf16[8,5248]{1,0:T(8,128)(2,1)S(1)} %get-tuple-element.45), channel_id=1, source_target_pairs={{0,7},{1,6},{2,5},{3,4},{4,3},{5,2},{6,1},{7,0},{8,15},{9,14},{10,... | collective-permute-start | bytes 251912 | tf_op jit(solution)/shard_map/ppermute | solution.py:246
  41.6 0.0 collective-permute-done.5.refs_0_
  41.6 1.4 %collective-permute-start.12 = (bf16[8,5248]{1,0:T(8,128)(2,1)S(1)}, bf16[8,5248]{1,0:T(8,128)(2,1)S(1)}, u32[]{:S(2)}, u32[]{:S(2)}) collective-permute-start(bf16[8,5248]{1,0:T(8,128)(2,1)S(1)} %get-tuple-element.46), channel_id=1, source_target_pairs={{0,2},{1,3},{2,0},{3,1},{4,6},{5,7},{6,4},{7,5},{8,10},{9,11},{10,... | collective-permute-start | bytes 251912 | tf_op jit(solution)/shard_map/ppermute | solution.py:246
  43.0 0.0 collective-permute-done.6.refs_1_
  43.0 2.1 %collective-permute-start.13 = (bf16[8,5248]{1,0:T(8,128)(2,1)S(1)}, bf16[8,5248]{1,0:T(8,128)(2,1)S(1)}, u32[]{:S(2)}, u32[]{:S(2)}) collective-permute-start(bf16[8,5248]{1,0:T(8,128)(2,1)S(1)} %get-tuple-element.47), channel_id=1, source_target_pairs={{0,3},{1,2},{2,1},{3,0},{4,7},{5,6},{6,5},{7,4},{8,11},{9,10},{10,... | collective-permute-start | bytes 251912 | tf_op jit(solution)/shard_map/ppermute | solution.py:246
  45.0 0.0 copy-done.7
  45.1 0.0 collective-permute-done.9.refs_3_
  45.1 0.0 collective-permute-done.10.refs_4_
  45.1 1.6 %collective-permute-done.11.refs_5_ = bf16[8,5248]{1,0:T(8,128)(2,1)S(1)} collective-permute-done((bf16[8,5248]{1,0:T(8,128)(2,1)S(1)}, bf16[8,5248]{1,0:T(8,128)(2,1)S(1)}, u32[]{:S(2)}, u32[]{:S(2)}) %collective-permute-start.11) | collective-permute-done | bytes 84000 | tf_op jit(solution)/shard_map/ppermute | solution.py:246
  46.6 0.3 collective-permute-done.12.refs_6_
  46.9 1.5 %collective-permute-done.13.refs_7_ = bf16[8,5248]{1,0:T(8,128)(2,1)S(1)} collective-permute-done((bf16[8,5248]{1,0:T(8,128)(2,1)S(1)}, bf16[8,5248]{1,0:T(8,128)(2,1)S(1)}, u32[]{:S(2)}, u32[]{:S(2)}) %collective-permute-start.13) | collective-permute-done | bytes 84000 | tf_op jit(solution)/shard_map/ppermute | solution.py:246
  48.4 0.0 copy-done.1
  48.4 1.1 %norm.1 = (bf16[128,1280]{1,0:T(8,128)(2,1)S(1)}, bf16[32,2,768]{2,1,0:T(2,128)(2,1)}) custom-call(bf16[128,1280]{1,0:T(8,128)(2,1)S(1)} %bitcast.23, f32[1,1280]{1,0:T(1,128)S(1)} %broadcast_in_dim.12.gain_ref, bf16[8,2688]{1,0:T(8,128)(2,1)S(1)} %collective-permute-done.5.refs_0_, bf16[8,2688]{1,0:T(8,128)(2,1)S(1)} %collective-permute-done.6.refs_1_, ...), custom_call_target="tpu_custom_call" | custom-call | flops 85983232 | bytes 1327104 | tf_op jit(solution)/shard_map/norm/pallas_call | solution.py:354
  49.5 3.6 %all-to-all-start = ((bf16[32,2,768]{2,1,0:T(2,128)(2,1)}), bf16[32,2,768]{2,1,0:T(2,128)(2,1)S(1)}, u32[]{:S(2)}, u32[]{:S(2)}) async-start(bf16[32,2,768]{2,1,0:T(2,128)(2,1)} %get-tuple-element.56), calls=%async_computation | async-start | bytes 196608 | tf_op jit(solution)/shard_map/all_to_all | solution.py:253
  53.2 0.0 copy-done.2
  53.2 0.0 copy-done.3
  53.2 0.0 copy-done.6
  53.2 1.1 %probs.1 = (f32[16,128,128]{2,1,0:T(8,128)S(1)}, f32[16,128,128]{2,1,0:T(8,128)S(1)}) custom-call(bf16[128,1280]{1,0:T(8,128)(2,1)S(1)} %bitcast.24, bf16[128,1280]{1,0:T(8,128)(2,1)S(1)} %bitcast.26, s32[1,32]{1,0:T(1,128)S(1)} %bitcast.29), custom_call_target="tpu_custom_call" | custom-call | flops 268435456 | bytes 2097152 | tf_op jit(solution)/shard_map/probs/pallas_call | solution.py:285
  54.3 0.0 copy-done.4
  54.3 2.4 %window.1 = (bf16[128,1280]{1,0:T(8,128)(2,1)}, bf16[128,1280]{1,0:T(8,128)(2,1)}, bf16[128,1280]{1,0:T(8,128)(2,1)}) custom-call(bf16[128,1280]{1,0:T(8,128)(2,1)S(1)} %get-tuple-element.50.g_ref, bf16[128,1280]{1,0:T(8,128)(2,1)S(1)} %bitcast.25, bf16[128,1280]{1,0:T(8,128)(2,1)S(1)} %bitcast.27, bf16[128,1280]{1,0:T(8,128)(2,1)S(1)} %bitcast.28, ...), custom_call_target="tpu_custom_call" | custom-call | flops 335544320 | bytes 4390912 | tf_op jit(solution)/shard_map/window/pallas_call | solution.py:410
  56.7 4.1 %all-to-all-done = bf16[32,2,768]{2,1,0:T(2,128)(2,1)S(1)} async-done(((bf16[32,2,768]{2,1,0:T(2,128)(2,1)}), bf16[32,2,768]{2,1,0:T(2,128)(2,1)S(1)}, u32[]{:S(2)}, u32[]{:S(2)}) %all-to-all-start) | async-done | bytes 98336 | tf_op jit(solution)/shard_map/all_to_all | solution.py:253
  60.8 0.6 %copy.15 = f32[4,2,8,128]{3,1,2,0:T(2,128)} copy(f32[4,2,8,128]{3,2,1,0:T(8,128)S(1)} %fusion) | data formatting | bytes 65536
  61.4 0.6 broadcast_multiply_fusion
  (5 shorter events, 0.0 us)
Async XLA Ops:
  1.8 10.1 %collective-permute-start.2 = (bf16[32,2048]{1,0:T(8,128)(2,1)S(1)}, bf16[32,2048]{1,0:T(8,128)(2,1)S(1)}, u32[]{:S(2)}, u32[]{:S(2)}) collective-permute-start(bf16[32,2048]{1,0:T(8,128)(2,1)S(1)} %get-tuple-element.57), channel_id=1, source_target_pairs={{0,24},{8,16},{16,8},{24,0},{1,25},{9,17},{17,9},{25,1},{2,26},{10... | collective-permute-start | bytes 393224 | tf_op jit(solution)/shard_map/ppermute | solution.py:246
  4.3 7.7 %collective-permute-start = (bf16[32,2048]{1,0:T(8,128)(2,1)S(1)}, bf16[32,2048]{1,0:T(8,128)(2,1)S(1)}, u32[]{:S(2)}, u32[]{:S(2)}) collective-permute-start(bf16[32,2048]{1,0:T(8,128)(2,1)S(1)} %get-tuple-element.58), channel_id=1, source_target_pairs={{0,16},{8,24},{16,0},{24,8},{1,17},{9,25},{17,1},{25,9},{2,18},{10... | collective-permute-start | bytes 393224 | tf_op jit(solution)/shard_map/ppermute | solution.py:246
  4.9 7.0 %collective-permute-start.1 = (bf16[32,2048]{1,0:T(8,128)(2,1)S(1)}, bf16[32,2048]{1,0:T(8,128)(2,1)S(1)}, u32[]{:S(2)}, u32[]{:S(2)}) collective-permute-start(bf16[32,2048]{1,0:T(8,128)(2,1)S(1)} %get-tuple-element.60), channel_id=1, source_target_pairs={{0,8},{8,0},{16,24},{24,16},{1,9},{9,1},{17,25},{25,17},{2,10},{10... | collective-permute-start | bytes 393224 | tf_op jit(solution)/shard_map/ppermute | solution.py:246
  5.0 7.0 %copy-start = (bf16[5120,2048]{1,0:T(8,128)(2,1)S(1)}, bf16[5120,2048]{1,0:T(8,128)(2,1)}, u32[]{:S(2)}) copy-start(bf16[5120,2048]{1,0:T(8,128)(2,1)} %refs_4_.3) | copy-start | bytes 62914564
  11.9 13.9 %copy-start.5 = (s32[1,32]{1,0:T(1,128)S(1)}, s32[1,32]{1,0:T(1,128)}, u32[]{:S(2)}) copy-start(s32[1,32]{1,0:T(1,128)} %refs_0_.3) | copy-start | bytes 388
  11.9 33.1 %copy-start.7 = (f32[1280]{0:T(1024)S(1)}, f32[1280]{0:T(1024)}, u32[]{:S(2)}) copy-start(f32[1280]{0:T(1024)} %param.12) | copy-start | bytes 15364
  12.0 36.5 %copy-start.1 = (bf16[1,128,1280]{2,1,0:T(8,128)(2,1)S(1)}, bf16[1,128,1280]{2,1,0:T(8,128)(2,1)}, u32[]{:S(2)}) copy-start(bf16[1,128,1280]{2,1,0:T(8,128)(2,1)} %param.11) | copy-start | bytes 983044
  12.0 41.2 %copy-start.2 = (bf16[1,128,1280]{2,1,0:T(8,128)(2,1)S(1)}, bf16[1,128,1280]{2,1,0:T(8,128)(2,1)}, u32[]{:S(2)}) copy-start(bf16[1,128,1280]{2,1,0:T(8,128)(2,1)} %param.14) | copy-start | bytes 983044
  12.0 41.2 %copy-start.3 = (bf16[1,128,1280]{2,1,0:T(8,128)(2,1)S(1)}, bf16[1,128,1280]{2,1,0:T(8,128)(2,1)}, u32[]{:S(2)}) copy-start(bf16[1,128,1280]{2,1,0:T(8,128)(2,1)} %param.15) | copy-start | bytes 983044
  12.0 41.2 %copy-start.6 = (s32[1,1,32]{2,1,0:T(1,128)S(1)}, s32[1,1,32]{2,1,0:T(1,128)}, u32[]{:S(2)}) copy-start(s32[1,1,32]{2,1,0:T(1,128)} %param.17) | copy-start | bytes 388
  12.0 42.3 %copy-start.4 = (bf16[1,128,1280]{2,1,0:T(8,128)(2,1)S(1)}, bf16[1,128,1280]{2,1,0:T(8,128)(2,1)}, u32[]{:S(2)}) copy-start(bf16[1,128,1280]{2,1,0:T(8,128)(2,1)} %param.16) | copy-start | bytes 983044
  15.1 3.6 %collective-permute-start.3 = (bf16[64,2560]{1,0:T(8,128)(2,1)S(1)}, bf16[64,2560]{1,0:T(8,128)(2,1)S(1)}, u32[]{:S(2)}, u32[]{:S(2)}) collective-permute-start(bf16[64,2560]{1,0:T(8,128)(2,1)S(1)} %get-tuple-element.32), channel_id=1, source_target_pairs={{0,8},{8,0},{16,24},{24,16},{1,9},{9,1},{17,25},{25,17},{2,10},{10... | collective-permute-start | bytes 983048 | tf_op jit(solution)/shard_map/ppermute | solution.py:246
  18.6 2.0 %collective-permute-start.7 = (bf16[64,2560]{1,0:T(8,128)(2,1)S(1)}, bf16[64,2560]{1,0:T(8,128)(2,1)S(1)}, u32[]{:S(2)}, u32[]{:S(2)}) collective-permute-start(bf16[64,2560]{1,0:T(8,128)(2,1)S(1)} %get-tuple-element.39), channel_id=1, source_target_pairs={{0,8},{8,0},{16,24},{24,16},{1,9},{9,1},{17,25},{25,17},{2,10},{10... | collective-permute-start | bytes 983048 | tf_op jit(solution)/shard_map/ppermute | solution.py:246
  18.8 7.1 %collective-permute-start.4 = (bf16[32,2560]{1,0:T(8,128)(2,1)S(1)}, bf16[32,2560]{1,0:T(8,128)(2,1)S(1)}, u32[]{:S(2)}, u32[]{:S(2)}) collective-permute-start(bf16[32,2560]{1,0:T(8,128)(2,1)S(1)} %get-tuple-element.34), channel_id=1, source_target_pairs={{0,16},{8,24},{16,0},{24,8},{1,17},{9,25},{17,1},{25,9},{2,18},{10... | collective-permute-start | bytes 491528 | tf_op jit(solution)/shard_map/ppermute | solution.py:246
  20.7 9.9 %collective-permute-start.8 = (bf16[32,2560]{1,0:T(8,128)(2,1)S(1)}, bf16[32,2560]{1,0:T(8,128)(2,1)S(1)}, u32[]{:S(2)}, u32[]{:S(2)}) collective-permute-start(bf16[32,2560]{1,0:T(8,128)(2,1)S(1)} %get-tuple-element.41), channel_id=1, source_target_pairs={{0,16},{8,24},{16,0},{24,8},{1,17},{9,25},{17,1},{25,9},{2,18},{10... | collective-permute-start | bytes 491528 | tf_op jit(solution)/shard_map/ppermute | solution.py:246
  26.3 15.3 %collective-permute-start.5 = (bf16[8,2688]{1,0:T(8,128)(2,1)S(1)}, bf16[8,2688]{1,0:T(8,128)(2,1)S(1)}, u32[]{:S(2)}, u32[]{:S(2)}) collective-permute-start(bf16[8,2688]{1,0:T(8,128)(2,1)S(1)} %get-tuple-element.36.refs_6_), channel_id=1, source_target_pairs={{0,4},{1,5},{2,6},{3,7},{4,0},{5,1},{6,2},{7,3},{8,12},{9,13},{10,... | collective-permute-start | bytes 129032 | tf_op jit(solution)/shard_map/ppermute | solution.py:246
  29.2 13.8 %collective-permute-start.6 = (bf16[8,2688]{1,0:T(8,128)(2,1)S(1)}, bf16[8,2688]{1,0:T(8,128)(2,1)S(1)}, u32[]{:S(2)}, u32[]{:S(2)}) collective-permute-start(bf16[8,2688]{1,0:T(8,128)(2,1)S(1)} %get-tuple-element.37.refs_7_), channel_id=1, source_target_pairs={{0,6},{1,7},{2,4},{3,5},{4,2},{5,3},{6,0},{7,1},{8,14},{9,15},{10,... | collective-permute-start | bytes 129032 | tf_op jit(solution)/shard_map/ppermute | solution.py:246
  31.2 5.6 %collective-permute-start.14 = (bf16[8,2560]{1,0:T(8,128)(2,1)S(1)}, bf16[8,2560]{1,0:T(8,128)(2,1)S(1)}, u32[]{:S(2)}, u32[]{:S(2)}) collective-permute-start(bf16[8,2560]{1,0:T(8,128)(2,1)S(1)} %get-tuple-element.48), channel_id=1, source_target_pairs={{0,4},{1,5},{2,6},{3,7},{4,0},{5,1},{6,2},{7,3},{8,12},{9,13},{10,... | collective-permute-start | bytes 122888 | tf_op jit(solution)/shard_map/ppermute | solution.py:246
  32.9 6.6 %collective-permute-start.15 = (bf16[8,2560]{1,0:T(8,128)(2,1)S(1)}, bf16[8,2560]{1,0:T(8,128)(2,1)S(1)}, u32[]{:S(2)}, u32[]{:S(2)}) collective-permute-start(bf16[8,2560]{1,0:T(8,128)(2,1)S(1)} %get-tuple-element.49), channel_id=1, source_target_pairs={{0,6},{1,7},{2,4},{3,5},{4,2},{5,3},{6,0},{7,1},{8,14},{9,15},{10,... | collective-permute-start | bytes 122888 | tf_op jit(solution)/shard_map/ppermute | solution.py:246
  33.8 11.2 %collective-permute-start.9 = (bf16[8,5248]{1,0:T(8,128)(2,1)S(1)}, bf16[8,5248]{1,0:T(8,128)(2,1)S(1)}, u32[]{:S(2)}, u32[]{:S(2)}) collective-permute-start(bf16[8,5248]{1,0:T(8,128)(2,1)S(1)} %get-tuple-element.43), channel_id=1, source_target_pairs={{0,5},{1,4},{2,7},{3,6},{4,1},{5,0},{6,3},{7,2},{8,13},{9,12},{10,... | collective-permute-start | bytes 251912 | tf_op jit(solution)/shard_map/ppermute | solution.py:246
  36.8 8.3 %collective-permute-start.10 = (bf16[8,5248]{1,0:T(8,128)(2,1)S(1)}, bf16[8,5248]{1,0:T(8,128)(2,1)S(1)}, u32[]{:S(2)}, u32[]{:S(2)}) collective-permute-start(bf16[8,5248]{1,0:T(8,128)(2,1)S(1)} %get-tuple-element.44), channel_id=1, source_target_pairs={{0,1},{1,0},{2,3},{3,2},{4,5},{5,4},{6,7},{7,6},{8,9},{9,8},{10,11... | collective-permute-start | bytes 251912 | tf_op jit(solution)/shard_map/ppermute | solution.py:246
  39.5 7.2 %collective-permute-start.11 = (bf16[8,5248]{1,0:T(8,128)(2,1)S(1)}, bf16[8,5248]{1,0:T(8,128)(2,1)S(1)}, u32[]{:S(2)}, u32[]{:S(2)}) collective-permute-start(bf16[8,5248]{1,0:T(8,128)(2,1)S(1)} %get-tuple-element.45), channel_id=1, source_target_pairs={{0,7},{1,6},{2,5},{3,4},{4,3},{5,2},{6,1},{7,0},{8,15},{9,14},{10,... | collective-permute-start | bytes 251912 | tf_op jit(solution)/shard_map/ppermute | solution.py:246
  41.6 5.4 %collective-permute-start.12 = (bf16[8,5248]{1,0:T(8,128)(2,1)S(1)}, bf16[8,5248]{1,0:T(8,128)(2,1)S(1)}, u32[]{:S(2)}, u32[]{:S(2)}) collective-permute-start(bf16[8,5248]{1,0:T(8,128)(2,1)S(1)} %get-tuple-element.46), channel_id=1, source_target_pairs={{0,2},{1,3},{2,0},{3,1},{4,6},{5,7},{6,4},{7,5},{8,10},{9,11},{10,... | collective-permute-start | bytes 251912 | tf_op jit(solution)/shard_map/ppermute | solution.py:246
  43.0 5.4 %collective-permute-start.13 = (bf16[8,5248]{1,0:T(8,128)(2,1)S(1)}, bf16[8,5248]{1,0:T(8,128)(2,1)S(1)}, u32[]{:S(2)}, u32[]{:S(2)}) collective-permute-start(bf16[8,5248]{1,0:T(8,128)(2,1)S(1)} %get-tuple-element.47), channel_id=1, source_target_pairs={{0,3},{1,2},{2,1},{3,0},{4,7},{5,6},{6,5},{7,4},{8,11},{9,10},{10,... | collective-permute-start | bytes 251912 | tf_op jit(solution)/shard_map/ppermute | solution.py:246
  49.5 11.2 %all-to-all-start = ((bf16[32,2,768]{2,1,0:T(2,128)(2,1)}), bf16[32,2,768]{2,1,0:T(2,128)(2,1)S(1)}, u32[]{:S(2)}, u32[]{:S(2)}) async-start(bf16[32,2,768]{2,1,0:T(2,128)(2,1)} %get-tuple-element.56), calls=%async_computation | async-start | bytes 196608 | tf_op jit(solution)/shard_map/all_to_all | solution.py:253

commit v15 on v14

--- a/solution.py
+++ b/solution.py
@@ -55,17 +55,16 @@
     x = jnp.concatenate([ref[...] for ref in x_refs], axis=0)
     if with_sum:
         refs[blocks + 4][...] = dot(jnp.ones((16, x.shape[0]), BF16), x, (1, 0))[:1]
-    x = x.T
     half = keep_ref.shape[0]
     for t in range(0, keep_ref.shape[1], tile):
-        product = dot(w_ref[first + t : first + t + tile], x, (1, 0)).T.astype(BF16)
+        product = dot(x, w_ref[first + t : first + t + tile], (1, 1)).astype(BF16)
         keep_ref[:, t : t + tile] = product[:half]
         send_ref[:, t : t + tile] = product[half:]
 
 
 def project(x_blocks, w_down, touched, first, width, with_sum):
     blocks, (rows, depth) = len(x_blocks), x_blocks[0].shape
-    tile = 1280
+    tile = 512
     while width % tile:
         tile //= 2
     out_shape = [jax.ShapeDtypeStruct((blocks * rows // 2, width), BF16)] * 2
@@ -422,6 +421,35 @@
     )(out_grads, queries, keys, values, probs, probs_t)
 
 
+def finish_kernel(width, gain_scale, bias_scale, shared_ref, gain_ref, bias_ref):
+    devices, lines, line_width = shared_ref.shape
+    total = jnp.sum(shared_ref[...].astype(F32), axis=0) * gain_scale
+    for line in range(lines):
+        at = line * line_width
+        end = min(at + line_width, width)
+        gain_ref[at:end] = total[line, : end - at]
+    start = width - (lines - 1) * line_width
+    for device in range(devices):
+        piece = line_width - start
+        own = shared_ref[device, lines - 1, start:].astype(F32) * bias_scale
+        bias_ref[device * piece : (device + 1) * piece] = own
+
+
+def finish(shared, width, gain_scale, bias_scale):
+    devices, lines, line_width = shared.shape
+    return pl.pallas_call(
+        functools.partial(finish_kernel, width, gain_scale, bias_scale),
+        out_shape=[
+            jax.ShapeDtypeStruct((width,), F32),
+            jax.ShapeDtypeStruct((devices * (lines * line_width - width),), F32),
+        ],
+        in_specs=vmem(1),
+        out_specs=vmem(2),
+        compiler_params=pltpu.CompilerParams(vmem_limit_bytes=VMEM_BYTES),
+        name="finish",
+    )(shared)
+
+
 def body(llm_grads, token_target, patches, gain, w_down, queries, keys, values, window_ids):
     grad_rows = llm_grads[0]
     rows = grad_rows.shape[0]
@@ -486,18 +514,15 @@
     else:
         share = jax.ShapeDtypeStruct((1, width), F32)
     out_grads, shared = norm_backward(routed, peers, places, patches[0], gain[None], share)
+    gain_scale = 1.0 / math.sqrt(devices * patches.shape[1])
+    bias_scale = 1.0 / math.sqrt(devices * rows)
     if carries:
-        shared = exchange(shared, ("img", "seq"), devices).astype(F32).reshape(devices, -1)
-        gain_total = jnp.sum(shared[:, :width], axis=0)
-        bias_total = shared[:, width:].reshape(-1)
+        shared = exchange(shared, ("img", "seq"), devices)
+        gain_grad, bias_grad = finish(shared, width, gain_scale, bias_scale)
     else:
-        gain_total = lax.psum(shared[0], ("img", "seq"))
-        bias_total = lax.all_gather(lax.psum(bias_part[0], "seq"), "img", tiled=True)
-    gain_grad = gain_total / math.sqrt(devices * patches.shape[1])
-    bias_grad = bias_total / math.sqrt(devices * rows)
+        gain_grad = lax.psum(shared[0], ("img", "seq")) * gain_scale
+        bias_grad = lax.all_gather(lax.psum(bias_part[0], "seq"), "img", tiled=True) * bias_scale
     grads = window_backward(out_grads, queries[0], keys[0], values[0], probs, probs_t)
-    gain_grad = gain_total / math.sqrt(devices * patches.shape[1])
-    bias_grad = bias_total / math.sqrt(devices * rows)
     return (grads[0][None], grads[1][None], grads[2][None], gain_grad, bias_grad)
 
 

time: 62.3 us -> 62.6 us (level)
  Pallas kernels: 11.7 us -> 13.4 us
  local copies, waits for them, and re-layouts: 8.8 us -> 8.15 us
  other arithmetic: 0.63 us -> 0 us
    pallas_call x2, Pallas kernels: 6.05 us -> 7.01 us  [project(): pl.pallas_call(functools.partial(project_kernel, blocks, first, tile, wit...]
    pallas_call x0 -> x1, Pallas kernels: none -> 0.73 us  [finish(): pl.pallas_call(functools.partial(finish_kernel, width, gain_scale, bias_s...]
    unnamed x18 -> x16, local copies, waits for them, and re-layouts: 7.65 us -> 7.01 us
  transfers between devices with their start and end apart: 17 -> 17, of which waited for: 6 -> 6; matrix products, arithmetic and copies ran while one was open for 0% -> 0% of each run, Pallas kernels for 12% -> 13%
where the time goes in v15:
time: 62.6 us; the launch traced here: 62.4 us
  starting transfers between devices  28.4 us (45%)
  Pallas kernels  13.4 us (21%)
  waiting for transfers between devices  11.6 us (19%)
  local copies, waits for them, and re-layouts  8.15 us (13%)
  between operations  0.84 us (1%)
    ppermute x16, starting transfers between devices, swap(): return lax.ppermute(x, axis, [(i, i ^ mask) for i in range(n)])  24.8 us
    ppermute x16, waiting for transfers between devices, swap(): return lax.ppermute(x, axis, [(i, i ^ mask) for i in range(n)])  7.55 us
    unnamed x16, local copies, waits for them, and re-layouts  7.01 us
    pallas_call x2, Pallas kernels, project(): pl.pallas_call(functools.partial(project_kernel, blocks, first, tile, wit...  7.01 us
    all_to_all x1, waiting for transfers between devices, exchange(): lax.all_to_all(x, axis, split_axis=0, concat_axis=0, tiled=True)  4.07 us
    all_to_all x1, starting transfers between devices, exchange(): lax.all_to_all(x, axis, split_axis=0, concat_axis=0, tiled=True)  3.63 us
    pallas_call x1, Pallas kernels, window_backward(): pl.pallas_call(window_kernel, out_shape=[shape] * 3, in_specs=vmem(6), ou...  2.38 us
  transfers between devices with their start and end apart: 17, of which 6 were waited for; matrix products, arithmetic and copies ran while one was open for 0% of the time, Pallas kernels for 13%

profile of v15, /device:TPU:0, one launch (start us, length us, event | category | flops | bytes accessed | tf_op | source)
XLA Modules:
  0.0 62.4 jit_solution(11047994695641642300)
XLA Ops:
  0.7 1.1 %dynamic-slice_bitcast_fusion = (bf16[32,2048]{1,0:T(8,128)(2,1)S(1)}, bf16[32,2048]{1,0:T(8,128)(2,1)S(1)}, bf16[32,2048]{1,0:T(8,128)(2,1)S(1)}, bf16[32,2048]{1,0:T(8,128)(2,1)S(1)}) fusion(bf16[1,32,8192]{2,1,0:T(8,128)(2,1)} %param.9, s32[]{:T(128)S(6)} %select_n.15, s32[]{:T(128)S(6)} %select_n.13, s32[]{:T(128)S(6)} %select_n.12, s32[]{:T(128)S(6)} %select_n.14), kind=kLoop, calls=%fused_computation | loop fusion | bytes 1048592 | tf_op jit(solution)/shard_map/dynamic_slice | solution.py:471
  1.8 2.5 %collective-permute-start.2 = (bf16[32,2048]{1,0:T(8,128)(2,1)S(1)}, bf16[32,2048]{1,0:T(8,128)(2,1)S(1)}, u32[]{:S(2)}, u32[]{:S(2)}) collective-permute-start(bf16[32,2048]{1,0:T(8,128)(2,1)S(1)} %get-tuple-element.61), channel_id=1, source_target_pairs={{0,24},{8,16},{16,8},{24,0},{1,25},{9,17},{17,9},{25,1},{2,26},{10... | collective-permute-start | bytes 393224 | tf_op jit(solution)/shard_map/ppermute | solution.py:245
  4.3 0.6 %collective-permute-start = (bf16[32,2048]{1,0:T(8,128)(2,1)S(1)}, bf16[32,2048]{1,0:T(8,128)(2,1)S(1)}, u32[]{:S(2)}, u32[]{:S(2)}) collective-permute-start(bf16[32,2048]{1,0:T(8,128)(2,1)S(1)} %get-tuple-element.62), channel_id=1, source_target_pairs={{0,16},{8,24},{16,0},{24,8},{1,17},{9,25},{17,1},{25,9},{2,18},{10... | collective-permute-start | bytes 393224 | tf_op jit(solution)/shard_map/ppermute | solution.py:245
  4.9 0.0 collective-permute-start.1
  5.0 0.0 copy-start
  5.0 7.0 %copy-done = bf16[5120,2048]{1,0:T(8,128)(2,1)S(1)} copy-done((bf16[5120,2048]{1,0:T(8,128)(2,1)S(1)}, bf16[5120,2048]{1,0:T(8,128)(2,1)}, u32[]{:S(2)}) %copy-start) | copy-done | bytes 20971544
  11.9 0.0 collective-permute-done.2.refs_3_
  11.9 0.0 collective-permute-done.refs_1_
  11.9 0.0 collective-permute-done.1.refs_2_
  11.9 0.0 copy-start.5
  11.9 0.0 copy-start.7
  12.0 0.0 copy-start.1
  12.0 0.0 copy-start.2
  12.0 0.0 copy-start.3
  12.0 0.0 copy-start.6
  12.0 0.0 copy-start.4
  12.0 3.5 %project.2 = (bf16[64,2560]{1,0:T(8,128)(2,1)S(1)}, bf16[64,2560]{1,0:T(8,128)(2,1)S(1)}, f32[1,2048]{1,0:T(1,128)S(1)}) custom-call(bf16[32,2048]{1,0:T(8,128)(2,1)S(1)} %get-tuple-element.63.refs_0_, bf16[32,2048]{1,0:T(8,128)(2,1)S(1)} %collective-permute-done.refs_1_, bf16[32,2048]{1,0:T(8,128)(2,1)S(1)} %collective-permute-done.1.refs_2_, ...), custom_call_target="tpu_custom_call" | custom-call | flops 1342177280 | bytes 10485760 | tf_op jit(solution)/shard_map/project/pallas_call | solution.py:73
  15.5 0.5 collective-permute-start.3
  16.1 3.5 %project.3 = (bf16[64,2560]{1,0:T(8,128)(2,1)S(1)}, bf16[64,2560]{1,0:T(8,128)(2,1)S(1)}) custom-call(bf16[32,2048]{1,0:T(8,128)(2,1)S(1)} %get-tuple-element.63.refs_0_, bf16[32,2048]{1,0:T(8,128)(2,1)S(1)} %collective-permute-done.refs_1_, bf16[32,2048]{1,0:T(8,128)(2,1)S(1)} %collective-permute-done.1.refs_2_, ...), custom_call_target="tpu_custom_call" | custom-call | flops 1342177280 | bytes 10485760 | tf_op jit(solution)/shard_map/project/pallas_call | solution.py:73
  19.6 0.1 collective-permute-start.7
  19.7 0.0 collective-permute-done.3.got_ref
  19.7 0.1 halve.2
  19.8 1.8 %collective-permute-start.4 = (bf16[32,2560]{1,0:T(8,128)(2,1)S(1)}, bf16[32,2560]{1,0:T(8,128)(2,1)S(1)}, u32[]{:S(2)}, u32[]{:S(2)}) collective-permute-start(bf16[32,2560]{1,0:T(8,128)(2,1)S(1)} %get-tuple-element.36), channel_id=1, source_target_pairs={{0,16},{8,24},{16,0},{24,8},{1,17},{9,25},{17,1},{25,9},{2,18},{10... | collective-permute-start | bytes 491528 | tf_op jit(solution)/shard_map/ppermute | solution.py:245
  21.6 0.0 collective-permute-done.7.got_ref
  21.6 0.1 halve.3
  21.7 1.2 %collective-permute-start.8 = (bf16[32,2560]{1,0:T(8,128)(2,1)S(1)}, bf16[32,2560]{1,0:T(8,128)(2,1)S(1)}, u32[]{:S(2)}, u32[]{:S(2)}) collective-permute-start(bf16[32,2560]{1,0:T(8,128)(2,1)S(1)} %get-tuple-element.43), channel_id=1, source_target_pairs={{0,16},{8,24},{16,0},{24,8},{1,17},{9,25},{17,1},{25,9},{2,18},{10... | collective-permute-start | bytes 491528 | tf_op jit(solution)/shard_map/ppermute | solution.py:245
  22.8 4.0 %collective-permute-done.4.refs_2_ = bf16[32,2560]{1,0:T(8,128)(2,1)S(1)} collective-permute-done((bf16[32,2560]{1,0:T(8,128)(2,1)S(1)}, bf16[32,2560]{1,0:T(8,128)(2,1)S(1)}, u32[]{:S(2)}, u32[]{:S(2)}) %collective-permute-start.4) | collective-permute-done | bytes 163872 | tf_op jit(solution)/shard_map/ppermute | solution.py:245
  26.8 0.0 copy-done.5
  26.8 0.4 pack.2
  27.2 2.9 %collective-permute-start.5 = (bf16[8,2688]{1,0:T(8,128)(2,1)S(1)}, bf16[8,2688]{1,0:T(8,128)(2,1)S(1)}, u32[]{:S(2)}, u32[]{:S(2)}) collective-permute-start(bf16[8,2688]{1,0:T(8,128)(2,1)S(1)} %get-tuple-element.38.refs_6_), channel_id=1, source_target_pairs={{0,4},{1,5},{2,6},{3,7},{4,0},{5,1},{6,2},{7,3},{8,12},{9,13},{10,... | collective-permute-start | bytes 129032 | tf_op jit(solution)/shard_map/ppermute | solution.py:245
  30.2 1.3 %collective-permute-start.6 = (bf16[8,2688]{1,0:T(8,128)(2,1)S(1)}, bf16[8,2688]{1,0:T(8,128)(2,1)S(1)}, u32[]{:S(2)}, u32[]{:S(2)}) collective-permute-start(bf16[8,2688]{1,0:T(8,128)(2,1)S(1)} %get-tuple-element.39.refs_7_), channel_id=1, source_target_pairs={{0,6},{1,7},{2,4},{3,5},{4,2},{5,3},{6,0},{7,1},{8,14},{9,15},{10,... | collective-permute-start | bytes 129032 | tf_op jit(solution)/shard_map/ppermute | solution.py:245
  31.5 0.0 collective-permute-done.8.refs_4_
  31.5 0.6 pack.3
  32.1 1.8 %collective-permute-start.14 = (bf16[8,2560]{1,0:T(8,128)(2,1)S(1)}, bf16[8,2560]{1,0:T(8,128)(2,1)S(1)}, u32[]{:S(2)}, u32[]{:S(2)}) collective-permute-start(bf16[8,2560]{1,0:T(8,128)(2,1)S(1)} %get-tuple-element.50), channel_id=1, source_target_pairs={{0,4},{1,5},{2,6},{3,7},{4,0},{5,1},{6,2},{7,3},{8,12},{9,13},{10,... | collective-permute-start | bytes 122888 | tf_op jit(solution)/shard_map/ppermute | solution.py:245
  33.9 0.9 %collective-permute-start.15 = (bf16[8,2560]{1,0:T(8,128)(2,1)S(1)}, bf16[8,2560]{1,0:T(8,128)(2,1)S(1)}, u32[]{:S(2)}, u32[]{:S(2)}) collective-permute-start(bf16[8,2560]{1,0:T(8,128)(2,1)S(1)} %get-tuple-element.51), channel_id=1, source_target_pairs={{0,6},{1,7},{2,4},{3,5},{4,2},{5,3},{6,0},{7,1},{8,14},{9,15},{10,... | collective-permute-start | bytes 122888 | tf_op jit(solution)/shard_map/ppermute | solution.py:245
  34.8 2.8 %collective-permute-start.9 = (bf16[8,5248]{1,0:T(8,128)(2,1)S(1)}, bf16[8,5248]{1,0:T(8,128)(2,1)S(1)}, u32[]{:S(2)}, u32[]{:S(2)}) collective-permute-start(bf16[8,5248]{1,0:T(8,128)(2,1)S(1)} %get-tuple-element.45), channel_id=1, source_target_pairs={{0,5},{1,4},{2,7},{3,6},{4,1},{5,0},{6,3},{7,2},{8,13},{9,12},{10,... | collective-permute-start | bytes 251912 | tf_op jit(solution)/shard_map/ppermute | solution.py:245
  37.6 0.1 collective-permute-done.14.refs_8_
  37.7 2.7 %collective-permute-start.10 = (bf16[8,5248]{1,0:T(8,128)(2,1)S(1)}, bf16[8,5248]{1,0:T(8,128)(2,1)S(1)}, u32[]{:S(2)}, u32[]{:S(2)}) collective-permute-start(bf16[8,5248]{1,0:T(8,128)(2,1)S(1)} %get-tuple-element.46), channel_id=1, source_target_pairs={{0,1},{1,0},{2,3},{3,2},{4,5},{5,4},{6,7},{7,6},{8,9},{9,8},{10,11... | collective-permute-start | bytes 251912 | tf_op jit(solution)/shard_map/ppermute | solution.py:245
  40.4 0.0 collective-permute-done.15.refs_9_
  40.4 2.0 %collective-permute-start.11 = (bf16[8,5248]{1,0:T(8,128)(2,1)S(1)}, bf16[8,5248]{1,0:T(8,128)(2,1)S(1)}, u32[]{:S(2)}, u32[]{:S(2)}) collective-permute-start(bf16[8,5248]{1,0:T(8,128)(2,1)S(1)} %get-tuple-element.47), channel_id=1, source_target_pairs={{0,7},{1,6},{2,5},{3,4},{4,3},{5,2},{6,1},{7,0},{8,15},{9,14},{10,... | collective-permute-start | bytes 251912 | tf_op jit(solution)/shard_map/ppermute | solution.py:245
  42.5 0.0 collective-permute-done.5.refs_0_
  42.5 1.4 %collective-permute-start.12 = (bf16[8,5248]{1,0:T(8,128)(2,1)S(1)}, bf16[8,5248]{1,0:T(8,128)(2,1)S(1)}, u32[]{:S(2)}, u32[]{:S(2)}) collective-permute-start(bf16[8,5248]{1,0:T(8,128)(2,1)S(1)} %get-tuple-element.48), channel_id=1, source_target_pairs={{0,2},{1,3},{2,0},{3,1},{4,6},{5,7},{6,4},{7,5},{8,10},{9,11},{10,... | collective-permute-start | bytes 251912 | tf_op jit(solution)/shard_map/ppermute | solution.py:245
  43.9 0.0 collective-permute-done.6.refs_1_
  43.9 2.1 %collective-permute-start.13 = (bf16[8,5248]{1,0:T(8,128)(2,1)S(1)}, bf16[8,5248]{1,0:T(8,128)(2,1)S(1)}, u32[]{:S(2)}, u32[]{:S(2)}) collective-permute-start(bf16[8,5248]{1,0:T(8,128)(2,1)S(1)} %get-tuple-element.49), channel_id=1, source_target_pairs={{0,3},{1,2},{2,1},{3,0},{4,7},{5,6},{6,5},{7,4},{8,11},{9,10},{10,... | collective-permute-start | bytes 251912 | tf_op jit(solution)/shard_map/ppermute | solution.py:245
  46.0 0.0 copy-done.7
  46.0 0.0 collective-permute-done.9.refs_3_
  46.0 0.0 collective-permute-done.10.refs_4_
  46.0 1.6 %collective-permute-done.11.refs_5_ = bf16[8,5248]{1,0:T(8,128)(2,1)S(1)} collective-permute-done((bf16[8,5248]{1,0:T(8,128)(2,1)S(1)}, bf16[8,5248]{1,0:T(8,128)(2,1)S(1)}, u32[]{:S(2)}, u32[]{:S(2)}) %collective-permute-start.11) | collective-permute-done | bytes 84000 | tf_op jit(solution)/shard_map/ppermute | solution.py:245
  47.6 0.2 collective-permute-done.12.refs_6_
  47.8 1.5 %collective-permute-done.13.refs_7_ = bf16[8,5248]{1,0:T(8,128)(2,1)S(1)} collective-permute-done((bf16[8,5248]{1,0:T(8,128)(2,1)S(1)}, bf16[8,5248]{1,0:T(8,128)(2,1)S(1)}, u32[]{:S(2)}, u32[]{:S(2)}) %collective-permute-start.13) | collective-permute-done | bytes 84000 | tf_op jit(solution)/shard_map/ppermute | solution.py:245
  49.4 0.0 copy-done.1
  49.4 1.1 %norm.1 = (bf16[128,1280]{1,0:T(8,128)(2,1)S(1)}, bf16[32,2,768]{2,1,0:T(2,128)(2,1)}) custom-call(bf16[128,1280]{1,0:T(8,128)(2,1)S(1)} %bitcast.17, f32[1,1280]{1,0:T(1,128)S(1)} %broadcast_in_dim.12.gain_ref, bf16[8,2688]{1,0:T(8,128)(2,1)S(1)} %collective-permute-done.5.refs_0_, bf16[8,2688]{1,0:T(8,128)(2,1)S(1)} %collective-permute-done.6.refs_1_, ...), custom_call_target="tpu_custom_call" | custom-call | flops 85983232 | bytes 1327104 | tf_op jit(solution)/shard_map/norm/pallas_call | solution.py:353
  50.5 3.6 %all-to-all-start = ((bf16[32,2,768]{2,1,0:T(2,128)(2,1)}), bf16[32,2,768]{2,1,0:T(2,128)(2,1)S(1)}, u32[]{:S(2)}, u32[]{:S(2)}) async-start(bf16[32,2,768]{2,1,0:T(2,128)(2,1)} %get-tuple-element.58), calls=%async_computation | async-start | bytes 196608 | tf_op jit(solution)/shard_map/all_to_all | solution.py:252
  54.1 0.0 copy-done.2
  54.1 0.0 copy-done.3
  54.2 0.0 copy-done.6
  54.2 1.1 %probs.1 = (f32[16,128,128]{2,1,0:T(8,128)S(1)}, f32[16,128,128]{2,1,0:T(8,128)S(1)}) custom-call(bf16[128,1280]{1,0:T(8,128)(2,1)S(1)} %bitcast.18, bf16[128,1280]{1,0:T(8,128)(2,1)S(1)} %bitcast.20, s32[1,32]{1,0:T(1,128)S(1)} %bitcast.23), custom_call_target="tpu_custom_call" | custom-call | flops 268435456 | bytes 2097152 | tf_op jit(solution)/shard_map/probs/pallas_call | solution.py:284
  55.2 0.0 copy-done.4
  55.2 2.4 %window.1 = (bf16[128,1280]{1,0:T(8,128)(2,1)}, bf16[128,1280]{1,0:T(8,128)(2,1)}, bf16[128,1280]{1,0:T(8,128)(2,1)}) custom-call(bf16[128,1280]{1,0:T(8,128)(2,1)S(1)} %get-tuple-element.52.g_ref, bf16[128,1280]{1,0:T(8,128)(2,1)S(1)} %bitcast.19, bf16[128,1280]{1,0:T(8,128)(2,1)S(1)} %bitcast.21, bf16[128,1280]{1,0:T(8,128)(2,1)S(1)} %bitcast.22, ...), custom_call_target="tpu_custom_call" | custom-call | flops 335544320 | bytes 4390912 | tf_op jit(solution)/shard_map/window/pallas_call | solution.py:409
  57.6 4.1 %all-to-all-done.shared_ref = bf16[32,2,768]{2,1,0:T(2,128)(2,1)S(1)} async-done(((bf16[32,2,768]{2,1,0:T(2,128)(2,1)}), bf16[32,2,768]{2,1,0:T(2,128)(2,1)S(1)}, u32[]{:S(2)}, u32[]{:S(2)}) %all-to-all-start) | async-done | bytes 98336 | tf_op jit(solution)/shard_map/all_to_all | solution.py:252
  61.7 0.7 %finish.1 = (f32[1280]{0:T(1024)}, f32[8192]{0:T(1024)}) custom-call(bf16[32,2,768]{2,1,0:T(2,128)(2,1)S(1)} %all-to-all-done.shared_ref), custom_call_target="tpu_custom_call" | custom-call | tf_op jit(solution)/shard_map/finish/pallas_call | solution.py:440
  (2 shorter events, 0.0 us)
Async XLA Ops:
  1.8 10.1 %collective-permute-start.2 = (bf16[32,2048]{1,0:T(8,128)(2,1)S(1)}, bf16[32,2048]{1,0:T(8,128)(2,1)S(1)}, u32[]{:S(2)}, u32[]{:S(2)}) collective-permute-start(bf16[32,2048]{1,0:T(8,128)(2,1)S(1)} %get-tuple-element.61), channel_id=1, source_target_pairs={{0,24},{8,16},{16,8},{24,0},{1,25},{9,17},{17,9},{25,1},{2,26},{10... | collective-permute-start | bytes 393224 | tf_op jit(solution)/shard_map/ppermute | solution.py:245
  4.3 7.7 %collective-permute-start = (bf16[32,2048]{1,0:T(8,128)(2,1)S(1)}, bf16[32,2048]{1,0:T(8,128)(2,1)S(1)}, u32[]{:S(2)}, u32[]{:S(2)}) collective-permute-start(bf16[32,2048]{1,0:T(8,128)(2,1)S(1)} %get-tuple-element.62), channel_id=1, source_target_pairs={{0,16},{8,24},{16,0},{24,8},{1,17},{9,25},{17,1},{25,9},{2,18},{10... | collective-permute-start | bytes 393224 | tf_op jit(solution)/shard_map/ppermute | solution.py:245
  4.9 7.0 %collective-permute-start.1 = (bf16[32,2048]{1,0:T(8,128)(2,1)S(1)}, bf16[32,2048]{1,0:T(8,128)(2,1)S(1)}, u32[]{:S(2)}, u32[]{:S(2)}) collective-permute-start(bf16[32,2048]{1,0:T(8,128)(2,1)S(1)} %get-tuple-element.64), channel_id=1, source_target_pairs={{0,8},{8,0},{16,24},{24,16},{1,9},{9,1},{17,25},{25,17},{2,10},{10... | collective-permute-start | bytes 393224 | tf_op jit(solution)/shard_map/ppermute | solution.py:245
  5.0 7.0 %copy-start = (bf16[5120,2048]{1,0:T(8,128)(2,1)S(1)}, bf16[5120,2048]{1,0:T(8,128)(2,1)}, u32[]{:S(2)}) copy-start(bf16[5120,2048]{1,0:T(8,128)(2,1)} %refs_4_.3) | copy-start | bytes 62914564
  11.9 14.9 %copy-start.5 = (s32[1,32]{1,0:T(1,128)S(1)}, s32[1,32]{1,0:T(1,128)}, u32[]{:S(2)}) copy-start(s32[1,32]{1,0:T(1,128)} %refs_0_.3) | copy-start | bytes 388
  11.9 34.0 %copy-start.7 = (f32[1280]{0:T(1024)S(1)}, f32[1280]{0:T(1024)}, u32[]{:S(2)}) copy-start(f32[1280]{0:T(1024)} %param.12) | copy-start | bytes 15364
  12.0 37.4 %copy-start.1 = (bf16[1,128,1280]{2,1,0:T(8,128)(2,1)S(1)}, bf16[1,128,1280]{2,1,0:T(8,128)(2,1)}, u32[]{:S(2)}) copy-start(bf16[1,128,1280]{2,1,0:T(8,128)(2,1)} %param.11) | copy-start | bytes 983044
  12.0 42.2 %copy-start.2 = (bf16[1,128,1280]{2,1,0:T(8,128)(2,1)S(1)}, bf16[1,128,1280]{2,1,0:T(8,128)(2,1)}, u32[]{:S(2)}) copy-start(bf16[1,128,1280]{2,1,0:T(8,128)(2,1)} %param.14) | copy-start | bytes 983044
  12.0 42.2 %copy-start.3 = (bf16[1,128,1280]{2,1,0:T(8,128)(2,1)S(1)}, bf16[1,128,1280]{2,1,0:T(8,128)(2,1)}, u32[]{:S(2)}) copy-start(bf16[1,128,1280]{2,1,0:T(8,128)(2,1)} %param.15) | copy-start | bytes 983044
  12.0 42.2 %copy-start.6 = (s32[1,1,32]{2,1,0:T(1,128)S(1)}, s32[1,1,32]{2,1,0:T(1,128)}, u32[]{:S(2)}) copy-start(s32[1,1,32]{2,1,0:T(1,128)} %param.17) | copy-start | bytes 388
  12.0 43.2 %copy-start.4 = (bf16[1,128,1280]{2,1,0:T(8,128)(2,1)S(1)}, bf16[1,128,1280]{2,1,0:T(8,128)(2,1)}, u32[]{:S(2)}) copy-start(bf16[1,128,1280]{2,1,0:T(8,128)(2,1)} %param.16) | copy-start | bytes 983044
  15.5 4.2 %collective-permute-start.3 = (bf16[64,2560]{1,0:T(8,128)(2,1)S(1)}, bf16[64,2560]{1,0:T(8,128)(2,1)S(1)}, u32[]{:S(2)}, u32[]{:S(2)}) collective-permute-start(bf16[64,2560]{1,0:T(8,128)(2,1)S(1)} %get-tuple-element.34), channel_id=1, source_target_pairs={{0,8},{8,0},{16,24},{24,16},{1,9},{9,1},{17,25},{25,17},{2,10},{10... | collective-permute-start | bytes 983048 | tf_op jit(solution)/shard_map/ppermute | solution.py:245
  19.6 2.0 %collective-permute-start.7 = (bf16[64,2560]{1,0:T(8,128)(2,1)S(1)}, bf16[64,2560]{1,0:T(8,128)(2,1)S(1)}, u32[]{:S(2)}, u32[]{:S(2)}) collective-permute-start(bf16[64,2560]{1,0:T(8,128)(2,1)S(1)} %get-tuple-element.41), channel_id=1, source_target_pairs={{0,8},{8,0},{16,24},{24,16},{1,9},{9,1},{17,25},{25,17},{2,10},{10... | collective-permute-start | bytes 983048 | tf_op jit(solution)/shard_map/ppermute | solution.py:245
  19.8 7.1 %collective-permute-start.4 = (bf16[32,2560]{1,0:T(8,128)(2,1)S(1)}, bf16[32,2560]{1,0:T(8,128)(2,1)S(1)}, u32[]{:S(2)}, u32[]{:S(2)}) collective-permute-start(bf16[32,2560]{1,0:T(8,128)(2,1)S(1)} %get-tuple-element.36), channel_id=1, source_target_pairs={{0,16},{8,24},{16,0},{24,8},{1,17},{9,25},{17,1},{25,9},{2,18},{10... | collective-permute-start | bytes 491528 | tf_op jit(solution)/shard_map/ppermute | solution.py:245
  21.7 9.8 %collective-permute-start.8 = (bf16[32,2560]{1,0:T(8,128)(2,1)S(1)}, bf16[32,2560]{1,0:T(8,128)(2,1)S(1)}, u32[]{:S(2)}, u32[]{:S(2)}) collective-permute-start(bf16[32,2560]{1,0:T(8,128)(2,1)S(1)} %get-tuple-element.43), channel_id=1, source_target_pairs={{0,16},{8,24},{16,0},{24,8},{1,17},{9,25},{17,1},{25,9},{2,18},{10... | collective-permute-start | bytes 491528 | tf_op jit(solution)/shard_map/ppermute | solution.py:245
  27.2 15.2 %collective-permute-start.5 = (bf16[8,2688]{1,0:T(8,128)(2,1)S(1)}, bf16[8,2688]{1,0:T(8,128)(2,1)S(1)}, u32[]{:S(2)}, u32[]{:S(2)}) collective-permute-start(bf16[8,2688]{1,0:T(8,128)(2,1)S(1)} %get-tuple-element.38.refs_6_), channel_id=1, source_target_pairs={{0,4},{1,5},{2,6},{3,7},{4,0},{5,1},{6,2},{7,3},{8,12},{9,13},{10,... | collective-permute-start | bytes 129032 | tf_op jit(solution)/shard_map/ppermute | solution.py:245
  30.2 13.8 %collective-permute-start.6 = (bf16[8,2688]{1,0:T(8,128)(2,1)S(1)}, bf16[8,2688]{1,0:T(8,128)(2,1)S(1)}, u32[]{:S(2)}, u32[]{:S(2)}) collective-permute-start(bf16[8,2688]{1,0:T(8,128)(2,1)S(1)} %get-tuple-element.39.refs_7_), channel_id=1, source_target_pairs={{0,6},{1,7},{2,4},{3,5},{4,2},{5,3},{6,0},{7,1},{8,14},{9,15},{10,... | collective-permute-start | bytes 129032 | tf_op jit(solution)/shard_map/ppermute | solution.py:245
  32.1 5.6 %collective-permute-start.14 = (bf16[8,2560]{1,0:T(8,128)(2,1)S(1)}, bf16[8,2560]{1,0:T(8,128)(2,1)S(1)}, u32[]{:S(2)}, u32[]{:S(2)}) collective-permute-start(bf16[8,2560]{1,0:T(8,128)(2,1)S(1)} %get-tuple-element.50), channel_id=1, source_target_pairs={{0,4},{1,5},{2,6},{3,7},{4,0},{5,1},{6,2},{7,3},{8,12},{9,13},{10,... | collective-permute-start | bytes 122888 | tf_op jit(solution)/shard_map/ppermute | solution.py:245
  33.9 6.6 %collective-permute-start.15 = (bf16[8,2560]{1,0:T(8,128)(2,1)S(1)}, bf16[8,2560]{1,0:T(8,128)(2,1)S(1)}, u32[]{:S(2)}, u32[]{:S(2)}) collective-permute-start(bf16[8,2560]{1,0:T(8,128)(2,1)S(1)} %get-tuple-element.51), channel_id=1, source_target_pairs={{0,6},{1,7},{2,4},{3,5},{4,2},{5,3},{6,0},{7,1},{8,14},{9,15},{10,... | collective-permute-start | bytes 122888 | tf_op jit(solution)/shard_map/ppermute | solution.py:245
  34.8 11.2 %collective-permute-start.9 = (bf16[8,5248]{1,0:T(8,128)(2,1)S(1)}, bf16[8,5248]{1,0:T(8,128)(2,1)S(1)}, u32[]{:S(2)}, u32[]{:S(2)}) collective-permute-start(bf16[8,5248]{1,0:T(8,128)(2,1)S(1)} %get-tuple-element.45), channel_id=1, source_target_pairs={{0,5},{1,4},{2,7},{3,6},{4,1},{5,0},{6,3},{7,2},{8,13},{9,12},{10,... | collective-permute-start | bytes 251912 | tf_op jit(solution)/shard_map/ppermute | solution.py:245
  37.7 8.2 %collective-permute-start.10 = (bf16[8,5248]{1,0:T(8,128)(2,1)S(1)}, bf16[8,5248]{1,0:T(8,128)(2,1)S(1)}, u32[]{:S(2)}, u32[]{:S(2)}) collective-permute-start(bf16[8,5248]{1,0:T(8,128)(2,1)S(1)} %get-tuple-element.46), channel_id=1, source_target_pairs={{0,1},{1,0},{2,3},{3,2},{4,5},{5,4},{6,7},{7,6},{8,9},{9,8},{10,11... | collective-permute-start | bytes 251912 | tf_op jit(solution)/shard_map/ppermute | solution.py:245
  40.4 7.2 %collective-permute-start.11 = (bf16[8,5248]{1,0:T(8,128)(2,1)S(1)}, bf16[8,5248]{1,0:T(8,128)(2,1)S(1)}, u32[]{:S(2)}, u32[]{:S(2)}) collective-permute-start(bf16[8,5248]{1,0:T(8,128)(2,1)S(1)} %get-tuple-element.47), channel_id=1, source_target_pairs={{0,7},{1,6},{2,5},{3,4},{4,3},{5,2},{6,1},{7,0},{8,15},{9,14},{10,... | collective-permute-start | bytes 251912 | tf_op jit(solution)/shard_map/ppermute | solution.py:245
  42.5 5.4 %collective-permute-start.12 = (bf16[8,5248]{1,0:T(8,128)(2,1)S(1)}, bf16[8,5248]{1,0:T(8,128)(2,1)S(1)}, u32[]{:S(2)}, u32[]{:S(2)}) collective-permute-start(bf16[8,5248]{1,0:T(8,128)(2,1)S(1)} %get-tuple-element.48), channel_id=1, source_target_pairs={{0,2},{1,3},{2,0},{3,1},{4,6},{5,7},{6,4},{7,5},{8,10},{9,11},{10,... | collective-permute-start | bytes 251912 | tf_op jit(solution)/shard_map/ppermute | solution.py:245
  43.9 5.5 %collective-permute-start.13 = (bf16[8,5248]{1,0:T(8,128)(2,1)S(1)}, bf16[8,5248]{1,0:T(8,128)(2,1)S(1)}, u32[]{:S(2)}, u32[]{:S(2)}) collective-permute-start(bf16[8,5248]{1,0:T(8,128)(2,1)S(1)} %get-tuple-element.49), channel_id=1, source_target_pairs={{0,3},{1,2},{2,1},{3,0},{4,7},{5,6},{6,5},{7,4},{8,11},{9,10},{10,... | collective-permute-start | bytes 251912 | tf_op jit(solution)/shard_map/ppermute | solution.py:245
  50.5 11.2 %all-to-all-start = ((bf16[32,2,768]{2,1,0:T(2,128)(2,1)}), bf16[32,2,768]{2,1,0:T(2,128)(2,1)S(1)}, u32[]{:S(2)}, u32[]{:S(2)}) async-start(bf16[32,2,768]{2,1,0:T(2,128)(2,1)} %get-tuple-element.58), calls=%async_computation | async-start | bytes 196608 | tf_op jit(solution)/shard_map/all_to_all | solution.py:252

commit v16 on v15

--- a/solution.py
+++ b/solution.py
@@ -55,9 +55,10 @@
     x = jnp.concatenate([ref[...] for ref in x_refs], axis=0)
     if with_sum:
         refs[blocks + 4][...] = dot(jnp.ones((16, x.shape[0]), BF16), x, (1, 0))[:1]
+    x = x.T
     half = keep_ref.shape[0]
     for t in range(0, keep_ref.shape[1], tile):
-        product = dot(x, w_ref[first + t : first + t + tile], (1, 1)).astype(BF16)
+        product = dot(w_ref[first + t : first + t + tile], x, (1, 0)).T.astype(BF16)
         keep_ref[:, t : t + tile] = product[:half]
         send_ref[:, t : t + tile] = product[half:]
 
@@ -421,7 +422,7 @@
     )(out_grads, queries, keys, values, probs, probs_t)
 
 
-def finish_kernel(width, gain_scale, bias_scale, shared_ref, gain_ref, bias_ref):
+def finish_kernel(width, images, gain_scale, bias_scale, shared_ref, gain_ref, bias_ref):
     devices, lines, line_width = shared_ref.shape
     total = jnp.sum(shared_ref[...].astype(F32), axis=0) * gain_scale
     for line in range(lines):
@@ -432,13 +433,14 @@
     for device in range(devices):
         piece = line_width - start
         own = shared_ref[device, lines - 1, start:].astype(F32) * bias_scale
-        bias_ref[device * piece : (device + 1) * piece] = own
-
-
-def finish(shared, width, gain_scale, bias_scale):
+        place = device % images * (devices // images) + device // images
+        bias_ref[place * piece : (place + 1) * piece] = own
+
+
+def finish(shared, width, images, gain_scale, bias_scale):
     devices, lines, line_width = shared.shape
     return pl.pallas_call(
-        functools.partial(finish_kernel, width, gain_scale, bias_scale),
+        functools.partial(finish_kernel, width, images, gain_scale, bias_scale),
         out_shape=[
             jax.ShapeDtypeStruct((width,), F32),
             jax.ShapeDtypeStruct((devices * (lines * line_width - width),), F32),
@@ -517,8 +519,8 @@
     gain_scale = 1.0 / math.sqrt(devices * patches.shape[1])
     bias_scale = 1.0 / math.sqrt(devices * rows)
     if carries:
-        shared = exchange(shared, ("img", "seq"), devices)
-        gain_grad, bias_grad = finish(shared, width, gain_scale, bias_scale)
+        shared = exchange(shared, ("seq", "img"), devices)
+        gain_grad, bias_grad = finish(shared, width, images, gain_scale, bias_scale)
     else:
         gain_grad = lax.psum(shared[0], ("img", "seq")) * gain_scale
         bias_grad = lax.all_gather(lax.psum(bias_part[0], "seq"), "img", tiled=True) * bias_scale

time: 62.6 us -> 61.9 us (0.989)
  Pallas kernels: 13.4 us -> 12.5 us
    pallas_call x2, Pallas kernels: 7.01 us -> 6.03 us  [project(): pl.pallas_call(functools.partial(project_kernel, blocks, first, tile, wit...]
  transfers between devices with their start and end apart: 17 -> 17, of which waited for: 6 -> 6; matrix products, arithmetic and copies ran while one was open for 0% -> 0% of each run, Pallas kernels for 13% -> 12%
where the time goes in v16:
time: 61.9 us; the launch traced here: 61.7 us
  starting transfers between devices  28.4 us (46%)
  Pallas kernels  12.5 us (20%)
  waiting for transfers between devices  11.9 us (19%)
  local copies, waits for them, and re-layouts  8.15 us (13%)
  between operations  0.83 us (1%)
    ppermute x16, starting transfers between devices, swap(): return lax.ppermute(x, axis, [(i, i ^ mask) for i in range(n)])  24.8 us
    ppermute x16, waiting for transfers between devices, swap(): return lax.ppermute(x, axis, [(i, i ^ mask) for i in range(n)])  7.53 us
    unnamed x16, local copies, waits for them, and re-layouts  7.01 us
    pallas_call x2, Pallas kernels, project(): pl.pallas_call(functools.partial(project_kernel, blocks, first, tile, wit...  6.03 us
    all_to_all x1, waiting for transfers between devices, exchange(): lax.all_to_all(x, axis, split_axis=0, concat_axis=0, tiled=True)  4.32 us
    all_to_all x1, starting transfers between devices, exchange(): lax.all_to_all(x, axis, split_axis=0, concat_axis=0, tiled=True)  3.62 us
    pallas_call x1, Pallas kernels, window_backward(): pl.pallas_call(window_kernel, out_shape=[shape] * 3, in_specs=vmem(6), ou...  2.38 us
  transfers between devices with their start and end apart: 17, of which 6 were waited for; matrix products, arithmetic and copies ran while one was open for 0% of the time, Pallas kernels for 12%

profile of v16, /device:TPU:0, one launch (start us, length us, event | category | flops | bytes accessed | tf_op | source)
XLA Modules:
  0.0 61.7 jit_solution(9648630916802553391)
XLA Ops:
  0.7 1.1 %dynamic-slice_bitcast_fusion = (bf16[32,2048]{1,0:T(8,128)(2,1)S(1)}, bf16[32,2048]{1,0:T(8,128)(2,1)S(1)}, bf16[32,2048]{1,0:T(8,128)(2,1)S(1)}, bf16[32,2048]{1,0:T(8,128)(2,1)S(1)}) fusion(bf16[1,32,8192]{2,1,0:T(8,128)(2,1)} %param.9, s32[]{:T(128)S(6)} %select_n.15, s32[]{:T(128)S(6)} %select_n.13, s32[]{:T(128)S(6)} %select_n.12, s32[]{:T(128)S(6)} %select_n.14), kind=kLoop, calls=%fused_computation | loop fusion | bytes 1048592 | tf_op jit(solution)/shard_map/dynamic_slice | solution.py:473
  1.8 2.5 %collective-permute-start.2 = (bf16[32,2048]{1,0:T(8,128)(2,1)S(1)}, bf16[32,2048]{1,0:T(8,128)(2,1)S(1)}, u32[]{:S(2)}, u32[]{:S(2)}) collective-permute-start(bf16[32,2048]{1,0:T(8,128)(2,1)S(1)} %get-tuple-element.61), channel_id=1, source_target_pairs={{0,24},{8,16},{16,8},{24,0},{1,25},{9,17},{17,9},{25,1},{2,26},{10... | collective-permute-start | bytes 393224 | tf_op jit(solution)/shard_map/ppermute | solution.py:246
  4.3 0.6 %collective-permute-start = (bf16[32,2048]{1,0:T(8,128)(2,1)S(1)}, bf16[32,2048]{1,0:T(8,128)(2,1)S(1)}, u32[]{:S(2)}, u32[]{:S(2)}) collective-permute-start(bf16[32,2048]{1,0:T(8,128)(2,1)S(1)} %get-tuple-element.62), channel_id=1, source_target_pairs={{0,16},{8,24},{16,0},{24,8},{1,17},{9,25},{17,1},{25,9},{2,18},{10... | collective-permute-start | bytes 393224 | tf_op jit(solution)/shard_map/ppermute | solution.py:246
  4.9 0.0 collective-permute-start.1
  5.0 0.0 copy-start
  5.0 7.0 %copy-done = bf16[5120,2048]{1,0:T(8,128)(2,1)S(1)} copy-done((bf16[5120,2048]{1,0:T(8,128)(2,1)S(1)}, bf16[5120,2048]{1,0:T(8,128)(2,1)}, u32[]{:S(2)}) %copy-start) | copy-done | bytes 20971544
  11.9 0.0 collective-permute-done.2.refs_3_
  11.9 0.0 collective-permute-done.refs_1_
  11.9 0.0 collective-permute-done.1.refs_2_
  11.9 0.0 copy-start.5
  11.9 0.0 copy-start.7
  12.0 0.0 copy-start.1
  12.0 0.0 copy-start.2
  12.0 0.0 copy-start.3
  12.0 0.0 copy-start.6
  12.0 0.0 copy-start.4
  12.0 3.1 %project.2 = (bf16[64,2560]{1,0:T(8,128)(2,1)S(1)}, bf16[64,2560]{1,0:T(8,128)(2,1)S(1)}, f32[1,2048]{1,0:T(1,128)S(1)}) custom-call(bf16[32,2048]{1,0:T(8,128)(2,1)S(1)} %get-tuple-element.63.refs_0_, bf16[32,2048]{1,0:T(8,128)(2,1)S(1)} %collective-permute-done.refs_1_, bf16[32,2048]{1,0:T(8,128)(2,1)S(1)} %collective-permute-done.1.refs_2_, ...), custom_call_target="tpu_custom_call" | custom-call | flops 1342177280 | bytes 10485760 | tf_op jit(solution)/shard_map/project/pallas_call | solution.py:74
  15.1 0.5 collective-permute-start.3
  15.6 3.0 %project.3 = (bf16[64,2560]{1,0:T(8,128)(2,1)S(1)}, bf16[64,2560]{1,0:T(8,128)(2,1)S(1)}) custom-call(bf16[32,2048]{1,0:T(8,128)(2,1)S(1)} %get-tuple-element.63.refs_0_, bf16[32,2048]{1,0:T(8,128)(2,1)S(1)} %collective-permute-done.refs_1_, bf16[32,2048]{1,0:T(8,128)(2,1)S(1)} %collective-permute-done.1.refs_2_, ...), custom_call_target="tpu_custom_call" | custom-call | flops 1342177280 | bytes 10485760 | tf_op jit(solution)/shard_map/project/pallas_call | solution.py:74
  18.6 0.1 collective-permute-start.7
  18.7 0.0 collective-permute-done.3.got_ref
  18.7 0.1 halve.2
  18.8 1.8 %collective-permute-start.4 = (bf16[32,2560]{1,0:T(8,128)(2,1)S(1)}, bf16[32,2560]{1,0:T(8,128)(2,1)S(1)}, u32[]{:S(2)}, u32[]{:S(2)}) collective-permute-start(bf16[32,2560]{1,0:T(8,128)(2,1)S(1)} %get-tuple-element.36), channel_id=1, source_target_pairs={{0,16},{8,24},{16,0},{24,8},{1,17},{9,25},{17,1},{25,9},{2,18},{10... | collective-permute-start | bytes 491528 | tf_op jit(solution)/shard_map/ppermute | solution.py:246
  20.6 0.0 collective-permute-done.7.got_ref
  20.6 0.1 halve.3
  20.7 1.2 %collective-permute-start.8 = (bf16[32,2560]{1,0:T(8,128)(2,1)S(1)}, bf16[32,2560]{1,0:T(8,128)(2,1)S(1)}, u32[]{:S(2)}, u32[]{:S(2)}) collective-permute-start(bf16[32,2560]{1,0:T(8,128)(2,1)S(1)} %get-tuple-element.43), channel_id=1, source_target_pairs={{0,16},{8,24},{16,0},{24,8},{1,17},{9,25},{17,1},{25,9},{2,18},{10... | collective-permute-start | bytes 491528 | tf_op jit(solution)/shard_map/ppermute | solution.py:246
  21.9 4.0 %collective-permute-done.4.refs_2_ = bf16[32,2560]{1,0:T(8,128)(2,1)S(1)} collective-permute-done((bf16[32,2560]{1,0:T(8,128)(2,1)S(1)}, bf16[32,2560]{1,0:T(8,128)(2,1)S(1)}, u32[]{:S(2)}, u32[]{:S(2)}) %collective-permute-start.4) | collective-permute-done | bytes 163872 | tf_op jit(solution)/shard_map/ppermute | solution.py:246
  25.9 0.0 copy-done.5
  25.9 0.4 pack.2
  26.3 2.9 %collective-permute-start.5 = (bf16[8,2688]{1,0:T(8,128)(2,1)S(1)}, bf16[8,2688]{1,0:T(8,128)(2,1)S(1)}, u32[]{:S(2)}, u32[]{:S(2)}) collective-permute-start(bf16[8,2688]{1,0:T(8,128)(2,1)S(1)} %get-tuple-element.38.refs_6_), channel_id=1, source_target_pairs={{0,4},{1,5},{2,6},{3,7},{4,0},{5,1},{6,2},{7,3},{8,12},{9,13},{10,... | collective-permute-start | bytes 129032 | tf_op jit(solution)/shard_map/ppermute | solution.py:246
  29.1 1.4 %collective-permute-start.6 = (bf16[8,2688]{1,0:T(8,128)(2,1)S(1)}, bf16[8,2688]{1,0:T(8,128)(2,1)S(1)}, u32[]{:S(2)}, u32[]{:S(2)}) collective-permute-start(bf16[8,2688]{1,0:T(8,128)(2,1)S(1)} %get-tuple-element.39.refs_7_), channel_id=1, source_target_pairs={{0,6},{1,7},{2,4},{3,5},{4,2},{5,3},{6,0},{7,1},{8,14},{9,15},{10,... | collective-permute-start | bytes 129032 | tf_op jit(solution)/shard_map/ppermute | solution.py:246
  30.5 0.0 collective-permute-done.8.refs_4_
  30.5 0.6 pack.3
  31.1 1.8 %collective-permute-start.14 = (bf16[8,2560]{1,0:T(8,128)(2,1)S(1)}, bf16[8,2560]{1,0:T(8,128)(2,1)S(1)}, u32[]{:S(2)}, u32[]{:S(2)}) collective-permute-start(bf16[8,2560]{1,0:T(8,128)(2,1)S(1)} %get-tuple-element.50), channel_id=1, source_target_pairs={{0,4},{1,5},{2,6},{3,7},{4,0},{5,1},{6,2},{7,3},{8,12},{9,13},{10,... | collective-permute-start | bytes 122888 | tf_op jit(solution)/shard_map/ppermute | solution.py:246
  32.9 0.9 %collective-permute-start.15 = (bf16[8,2560]{1,0:T(8,128)(2,1)S(1)}, bf16[8,2560]{1,0:T(8,128)(2,1)S(1)}, u32[]{:S(2)}, u32[]{:S(2)}) collective-permute-start(bf16[8,2560]{1,0:T(8,128)(2,1)S(1)} %get-tuple-element.51), channel_id=1, source_target_pairs={{0,6},{1,7},{2,4},{3,5},{4,2},{5,3},{6,0},{7,1},{8,14},{9,15},{10,... | collective-permute-start | bytes 122888 | tf_op jit(solution)/shard_map/ppermute | solution.py:246
  33.8 2.8 %collective-permute-start.9 = (bf16[8,5248]{1,0:T(8,128)(2,1)S(1)}, bf16[8,5248]{1,0:T(8,128)(2,1)S(1)}, u32[]{:S(2)}, u32[]{:S(2)}) collective-permute-start(bf16[8,5248]{1,0:T(8,128)(2,1)S(1)} %get-tuple-element.45), channel_id=1, source_target_pairs={{0,5},{1,4},{2,7},{3,6},{4,1},{5,0},{6,3},{7,2},{8,13},{9,12},{10,... | collective-permute-start | bytes 251912 | tf_op jit(solution)/shard_map/ppermute | solution.py:246
  36.6 0.1 collective-permute-done.14.refs_8_
  36.7 2.7 %collective-permute-start.10 = (bf16[8,5248]{1,0:T(8,128)(2,1)S(1)}, bf16[8,5248]{1,0:T(8,128)(2,1)S(1)}, u32[]{:S(2)}, u32[]{:S(2)}) collective-permute-start(bf16[8,5248]{1,0:T(8,128)(2,1)S(1)} %get-tuple-element.46), channel_id=1, source_target_pairs={{0,1},{1,0},{2,3},{3,2},{4,5},{5,4},{6,7},{7,6},{8,9},{9,8},{10,11... | collective-permute-start | bytes 251912 | tf_op jit(solution)/shard_map/ppermute | solution.py:246
  39.4 0.0 collective-permute-done.15.refs_9_
  39.4 2.1 %collective-permute-start.11 = (bf16[8,5248]{1,0:T(8,128)(2,1)S(1)}, bf16[8,5248]{1,0:T(8,128)(2,1)S(1)}, u32[]{:S(2)}, u32[]{:S(2)}) collective-permute-start(bf16[8,5248]{1,0:T(8,128)(2,1)S(1)} %get-tuple-element.47), channel_id=1, source_target_pairs={{0,7},{1,6},{2,5},{3,4},{4,3},{5,2},{6,1},{7,0},{8,15},{9,14},{10,... | collective-permute-start | bytes 251912 | tf_op jit(solution)/shard_map/ppermute | solution.py:246
  41.5 0.0 collective-permute-done.5.refs_0_
  41.5 1.4 %collective-permute-start.12 = (bf16[8,5248]{1,0:T(8,128)(2,1)S(1)}, bf16[8,5248]{1,0:T(8,128)(2,1)S(1)}, u32[]{:S(2)}, u32[]{:S(2)}) collective-permute-start(bf16[8,5248]{1,0:T(8,128)(2,1)S(1)} %get-tuple-element.48), channel_id=1, source_target_pairs={{0,2},{1,3},{2,0},{3,1},{4,6},{5,7},{6,4},{7,5},{8,10},{9,11},{10,... | collective-permute-start | bytes 251912 | tf_op jit(solution)/shard_map/ppermute | solution.py:246
  42.9 0.0 collective-permute-done.6.refs_1_
  42.9 2.1 %collective-permute-start.13 = (bf16[8,5248]{1,0:T(8,128)(2,1)S(1)}, bf16[8,5248]{1,0:T(8,128)(2,1)S(1)}, u32[]{:S(2)}, u32[]{:S(2)}) collective-permute-start(bf16[8,5248]{1,0:T(8,128)(2,1)S(1)} %get-tuple-element.49), channel_id=1, source_target_pairs={{0,3},{1,2},{2,1},{3,0},{4,7},{5,6},{6,5},{7,4},{8,11},{9,10},{10,... | collective-permute-start | bytes 251912 | tf_op jit(solution)/shard_map/ppermute | solution.py:246
  45.0 0.0 copy-done.7
  45.0 0.0 collective-permute-done.9.refs_3_
  45.0 0.0 collective-permute-done.10.refs_4_
  45.0 1.6 %collective-permute-done.11.refs_5_ = bf16[8,5248]{1,0:T(8,128)(2,1)S(1)} collective-permute-done((bf16[8,5248]{1,0:T(8,128)(2,1)S(1)}, bf16[8,5248]{1,0:T(8,128)(2,1)S(1)}, u32[]{:S(2)}, u32[]{:S(2)}) %collective-permute-start.11) | collective-permute-done | bytes 84000 | tf_op jit(solution)/shard_map/ppermute | solution.py:246
  46.6 0.2 collective-permute-done.12.refs_6_
  46.9 1.5 %collective-permute-done.13.refs_7_ = bf16[8,5248]{1,0:T(8,128)(2,1)S(1)} collective-permute-done((bf16[8,5248]{1,0:T(8,128)(2,1)S(1)}, bf16[8,5248]{1,0:T(8,128)(2,1)S(1)}, u32[]{:S(2)}, u32[]{:S(2)}) %collective-permute-start.13) | collective-permute-done | bytes 84000 | tf_op jit(solution)/shard_map/ppermute | solution.py:246
  48.4 0.0 copy-done.1
  48.4 1.1 %norm.1 = (bf16[128,1280]{1,0:T(8,128)(2,1)S(1)}, bf16[32,2,768]{2,1,0:T(2,128)(2,1)}) custom-call(bf16[128,1280]{1,0:T(8,128)(2,1)S(1)} %bitcast.17, f32[1,1280]{1,0:T(1,128)S(1)} %broadcast_in_dim.12.gain_ref, bf16[8,2688]{1,0:T(8,128)(2,1)S(1)} %collective-permute-done.5.refs_0_, bf16[8,2688]{1,0:T(8,128)(2,1)S(1)} %collective-permute-done.6.refs_1_, ...), custom_call_target="tpu_custom_call" | custom-call | flops 85983232 | bytes 1327104 | tf_op jit(solution)/shard_map/norm/pallas_call | solution.py:354
  49.5 3.6 %all-to-all-start = ((bf16[32,2,768]{2,1,0:T(2,128)(2,1)}), bf16[32,2,768]{2,1,0:T(2,128)(2,1)S(1)}, u32[]{:S(2)}, u32[]{:S(2)}) async-start(bf16[32,2,768]{2,1,0:T(2,128)(2,1)} %get-tuple-element.58), calls=%async_computation | async-start | bytes 196608 | tf_op jit(solution)/shard_map/all_to_all | solution.py:253
  53.1 0.0 copy-done.2
  53.2 0.0 copy-done.3
  53.2 0.0 copy-done.6
  53.2 1.1 %probs.1 = (f32[16,128,128]{2,1,0:T(8,128)S(1)}, f32[16,128,128]{2,1,0:T(8,128)S(1)}) custom-call(bf16[128,1280]{1,0:T(8,128)(2,1)S(1)} %bitcast.18, bf16[128,1280]{1,0:T(8,128)(2,1)S(1)} %bitcast.20, s32[1,32]{1,0:T(1,128)S(1)} %bitcast.23), custom_call_target="tpu_custom_call" | custom-call | flops 268435456 | bytes 2097152 | tf_op jit(solution)/shard_map/probs/pallas_call | solution.py:285
  54.2 0.0 copy-done.4
  54.3 2.4 %window.1 = (bf16[128,1280]{1,0:T(8,128)(2,1)}, bf16[128,1280]{1,0:T(8,128)(2,1)}, bf16[128,1280]{1,0:T(8,128)(2,1)}) custom-call(bf16[128,1280]{1,0:T(8,128)(2,1)S(1)} %get-tuple-element.52.g_ref, bf16[128,1280]{1,0:T(8,128)(2,1)S(1)} %bitcast.19, bf16[128,1280]{1,0:T(8,128)(2,1)S(1)} %bitcast.21, bf16[128,1280]{1,0:T(8,128)(2,1)S(1)} %bitcast.22, ...), custom_call_target="tpu_custom_call" | custom-call | flops 335544320 | bytes 4390912 | tf_op jit(solution)/shard_map/window/pallas_call | solution.py:410
  56.6 4.3 %all-to-all-done.shared_ref = bf16[32,2,768]{2,1,0:T(2,128)(2,1)S(1)} async-done(((bf16[32,2,768]{2,1,0:T(2,128)(2,1)}), bf16[32,2,768]{2,1,0:T(2,128)(2,1)S(1)}, u32[]{:S(2)}, u32[]{:S(2)}) %all-to-all-start) | async-done | bytes 98336 | tf_op jit(solution)/shard_map/all_to_all | solution.py:253
  61.0 0.7 %finish.1 = (f32[1280]{0:T(1024)}, f32[8192]{0:T(1024)}) custom-call(bf16[32,2,768]{2,1,0:T(2,128)(2,1)S(1)} %all-to-all-done.shared_ref), custom_call_target="tpu_custom_call" | custom-call | tf_op jit(solution)/shard_map/finish/pallas_call | solution.py:442
  (2 shorter events, 0.0 us)
Async XLA Ops:
  1.8 10.1 %collective-permute-start.2 = (bf16[32,2048]{1,0:T(8,128)(2,1)S(1)}, bf16[32,2048]{1,0:T(8,128)(2,1)S(1)}, u32[]{:S(2)}, u32[]{:S(2)}) collective-permute-start(bf16[32,2048]{1,0:T(8,128)(2,1)S(1)} %get-tuple-element.61), channel_id=1, source_target_pairs={{0,24},{8,16},{16,8},{24,0},{1,25},{9,17},{17,9},{25,1},{2,26},{10... | collective-permute-start | bytes 393224 | tf_op jit(solution)/shard_map/ppermute | solution.py:246
  4.3 7.7 %collective-permute-start = (bf16[32,2048]{1,0:T(8,128)(2,1)S(1)}, bf16[32,2048]{1,0:T(8,128)(2,1)S(1)}, u32[]{:S(2)}, u32[]{:S(2)}) collective-permute-start(bf16[32,2048]{1,0:T(8,128)(2,1)S(1)} %get-tuple-element.62), channel_id=1, source_target_pairs={{0,16},{8,24},{16,0},{24,8},{1,17},{9,25},{17,1},{25,9},{2,18},{10... | collective-permute-start | bytes 393224 | tf_op jit(solution)/shard_map/ppermute | solution.py:246
  4.9 7.0 %collective-permute-start.1 = (bf16[32,2048]{1,0:T(8,128)(2,1)S(1)}, bf16[32,2048]{1,0:T(8,128)(2,1)S(1)}, u32[]{:S(2)}, u32[]{:S(2)}) collective-permute-start(bf16[32,2048]{1,0:T(8,128)(2,1)S(1)} %get-tuple-element.64), channel_id=1, source_target_pairs={{0,8},{8,0},{16,24},{24,16},{1,9},{9,1},{17,25},{25,17},{2,10},{10... | collective-permute-start | bytes 393224 | tf_op jit(solution)/shard_map/ppermute | solution.py:246
  5.0 7.0 %copy-start = (bf16[5120,2048]{1,0:T(8,128)(2,1)S(1)}, bf16[5120,2048]{1,0:T(8,128)(2,1)}, u32[]{:S(2)}) copy-start(bf16[5120,2048]{1,0:T(8,128)(2,1)} %refs_4_.3) | copy-start | bytes 62914564
  11.9 13.9 %copy-start.5 = (s32[1,32]{1,0:T(1,128)S(1)}, s32[1,32]{1,0:T(1,128)}, u32[]{:S(2)}) copy-start(s32[1,32]{1,0:T(1,128)} %refs_0_.3) | copy-start | bytes 388
  11.9 33.0 %copy-start.7 = (f32[1280]{0:T(1024)S(1)}, f32[1280]{0:T(1024)}, u32[]{:S(2)}) copy-start(f32[1280]{0:T(1024)} %param.12) | copy-start | bytes 15364
  12.0 36.4 %copy-start.1 = (bf16[1,128,1280]{2,1,0:T(8,128)(2,1)S(1)}, bf16[1,128,1280]{2,1,0:T(8,128)(2,1)}, u32[]{:S(2)}) copy-start(bf16[1,128,1280]{2,1,0:T(8,128)(2,1)} %param.11) | copy-start | bytes 983044
  12.0 41.2 %copy-start.2 = (bf16[1,128,1280]{2,1,0:T(8,128)(2,1)S(1)}, bf16[1,128,1280]{2,1,0:T(8,128)(2,1)}, u32[]{:S(2)}) copy-start(bf16[1,128,1280]{2,1,0:T(8,128)(2,1)} %param.14) | copy-start | bytes 983044
  12.0 41.2 %copy-start.3 = (bf16[1,128,1280]{2,1,0:T(8,128)(2,1)S(1)}, bf16[1,128,1280]{2,1,0:T(8,128)(2,1)}, u32[]{:S(2)}) copy-start(bf16[1,128,1280]{2,1,0:T(8,128)(2,1)} %param.15) | copy-start | bytes 983044
  12.0 41.2 %copy-start.6 = (s32[1,1,32]{2,1,0:T(1,128)S(1)}, s32[1,1,32]{2,1,0:T(1,128)}, u32[]{:S(2)}) copy-start(s32[1,1,32]{2,1,0:T(1,128)} %param.17) | copy-start | bytes 388
  12.0 42.2 %copy-start.4 = (bf16[1,128,1280]{2,1,0:T(8,128)(2,1)S(1)}, bf16[1,128,1280]{2,1,0:T(8,128)(2,1)}, u32[]{:S(2)}) copy-start(bf16[1,128,1280]{2,1,0:T(8,128)(2,1)} %param.16) | copy-start | bytes 983044
  15.1 3.6 %collective-permute-start.3 = (bf16[64,2560]{1,0:T(8,128)(2,1)S(1)}, bf16[64,2560]{1,0:T(8,128)(2,1)S(1)}, u32[]{:S(2)}, u32[]{:S(2)}) collective-permute-start(bf16[64,2560]{1,0:T(8,128)(2,1)S(1)} %get-tuple-element.34), channel_id=1, source_target_pairs={{0,8},{8,0},{16,24},{24,16},{1,9},{9,1},{17,25},{25,17},{2,10},{10... | collective-permute-start | bytes 983048 | tf_op jit(solution)/shard_map/ppermute | solution.py:246
  18.6 2.0 %collective-permute-start.7 = (bf16[64,2560]{1,0:T(8,128)(2,1)S(1)}, bf16[64,2560]{1,0:T(8,128)(2,1)S(1)}, u32[]{:S(2)}, u32[]{:S(2)}) collective-permute-start(bf16[64,2560]{1,0:T(8,128)(2,1)S(1)} %get-tuple-element.41), channel_id=1, source_target_pairs={{0,8},{8,0},{16,24},{24,16},{1,9},{9,1},{17,25},{25,17},{2,10},{10... | collective-permute-start | bytes 983048 | tf_op jit(solution)/shard_map/ppermute | solution.py:246
  18.8 7.1 %collective-permute-start.4 = (bf16[32,2560]{1,0:T(8,128)(2,1)S(1)}, bf16[32,2560]{1,0:T(8,128)(2,1)S(1)}, u32[]{:S(2)}, u32[]{:S(2)}) collective-permute-start(bf16[32,2560]{1,0:T(8,128)(2,1)S(1)} %get-tuple-element.36), channel_id=1, source_target_pairs={{0,16},{8,24},{16,0},{24,8},{1,17},{9,25},{17,1},{25,9},{2,18},{10... | collective-permute-start | bytes 491528 | tf_op jit(solution)/shard_map/ppermute | solution.py:246
  20.7 9.8 %collective-permute-start.8 = (bf16[32,2560]{1,0:T(8,128)(2,1)S(1)}, bf16[32,2560]{1,0:T(8,128)(2,1)S(1)}, u32[]{:S(2)}, u32[]{:S(2)}) collective-permute-start(bf16[32,2560]{1,0:T(8,128)(2,1)S(1)} %get-tuple-element.43), channel_id=1, source_target_pairs={{0,16},{8,24},{16,0},{24,8},{1,17},{9,25},{17,1},{25,9},{2,18},{10... | collective-permute-start | bytes 491528 | tf_op jit(solution)/shard_map/ppermute | solution.py:246
  26.3 15.2 %collective-permute-start.5 = (bf16[8,2688]{1,0:T(8,128)(2,1)S(1)}, bf16[8,2688]{1,0:T(8,128)(2,1)S(1)}, u32[]{:S(2)}, u32[]{:S(2)}) collective-permute-start(bf16[8,2688]{1,0:T(8,128)(2,1)S(1)} %get-tuple-element.38.refs_6_), channel_id=1, source_target_pairs={{0,4},{1,5},{2,6},{3,7},{4,0},{5,1},{6,2},{7,3},{8,12},{9,13},{10,... | collective-permute-start | bytes 129032 | tf_op jit(solution)/shard_map/ppermute | solution.py:246
  29.1 13.8 %collective-permute-start.6 = (bf16[8,2688]{1,0:T(8,128)(2,1)S(1)}, bf16[8,2688]{1,0:T(8,128)(2,1)S(1)}, u32[]{:S(2)}, u32[]{:S(2)}) collective-permute-start(bf16[8,2688]{1,0:T(8,128)(2,1)S(1)} %get-tuple-element.39.refs_7_), channel_id=1, source_target_pairs={{0,6},{1,7},{2,4},{3,5},{4,2},{5,3},{6,0},{7,1},{8,14},{9,15},{10,... | collective-permute-start | bytes 129032 | tf_op jit(solution)/shard_map/ppermute | solution.py:246
  31.1 5.6 %collective-permute-start.14 = (bf16[8,2560]{1,0:T(8,128)(2,1)S(1)}, bf16[8,2560]{1,0:T(8,128)(2,1)S(1)}, u32[]{:S(2)}, u32[]{:S(2)}) collective-permute-start(bf16[8,2560]{1,0:T(8,128)(2,1)S(1)} %get-tuple-element.50), channel_id=1, source_target_pairs={{0,4},{1,5},{2,6},{3,7},{4,0},{5,1},{6,2},{7,3},{8,12},{9,13},{10,... | collective-permute-start | bytes 122888 | tf_op jit(solution)/shard_map/ppermute | solution.py:246
  32.9 6.6 %collective-permute-start.15 = (bf16[8,2560]{1,0:T(8,128)(2,1)S(1)}, bf16[8,2560]{1,0:T(8,128)(2,1)S(1)}, u32[]{:S(2)}, u32[]{:S(2)}) collective-permute-start(bf16[8,2560]{1,0:T(8,128)(2,1)S(1)} %get-tuple-element.51), channel_id=1, source_target_pairs={{0,6},{1,7},{2,4},{3,5},{4,2},{5,3},{6,0},{7,1},{8,14},{9,15},{10,... | collective-permute-start | bytes 122888 | tf_op jit(solution)/shard_map/ppermute | solution.py:246
  33.8 11.2 %collective-permute-start.9 = (bf16[8,5248]{1,0:T(8,128)(2,1)S(1)}, bf16[8,5248]{1,0:T(8,128)(2,1)S(1)}, u32[]{:S(2)}, u32[]{:S(2)}) collective-permute-start(bf16[8,5248]{1,0:T(8,128)(2,1)S(1)} %get-tuple-element.45), channel_id=1, source_target_pairs={{0,5},{1,4},{2,7},{3,6},{4,1},{5,0},{6,3},{7,2},{8,13},{9,12},{10,... | collective-permute-start | bytes 251912 | tf_op jit(solution)/shard_map/ppermute | solution.py:246
  36.7 8.3 %collective-permute-start.10 = (bf16[8,5248]{1,0:T(8,128)(2,1)S(1)}, bf16[8,5248]{1,0:T(8,128)(2,1)S(1)}, u32[]{:S(2)}, u32[]{:S(2)}) collective-permute-start(bf16[8,5248]{1,0:T(8,128)(2,1)S(1)} %get-tuple-element.46), channel_id=1, source_target_pairs={{0,1},{1,0},{2,3},{3,2},{4,5},{5,4},{6,7},{7,6},{8,9},{9,8},{10,11... | collective-permute-start | bytes 251912 | tf_op jit(solution)/shard_map/ppermute | solution.py:246
  39.4 7.2 %collective-permute-start.11 = (bf16[8,5248]{1,0:T(8,128)(2,1)S(1)}, bf16[8,5248]{1,0:T(8,128)(2,1)S(1)}, u32[]{:S(2)}, u32[]{:S(2)}) collective-permute-start(bf16[8,5248]{1,0:T(8,128)(2,1)S(1)} %get-tuple-element.47), channel_id=1, source_target_pairs={{0,7},{1,6},{2,5},{3,4},{4,3},{5,2},{6,1},{7,0},{8,15},{9,14},{10,... | collective-permute-start | bytes 251912 | tf_op jit(solution)/shard_map/ppermute | solution.py:246
  41.5 5.4 %collective-permute-start.12 = (bf16[8,5248]{1,0:T(8,128)(2,1)S(1)}, bf16[8,5248]{1,0:T(8,128)(2,1)S(1)}, u32[]{:S(2)}, u32[]{:S(2)}) collective-permute-start(bf16[8,5248]{1,0:T(8,128)(2,1)S(1)} %get-tuple-element.48), channel_id=1, source_target_pairs={{0,2},{1,3},{2,0},{3,1},{4,6},{5,7},{6,4},{7,5},{8,10},{9,11},{10,... | collective-permute-start | bytes 251912 | tf_op jit(solution)/shard_map/ppermute | solution.py:246
  42.9 5.5 %collective-permute-start.13 = (bf16[8,5248]{1,0:T(8,128)(2,1)S(1)}, bf16[8,5248]{1,0:T(8,128)(2,1)S(1)}, u32[]{:S(2)}, u32[]{:S(2)}) collective-permute-start(bf16[8,5248]{1,0:T(8,128)(2,1)S(1)} %get-tuple-element.49), channel_id=1, source_target_pairs={{0,3},{1,2},{2,1},{3,0},{4,7},{5,6},{6,5},{7,4},{8,11},{9,10},{10,... | collective-permute-start | bytes 251912 | tf_op jit(solution)/shard_map/ppermute | solution.py:246
  49.5 11.4 %all-to-all-start = ((bf16[32,2,768]{2,1,0:T(2,128)(2,1)}), bf16[32,2,768]{2,1,0:T(2,128)(2,1)S(1)}, u32[]{:S(2)}, u32[]{:S(2)}) async-start(bf16[32,2,768]{2,1,0:T(2,128)(2,1)} %get-tuple-element.58), calls=%async_computation | async-start | bytes 196608 | tf_op jit(solution)/shard_map/all_to_all | solution.py:253

commit v17 on v16

--- a/solution.py
+++ b/solution.py
@@ -129,11 +129,7 @@
 
 
 def peer_masks(peers):
-    return (0, 5, 1, 7, 2, 3, 4, 6) if peers == 8 else tuple(range(peers))
-
-
-def early_masks(peers):
-    return (4, 6) if peers == 8 else ()
+    return (0, 4, 6, 1, 5, 2, 7, 3) if peers == 8 else tuple(range(peers))
 
 
 def block_peer(block, masks, me):
@@ -143,11 +139,9 @@
     return peer
 
 
-def pack_kernel(
-    peers, capacity, chunks, masks, starts, direct, carries, after, me_ref, *refs
-):
-    targets_ref, terms, refs = refs[0], refs[1 : 2 * chunks + 1], refs[2 * chunks + 1 :]
-    outs = refs[after + carries :]
+def pack_kernel(peers, capacity, masks, direct, labelled, carries, me_ref, *refs):
+    targets_ref, kept_ref, got_ref, refs = refs[0], refs[1], refs[2], refs[3:]
+    outs = refs[carries:]
     targets = targets_ref[...]
     rows = targets.shape[1]
     dest = targets // rows
@@ -165,7 +159,7 @@
     chosen = jnp.logical_and(dest == holder, rank == slot % capacity)
     selector = chosen.astype(F32).astype(BF16)
     parts = []
-    if carries:
+    if labelled and carries:
         local = jnp.broadcast_to((local + 1).astype(F32), (16, rows)).astype(BF16)
         labels = dot(local, selector, (1, 1))[:1] - 1.0
         square = (slots, slots)
@@ -190,51 +184,42 @@
                     here = jnp.logical_and(peer == p, row == level * pieces + piece)
                     extra = jnp.where(here, line, extra)
         parts.append(extra)
-    else:
+    elif labelled:
         label = jnp.sum(jnp.where(chosen, local + 1, 0), axis=1, keepdims=True) - 1
         parts.append(jnp.broadcast_to(label.astype(F32), (slots, LANES)))
-    for chunk in range(chunks):
-        kept, got = terms[2 * chunk : 2 * chunk + 2]
-        total = (kept[...].astype(F32) + got[...].astype(F32)).astype(BF16)
-        parts.append(dot(selector, total, (1, 0)))
+    total = (kept_ref[...].astype(F32) + got_ref[...].astype(F32)).astype(BF16)
+    parts.append(dot(selector, total, (1, 0)))
     if not direct:
-        masks, starts, capacity = masks[:1], starts[:1], slots
-    for block, start in enumerate(starts):
-        at = 0
-        for part in parts[start:]:
-            end = at + part.shape[1]
+        capacity = slots
+    at = 0
+    for part in parts:
+        end = at + part.shape[1]
+        for block, out_ref in enumerate(outs):
             rows_of_block = part[block * capacity : (block + 1) * capacity]
-            outs[block][:, at:end] = rows_of_block.astype(BF16)
-            at = end
-
-
-def pack(terms, targets, me, sums, after, peers, capacity, masks, starts, direct):
-    rows = targets.shape[1]
+            out_ref[:, at:end] = rows_of_block.astype(BF16)
+        at = end
+
+
+def pack(kept, got, targets, me, sums, peers, capacity, direct, labelled):
+    rows, width = kept.shape
     carries = sums is not None
-    widths = [LANES] + [kept.shape[1] for kept, _ in terms]
-    operands = [me, targets] + [x for pair in terms for x in pair] + ([sums] if carries else [])
-    blocks = len(operands) - 1
-    operands += after
+    width = width + (LANES if labelled else 0)
+    operands = [me, targets, kept, got] + ([sums] if carries else [])
     if direct:
-        out_shape = [
-            jax.ShapeDtypeStruct((capacity, sum(widths[start:])), BF16) for start in starts
-        ]
+        out_shape = [jax.ShapeDtypeStruct((capacity, width), BF16)] * peers
     else:
-        out_shape = [jax.ShapeDtypeStruct((peers * capacity, sum(widths)), BF16)]
+        out_shape = [jax.ShapeDtypeStruct((peers * capacity, width), BF16)]
     return pl.pallas_call(
         functools.partial(
-            pack_kernel, peers, capacity, len(terms), masks, starts, direct, carries,
-            len(after),
+            pack_kernel, peers, capacity, peer_masks(peers), direct, labelled, carries
         ),
         out_shape=out_shape,
-        in_specs=[pl.BlockSpec(memory_space=pltpu.SMEM)]
-        + vmem(blocks)
-        + [pl.BlockSpec(memory_space=pl.ANY)] * len(after),
+        in_specs=[pl.BlockSpec(memory_space=pltpu.SMEM)] + vmem(len(operands) - 1),
         out_specs=vmem(len(out_shape)),
         compiler_params=pltpu.CompilerParams(vmem_limit_bytes=VMEM_BYTES),
         cost_estimate=pl.CostEstimate(
-            flops=2 * rows * len(masks) * capacity * sum(widths),
-            bytes_accessed=(6 * rows + 2 * len(masks) * capacity) * sum(widths),
+            flops=2 * rows * peers * capacity * width,
+            bytes_accessed=(6 * rows + 2 * peers * capacity) * width,
             transcendentals=0,
         ),
         name="pack",
@@ -297,21 +282,24 @@
     )(queries, keys, ids)
 
 
-def norm_kernel(peers, early, carries, patches_ref, gain_ref, *refs):
-    pieces, (out_ref, share_ref) = refs[:-2], refs[-2:]
+def norm_kernel(peers, carries, me_ref, patches_ref, gain_ref, *refs):
+    pieces, (out_ref, share_ref, blocks_ref) = refs[:-3], refs[-3:]
     patches, width = patches_ref.shape
-    pieces = [ref[...].astype(F32) for ref in pieces]
-    pieces, begun = pieces[len(early) :], pieces[: len(early)]
-    for place, begin in zip(early, begun):
-        pieces[place] = jnp.concatenate([begin, pieces[place]], axis=1)
-    routed = jnp.concatenate(pieces, axis=0) if len(pieces) > 1 else pieces[0]
+    blocks, rest = pieces[:-1], pieces[-1]
+    capacity = rest.shape[0] // peers
+    if len(blocks) > 1:
+        for mask, ref in zip(peer_masks(peers), blocks):
+            start = pl.multiple_of((me_ref[0] ^ mask) * capacity, capacity)
+            blocks_ref[pl.ds(start, capacity), :] = ref[...].astype(F32)
+    else:
+        blocks_ref[...] = blocks[0][...].astype(F32)
+    routed = jnp.concatenate([blocks_ref[...], rest[...].astype(F32)], axis=1)
     slots = routed.shape[0]
     per_token = routed.shape[1] // width
     columns = [routed[:, LANES + c * width : LANES + (c + 1) * width] for c in range(per_token)]
     held = jnp.concatenate(columns, axis=0).astype(BF16)
     lanes = per_token * slots
     extra = routed[:, :LANES]
-    capacity = slots // peers
     if carries:
         place = iota((slots, LANES), 0) % capacity
         labels = jnp.where(place == capacity - 1, extra, 0.0).astype(BF16)
@@ -348,14 +336,15 @@
     ).astype(BF16)
 
 
-def norm_backward(received, peers, early, patches, gain, share):
+def norm_backward(received, me, peers, patches, gain, share):
     count, width = patches.shape
     routed = sum(x.size for x in received)
     return pl.pallas_call(
-        functools.partial(norm_kernel, peers, early, len(share.shape) == 3),
+        functools.partial(norm_kernel, peers, len(share.shape) == 3),
         out_shape=[jax.ShapeDtypeStruct((count, width), BF16), share],
-        in_specs=vmem(2 + len(received)),
+        in_specs=[pl.BlockSpec(memory_space=pltpu.SMEM)] + vmem(2 + len(received)),
         out_specs=vmem(2),
+        scratch_shapes=[pltpu.VMEM((received[-1].shape[0], received[0].shape[1]), F32)],
         compiler_params=pltpu.CompilerParams(vmem_limit_bytes=VMEM_BYTES),
         cost_estimate=pl.CostEstimate(
             flops=2 * count * routed,
@@ -363,7 +352,7 @@
             transcendentals=0,
         ),
         name="norm",
-    )(patches, gain, *received)
+    )(me, patches, gain, *received)
 
 
 def window_kernel(g_ref, q_ref, k_ref, v_ref, probs_ref, probs_t_ref, dq_ref, dk_ref, dv_ref):
@@ -488,34 +477,23 @@
             kept, sent = halve(kept, swap(sent, "img", mask))
             mask *= 2
         terms.append((kept, swap(sent, "img", mask)))
-    masks = peer_masks(peers)
-    early = early_masks(peers) if direct else ()
-    places = tuple(masks.index(mask) for mask in early)
     place = me.reshape(1)
+    (kept, got), (last_kept, last_got) = terms
     sums = bias_part if carries else None
-    begun = []
-    if early:
-        begun = list(
-            pack(
-                terms[:1], token_target, place, sums, [], peers, capacity, early,
-                (0,) * len(early), direct,
-            )
-        )
-    starts = tuple(2 if mask in early else 0 for mask in masks)
-    packed = pack(
-        terms, token_target, place, sums, begun, peers, capacity, masks, starts, direct
-    )
+    blocks = pack(kept, got, token_target, place, sums, peers, capacity, direct, True)
+    rest = pack(last_kept, last_got, token_target, place, None, peers, capacity, False, False)[0]
     if direct:
-        routed = [swap(x, "seq", mask) if mask else x for x, mask in zip(packed, masks)]
+        masks = peer_masks(peers)
+        routed = [swap(x, "seq", mask) if mask else x for x, mask in zip(blocks, masks)]
     else:
-        routed = [exchange(packed[0], "seq", peers)]
-    routed = [swap(block, "seq", mask) for block, mask in zip(begun, early)] + routed
+        routed = [exchange(blocks[0], "seq", peers)]
+    routed = routed + [exchange(rest, "seq", peers)]
 
     if carries:
         share = jax.ShapeDtypeStruct((devices, 2, (width + pieces * LANES) // 2), BF16)
     else:
         share = jax.ShapeDtypeStruct((1, width), F32)
-    out_grads, shared = norm_backward(routed, peers, places, patches[0], gain[None], share)
+    out_grads, shared = norm_backward(routed, place, peers, patches[0], gain[None], share)
     gain_scale = 1.0 / math.sqrt(devices * patches.shape[1])
     bias_scale = 1.0 / math.sqrt(devices * rows)
     if carries:

time: 61.9 us -> 66.1 us (1.068)
  waiting for transfers between devices: 11.9 us -> 15.3 us
    ppermute x16 -> x14, starting transfers between devices: 24.8 us -> 18.8 us  [swap(): return lax.ppermute(x, axis, [(i, i ^ mask) for i in range(n)])]
    all_to_all x1 -> x2, starting transfers between devices: 3.62 us -> 9.24 us  [exchange(): lax.all_to_all(x, axis, split_axis=0, concat_axis=0, tiled=True)]
    ppermute x16 -> x14, waiting for transfers between devices: 7.53 us -> 11 us  [swap(): return lax.ppermute(x, axis, [(i, i ^ mask) for i in range(n)])]
    unnamed x16 -> x26, local copies, waits for them, and re-layouts: 7.01 us -> 7.37 us
    all_to_all x1 -> x2, waiting for transfers between devices: 4.32 us -> 4.33 us  [exchange(): lax.all_to_all(x, axis, split_axis=0, concat_axis=0, tiled=True)]
  transfers between devices with their start and end apart: 17 -> 16, of which waited for: 6 -> 7; matrix products, arithmetic and copies ran while one was open for 0% -> 0% of each run, Pallas kernels for 12% -> 12%
where the time goes in v17:
time: 66.1 us; the launch traced here: 65.8 us
  starting transfers between devices  28 us (42%)
  waiting for transfers between devices  15.3 us (23%)
  Pallas kernels  13 us (20%)
  local copies, waits for them, and re-layouts  8.51 us (13%)
  between operations  0.88 us (1%)
    ppermute x14, starting transfers between devices, swap(): return lax.ppermute(x, axis, [(i, i ^ mask) for i in range(n)])  18.8 us
    ppermute x14, waiting for transfers between devices, swap(): return lax.ppermute(x, axis, [(i, i ^ mask) for i in range(n)])  11 us
    all_to_all x2, starting transfers between devices, exchange(): lax.all_to_all(x, axis, split_axis=0, concat_axis=0, tiled=True)  9.24 us
    unnamed x26, local copies, waits for them, and re-layouts  7.37 us
    pallas_call x2, Pallas kernels, project(): pl.pallas_call(functools.partial(project_kernel, blocks, first, tile, wit...  6.02 us
    all_to_all x2, waiting for transfers between devices, exchange(): lax.all_to_all(x, axis, split_axis=0, concat_axis=0, tiled=True)  4.33 us
    pallas_call x1, Pallas kernels, window_backward(): pl.pallas_call(window_kernel, out_shape=[shape] * 3, in_specs=vmem(6), ou...  2.38 us
    pallas_call x2, Pallas kernels, pack(): pl.pallas_call(functools.partial(pack_kernel, peers, capacity, peer_masks...  1.56 us
  transfers between devices with their start and end apart: 16, of which 7 were waited for; matrix products, arithmetic and copies ran while one was open for 0% of the time, Pallas kernels for 12%

profile of v17, /device:TPU:0, one launch (start us, length us, event | category | flops | bytes accessed | tf_op | source)
XLA Modules:
  0.0 65.8 jit_solution(13655178063942327153)
XLA Ops:
  0.7 1.1 %dynamic-slice_bitcast_fusion = (bf16[32,2048]{1,0:T(8,128)(2,1)S(1)}, bf16[32,2048]{1,0:T(8,128)(2,1)S(1)}, bf16[32,2048]{1,0:T(8,128)(2,1)S(1)}, bf16[32,2048]{1,0:T(8,128)(2,1)S(1)}) fusion(bf16[1,32,8192]{2,1,0:T(8,128)(2,1)} %param.9, s32[]{:T(128)S(6)} %select_n.15, s32[]{:T(128)S(6)} %select_n.13, s32[]{:T(128)S(6)} %select_n.12, s32[]{:T(128)S(6)} %select_n.14), kind=kLoop, calls=%fused_computation | loop fusion | bytes 1048592 | tf_op jit(solution)/shard_map/dynamic_slice | solution.py:462
  1.8 2.5 %collective-permute-start.2 = (bf16[32,2048]{1,0:T(8,128)(2,1)S(1)}, bf16[32,2048]{1,0:T(8,128)(2,1)S(1)}, u32[]{:S(2)}, u32[]{:S(2)}) collective-permute-start(bf16[32,2048]{1,0:T(8,128)(2,1)S(1)} %get-tuple-element.57), channel_id=1, source_target_pairs={{0,24},{8,16},{16,8},{24,0},{1,25},{9,17},{17,9},{25,1},{2,26},{10... | collective-permute-start | bytes 393224 | tf_op jit(solution)/shard_map/ppermute | solution.py:231
  4.3 0.6 collective-permute-start
  4.9 0.0 collective-permute-start.1
  5.0 7.0 %copy-done = bf16[5120,2048]{1,0:T(8,128)(2,1)S(1)} copy-done((bf16[5120,2048]{1,0:T(8,128)(2,1)S(1)}, bf16[5120,2048]{1,0:T(8,128)(2,1)}, u32[]{:S(2)}) %copy-start) | copy-done | bytes 20971544
  11.9 0.0 collective-permute-done.2.refs_3_
  11.9 0.0 collective-permute-done.refs_1_
  11.9 0.0 collective-permute-done.1.refs_2_
  12.0 0.0 slice-start.3
  12.0 0.0 slice-start.4
  12.0 0.0 copy-start.5
  12.0 0.0 copy-start.7
  12.0 0.0 copy-start.1
  12.0 0.0 copy-start.2
  12.0 0.0 copy-start.3
  12.0 0.0 copy-start.6
  12.1 0.0 copy-start.4
  12.1 3.0 %project.3 = (bf16[64,2560]{1,0:T(8,128)(2,1)S(1)}, bf16[64,2560]{1,0:T(8,128)(2,1)S(1)}) custom-call(bf16[32,2048]{1,0:T(8,128)(2,1)S(1)} %get-tuple-element.59.refs_0_, bf16[32,2048]{1,0:T(8,128)(2,1)S(1)} %collective-permute-done.refs_1_, bf16[32,2048]{1,0:T(8,128)(2,1)S(1)} %collective-permute-done.1.refs_2_, ...), custom_call_target="tpu_custom_call" | custom-call | flops 1342177280 | bytes 10485760 | tf_op jit(solution)/shard_map/project/pallas_call | solution.py:74
  15.0 0.5 collective-permute-start.12
  15.6 1.3 %collective-permute-done.12.got_ref = bf16[64,2560]{1,0:T(8,128)(2,1)S(1)} collective-permute-done((bf16[64,2560]{1,0:T(8,128)(2,1)S(1)}, bf16[64,2560]{1,0:T(8,128)(2,1)S(1)}, u32[]{:S(2)}, u32[]{:S(2)}) %collective-permute-start.12) | collective-permute-done | bytes 327712 | tf_op jit(solution)/shard_map/ppermute | solution.py:231
  16.8 0.1 halve.3
  16.9 1.7 %collective-permute-start.13 = (bf16[32,2560]{1,0:T(8,128)(2,1)S(1)}, bf16[32,2560]{1,0:T(8,128)(2,1)S(1)}, u32[]{:S(2)}, u32[]{:S(2)}) collective-permute-start(bf16[32,2560]{1,0:T(8,128)(2,1)S(1)} %get-tuple-element.47), channel_id=1, source_target_pairs={{0,16},{8,24},{16,0},{24,8},{1,17},{9,25},{17,1},{25,9},{2,18},{10... | collective-permute-start | bytes 491528 | tf_op jit(solution)/shard_map/ppermute | solution.py:231
  18.6 0.0 slice-done
  18.6 0.0 slice-done.1
  18.6 0.0 slice-done.2
  18.6 0.0 slice-done.3
  18.6 0.3 slice-done.4
  19.0 3.0 %project.2 = (bf16[64,2560]{1,0:T(8,128)(2,1)S(1)}, bf16[64,2560]{1,0:T(8,128)(2,1)S(1)}, f32[1,2048]{1,0:T(1,128)S(1)}) custom-call(bf16[32,2048]{1,0:T(8,128)(2,1)S(1)} %get-tuple-element.59.refs_0_, bf16[32,2048]{1,0:T(8,128)(2,1)S(1)} %collective-permute-done.refs_1_, bf16[32,2048]{1,0:T(8,128)(2,1)S(1)} %collective-permute-done.1.refs_2_, ...), custom_call_target="tpu_custom_call" | custom-call | flops 1342177280 | bytes 10485760 | tf_op jit(solution)/shard_map/project/pallas_call | solution.py:74
  22.0 0.5 collective-permute-start.3
  22.6 0.9 %collective-permute-done.13.refs_2_ = bf16[32,2560]{1,0:T(8,128)(2,1)S(1)} collective-permute-done((bf16[32,2560]{1,0:T(8,128)(2,1)S(1)}, bf16[32,2560]{1,0:T(8,128)(2,1)S(1)}, u32[]{:S(2)}, u32[]{:S(2)}) %collective-permute-start.13) | collective-permute-done | bytes 163872 | tf_op jit(solution)/shard_map/ppermute | solution.py:231
  23.5 0.0 copy-done.5
  23.5 1.0 %pack.3 = bf16[64,2560]{1,0:T(8,128)(2,1)} custom-call(s32[1]{0:T(128)} %bitcast.me_ref, s32[1,32]{1,0:T(1,128)S(1)} %copy-done.5, f32[32,2560]{1,0:T(8,128)S(1)} %get-tuple-element.46.refs_1_, bf16[32,2560]{1,0:T(8,128)(2,1)S(1)} %collective-permute-done.13.refs_2_), custom_call_target="tpu_custom_call" | custom-call | flops 10485760 | bytes 819200 | tf_op jit(solution)/shard_map/pack/pallas_call | solution.py:212
  24.5 5.8 %all-to-all-start = ((bf16[8,8,2560]{2,1,0:T(8,128)(2,1)}), bf16[8,8,2560]{2,1,0:T(8,128)(2,1)S(1)}, u32[]{:S(2)}, u32[]{:S(2)}) async-start(bf16[8,8,2560]{2,1,0:T(8,128)(2,1)} %bitcast.6), calls=%async_computation | async-start | bytes 655360 | tf_op jit(solution)/shard_map/all_to_all | solution.py:238
  30.3 0.0 collective-permute-done.3.got_ref
  30.3 0.1 halve.2
  30.4 1.5 %collective-permute-start.4 = (bf16[32,2560]{1,0:T(8,128)(2,1)S(1)}, bf16[32,2560]{1,0:T(8,128)(2,1)S(1)}, u32[]{:S(2)}, u32[]{:S(2)}) collective-permute-start(bf16[32,2560]{1,0:T(8,128)(2,1)S(1)} %get-tuple-element.34), channel_id=1, source_target_pairs={{0,16},{8,24},{16,0},{24,8},{1,17},{9,25},{17,1},{25,9},{2,18},{10... | collective-permute-start | bytes 491528 | tf_op jit(solution)/shard_map/ppermute | solution.py:231
  31.9 3.9 %collective-permute-done.4.refs_2_ = bf16[32,2560]{1,0:T(8,128)(2,1)S(1)} collective-permute-done((bf16[32,2560]{1,0:T(8,128)(2,1)S(1)}, bf16[32,2560]{1,0:T(8,128)(2,1)S(1)}, u32[]{:S(2)}, u32[]{:S(2)}) %collective-permute-start.4) | collective-permute-done | bytes 163872 | tf_op jit(solution)/shard_map/ppermute | solution.py:231
  35.8 0.5 pack.2
  36.3 3.0 %collective-permute-start.5 = (bf16[8,2688]{1,0:T(8,128)(2,1)S(1)}, bf16[8,2688]{1,0:T(8,128)(2,1)S(1)}, u32[]{:S(2)}, u32[]{:S(2)}) collective-permute-start(bf16[8,2688]{1,0:T(8,128)(2,1)S(1)} %get-tuple-element.37), channel_id=1, source_target_pairs={{0,4},{1,5},{2,6},{3,7},{4,0},{5,1},{6,2},{7,3},{8,12},{9,13},{10,... | collective-permute-start | bytes 129032 | tf_op jit(solution)/shard_map/ppermute | solution.py:231
  39.3 1.5 %collective-permute-start.6 = (bf16[8,2688]{1,0:T(8,128)(2,1)S(1)}, bf16[8,2688]{1,0:T(8,128)(2,1)S(1)}, u32[]{:S(2)}, u32[]{:S(2)}) collective-permute-start(bf16[8,2688]{1,0:T(8,128)(2,1)S(1)} %get-tuple-element.38), channel_id=1, source_target_pairs={{0,6},{1,7},{2,4},{3,5},{4,2},{5,3},{6,0},{7,1},{8,14},{9,15},{10,... | collective-permute-start | bytes 129032 | tf_op jit(solution)/shard_map/ppermute | solution.py:231
  40.8 1.5 %collective-permute-start.7 = (bf16[8,2688]{1,0:T(8,128)(2,1)S(1)}, bf16[8,2688]{1,0:T(8,128)(2,1)S(1)}, u32[]{:S(2)}, u32[]{:S(2)}) collective-permute-start(bf16[8,2688]{1,0:T(8,128)(2,1)S(1)} %get-tuple-element.39), channel_id=1, source_target_pairs={{0,1},{1,0},{2,3},{3,2},{4,5},{5,4},{6,7},{7,6},{8,9},{9,8},{10,11... | collective-permute-start | bytes 129032 | tf_op jit(solution)/shard_map/ppermute | solution.py:231
  42.2 1.5 %collective-permute-start.8 = (bf16[8,2688]{1,0:T(8,128)(2,1)S(1)}, bf16[8,2688]{1,0:T(8,128)(2,1)S(1)}, u32[]{:S(2)}, u32[]{:S(2)}) collective-permute-start(bf16[8,2688]{1,0:T(8,128)(2,1)S(1)} %get-tuple-element.40), channel_id=1, source_target_pairs={{0,5},{1,4},{2,7},{3,6},{4,1},{5,0},{6,3},{7,2},{8,13},{9,12},{10,... | collective-permute-start | bytes 129032 | tf_op jit(solution)/shard_map/ppermute | solution.py:231
  43.7 1.5 %collective-permute-start.9 = (bf16[8,2688]{1,0:T(8,128)(2,1)S(1)}, bf16[8,2688]{1,0:T(8,128)(2,1)S(1)}, u32[]{:S(2)}, u32[]{:S(2)}) collective-permute-start(bf16[8,2688]{1,0:T(8,128)(2,1)S(1)} %get-tuple-element.41), channel_id=1, source_target_pairs={{0,2},{1,3},{2,0},{3,1},{4,6},{5,7},{6,4},{7,5},{8,10},{9,11},{10,... | collective-permute-start | bytes 129032 | tf_op jit(solution)/shard_map/ppermute | solution.py:231
  45.1 0.0 collective-permute-done.5.refs_1_
  45.1 2.6 %collective-permute-start.10 = (bf16[8,2688]{1,0:T(8,128)(2,1)S(1)}, bf16[8,2688]{1,0:T(8,128)(2,1)S(1)}, u32[]{:S(2)}, u32[]{:S(2)}) collective-permute-start(bf16[8,2688]{1,0:T(8,128)(2,1)S(1)} %get-tuple-element.42), channel_id=1, source_target_pairs={{0,7},{1,6},{2,5},{3,4},{4,3},{5,2},{6,1},{7,0},{8,15},{9,14},{10,... | collective-permute-start | bytes 129032 | tf_op jit(solution)/shard_map/ppermute | solution.py:231
  47.7 0.0 collective-permute-done.6.refs_2_
  47.7 0.0 collective-permute-start.11
  47.7 0.0 copy-done.7
  47.7 0.0 collective-permute-done.7.refs_3_
  47.7 0.7 %collective-permute-done.8.refs_4_ = bf16[8,2688]{1,0:T(8,128)(2,1)S(1)} collective-permute-done((bf16[8,2688]{1,0:T(8,128)(2,1)S(1)}, bf16[8,2688]{1,0:T(8,128)(2,1)S(1)}, u32[]{:S(2)}, u32[]{:S(2)}) %collective-permute-start.8) | collective-permute-done | bytes 43040 | tf_op jit(solution)/shard_map/ppermute | solution.py:231
  48.4 0.0 collective-permute-done.9.refs_5_
  48.4 3.5 %collective-permute-done.10.refs_6_ = bf16[8,2688]{1,0:T(8,128)(2,1)S(1)} collective-permute-done((bf16[8,2688]{1,0:T(8,128)(2,1)S(1)}, bf16[8,2688]{1,0:T(8,128)(2,1)S(1)}, u32[]{:S(2)}, u32[]{:S(2)}) %collective-permute-start.10) | collective-permute-done | bytes 43040 | tf_op jit(solution)/shard_map/ppermute | solution.py:231
  51.9 0.8 %collective-permute-done.11.refs_7_ = bf16[8,2688]{1,0:T(8,128)(2,1)S(1)} collective-permute-done((bf16[8,2688]{1,0:T(8,128)(2,1)S(1)}, bf16[8,2688]{1,0:T(8,128)(2,1)S(1)}, u32[]{:S(2)}, u32[]{:S(2)}) %collective-permute-start.11) | collective-permute-done | bytes 43040 | tf_op jit(solution)/shard_map/ppermute | solution.py:231
  52.6 0.0 all-to-all-done
  52.6 0.0 copy-done.1
  52.6 1.1 %norm.1 = (bf16[128,1280]{1,0:T(8,128)(2,1)S(1)}, bf16[32,2,768]{2,1,0:T(2,128)(2,1)}) custom-call(s32[1]{0:T(128)} %bitcast.me_ref, bf16[128,1280]{1,0:T(8,128)(2,1)S(1)} %bitcast.22, f32[1,1280]{1,0:T(1,128)S(1)} %broadcast_in_dim.12.gain_ref, bf16[8,2688]{1,0:T(8,128)(2,1)S(1)} %get-tuple-element.36.refs_0_, ...), custom_call_target="tpu_custom_call" | custom-call | flops 85983232 | bytes 1327104 | tf_op jit(solution)/shard_map/norm/pallas_call | solution.py:342
  53.8 3.4 %all-to-all-start.1 = ((bf16[32,2,768]{2,1,0:T(2,128)(2,1)}), bf16[32,2,768]{2,1,0:T(2,128)(2,1)S(1)}, u32[]{:S(2)}, u32[]{:S(2)}) async-start(bf16[32,2,768]{2,1,0:T(2,128)(2,1)} %get-tuple-element.54), calls=%async_computation.1 | async-start | bytes 196608 | tf_op jit(solution)/shard_map/all_to_all | solution.py:238
  57.2 0.0 copy-done.2
  57.2 0.0 copy-done.3
  57.2 0.0 copy-done.6
  57.2 1.1 %probs.1 = (f32[16,128,128]{2,1,0:T(8,128)S(1)}, f32[16,128,128]{2,1,0:T(8,128)S(1)}) custom-call(bf16[128,1280]{1,0:T(8,128)(2,1)S(1)} %bitcast.23, bf16[128,1280]{1,0:T(8,128)(2,1)S(1)} %bitcast.25, s32[1,32]{1,0:T(1,128)S(1)} %bitcast.28), custom_call_target="tpu_custom_call" | custom-call | flops 268435456 | bytes 2097152 | tf_op jit(solution)/shard_map/probs/pallas_call | solution.py:270
  58.3 2.4 %window.1 = (bf16[128,1280]{1,0:T(8,128)(2,1)}, bf16[128,1280]{1,0:T(8,128)(2,1)}, bf16[128,1280]{1,0:T(8,128)(2,1)}) custom-call(bf16[128,1280]{1,0:T(8,128)(2,1)S(1)} %get-tuple-element.48.g_ref, bf16[128,1280]{1,0:T(8,128)(2,1)S(1)} %bitcast.24, bf16[128,1280]{1,0:T(8,128)(2,1)S(1)} %bitcast.26, bf16[128,1280]{1,0:T(8,128)(2,1)S(1)} %bitcast.27, ...), custom_call_target="tpu_custom_call" | custom-call | flops 335544320 | bytes 4390912 | tf_op jit(solution)/shard_map/window/pallas_call | solution.py:399
  60.7 4.3 %all-to-all-done.1.shared_ref = bf16[32,2,768]{2,1,0:T(2,128)(2,1)S(1)} async-done(((bf16[32,2,768]{2,1,0:T(2,128)(2,1)}), bf16[32,2,768]{2,1,0:T(2,128)(2,1)S(1)}, u32[]{:S(2)}, u32[]{:S(2)}) %all-to-all-start.1) | async-done | bytes 98336 | tf_op jit(solution)/shard_map/all_to_all | solution.py:238
  65.0 0.7 %finish.1 = (f32[1280]{0:T(1024)}, f32[8192]{0:T(1024)}) custom-call(bf16[32,2,768]{2,1,0:T(2,128)(2,1)S(1)} %all-to-all-done.1.shared_ref), custom_call_target="tpu_custom_call" | custom-call | tf_op jit(solution)/shard_map/finish/pallas_call | solution.py:431
  (8 shorter events, 0.0 us)
Async XLA Ops:
  1.8 10.1 %collective-permute-start.2 = (bf16[32,2048]{1,0:T(8,128)(2,1)S(1)}, bf16[32,2048]{1,0:T(8,128)(2,1)S(1)}, u32[]{:S(2)}, u32[]{:S(2)}) collective-permute-start(bf16[32,2048]{1,0:T(8,128)(2,1)S(1)} %get-tuple-element.57), channel_id=1, source_target_pairs={{0,24},{8,16},{16,8},{24,0},{1,25},{9,17},{17,9},{25,1},{2,26},{10... | collective-permute-start | bytes 393224 | tf_op jit(solution)/shard_map/ppermute | solution.py:231
  4.3 7.7 %collective-permute-start = (bf16[32,2048]{1,0:T(8,128)(2,1)S(1)}, bf16[32,2048]{1,0:T(8,128)(2,1)S(1)}, u32[]{:S(2)}, u32[]{:S(2)}) collective-permute-start(bf16[32,2048]{1,0:T(8,128)(2,1)S(1)} %get-tuple-element.58), channel_id=1, source_target_pairs={{0,16},{8,24},{16,0},{24,8},{1,17},{9,25},{17,1},{25,9},{2,18},{10... | collective-permute-start | bytes 393224 | tf_op jit(solution)/shard_map/ppermute | solution.py:231
  4.9 7.0 %collective-permute-start.1 = (bf16[32,2048]{1,0:T(8,128)(2,1)S(1)}, bf16[32,2048]{1,0:T(8,128)(2,1)S(1)}, u32[]{:S(2)}, u32[]{:S(2)}) collective-permute-start(bf16[32,2048]{1,0:T(8,128)(2,1)S(1)} %get-tuple-element.60), channel_id=1, source_target_pairs={{0,8},{8,0},{16,24},{24,16},{1,9},{9,1},{17,25},{25,17},{2,10},{10... | collective-permute-start | bytes 393224 | tf_op jit(solution)/shard_map/ppermute | solution.py:231
  5.0 7.0 %copy-start = (bf16[5120,2048]{1,0:T(8,128)(2,1)S(1)}, bf16[5120,2048]{1,0:T(8,128)(2,1)}, u32[]{:S(2)}) copy-start(bf16[5120,2048]{1,0:T(8,128)(2,1)} %refs_4_.3) | copy-start | bytes 62914564
  11.9 6.7 %slice-start = ((s8[20971520]{0:T(1024)(128)(4,1)}), s8[4194304]{0:T(1024)(128)(4,1)S(1)}, s32[]{:S(2)}) async-start(s8[20971520]{0:T(1024)(128)(4,1)} %bitcast.19), calls=%async_computation.2 | async-start | bytes 8388608
  11.9 6.7 %slice-start.1 = ((s8[20971520]{0:T(1024)(128)(4,1)}), s8[4194304]{0:T(1024)(128)(4,1)S(1)}, s32[]{:S(2)}) async-start(s8[20971520]{0:T(1024)(128)(4,1)} %bitcast.19), calls=%async_computation.3 | async-start | bytes 8388608
  11.9 6.7 %slice-start.2 = ((s8[20971520]{0:T(1024)(128)(4,1)}), s8[4194304]{0:T(1024)(128)(4,1)S(1)}, s32[]{:S(2)}) async-start(s8[20971520]{0:T(1024)(128)(4,1)} %bitcast.19), calls=%async_computation.4 | async-start | bytes 8388608
  12.0 6.7 %slice-start.3 = ((s8[20971520]{0:T(1024)(128)(4,1)}), s8[4194304]{0:T(1024)(128)(4,1)S(1)}, s32[]{:S(2)}) async-start(s8[20971520]{0:T(1024)(128)(4,1)} %bitcast.19), calls=%async_computation.5 | async-start | bytes 8388608
  12.0 7.0 %slice-start.4 = ((s8[20971520]{0:T(1024)(128)(4,1)}), s8[4194304]{0:T(1024)(128)(4,1)S(1)}, s32[]{:S(2)}) async-start(s8[20971520]{0:T(1024)(128)(4,1)} %bitcast.19), calls=%async_computation.6 | async-start | bytes 8388608
  12.0 11.5 %copy-start.5 = (s32[1,32]{1,0:T(1,128)S(1)}, s32[1,32]{1,0:T(1,128)}, u32[]{:S(2)}) copy-start(s32[1,32]{1,0:T(1,128)} %refs_0_.3) | copy-start | bytes 388
  12.0 35.7 %copy-start.7 = (f32[1280]{0:T(1024)S(1)}, f32[1280]{0:T(1024)}, u32[]{:S(2)}) copy-start(f32[1280]{0:T(1024)} %param.12) | copy-start | bytes 15364
  12.0 40.6 %copy-start.1 = (bf16[1,128,1280]{2,1,0:T(8,128)(2,1)S(1)}, bf16[1,128,1280]{2,1,0:T(8,128)(2,1)}, u32[]{:S(2)}) copy-start(bf16[1,128,1280]{2,1,0:T(8,128)(2,1)} %param.11) | copy-start | bytes 983044
  12.0 45.2 %copy-start.2 = (bf16[1,128,1280]{2,1,0:T(8,128)(2,1)S(1)}, bf16[1,128,1280]{2,1,0:T(8,128)(2,1)}, u32[]{:S(2)}) copy-start(bf16[1,128,1280]{2,1,0:T(8,128)(2,1)} %param.14) | copy-start | bytes 983044
  12.0 45.2 %copy-start.3 = (bf16[1,128,1280]{2,1,0:T(8,128)(2,1)S(1)}, bf16[1,128,1280]{2,1,0:T(8,128)(2,1)}, u32[]{:S(2)}) copy-start(bf16[1,128,1280]{2,1,0:T(8,128)(2,1)} %param.15) | copy-start | bytes 983044
  12.0 45.2 %copy-start.6 = (s32[1,1,32]{2,1,0:T(1,128)S(1)}, s32[1,1,32]{2,1,0:T(1,128)}, u32[]{:S(2)}) copy-start(s32[1,1,32]{2,1,0:T(1,128)} %param.17) | copy-start | bytes 388
  12.1 46.3 %copy-start.4 = (bf16[1,128,1280]{2,1,0:T(8,128)(2,1)S(1)}, bf16[1,128,1280]{2,1,0:T(8,128)(2,1)}, u32[]{:S(2)}) copy-start(bf16[1,128,1280]{2,1,0:T(8,128)(2,1)} %param.16) | copy-start | bytes 983044
  15.0 1.8 %collective-permute-start.12 = (bf16[64,2560]{1,0:T(8,128)(2,1)S(1)}, bf16[64,2560]{1,0:T(8,128)(2,1)S(1)}, u32[]{:S(2)}, u32[]{:S(2)}) collective-permute-start(bf16[64,2560]{1,0:T(8,128)(2,1)S(1)} %get-tuple-element.45), channel_id=1, source_target_pairs={{0,8},{8,0},{16,24},{24,16},{1,9},{9,1},{17,25},{25,17},{2,10},{10... | collective-permute-start | bytes 983048 | tf_op jit(solution)/shard_map/ppermute | solution.py:231
  16.9 6.5 %collective-permute-start.13 = (bf16[32,2560]{1,0:T(8,128)(2,1)S(1)}, bf16[32,2560]{1,0:T(8,128)(2,1)S(1)}, u32[]{:S(2)}, u32[]{:S(2)}) collective-permute-start(bf16[32,2560]{1,0:T(8,128)(2,1)S(1)} %get-tuple-element.47), channel_id=1, source_target_pairs={{0,16},{8,24},{16,0},{24,8},{1,17},{9,25},{17,1},{25,9},{2,18},{10... | collective-permute-start | bytes 491528 | tf_op jit(solution)/shard_map/ppermute | solution.py:231
  22.0 8.3 %collective-permute-start.3 = (bf16[64,2560]{1,0:T(8,128)(2,1)S(1)}, bf16[64,2560]{1,0:T(8,128)(2,1)S(1)}, u32[]{:S(2)}, u32[]{:S(2)}) collective-permute-start(bf16[64,2560]{1,0:T(8,128)(2,1)S(1)} %get-tuple-element.32), channel_id=1, source_target_pairs={{0,8},{8,0},{16,24},{24,16},{1,9},{9,1},{17,25},{25,17},{2,10},{10... | collective-permute-start | bytes 983048 | tf_op jit(solution)/shard_map/ppermute | solution.py:231
  24.5 28.1 %all-to-all-start = ((bf16[8,8,2560]{2,1,0:T(8,128)(2,1)}), bf16[8,8,2560]{2,1,0:T(8,128)(2,1)S(1)}, u32[]{:S(2)}, u32[]{:S(2)}) async-start(bf16[8,8,2560]{2,1,0:T(8,128)(2,1)} %bitcast.6), calls=%async_computation | async-start | bytes 655360 | tf_op jit(solution)/shard_map/all_to_all | solution.py:238
  30.4 5.4 %collective-permute-start.4 = (bf16[32,2560]{1,0:T(8,128)(2,1)S(1)}, bf16[32,2560]{1,0:T(8,128)(2,1)S(1)}, u32[]{:S(2)}, u32[]{:S(2)}) collective-permute-start(bf16[32,2560]{1,0:T(8,128)(2,1)S(1)} %get-tuple-element.34), channel_id=1, source_target_pairs={{0,16},{8,24},{16,0},{24,8},{1,17},{9,25},{17,1},{25,9},{2,18},{10... | collective-permute-start | bytes 491528 | tf_op jit(solution)/shard_map/ppermute | solution.py:231
  36.3 8.8 %collective-permute-start.5 = (bf16[8,2688]{1,0:T(8,128)(2,1)S(1)}, bf16[8,2688]{1,0:T(8,128)(2,1)S(1)}, u32[]{:S(2)}, u32[]{:S(2)}) collective-permute-start(bf16[8,2688]{1,0:T(8,128)(2,1)S(1)} %get-tuple-element.37), channel_id=1, source_target_pairs={{0,4},{1,5},{2,6},{3,7},{4,0},{5,1},{6,2},{7,3},{8,12},{9,13},{10,... | collective-permute-start | bytes 129032 | tf_op jit(solution)/shard_map/ppermute | solution.py:231
  39.3 8.4 %collective-permute-start.6 = (bf16[8,2688]{1,0:T(8,128)(2,1)S(1)}, bf16[8,2688]{1,0:T(8,128)(2,1)S(1)}, u32[]{:S(2)}, u32[]{:S(2)}) collective-permute-start(bf16[8,2688]{1,0:T(8,128)(2,1)S(1)} %get-tuple-element.38), channel_id=1, source_target_pairs={{0,6},{1,7},{2,4},{3,5},{4,2},{5,3},{6,0},{7,1},{8,14},{9,15},{10,... | collective-permute-start | bytes 129032 | tf_op jit(solution)/shard_map/ppermute | solution.py:231
  40.8 7.0 %collective-permute-start.7 = (bf16[8,2688]{1,0:T(8,128)(2,1)S(1)}, bf16[8,2688]{1,0:T(8,128)(2,1)S(1)}, u32[]{:S(2)}, u32[]{:S(2)}) collective-permute-start(bf16[8,2688]{1,0:T(8,128)(2,1)S(1)} %get-tuple-element.39), channel_id=1, source_target_pairs={{0,1},{1,0},{2,3},{3,2},{4,5},{5,4},{6,7},{7,6},{8,9},{9,8},{10,11... | collective-permute-start | bytes 129032 | tf_op jit(solution)/shard_map/ppermute | solution.py:231
  42.2 6.2 %collective-permute-start.8 = (bf16[8,2688]{1,0:T(8,128)(2,1)S(1)}, bf16[8,2688]{1,0:T(8,128)(2,1)S(1)}, u32[]{:S(2)}, u32[]{:S(2)}) collective-permute-start(bf16[8,2688]{1,0:T(8,128)(2,1)S(1)} %get-tuple-element.40), channel_id=1, source_target_pairs={{0,5},{1,4},{2,7},{3,6},{4,1},{5,0},{6,3},{7,2},{8,13},{9,12},{10,... | collective-permute-start | bytes 129032 | tf_op jit(solution)/shard_map/ppermute | solution.py:231
  43.7 4.7 %collective-permute-start.9 = (bf16[8,2688]{1,0:T(8,128)(2,1)S(1)}, bf16[8,2688]{1,0:T(8,128)(2,1)S(1)}, u32[]{:S(2)}, u32[]{:S(2)}) collective-permute-start(bf16[8,2688]{1,0:T(8,128)(2,1)S(1)} %get-tuple-element.41), channel_id=1, source_target_pairs={{0,2},{1,3},{2,0},{3,1},{4,6},{5,7},{6,4},{7,5},{8,10},{9,11},{10,... | collective-permute-start | bytes 129032 | tf_op jit(solution)/shard_map/ppermute | solution.py:231
  45.1 6.7 %collective-permute-start.10 = (bf16[8,2688]{1,0:T(8,128)(2,1)S(1)}, bf16[8,2688]{1,0:T(8,128)(2,1)S(1)}, u32[]{:S(2)}, u32[]{:S(2)}) collective-permute-start(bf16[8,2688]{1,0:T(8,128)(2,1)S(1)} %get-tuple-element.42), channel_id=1, source_target_pairs={{0,7},{1,6},{2,5},{3,4},{4,3},{5,2},{6,1},{7,0},{8,15},{9,14},{10,... | collective-permute-start | bytes 129032 | tf_op jit(solution)/shard_map/ppermute | solution.py:231
  47.7 4.9 %collective-permute-start.11 = (bf16[8,2688]{1,0:T(8,128)(2,1)S(1)}, bf16[8,2688]{1,0:T(8,128)(2,1)S(1)}, u32[]{:S(2)}, u32[]{:S(2)}) collective-permute-start(bf16[8,2688]{1,0:T(8,128)(2,1)S(1)} %get-tuple-element.43), channel_id=1, source_target_pairs={{0,3},{1,2},{2,1},{3,0},{4,7},{5,6},{6,5},{7,4},{8,11},{9,10},{10,... | collective-permute-start | bytes 129032 | tf_op jit(solution)/shard_map/ppermute | solution.py:231
  53.8 11.2 %all-to-all-start.1 = ((bf16[32,2,768]{2,1,0:T(2,128)(2,1)}), bf16[32,2,768]{2,1,0:T(2,128)(2,1)S(1)}, u32[]{:S(2)}, u32[]{:S(2)}) async-start(bf16[32,2,768]{2,1,0:T(2,128)(2,1)} %get-tuple-element.54), calls=%async_computation.1 | async-start | bytes 196608 | tf_op jit(solution)/shard_map/all_to_all | solution.py:238

commit v18 on v16

--- a/solution.py
+++ b/solution.py
@@ -129,11 +129,11 @@
 
 
 def peer_masks(peers):
-    return (0, 5, 1, 7, 2, 3, 4, 6) if peers == 8 else tuple(range(peers))
+    return (0, 4, 1, 6, 2, 5, 3, 7) if peers == 8 else tuple(range(peers))
 
 
 def early_masks(peers):
-    return (4, 6) if peers == 8 else ()
+    return ()
 
 
 def block_peer(block, masks, me):

time: 61.9 us -> 62 us (level)
  waiting for transfers between devices: 11.9 us -> 15.6 us
  starting transfers between devices: 28.4 us -> 25.1 us
    ppermute x16 -> x14, waiting for transfers between devices: 7.53 us -> 11.2 us  [swap(): return lax.ppermute(x, axis, [(i, i ^ mask) for i in range(n)])]
    ppermute x16 -> x14, starting transfers between devices: 24.8 us -> 21.1 us  [swap(): return lax.ppermute(x, axis, [(i, i ^ mask) for i in range(n)])]
  transfers between devices with their start and end apart: 17 -> 15, of which waited for: 6 -> 6; matrix products, arithmetic and copies ran while one was open for 0% -> 0% of each run, Pallas kernels for 12% -> 11%
where the time goes in v18:
time: 62 us; the launch traced here: 61.8 us
  starting transfers between devices  25.1 us (40%)
  waiting for transfers between devices  15.6 us (25%)
  Pallas kernels  12.1 us (20%)
  local copies, waits for them, and re-layouts  8.15 us (13%)
  between operations  0.82 us (1%)
    ppermute x14, starting transfers between devices, swap(): return lax.ppermute(x, axis, [(i, i ^ mask) for i in range(n)])  21.1 us
    ppermute x14, waiting for transfers between devices, swap(): return lax.ppermute(x, axis, [(i, i ^ mask) for i in range(n)])  11.2 us
    unnamed x16, local copies, waits for them, and re-layouts  7.01 us
    pallas_call x2, Pallas kernels, project(): pl.pallas_call(functools.partial(project_kernel, blocks, first, tile, wit...  6.03 us
    all_to_all x1, waiting for transfers between devices, exchange(): lax.all_to_all(x, axis, split_axis=0, concat_axis=0, tiled=True)  4.32 us
    all_to_all x1, starting transfers between devices, exchange(): lax.all_to_all(x, axis, split_axis=0, concat_axis=0, tiled=True)  4.02 us
    pallas_call x1, Pallas kernels, window_backward(): pl.pallas_call(window_kernel, out_shape=[shape] * 3, in_specs=vmem(6), ou...  2.38 us
  transfers between devices with their start and end apart: 15, of which 6 were waited for; matrix products, arithmetic and copies ran while one was open for 0% of the time, Pallas kernels for 11%

profile of v18, /device:TPU:0, one launch (start us, length us, event | category | flops | bytes accessed | tf_op | source)
XLA Modules:
  0.0 61.8 jit_solution(2140463540353601167)
XLA Ops:
  0.7 1.1 %dynamic-slice_bitcast_fusion = (bf16[32,2048]{1,0:T(8,128)(2,1)S(1)}, bf16[32,2048]{1,0:T(8,128)(2,1)S(1)}, bf16[32,2048]{1,0:T(8,128)(2,1)S(1)}, bf16[32,2048]{1,0:T(8,128)(2,1)S(1)}) fusion(bf16[1,32,8192]{2,1,0:T(8,128)(2,1)} %param.9, s32[]{:T(128)S(6)} %select_n.15, s32[]{:T(128)S(6)} %select_n.13, s32[]{:T(128)S(6)} %select_n.12, s32[]{:T(128)S(6)} %select_n.14), kind=kLoop, calls=%fused_computation | loop fusion | bytes 1048592 | tf_op jit(solution)/shard_map/dynamic_slice | solution.py:473
  1.8 2.5 %collective-permute-start.2 = (bf16[32,2048]{1,0:T(8,128)(2,1)S(1)}, bf16[32,2048]{1,0:T(8,128)(2,1)S(1)}, u32[]{:S(2)}, u32[]{:S(2)}) collective-permute-start(bf16[32,2048]{1,0:T(8,128)(2,1)S(1)} %get-tuple-element.57), channel_id=1, source_target_pairs={{0,24},{8,16},{16,8},{24,0},{1,25},{9,17},{17,9},{25,1},{2,26},{10... | collective-permute-start | bytes 393224 | tf_op jit(solution)/shard_map/ppermute | solution.py:246
  4.3 0.6 %collective-permute-start = (bf16[32,2048]{1,0:T(8,128)(2,1)S(1)}, bf16[32,2048]{1,0:T(8,128)(2,1)S(1)}, u32[]{:S(2)}, u32[]{:S(2)}) collective-permute-start(bf16[32,2048]{1,0:T(8,128)(2,1)S(1)} %get-tuple-element.58), channel_id=1, source_target_pairs={{0,16},{8,24},{16,0},{24,8},{1,17},{9,25},{17,1},{25,9},{2,18},{10... | collective-permute-start | bytes 393224 | tf_op jit(solution)/shard_map/ppermute | solution.py:246
  4.9 0.0 collective-permute-start.1
  5.0 0.0 copy-start
  5.0 7.0 %copy-done = bf16[5120,2048]{1,0:T(8,128)(2,1)S(1)} copy-done((bf16[5120,2048]{1,0:T(8,128)(2,1)S(1)}, bf16[5120,2048]{1,0:T(8,128)(2,1)}, u32[]{:S(2)}) %copy-start) | copy-done | bytes 20971544
  11.9 0.0 collective-permute-done.2.refs_3_
  11.9 0.0 collective-permute-done.refs_1_
  11.9 0.0 collective-permute-done.1.refs_2_
  11.9 0.0 copy-start.5
  11.9 0.0 copy-start.7
  12.0 0.0 copy-start.1
  12.0 0.0 copy-start.2
  12.0 0.0 copy-start.3
  12.0 0.0 copy-start.6
  12.0 0.0 copy-start.4
  12.0 3.1 %project.2 = (bf16[64,2560]{1,0:T(8,128)(2,1)S(1)}, bf16[64,2560]{1,0:T(8,128)(2,1)S(1)}, f32[1,2048]{1,0:T(1,128)S(1)}) custom-call(bf16[32,2048]{1,0:T(8,128)(2,1)S(1)} %get-tuple-element.59.refs_0_, bf16[32,2048]{1,0:T(8,128)(2,1)S(1)} %collective-permute-done.refs_1_, bf16[32,2048]{1,0:T(8,128)(2,1)S(1)} %collective-permute-done.1.refs_2_, ...), custom_call_target="tpu_custom_call" | custom-call | flops 1342177280 | bytes 10485760 | tf_op jit(solution)/shard_map/project/pallas_call | solution.py:74
  15.1 0.5 collective-permute-start.3
  15.6 3.0 %project.3 = (bf16[64,2560]{1,0:T(8,128)(2,1)S(1)}, bf16[64,2560]{1,0:T(8,128)(2,1)S(1)}) custom-call(bf16[32,2048]{1,0:T(8,128)(2,1)S(1)} %get-tuple-element.59.refs_0_, bf16[32,2048]{1,0:T(8,128)(2,1)S(1)} %collective-permute-done.refs_1_, bf16[32,2048]{1,0:T(8,128)(2,1)S(1)} %collective-permute-done.1.refs_2_, ...), custom_call_target="tpu_custom_call" | custom-call | flops 1342177280 | bytes 10485760 | tf_op jit(solution)/shard_map/project/pallas_call | solution.py:74
  18.6 0.1 collective-permute-start.5
  18.7 0.0 collective-permute-done.3.got_ref
  18.7 0.1 halve.2
  18.8 1.8 %collective-permute-start.4 = (bf16[32,2560]{1,0:T(8,128)(2,1)S(1)}, bf16[32,2560]{1,0:T(8,128)(2,1)S(1)}, u32[]{:S(2)}, u32[]{:S(2)}) collective-permute-start(bf16[32,2560]{1,0:T(8,128)(2,1)S(1)} %get-tuple-element.34), channel_id=1, source_target_pairs={{0,16},{8,24},{16,0},{24,8},{1,17},{9,25},{17,1},{25,9},{2,18},{10... | collective-permute-start | bytes 491528 | tf_op jit(solution)/shard_map/ppermute | solution.py:246
  20.6 0.0 collective-permute-done.5.got_ref
  20.6 0.1 halve.3
  20.7 1.2 %collective-permute-start.6 = (bf16[32,2560]{1,0:T(8,128)(2,1)S(1)}, bf16[32,2560]{1,0:T(8,128)(2,1)S(1)}, u32[]{:S(2)}, u32[]{:S(2)}) collective-permute-start(bf16[32,2560]{1,0:T(8,128)(2,1)S(1)} %get-tuple-element.38), channel_id=1, source_target_pairs={{0,16},{8,24},{16,0},{24,8},{1,17},{9,25},{17,1},{25,9},{2,18},{10... | collective-permute-start | bytes 491528 | tf_op jit(solution)/shard_map/ppermute | solution.py:246
  21.9 4.0 %collective-permute-done.4.refs_2_ = bf16[32,2560]{1,0:T(8,128)(2,1)S(1)} collective-permute-done((bf16[32,2560]{1,0:T(8,128)(2,1)S(1)}, bf16[32,2560]{1,0:T(8,128)(2,1)S(1)}, u32[]{:S(2)}, u32[]{:S(2)}) %collective-permute-start.4) | collective-permute-done | bytes 163872 | tf_op jit(solution)/shard_map/ppermute | solution.py:246
  25.9 3.1 %collective-permute-done.6.refs_4_ = bf16[32,2560]{1,0:T(8,128)(2,1)S(1)} collective-permute-done((bf16[32,2560]{1,0:T(8,128)(2,1)S(1)}, bf16[32,2560]{1,0:T(8,128)(2,1)S(1)}, u32[]{:S(2)}, u32[]{:S(2)}) %collective-permute-start.6) | collective-permute-done | bytes 163872 | tf_op jit(solution)/shard_map/ppermute | solution.py:246
  28.9 0.0 copy-done.5
  28.9 0.7 %pack.1 = (bf16[8,5248]{1,0:T(8,128)(2,1)S(1)}, bf16[8,5248]{1,0:T(8,128)(2,1)S(1)}, bf16[8,5248]{1,0:T(8,128)(2,1)S(1)}, bf16[8,5248]{1,0:T(8,128)(2,1)S(1)}, b...) custom-call(s32[1]{0:T(128)} %bitcast.1.me_ref, ...), custom_call_target="tpu_custom_call" | custom-call | flops 21495808 | bytes 1679360 | tf_op jit(solution)/shard_map/pack/pallas_call | solution.py:224
  29.6 2.7 %collective-permute-start.7 = (bf16[8,5248]{1,0:T(8,128)(2,1)S(1)}, bf16[8,5248]{1,0:T(8,128)(2,1)S(1)}, u32[]{:S(2)}, u32[]{:S(2)}) collective-permute-start(bf16[8,5248]{1,0:T(8,128)(2,1)S(1)} %get-tuple-element.41), channel_id=1, source_target_pairs={{0,4},{1,5},{2,6},{3,7},{4,0},{5,1},{6,2},{7,3},{8,12},{9,13},{10,... | collective-permute-start | bytes 251912 | tf_op jit(solution)/shard_map/ppermute | solution.py:246
  32.3 1.5 %collective-permute-start.8 = (bf16[8,5248]{1,0:T(8,128)(2,1)S(1)}, bf16[8,5248]{1,0:T(8,128)(2,1)S(1)}, u32[]{:S(2)}, u32[]{:S(2)}) collective-permute-start(bf16[8,5248]{1,0:T(8,128)(2,1)S(1)} %get-tuple-element.42), channel_id=1, source_target_pairs={{0,1},{1,0},{2,3},{3,2},{4,5},{5,4},{6,7},{7,6},{8,9},{9,8},{10,11... | collective-permute-start | bytes 251912 | tf_op jit(solution)/shard_map/ppermute | solution.py:246
  33.8 1.4 %collective-permute-start.9 = (bf16[8,5248]{1,0:T(8,128)(2,1)S(1)}, bf16[8,5248]{1,0:T(8,128)(2,1)S(1)}, u32[]{:S(2)}, u32[]{:S(2)}) collective-permute-start(bf16[8,5248]{1,0:T(8,128)(2,1)S(1)} %get-tuple-element.43), channel_id=1, source_target_pairs={{0,6},{1,7},{2,4},{3,5},{4,2},{5,3},{6,0},{7,1},{8,14},{9,15},{10,... | collective-permute-start | bytes 251912 | tf_op jit(solution)/shard_map/ppermute | solution.py:246
  35.1 0.2 collective-permute-start.10
  35.3 2.8 %collective-permute-start.11 = (bf16[8,5248]{1,0:T(8,128)(2,1)S(1)}, bf16[8,5248]{1,0:T(8,128)(2,1)S(1)}, u32[]{:S(2)}, u32[]{:S(2)}) collective-permute-start(bf16[8,5248]{1,0:T(8,128)(2,1)S(1)} %get-tuple-element.45), channel_id=1, source_target_pairs={{0,5},{1,4},{2,7},{3,6},{4,1},{5,0},{6,3},{7,2},{8,13},{9,12},{10,... | collective-permute-start | bytes 251912 | tf_op jit(solution)/shard_map/ppermute | solution.py:246
  38.1 0.0 collective-permute-done.7.refs_1_
  38.1 2.8 %collective-permute-start.12 = (bf16[8,5248]{1,0:T(8,128)(2,1)S(1)}, bf16[8,5248]{1,0:T(8,128)(2,1)S(1)}, u32[]{:S(2)}, u32[]{:S(2)}) collective-permute-start(bf16[8,5248]{1,0:T(8,128)(2,1)S(1)} %get-tuple-element.46), channel_id=1, source_target_pairs={{0,3},{1,2},{2,1},{3,0},{4,7},{5,6},{6,5},{7,4},{8,11},{9,10},{10,... | collective-permute-start | bytes 251912 | tf_op jit(solution)/shard_map/ppermute | solution.py:246
  40.9 0.0 collective-permute-done.8.refs_2_
  40.9 3.0 %collective-permute-start.13 = (bf16[8,5248]{1,0:T(8,128)(2,1)S(1)}, bf16[8,5248]{1,0:T(8,128)(2,1)S(1)}, u32[]{:S(2)}, u32[]{:S(2)}) collective-permute-start(bf16[8,5248]{1,0:T(8,128)(2,1)S(1)} %get-tuple-element.47), channel_id=1, source_target_pairs={{0,7},{1,6},{2,5},{3,4},{4,3},{5,2},{6,1},{7,0},{8,15},{9,14},{10,... | collective-permute-start | bytes 251912 | tf_op jit(solution)/shard_map/ppermute | solution.py:246
  43.9 0.0 copy-done.7
  43.9 0.0 collective-permute-done.9.refs_3_
  43.9 0.0 collective-permute-done.10.refs_4_
  43.9 1.6 %collective-permute-done.11.refs_5_ = bf16[8,5248]{1,0:T(8,128)(2,1)S(1)} collective-permute-done((bf16[8,5248]{1,0:T(8,128)(2,1)S(1)}, bf16[8,5248]{1,0:T(8,128)(2,1)S(1)}, u32[]{:S(2)}, u32[]{:S(2)}) %collective-permute-start.11) | collective-permute-done | bytes 84000 | tf_op jit(solution)/shard_map/ppermute | solution.py:246
  45.6 0.3 collective-permute-done.12.refs_6_
  45.9 2.2 %collective-permute-done.13.refs_7_ = bf16[8,5248]{1,0:T(8,128)(2,1)S(1)} collective-permute-done((bf16[8,5248]{1,0:T(8,128)(2,1)S(1)}, bf16[8,5248]{1,0:T(8,128)(2,1)S(1)}, u32[]{:S(2)}, u32[]{:S(2)}) %collective-permute-start.13) | collective-permute-done | bytes 84000 | tf_op jit(solution)/shard_map/ppermute | solution.py:246
  48.1 0.0 copy-done.1
  48.1 1.1 %norm.1 = (bf16[128,1280]{1,0:T(8,128)(2,1)S(1)}, bf16[32,2,768]{2,1,0:T(2,128)(2,1)}) custom-call(bf16[128,1280]{1,0:T(8,128)(2,1)S(1)} %bitcast.17, f32[1,1280]{1,0:T(1,128)S(1)} %broadcast_in_dim.12.gain_ref, bf16[8,5248]{1,0:T(8,128)(2,1)S(1)} %get-tuple-element.40.refs_0_, bf16[8,5248]{1,0:T(8,128)(2,1)S(1)} %collective-permute-done.7.refs_1_, ...), custom_call_target="tpu_custom_call" | custom-call | flops 85983232 | bytes 1327104 | tf_op jit(solution)/shard_map/norm/pallas_call | solution.py:354
  49.2 4.0 %all-to-all-start = ((bf16[32,2,768]{2,1,0:T(2,128)(2,1)}), bf16[32,2,768]{2,1,0:T(2,128)(2,1)S(1)}, u32[]{:S(2)}, u32[]{:S(2)}) async-start(bf16[32,2,768]{2,1,0:T(2,128)(2,1)} %get-tuple-element.54), calls=%async_computation | async-start | bytes 196608 | tf_op jit(solution)/shard_map/all_to_all | solution.py:253
  53.2 0.0 copy-done.2
  53.2 0.0 copy-done.3
  53.2 0.0 copy-done.6
  53.2 1.1 %probs.1 = (f32[16,128,128]{2,1,0:T(8,128)S(1)}, f32[16,128,128]{2,1,0:T(8,128)S(1)}) custom-call(bf16[128,1280]{1,0:T(8,128)(2,1)S(1)} %bitcast.18, bf16[128,1280]{1,0:T(8,128)(2,1)S(1)} %bitcast.20, s32[1,32]{1,0:T(1,128)S(1)} %bitcast.23), custom_call_target="tpu_custom_call" | custom-call | flops 268435456 | bytes 2097152 | tf_op jit(solution)/shard_map/probs/pallas_call | solution.py:285
  54.3 0.0 copy-done.4
  54.3 2.4 %window.1 = (bf16[128,1280]{1,0:T(8,128)(2,1)}, bf16[128,1280]{1,0:T(8,128)(2,1)}, bf16[128,1280]{1,0:T(8,128)(2,1)}) custom-call(bf16[128,1280]{1,0:T(8,128)(2,1)S(1)} %get-tuple-element.48.g_ref, bf16[128,1280]{1,0:T(8,128)(2,1)S(1)} %bitcast.19, bf16[128,1280]{1,0:T(8,128)(2,1)S(1)} %bitcast.21, bf16[128,1280]{1,0:T(8,128)(2,1)S(1)} %bitcast.22, ...), custom_call_target="tpu_custom_call" | custom-call | flops 335544320 | bytes 4390912 | tf_op jit(solution)/shard_map/window/pallas_call | solution.py:410
  56.7 4.3 %all-to-all-done.shared_ref = bf16[32,2,768]{2,1,0:T(2,128)(2,1)S(1)} async-done(((bf16[32,2,768]{2,1,0:T(2,128)(2,1)}), bf16[32,2,768]{2,1,0:T(2,128)(2,1)S(1)}, u32[]{:S(2)}, u32[]{:S(2)}) %all-to-all-start) | async-done | bytes 98336 | tf_op jit(solution)/shard_map/all_to_all | solution.py:253
  61.0 0.7 %finish.1 = (f32[1280]{0:T(1024)}, f32[8192]{0:T(1024)}) custom-call(bf16[32,2,768]{2,1,0:T(2,128)(2,1)S(1)} %all-to-all-done.shared_ref), custom_call_target="tpu_custom_call" | custom-call | tf_op jit(solution)/shard_map/finish/pallas_call | solution.py:442
  (2 shorter events, 0.0 us)
Async XLA Ops:
  1.8 10.1 %collective-permute-start.2 = (bf16[32,2048]{1,0:T(8,128)(2,1)S(1)}, bf16[32,2048]{1,0:T(8,128)(2,1)S(1)}, u32[]{:S(2)}, u32[]{:S(2)}) collective-permute-start(bf16[32,2048]{1,0:T(8,128)(2,1)S(1)} %get-tuple-element.57), channel_id=1, source_target_pairs={{0,24},{8,16},{16,8},{24,0},{1,25},{9,17},{17,9},{25,1},{2,26},{10... | collective-permute-start | bytes 393224 | tf_op jit(solution)/shard_map/ppermute | solution.py:246
  4.3 7.7 %collective-permute-start = (bf16[32,2048]{1,0:T(8,128)(2,1)S(1)}, bf16[32,2048]{1,0:T(8,128)(2,1)S(1)}, u32[]{:S(2)}, u32[]{:S(2)}) collective-permute-start(bf16[32,2048]{1,0:T(8,128)(2,1)S(1)} %get-tuple-element.58), channel_id=1, source_target_pairs={{0,16},{8,24},{16,0},{24,8},{1,17},{9,25},{17,1},{25,9},{2,18},{10... | collective-permute-start | bytes 393224 | tf_op jit(solution)/shard_map/ppermute | solution.py:246
  4.9 7.0 %collective-permute-start.1 = (bf16[32,2048]{1,0:T(8,128)(2,1)S(1)}, bf16[32,2048]{1,0:T(8,128)(2,1)S(1)}, u32[]{:S(2)}, u32[]{:S(2)}) collective-permute-start(bf16[32,2048]{1,0:T(8,128)(2,1)S(1)} %get-tuple-element.60), channel_id=1, source_target_pairs={{0,8},{8,0},{16,24},{24,16},{1,9},{9,1},{17,25},{25,17},{2,10},{10... | collective-permute-start | bytes 393224 | tf_op jit(solution)/shard_map/ppermute | solution.py:246
  5.0 7.0 %copy-start = (bf16[5120,2048]{1,0:T(8,128)(2,1)S(1)}, bf16[5120,2048]{1,0:T(8,128)(2,1)}, u32[]{:S(2)}) copy-start(bf16[5120,2048]{1,0:T(8,128)(2,1)} %refs_4_.3) | copy-start | bytes 62914564
  11.9 17.0 %copy-start.5 = (s32[1,32]{1,0:T(1,128)S(1)}, s32[1,32]{1,0:T(1,128)}, u32[]{:S(2)}) copy-start(s32[1,32]{1,0:T(1,128)} %refs_0_.1) | copy-start | bytes 388
  11.9 32.0 %copy-start.7 = (f32[1280]{0:T(1024)S(1)}, f32[1280]{0:T(1024)}, u32[]{:S(2)}) copy-start(f32[1280]{0:T(1024)} %param.12) | copy-start | bytes 15364
  12.0 36.1 %copy-start.1 = (bf16[1,128,1280]{2,1,0:T(8,128)(2,1)S(1)}, bf16[1,128,1280]{2,1,0:T(8,128)(2,1)}, u32[]{:S(2)}) copy-start(bf16[1,128,1280]{2,1,0:T(8,128)(2,1)} %param.11) | copy-start | bytes 983044
  12.0 41.2 %copy-start.2 = (bf16[1,128,1280]{2,1,0:T(8,128)(2,1)S(1)}, bf16[1,128,1280]{2,1,0:T(8,128)(2,1)}, u32[]{:S(2)}) copy-start(bf16[1,128,1280]{2,1,0:T(8,128)(2,1)} %param.14) | copy-start | bytes 983044
  12.0 41.2 %copy-start.3 = (bf16[1,128,1280]{2,1,0:T(8,128)(2,1)S(1)}, bf16[1,128,1280]{2,1,0:T(8,128)(2,1)}, u32[]{:S(2)}) copy-start(bf16[1,128,1280]{2,1,0:T(8,128)(2,1)} %param.15) | copy-start | bytes 983044
  12.0 41.2 %copy-start.6 = (s32[1,1,32]{2,1,0:T(1,128)S(1)}, s32[1,1,32]{2,1,0:T(1,128)}, u32[]{:S(2)}) copy-start(s32[1,1,32]{2,1,0:T(1,128)} %param.17) | copy-start | bytes 388
  12.0 42.3 %copy-start.4 = (bf16[1,128,1280]{2,1,0:T(8,128)(2,1)S(1)}, bf16[1,128,1280]{2,1,0:T(8,128)(2,1)}, u32[]{:S(2)}) copy-start(bf16[1,128,1280]{2,1,0:T(8,128)(2,1)} %param.16) | copy-start | bytes 983044
  15.1 3.6 %collective-permute-start.3 = (bf16[64,2560]{1,0:T(8,128)(2,1)S(1)}, bf16[64,2560]{1,0:T(8,128)(2,1)S(1)}, u32[]{:S(2)}, u32[]{:S(2)}) collective-permute-start(bf16[64,2560]{1,0:T(8,128)(2,1)S(1)} %get-tuple-element.32), channel_id=1, source_target_pairs={{0,8},{8,0},{16,24},{24,16},{1,9},{9,1},{17,25},{25,17},{2,10},{10... | collective-permute-start | bytes 983048 | tf_op jit(solution)/shard_map/ppermute | solution.py:246
  18.6 2.0 %collective-permute-start.5 = (bf16[64,2560]{1,0:T(8,128)(2,1)S(1)}, bf16[64,2560]{1,0:T(8,128)(2,1)S(1)}, u32[]{:S(2)}, u32[]{:S(2)}) collective-permute-start(bf16[64,2560]{1,0:T(8,128)(2,1)S(1)} %get-tuple-element.36), channel_id=1, source_target_pairs={{0,8},{8,0},{16,24},{24,16},{1,9},{9,1},{17,25},{25,17},{2,10},{10... | collective-permute-start | bytes 983048 | tf_op jit(solution)/shard_map/ppermute | solution.py:246
  18.8 7.1 %collective-permute-start.4 = (bf16[32,2560]{1,0:T(8,128)(2,1)S(1)}, bf16[32,2560]{1,0:T(8,128)(2,1)S(1)}, u32[]{:S(2)}, u32[]{:S(2)}) collective-permute-start(bf16[32,2560]{1,0:T(8,128)(2,1)S(1)} %get-tuple-element.34), channel_id=1, source_target_pairs={{0,16},{8,24},{16,0},{24,8},{1,17},{9,25},{17,1},{25,9},{2,18},{10... | collective-permute-start | bytes 491528 | tf_op jit(solution)/shard_map/ppermute | solution.py:246
  20.7 8.2 %collective-permute-start.6 = (bf16[32,2560]{1,0:T(8,128)(2,1)S(1)}, bf16[32,2560]{1,0:T(8,128)(2,1)S(1)}, u32[]{:S(2)}, u32[]{:S(2)}) collective-permute-start(bf16[32,2560]{1,0:T(8,128)(2,1)S(1)} %get-tuple-element.38), channel_id=1, source_target_pairs={{0,16},{8,24},{16,0},{24,8},{1,17},{9,25},{17,1},{25,9},{2,18},{10... | collective-permute-start | bytes 491528 | tf_op jit(solution)/shard_map/ppermute | solution.py:246
  29.6 8.5 %collective-permute-start.7 = (bf16[8,5248]{1,0:T(8,128)(2,1)S(1)}, bf16[8,5248]{1,0:T(8,128)(2,1)S(1)}, u32[]{:S(2)}, u32[]{:S(2)}) collective-permute-start(bf16[8,5248]{1,0:T(8,128)(2,1)S(1)} %get-tuple-element.41), channel_id=1, source_target_pairs={{0,4},{1,5},{2,6},{3,7},{4,0},{5,1},{6,2},{7,3},{8,12},{9,13},{10,... | collective-permute-start | bytes 251912 | tf_op jit(solution)/shard_map/ppermute | solution.py:246
  32.3 8.6 %collective-permute-start.8 = (bf16[8,5248]{1,0:T(8,128)(2,1)S(1)}, bf16[8,5248]{1,0:T(8,128)(2,1)S(1)}, u32[]{:S(2)}, u32[]{:S(2)}) collective-permute-start(bf16[8,5248]{1,0:T(8,128)(2,1)S(1)} %get-tuple-element.42), channel_id=1, source_target_pairs={{0,1},{1,0},{2,3},{3,2},{4,5},{5,4},{6,7},{7,6},{8,9},{9,8},{10,11... | collective-permute-start | bytes 251912 | tf_op jit(solution)/shard_map/ppermute | solution.py:246
  33.8 10.2 %collective-permute-start.9 = (bf16[8,5248]{1,0:T(8,128)(2,1)S(1)}, bf16[8,5248]{1,0:T(8,128)(2,1)S(1)}, u32[]{:S(2)}, u32[]{:S(2)}) collective-permute-start(bf16[8,5248]{1,0:T(8,128)(2,1)S(1)} %get-tuple-element.43), channel_id=1, source_target_pairs={{0,6},{1,7},{2,4},{3,5},{4,2},{5,3},{6,0},{7,1},{8,14},{9,15},{10,... | collective-permute-start | bytes 251912 | tf_op jit(solution)/shard_map/ppermute | solution.py:246
  35.1 8.8 %collective-permute-start.10 = (bf16[8,5248]{1,0:T(8,128)(2,1)S(1)}, bf16[8,5248]{1,0:T(8,128)(2,1)S(1)}, u32[]{:S(2)}, u32[]{:S(2)}) collective-permute-start(bf16[8,5248]{1,0:T(8,128)(2,1)S(1)} %get-tuple-element.44), channel_id=1, source_target_pairs={{0,2},{1,3},{2,0},{3,1},{4,6},{5,7},{6,4},{7,5},{8,10},{9,11},{10,... | collective-permute-start | bytes 251912 | tf_op jit(solution)/shard_map/ppermute | solution.py:246
  35.3 10.2 %collective-permute-start.11 = (bf16[8,5248]{1,0:T(8,128)(2,1)S(1)}, bf16[8,5248]{1,0:T(8,128)(2,1)S(1)}, u32[]{:S(2)}, u32[]{:S(2)}) collective-permute-start(bf16[8,5248]{1,0:T(8,128)(2,1)S(1)} %get-tuple-element.45), channel_id=1, source_target_pairs={{0,5},{1,4},{2,7},{3,6},{4,1},{5,0},{6,3},{7,2},{8,13},{9,12},{10,... | collective-permute-start | bytes 251912 | tf_op jit(solution)/shard_map/ppermute | solution.py:246
  38.1 7.7 %collective-permute-start.12 = (bf16[8,5248]{1,0:T(8,128)(2,1)S(1)}, bf16[8,5248]{1,0:T(8,128)(2,1)S(1)}, u32[]{:S(2)}, u32[]{:S(2)}) collective-permute-start(bf16[8,5248]{1,0:T(8,128)(2,1)S(1)} %get-tuple-element.46), channel_id=1, source_target_pairs={{0,3},{1,2},{2,1},{3,0},{4,7},{5,6},{6,5},{7,4},{8,11},{9,10},{10,... | collective-permute-start | bytes 251912 | tf_op jit(solution)/shard_map/ppermute | solution.py:246
  40.9 7.2 %collective-permute-start.13 = (bf16[8,5248]{1,0:T(8,128)(2,1)S(1)}, bf16[8,5248]{1,0:T(8,128)(2,1)S(1)}, u32[]{:S(2)}, u32[]{:S(2)}) collective-permute-start(bf16[8,5248]{1,0:T(8,128)(2,1)S(1)} %get-tuple-element.47), channel_id=1, source_target_pairs={{0,7},{1,6},{2,5},{3,4},{4,3},{5,2},{6,1},{7,0},{8,15},{9,14},{10,... | collective-permute-start | bytes 251912 | tf_op jit(solution)/shard_map/ppermute | solution.py:246
  49.2 11.8 %all-to-all-start = ((bf16[32,2,768]{2,1,0:T(2,128)(2,1)}), bf16[32,2,768]{2,1,0:T(2,128)(2,1)S(1)}, u32[]{:S(2)}, u32[]{:S(2)}) async-start(bf16[32,2,768]{2,1,0:T(2,128)(2,1)} %get-tuple-element.54), calls=%async_computation | async-start | bytes 196608 | tf_op jit(solution)/shard_map/all_to_all | solution.py:253

commit v19 on v18

--- a/solution.py
+++ b/solution.py
@@ -424,7 +424,8 @@
 
 def finish_kernel(width, images, gain_scale, bias_scale, shared_ref, gain_ref, bias_ref):
     devices, lines, line_width = shared_ref.shape
-    total = jnp.sum(shared_ref[...].astype(F32), axis=0) * gain_scale
+    shared = shared_ref[...].astype(F32)
+    total = jnp.sum(shared, axis=0) * gain_scale
     for line in range(lines):
         at = line * line_width
         end = min(at + line_width, width)
@@ -432,7 +433,7 @@
     start = width - (lines - 1) * line_width
     for device in range(devices):
         piece = line_width - start
-        own = shared_ref[device, lines - 1, start:].astype(F32) * bias_scale
+        own = shared[device, lines - 1, start:] * bias_scale
         place = device % images * (devices // images) + device // images
         bias_ref[place * piece : (place + 1) * piece] = own
 

time: 62 us -> 62 us (level)
  no operation moved by 1% of the time
where the time goes in v19:
time: 62 us; the launch traced here: 61.8 us
  starting transfers between devices  25.1 us (40%)
  waiting for transfers between devices  15.6 us (25%)
  Pallas kernels  12.1 us (20%)
  local copies, waits for them, and re-layouts  8.15 us (13%)
  between operations  0.82 us (1%)
    ppermute x14, starting transfers between devices, swap(): return lax.ppermute(x, axis, [(i, i ^ mask) for i in range(n)])  21.1 us
    ppermute x14, waiting for transfers between devices, swap(): return lax.ppermute(x, axis, [(i, i ^ mask) for i in range(n)])  11.2 us
    unnamed x16, local copies, waits for them, and re-layouts  7.01 us
    pallas_call x2, Pallas kernels, project(): pl.pallas_call(functools.partial(project_kernel, blocks, first, tile, wit...  6.03 us
    all_to_all x1, waiting for transfers between devices, exchange(): lax.all_to_all(x, axis, split_axis=0, concat_axis=0, tiled=True)  4.32 us
    all_to_all x1, starting transfers between devices, exchange(): lax.all_to_all(x, axis, split_axis=0, concat_axis=0, tiled=True)  4.02 us
    pallas_call x1, Pallas kernels, window_backward(): pl.pallas_call(window_kernel, out_shape=[shape] * 3, in_specs=vmem(6), ou...  2.38 us
  transfers between devices with their start and end apart: 15, of which 6 were waited for; matrix products, arithmetic and copies ran while one was open for 0% of the time, Pallas kernels for 11%

profile of v19, /device:TPU:0, one launch (start us, length us, event | category | flops | bytes accessed | tf_op | source)
XLA Modules:
  0.0 61.8 jit_solution(3995970844860358836)
XLA Ops:
  0.7 1.1 %dynamic-slice_bitcast_fusion = (bf16[32,2048]{1,0:T(8,128)(2,1)S(1)}, bf16[32,2048]{1,0:T(8,128)(2,1)S(1)}, bf16[32,2048]{1,0:T(8,128)(2,1)S(1)}, bf16[32,2048]{1,0:T(8,128)(2,1)S(1)}) fusion(bf16[1,32,8192]{2,1,0:T(8,128)(2,1)} %param.9, s32[]{:T(128)S(6)} %select_n.15, s32[]{:T(128)S(6)} %select_n.13, s32[]{:T(128)S(6)} %select_n.12, s32[]{:T(128)S(6)} %select_n.14), kind=kLoop, calls=%fused_computation | loop fusion | bytes 1048592 | tf_op jit(solution)/shard_map/dynamic_slice | solution.py:474
  1.8 2.5 %collective-permute-start.2 = (bf16[32,2048]{1,0:T(8,128)(2,1)S(1)}, bf16[32,2048]{1,0:T(8,128)(2,1)S(1)}, u32[]{:S(2)}, u32[]{:S(2)}) collective-permute-start(bf16[32,2048]{1,0:T(8,128)(2,1)S(1)} %get-tuple-element.57), channel_id=1, source_target_pairs={{0,24},{8,16},{16,8},{24,0},{1,25},{9,17},{17,9},{25,1},{2,26},{10... | collective-permute-start | bytes 393224 | tf_op jit(solution)/shard_map/ppermute | solution.py:246
  4.3 0.6 %collective-permute-start = (bf16[32,2048]{1,0:T(8,128)(2,1)S(1)}, bf16[32,2048]{1,0:T(8,128)(2,1)S(1)}, u32[]{:S(2)}, u32[]{:S(2)}) collective-permute-start(bf16[32,2048]{1,0:T(8,128)(2,1)S(1)} %get-tuple-element.58), channel_id=1, source_target_pairs={{0,16},{8,24},{16,0},{24,8},{1,17},{9,25},{17,1},{25,9},{2,18},{10... | collective-permute-start | bytes 393224 | tf_op jit(solution)/shard_map/ppermute | solution.py:246
  4.9 0.0 collective-permute-start.1
  5.0 0.0 copy-start
  5.0 7.0 %copy-done = bf16[5120,2048]{1,0:T(8,128)(2,1)S(1)} copy-done((bf16[5120,2048]{1,0:T(8,128)(2,1)S(1)}, bf16[5120,2048]{1,0:T(8,128)(2,1)}, u32[]{:S(2)}) %copy-start) | copy-done | bytes 20971544
  11.9 0.0 collective-permute-done.2.refs_3_
  11.9 0.0 collective-permute-done.refs_1_
  11.9 0.0 collective-permute-done.1.refs_2_
  11.9 0.0 copy-start.5
  11.9 0.0 copy-start.7
  12.0 0.0 copy-start.1
  12.0 0.0 copy-start.2
  12.0 0.0 copy-start.3
  12.0 0.0 copy-start.6
  12.0 0.0 copy-start.4
  12.0 3.1 %project.2 = (bf16[64,2560]{1,0:T(8,128)(2,1)S(1)}, bf16[64,2560]{1,0:T(8,128)(2,1)S(1)}, f32[1,2048]{1,0:T(1,128)S(1)}) custom-call(bf16[32,2048]{1,0:T(8,128)(2,1)S(1)} %get-tuple-element.59.refs_0_, bf16[32,2048]{1,0:T(8,128)(2,1)S(1)} %collective-permute-done.refs_1_, bf16[32,2048]{1,0:T(8,128)(2,1)S(1)} %collective-permute-done.1.refs_2_, ...), custom_call_target="tpu_custom_call" | custom-call | flops 1342177280 | bytes 10485760 | tf_op jit(solution)/shard_map/project/pallas_call | solution.py:74
  15.1 0.5 collective-permute-start.3
  15.6 3.0 %project.3 = (bf16[64,2560]{1,0:T(8,128)(2,1)S(1)}, bf16[64,2560]{1,0:T(8,128)(2,1)S(1)}) custom-call(bf16[32,2048]{1,0:T(8,128)(2,1)S(1)} %get-tuple-element.59.refs_0_, bf16[32,2048]{1,0:T(8,128)(2,1)S(1)} %collective-permute-done.refs_1_, bf16[32,2048]{1,0:T(8,128)(2,1)S(1)} %collective-permute-done.1.refs_2_, ...), custom_call_target="tpu_custom_call" | custom-call | flops 1342177280 | bytes 10485760 | tf_op jit(solution)/shard_map/project/pallas_call | solution.py:74
  18.6 0.1 collective-permute-start.5
  18.7 0.0 collective-permute-done.3.got_ref
  18.7 0.1 halve.2
  18.8 1.8 %collective-permute-start.4 = (bf16[32,2560]{1,0:T(8,128)(2,1)S(1)}, bf16[32,2560]{1,0:T(8,128)(2,1)S(1)}, u32[]{:S(2)}, u32[]{:S(2)}) collective-permute-start(bf16[32,2560]{1,0:T(8,128)(2,1)S(1)} %get-tuple-element.34), channel_id=1, source_target_pairs={{0,16},{8,24},{16,0},{24,8},{1,17},{9,25},{17,1},{25,9},{2,18},{10... | collective-permute-start | bytes 491528 | tf_op jit(solution)/shard_map/ppermute | solution.py:246
  20.6 0.0 collective-permute-done.5.got_ref
  20.6 0.1 halve.3
  20.7 1.2 %collective-permute-start.6 = (bf16[32,2560]{1,0:T(8,128)(2,1)S(1)}, bf16[32,2560]{1,0:T(8,128)(2,1)S(1)}, u32[]{:S(2)}, u32[]{:S(2)}) collective-permute-start(bf16[32,2560]{1,0:T(8,128)(2,1)S(1)} %get-tuple-element.38), channel_id=1, source_target_pairs={{0,16},{8,24},{16,0},{24,8},{1,17},{9,25},{17,1},{25,9},{2,18},{10... | collective-permute-start | bytes 491528 | tf_op jit(solution)/shard_map/ppermute | solution.py:246
  21.9 4.0 %collective-permute-done.4.refs_2_ = bf16[32,2560]{1,0:T(8,128)(2,1)S(1)} collective-permute-done((bf16[32,2560]{1,0:T(8,128)(2,1)S(1)}, bf16[32,2560]{1,0:T(8,128)(2,1)S(1)}, u32[]{:S(2)}, u32[]{:S(2)}) %collective-permute-start.4) | collective-permute-done | bytes 163872 | tf_op jit(solution)/shard_map/ppermute | solution.py:246
  25.9 3.1 %collective-permute-done.6.refs_4_ = bf16[32,2560]{1,0:T(8,128)(2,1)S(1)} collective-permute-done((bf16[32,2560]{1,0:T(8,128)(2,1)S(1)}, bf16[32,2560]{1,0:T(8,128)(2,1)S(1)}, u32[]{:S(2)}, u32[]{:S(2)}) %collective-permute-start.6) | collective-permute-done | bytes 163872 | tf_op jit(solution)/shard_map/ppermute | solution.py:246
  28.9 0.0 copy-done.5
  28.9 0.7 %pack.1 = (bf16[8,5248]{1,0:T(8,128)(2,1)S(1)}, bf16[8,5248]{1,0:T(8,128)(2,1)S(1)}, bf16[8,5248]{1,0:T(8,128)(2,1)S(1)}, bf16[8,5248]{1,0:T(8,128)(2,1)S(1)}, b...) custom-call(s32[1]{0:T(128)} %bitcast.1.me_ref, ...), custom_call_target="tpu_custom_call" | custom-call | flops 21495808 | bytes 1679360 | tf_op jit(solution)/shard_map/pack/pallas_call | solution.py:224
  29.6 2.7 %collective-permute-start.7 = (bf16[8,5248]{1,0:T(8,128)(2,1)S(1)}, bf16[8,5248]{1,0:T(8,128)(2,1)S(1)}, u32[]{:S(2)}, u32[]{:S(2)}) collective-permute-start(bf16[8,5248]{1,0:T(8,128)(2,1)S(1)} %get-tuple-element.41), channel_id=1, source_target_pairs={{0,4},{1,5},{2,6},{3,7},{4,0},{5,1},{6,2},{7,3},{8,12},{9,13},{10,... | collective-permute-start | bytes 251912 | tf_op jit(solution)/shard_map/ppermute | solution.py:246
  32.3 1.5 %collective-permute-start.8 = (bf16[8,5248]{1,0:T(8,128)(2,1)S(1)}, bf16[8,5248]{1,0:T(8,128)(2,1)S(1)}, u32[]{:S(2)}, u32[]{:S(2)}) collective-permute-start(bf16[8,5248]{1,0:T(8,128)(2,1)S(1)} %get-tuple-element.42), channel_id=1, source_target_pairs={{0,1},{1,0},{2,3},{3,2},{4,5},{5,4},{6,7},{7,6},{8,9},{9,8},{10,11... | collective-permute-start | bytes 251912 | tf_op jit(solution)/shard_map/ppermute | solution.py:246
  33.8 1.4 %collective-permute-start.9 = (bf16[8,5248]{1,0:T(8,128)(2,1)S(1)}, bf16[8,5248]{1,0:T(8,128)(2,1)S(1)}, u32[]{:S(2)}, u32[]{:S(2)}) collective-permute-start(bf16[8,5248]{1,0:T(8,128)(2,1)S(1)} %get-tuple-element.43), channel_id=1, source_target_pairs={{0,6},{1,7},{2,4},{3,5},{4,2},{5,3},{6,0},{7,1},{8,14},{9,15},{10,... | collective-permute-start | bytes 251912 | tf_op jit(solution)/shard_map/ppermute | solution.py:246
  35.1 0.2 collective-permute-start.10
  35.3 2.8 %collective-permute-start.11 = (bf16[8,5248]{1,0:T(8,128)(2,1)S(1)}, bf16[8,5248]{1,0:T(8,128)(2,1)S(1)}, u32[]{:S(2)}, u32[]{:S(2)}) collective-permute-start(bf16[8,5248]{1,0:T(8,128)(2,1)S(1)} %get-tuple-element.45), channel_id=1, source_target_pairs={{0,5},{1,4},{2,7},{3,6},{4,1},{5,0},{6,3},{7,2},{8,13},{9,12},{10,... | collective-permute-start | bytes 251912 | tf_op jit(solution)/shard_map/ppermute | solution.py:246
  38.1 0.0 collective-permute-done.7.refs_1_
  38.1 2.8 %collective-permute-start.12 = (bf16[8,5248]{1,0:T(8,128)(2,1)S(1)}, bf16[8,5248]{1,0:T(8,128)(2,1)S(1)}, u32[]{:S(2)}, u32[]{:S(2)}) collective-permute-start(bf16[8,5248]{1,0:T(8,128)(2,1)S(1)} %get-tuple-element.46), channel_id=1, source_target_pairs={{0,3},{1,2},{2,1},{3,0},{4,7},{5,6},{6,5},{7,4},{8,11},{9,10},{10,... | collective-permute-start | bytes 251912 | tf_op jit(solution)/shard_map/ppermute | solution.py:246
  40.9 0.0 collective-permute-done.8.refs_2_
  40.9 3.0 %collective-permute-start.13 = (bf16[8,5248]{1,0:T(8,128)(2,1)S(1)}, bf16[8,5248]{1,0:T(8,128)(2,1)S(1)}, u32[]{:S(2)}, u32[]{:S(2)}) collective-permute-start(bf16[8,5248]{1,0:T(8,128)(2,1)S(1)} %get-tuple-element.47), channel_id=1, source_target_pairs={{0,7},{1,6},{2,5},{3,4},{4,3},{5,2},{6,1},{7,0},{8,15},{9,14},{10,... | collective-permute-start | bytes 251912 | tf_op jit(solution)/shard_map/ppermute | solution.py:246
  43.9 0.0 copy-done.7
  43.9 0.0 collective-permute-done.9.refs_3_
  43.9 0.0 collective-permute-done.10.refs_4_
  43.9 1.6 %collective-permute-done.11.refs_5_ = bf16[8,5248]{1,0:T(8,128)(2,1)S(1)} collective-permute-done((bf16[8,5248]{1,0:T(8,128)(2,1)S(1)}, bf16[8,5248]{1,0:T(8,128)(2,1)S(1)}, u32[]{:S(2)}, u32[]{:S(2)}) %collective-permute-start.11) | collective-permute-done | bytes 84000 | tf_op jit(solution)/shard_map/ppermute | solution.py:246
  45.6 0.3 collective-permute-done.12.refs_6_
  45.9 2.2 %collective-permute-done.13.refs_7_ = bf16[8,5248]{1,0:T(8,128)(2,1)S(1)} collective-permute-done((bf16[8,5248]{1,0:T(8,128)(2,1)S(1)}, bf16[8,5248]{1,0:T(8,128)(2,1)S(1)}, u32[]{:S(2)}, u32[]{:S(2)}) %collective-permute-start.13) | collective-permute-done | bytes 84000 | tf_op jit(solution)/shard_map/ppermute | solution.py:246
  48.1 0.0 copy-done.1
  48.1 1.1 %norm.1 = (bf16[128,1280]{1,0:T(8,128)(2,1)S(1)}, bf16[32,2,768]{2,1,0:T(2,128)(2,1)}) custom-call(bf16[128,1280]{1,0:T(8,128)(2,1)S(1)} %bitcast.17, f32[1,1280]{1,0:T(1,128)S(1)} %broadcast_in_dim.12.gain_ref, bf16[8,5248]{1,0:T(8,128)(2,1)S(1)} %get-tuple-element.40.refs_0_, bf16[8,5248]{1,0:T(8,128)(2,1)S(1)} %collective-permute-done.7.refs_1_, ...), custom_call_target="tpu_custom_call" | custom-call | flops 85983232 | bytes 1327104 | tf_op jit(solution)/shard_map/norm/pallas_call | solution.py:354
  49.2 4.0 %all-to-all-start = ((bf16[32,2,768]{2,1,0:T(2,128)(2,1)}), bf16[32,2,768]{2,1,0:T(2,128)(2,1)S(1)}, u32[]{:S(2)}, u32[]{:S(2)}) async-start(bf16[32,2,768]{2,1,0:T(2,128)(2,1)} %get-tuple-element.54), calls=%async_computation | async-start | bytes 196608 | tf_op jit(solution)/shard_map/all_to_all | solution.py:253
  53.2 0.0 copy-done.2
  53.2 0.0 copy-done.3
  53.2 0.0 copy-done.6
  53.2 1.1 %probs.1 = (f32[16,128,128]{2,1,0:T(8,128)S(1)}, f32[16,128,128]{2,1,0:T(8,128)S(1)}) custom-call(bf16[128,1280]{1,0:T(8,128)(2,1)S(1)} %bitcast.18, bf16[128,1280]{1,0:T(8,128)(2,1)S(1)} %bitcast.20, s32[1,32]{1,0:T(1,128)S(1)} %bitcast.23), custom_call_target="tpu_custom_call" | custom-call | flops 268435456 | bytes 2097152 | tf_op jit(solution)/shard_map/probs/pallas_call | solution.py:285
  54.3 0.0 copy-done.4
  54.3 2.4 %window.1 = (bf16[128,1280]{1,0:T(8,128)(2,1)}, bf16[128,1280]{1,0:T(8,128)(2,1)}, bf16[128,1280]{1,0:T(8,128)(2,1)}) custom-call(bf16[128,1280]{1,0:T(8,128)(2,1)S(1)} %get-tuple-element.48.g_ref, bf16[128,1280]{1,0:T(8,128)(2,1)S(1)} %bitcast.19, bf16[128,1280]{1,0:T(8,128)(2,1)S(1)} %bitcast.21, bf16[128,1280]{1,0:T(8,128)(2,1)S(1)} %bitcast.22, ...), custom_call_target="tpu_custom_call" | custom-call | flops 335544320 | bytes 4390912 | tf_op jit(solution)/shard_map/window/pallas_call | solution.py:410
  56.7 4.3 %all-to-all-done.shared_ref = bf16[32,2,768]{2,1,0:T(2,128)(2,1)S(1)} async-done(((bf16[32,2,768]{2,1,0:T(2,128)(2,1)}), bf16[32,2,768]{2,1,0:T(2,128)(2,1)S(1)}, u32[]{:S(2)}, u32[]{:S(2)}) %all-to-all-start) | async-done | bytes 98336 | tf_op jit(solution)/shard_map/all_to_all | solution.py:253
  61.0 0.7 %finish.1 = (f32[1280]{0:T(1024)}, f32[8192]{0:T(1024)}) custom-call(bf16[32,2,768]{2,1,0:T(2,128)(2,1)S(1)} %all-to-all-done.shared_ref), custom_call_target="tpu_custom_call" | custom-call | tf_op jit(solution)/shard_map/finish/pallas_call | solution.py:443
  (2 shorter events, 0.0 us)
Async XLA Ops:
  1.8 10.1 %collective-permute-start.2 = (bf16[32,2048]{1,0:T(8,128)(2,1)S(1)}, bf16[32,2048]{1,0:T(8,128)(2,1)S(1)}, u32[]{:S(2)}, u32[]{:S(2)}) collective-permute-start(bf16[32,2048]{1,0:T(8,128)(2,1)S(1)} %get-tuple-element.57), channel_id=1, source_target_pairs={{0,24},{8,16},{16,8},{24,0},{1,25},{9,17},{17,9},{25,1},{2,26},{10... | collective-permute-start | bytes 393224 | tf_op jit(solution)/shard_map/ppermute | solution.py:246
  4.3 7.7 %collective-permute-start = (bf16[32,2048]{1,0:T(8,128)(2,1)S(1)}, bf16[32,2048]{1,0:T(8,128)(2,1)S(1)}, u32[]{:S(2)}, u32[]{:S(2)}) collective-permute-start(bf16[32,2048]{1,0:T(8,128)(2,1)S(1)} %get-tuple-element.58), channel_id=1, source_target_pairs={{0,16},{8,24},{16,0},{24,8},{1,17},{9,25},{17,1},{25,9},{2,18},{10... | collective-permute-start | bytes 393224 | tf_op jit(solution)/shard_map/ppermute | solution.py:246
  4.9 7.0 %collective-permute-start.1 = (bf16[32,2048]{1,0:T(8,128)(2,1)S(1)}, bf16[32,2048]{1,0:T(8,128)(2,1)S(1)}, u32[]{:S(2)}, u32[]{:S(2)}) collective-permute-start(bf16[32,2048]{1,0:T(8,128)(2,1)S(1)} %get-tuple-element.60), channel_id=1, source_target_pairs={{0,8},{8,0},{16,24},{24,16},{1,9},{9,1},{17,25},{25,17},{2,10},{10... | collective-permute-start | bytes 393224 | tf_op jit(solution)/shard_map/ppermute | solution.py:246
  5.0 7.0 %copy-start = (bf16[5120,2048]{1,0:T(8,128)(2,1)S(1)}, bf16[5120,2048]{1,0:T(8,128)(2,1)}, u32[]{:S(2)}) copy-start(bf16[5120,2048]{1,0:T(8,128)(2,1)} %refs_4_.3) | copy-start | bytes 62914564
  11.9 17.0 %copy-start.5 = (s32[1,32]{1,0:T(1,128)S(1)}, s32[1,32]{1,0:T(1,128)}, u32[]{:S(2)}) copy-start(s32[1,32]{1,0:T(1,128)} %refs_0_.1) | copy-start | bytes 388
  11.9 32.0 %copy-start.7 = (f32[1280]{0:T(1024)S(1)}, f32[1280]{0:T(1024)}, u32[]{:S(2)}) copy-start(f32[1280]{0:T(1024)} %param.12) | copy-start | bytes 15364
  12.0 36.1 %copy-start.1 = (bf16[1,128,1280]{2,1,0:T(8,128)(2,1)S(1)}, bf16[1,128,1280]{2,1,0:T(8,128)(2,1)}, u32[]{:S(2)}) copy-start(bf16[1,128,1280]{2,1,0:T(8,128)(2,1)} %param.11) | copy-start | bytes 983044
  12.0 41.2 %copy-start.2 = (bf16[1,128,1280]{2,1,0:T(8,128)(2,1)S(1)}, bf16[1,128,1280]{2,1,0:T(8,128)(2,1)}, u32[]{:S(2)}) copy-start(bf16[1,128,1280]{2,1,0:T(8,128)(2,1)} %param.14) | copy-start | bytes 983044
  12.0 41.2 %copy-start.3 = (bf16[1,128,1280]{2,1,0:T(8,128)(2,1)S(1)}, bf16[1,128,1280]{2,1,0:T(8,128)(2,1)}, u32[]{:S(2)}) copy-start(bf16[1,128,1280]{2,1,0:T(8,128)(2,1)} %param.15) | copy-start | bytes 983044
  12.0 41.2 %copy-start.6 = (s32[1,1,32]{2,1,0:T(1,128)S(1)}, s32[1,1,32]{2,1,0:T(1,128)}, u32[]{:S(2)}) copy-start(s32[1,1,32]{2,1,0:T(1,128)} %param.17) | copy-start | bytes 388
  12.0 42.3 %copy-start.4 = (bf16[1,128,1280]{2,1,0:T(8,128)(2,1)S(1)}, bf16[1,128,1280]{2,1,0:T(8,128)(2,1)}, u32[]{:S(2)}) copy-start(bf16[1,128,1280]{2,1,0:T(8,128)(2,1)} %param.16) | copy-start | bytes 983044
  15.1 3.6 %collective-permute-start.3 = (bf16[64,2560]{1,0:T(8,128)(2,1)S(1)}, bf16[64,2560]{1,0:T(8,128)(2,1)S(1)}, u32[]{:S(2)}, u32[]{:S(2)}) collective-permute-start(bf16[64,2560]{1,0:T(8,128)(2,1)S(1)} %get-tuple-element.32), channel_id=1, source_target_pairs={{0,8},{8,0},{16,24},{24,16},{1,9},{9,1},{17,25},{25,17},{2,10},{10... | collective-permute-start | bytes 983048 | tf_op jit(solution)/shard_map/ppermute | solution.py:246
  18.6 2.0 %collective-permute-start.5 = (bf16[64,2560]{1,0:T(8,128)(2,1)S(1)}, bf16[64,2560]{1,0:T(8,128)(2,1)S(1)}, u32[]{:S(2)}, u32[]{:S(2)}) collective-permute-start(bf16[64,2560]{1,0:T(8,128)(2,1)S(1)} %get-tuple-element.36), channel_id=1, source_target_pairs={{0,8},{8,0},{16,24},{24,16},{1,9},{9,1},{17,25},{25,17},{2,10},{10... | collective-permute-start | bytes 983048 | tf_op jit(solution)/shard_map/ppermute | solution.py:246
  18.8 7.1 %collective-permute-start.4 = (bf16[32,2560]{1,0:T(8,128)(2,1)S(1)}, bf16[32,2560]{1,0:T(8,128)(2,1)S(1)}, u32[]{:S(2)}, u32[]{:S(2)}) collective-permute-start(bf16[32,2560]{1,0:T(8,128)(2,1)S(1)} %get-tuple-element.34), channel_id=1, source_target_pairs={{0,16},{8,24},{16,0},{24,8},{1,17},{9,25},{17,1},{25,9},{2,18},{10... | collective-permute-start | bytes 491528 | tf_op jit(solution)/shard_map/ppermute | solution.py:246
  20.7 8.2 %collective-permute-start.6 = (bf16[32,2560]{1,0:T(8,128)(2,1)S(1)}, bf16[32,2560]{1,0:T(8,128)(2,1)S(1)}, u32[]{:S(2)}, u32[]{:S(2)}) collective-permute-start(bf16[32,2560]{1,0:T(8,128)(2,1)S(1)} %get-tuple-element.38), channel_id=1, source_target_pairs={{0,16},{8,24},{16,0},{24,8},{1,17},{9,25},{17,1},{25,9},{2,18},{10... | collective-permute-start | bytes 491528 | tf_op jit(solution)/shard_map/ppermute | solution.py:246
  29.6 8.5 %collective-permute-start.7 = (bf16[8,5248]{1,0:T(8,128)(2,1)S(1)}, bf16[8,5248]{1,0:T(8,128)(2,1)S(1)}, u32[]{:S(2)}, u32[]{:S(2)}) collective-permute-start(bf16[8,5248]{1,0:T(8,128)(2,1)S(1)} %get-tuple-element.41), channel_id=1, source_target_pairs={{0,4},{1,5},{2,6},{3,7},{4,0},{5,1},{6,2},{7,3},{8,12},{9,13},{10,... | collective-permute-start | bytes 251912 | tf_op jit(solution)/shard_map/ppermute | solution.py:246
  32.3 8.6 %collective-permute-start.8 = (bf16[8,5248]{1,0:T(8,128)(2,1)S(1)}, bf16[8,5248]{1,0:T(8,128)(2,1)S(1)}, u32[]{:S(2)}, u32[]{:S(2)}) collective-permute-start(bf16[8,5248]{1,0:T(8,128)(2,1)S(1)} %get-tuple-element.42), channel_id=1, source_target_pairs={{0,1},{1,0},{2,3},{3,2},{4,5},{5,4},{6,7},{7,6},{8,9},{9,8},{10,11... | collective-permute-start | bytes 251912 | tf_op jit(solution)/shard_map/ppermute | solution.py:246
  33.8 10.2 %collective-permute-start.9 = (bf16[8,5248]{1,0:T(8,128)(2,1)S(1)}, bf16[8,5248]{1,0:T(8,128)(2,1)S(1)}, u32[]{:S(2)}, u32[]{:S(2)}) collective-permute-start(bf16[8,5248]{1,0:T(8,128)(2,1)S(1)} %get-tuple-element.43), channel_id=1, source_target_pairs={{0,6},{1,7},{2,4},{3,5},{4,2},{5,3},{6,0},{7,1},{8,14},{9,15},{10,... | collective-permute-start | bytes 251912 | tf_op jit(solution)/shard_map/ppermute | solution.py:246
  35.1 8.8 %collective-permute-start.10 = (bf16[8,5248]{1,0:T(8,128)(2,1)S(1)}, bf16[8,5248]{1,0:T(8,128)(2,1)S(1)}, u32[]{:S(2)}, u32[]{:S(2)}) collective-permute-start(bf16[8,5248]{1,0:T(8,128)(2,1)S(1)} %get-tuple-element.44), channel_id=1, source_target_pairs={{0,2},{1,3},{2,0},{3,1},{4,6},{5,7},{6,4},{7,5},{8,10},{9,11},{10,... | collective-permute-start | bytes 251912 | tf_op jit(solution)/shard_map/ppermute | solution.py:246
  35.3 10.2 %collective-permute-start.11 = (bf16[8,5248]{1,0:T(8,128)(2,1)S(1)}, bf16[8,5248]{1,0:T(8,128)(2,1)S(1)}, u32[]{:S(2)}, u32[]{:S(2)}) collective-permute-start(bf16[8,5248]{1,0:T(8,128)(2,1)S(1)} %get-tuple-element.45), channel_id=1, source_target_pairs={{0,5},{1,4},{2,7},{3,6},{4,1},{5,0},{6,3},{7,2},{8,13},{9,12},{10,... | collective-permute-start | bytes 251912 | tf_op jit(solution)/shard_map/ppermute | solution.py:246
  38.1 7.7 %collective-permute-start.12 = (bf16[8,5248]{1,0:T(8,128)(2,1)S(1)}, bf16[8,5248]{1,0:T(8,128)(2,1)S(1)}, u32[]{:S(2)}, u32[]{:S(2)}) collective-permute-start(bf16[8,5248]{1,0:T(8,128)(2,1)S(1)} %get-tuple-element.46), channel_id=1, source_target_pairs={{0,3},{1,2},{2,1},{3,0},{4,7},{5,6},{6,5},{7,4},{8,11},{9,10},{10,... | collective-permute-start | bytes 251912 | tf_op jit(solution)/shard_map/ppermute | solution.py:246
  40.9 7.2 %collective-permute-start.13 = (bf16[8,5248]{1,0:T(8,128)(2,1)S(1)}, bf16[8,5248]{1,0:T(8,128)(2,1)S(1)}, u32[]{:S(2)}, u32[]{:S(2)}) collective-permute-start(bf16[8,5248]{1,0:T(8,128)(2,1)S(1)} %get-tuple-element.47), channel_id=1, source_target_pairs={{0,7},{1,6},{2,5},{3,4},{4,3},{5,2},{6,1},{7,0},{8,15},{9,14},{10,... | collective-permute-start | bytes 251912 | tf_op jit(solution)/shard_map/ppermute | solution.py:246
  49.2 11.8 %all-to-all-start = ((bf16[32,2,768]{2,1,0:T(2,128)(2,1)}), bf16[32,2,768]{2,1,0:T(2,128)(2,1)S(1)}, u32[]{:S(2)}, u32[]{:S(2)}) async-start(bf16[32,2,768]{2,1,0:T(2,128)(2,1)} %get-tuple-element.54), calls=%async_computation | async-start | bytes 196608 | tf_op jit(solution)/shard_map/all_to_all | solution.py:253

commit v20 on v19

--- a/solution.py
+++ b/solution.py
@@ -129,7 +129,7 @@
 
 
 def peer_masks(peers):
-    return (0, 4, 1, 6, 2, 5, 3, 7) if peers == 8 else tuple(range(peers))
+    return (0, 7, 1, 6, 2, 5, 3, 4) if peers == 8 else tuple(range(peers))
 
 
 def early_masks(peers):

time: 62 us -> 61.9 us (level)
  starting transfers between devices: 25.1 us -> 24.1 us
  waiting for transfers between devices: 15.6 us -> 16.5 us
    ppermute x14, starting transfers between devices: 21.1 us -> 20.1 us  [swap(): return lax.ppermute(x, axis, [(i, i ^ mask) for i in range(n)])]
    ppermute x14, waiting for transfers between devices: 11.2 us -> 12.2 us  [swap(): return lax.ppermute(x, axis, [(i, i ^ mask) for i in range(n)])]
  transfers between devices with their start and end apart: 15 -> 15, of which waited for: 6 -> 5; matrix products, arithmetic and copies ran while one was open for 0% -> 0% of each run, Pallas kernels for 11% -> 11%
where the time goes in v20:
time: 61.9 us; the launch traced here: 61.7 us
  starting transfers between devices  24.1 us (39%)
  waiting for transfers between devices  16.5 us (27%)
  Pallas kernels  12.1 us (20%)
  local copies, waits for them, and re-layouts  8.15 us (13%)
  between operations  0.83 us (1%)
    ppermute x14, starting transfers between devices, swap(): return lax.ppermute(x, axis, [(i, i ^ mask) for i in range(n)])  20.1 us
    ppermute x14, waiting for transfers between devices, swap(): return lax.ppermute(x, axis, [(i, i ^ mask) for i in range(n)])  12.2 us
    unnamed x16, local copies, waits for them, and re-layouts  7.01 us
    pallas_call x2, Pallas kernels, project(): pl.pallas_call(functools.partial(project_kernel, blocks, first, tile, wit...  6.03 us
    all_to_all x1, waiting for transfers between devices, exchange(): lax.all_to_all(x, axis, split_axis=0, concat_axis=0, tiled=True)  4.32 us
    all_to_all x1, starting transfers between devices, exchange(): lax.all_to_all(x, axis, split_axis=0, concat_axis=0, tiled=True)  4 us
    pallas_call x1, Pallas kernels, window_backward(): pl.pallas_call(window_kernel, out_shape=[shape] * 3, in_specs=vmem(6), ou...  2.38 us
  transfers between devices with their start and end apart: 15, of which 5 were waited for; matrix products, arithmetic and copies ran while one was open for 0% of the time, Pallas kernels for 11%

profile of v20, /device:TPU:0, one launch (start us, length us, event | category | flops | bytes accessed | tf_op | source)
XLA Modules:
  0.0 61.7 jit_solution(504707548823589901)
XLA Ops:
  0.7 1.1 %dynamic-slice_bitcast_fusion = (bf16[32,2048]{1,0:T(8,128)(2,1)S(1)}, bf16[32,2048]{1,0:T(8,128)(2,1)S(1)}, bf16[32,2048]{1,0:T(8,128)(2,1)S(1)}, bf16[32,2048]{1,0:T(8,128)(2,1)S(1)}) fusion(bf16[1,32,8192]{2,1,0:T(8,128)(2,1)} %param.9, s32[]{:T(128)S(6)} %select_n.15, s32[]{:T(128)S(6)} %select_n.13, s32[]{:T(128)S(6)} %select_n.12, s32[]{:T(128)S(6)} %select_n.14), kind=kLoop, calls=%fused_computation | loop fusion | bytes 1048592 | tf_op jit(solution)/shard_map/dynamic_slice | solution.py:474
  1.8 2.5 %collective-permute-start.2 = (bf16[32,2048]{1,0:T(8,128)(2,1)S(1)}, bf16[32,2048]{1,0:T(8,128)(2,1)S(1)}, u32[]{:S(2)}, u32[]{:S(2)}) collective-permute-start(bf16[32,2048]{1,0:T(8,128)(2,1)S(1)} %get-tuple-element.57), channel_id=1, source_target_pairs={{0,24},{8,16},{16,8},{24,0},{1,25},{9,17},{17,9},{25,1},{2,26},{10... | collective-permute-start | bytes 393224 | tf_op jit(solution)/shard_map/ppermute | solution.py:246
  4.3 0.6 %collective-permute-start = (bf16[32,2048]{1,0:T(8,128)(2,1)S(1)}, bf16[32,2048]{1,0:T(8,128)(2,1)S(1)}, u32[]{:S(2)}, u32[]{:S(2)}) collective-permute-start(bf16[32,2048]{1,0:T(8,128)(2,1)S(1)} %get-tuple-element.58), channel_id=1, source_target_pairs={{0,16},{8,24},{16,0},{24,8},{1,17},{9,25},{17,1},{25,9},{2,18},{10... | collective-permute-start | bytes 393224 | tf_op jit(solution)/shard_map/ppermute | solution.py:246
  4.9 0.0 collective-permute-start.1
  5.0 0.0 copy-start
  5.0 7.0 %copy-done = bf16[5120,2048]{1,0:T(8,128)(2,1)S(1)} copy-done((bf16[5120,2048]{1,0:T(8,128)(2,1)S(1)}, bf16[5120,2048]{1,0:T(8,128)(2,1)}, u32[]{:S(2)}) %copy-start) | copy-done | bytes 20971544
  11.9 0.0 collective-permute-done.2.refs_3_
  11.9 0.0 collective-permute-done.refs_1_
  11.9 0.0 collective-permute-done.1.refs_2_
  11.9 0.0 copy-start.5
  11.9 0.0 copy-start.7
  12.0 0.0 copy-start.1
  12.0 0.0 copy-start.2
  12.0 0.0 copy-start.3
  12.0 0.0 copy-start.6
  12.0 0.0 copy-start.4
  12.0 3.1 %project.2 = (bf16[64,2560]{1,0:T(8,128)(2,1)S(1)}, bf16[64,2560]{1,0:T(8,128)(2,1)S(1)}, f32[1,2048]{1,0:T(1,128)S(1)}) custom-call(bf16[32,2048]{1,0:T(8,128)(2,1)S(1)} %get-tuple-element.59.refs_0_, bf16[32,2048]{1,0:T(8,128)(2,1)S(1)} %collective-permute-done.refs_1_, bf16[32,2048]{1,0:T(8,128)(2,1)S(1)} %collective-permute-done.1.refs_2_, ...), custom_call_target="tpu_custom_call" | custom-call | flops 1342177280 | bytes 10485760 | tf_op jit(solution)/shard_map/project/pallas_call | solution.py:74
  15.1 0.5 collective-permute-start.3
  15.6 3.0 %project.3 = (bf16[64,2560]{1,0:T(8,128)(2,1)S(1)}, bf16[64,2560]{1,0:T(8,128)(2,1)S(1)}) custom-call(bf16[32,2048]{1,0:T(8,128)(2,1)S(1)} %get-tuple-element.59.refs_0_, bf16[32,2048]{1,0:T(8,128)(2,1)S(1)} %collective-permute-done.refs_1_, bf16[32,2048]{1,0:T(8,128)(2,1)S(1)} %collective-permute-done.1.refs_2_, ...), custom_call_target="tpu_custom_call" | custom-call | flops 1342177280 | bytes 10485760 | tf_op jit(solution)/shard_map/project/pallas_call | solution.py:74
  18.6 0.1 collective-permute-start.5
  18.7 0.0 collective-permute-done.3.got_ref
  18.7 0.1 halve.2
  18.8 1.8 %collective-permute-start.4 = (bf16[32,2560]{1,0:T(8,128)(2,1)S(1)}, bf16[32,2560]{1,0:T(8,128)(2,1)S(1)}, u32[]{:S(2)}, u32[]{:S(2)}) collective-permute-start(bf16[32,2560]{1,0:T(8,128)(2,1)S(1)} %get-tuple-element.34), channel_id=1, source_target_pairs={{0,16},{8,24},{16,0},{24,8},{1,17},{9,25},{17,1},{25,9},{2,18},{10... | collective-permute-start | bytes 491528 | tf_op jit(solution)/shard_map/ppermute | solution.py:246
  20.6 0.0 collective-permute-done.5.got_ref
  20.6 0.1 halve.3
  20.7 1.2 %collective-permute-start.6 = (bf16[32,2560]{1,0:T(8,128)(2,1)S(1)}, bf16[32,2560]{1,0:T(8,128)(2,1)S(1)}, u32[]{:S(2)}, u32[]{:S(2)}) collective-permute-start(bf16[32,2560]{1,0:T(8,128)(2,1)S(1)} %get-tuple-element.38), channel_id=1, source_target_pairs={{0,16},{8,24},{16,0},{24,8},{1,17},{9,25},{17,1},{25,9},{2,18},{10... | collective-permute-start | bytes 491528 | tf_op jit(solution)/shard_map/ppermute | solution.py:246
  21.9 4.0 %collective-permute-done.4.refs_2_ = bf16[32,2560]{1,0:T(8,128)(2,1)S(1)} collective-permute-done((bf16[32,2560]{1,0:T(8,128)(2,1)S(1)}, bf16[32,2560]{1,0:T(8,128)(2,1)S(1)}, u32[]{:S(2)}, u32[]{:S(2)}) %collective-permute-start.4) | collective-permute-done | bytes 163872 | tf_op jit(solution)/shard_map/ppermute | solution.py:246
  25.9 3.1 %collective-permute-done.6.refs_4_ = bf16[32,2560]{1,0:T(8,128)(2,1)S(1)} collective-permute-done((bf16[32,2560]{1,0:T(8,128)(2,1)S(1)}, bf16[32,2560]{1,0:T(8,128)(2,1)S(1)}, u32[]{:S(2)}, u32[]{:S(2)}) %collective-permute-start.6) | collective-permute-done | bytes 163872 | tf_op jit(solution)/shard_map/ppermute | solution.py:246
  28.9 0.0 copy-done.5
  28.9 0.7 %pack.1 = (bf16[8,5248]{1,0:T(8,128)(2,1)S(1)}, bf16[8,5248]{1,0:T(8,128)(2,1)S(1)}, bf16[8,5248]{1,0:T(8,128)(2,1)S(1)}, bf16[8,5248]{1,0:T(8,128)(2,1)S(1)}, b...) custom-call(s32[1]{0:T(128)} %bitcast.1.me_ref, ...), custom_call_target="tpu_custom_call" | custom-call | flops 21495808 | bytes 1679360 | tf_op jit(solution)/shard_map/pack/pallas_call | solution.py:224
  29.6 4.6 %collective-permute-start.7 = (bf16[8,5248]{1,0:T(8,128)(2,1)S(1)}, bf16[8,5248]{1,0:T(8,128)(2,1)S(1)}, u32[]{:S(2)}, u32[]{:S(2)}) collective-permute-start(bf16[8,5248]{1,0:T(8,128)(2,1)S(1)} %get-tuple-element.41), channel_id=1, source_target_pairs={{0,7},{1,6},{2,5},{3,4},{4,3},{5,2},{6,1},{7,0},{8,15},{9,14},{10,... | collective-permute-start | bytes 251912 | tf_op jit(solution)/shard_map/ppermute | solution.py:246
  34.2 0.6 collective-permute-start.8
  34.8 0.2 collective-permute-start.9
  35.0 0.0 collective-permute-start.10
  35.0 5.1 %collective-permute-start.11 = (bf16[8,5248]{1,0:T(8,128)(2,1)S(1)}, bf16[8,5248]{1,0:T(8,128)(2,1)S(1)}, u32[]{:S(2)}, u32[]{:S(2)}) collective-permute-start(bf16[8,5248]{1,0:T(8,128)(2,1)S(1)} %get-tuple-element.45), channel_id=1, source_target_pairs={{0,5},{1,4},{2,7},{3,6},{4,1},{5,0},{6,3},{7,2},{8,13},{9,12},{10,... | collective-permute-start | bytes 251912 | tf_op jit(solution)/shard_map/ppermute | solution.py:246
  40.1 0.0 collective-permute-done.7.refs_1_
  40.1 0.0 collective-permute-start.12
  40.1 0.0 collective-permute-done.8.refs_2_
  40.1 2.8 %collective-permute-start.13 = (bf16[8,5248]{1,0:T(8,128)(2,1)S(1)}, bf16[8,5248]{1,0:T(8,128)(2,1)S(1)}, u32[]{:S(2)}, u32[]{:S(2)}) collective-permute-start(bf16[8,5248]{1,0:T(8,128)(2,1)S(1)} %get-tuple-element.47), channel_id=1, source_target_pairs={{0,4},{1,5},{2,6},{3,7},{4,0},{5,1},{6,2},{7,3},{8,12},{9,13},{10,... | collective-permute-start | bytes 251912 | tf_op jit(solution)/shard_map/ppermute | solution.py:246
  42.9 0.0 copy-done.7
  42.9 0.0 collective-permute-done.9.refs_3_
  42.9 0.0 collective-permute-done.10.refs_4_
  42.9 3.4 %collective-permute-done.11.refs_5_ = bf16[8,5248]{1,0:T(8,128)(2,1)S(1)} collective-permute-done((bf16[8,5248]{1,0:T(8,128)(2,1)S(1)}, bf16[8,5248]{1,0:T(8,128)(2,1)S(1)}, u32[]{:S(2)}, u32[]{:S(2)}) %collective-permute-start.11) | collective-permute-done | bytes 84000 | tf_op jit(solution)/shard_map/ppermute | solution.py:246
  46.3 0.0 collective-permute-done.12.refs_6_
  46.3 1.7 %collective-permute-done.13.refs_7_ = bf16[8,5248]{1,0:T(8,128)(2,1)S(1)} collective-permute-done((bf16[8,5248]{1,0:T(8,128)(2,1)S(1)}, bf16[8,5248]{1,0:T(8,128)(2,1)S(1)}, u32[]{:S(2)}, u32[]{:S(2)}) %collective-permute-start.13) | collective-permute-done | bytes 84000 | tf_op jit(solution)/shard_map/ppermute | solution.py:246
  48.0 0.0 copy-done.1
  48.0 1.1 %norm.1 = (bf16[128,1280]{1,0:T(8,128)(2,1)S(1)}, bf16[32,2,768]{2,1,0:T(2,128)(2,1)}) custom-call(bf16[128,1280]{1,0:T(8,128)(2,1)S(1)} %bitcast.17, f32[1,1280]{1,0:T(1,128)S(1)} %broadcast_in_dim.12.gain_ref, bf16[8,5248]{1,0:T(8,128)(2,1)S(1)} %get-tuple-element.40.refs_0_, bf16[8,5248]{1,0:T(8,128)(2,1)S(1)} %collective-permute-done.7.refs_1_, ...), custom_call_target="tpu_custom_call" | custom-call | flops 85983232 | bytes 1327104 | tf_op jit(solution)/shard_map/norm/pallas_call | solution.py:354
  49.1 4.0 %all-to-all-start = ((bf16[32,2,768]{2,1,0:T(2,128)(2,1)}), bf16[32,2,768]{2,1,0:T(2,128)(2,1)S(1)}, u32[]{:S(2)}, u32[]{:S(2)}) async-start(bf16[32,2,768]{2,1,0:T(2,128)(2,1)} %get-tuple-element.54), calls=%async_computation | async-start | bytes 196608 | tf_op jit(solution)/shard_map/all_to_all | solution.py:253
  53.1 0.0 copy-done.2
  53.1 0.0 copy-done.3
  53.1 0.0 copy-done.6
  53.2 1.1 %probs.1 = (f32[16,128,128]{2,1,0:T(8,128)S(1)}, f32[16,128,128]{2,1,0:T(8,128)S(1)}) custom-call(bf16[128,1280]{1,0:T(8,128)(2,1)S(1)} %bitcast.18, bf16[128,1280]{1,0:T(8,128)(2,1)S(1)} %bitcast.20, s32[1,32]{1,0:T(1,128)S(1)} %bitcast.23), custom_call_target="tpu_custom_call" | custom-call | flops 268435456 | bytes 2097152 | tf_op jit(solution)/shard_map/probs/pallas_call | solution.py:285
  54.2 0.0 copy-done.4
  54.2 2.4 %window.1 = (bf16[128,1280]{1,0:T(8,128)(2,1)}, bf16[128,1280]{1,0:T(8,128)(2,1)}, bf16[128,1280]{1,0:T(8,128)(2,1)}) custom-call(bf16[128,1280]{1,0:T(8,128)(2,1)S(1)} %get-tuple-element.48.g_ref, bf16[128,1280]{1,0:T(8,128)(2,1)S(1)} %bitcast.19, bf16[128,1280]{1,0:T(8,128)(2,1)S(1)} %bitcast.21, bf16[128,1280]{1,0:T(8,128)(2,1)S(1)} %bitcast.22, ...), custom_call_target="tpu_custom_call" | custom-call | flops 335544320 | bytes 4390912 | tf_op jit(solution)/shard_map/window/pallas_call | solution.py:410
  56.6 4.3 %all-to-all-done.shared_ref = bf16[32,2,768]{2,1,0:T(2,128)(2,1)S(1)} async-done(((bf16[32,2,768]{2,1,0:T(2,128)(2,1)}), bf16[32,2,768]{2,1,0:T(2,128)(2,1)S(1)}, u32[]{:S(2)}, u32[]{:S(2)}) %all-to-all-start) | async-done | bytes 98336 | tf_op jit(solution)/shard_map/all_to_all | solution.py:253
  60.9 0.7 %finish.1 = (f32[1280]{0:T(1024)}, f32[8192]{0:T(1024)}) custom-call(bf16[32,2,768]{2,1,0:T(2,128)(2,1)S(1)} %all-to-all-done.shared_ref), custom_call_target="tpu_custom_call" | custom-call | tf_op jit(solution)/shard_map/finish/pallas_call | solution.py:443
  (2 shorter events, 0.0 us)
Async XLA Ops:
  1.8 10.1 %collective-permute-start.2 = (bf16[32,2048]{1,0:T(8,128)(2,1)S(1)}, bf16[32,2048]{1,0:T(8,128)(2,1)S(1)}, u32[]{:S(2)}, u32[]{:S(2)}) collective-permute-start(bf16[32,2048]{1,0:T(8,128)(2,1)S(1)} %get-tuple-element.57), channel_id=1, source_target_pairs={{0,24},{8,16},{16,8},{24,0},{1,25},{9,17},{17,9},{25,1},{2,26},{10... | collective-permute-start | bytes 393224 | tf_op jit(solution)/shard_map/ppermute | solution.py:246
  4.3 7.7 %collective-permute-start = (bf16[32,2048]{1,0:T(8,128)(2,1)S(1)}, bf16[32,2048]{1,0:T(8,128)(2,1)S(1)}, u32[]{:S(2)}, u32[]{:S(2)}) collective-permute-start(bf16[32,2048]{1,0:T(8,128)(2,1)S(1)} %get-tuple-element.58), channel_id=1, source_target_pairs={{0,16},{8,24},{16,0},{24,8},{1,17},{9,25},{17,1},{25,9},{2,18},{10... | collective-permute-start | bytes 393224 | tf_op jit(solution)/shard_map/ppermute | solution.py:246
  4.9 7.0 %collective-permute-start.1 = (bf16[32,2048]{1,0:T(8,128)(2,1)S(1)}, bf16[32,2048]{1,0:T(8,128)(2,1)S(1)}, u32[]{:S(2)}, u32[]{:S(2)}) collective-permute-start(bf16[32,2048]{1,0:T(8,128)(2,1)S(1)} %get-tuple-element.60), channel_id=1, source_target_pairs={{0,8},{8,0},{16,24},{24,16},{1,9},{9,1},{17,25},{25,17},{2,10},{10... | collective-permute-start | bytes 393224 | tf_op jit(solution)/shard_map/ppermute | solution.py:246
  5.0 7.0 %copy-start = (bf16[5120,2048]{1,0:T(8,128)(2,1)S(1)}, bf16[5120,2048]{1,0:T(8,128)(2,1)}, u32[]{:S(2)}) copy-start(bf16[5120,2048]{1,0:T(8,128)(2,1)} %refs_4_.3) | copy-start | bytes 62914564
  11.9 17.0 %copy-start.5 = (s32[1,32]{1,0:T(1,128)S(1)}, s32[1,32]{1,0:T(1,128)}, u32[]{:S(2)}) copy-start(s32[1,32]{1,0:T(1,128)} %refs_0_.1) | copy-start | bytes 388
  11.9 30.9 %copy-start.7 = (f32[1280]{0:T(1024)S(1)}, f32[1280]{0:T(1024)}, u32[]{:S(2)}) copy-start(f32[1280]{0:T(1024)} %param.12) | copy-start | bytes 15364
  12.0 36.1 %copy-start.1 = (bf16[1,128,1280]{2,1,0:T(8,128)(2,1)S(1)}, bf16[1,128,1280]{2,1,0:T(8,128)(2,1)}, u32[]{:S(2)}) copy-start(bf16[1,128,1280]{2,1,0:T(8,128)(2,1)} %param.11) | copy-start | bytes 983044
  12.0 41.2 %copy-start.2 = (bf16[1,128,1280]{2,1,0:T(8,128)(2,1)S(1)}, bf16[1,128,1280]{2,1,0:T(8,128)(2,1)}, u32[]{:S(2)}) copy-start(bf16[1,128,1280]{2,1,0:T(8,128)(2,1)} %param.14) | copy-start | bytes 983044
  12.0 41.2 %copy-start.3 = (bf16[1,128,1280]{2,1,0:T(8,128)(2,1)S(1)}, bf16[1,128,1280]{2,1,0:T(8,128)(2,1)}, u32[]{:S(2)}) copy-start(bf16[1,128,1280]{2,1,0:T(8,128)(2,1)} %param.15) | copy-start | bytes 983044
  12.0 41.2 %copy-start.6 = (s32[1,1,32]{2,1,0:T(1,128)S(1)}, s32[1,1,32]{2,1,0:T(1,128)}, u32[]{:S(2)}) copy-start(s32[1,1,32]{2,1,0:T(1,128)} %param.17) | copy-start | bytes 388
  12.0 42.2 %copy-start.4 = (bf16[1,128,1280]{2,1,0:T(8,128)(2,1)S(1)}, bf16[1,128,1280]{2,1,0:T(8,128)(2,1)}, u32[]{:S(2)}) copy-start(bf16[1,128,1280]{2,1,0:T(8,128)(2,1)} %param.16) | copy-start | bytes 983044
  15.1 3.6 %collective-permute-start.3 = (bf16[64,2560]{1,0:T(8,128)(2,1)S(1)}, bf16[64,2560]{1,0:T(8,128)(2,1)S(1)}, u32[]{:S(2)}, u32[]{:S(2)}) collective-permute-start(bf16[64,2560]{1,0:T(8,128)(2,1)S(1)} %get-tuple-element.32), channel_id=1, source_target_pairs={{0,8},{8,0},{16,24},{24,16},{1,9},{9,1},{17,25},{25,17},{2,10},{10... | collective-permute-start | bytes 983048 | tf_op jit(solution)/shard_map/ppermute | solution.py:246
  18.6 2.0 %collective-permute-start.5 = (bf16[64,2560]{1,0:T(8,128)(2,1)S(1)}, bf16[64,2560]{1,0:T(8,128)(2,1)S(1)}, u32[]{:S(2)}, u32[]{:S(2)}) collective-permute-start(bf16[64,2560]{1,0:T(8,128)(2,1)S(1)} %get-tuple-element.36), channel_id=1, source_target_pairs={{0,8},{8,0},{16,24},{24,16},{1,9},{9,1},{17,25},{25,17},{2,10},{10... | collective-permute-start | bytes 983048 | tf_op jit(solution)/shard_map/ppermute | solution.py:246
  18.8 7.1 %collective-permute-start.4 = (bf16[32,2560]{1,0:T(8,128)(2,1)S(1)}, bf16[32,2560]{1,0:T(8,128)(2,1)S(1)}, u32[]{:S(2)}, u32[]{:S(2)}) collective-permute-start(bf16[32,2560]{1,0:T(8,128)(2,1)S(1)} %get-tuple-element.34), channel_id=1, source_target_pairs={{0,16},{8,24},{16,0},{24,8},{1,17},{9,25},{17,1},{25,9},{2,18},{10... | collective-permute-start | bytes 491528 | tf_op jit(solution)/shard_map/ppermute | solution.py:246
  20.7 8.2 %collective-permute-start.6 = (bf16[32,2560]{1,0:T(8,128)(2,1)S(1)}, bf16[32,2560]{1,0:T(8,128)(2,1)S(1)}, u32[]{:S(2)}, u32[]{:S(2)}) collective-permute-start(bf16[32,2560]{1,0:T(8,128)(2,1)S(1)} %get-tuple-element.38), channel_id=1, source_target_pairs={{0,16},{8,24},{16,0},{24,8},{1,17},{9,25},{17,1},{25,9},{2,18},{10... | collective-permute-start | bytes 491528 | tf_op jit(solution)/shard_map/ppermute | solution.py:246
  29.6 10.4 %collective-permute-start.7 = (bf16[8,5248]{1,0:T(8,128)(2,1)S(1)}, bf16[8,5248]{1,0:T(8,128)(2,1)S(1)}, u32[]{:S(2)}, u32[]{:S(2)}) collective-permute-start(bf16[8,5248]{1,0:T(8,128)(2,1)S(1)} %get-tuple-element.41), channel_id=1, source_target_pairs={{0,7},{1,6},{2,5},{3,4},{4,3},{5,2},{6,1},{7,0},{8,15},{9,14},{10,... | collective-permute-start | bytes 251912 | tf_op jit(solution)/shard_map/ppermute | solution.py:246
  34.2 5.9 %collective-permute-start.8 = (bf16[8,5248]{1,0:T(8,128)(2,1)S(1)}, bf16[8,5248]{1,0:T(8,128)(2,1)S(1)}, u32[]{:S(2)}, u32[]{:S(2)}) collective-permute-start(bf16[8,5248]{1,0:T(8,128)(2,1)S(1)} %get-tuple-element.42), channel_id=1, source_target_pairs={{0,1},{1,0},{2,3},{3,2},{4,5},{5,4},{6,7},{7,6},{8,9},{9,8},{10,11... | collective-permute-start | bytes 251912 | tf_op jit(solution)/shard_map/ppermute | solution.py:246
  34.8 8.1 %collective-permute-start.9 = (bf16[8,5248]{1,0:T(8,128)(2,1)S(1)}, bf16[8,5248]{1,0:T(8,128)(2,1)S(1)}, u32[]{:S(2)}, u32[]{:S(2)}) collective-permute-start(bf16[8,5248]{1,0:T(8,128)(2,1)S(1)} %get-tuple-element.43), channel_id=1, source_target_pairs={{0,6},{1,7},{2,4},{3,5},{4,2},{5,3},{6,0},{7,1},{8,14},{9,15},{10,... | collective-permute-start | bytes 251912 | tf_op jit(solution)/shard_map/ppermute | solution.py:246
  35.0 8.0 %collective-permute-start.10 = (bf16[8,5248]{1,0:T(8,128)(2,1)S(1)}, bf16[8,5248]{1,0:T(8,128)(2,1)S(1)}, u32[]{:S(2)}, u32[]{:S(2)}) collective-permute-start(bf16[8,5248]{1,0:T(8,128)(2,1)S(1)} %get-tuple-element.44), channel_id=1, source_target_pairs={{0,2},{1,3},{2,0},{3,1},{4,6},{5,7},{6,4},{7,5},{8,10},{9,11},{10,... | collective-permute-start | bytes 251912 | tf_op jit(solution)/shard_map/ppermute | solution.py:246
  35.0 11.3 %collective-permute-start.11 = (bf16[8,5248]{1,0:T(8,128)(2,1)S(1)}, bf16[8,5248]{1,0:T(8,128)(2,1)S(1)}, u32[]{:S(2)}, u32[]{:S(2)}) collective-permute-start(bf16[8,5248]{1,0:T(8,128)(2,1)S(1)} %get-tuple-element.45), channel_id=1, source_target_pairs={{0,5},{1,4},{2,7},{3,6},{4,1},{5,0},{6,3},{7,2},{8,13},{9,12},{10,... | collective-permute-start | bytes 251912 | tf_op jit(solution)/shard_map/ppermute | solution.py:246
  40.1 6.2 %collective-permute-start.12 = (bf16[8,5248]{1,0:T(8,128)(2,1)S(1)}, bf16[8,5248]{1,0:T(8,128)(2,1)S(1)}, u32[]{:S(2)}, u32[]{:S(2)}) collective-permute-start(bf16[8,5248]{1,0:T(8,128)(2,1)S(1)} %get-tuple-element.46), channel_id=1, source_target_pairs={{0,3},{1,2},{2,1},{3,0},{4,7},{5,6},{6,5},{7,4},{8,11},{9,10},{10,... | collective-permute-start | bytes 251912 | tf_op jit(solution)/shard_map/ppermute | solution.py:246
  40.1 8.0 %collective-permute-start.13 = (bf16[8,5248]{1,0:T(8,128)(2,1)S(1)}, bf16[8,5248]{1,0:T(8,128)(2,1)S(1)}, u32[]{:S(2)}, u32[]{:S(2)}) collective-permute-start(bf16[8,5248]{1,0:T(8,128)(2,1)S(1)} %get-tuple-element.47), channel_id=1, source_target_pairs={{0,4},{1,5},{2,6},{3,7},{4,0},{5,1},{6,2},{7,3},{8,12},{9,13},{10,... | collective-permute-start | bytes 251912 | tf_op jit(solution)/shard_map/ppermute | solution.py:246
  49.1 11.8 %all-to-all-start = ((bf16[32,2,768]{2,1,0:T(2,128)(2,1)}), bf16[32,2,768]{2,1,0:T(2,128)(2,1)S(1)}, u32[]{:S(2)}, u32[]{:S(2)}) async-start(bf16[32,2,768]{2,1,0:T(2,128)(2,1)} %get-tuple-element.54), calls=%async_computation | async-start | bytes 196608 | tf_op jit(solution)/shard_map/all_to_all | solution.py:253

commit v21 on v20

--- a/solution.py
+++ b/solution.py
@@ -11,7 +11,7 @@
 HEADS = 16
 HEAD_DIM = 80
 LANES = 128
-CHUNKS = (2, 2)
+CHUNKS = (3, 1)
 DIRECT = 8
 VMEM_BYTES = 16 * 1024 * 1024
 

time: 61.9 us -> 61.9 us (level)
  transfers between devices with their start and end apart: 15 -> 15, of which waited for: 5 -> 4; matrix products, arithmetic and copies ran while one was open for 0% -> 0% of each run, Pallas kernels for 11% -> 8%
where the time goes in v21:
time: 61.9 us; the launch traced here: 61.6 us
  starting transfers between devices  23.8 us (38%)
  waiting for transfers between devices  16.8 us (27%)
  Pallas kernels  12.1 us (20%)
  local copies, waits for them, and re-layouts  8.15 us (13%)
  between operations  0.83 us (1%)
    ppermute x14, starting transfers between devices, swap(): return lax.ppermute(x, axis, [(i, i ^ mask) for i in range(n)])  19.8 us
    ppermute x14, waiting for transfers between devices, swap(): return lax.ppermute(x, axis, [(i, i ^ mask) for i in range(n)])  12.5 us
    unnamed x16, local copies, waits for them, and re-layouts  7.01 us
    pallas_call x2, Pallas kernels, project(): pl.pallas_call(functools.partial(project_kernel, blocks, first, tile, wit...  5.96 us
    all_to_all x1, waiting for transfers between devices, exchange(): lax.all_to_all(x, axis, split_axis=0, concat_axis=0, tiled=True)  4.32 us
    all_to_all x1, starting transfers between devices, exchange(): lax.all_to_all(x, axis, split_axis=0, concat_axis=0, tiled=True)  3.99 us
    pallas_call x1, Pallas kernels, window_backward(): pl.pallas_call(window_kernel, out_shape=[shape] * 3, in_specs=vmem(6), ou...  2.38 us
  transfers between devices with their start and end apart: 15, of which 4 were waited for; matrix products, arithmetic and copies ran while one was open for 0% of the time, Pallas kernels for 8%

profile of v21, /device:TPU:0, one launch (start us, length us, event | category | flops | bytes accessed | tf_op | source)
XLA Modules:
  0.0 61.6 jit_solution(68828182308948711)
XLA Ops:
  0.7 1.1 %dynamic-slice_bitcast_fusion = (bf16[32,2048]{1,0:T(8,128)(2,1)S(1)}, bf16[32,2048]{1,0:T(8,128)(2,1)S(1)}, bf16[32,2048]{1,0:T(8,128)(2,1)S(1)}, bf16[32,2048]{1,0:T(8,128)(2,1)S(1)}) fusion(bf16[1,32,8192]{2,1,0:T(8,128)(2,1)} %param.9, s32[]{:T(128)S(6)} %select_n.15, s32[]{:T(128)S(6)} %select_n.13, s32[]{:T(128)S(6)} %select_n.12, s32[]{:T(128)S(6)} %select_n.14), kind=kLoop, calls=%fused_computation | loop fusion | bytes 1048592 | tf_op jit(solution)/shard_map/dynamic_slice | solution.py:474
  1.8 2.5 %collective-permute-start.2 = (bf16[32,2048]{1,0:T(8,128)(2,1)S(1)}, bf16[32,2048]{1,0:T(8,128)(2,1)S(1)}, u32[]{:S(2)}, u32[]{:S(2)}) collective-permute-start(bf16[32,2048]{1,0:T(8,128)(2,1)S(1)} %get-tuple-element.57), channel_id=1, source_target_pairs={{0,24},{8,16},{16,8},{24,0},{1,25},{9,17},{17,9},{25,1},{2,26},{10... | collective-permute-start | bytes 393224 | tf_op jit(solution)/shard_map/ppermute | solution.py:246
  4.3 0.6 %collective-permute-start = (bf16[32,2048]{1,0:T(8,128)(2,1)S(1)}, bf16[32,2048]{1,0:T(8,128)(2,1)S(1)}, u32[]{:S(2)}, u32[]{:S(2)}) collective-permute-start(bf16[32,2048]{1,0:T(8,128)(2,1)S(1)} %get-tuple-element.58), channel_id=1, source_target_pairs={{0,16},{8,24},{16,0},{24,8},{1,17},{9,25},{17,1},{25,9},{2,18},{10... | collective-permute-start | bytes 393224 | tf_op jit(solution)/shard_map/ppermute | solution.py:246
  4.9 0.0 collective-permute-start.1
  5.0 0.0 copy-start
  5.0 7.0 %copy-done = bf16[5120,2048]{1,0:T(8,128)(2,1)S(1)} copy-done((bf16[5120,2048]{1,0:T(8,128)(2,1)S(1)}, bf16[5120,2048]{1,0:T(8,128)(2,1)}, u32[]{:S(2)}) %copy-start) | copy-done | bytes 20971544
  11.9 0.0 collective-permute-done.2.refs_3_
  11.9 0.0 collective-permute-done.refs_1_
  11.9 0.0 collective-permute-done.1.refs_2_
  11.9 0.0 copy-start.5
  11.9 0.0 copy-start.7
  12.0 0.0 copy-start.1
  12.0 0.0 copy-start.2
  12.0 0.0 copy-start.3
  12.0 0.0 copy-start.6
  12.0 0.0 copy-start.4
  12.0 4.4 %project.2 = (bf16[64,3840]{1,0:T(8,128)(2,1)S(1)}, bf16[64,3840]{1,0:T(8,128)(2,1)S(1)}, f32[1,2048]{1,0:T(1,128)S(1)}) custom-call(bf16[32,2048]{1,0:T(8,128)(2,1)S(1)} %get-tuple-element.59.refs_0_, bf16[32,2048]{1,0:T(8,128)(2,1)S(1)} %collective-permute-done.refs_1_, bf16[32,2048]{1,0:T(8,128)(2,1)S(1)} %collective-permute-done.1.refs_2_, ...), custom_call_target="tpu_custom_call" | custom-call | flops 2013265920 | bytes 15728640 | tf_op jit(solution)/shard_map/project/pallas_call | solution.py:74
  16.4 0.5 collective-permute-start.3
  16.9 1.6 %project.3 = (bf16[64,1280]{1,0:T(8,128)(2,1)S(1)}, bf16[64,1280]{1,0:T(8,128)(2,1)S(1)}) custom-call(bf16[32,2048]{1,0:T(8,128)(2,1)S(1)} %get-tuple-element.59.refs_0_, bf16[32,2048]{1,0:T(8,128)(2,1)S(1)} %collective-permute-done.refs_1_, bf16[32,2048]{1,0:T(8,128)(2,1)S(1)} %collective-permute-done.1.refs_2_, ...), custom_call_target="tpu_custom_call" | custom-call | flops 671088640 | bytes 5242880 | tf_op jit(solution)/shard_map/project/pallas_call | solution.py:74
  18.5 0.1 collective-permute-start.5
  18.6 0.0 collective-permute-done.3.got_ref
  18.6 0.1 halve.2
  18.8 1.8 %collective-permute-start.4 = (bf16[32,3840]{1,0:T(8,128)(2,1)S(1)}, bf16[32,3840]{1,0:T(8,128)(2,1)S(1)}, u32[]{:S(2)}, u32[]{:S(2)}) collective-permute-start(bf16[32,3840]{1,0:T(8,128)(2,1)S(1)} %get-tuple-element.34), channel_id=1, source_target_pairs={{0,16},{8,24},{16,0},{24,8},{1,17},{9,25},{17,1},{25,9},{2,18},{10... | collective-permute-start | bytes 737288 | tf_op jit(solution)/shard_map/ppermute | solution.py:246
  20.6 0.0 collective-permute-done.5.got_ref
  20.6 0.9 %collective-permute-start.6 = (bf16[32,1280]{1,0:T(8,128)(2,1)S(1)}, bf16[32,1280]{1,0:T(8,128)(2,1)S(1)}, u32[]{:S(2)}, u32[]{:S(2)}) collective-permute-start(bf16[32,1280]{1,0:T(8,128)(2,1)S(1)} %get-tuple-element.38), channel_id=1, source_target_pairs={{0,16},{8,24},{16,0},{24,8},{1,17},{9,25},{17,1},{25,9},{2,18},{10... | collective-permute-start | bytes 245768 | tf_op jit(solution)/shard_map/ppermute | solution.py:246
  21.5 7.4 %collective-permute-done.6.refs_4_ = bf16[32,1280]{1,0:T(8,128)(2,1)S(1)} collective-permute-done((bf16[32,1280]{1,0:T(8,128)(2,1)S(1)}, bf16[32,1280]{1,0:T(8,128)(2,1)S(1)}, u32[]{:S(2)}, u32[]{:S(2)}) %collective-permute-start.6) | collective-permute-done | bytes 81952 | tf_op jit(solution)/shard_map/ppermute | solution.py:246
  28.9 0.0 collective-permute-done.4.refs_2_
  28.9 0.0 copy-done.5
  28.9 0.7 %pack.1 = (bf16[8,5248]{1,0:T(8,128)(2,1)S(1)}, bf16[8,5248]{1,0:T(8,128)(2,1)S(1)}, bf16[8,5248]{1,0:T(8,128)(2,1)S(1)}, bf16[8,5248]{1,0:T(8,128)(2,1)S(1)}, b...) custom-call(s32[1]{0:T(128)} %bitcast.1.me_ref, ...), custom_call_target="tpu_custom_call" | custom-call | flops 21495808 | bytes 1679360 | tf_op jit(solution)/shard_map/pack/pallas_call | solution.py:224
  29.6 4.6 %collective-permute-start.7 = (bf16[8,5248]{1,0:T(8,128)(2,1)S(1)}, bf16[8,5248]{1,0:T(8,128)(2,1)S(1)}, u32[]{:S(2)}, u32[]{:S(2)}) collective-permute-start(bf16[8,5248]{1,0:T(8,128)(2,1)S(1)} %get-tuple-element.41), channel_id=1, source_target_pairs={{0,7},{1,6},{2,5},{3,4},{4,3},{5,2},{6,1},{7,0},{8,15},{9,14},{10,... | collective-permute-start | bytes 251912 | tf_op jit(solution)/shard_map/ppermute | solution.py:246
  34.2 0.6 collective-permute-start.8
  34.7 0.2 collective-permute-start.9
  34.9 0.0 collective-permute-start.10
  34.9 5.1 %collective-permute-start.11 = (bf16[8,5248]{1,0:T(8,128)(2,1)S(1)}, bf16[8,5248]{1,0:T(8,128)(2,1)S(1)}, u32[]{:S(2)}, u32[]{:S(2)}) collective-permute-start(bf16[8,5248]{1,0:T(8,128)(2,1)S(1)} %get-tuple-element.45), channel_id=1, source_target_pairs={{0,5},{1,4},{2,7},{3,6},{4,1},{5,0},{6,3},{7,2},{8,13},{9,12},{10,... | collective-permute-start | bytes 251912 | tf_op jit(solution)/shard_map/ppermute | solution.py:246
  40.0 0.0 collective-permute-done.7.refs_1_
  40.0 0.0 collective-permute-start.12
  40.0 0.0 collective-permute-done.8.refs_2_
  40.0 2.8 %collective-permute-start.13 = (bf16[8,5248]{1,0:T(8,128)(2,1)S(1)}, bf16[8,5248]{1,0:T(8,128)(2,1)S(1)}, u32[]{:S(2)}, u32[]{:S(2)}) collective-permute-start(bf16[8,5248]{1,0:T(8,128)(2,1)S(1)} %get-tuple-element.47), channel_id=1, source_target_pairs={{0,4},{1,5},{2,6},{3,7},{4,0},{5,1},{6,2},{7,3},{8,12},{9,13},{10,... | collective-permute-start | bytes 251912 | tf_op jit(solution)/shard_map/ppermute | solution.py:246
  42.9 0.0 copy-done.7
  42.9 0.0 collective-permute-done.9.refs_3_
  42.9 0.0 collective-permute-done.10.refs_4_
  42.9 3.4 %collective-permute-done.11.refs_5_ = bf16[8,5248]{1,0:T(8,128)(2,1)S(1)} collective-permute-done((bf16[8,5248]{1,0:T(8,128)(2,1)S(1)}, bf16[8,5248]{1,0:T(8,128)(2,1)S(1)}, u32[]{:S(2)}, u32[]{:S(2)}) %collective-permute-start.11) | collective-permute-done | bytes 84000 | tf_op jit(solution)/shard_map/ppermute | solution.py:246
  46.3 0.0 collective-permute-done.12.refs_6_
  46.3 1.7 %collective-permute-done.13.refs_7_ = bf16[8,5248]{1,0:T(8,128)(2,1)S(1)} collective-permute-done((bf16[8,5248]{1,0:T(8,128)(2,1)S(1)}, bf16[8,5248]{1,0:T(8,128)(2,1)S(1)}, u32[]{:S(2)}, u32[]{:S(2)}) %collective-permute-start.13) | collective-permute-done | bytes 84000 | tf_op jit(solution)/shard_map/ppermute | solution.py:246
  48.0 0.0 copy-done.1
  48.0 1.1 %norm.1 = (bf16[128,1280]{1,0:T(8,128)(2,1)S(1)}, bf16[32,2,768]{2,1,0:T(2,128)(2,1)}) custom-call(bf16[128,1280]{1,0:T(8,128)(2,1)S(1)} %bitcast.17, f32[1,1280]{1,0:T(1,128)S(1)} %broadcast_in_dim.12.gain_ref, bf16[8,5248]{1,0:T(8,128)(2,1)S(1)} %get-tuple-element.40.refs_0_, bf16[8,5248]{1,0:T(8,128)(2,1)S(1)} %collective-permute-done.7.refs_1_, ...), custom_call_target="tpu_custom_call" | custom-call | flops 85983232 | bytes 1327104 | tf_op jit(solution)/shard_map/norm/pallas_call | solution.py:354
  49.1 4.0 %all-to-all-start = ((bf16[32,2,768]{2,1,0:T(2,128)(2,1)}), bf16[32,2,768]{2,1,0:T(2,128)(2,1)S(1)}, u32[]{:S(2)}, u32[]{:S(2)}) async-start(bf16[32,2,768]{2,1,0:T(2,128)(2,1)} %get-tuple-element.54), calls=%async_computation | async-start | bytes 196608 | tf_op jit(solution)/shard_map/all_to_all | solution.py:253
  53.1 0.0 copy-done.2
  53.1 0.0 copy-done.3
  53.1 0.0 copy-done.6
  53.1 1.1 %probs.1 = (f32[16,128,128]{2,1,0:T(8,128)S(1)}, f32[16,128,128]{2,1,0:T(8,128)S(1)}) custom-call(bf16[128,1280]{1,0:T(8,128)(2,1)S(1)} %bitcast.18, bf16[128,1280]{1,0:T(8,128)(2,1)S(1)} %bitcast.20, s32[1,32]{1,0:T(1,128)S(1)} %bitcast.23), custom_call_target="tpu_custom_call" | custom-call | flops 268435456 | bytes 2097152 | tf_op jit(solution)/shard_map/probs/pallas_call | solution.py:285
  54.2 0.0 copy-done.4
  54.2 2.4 %window.1 = (bf16[128,1280]{1,0:T(8,128)(2,1)}, bf16[128,1280]{1,0:T(8,128)(2,1)}, bf16[128,1280]{1,0:T(8,128)(2,1)}) custom-call(bf16[128,1280]{1,0:T(8,128)(2,1)S(1)} %get-tuple-element.48.g_ref, bf16[128,1280]{1,0:T(8,128)(2,1)S(1)} %bitcast.19, bf16[128,1280]{1,0:T(8,128)(2,1)S(1)} %bitcast.21, bf16[128,1280]{1,0:T(8,128)(2,1)S(1)} %bitcast.22, ...), custom_call_target="tpu_custom_call" | custom-call | flops 335544320 | bytes 4390912 | tf_op jit(solution)/shard_map/window/pallas_call | solution.py:410
  56.6 4.3 %all-to-all-done.shared_ref = bf16[32,2,768]{2,1,0:T(2,128)(2,1)S(1)} async-done(((bf16[32,2,768]{2,1,0:T(2,128)(2,1)}), bf16[32,2,768]{2,1,0:T(2,128)(2,1)S(1)}, u32[]{:S(2)}, u32[]{:S(2)}) %all-to-all-start) | async-done | bytes 98336 | tf_op jit(solution)/shard_map/all_to_all | solution.py:253
  60.9 0.7 %finish.1 = (f32[1280]{0:T(1024)}, f32[8192]{0:T(1024)}) custom-call(bf16[32,2,768]{2,1,0:T(2,128)(2,1)S(1)} %all-to-all-done.shared_ref), custom_call_target="tpu_custom_call" | custom-call | tf_op jit(solution)/shard_map/finish/pallas_call | solution.py:443
  (3 shorter events, 0.0 us)
Async XLA Ops:
  1.8 10.1 %collective-permute-start.2 = (bf16[32,2048]{1,0:T(8,128)(2,1)S(1)}, bf16[32,2048]{1,0:T(8,128)(2,1)S(1)}, u32[]{:S(2)}, u32[]{:S(2)}) collective-permute-start(bf16[32,2048]{1,0:T(8,128)(2,1)S(1)} %get-tuple-element.57), channel_id=1, source_target_pairs={{0,24},{8,16},{16,8},{24,0},{1,25},{9,17},{17,9},{25,1},{2,26},{10... | collective-permute-start | bytes 393224 | tf_op jit(solution)/shard_map/ppermute | solution.py:246
  4.3 7.7 %collective-permute-start = (bf16[32,2048]{1,0:T(8,128)(2,1)S(1)}, bf16[32,2048]{1,0:T(8,128)(2,1)S(1)}, u32[]{:S(2)}, u32[]{:S(2)}) collective-permute-start(bf16[32,2048]{1,0:T(8,128)(2,1)S(1)} %get-tuple-element.58), channel_id=1, source_target_pairs={{0,16},{8,24},{16,0},{24,8},{1,17},{9,25},{17,1},{25,9},{2,18},{10... | collective-permute-start | bytes 393224 | tf_op jit(solution)/shard_map/ppermute | solution.py:246
  4.9 7.0 %collective-permute-start.1 = (bf16[32,2048]{1,0:T(8,128)(2,1)S(1)}, bf16[32,2048]{1,0:T(8,128)(2,1)S(1)}, u32[]{:S(2)}, u32[]{:S(2)}) collective-permute-start(bf16[32,2048]{1,0:T(8,128)(2,1)S(1)} %get-tuple-element.60), channel_id=1, source_target_pairs={{0,8},{8,0},{16,24},{24,16},{1,9},{9,1},{17,25},{25,17},{2,10},{10... | collective-permute-start | bytes 393224 | tf_op jit(solution)/shard_map/ppermute | solution.py:246
  5.0 7.0 %copy-start = (bf16[5120,2048]{1,0:T(8,128)(2,1)S(1)}, bf16[5120,2048]{1,0:T(8,128)(2,1)}, u32[]{:S(2)}) copy-start(bf16[5120,2048]{1,0:T(8,128)(2,1)} %refs_4_.3) | copy-start | bytes 62914564
  11.9 17.0 %copy-start.5 = (s32[1,32]{1,0:T(1,128)S(1)}, s32[1,32]{1,0:T(1,128)}, u32[]{:S(2)}) copy-start(s32[1,32]{1,0:T(1,128)} %refs_0_.1) | copy-start | bytes 388
  11.9 30.9 %copy-start.7 = (f32[1280]{0:T(1024)S(1)}, f32[1280]{0:T(1024)}, u32[]{:S(2)}) copy-start(f32[1280]{0:T(1024)} %param.12) | copy-start | bytes 15364
  12.0 36.0 %copy-start.1 = (bf16[1,128,1280]{2,1,0:T(8,128)(2,1)S(1)}, bf16[1,128,1280]{2,1,0:T(8,128)(2,1)}, u32[]{:S(2)}) copy-start(bf16[1,128,1280]{2,1,0:T(8,128)(2,1)} %param.11) | copy-start | bytes 983044
  12.0 41.1 %copy-start.2 = (bf16[1,128,1280]{2,1,0:T(8,128)(2,1)S(1)}, bf16[1,128,1280]{2,1,0:T(8,128)(2,1)}, u32[]{:S(2)}) copy-start(bf16[1,128,1280]{2,1,0:T(8,128)(2,1)} %param.14) | copy-start | bytes 983044
  12.0 41.1 %copy-start.3 = (bf16[1,128,1280]{2,1,0:T(8,128)(2,1)S(1)}, bf16[1,128,1280]{2,1,0:T(8,128)(2,1)}, u32[]{:S(2)}) copy-start(bf16[1,128,1280]{2,1,0:T(8,128)(2,1)} %param.15) | copy-start | bytes 983044
  12.0 41.1 %copy-start.6 = (s32[1,1,32]{2,1,0:T(1,128)S(1)}, s32[1,1,32]{2,1,0:T(1,128)}, u32[]{:S(2)}) copy-start(s32[1,1,32]{2,1,0:T(1,128)} %param.17) | copy-start | bytes 388
  12.0 42.2 %copy-start.4 = (bf16[1,128,1280]{2,1,0:T(8,128)(2,1)S(1)}, bf16[1,128,1280]{2,1,0:T(8,128)(2,1)}, u32[]{:S(2)}) copy-start(bf16[1,128,1280]{2,1,0:T(8,128)(2,1)} %param.16) | copy-start | bytes 983044
  16.4 2.2 %collective-permute-start.3 = (bf16[64,3840]{1,0:T(8,128)(2,1)S(1)}, bf16[64,3840]{1,0:T(8,128)(2,1)S(1)}, u32[]{:S(2)}, u32[]{:S(2)}) collective-permute-start(bf16[64,3840]{1,0:T(8,128)(2,1)S(1)} %get-tuple-element.32), channel_id=1, source_target_pairs={{0,8},{8,0},{16,24},{24,16},{1,9},{9,1},{17,25},{25,17},{2,10},{10... | collective-permute-start | bytes 1474568 | tf_op jit(solution)/shard_map/ppermute | solution.py:246
  18.5 2.0 %collective-permute-start.5 = (bf16[64,1280]{1,0:T(8,128)(2,1)S(1)}, bf16[64,1280]{1,0:T(8,128)(2,1)S(1)}, u32[]{:S(2)}, u32[]{:S(2)}) collective-permute-start(bf16[64,1280]{1,0:T(8,128)(2,1)S(1)} %get-tuple-element.36), channel_id=1, source_target_pairs={{0,8},{8,0},{16,24},{24,16},{1,9},{9,1},{17,25},{25,17},{2,10},{10... | collective-permute-start | bytes 491528 | tf_op jit(solution)/shard_map/ppermute | solution.py:246
  18.8 10.1 %collective-permute-start.4 = (bf16[32,3840]{1,0:T(8,128)(2,1)S(1)}, bf16[32,3840]{1,0:T(8,128)(2,1)S(1)}, u32[]{:S(2)}, u32[]{:S(2)}) collective-permute-start(bf16[32,3840]{1,0:T(8,128)(2,1)S(1)} %get-tuple-element.34), channel_id=1, source_target_pairs={{0,16},{8,24},{16,0},{24,8},{1,17},{9,25},{17,1},{25,9},{2,18},{10... | collective-permute-start | bytes 737288 | tf_op jit(solution)/shard_map/ppermute | solution.py:246
  20.6 8.3 %collective-permute-start.6 = (bf16[32,1280]{1,0:T(8,128)(2,1)S(1)}, bf16[32,1280]{1,0:T(8,128)(2,1)S(1)}, u32[]{:S(2)}, u32[]{:S(2)}) collective-permute-start(bf16[32,1280]{1,0:T(8,128)(2,1)S(1)} %get-tuple-element.38), channel_id=1, source_target_pairs={{0,16},{8,24},{16,0},{24,8},{1,17},{9,25},{17,1},{25,9},{2,18},{10... | collective-permute-start | bytes 245768 | tf_op jit(solution)/shard_map/ppermute | solution.py:246
  29.6 10.4 %collective-permute-start.7 = (bf16[8,5248]{1,0:T(8,128)(2,1)S(1)}, bf16[8,5248]{1,0:T(8,128)(2,1)S(1)}, u32[]{:S(2)}, u32[]{:S(2)}) collective-permute-start(bf16[8,5248]{1,0:T(8,128)(2,1)S(1)} %get-tuple-element.41), channel_id=1, source_target_pairs={{0,7},{1,6},{2,5},{3,4},{4,3},{5,2},{6,1},{7,0},{8,15},{9,14},{10,... | collective-permute-start | bytes 251912 | tf_op jit(solution)/shard_map/ppermute | solution.py:246
  34.2 5.9 %collective-permute-start.8 = (bf16[8,5248]{1,0:T(8,128)(2,1)S(1)}, bf16[8,5248]{1,0:T(8,128)(2,1)S(1)}, u32[]{:S(2)}, u32[]{:S(2)}) collective-permute-start(bf16[8,5248]{1,0:T(8,128)(2,1)S(1)} %get-tuple-element.42), channel_id=1, source_target_pairs={{0,1},{1,0},{2,3},{3,2},{4,5},{5,4},{6,7},{7,6},{8,9},{9,8},{10,11... | collective-permute-start | bytes 251912 | tf_op jit(solution)/shard_map/ppermute | solution.py:246
  34.7 8.1 %collective-permute-start.9 = (bf16[8,5248]{1,0:T(8,128)(2,1)S(1)}, bf16[8,5248]{1,0:T(8,128)(2,1)S(1)}, u32[]{:S(2)}, u32[]{:S(2)}) collective-permute-start(bf16[8,5248]{1,0:T(8,128)(2,1)S(1)} %get-tuple-element.43), channel_id=1, source_target_pairs={{0,6},{1,7},{2,4},{3,5},{4,2},{5,3},{6,0},{7,1},{8,14},{9,15},{10,... | collective-permute-start | bytes 251912 | tf_op jit(solution)/shard_map/ppermute | solution.py:246
  34.9 7.9 %collective-permute-start.10 = (bf16[8,5248]{1,0:T(8,128)(2,1)S(1)}, bf16[8,5248]{1,0:T(8,128)(2,1)S(1)}, u32[]{:S(2)}, u32[]{:S(2)}) collective-permute-start(bf16[8,5248]{1,0:T(8,128)(2,1)S(1)} %get-tuple-element.44), channel_id=1, source_target_pairs={{0,2},{1,3},{2,0},{3,1},{4,6},{5,7},{6,4},{7,5},{8,10},{9,11},{10,... | collective-permute-start | bytes 251912 | tf_op jit(solution)/shard_map/ppermute | solution.py:246
  34.9 11.3 %collective-permute-start.11 = (bf16[8,5248]{1,0:T(8,128)(2,1)S(1)}, bf16[8,5248]{1,0:T(8,128)(2,1)S(1)}, u32[]{:S(2)}, u32[]{:S(2)}) collective-permute-start(bf16[8,5248]{1,0:T(8,128)(2,1)S(1)} %get-tuple-element.45), channel_id=1, source_target_pairs={{0,5},{1,4},{2,7},{3,6},{4,1},{5,0},{6,3},{7,2},{8,13},{9,12},{10,... | collective-permute-start | bytes 251912 | tf_op jit(solution)/shard_map/ppermute | solution.py:246
  40.0 6.2 %collective-permute-start.12 = (bf16[8,5248]{1,0:T(8,128)(2,1)S(1)}, bf16[8,5248]{1,0:T(8,128)(2,1)S(1)}, u32[]{:S(2)}, u32[]{:S(2)}) collective-permute-start(bf16[8,5248]{1,0:T(8,128)(2,1)S(1)} %get-tuple-element.46), channel_id=1, source_target_pairs={{0,3},{1,2},{2,1},{3,0},{4,7},{5,6},{6,5},{7,4},{8,11},{9,10},{10,... | collective-permute-start | bytes 251912 | tf_op jit(solution)/shard_map/ppermute | solution.py:246
  40.0 7.9 %collective-permute-start.13 = (bf16[8,5248]{1,0:T(8,128)(2,1)S(1)}, bf16[8,5248]{1,0:T(8,128)(2,1)S(1)}, u32[]{:S(2)}, u32[]{:S(2)}) collective-permute-start(bf16[8,5248]{1,0:T(8,128)(2,1)S(1)} %get-tuple-element.47), channel_id=1, source_target_pairs={{0,4},{1,5},{2,6},{3,7},{4,0},{5,1},{6,2},{7,3},{8,12},{9,13},{10,... | collective-permute-start | bytes 251912 | tf_op jit(solution)/shard_map/ppermute | solution.py:246
  49.1 11.8 %all-to-all-start = ((bf16[32,2,768]{2,1,0:T(2,128)(2,1)}), bf16[32,2,768]{2,1,0:T(2,128)(2,1)S(1)}, u32[]{:S(2)}, u32[]{:S(2)}) async-start(bf16[32,2,768]{2,1,0:T(2,128)(2,1)} %get-tuple-element.54), calls=%async_computation | async-start | bytes 196608 | tf_op jit(solution)/shard_map/all_to_all | solution.py:253

commit v22 on v21

--- a/solution.py
+++ b/solution.py
@@ -129,7 +129,7 @@
 
 
 def peer_masks(peers):
-    return (0, 7, 1, 6, 2, 5, 3, 4) if peers == 8 else tuple(range(peers))
+    return (0, 5, 1, 7, 2, 3, 4, 6) if peers == 8 else tuple(range(peers))
 
 
 def early_masks(peers):

time: 61.9 us -> 61.4 us (level)
  waiting for transfers between devices: 16.8 us -> 15.6 us
  starting transfers between devices: 23.8 us -> 24.5 us
    ppermute x14, waiting for transfers between devices: 12.5 us -> 11.3 us  [swap(): return lax.ppermute(x, axis, [(i, i ^ mask) for i in range(n)])]
where the time goes in v22:
time: 61.4 us; the launch traced here: 61.2 us
  starting transfers between devices  24.5 us (40%)
  waiting for transfers between devices  15.6 us (25%)
  Pallas kernels  12.1 us (20%)
  local copies, waits for them, and re-layouts  8.15 us (13%)
  between operations  0.83 us (1%)
    ppermute x14, starting transfers between devices, swap(): return lax.ppermute(x, axis, [(i, i ^ mask) for i in range(n)])  20.2 us
    ppermute x14, waiting for transfers between devices, swap(): return lax.ppermute(x, axis, [(i, i ^ mask) for i in range(n)])  11.3 us
    unnamed x16, local copies, waits for them, and re-layouts  7.01 us
    pallas_call x2, Pallas kernels, project(): pl.pallas_call(functools.partial(project_kernel, blocks, first, tile, wit...  5.96 us
    all_to_all x1, starting transfers between devices, exchange(): lax.all_to_all(x, axis, split_axis=0, concat_axis=0, tiled=True)  4.37 us
    all_to_all x1, waiting for transfers between devices, exchange(): lax.all_to_all(x, axis, split_axis=0, concat_axis=0, tiled=True)  4.32 us
    pallas_call x1, Pallas kernels, window_backward(): pl.pallas_call(window_kernel, out_shape=[shape] * 3, in_specs=vmem(6), ou...  2.38 us
  transfers between devices with their start and end apart: 15, of which 4 were waited for; matrix products, arithmetic and copies ran while one was open for 0% of the time, Pallas kernels for 8%

profile of v22, /device:TPU:0, one launch (start us, length us, event | category | flops | bytes accessed | tf_op | source)
XLA Modules:
  0.0 61.2 jit_solution(13851992252226628723)
XLA Ops:
  0.7 1.1 %dynamic-slice_bitcast_fusion = (bf16[32,2048]{1,0:T(8,128)(2,1)S(1)}, bf16[32,2048]{1,0:T(8,128)(2,1)S(1)}, bf16[32,2048]{1,0:T(8,128)(2,1)S(1)}, bf16[32,2048]{1,0:T(8,128)(2,1)S(1)}) fusion(bf16[1,32,8192]{2,1,0:T(8,128)(2,1)} %param.9, s32[]{:T(128)S(6)} %select_n.15, s32[]{:T(128)S(6)} %select_n.13, s32[]{:T(128)S(6)} %select_n.12, s32[]{:T(128)S(6)} %select_n.14), kind=kLoop, calls=%fused_computation | loop fusion | bytes 1048592 | tf_op jit(solution)/shard_map/dynamic_slice | solution.py:474
  1.8 2.5 %collective-permute-start.2 = (bf16[32,2048]{1,0:T(8,128)(2,1)S(1)}, bf16[32,2048]{1,0:T(8,128)(2,1)S(1)}, u32[]{:S(2)}, u32[]{:S(2)}) collective-permute-start(bf16[32,2048]{1,0:T(8,128)(2,1)S(1)} %get-tuple-element.57), channel_id=1, source_target_pairs={{0,24},{8,16},{16,8},{24,0},{1,25},{9,17},{17,9},{25,1},{2,26},{10... | collective-permute-start | bytes 393224 | tf_op jit(solution)/shard_map/ppermute | solution.py:246
  4.3 0.6 %collective-permute-start = (bf16[32,2048]{1,0:T(8,128)(2,1)S(1)}, bf16[32,2048]{1,0:T(8,128)(2,1)S(1)}, u32[]{:S(2)}, u32[]{:S(2)}) collective-permute-start(bf16[32,2048]{1,0:T(8,128)(2,1)S(1)} %get-tuple-element.58), channel_id=1, source_target_pairs={{0,16},{8,24},{16,0},{24,8},{1,17},{9,25},{17,1},{25,9},{2,18},{10... | collective-permute-start | bytes 393224 | tf_op jit(solution)/shard_map/ppermute | solution.py:246
  4.9 0.0 collective-permute-start.1
  5.0 0.0 copy-start
  5.0 7.0 %copy-done = bf16[5120,2048]{1,0:T(8,128)(2,1)S(1)} copy-done((bf16[5120,2048]{1,0:T(8,128)(2,1)S(1)}, bf16[5120,2048]{1,0:T(8,128)(2,1)}, u32[]{:S(2)}) %copy-start) | copy-done | bytes 20971544
  11.9 0.0 collective-permute-done.2.refs_3_
  11.9 0.0 collective-permute-done.refs_1_
  11.9 0.0 collective-permute-done.1.refs_2_
  11.9 0.0 copy-start.5
  11.9 0.0 copy-start.7
  12.0 0.0 copy-start.1
  12.0 0.0 copy-start.2
  12.0 0.0 copy-start.3
  12.0 0.0 copy-start.6
  12.0 0.0 copy-start.4
  12.0 4.4 %project.2 = (bf16[64,3840]{1,0:T(8,128)(2,1)S(1)}, bf16[64,3840]{1,0:T(8,128)(2,1)S(1)}, f32[1,2048]{1,0:T(1,128)S(1)}) custom-call(bf16[32,2048]{1,0:T(8,128)(2,1)S(1)} %get-tuple-element.59.refs_0_, bf16[32,2048]{1,0:T(8,128)(2,1)S(1)} %collective-permute-done.refs_1_, bf16[32,2048]{1,0:T(8,128)(2,1)S(1)} %collective-permute-done.1.refs_2_, ...), custom_call_target="tpu_custom_call" | custom-call | flops 2013265920 | bytes 15728640 | tf_op jit(solution)/shard_map/project/pallas_call | solution.py:74
  16.4 0.5 collective-permute-start.3
  16.9 1.6 %project.3 = (bf16[64,1280]{1,0:T(8,128)(2,1)S(1)}, bf16[64,1280]{1,0:T(8,128)(2,1)S(1)}) custom-call(bf16[32,2048]{1,0:T(8,128)(2,1)S(1)} %get-tuple-element.59.refs_0_, bf16[32,2048]{1,0:T(8,128)(2,1)S(1)} %collective-permute-done.refs_1_, bf16[32,2048]{1,0:T(8,128)(2,1)S(1)} %collective-permute-done.1.refs_2_, ...), custom_call_target="tpu_custom_call" | custom-call | flops 671088640 | bytes 5242880 | tf_op jit(solution)/shard_map/project/pallas_call | solution.py:74
  18.5 0.1 collective-permute-start.5
  18.6 0.0 collective-permute-done.3.got_ref
  18.6 0.1 halve.2
  18.8 1.8 %collective-permute-start.4 = (bf16[32,3840]{1,0:T(8,128)(2,1)S(1)}, bf16[32,3840]{1,0:T(8,128)(2,1)S(1)}, u32[]{:S(2)}, u32[]{:S(2)}) collective-permute-start(bf16[32,3840]{1,0:T(8,128)(2,1)S(1)} %get-tuple-element.34), channel_id=1, source_target_pairs={{0,16},{8,24},{16,0},{24,8},{1,17},{9,25},{17,1},{25,9},{2,18},{10... | collective-permute-start | bytes 737288 | tf_op jit(solution)/shard_map/ppermute | solution.py:246
  20.6 0.0 collective-permute-done.5.got_ref
  20.6 0.9 %collective-permute-start.6 = (bf16[32,1280]{1,0:T(8,128)(2,1)S(1)}, bf16[32,1280]{1,0:T(8,128)(2,1)S(1)}, u32[]{:S(2)}, u32[]{:S(2)}) collective-permute-start(bf16[32,1280]{1,0:T(8,128)(2,1)S(1)} %get-tuple-element.38), channel_id=1, source_target_pairs={{0,16},{8,24},{16,0},{24,8},{1,17},{9,25},{17,1},{25,9},{2,18},{10... | collective-permute-start | bytes 245768 | tf_op jit(solution)/shard_map/ppermute | solution.py:246
  21.5 7.4 %collective-permute-done.6.refs_4_ = bf16[32,1280]{1,0:T(8,128)(2,1)S(1)} collective-permute-done((bf16[32,1280]{1,0:T(8,128)(2,1)S(1)}, bf16[32,1280]{1,0:T(8,128)(2,1)S(1)}, u32[]{:S(2)}, u32[]{:S(2)}) %collective-permute-start.6) | collective-permute-done | bytes 81952 | tf_op jit(solution)/shard_map/ppermute | solution.py:246
  28.9 0.0 collective-permute-done.4.refs_2_
  28.9 0.0 copy-done.5
  28.9 0.7 %pack.1 = (bf16[8,5248]{1,0:T(8,128)(2,1)S(1)}, bf16[8,5248]{1,0:T(8,128)(2,1)S(1)}, bf16[8,5248]{1,0:T(8,128)(2,1)S(1)}, bf16[8,5248]{1,0:T(8,128)(2,1)S(1)}, b...) custom-call(s32[1]{0:T(128)} %bitcast.1.me_ref, ...), custom_call_target="tpu_custom_call" | custom-call | flops 21495808 | bytes 1679360 | tf_op jit(solution)/shard_map/pack/pallas_call | solution.py:224
  29.6 3.6 %collective-permute-start.7 = (bf16[8,5248]{1,0:T(8,128)(2,1)S(1)}, bf16[8,5248]{1,0:T(8,128)(2,1)S(1)}, u32[]{:S(2)}, u32[]{:S(2)}) collective-permute-start(bf16[8,5248]{1,0:T(8,128)(2,1)S(1)} %get-tuple-element.41), channel_id=1, source_target_pairs={{0,5},{1,4},{2,7},{3,6},{4,1},{5,0},{6,3},{7,2},{8,13},{9,12},{10,... | collective-permute-start | bytes 251912 | tf_op jit(solution)/shard_map/ppermute | solution.py:246
  33.2 0.6 collective-permute-start.8
  33.7 2.3 %collective-permute-start.9 = (bf16[8,5248]{1,0:T(8,128)(2,1)S(1)}, bf16[8,5248]{1,0:T(8,128)(2,1)S(1)}, u32[]{:S(2)}, u32[]{:S(2)}) collective-permute-start(bf16[8,5248]{1,0:T(8,128)(2,1)S(1)} %get-tuple-element.43), channel_id=1, source_target_pairs={{0,7},{1,6},{2,5},{3,4},{4,3},{5,2},{6,1},{7,0},{8,15},{9,14},{10,... | collective-permute-start | bytes 251912 | tf_op jit(solution)/shard_map/ppermute | solution.py:246
  36.0 0.0 collective-permute-start.10
  36.0 2.0 %collective-permute-start.11 = (bf16[8,5248]{1,0:T(8,128)(2,1)S(1)}, bf16[8,5248]{1,0:T(8,128)(2,1)S(1)}, u32[]{:S(2)}, u32[]{:S(2)}) collective-permute-start(bf16[8,5248]{1,0:T(8,128)(2,1)S(1)} %get-tuple-element.45), channel_id=1, source_target_pairs={{0,3},{1,2},{2,1},{3,0},{4,7},{5,6},{6,5},{7,4},{8,11},{9,10},{10,... | collective-permute-start | bytes 251912 | tf_op jit(solution)/shard_map/ppermute | solution.py:246
  38.0 0.0 collective-permute-done.7.refs_1_
  38.0 1.7 %collective-permute-start.12 = (bf16[8,5248]{1,0:T(8,128)(2,1)S(1)}, bf16[8,5248]{1,0:T(8,128)(2,1)S(1)}, u32[]{:S(2)}, u32[]{:S(2)}) collective-permute-start(bf16[8,5248]{1,0:T(8,128)(2,1)S(1)} %get-tuple-element.46), channel_id=1, source_target_pairs={{0,4},{1,5},{2,6},{3,7},{4,0},{5,1},{6,2},{7,3},{8,12},{9,13},{10,... | collective-permute-start | bytes 251912 | tf_op jit(solution)/shard_map/ppermute | solution.py:246
  39.7 0.0 collective-permute-done.8.refs_2_
  39.7 3.5 %collective-permute-start.13 = (bf16[8,5248]{1,0:T(8,128)(2,1)S(1)}, bf16[8,5248]{1,0:T(8,128)(2,1)S(1)}, u32[]{:S(2)}, u32[]{:S(2)}) collective-permute-start(bf16[8,5248]{1,0:T(8,128)(2,1)S(1)} %get-tuple-element.47), channel_id=1, source_target_pairs={{0,6},{1,7},{2,4},{3,5},{4,2},{5,3},{6,0},{7,1},{8,14},{9,15},{10,... | collective-permute-start | bytes 251912 | tf_op jit(solution)/shard_map/ppermute | solution.py:246
  43.2 0.0 copy-done.7
  43.2 0.0 collective-permute-done.9.refs_3_
  43.2 0.0 collective-permute-done.10.refs_4_
  43.3 0.6 collective-permute-done.11.refs_5_
  43.8 3.3 %collective-permute-done.12.refs_6_ = bf16[8,5248]{1,0:T(8,128)(2,1)S(1)} collective-permute-done((bf16[8,5248]{1,0:T(8,128)(2,1)S(1)}, bf16[8,5248]{1,0:T(8,128)(2,1)S(1)}, u32[]{:S(2)}, u32[]{:S(2)}) %collective-permute-start.12) | collective-permute-done | bytes 84000 | tf_op jit(solution)/shard_map/ppermute | solution.py:246
  47.2 0.0 collective-permute-done.13.refs_7_
  47.2 0.0 copy-done.1
  47.2 1.1 %norm.1 = (bf16[128,1280]{1,0:T(8,128)(2,1)S(1)}, bf16[32,2,768]{2,1,0:T(2,128)(2,1)}) custom-call(bf16[128,1280]{1,0:T(8,128)(2,1)S(1)} %bitcast.17, f32[1,1280]{1,0:T(1,128)S(1)} %broadcast_in_dim.12.gain_ref, bf16[8,5248]{1,0:T(8,128)(2,1)S(1)} %get-tuple-element.40.refs_0_, bf16[8,5248]{1,0:T(8,128)(2,1)S(1)} %collective-permute-done.7.refs_1_, ...), custom_call_target="tpu_custom_call" | custom-call | flops 85983232 | bytes 1327104 | tf_op jit(solution)/shard_map/norm/pallas_call | solution.py:354
  48.3 4.4 %all-to-all-start = ((bf16[32,2,768]{2,1,0:T(2,128)(2,1)}), bf16[32,2,768]{2,1,0:T(2,128)(2,1)S(1)}, u32[]{:S(2)}, u32[]{:S(2)}) async-start(bf16[32,2,768]{2,1,0:T(2,128)(2,1)} %get-tuple-element.54), calls=%async_computation | async-start | bytes 196608 | tf_op jit(solution)/shard_map/all_to_all | solution.py:253
  52.7 0.0 copy-done.2
  52.7 0.0 copy-done.3
  52.7 0.0 copy-done.6
  52.7 1.1 %probs.1 = (f32[16,128,128]{2,1,0:T(8,128)S(1)}, f32[16,128,128]{2,1,0:T(8,128)S(1)}) custom-call(bf16[128,1280]{1,0:T(8,128)(2,1)S(1)} %bitcast.18, bf16[128,1280]{1,0:T(8,128)(2,1)S(1)} %bitcast.20, s32[1,32]{1,0:T(1,128)S(1)} %bitcast.23), custom_call_target="tpu_custom_call" | custom-call | flops 268435456 | bytes 2097152 | tf_op jit(solution)/shard_map/probs/pallas_call | solution.py:285
  53.8 0.0 copy-done.4
  53.8 2.4 %window.1 = (bf16[128,1280]{1,0:T(8,128)(2,1)}, bf16[128,1280]{1,0:T(8,128)(2,1)}, bf16[128,1280]{1,0:T(8,128)(2,1)}) custom-call(bf16[128,1280]{1,0:T(8,128)(2,1)S(1)} %get-tuple-element.48.g_ref, bf16[128,1280]{1,0:T(8,128)(2,1)S(1)} %bitcast.19, bf16[128,1280]{1,0:T(8,128)(2,1)S(1)} %bitcast.21, bf16[128,1280]{1,0:T(8,128)(2,1)S(1)} %bitcast.22, ...), custom_call_target="tpu_custom_call" | custom-call | flops 335544320 | bytes 4390912 | tf_op jit(solution)/shard_map/window/pallas_call | solution.py:410
  56.1 4.3 %all-to-all-done.shared_ref = bf16[32,2,768]{2,1,0:T(2,128)(2,1)S(1)} async-done(((bf16[32,2,768]{2,1,0:T(2,128)(2,1)}), bf16[32,2,768]{2,1,0:T(2,128)(2,1)S(1)}, u32[]{:S(2)}, u32[]{:S(2)}) %all-to-all-start) | async-done | bytes 98336 | tf_op jit(solution)/shard_map/all_to_all | solution.py:253
  60.5 0.7 %finish.1 = (f32[1280]{0:T(1024)}, f32[8192]{0:T(1024)}) custom-call(bf16[32,2,768]{2,1,0:T(2,128)(2,1)S(1)} %all-to-all-done.shared_ref), custom_call_target="tpu_custom_call" | custom-call | tf_op jit(solution)/shard_map/finish/pallas_call | solution.py:443
  (3 shorter events, 0.0 us)
Async XLA Ops:
  1.8 10.1 %collective-permute-start.2 = (bf16[32,2048]{1,0:T(8,128)(2,1)S(1)}, bf16[32,2048]{1,0:T(8,128)(2,1)S(1)}, u32[]{:S(2)}, u32[]{:S(2)}) collective-permute-start(bf16[32,2048]{1,0:T(8,128)(2,1)S(1)} %get-tuple-element.57), channel_id=1, source_target_pairs={{0,24},{8,16},{16,8},{24,0},{1,25},{9,17},{17,9},{25,1},{2,26},{10... | collective-permute-start | bytes 393224 | tf_op jit(solution)/shard_map/ppermute | solution.py:246
  4.3 7.7 %collective-permute-start = (bf16[32,2048]{1,0:T(8,128)(2,1)S(1)}, bf16[32,2048]{1,0:T(8,128)(2,1)S(1)}, u32[]{:S(2)}, u32[]{:S(2)}) collective-permute-start(bf16[32,2048]{1,0:T(8,128)(2,1)S(1)} %get-tuple-element.58), channel_id=1, source_target_pairs={{0,16},{8,24},{16,0},{24,8},{1,17},{9,25},{17,1},{25,9},{2,18},{10... | collective-permute-start | bytes 393224 | tf_op jit(solution)/shard_map/ppermute | solution.py:246
  4.9 7.0 %collective-permute-start.1 = (bf16[32,2048]{1,0:T(8,128)(2,1)S(1)}, bf16[32,2048]{1,0:T(8,128)(2,1)S(1)}, u32[]{:S(2)}, u32[]{:S(2)}) collective-permute-start(bf16[32,2048]{1,0:T(8,128)(2,1)S(1)} %get-tuple-element.60), channel_id=1, source_target_pairs={{0,8},{8,0},{16,24},{24,16},{1,9},{9,1},{17,25},{25,17},{2,10},{10... | collective-permute-start | bytes 393224 | tf_op jit(solution)/shard_map/ppermute | solution.py:246
  5.0 7.0 %copy-start = (bf16[5120,2048]{1,0:T(8,128)(2,1)S(1)}, bf16[5120,2048]{1,0:T(8,128)(2,1)}, u32[]{:S(2)}) copy-start(bf16[5120,2048]{1,0:T(8,128)(2,1)} %refs_4_.3) | copy-start | bytes 62914564
  11.9 17.0 %copy-start.5 = (s32[1,32]{1,0:T(1,128)S(1)}, s32[1,32]{1,0:T(1,128)}, u32[]{:S(2)}) copy-start(s32[1,32]{1,0:T(1,128)} %refs_0_.1) | copy-start | bytes 388
  11.9 31.3 %copy-start.7 = (f32[1280]{0:T(1024)S(1)}, f32[1280]{0:T(1024)}, u32[]{:S(2)}) copy-start(f32[1280]{0:T(1024)} %param.12) | copy-start | bytes 15364
  12.0 35.2 %copy-start.1 = (bf16[1,128,1280]{2,1,0:T(8,128)(2,1)S(1)}, bf16[1,128,1280]{2,1,0:T(8,128)(2,1)}, u32[]{:S(2)}) copy-start(bf16[1,128,1280]{2,1,0:T(8,128)(2,1)} %param.11) | copy-start | bytes 983044
  12.0 40.7 %copy-start.2 = (bf16[1,128,1280]{2,1,0:T(8,128)(2,1)S(1)}, bf16[1,128,1280]{2,1,0:T(8,128)(2,1)}, u32[]{:S(2)}) copy-start(bf16[1,128,1280]{2,1,0:T(8,128)(2,1)} %param.14) | copy-start | bytes 983044
  12.0 40.7 %copy-start.3 = (bf16[1,128,1280]{2,1,0:T(8,128)(2,1)S(1)}, bf16[1,128,1280]{2,1,0:T(8,128)(2,1)}, u32[]{:S(2)}) copy-start(bf16[1,128,1280]{2,1,0:T(8,128)(2,1)} %param.15) | copy-start | bytes 983044
  12.0 40.7 %copy-start.6 = (s32[1,1,32]{2,1,0:T(1,128)S(1)}, s32[1,1,32]{2,1,0:T(1,128)}, u32[]{:S(2)}) copy-start(s32[1,1,32]{2,1,0:T(1,128)} %param.17) | copy-start | bytes 388
  12.0 41.8 %copy-start.4 = (bf16[1,128,1280]{2,1,0:T(8,128)(2,1)S(1)}, bf16[1,128,1280]{2,1,0:T(8,128)(2,1)}, u32[]{:S(2)}) copy-start(bf16[1,128,1280]{2,1,0:T(8,128)(2,1)} %param.16) | copy-start | bytes 983044
  16.4 2.2 %collective-permute-start.3 = (bf16[64,3840]{1,0:T(8,128)(2,1)S(1)}, bf16[64,3840]{1,0:T(8,128)(2,1)S(1)}, u32[]{:S(2)}, u32[]{:S(2)}) collective-permute-start(bf16[64,3840]{1,0:T(8,128)(2,1)S(1)} %get-tuple-element.32), channel_id=1, source_target_pairs={{0,8},{8,0},{16,24},{24,16},{1,9},{9,1},{17,25},{25,17},{2,10},{10... | collective-permute-start | bytes 1474568 | tf_op jit(solution)/shard_map/ppermute | solution.py:246
  18.5 2.0 %collective-permute-start.5 = (bf16[64,1280]{1,0:T(8,128)(2,1)S(1)}, bf16[64,1280]{1,0:T(8,128)(2,1)S(1)}, u32[]{:S(2)}, u32[]{:S(2)}) collective-permute-start(bf16[64,1280]{1,0:T(8,128)(2,1)S(1)} %get-tuple-element.36), channel_id=1, source_target_pairs={{0,8},{8,0},{16,24},{24,16},{1,9},{9,1},{17,25},{25,17},{2,10},{10... | collective-permute-start | bytes 491528 | tf_op jit(solution)/shard_map/ppermute | solution.py:246
  18.8 10.1 %collective-permute-start.4 = (bf16[32,3840]{1,0:T(8,128)(2,1)S(1)}, bf16[32,3840]{1,0:T(8,128)(2,1)S(1)}, u32[]{:S(2)}, u32[]{:S(2)}) collective-permute-start(bf16[32,3840]{1,0:T(8,128)(2,1)S(1)} %get-tuple-element.34), channel_id=1, source_target_pairs={{0,16},{8,24},{16,0},{24,8},{1,17},{9,25},{17,1},{25,9},{2,18},{10... | collective-permute-start | bytes 737288 | tf_op jit(solution)/shard_map/ppermute | solution.py:246
  20.6 8.3 %collective-permute-start.6 = (bf16[32,1280]{1,0:T(8,128)(2,1)S(1)}, bf16[32,1280]{1,0:T(8,128)(2,1)S(1)}, u32[]{:S(2)}, u32[]{:S(2)}) collective-permute-start(bf16[32,1280]{1,0:T(8,128)(2,1)S(1)} %get-tuple-element.38), channel_id=1, source_target_pairs={{0,16},{8,24},{16,0},{24,8},{1,17},{9,25},{17,1},{25,9},{2,18},{10... | collective-permute-start | bytes 245768 | tf_op jit(solution)/shard_map/ppermute | solution.py:246
  29.6 8.4 %collective-permute-start.7 = (bf16[8,5248]{1,0:T(8,128)(2,1)S(1)}, bf16[8,5248]{1,0:T(8,128)(2,1)S(1)}, u32[]{:S(2)}, u32[]{:S(2)}) collective-permute-start(bf16[8,5248]{1,0:T(8,128)(2,1)S(1)} %get-tuple-element.41), channel_id=1, source_target_pairs={{0,5},{1,4},{2,7},{3,6},{4,1},{5,0},{6,3},{7,2},{8,13},{9,12},{10,... | collective-permute-start | bytes 251912 | tf_op jit(solution)/shard_map/ppermute | solution.py:246
  33.2 6.5 %collective-permute-start.8 = (bf16[8,5248]{1,0:T(8,128)(2,1)S(1)}, bf16[8,5248]{1,0:T(8,128)(2,1)S(1)}, u32[]{:S(2)}, u32[]{:S(2)}) collective-permute-start(bf16[8,5248]{1,0:T(8,128)(2,1)S(1)} %get-tuple-element.42), channel_id=1, source_target_pairs={{0,1},{1,0},{2,3},{3,2},{4,5},{5,4},{6,7},{7,6},{8,9},{9,8},{10,11... | collective-permute-start | bytes 251912 | tf_op jit(solution)/shard_map/ppermute | solution.py:246
  33.7 9.5 %collective-permute-start.9 = (bf16[8,5248]{1,0:T(8,128)(2,1)S(1)}, bf16[8,5248]{1,0:T(8,128)(2,1)S(1)}, u32[]{:S(2)}, u32[]{:S(2)}) collective-permute-start(bf16[8,5248]{1,0:T(8,128)(2,1)S(1)} %get-tuple-element.43), channel_id=1, source_target_pairs={{0,7},{1,6},{2,5},{3,4},{4,3},{5,2},{6,1},{7,0},{8,15},{9,14},{10,... | collective-permute-start | bytes 251912 | tf_op jit(solution)/shard_map/ppermute | solution.py:246
  36.0 7.3 %collective-permute-start.10 = (bf16[8,5248]{1,0:T(8,128)(2,1)S(1)}, bf16[8,5248]{1,0:T(8,128)(2,1)S(1)}, u32[]{:S(2)}, u32[]{:S(2)}) collective-permute-start(bf16[8,5248]{1,0:T(8,128)(2,1)S(1)} %get-tuple-element.44), channel_id=1, source_target_pairs={{0,2},{1,3},{2,0},{3,1},{4,6},{5,7},{6,4},{7,5},{8,10},{9,11},{10,... | collective-permute-start | bytes 251912 | tf_op jit(solution)/shard_map/ppermute | solution.py:246
  36.0 7.9 %collective-permute-start.11 = (bf16[8,5248]{1,0:T(8,128)(2,1)S(1)}, bf16[8,5248]{1,0:T(8,128)(2,1)S(1)}, u32[]{:S(2)}, u32[]{:S(2)}) collective-permute-start(bf16[8,5248]{1,0:T(8,128)(2,1)S(1)} %get-tuple-element.45), channel_id=1, source_target_pairs={{0,3},{1,2},{2,1},{3,0},{4,7},{5,6},{6,5},{7,4},{8,11},{9,10},{10,... | collective-permute-start | bytes 251912 | tf_op jit(solution)/shard_map/ppermute | solution.py:246
  38.0 9.2 %collective-permute-start.12 = (bf16[8,5248]{1,0:T(8,128)(2,1)S(1)}, bf16[8,5248]{1,0:T(8,128)(2,1)S(1)}, u32[]{:S(2)}, u32[]{:S(2)}) collective-permute-start(bf16[8,5248]{1,0:T(8,128)(2,1)S(1)} %get-tuple-element.46), channel_id=1, source_target_pairs={{0,4},{1,5},{2,6},{3,7},{4,0},{5,1},{6,2},{7,3},{8,12},{9,13},{10,... | collective-permute-start | bytes 251912 | tf_op jit(solution)/shard_map/ppermute | solution.py:246
  39.7 7.5 %collective-permute-start.13 = (bf16[8,5248]{1,0:T(8,128)(2,1)S(1)}, bf16[8,5248]{1,0:T(8,128)(2,1)S(1)}, u32[]{:S(2)}, u32[]{:S(2)}) collective-permute-start(bf16[8,5248]{1,0:T(8,128)(2,1)S(1)} %get-tuple-element.47), channel_id=1, source_target_pairs={{0,6},{1,7},{2,4},{3,5},{4,2},{5,3},{6,0},{7,1},{8,14},{9,15},{10,... | collective-permute-start | bytes 251912 | tf_op jit(solution)/shard_map/ppermute | solution.py:246
  48.3 12.2 %all-to-all-start = ((bf16[32,2,768]{2,1,0:T(2,128)(2,1)}), bf16[32,2,768]{2,1,0:T(2,128)(2,1)S(1)}, u32[]{:S(2)}, u32[]{:S(2)}) async-start(bf16[32,2,768]{2,1,0:T(2,128)(2,1)} %get-tuple-element.54), calls=%async_computation | async-start | bytes 196608 | tf_op jit(solution)/shard_map/all_to_all | solution.py:253
